TPU v7x, 32 devices: a whole 2x2x4 slice. The times are simulated.
32 devices in a mesh: groups: 2 (over x), expert: 2 (over core), tensor: 8 (over z, y).
Axes of the slice: x: 2, y: 2, z: 4, core: 2. Of those that a mesh axis runs over, the one named last changes fastest.
Arguments:
- tokens: bfloat16 [2048, 6144], P(('groups', 'expert', 'tensor')), parts along dimension 0, may hold values from -6 to 6
- expert_ids: int32 [2048, 2], P(('groups', 'expert', 'tensor')), parts along dimension 0, may hold values from 0 to 7, all different within a row; in each aligned block of 64 rows (0 to 63, 64 to 127, ...) at most 24 rows name the same one
- gate_probs: float32 [2048, 2], P(('groups', 'expert', 'tensor')), parts along dimension 0, may hold values from 0.1 to 1
- w_gate: bfloat16 [2, 6144, 8192], P('expert', None, 'tensor'), may hold values from -0.078125 to 0.078125
- w_up: bfloat16 [2, 6144, 8192], P('expert', None, 'tensor'), may hold values from -0.078125 to 0.078125
- w_down: bfloat16 [2, 8192, 6144], P('expert', 'tensor'), may hold values from -0.0625 to 0.0625
Outputs:
- mixed: bfloat16 [2048, 6144], P(('groups', 'expert', 'tensor')), parts along dimension 0
There are 2 independent parts, one for each index of `groups`. A program takes and returns all parts, laid end to end along the dimension named above; an argument that names none is the same for every part. Nothing has to cross between parts.
Inputs may be any that keep to these rules, and one draw needn't show every extreme that they name: `expert_ids`: in the rows of one device, each expert is named by at most 24 rows; each row names 2 different experts.
All inputs are finite; a program needn't handle non-finite values.
Results may differ from a plain program's by a relative error of at most 0.015.
Values may be sent and summed in bfloat16 or wider, within the bound.
No kernel may reach another device: no remote copies, remote signals or barrier semaphores. Data moves between devices by JAX's collectives and lax.ppermute only.
A program may use at most 128 MiB of HBM per device.

v0:
```python
import jax
import jax.numpy as jnp
from jax import lax
from jax.sharding import PartitionSpec as P

CAP = 24


def routing(expert_ids, gate_probs, held_count, slots):
    experts = jnp.arange(held_count)
    matches = expert_ids[:, :, None] == experts[None, None, :]
    member = jnp.any(matches, axis=1).astype(jnp.int32)
    weight = jnp.sum(jnp.where(matches, gate_probs[:, :, None], jnp.float32(0.0)), axis=1)
    slot_index = jnp.cumsum(member, axis=0) - member
    column = jnp.arange(slots)
    dispatch_map = (member[None, :, :] == 1) & (slot_index[None, :, :] == column[:, None, None])
    return (jnp.transpose(dispatch_map, (2, 0, 1)), weight)


def per_device(tokens, expert_ids, gate_probs, w_gate, w_up, w_down):
    held_count = lax.axis_size("expert")
    model_width = tokens.shape[1]
    dispatch_map, weight = routing(expert_ids, gate_probs, held_count, CAP)
    outgoing = jnp.dot(
        dispatch_map.astype(jnp.bfloat16).reshape(held_count * CAP, tokens.shape[0]),
        tokens,
        preferred_element_type=jnp.float32,
    )
    outgoing = outgoing.astype(jnp.bfloat16).reshape(held_count, CAP, model_width)
    gate_cols = w_gate[0]
    up_cols = w_up[0]
    down_rows = w_down[0]
    arrived = lax.all_to_all(outgoing, "expert", split_axis=0, concat_axis=0, tiled=True)
    arrived_rows = arrived.reshape(held_count * CAP, model_width)
    piece = lax.all_gather(arrived_rows, "tensor", axis=0, tiled=True)
    gate_part = jnp.dot(piece, gate_cols, preferred_element_type=jnp.float32)
    up_part = jnp.dot(piece, up_cols, preferred_element_type=jnp.float32)
    hidden = (jax.nn.silu(gate_part) * up_part).astype(jnp.bfloat16)
    summed = lax.psum_scatter(
        jnp.dot(hidden, down_rows, preferred_element_type=jnp.float32).astype(jnp.bfloat16),
        "tensor",
        scatter_dimension=0,
        tiled=True,
    )
    expert_out = summed.reshape(held_count, CAP, model_width)
    returned = lax.all_to_all(expert_out, "expert", split_axis=0, concat_axis=0, tiled=True)
    combine = dispatch_map.astype(jnp.float32) * jnp.transpose(weight)[:, None, :]
    mixed = jnp.einsum("wcr,wcd->rd", combine, returned.astype(jnp.float32))
    return mixed.astype(jnp.bfloat16)


def solution(mesh):
    in_specs = (
        P(("groups", "expert", "tensor"), None),
        P(("groups", "expert", "tensor"), None),
        P(("groups", "expert", "tensor"), None),
        P("expert", None, "tensor"),
        P("expert", None, "tensor"),
        P("expert", "tensor", None),
    )
    out_specs = P(("groups", "expert", "tensor"), None)
    return jax.shard_map(
        per_device, mesh=mesh, in_specs=in_specs, out_specs=out_specs, check_vma=False
    )
```

profile of v0, /device:TPU:0, one launch (start us, length us, event | category | flops | bytes accessed | tf_op | source)
XLA Modules:
  0.0 233.9 jit_solution(11776081053137516389)
XLA Ops:
  6.5 0.0 copy-start
  6.5 0.0 all-gather.2.cloned.1.call-start
  6.5 0.8 fusion.23
  7.3 0.0 copy-start.3
  7.3 0.1 copy.17
  7.4 0.1 reduce_window_sum.11
  7.5 0.1 copy.18
  7.6 0.0 copy-start.1
  7.6 0.1 eq.64
  7.7 0.1 fusion.18
  7.8 0.0 copy-done
  7.8 0.3 convolution_convert_fusion
  8.1 5.0 %all_to_all.10 = bf16[2,24,6144]{2,1,0:T(8,128)(2,1)} all-to-all(bf16[2,24,6144]{2,1,0:T(8,128)(2,1)S(1)} %bitcast.39), channel_id=1, replica_groups=mesh['groups'=2,'expert'=2,'tensor'=8] {'expert'}, dimensions={0} | all-to-all | bytes 1179648 | tf_op jit(solution)/shard_map/all_to_all | solution.py:33
  13.1 0.0 all-gather.2.cloned.1.call-update
  13.1 0.0 reduce-scatter.2.cloned.1.call-start
  13.1 82.7 %all-gather.2.cloned.1.call-done = bf16[384,6144]{1,0:T(8,128)(2,1)} async-done(((bf16[48,6144]{1,0:T(8,128)(2,1)}), bf16[384,6144]{1,0:T(8,128)(2,1)}) %all-gather.2.cloned.1.call-update) | async-done | bytes 4718608 | tf_op jit(solution)/shard_map/all_gather | solution.py:35
  95.8 9.4 %fusion.4 = f32[384,1024]{1,0:T(8,128)S(1)} fusion(bf16[384,6144]{1,0:T(8,128)(2,1)} %all-gather.2.cloned.1.call-done, bf16[1,6144,1024]{2,1,0:T(8,128)(2,1)} %param.9), kind=kOutput, calls=%fused_computation.4 | convolution fusion | flops 4831838208 | bytes 18874368 | tf_op jit(solution)/shard_map/dot_general | solution.py:36
  105.2 0.0 copy-done.3
  105.2 0.0 copy-done.1
  105.2 21.7 %fusion.6 = bf16[384,6144]{1,0:T(8,128)(2,1)} fusion(bf16[1,1024,6144]{2,1,0:T(8,128)(2,1)} %param.11, f32[384,1024]{1,0:T(8,128)S(1)} %fusion.4, bf16[384,6144]{1,0:T(8,128)(2,1)} %all-gather.2.cloned.1.call-done, bf16[1,6144,1024]{2,1,0:T(8,128)(2,1)} %param.10), kind=kOutput, calls=%fused_computation.6 | convolution fusion | flops 9668395008 | bytes 36175872 | tf_op jit(solution)/shard_map/dot_general | solution.py:40
  127.0 0.0 copy-start.5
  127.0 0.0 copy-start.6
  127.0 0.0 copy-start.2
  127.0 0.0 copy-start.4
  127.0 0.0 reduce-scatter.2.cloned.1.call-update
  127.0 0.6 copy-done.5
  127.6 0.0 copy-done.6
  127.7 92.9 %reduce-scatter.2.cloned.1.call-done = bf16[48,6144]{1,0:T(8,128)(2,1)} async-done(((bf16[384,6144]{1,0:T(8,128)(2,1)}), bf16[48,6144]{1,0:T(8,128)(2,1)}) %reduce-scatter.2.cloned.1.call-update) | async-done | bytes 589840 | tf_op jit(solution)/shard_map/reduce_scatter | solution.py:39
  220.5 5.3 %all_to_all.11 = bf16[2,24,6144]{2,1,0:T(8,128)(2,1)S(1)} all-to-all(bf16[2,24,6144]{2,1,0:T(8,128)(2,1)} %bitcast.40), channel_id=1, replica_groups=mesh['groups'=2,'expert'=2,'tensor'=8] {'expert'}, dimensions={0} | all-to-all | bytes 1179648 | tf_op jit(solution)/shard_map/all_to_all | solution.py:46
  225.8 0.0 copy-done.2
  225.8 0.0 copy-done.4
  225.8 1.3 fusion.9
  (4 shorter events, 0.0 us)
Async XLA Ops:
  6.5 1.2 copy-start
  6.5 89.3 %all-gather.2.cloned.1.call-start = ((), (), s32[]{:S(2)}) async-start(), calls=%async_computation.3 | async-start | bytes 5308416 | tf_op jit(solution)/shard_map/all_gather | solution.py:35
  7.3 97.9 %copy-start.3 = (pred[2,64]{1,0:T(4,128)(4,1)}, pred[2,64]{1,0:T(4,128)(4,1)S(1)}, u32[]{:S(2)}) copy-start(pred[2,64]{1,0:T(4,128)(4,1)S(1)} %get-tuple-element.5) | copy-start | bytes 388
  7.6 97.6 %copy-start.1 = (s32[2,64]{1,0:T(2,128)}, s32[2,64]{1,0:T(2,128)S(1)}, u32[]{:S(2)}) copy-start(s32[2,64]{1,0:T(2,128)S(1)} %subtract_bitcast_fusion) | copy-start | bytes 1540
  13.1 207.4 %reduce-scatter.2.cloned.1.call-start = ((), (), s32[]{:S(2)}) async-start(), calls=%async_computation.4 | async-start | bytes 5308416 | tf_op jit(solution)/shard_map/reduce_scatter | solution.py:39
  127.0 0.7 copy-start.5
  127.0 0.7 copy-start.6
  127.0 98.8 %copy-start.2 = (s32[2,64]{1,0:T(2,128)S(1)}, s32[2,64]{1,0:T(2,128)}, u32[]{:S(2)}) copy-start(s32[2,64]{1,0:T(2,128)} %copy-done.1) | copy-start | bytes 1540
  127.0 98.8 %copy-start.4 = (pred[2,64]{1,0:T(4,128)(4,1)S(1)}, pred[2,64]{1,0:T(4,128)(4,1)}, u32[]{:S(2)}) copy-start(pred[2,64]{1,0:T(4,128)(4,1)} %copy-done.3) | copy-start | bytes 388
Sparse Core Ops, SparseCore 0:
  13.2 82.5 all-gather.1
  127.1 93.3 reduce-scatter.1
where the time goes:
time: 234 us
  waiting for transfers between devices  176 us (75%)
  matrix products  32.7 us (14%)
  between operations  13.5 us (6%)
  blocking collectives  10.2 us (4%)
    reduce_scatter x1, waiting for transfers between devices, per_device(): lax.psum_scatter(jnp.dot(hidden, down_rows, preferred_element_type=jnp.fl...  92.9 us
    all_gather x1, waiting for transfers between devices, per_device(): piece = lax.all_gather(arrived_rows, 'tensor', axis=0, tiled=True)  82.7 us
    dot_general x1, matrix products, per_device(): jnp.dot(hidden, down_rows, preferred_element_type=jnp.float32)  21.7 us
    dot_general x1, matrix products, per_device(): gate_part = jnp.dot(piece, gate_cols, preferred_element_type=jnp.float32)  9.37 us
    all_to_all x1, blocking collectives, per_device(): lax.all_to_all(expert_out, 'expert', split_axis=0, concat_axis=0, tiled=T...  5.27 us
    all_to_all x1, blocking collectives, per_device(): lax.all_to_all(outgoing, 'expert', split_axis=0, concat_axis=0, tiled=True)  4.98 us
  transfers between devices with their start and end apart: 2, of which 2 were waited for; matrix products, arithmetic and copies ran while one was open for 0% of the time, Pallas kernels for 0%

commit v1 on v0

v1 whole, which is shorter than its diff:
```python
import jax
import jax.numpy as jnp
from jax import lax
from jax.sharding import PartitionSpec as P

CAP = 24
COLUMN_CHUNKS = 2


def ring_of(count):
    return list(range(0, count, 2)) + list(range(count - 1, 0, -2))


def routing(expert_ids, gate_probs, experts, slots):
    matches = expert_ids[:, :, None] == experts[None, None, :]
    member = jnp.any(matches, axis=1).astype(jnp.int32)
    weight = jnp.sum(jnp.where(matches, gate_probs[:, :, None], jnp.float32(0.0)), axis=1)
    slot_index = jnp.cumsum(member, axis=0) - member
    column = jnp.arange(slots)
    dispatch_map = (member[None, :, :] == 1) & (slot_index[None, :, :] == column[:, None, None])
    return (jnp.transpose(dispatch_map, (2, 0, 1)), weight)


def per_device(tokens, expert_ids, gate_probs, w_gate, w_up, w_down):
    n_tensor = lax.axis_size("tensor")
    model_width = tokens.shape[1]
    half = n_tensor // 2
    ring = ring_of(n_tensor)
    right = [(ring[i], ring[(i + 1) % n_tensor]) for i in range(n_tensor)]
    left = [(b, a) for a, b in right]
    swap = [(0, 1), (1, 0)]

    me = lax.axis_index("expert")
    experts = jnp.stack([me, 1 - me])
    dispatch_map, weight = routing(expert_ids, gate_probs, experts, CAP)
    outgoing = jnp.dot(
        dispatch_map.astype(jnp.bfloat16).reshape(2 * CAP, tokens.shape[0]),
        tokens,
        preferred_element_type=jnp.float32,
    ).astype(jnp.bfloat16)
    arrived = lax.ppermute(outgoing[CAP:], "expert", swap)
    own = jnp.concatenate([outgoing[:CAP], arrived], axis=0)

    width = model_width // COLUMN_CHUNKS
    gate_part = 0.0
    up_part = 0.0
    for c in range(COLUMN_CHUNKS):
        cols = slice(c * width, (c + 1) * width)
        block = own[:, cols]
        from_left = [block]
        from_right = [block]
        for _ in range(half - 1):
            from_left.append(lax.ppermute(from_left[-1], "tensor", right))
            from_right.append(lax.ppermute(from_right[-1], "tensor", left))
        far_a = lax.ppermute(from_left[-1][:CAP], "tensor", right)
        far_b = lax.ppermute(from_right[-1][CAP:], "tensor", left)
        rows = jnp.concatenate(from_left + from_right[1:] + [far_a, far_b], axis=0)
        gate_part += jnp.dot(rows, w_gate[0, cols], preferred_element_type=jnp.float32)
        up_part += jnp.dot(rows, w_up[0, cols], preferred_element_type=jnp.float32)
    hidden = (jax.nn.silu(gate_part) * up_part).astype(jnp.bfloat16)

    sums = []
    for c in range(COLUMN_CHUNKS):
        cols = slice(c * width, (c + 1) * width)
        part = jnp.dot(hidden, w_down[0][:, cols], preferred_element_type=jnp.float32).astype(jnp.bfloat16)
        part = part.reshape(n_tensor, 2 * CAP, width)
        to_left = [part[k] for k in range(half)]
        to_right = [part[0]] + [part[half + k] for k in range(half - 1)]
        far = part[n_tensor - 1]
        got_a = lax.ppermute(far[:CAP], "tensor", right)
        got_b = lax.ppermute(far[CAP:], "tensor", left)
        for k in range(half - 1, 0, -1):
            send_a = to_right[k].astype(jnp.float32)
            send_b = to_left[k].astype(jnp.float32)
            if k == half - 1:
                send_a = jnp.concatenate([send_a[:CAP] + got_a.astype(jnp.float32), send_a[CAP:]], axis=0)
                send_b = jnp.concatenate([send_b[:CAP], send_b[CAP:] + got_b.astype(jnp.float32)], axis=0)
            else:
                send_a = send_a + got_a.astype(jnp.float32)
                send_b = send_b + got_b.astype(jnp.float32)
            got_a = lax.ppermute(send_a.astype(jnp.bfloat16), "tensor", right)
            got_b = lax.ppermute(send_b.astype(jnp.bfloat16), "tensor", left)
        sums.append((part[0].astype(jnp.float32) + got_a.astype(jnp.float32) + got_b.astype(jnp.float32)).astype(jnp.bfloat16))
    expert_out = jnp.concatenate(sums, axis=1)
    returned = lax.ppermute(expert_out[CAP:], "expert", swap)
    returned = jnp.stack([expert_out[:CAP], returned])
    combine = dispatch_map.astype(jnp.float32) * jnp.transpose(weight)[:, None, :]
    mixed = jnp.einsum("wcr,wcd->rd", combine, returned.astype(jnp.float32))
    return mixed.astype(jnp.bfloat16)


def solution(mesh):
    in_specs = (
        P(("groups", "expert", "tensor"), None),
        P(("groups", "expert", "tensor"), None),
        P(("groups", "expert", "tensor"), None),
        P("expert", None, "tensor"),
        P("expert", None, "tensor"),
        P("expert", "tensor", None),
    )
    out_specs = P(("groups", "expert", "tensor"), None)
    return jax.shard_map(
        per_device, mesh=mesh, in_specs=in_specs, out_specs=out_specs, check_vma=False
    )
```

time: 234 us -> 131 us (0.56)
  waiting for transfers between devices: 176 us -> 70.5 us
  starting transfers between devices: 0.04 us -> 35.1 us
  between operations: 13.5 us -> 0.5 us
  matrix products: 32.7 us -> 21.1 us
  blocking collectives: 10.2 us -> 0 us
    reduce_scatter x1 -> x0, waiting for transfers between devices: 92.9 us -> none  [per_device(): lax.psum_scatter(jnp.dot(hidden, down_rows, preferred_element_type=jnp.fl...]
    all_gather x1 -> x0, waiting for transfers between devices: 82.7 us -> none  [per_device(): piece = lax.all_gather(arrived_rows, 'tensor', axis=0, tiled=True)]
    ppermute x0 -> x34, waiting for transfers between devices: none -> 70.5 us  [the longest x6 26.5 us: per_device(): from_right.append(lax.ppermute(from_right[-1], 'tensor', left))]
    ppermute x0 -> x34, starting transfers between devices: none -> 35.1 us  [the longest x6 12.8 us: per_device(): from_right.append(lax.ppermute(from_right[-1], 'tensor', left))]
    dot_general x3 -> x7, matrix products: 31.4 us -> 19.8 us  [the longest x2 8.65 us: per_device(): jnp.dot(hidden, w_down[0][:, cols], preferred_element_type=jnp.float32)]
    all_to_all x2 -> x0, blocking collectives: 10.2 us -> none  [the longest x1 5.27 us: per_device(): lax.all_to_all(expert_out, 'expert', split_axis=0, concat_axis=0, tiled=T...]
  transfers between devices with their start and end apart: 2 -> 34, of which waited for: 2 -> 20; matrix products, arithmetic and copies ran while one was open for 0% -> 5% of each run, Pallas kernels for 0% -> 0%
where the time goes in v1:
time: 131 us
  waiting for transfers between devices  70.5 us (54%)
  starting transfers between devices  35.1 us (27%)
  matrix products  21.1 us (16%)
  other arithmetic  2.35 us (2%)
  local copies, waits for them, and re-layouts  1.53 us (1%)
    ppermute x6, waiting for transfers between devices, per_device(): from_right.append(lax.ppermute(from_right[-1], 'tensor', left))  26.5 us
    ppermute x6, waiting for transfers between devices, per_device(): got_a = lax.ppermute(send_a.astype(jnp.bfloat16), 'tensor', right)  22.1 us
    ppermute x6, starting transfers between devices, per_device(): from_right.append(lax.ppermute(from_right[-1], 'tensor', left))  12.8 us
    ppermute x6, waiting for transfers between devices, per_device(): got_b = lax.ppermute(send_b.astype(jnp.bfloat16), 'tensor', left)  11.2 us
    ppermute x6, starting transfers between devices, per_device(): got_b = lax.ppermute(send_b.astype(jnp.bfloat16), 'tensor', left)  9.84 us
    dot_general x2, matrix products, per_device(): jnp.dot(hidden, w_down[0][:, cols], preferred_element_type=jnp.float32)  8.65 us
    dot_general x2, matrix products, per_device(): up_part += jnp.dot(rows, w_up[0, cols], preferred_element_type=jnp.float32)  5.54 us
    dot_general x2, matrix products, per_device(): jnp.dot(rows, w_gate[0, cols], preferred_element_type=jnp.float32)  5.31 us
  transfers between devices with their start and end apart: 34, of which 20 were waited for; matrix products, arithmetic and copies ran while one was open for 5% of the time, Pallas kernels for 0%

profile of v1, /device:TPU:0, one launch (start us, length us, event | category | flops | bytes accessed | tf_op | source)
XLA Modules:
  0.0 131.1 jit_solution(5005452158118424888)
XLA Ops:
  0.2 0.8 compare_reduce_fusion
  1.4 0.3 convolution_convert_fusion
  1.7 0.5 collective-permute-start
  2.3 1.2 collective-permute-done
  3.5 0.1 constant_dynamic-update-slice_fusion.8
  3.6 2.9 %collective-permute-start.4 = (bf16[48,3072]{1,0:T(8,128)(2,1)S(1)}, bf16[48,3072]{1,0:T(8,128)(2,1)S(1)}, u32[]{:S(2)}, u32[]{:S(2)}) collective-permute-start(bf16[48,3072]{1,0:T(8,128)(2,1)S(1)} %get-tuple-element.6), channel_id=1, source_target_pairs={{2,0},{4,2},{6,4},{7,6},{5,7},{3,5},{1,3},{0,1},{10,8},{12,10},{14... | collective-permute-start | bytes 884744 | tf_op jit(solution)/shard_map/ppermute | solution.py:54
  6.5 0.1 collective-permute-start.1
  6.7 1.9 %collective-permute-start.12 = (bf16[48,3072]{1,0:T(8,128)(2,1)S(1)}, bf16[48,3072]{1,0:T(8,128)(2,1)S(1)}, u32[]{:S(2)}, u32[]{:S(2)}) collective-permute-start(bf16[48,3072]{1,0:T(8,128)(2,1)S(1)} %get-tuple-element.28), channel_id=1, source_target_pairs={{2,0},{4,2},{6,4},{7,6},{5,7},{3,5},{1,3},{0,1},{10,8},{12,10},{14... | collective-permute-start | bytes 884744 | tf_op jit(solution)/shard_map/ppermute | solution.py:54
  8.6 0.1 collective-permute-start.9
  8.7 5.7 %collective-permute-done.4 = bf16[48,3072]{1,0:T(8,128)(2,1)S(1)} collective-permute-done((bf16[48,3072]{1,0:T(8,128)(2,1)S(1)}, bf16[48,3072]{1,0:T(8,128)(2,1)S(1)}, u32[]{:S(2)}, u32[]{:S(2)}) %collective-permute-start.4) | collective-permute-done | bytes 294944 | tf_op jit(solution)/shard_map/ppermute | solution.py:54
  14.4 2.0 %collective-permute-start.5 = (bf16[48,3072]{1,0:T(8,128)(2,1)S(1)}, bf16[48,3072]{1,0:T(8,128)(2,1)S(1)}, u32[]{:S(2)}, u32[]{:S(2)}) collective-permute-start(bf16[48,3072]{1,0:T(8,128)(2,1)S(1)} %collective-permute-done.4), channel_id=1, source_target_pairs={{2,0},{4,2},{6,4},{7,6},{5,7},{3,5},{1,3},{0,1},{10,8},{12,10},{14... | collective-permute-start | bytes 884744 | tf_op jit(solution)/shard_map/ppermute | solution.py:54
  16.5 4.2 %collective-permute-done.12 = bf16[48,3072]{1,0:T(8,128)(2,1)S(1)} collective-permute-done((bf16[48,3072]{1,0:T(8,128)(2,1)S(1)}, bf16[48,3072]{1,0:T(8,128)(2,1)S(1)}, u32[]{:S(2)}, u32[]{:S(2)}) %collective-permute-start.12) | collective-permute-done | bytes 294944 | tf_op jit(solution)/shard_map/ppermute | solution.py:54
  20.7 2.0 %collective-permute-start.13 = (bf16[48,3072]{1,0:T(8,128)(2,1)S(1)}, bf16[48,3072]{1,0:T(8,128)(2,1)S(1)}, u32[]{:S(2)}, u32[]{:S(2)}) collective-permute-start(bf16[48,3072]{1,0:T(8,128)(2,1)S(1)} %collective-permute-done.12), channel_id=1, source_target_pairs={{2,0},{4,2},{6,4},{7,6},{5,7},{3,5},{1,3},{0,1},{10,8},{12,10},{14... | collective-permute-start | bytes 884744 | tf_op jit(solution)/shard_map/ppermute | solution.py:54
  22.9 4.1 %collective-permute-done.5 = bf16[48,3072]{1,0:T(8,128)(2,1)S(1)} collective-permute-done((bf16[48,3072]{1,0:T(8,128)(2,1)S(1)}, bf16[48,3072]{1,0:T(8,128)(2,1)S(1)}, u32[]{:S(2)}, u32[]{:S(2)}) %collective-permute-start.5) | collective-permute-done | bytes 294944 | tf_op jit(solution)/shard_map/ppermute | solution.py:54
  27.0 2.0 %collective-permute-start.6 = (bf16[48,3072]{1,0:T(8,128)(2,1)S(1)}, bf16[48,3072]{1,0:T(8,128)(2,1)S(1)}, u32[]{:S(2)}, u32[]{:S(2)}) collective-permute-start(bf16[48,3072]{1,0:T(8,128)(2,1)S(1)} %collective-permute-done.5), channel_id=1, source_target_pairs={{2,0},{4,2},{6,4},{7,6},{5,7},{3,5},{1,3},{0,1},{10,8},{12,10},{14... | collective-permute-start | bytes 884744 | tf_op jit(solution)/shard_map/ppermute | solution.py:54
  29.1 4.2 %collective-permute-done.13 = bf16[48,3072]{1,0:T(8,128)(2,1)S(1)} collective-permute-done((bf16[48,3072]{1,0:T(8,128)(2,1)S(1)}, bf16[48,3072]{1,0:T(8,128)(2,1)S(1)}, u32[]{:S(2)}, u32[]{:S(2)}) %collective-permute-start.13) | collective-permute-done | bytes 294944 | tf_op jit(solution)/shard_map/ppermute | solution.py:54
  33.3 2.0 %collective-permute-start.14 = (bf16[48,3072]{1,0:T(8,128)(2,1)S(1)}, bf16[48,3072]{1,0:T(8,128)(2,1)S(1)}, u32[]{:S(2)}, u32[]{:S(2)}) collective-permute-start(bf16[48,3072]{1,0:T(8,128)(2,1)S(1)} %collective-permute-done.13), channel_id=1, source_target_pairs={{2,0},{4,2},{6,4},{7,6},{5,7},{3,5},{1,3},{0,1},{10,8},{12,10},{14... | collective-permute-start | bytes 884744 | tf_op jit(solution)/shard_map/ppermute | solution.py:54
  35.5 4.1 %collective-permute-done.6 = bf16[48,3072]{1,0:T(8,128)(2,1)S(1)} collective-permute-done((bf16[48,3072]{1,0:T(8,128)(2,1)S(1)}, bf16[48,3072]{1,0:T(8,128)(2,1)S(1)}, u32[]{:S(2)}, u32[]{:S(2)}) %collective-permute-start.6) | collective-permute-done | bytes 294944 | tf_op jit(solution)/shard_map/ppermute | solution.py:54
  39.7 2.1 %collective-permute-start.8 = (bf16[24,3072]{1,0:T(8,128)(2,1)S(1)}, bf16[24,3072]{1,0:T(8,128)(2,1)S(1)}, u32[]{:S(2)}, u32[]{:S(2)}) collective-permute-start(bf16[24,3072]{1,0:T(8,128)(2,1)S(1)} %slice.213), channel_id=1, source_target_pairs={{2,0},{4,2},{6,4},{7,6},{5,7},{3,5},{1,3},{0,1},{10,8},{12,10},{14... | collective-permute-start | bytes 442376 | tf_op jit(solution)/shard_map/ppermute | solution.py:56
  41.7 0.1 collective-permute-start.7
  41.9 4.1 %collective-permute-done.14 = bf16[48,3072]{1,0:T(8,128)(2,1)S(1)} collective-permute-done((bf16[48,3072]{1,0:T(8,128)(2,1)S(1)}, bf16[48,3072]{1,0:T(8,128)(2,1)S(1)}, u32[]{:S(2)}, u32[]{:S(2)}) %collective-permute-start.14) | collective-permute-done | bytes 294944 | tf_op jit(solution)/shard_map/ppermute | solution.py:54
  46.0 2.1 %collective-permute-start.16 = (bf16[24,3072]{1,0:T(8,128)(2,1)S(1)}, bf16[24,3072]{1,0:T(8,128)(2,1)S(1)}, u32[]{:S(2)}, u32[]{:S(2)}) collective-permute-start(bf16[24,3072]{1,0:T(8,128)(2,1)S(1)} %slice.215), channel_id=1, source_target_pairs={{2,0},{4,2},{6,4},{7,6},{5,7},{3,5},{1,3},{0,1},{10,8},{12,10},{14... | collective-permute-start | bytes 442376 | tf_op jit(solution)/shard_map/ppermute | solution.py:56
  48.1 0.3 collective-permute-start.15
  48.6 4.8 %collective-permute-done.15 = bf16[24,3072]{1,0:T(8,128)(2,1)S(1)} collective-permute-done((bf16[24,3072]{1,0:T(8,128)(2,1)S(1)}, bf16[24,3072]{1,0:T(8,128)(2,1)S(1)}, u32[]{:S(2)}, u32[]{:S(2)}) %collective-permute-start.15) | collective-permute-done | bytes 147488 | tf_op jit(solution)/shard_map/ppermute | solution.py:55
  53.5 2.7 %fusion.5 = f32[384,1024]{1,0:T(8,128)S(1)} fusion(bf16[384,3072]{1,0:T(8,128)(2,1)S(1)} %constant_dynamic-update-slice_fusion.9, bf16[1,6144,1024]{2,1,0:T(8,128)(2,1)S(1)} %copy-done.4), kind=kOutput, calls=%fused_computation.7 | convolution fusion | flops 2415919104 | bytes 10223616 | tf_op jit(solution)/shard_map/dot_general | solution.py:59
  56.2 0.8 slice-done.2
  57.0 2.7 %fusion.9 = f32[384,1024]{1,0:T(8,128)S(1)} fusion(bf16[384,3072]{1,0:T(8,128)(2,1)S(1)} %constant_dynamic-update-slice_fusion.9, bf16[1,6144,1024]{2,1,0:T(8,128)(2,1)S(1)} %bitcast.46), kind=kOutput, calls=%fused_computation.11 | convolution fusion | flops 2415919104 | bytes 10223616 | tf_op jit(solution)/shard_map/dot_general | solution.py:58
  59.7 2.6 %fusion.11 = f32[384,1024]{1,0:T(8,128)S(1)} fusion(bf16[384,3072]{1,0:T(8,128)(2,1)S(1)} %constant_dynamic-update-slice_fusion, bf16[1,6144,1024]{2,1,0:T(8,128)(2,1)S(1)} %bitcast.46), kind=kOutput, calls=%fused_computation.13 | convolution fusion | flops 2415919104 | bytes 10223616 | tf_op jit(solution)/shard_map/dot_general | solution.py:58
  62.4 2.9 %multiply_convert_fusion = bf16[384,1024]{1,0:T(8,128)(2,1)S(1)} fusion(f32[384,1024]{1,0:T(8,128)S(1)} %fusion.5, f32[384,1024]{1,0:T(8,128)S(1)} %fusion.11, f32[384,1024]{1,0:T(8,128)S(1)} %fusion.9, bf16[384,3072]{1,0:T(8,128)(2,1)S(1)} %constant_dynamic-update-slice_fusion, bf16[1,6144,1024]{2,1,0:T(8,128)(2,1)S(1)} %copy-done.4), kind=kOutput, calls=%fused_computation.21 | convolution fusion | flops 2419064832 | bytes 14155776 | tf_op jit(solution)/shard_map/dot_general | solution.py:59
  65.3 5.8 %fusion.20 = bf16[384,3072]{1,0:T(8,128)(2,1)S(1)} fusion(bf16[384,1024]{1,0:T(8,128)(2,1)S(1)} %multiply_convert_fusion, bf16[1024,6144]{1,0:T(8,128)(2,1)} %bitcast.47), kind=kOutput, calls=%fused_computation.20 | convolution fusion | flops 2417098752 | bytes 9437184 | tf_op jit(solution)/shard_map/dot_general | solution.py:65
  71.1 2.9 %fusion.17 = bf16[384,3072]{1,0:T(8,128)(2,1)S(1)} fusion(bf16[384,1024]{1,0:T(8,128)(2,1)S(1)} %multiply_convert_fusion, bf16[1024,6144]{1,0:T(8,128)(2,1)S(1)} %bitcast.50), kind=kOutput, calls=%fused_computation.19 | convolution fusion | flops 2417098752 | bytes 9437184 | tf_op jit(solution)/shard_map/dot_general | solution.py:65
  74.0 0.2 collective-permute-start.25
  74.3 1.8 %collective-permute-start.29 = (bf16[24,3072]{1,0:T(8,128)(2,1)S(1)}, bf16[24,3072]{1,0:T(8,128)(2,1)S(1)}, u32[]{:S(2)}, u32[]{:S(2)}) collective-permute-start(bf16[24,3072]{1,0:T(8,128)(2,1)S(1)} %get-tuple-element.22), channel_id=1, source_target_pairs={{2,0},{4,2},{6,4},{7,6},{5,7},{3,5},{1,3},{0,1},{10,8},{12,10},{14... | collective-permute-start | bytes 442376 | tf_op jit(solution)/shard_map/ppermute | solution.py:71
  76.2 0.2 collective-permute-start.17
  76.4 1.8 %collective-permute-start.21 = (bf16[24,3072]{1,0:T(8,128)(2,1)S(1)}, bf16[24,3072]{1,0:T(8,128)(2,1)S(1)}, u32[]{:S(2)}, u32[]{:S(2)}) collective-permute-start(bf16[24,3072]{1,0:T(8,128)(2,1)S(1)} %get-tuple-element.14), channel_id=1, source_target_pairs={{2,0},{4,2},{6,4},{7,6},{5,7},{3,5},{1,3},{0,1},{10,8},{12,10},{14... | collective-permute-start | bytes 442376 | tf_op jit(solution)/shard_map/ppermute | solution.py:71
  78.2 1.5 %collective-permute-done.25 = bf16[24,3072]{1,0:T(8,128)(2,1)S(1)} collective-permute-done((bf16[24,3072]{1,0:T(8,128)(2,1)S(1)}, bf16[24,3072]{1,0:T(8,128)(2,1)S(1)}, u32[]{:S(2)}, u32[]{:S(2)}) %collective-permute-start.25) | collective-permute-done | bytes 147488 | tf_op jit(solution)/shard_map/ppermute | solution.py:70
  79.7 0.7 collective-permute-done.29
  80.5 1.7 %collective-permute-start.30 = (bf16[48,3072]{1,0:T(8,128)(2,1)S(1)}, bf16[48,3072]{1,0:T(8,128)(2,1)S(1)}, u32[]{:S(2)}, u32[]{:S(2)}) collective-permute-start(bf16[48,3072]{1,0:T(8,128)(2,1)S(1)} %pad_maximum_fusion.5), channel_id=1, source_target_pairs={{2,0},{4,2},{6,4},{7,6},{5,7},{3,5},{1,3},{0,1},{10,8},{12,10},{14... | collective-permute-start | bytes 884744 | tf_op jit(solution)/shard_map/ppermute | solution.py:82
  82.2 0.4 collective-permute-start.26
  82.6 0.9 collective-permute-done.21
  83.6 1.7 %collective-permute-start.22 = (bf16[48,3072]{1,0:T(8,128)(2,1)S(1)}, bf16[48,3072]{1,0:T(8,128)(2,1)S(1)}, u32[]{:S(2)}, u32[]{:S(2)}) collective-permute-start(bf16[48,3072]{1,0:T(8,128)(2,1)S(1)} %pad_maximum_fusion.3), channel_id=1, source_target_pairs={{2,0},{4,2},{6,4},{7,6},{5,7},{3,5},{1,3},{0,1},{10,8},{12,10},{14... | collective-permute-start | bytes 884744 | tf_op jit(solution)/shard_map/ppermute | solution.py:82
  85.4 0.4 collective-permute-start.18
  85.8 6.4 %collective-permute-done.26 = bf16[48,3072]{1,0:T(8,128)(2,1)S(1)} collective-permute-done((bf16[48,3072]{1,0:T(8,128)(2,1)S(1)}, bf16[48,3072]{1,0:T(8,128)(2,1)S(1)}, u32[]{:S(2)}, u32[]{:S(2)}) %collective-permute-start.26) | collective-permute-done | bytes 294944 | tf_op jit(solution)/shard_map/ppermute | solution.py:81
  92.3 0.4 collective-permute-start.27
  92.7 5.8 %collective-permute-done.18 = bf16[48,3072]{1,0:T(8,128)(2,1)S(1)} collective-permute-done((bf16[48,3072]{1,0:T(8,128)(2,1)S(1)}, bf16[48,3072]{1,0:T(8,128)(2,1)S(1)}, u32[]{:S(2)}, u32[]{:S(2)}) %collective-permute-start.18) | collective-permute-done | bytes 294944 | tf_op jit(solution)/shard_map/ppermute | solution.py:81
  98.6 0.4 collective-permute-start.19
  99.0 5.8 %collective-permute-done.27 = bf16[48,3072]{1,0:T(8,128)(2,1)S(1)} collective-permute-done((bf16[48,3072]{1,0:T(8,128)(2,1)S(1)}, bf16[48,3072]{1,0:T(8,128)(2,1)S(1)}, u32[]{:S(2)}, u32[]{:S(2)}) %collective-permute-start.27) | collective-permute-done | bytes 294944 | tf_op jit(solution)/shard_map/ppermute | solution.py:81
  104.9 0.1 add_convert_fusion.3
  105.0 0.4 collective-permute-start.28
  105.4 1.7 %collective-permute-start.31 = (bf16[48,3072]{1,0:T(8,128)(2,1)S(1)}, bf16[48,3072]{1,0:T(8,128)(2,1)S(1)}, u32[]{:S(2)}, u32[]{:S(2)}) collective-permute-start(bf16[48,3072]{1,0:T(8,128)(2,1)S(1)} %get-tuple-element.18), channel_id=1, source_target_pairs={{2,0},{4,2},{6,4},{7,6},{5,7},{3,5},{1,3},{0,1},{10,8},{12,10},{14... | collective-permute-start | bytes 884744 | tf_op jit(solution)/shard_map/ppermute | solution.py:82
  107.1 4.1 %collective-permute-done.19 = bf16[48,3072]{1,0:T(8,128)(2,1)S(1)} collective-permute-done((bf16[48,3072]{1,0:T(8,128)(2,1)S(1)}, bf16[48,3072]{1,0:T(8,128)(2,1)S(1)}, u32[]{:S(2)}, u32[]{:S(2)}) %collective-permute-start.19) | collective-permute-done | bytes 294944 | tf_op jit(solution)/shard_map/ppermute | solution.py:81
  111.2 0.2 add_convert_fusion.8
  111.3 0.4 collective-permute-start.20
  111.8 1.7 %collective-permute-start.23 = (bf16[48,3072]{1,0:T(8,128)(2,1)S(1)}, bf16[48,3072]{1,0:T(8,128)(2,1)S(1)}, u32[]{:S(2)}, u32[]{:S(2)}) collective-permute-start(bf16[48,3072]{1,0:T(8,128)(2,1)S(1)} %get-tuple-element.10), channel_id=1, source_target_pairs={{2,0},{4,2},{6,4},{7,6},{5,7},{3,5},{1,3},{0,1},{10,8},{12,10},{14... | collective-permute-start | bytes 884744 | tf_op jit(solution)/shard_map/ppermute | solution.py:82
  113.4 2.0 %collective-permute-done.31 = bf16[48,3072]{1,0:T(8,128)(2,1)S(1)} collective-permute-done((bf16[48,3072]{1,0:T(8,128)(2,1)S(1)}, bf16[48,3072]{1,0:T(8,128)(2,1)S(1)}, u32[]{:S(2)}, u32[]{:S(2)}) %collective-permute-start.31) | collective-permute-done | bytes 294944 | tf_op jit(solution)/shard_map/ppermute | solution.py:82
  115.5 1.7 %collective-permute-start.32 = (bf16[48,3072]{1,0:T(8,128)(2,1)S(1)}, bf16[48,3072]{1,0:T(8,128)(2,1)S(1)}, u32[]{:S(2)}, u32[]{:S(2)}) collective-permute-start(bf16[48,3072]{1,0:T(8,128)(2,1)S(1)} %add_convert_fusion.1), channel_id=1, source_target_pairs={{2,0},{4,2},{6,4},{7,6},{5,7},{3,5},{1,3},{0,1},{10,8},{12,10},{14... | collective-permute-start | bytes 884744 | tf_op jit(solution)/shard_map/ppermute | solution.py:82
  117.2 4.0 %collective-permute-done.23 = bf16[48,3072]{1,0:T(8,128)(2,1)S(1)} collective-permute-done((bf16[48,3072]{1,0:T(8,128)(2,1)S(1)}, bf16[48,3072]{1,0:T(8,128)(2,1)S(1)}, u32[]{:S(2)}, u32[]{:S(2)}) %collective-permute-start.23) | collective-permute-done | bytes 294944 | tf_op jit(solution)/shard_map/ppermute | solution.py:82
  121.3 1.4 %collective-permute-start.24 = (bf16[48,3072]{1,0:T(8,128)(2,1)S(1)}, bf16[48,3072]{1,0:T(8,128)(2,1)S(1)}, u32[]{:S(2)}, u32[]{:S(2)}) collective-permute-start(bf16[48,3072]{1,0:T(8,128)(2,1)S(1)} %add_convert_fusion.6), channel_id=1, source_target_pairs={{2,0},{4,2},{6,4},{7,6},{5,7},{3,5},{1,3},{0,1},{10,8},{12,10},{14... | collective-permute-start | bytes 884744 | tf_op jit(solution)/shard_map/ppermute | solution.py:82
  122.7 1.7 %collective-permute-done.32 = bf16[48,3072]{1,0:T(8,128)(2,1)S(1)} collective-permute-done((bf16[48,3072]{1,0:T(8,128)(2,1)S(1)}, bf16[48,3072]{1,0:T(8,128)(2,1)S(1)}, u32[]{:S(2)}, u32[]{:S(2)}) %collective-permute-start.32) | collective-permute-done | bytes 294944 | tf_op jit(solution)/shard_map/ppermute | solution.py:82
  124.3 0.1 add_convert_fusion
  124.5 3.6 %collective-permute-done.24 = bf16[48,3072]{1,0:T(8,128)(2,1)S(1)} collective-permute-done((bf16[48,3072]{1,0:T(8,128)(2,1)S(1)}, bf16[48,3072]{1,0:T(8,128)(2,1)S(1)}, u32[]{:S(2)}, u32[]{:S(2)}) %collective-permute-start.24) | collective-permute-done | bytes 294944 | tf_op jit(solution)/shard_map/ppermute | solution.py:82
  128.0 0.1 add_convert_fusion.5
  128.4 1.5 %collective-permute-done.33 = bf16[24,6144]{1,0:T(8,128)(2,1)S(1)} collective-permute-done((bf16[24,6144]{1,0:T(8,128)(2,1)S(1)}, bf16[24,6144]{1,0:T(8,128)(2,1)S(1)}, u32[]{:S(2)}, u32[]{:S(2)}) %collective-permute-start.33) | collective-permute-done | bytes 294944 | tf_op jit(solution)/shard_map/ppermute | solution.py:85
  129.8 1.3 fusion
  (86 shorter events, 2.3 us)
Async XLA Ops:
  0.0 1.4 %copy-start = (bf16[64,6144]{1,0:T(8,128)(2,1)S(1)}, bf16[64,6144]{1,0:T(8,128)(2,1)}, u32[]{:S(2)}) copy-start(bf16[64,6144]{1,0:T(8,128)(2,1)} %param.6) | copy-start | bytes 2359300
  1.4 52.1 %copy-start.4 = (bf16[1,6144,1024]{2,1,0:T(8,128)(2,1)S(1)}, bf16[1,6144,1024]{2,1,0:T(8,128)(2,1)}, u32[]{:S(2)}) copy-start(bf16[1,6144,1024]{2,1,0:T(8,128)(2,1)} %param.10) | copy-start | bytes 37748740
  1.7 1.7 %collective-permute-start = (bf16[24,6144]{1,0:T(8,128)(2,1)S(1)}, bf16[24,6144]{1,0:T(8,128)(2,1)S(1)}, u32[]{:S(2)}, u32[]{:S(2)}) collective-permute-start(bf16[24,6144]{1,0:T(8,128)(2,1)S(1)} %get-tuple-element.30), channel_id=1, source_target_pairs={{0,8},{8,0},{1,9},{9,1},{2,10},{10,2},{3,11},{11,3},{4,12},{12,4},... | collective-permute-start | bytes 884744 | tf_op jit(solution)/shard_map/ppermute | solution.py:41
  3.6 10.8 %collective-permute-start.4 = (bf16[48,3072]{1,0:T(8,128)(2,1)S(1)}, bf16[48,3072]{1,0:T(8,128)(2,1)S(1)}, u32[]{:S(2)}, u32[]{:S(2)}) collective-permute-start(bf16[48,3072]{1,0:T(8,128)(2,1)S(1)} %get-tuple-element.6), channel_id=1, source_target_pairs={{2,0},{4,2},{6,4},{7,6},{5,7},{3,5},{1,3},{0,1},{10,8},{12,10},{14... | collective-permute-start | bytes 884744 | tf_op jit(solution)/shard_map/ppermute | solution.py:54
  6.5 9.9 %collective-permute-start.1 = (bf16[48,3072]{1,0:T(8,128)(2,1)S(1)}, bf16[48,3072]{1,0:T(8,128)(2,1)S(1)}, u32[]{:S(2)}, u32[]{:S(2)}) collective-permute-start(bf16[48,3072]{1,0:T(8,128)(2,1)S(1)} %get-tuple-element.6), channel_id=1, source_target_pairs={{0,2},{2,4},{4,6},{6,7},{7,5},{5,3},{3,1},{1,0},{8,10},{10,12},{12... | collective-permute-start | bytes 884744 | tf_op jit(solution)/shard_map/ppermute | solution.py:53
  6.7 14.0 %collective-permute-start.12 = (bf16[48,3072]{1,0:T(8,128)(2,1)S(1)}, bf16[48,3072]{1,0:T(8,128)(2,1)S(1)}, u32[]{:S(2)}, u32[]{:S(2)}) collective-permute-start(bf16[48,3072]{1,0:T(8,128)(2,1)S(1)} %get-tuple-element.28), channel_id=1, source_target_pairs={{2,0},{4,2},{6,4},{7,6},{5,7},{3,5},{1,3},{0,1},{10,8},{12,10},{14... | collective-permute-start | bytes 884744 | tf_op jit(solution)/shard_map/ppermute | solution.py:54
  8.6 14.2 %collective-permute-start.9 = (bf16[48,3072]{1,0:T(8,128)(2,1)S(1)}, bf16[48,3072]{1,0:T(8,128)(2,1)S(1)}, u32[]{:S(2)}, u32[]{:S(2)}) collective-permute-start(bf16[48,3072]{1,0:T(8,128)(2,1)S(1)} %get-tuple-element.28), channel_id=1, source_target_pairs={{0,2},{2,4},{4,6},{6,7},{7,5},{5,3},{3,1},{1,0},{8,10},{10,12},{12... | collective-permute-start | bytes 884744 | tf_op jit(solution)/shard_map/ppermute | solution.py:53
  14.4 12.6 %collective-permute-start.5 = (bf16[48,3072]{1,0:T(8,128)(2,1)S(1)}, bf16[48,3072]{1,0:T(8,128)(2,1)S(1)}, u32[]{:S(2)}, u32[]{:S(2)}) collective-permute-start(bf16[48,3072]{1,0:T(8,128)(2,1)S(1)} %collective-permute-done.4), channel_id=1, source_target_pairs={{2,0},{4,2},{6,4},{7,6},{5,7},{3,5},{1,3},{0,1},{10,8},{12,10},{14... | collective-permute-start | bytes 884744 | tf_op jit(solution)/shard_map/ppermute | solution.py:54
  16.4 12.6 %collective-permute-start.2 = (bf16[48,3072]{1,0:T(8,128)(2,1)S(1)}, bf16[48,3072]{1,0:T(8,128)(2,1)S(1)}, u32[]{:S(2)}, u32[]{:S(2)}) collective-permute-start(bf16[48,3072]{1,0:T(8,128)(2,1)S(1)} %collective-permute-done.1), channel_id=1, source_target_pairs={{0,2},{2,4},{4,6},{6,7},{7,5},{5,3},{3,1},{1,0},{8,10},{10,12},{12... | collective-permute-start | bytes 884744 | tf_op jit(solution)/shard_map/ppermute | solution.py:53
  20.7 12.6 %collective-permute-start.13 = (bf16[48,3072]{1,0:T(8,128)(2,1)S(1)}, bf16[48,3072]{1,0:T(8,128)(2,1)S(1)}, u32[]{:S(2)}, u32[]{:S(2)}) collective-permute-start(bf16[48,3072]{1,0:T(8,128)(2,1)S(1)} %collective-permute-done.12), channel_id=1, source_target_pairs={{2,0},{4,2},{6,4},{7,6},{5,7},{3,5},{1,3},{0,1},{10,8},{12,10},{14... | collective-permute-start | bytes 884744 | tf_op jit(solution)/shard_map/ppermute | solution.py:54
  22.7 12.6 %collective-permute-start.10 = (bf16[48,3072]{1,0:T(8,128)(2,1)S(1)}, bf16[48,3072]{1,0:T(8,128)(2,1)S(1)}, u32[]{:S(2)}, u32[]{:S(2)}) collective-permute-start(bf16[48,3072]{1,0:T(8,128)(2,1)S(1)} %collective-permute-done.9), channel_id=1, source_target_pairs={{0,2},{2,4},{4,6},{6,7},{7,5},{5,3},{3,1},{1,0},{8,10},{10,12},{12... | collective-permute-start | bytes 884744 | tf_op jit(solution)/shard_map/ppermute | solution.py:53
  27.0 12.6 %collective-permute-start.6 = (bf16[48,3072]{1,0:T(8,128)(2,1)S(1)}, bf16[48,3072]{1,0:T(8,128)(2,1)S(1)}, u32[]{:S(2)}, u32[]{:S(2)}) collective-permute-start(bf16[48,3072]{1,0:T(8,128)(2,1)S(1)} %collective-permute-done.5), channel_id=1, source_target_pairs={{2,0},{4,2},{6,4},{7,6},{5,7},{3,5},{1,3},{0,1},{10,8},{12,10},{14... | collective-permute-start | bytes 884744 | tf_op jit(solution)/shard_map/ppermute | solution.py:54
  29.1 12.7 %collective-permute-start.3 = (bf16[48,3072]{1,0:T(8,128)(2,1)S(1)}, bf16[48,3072]{1,0:T(8,128)(2,1)S(1)}, u32[]{:S(2)}, u32[]{:S(2)}) collective-permute-start(bf16[48,3072]{1,0:T(8,128)(2,1)S(1)} %collective-permute-done.2), channel_id=1, source_target_pairs={{0,2},{2,4},{4,6},{6,7},{7,5},{5,3},{3,1},{1,0},{8,10},{10,12},{12... | collective-permute-start | bytes 884744 | tf_op jit(solution)/shard_map/ppermute | solution.py:53
  33.3 12.6 %collective-permute-start.14 = (bf16[48,3072]{1,0:T(8,128)(2,1)S(1)}, bf16[48,3072]{1,0:T(8,128)(2,1)S(1)}, u32[]{:S(2)}, u32[]{:S(2)}) collective-permute-start(bf16[48,3072]{1,0:T(8,128)(2,1)S(1)} %collective-permute-done.13), channel_id=1, source_target_pairs={{2,0},{4,2},{6,4},{7,6},{5,7},{3,5},{1,3},{0,1},{10,8},{12,10},{14... | collective-permute-start | bytes 884744 | tf_op jit(solution)/shard_map/ppermute | solution.py:54
  35.4 12.7 %collective-permute-start.11 = (bf16[48,3072]{1,0:T(8,128)(2,1)S(1)}, bf16[48,3072]{1,0:T(8,128)(2,1)S(1)}, u32[]{:S(2)}, u32[]{:S(2)}) collective-permute-start(bf16[48,3072]{1,0:T(8,128)(2,1)S(1)} %collective-permute-done.10), channel_id=1, source_target_pairs={{0,2},{2,4},{4,6},{6,7},{7,5},{5,3},{3,1},{1,0},{8,10},{10,12},{12... | collective-permute-start | bytes 884744 | tf_op jit(solution)/shard_map/ppermute | solution.py:53
  39.7 20.0 %collective-permute-start.8 = (bf16[24,3072]{1,0:T(8,128)(2,1)S(1)}, bf16[24,3072]{1,0:T(8,128)(2,1)S(1)}, u32[]{:S(2)}, u32[]{:S(2)}) collective-permute-start(bf16[24,3072]{1,0:T(8,128)(2,1)S(1)} %slice.213), channel_id=1, source_target_pairs={{2,0},{4,2},{6,4},{7,6},{5,7},{3,5},{1,3},{0,1},{10,8},{12,10},{14... | collective-permute-start | bytes 442376 | tf_op jit(solution)/shard_map/ppermute | solution.py:56
  41.7 17.9 %collective-permute-start.7 = (bf16[24,3072]{1,0:T(8,128)(2,1)S(1)}, bf16[24,3072]{1,0:T(8,128)(2,1)S(1)}, u32[]{:S(2)}, u32[]{:S(2)}) collective-permute-start(bf16[24,3072]{1,0:T(8,128)(2,1)S(1)} %slice.212), channel_id=1, source_target_pairs={{0,2},{2,4},{4,6},{6,7},{7,5},{5,3},{3,1},{1,0},{8,10},{10,12},{12... | collective-permute-start | bytes 442376 | tf_op jit(solution)/shard_map/ppermute | solution.py:55
  46.0 10.2 %slice-start = ((s8[12582912]{0:T(1024)(128)(4,1)}), s8[4194304]{0:T(1024)(128)(4,1)S(1)}, s32[]{:S(2)}) async-start(s8[12582912]{0:T(1024)(128)(4,1)} %bitcast.45), calls=%async_computation | async-start | bytes 8388608
  46.0 7.5 %collective-permute-start.16 = (bf16[24,3072]{1,0:T(8,128)(2,1)S(1)}, bf16[24,3072]{1,0:T(8,128)(2,1)S(1)}, u32[]{:S(2)}, u32[]{:S(2)}) collective-permute-start(bf16[24,3072]{1,0:T(8,128)(2,1)S(1)} %slice.215), channel_id=1, source_target_pairs={{2,0},{4,2},{6,4},{7,6},{5,7},{3,5},{1,3},{0,1},{10,8},{12,10},{14... | collective-permute-start | bytes 442376 | tf_op jit(solution)/shard_map/ppermute | solution.py:56
  48.1 5.4 %collective-permute-start.15 = (bf16[24,3072]{1,0:T(8,128)(2,1)S(1)}, bf16[24,3072]{1,0:T(8,128)(2,1)S(1)}, u32[]{:S(2)}, u32[]{:S(2)}) collective-permute-start(bf16[24,3072]{1,0:T(8,128)(2,1)S(1)} %slice.214), channel_id=1, source_target_pairs={{0,2},{2,4},{4,6},{6,7},{7,5},{5,3},{3,1},{1,0},{8,10},{10,12},{12... | collective-permute-start | bytes 442376 | tf_op jit(solution)/shard_map/ppermute | solution.py:55
  53.5 2.7 %slice-start.1 = ((s8[12582912]{0:T(1024)(128)(4,1)}), s8[4194304]{0:T(1024)(128)(4,1)S(1)}, s32[]{:S(2)}) async-start(s8[12582912]{0:T(1024)(128)(4,1)} %bitcast.45), calls=%async_computation.1 | async-start | bytes 8388608
  53.5 3.5 %slice-start.2 = ((s8[12582912]{0:T(1024)(128)(4,1)}), s8[4194304]{0:T(1024)(128)(4,1)S(1)}, s32[]{:S(2)}) async-start(s8[12582912]{0:T(1024)(128)(4,1)} %bitcast.45), calls=%async_computation.2 | async-start | bytes 8388608
  62.4 8.7 %slice-start.3 = ((s8[12582912]{0:T(1024)(128)(4,1)}), s8[4194304]{0:T(1024)(128)(4,1)S(1)}, s32[]{:S(2)}) async-start(s8[12582912]{0:T(1024)(128)(4,1)} %bitcast.48), calls=%async_computation.3 | async-start | bytes 8388608
  62.4 8.7 %slice-start.4 = ((s8[12582912]{0:T(1024)(128)(4,1)}), s8[4194304]{0:T(1024)(128)(4,1)S(1)}, s32[]{:S(2)}) async-start(s8[12582912]{0:T(1024)(128)(4,1)} %bitcast.48), calls=%async_computation.4 | async-start | bytes 8388608
  65.3 5.8 %slice-start.5 = ((s8[12582912]{0:T(1024)(128)(4,1)}), s8[4194304]{0:T(1024)(128)(4,1)S(1)}, s32[]{:S(2)}) async-start(s8[12582912]{0:T(1024)(128)(4,1)} %bitcast.48), calls=%async_computation.5 | async-start | bytes 8388608
  74.0 5.7 %collective-permute-start.25 = (bf16[24,3072]{1,0:T(8,128)(2,1)S(1)}, bf16[24,3072]{1,0:T(8,128)(2,1)S(1)}, u32[]{:S(2)}, u32[]{:S(2)}) collective-permute-start(bf16[24,3072]{1,0:T(8,128)(2,1)S(1)} %get-tuple-element.21), channel_id=1, source_target_pairs={{0,2},{2,4},{4,6},{6,7},{7,5},{5,3},{3,1},{1,0},{8,10},{10,12},{12... | collective-permute-start | bytes 442376 | tf_op jit(solution)/shard_map/ppermute | solution.py:70
  74.3 6.1 %collective-permute-start.29 = (bf16[24,3072]{1,0:T(8,128)(2,1)S(1)}, bf16[24,3072]{1,0:T(8,128)(2,1)S(1)}, u32[]{:S(2)}, u32[]{:S(2)}) collective-permute-start(bf16[24,3072]{1,0:T(8,128)(2,1)S(1)} %get-tuple-element.22), channel_id=1, source_target_pairs={{2,0},{4,2},{6,4},{7,6},{5,7},{3,5},{1,3},{0,1},{10,8},{12,10},{14... | collective-permute-start | bytes 442376 | tf_op jit(solution)/shard_map/ppermute | solution.py:71
  76.2 6.5 %collective-permute-start.17 = (bf16[24,3072]{1,0:T(8,128)(2,1)S(1)}, bf16[24,3072]{1,0:T(8,128)(2,1)S(1)}, u32[]{:S(2)}, u32[]{:S(2)}) collective-permute-start(bf16[24,3072]{1,0:T(8,128)(2,1)S(1)} %get-tuple-element.13), channel_id=1, source_target_pairs={{0,2},{2,4},{4,6},{6,7},{7,5},{5,3},{3,1},{1,0},{8,10},{10,12},{12... | collective-permute-start | bytes 442376 | tf_op jit(solution)/shard_map/ppermute | solution.py:70
  76.4 7.2 %collective-permute-start.21 = (bf16[24,3072]{1,0:T(8,128)(2,1)S(1)}, bf16[24,3072]{1,0:T(8,128)(2,1)S(1)}, u32[]{:S(2)}, u32[]{:S(2)}) collective-permute-start(bf16[24,3072]{1,0:T(8,128)(2,1)S(1)} %get-tuple-element.14), channel_id=1, source_target_pairs={{2,0},{4,2},{6,4},{7,6},{5,7},{3,5},{1,3},{0,1},{10,8},{12,10},{14... | collective-permute-start | bytes 442376 | tf_op jit(solution)/shard_map/ppermute | solution.py:71
  80.5 18.6 %collective-permute-start.30 = (bf16[48,3072]{1,0:T(8,128)(2,1)S(1)}, bf16[48,3072]{1,0:T(8,128)(2,1)S(1)}, u32[]{:S(2)}, u32[]{:S(2)}) collective-permute-start(bf16[48,3072]{1,0:T(8,128)(2,1)S(1)} %pad_maximum_fusion.5), channel_id=1, source_target_pairs={{2,0},{4,2},{6,4},{7,6},{5,7},{3,5},{1,3},{0,1},{10,8},{12,10},{14... | collective-permute-start | bytes 884744 | tf_op jit(solution)/shard_map/ppermute | solution.py:82
  82.2 10.0 %collective-permute-start.26 = (bf16[48,3072]{1,0:T(8,128)(2,1)S(1)}, bf16[48,3072]{1,0:T(8,128)(2,1)S(1)}, u32[]{:S(2)}, u32[]{:S(2)}) collective-permute-start(bf16[48,3072]{1,0:T(8,128)(2,1)S(1)} %pad_maximum_fusion.4), channel_id=1, source_target_pairs={{0,2},{2,4},{4,6},{6,7},{7,5},{5,3},{3,1},{1,0},{8,10},{10,12},{12... | collective-permute-start | bytes 884744 | tf_op jit(solution)/shard_map/ppermute | solution.py:81
  83.6 23.4 %collective-permute-start.22 = (bf16[48,3072]{1,0:T(8,128)(2,1)S(1)}, bf16[48,3072]{1,0:T(8,128)(2,1)S(1)}, u32[]{:S(2)}, u32[]{:S(2)}) collective-permute-start(bf16[48,3072]{1,0:T(8,128)(2,1)S(1)} %pad_maximum_fusion.3), channel_id=1, source_target_pairs={{2,0},{4,2},{6,4},{7,6},{5,7},{3,5},{1,3},{0,1},{10,8},{12,10},{14... | collective-permute-start | bytes 884744 | tf_op jit(solution)/shard_map/ppermute | solution.py:82
  85.4 13.2 %collective-permute-start.18 = (bf16[48,3072]{1,0:T(8,128)(2,1)S(1)}, bf16[48,3072]{1,0:T(8,128)(2,1)S(1)}, u32[]{:S(2)}, u32[]{:S(2)}) collective-permute-start(bf16[48,3072]{1,0:T(8,128)(2,1)S(1)} %pad_maximum_fusion.2), channel_id=1, source_target_pairs={{0,2},{2,4},{4,6},{6,7},{7,5},{5,3},{3,1},{1,0},{8,10},{10,12},{12... | collective-permute-start | bytes 884744 | tf_op jit(solution)/shard_map/ppermute | solution.py:81
  92.3 12.6 %collective-permute-start.27 = (bf16[48,3072]{1,0:T(8,128)(2,1)S(1)}, bf16[48,3072]{1,0:T(8,128)(2,1)S(1)}, u32[]{:S(2)}, u32[]{:S(2)}) collective-permute-start(bf16[48,3072]{1,0:T(8,128)(2,1)S(1)} %add_convert_fusion.4), channel_id=1, source_target_pairs={{0,2},{2,4},{4,6},{6,7},{7,5},{5,3},{3,1},{1,0},{8,10},{10,12},{12... | collective-permute-start | bytes 884744 | tf_op jit(solution)/shard_map/ppermute | solution.py:81
  98.6 12.6 %collective-permute-start.19 = (bf16[48,3072]{1,0:T(8,128)(2,1)S(1)}, bf16[48,3072]{1,0:T(8,128)(2,1)S(1)}, u32[]{:S(2)}, u32[]{:S(2)}) collective-permute-start(bf16[48,3072]{1,0:T(8,128)(2,1)S(1)} %add_convert_fusion.9), channel_id=1, source_target_pairs={{0,2},{2,4},{4,6},{6,7},{7,5},{5,3},{3,1},{1,0},{8,10},{10,12},{12... | collective-permute-start | bytes 884744 | tf_op jit(solution)/shard_map/ppermute | solution.py:81
  105.0 17.7 %collective-permute-start.28 = (bf16[48,3072]{1,0:T(8,128)(2,1)S(1)}, bf16[48,3072]{1,0:T(8,128)(2,1)S(1)}, u32[]{:S(2)}, u32[]{:S(2)}) collective-permute-start(bf16[48,3072]{1,0:T(8,128)(2,1)S(1)} %get-tuple-element.17), channel_id=1, source_target_pairs={{0,2},{2,4},{4,6},{6,7},{7,5},{5,3},{3,1},{1,0},{8,10},{10,12},{12... | collective-permute-start | bytes 884744 | tf_op jit(solution)/shard_map/ppermute | solution.py:81
  105.4 9.9 %collective-permute-start.31 = (bf16[48,3072]{1,0:T(8,128)(2,1)S(1)}, bf16[48,3072]{1,0:T(8,128)(2,1)S(1)}, u32[]{:S(2)}, u32[]{:S(2)}) collective-permute-start(bf16[48,3072]{1,0:T(8,128)(2,1)S(1)} %get-tuple-element.18), channel_id=1, source_target_pairs={{2,0},{4,2},{6,4},{7,6},{5,7},{3,5},{1,3},{0,1},{10,8},{12,10},{14... | collective-permute-start | bytes 884744 | tf_op jit(solution)/shard_map/ppermute | solution.py:82
  111.3 13.1 %collective-permute-start.20 = (bf16[48,3072]{1,0:T(8,128)(2,1)S(1)}, bf16[48,3072]{1,0:T(8,128)(2,1)S(1)}, u32[]{:S(2)}, u32[]{:S(2)}) collective-permute-start(bf16[48,3072]{1,0:T(8,128)(2,1)S(1)} %get-tuple-element.9), channel_id=1, source_target_pairs={{0,2},{2,4},{4,6},{6,7},{7,5},{5,3},{3,1},{1,0},{8,10},{10,12},{12... | collective-permute-start | bytes 884744 | tf_op jit(solution)/shard_map/ppermute | solution.py:81
  111.8 9.4 %collective-permute-start.23 = (bf16[48,3072]{1,0:T(8,128)(2,1)S(1)}, bf16[48,3072]{1,0:T(8,128)(2,1)S(1)}, u32[]{:S(2)}, u32[]{:S(2)}) collective-permute-start(bf16[48,3072]{1,0:T(8,128)(2,1)S(1)} %get-tuple-element.10), channel_id=1, source_target_pairs={{2,0},{4,2},{6,4},{7,6},{5,7},{3,5},{1,3},{0,1},{10,8},{12,10},{14... | collective-permute-start | bytes 884744 | tf_op jit(solution)/shard_map/ppermute | solution.py:82
  115.4 12.8 %copy-start.2 = (s32[64,2]{0,1:T(2,128)S(1)}, s32[64,2]{0,1:T(2,128)}, u32[]{:S(2)}) copy-start(s32[64,2]{0,1:T(2,128)} %param.7) | copy-start | bytes 1540
  115.5 12.8 %copy-start.3 = (f32[64,2]{0,1:T(2,128)S(1)}, f32[64,2]{0,1:T(2,128)}, u32[]{:S(2)}) copy-start(f32[64,2]{0,1:T(2,128)} %param.8) | copy-start | bytes 1540
  115.5 8.9 %collective-permute-start.32 = (bf16[48,3072]{1,0:T(8,128)(2,1)S(1)}, bf16[48,3072]{1,0:T(8,128)(2,1)S(1)}, u32[]{:S(2)}, u32[]{:S(2)}) collective-permute-start(bf16[48,3072]{1,0:T(8,128)(2,1)S(1)} %add_convert_fusion.1), channel_id=1, source_target_pairs={{2,0},{4,2},{6,4},{7,6},{5,7},{3,5},{1,3},{0,1},{10,8},{12,10},{14... | collective-permute-start | bytes 884744 | tf_op jit(solution)/shard_map/ppermute | solution.py:82
  121.2 10.0 %copy-start.1 = (bf16[64,6144]{1,0:T(8,128)(2,1)S(1)}, bf16[64,6144]{1,0:T(8,128)(2,1)}, u32[]{:S(2)}) copy-start(bf16[64,6144]{1,0:T(8,128)(2,1)} %param.6) | copy-start | bytes 2359300
  121.3 6.8 %collective-permute-start.24 = (bf16[48,3072]{1,0:T(8,128)(2,1)S(1)}, bf16[48,3072]{1,0:T(8,128)(2,1)S(1)}, u32[]{:S(2)}, u32[]{:S(2)}) collective-permute-start(bf16[48,3072]{1,0:T(8,128)(2,1)S(1)} %add_convert_fusion.6), channel_id=1, source_target_pairs={{2,0},{4,2},{6,4},{7,6},{5,7},{3,5},{1,3},{0,1},{10,8},{12,10},{14... | collective-permute-start | bytes 884744 | tf_op jit(solution)/shard_map/ppermute | solution.py:82
  128.2 1.6 %collective-permute-start.33 = (bf16[24,6144]{1,0:T(8,128)(2,1)S(1)}, bf16[24,6144]{1,0:T(8,128)(2,1)S(1)}, u32[]{:S(2)}, u32[]{:S(2)}) collective-permute-start(bf16[24,6144]{1,0:T(8,128)(2,1)S(1)} %get-tuple-element.26), channel_id=1, source_target_pairs={{0,8},{8,0},{1,9},{9,1},{2,10},{10,2},{3,11},{11,3},{4,12},{12,4},... | collective-permute-start | bytes 884744 | tf_op jit(solution)/shard_map/ppermute | solution.py:85

commit v2 on v1

--- a/solution.py
+++ b/solution.py
@@ -4,7 +4,9 @@
 from jax.sharding import PartitionSpec as P
 
 CAP = 24
-COLUMN_CHUNKS = 2
+GATHER_CHUNKS = 4
+SUM_CHUNKS = 2
+STREAMS = 2
 
 
 def ring_of(count):
@@ -41,34 +43,47 @@
     arrived = lax.ppermute(outgoing[CAP:], "expert", swap)
     own = jnp.concatenate([outgoing[:CAP], arrived], axis=0)
 
-    width = model_width // COLUMN_CHUNKS
+    width = model_width // GATHER_CHUNKS
     gate_part = 0.0
     up_part = 0.0
-    for c in range(COLUMN_CHUNKS):
+    last = [None] * STREAMS
+    for c in range(GATHER_CHUNKS):
         cols = slice(c * width, (c + 1) * width)
         block = own[:, cols]
+        if last[c % STREAMS] is not None:
+            block, _ = lax.optimization_barrier((block, last[c % STREAMS]))
         from_left = [block]
         from_right = [block]
         for _ in range(half - 1):
-            from_left.append(lax.ppermute(from_left[-1], "tensor", right))
-            from_right.append(lax.ppermute(from_right[-1], "tensor", left))
-        far_a = lax.ppermute(from_left[-1][:CAP], "tensor", right)
-        far_b = lax.ppermute(from_right[-1][CAP:], "tensor", left)
-        rows = jnp.concatenate(from_left + from_right[1:] + [far_a, far_b], axis=0)
+            pair = (
+                lax.ppermute(from_left[-1], "tensor", right),
+                lax.ppermute(from_right[-1], "tensor", left),
+            )
+            pair = lax.optimization_barrier(pair)
+            from_left.append(pair[0])
+            from_right.append(pair[1])
+        far = (
+            lax.ppermute(from_left[-1][:CAP], "tensor", right),
+            lax.ppermute(from_right[-1][CAP:], "tensor", left),
+        )
+        far = lax.optimization_barrier(far)
+        last[c % STREAMS] = far[0]
+        rows = jnp.concatenate(from_left + from_right[1:] + list(far), axis=0)
         gate_part += jnp.dot(rows, w_gate[0, cols], preferred_element_type=jnp.float32)
         up_part += jnp.dot(rows, w_up[0, cols], preferred_element_type=jnp.float32)
     hidden = (jax.nn.silu(gate_part) * up_part).astype(jnp.bfloat16)
 
+    width = model_width // SUM_CHUNKS
     sums = []
-    for c in range(COLUMN_CHUNKS):
+    for c in range(SUM_CHUNKS):
         cols = slice(c * width, (c + 1) * width)
         part = jnp.dot(hidden, w_down[0][:, cols], preferred_element_type=jnp.float32).astype(jnp.bfloat16)
         part = part.reshape(n_tensor, 2 * CAP, width)
         to_left = [part[k] for k in range(half)]
         to_right = [part[0]] + [part[half + k] for k in range(half - 1)]
         far = part[n_tensor - 1]
-        got_a = lax.ppermute(far[:CAP], "tensor", right)
-        got_b = lax.ppermute(far[CAP:], "tensor", left)
+        got = (lax.ppermute(far[:CAP], "tensor", right), lax.ppermute(far[CAP:], "tensor", left))
+        got_a, got_b = lax.optimization_barrier(got)
         for k in range(half - 1, 0, -1):
             send_a = to_right[k].astype(jnp.float32)
             send_b = to_left[k].astype(jnp.float32)
@@ -78,8 +93,11 @@
             else:
                 send_a = send_a + got_a.astype(jnp.float32)
                 send_b = send_b + got_b.astype(jnp.float32)
-            got_a = lax.ppermute(send_a.astype(jnp.bfloat16), "tensor", right)
-            got_b = lax.ppermute(send_b.astype(jnp.bfloat16), "tensor", left)
+            got = (
+                lax.ppermute(send_a.astype(jnp.bfloat16), "tensor", right),
+                lax.ppermute(send_b.astype(jnp.bfloat16), "tensor", left),
+            )
+            got_a, got_b = lax.optimization_barrier(got)
         sums.append((part[0].astype(jnp.float32) + got_a.astype(jnp.float32) + got_b.astype(jnp.float32)).astype(jnp.bfloat16))
     expert_out = jnp.concatenate(sums, axis=1)
     returned = lax.ppermute(expert_out[CAP:], "expert", swap)

time: 131 us -> 134 us (1.023)
  waiting for transfers between devices: 70.5 us -> 47.8 us
  starting transfers between devices: 35.1 us -> 51.5 us
  matrix products: 21.1 us -> 30.4 us
    ppermute x32 -> x48, waiting for transfers between devices: 67.8 us -> 45.5 us  [the longest x6 9.95 us: per_device(): lax.ppermute(send_a.astype(jnp.bfloat16), 'tensor', right)]
    ppermute x32 -> x48, starting transfers between devices: 34.6 us -> 50.9 us  [the longest x12 13 us: per_device(): lax.ppermute(from_right[-1], 'tensor', left)]
    dot_general x2 -> x4, matrix products: 5.54 us -> 14.1 us  [per_device(): up_part += jnp.dot(rows, w_up[0, cols], preferred_element_type=jnp.float32)]
    dot_general x2 -> x4, matrix products: 5.31 us -> 9.04 us  [per_device(): jnp.dot(rows, w_gate[0, cols], preferred_element_type=jnp.float32)]
    dot_general x2, matrix products: 8.65 us -> 5.67 us  [per_device(): jnp.dot(hidden, w_down[0][:, cols], preferred_element_type=jnp.float32)]
  transfers between devices with their start and end apart: 34 -> 50, of which waited for: 20 -> 35; matrix products, arithmetic and copies ran while one was open for 5% -> 13% of each run, Pallas kernels for 0% -> 0%
where the time goes in v2:
time: 134 us
  starting transfers between devices  51.5 us (38%)
  waiting for transfers between devices  47.8 us (36%)
  matrix products  30.4 us (23%)
  other arithmetic  2.33 us (2%)
  local copies, waits for them, and re-layouts  1.68 us (1%)
    dot_general x4, matrix products, per_device(): up_part += jnp.dot(rows, w_up[0, cols], preferred_element_type=jnp.float32)  14.1 us
    ppermute x12, starting transfers between devices, per_device(): lax.ppermute(from_right[-1], 'tensor', left)  13 us
    ppermute x12, starting transfers between devices, per_device(): lax.ppermute(from_left[-1], 'tensor', right)  12.5 us
    ppermute x6, waiting for transfers between devices, per_device(): lax.ppermute(send_a.astype(jnp.bfloat16), 'tensor', right)  9.95 us
    ppermute x6, waiting for transfers between devices, per_device(): lax.ppermute(send_b.astype(jnp.bfloat16), 'tensor', left)  9.52 us
    ppermute x12, waiting for transfers between devices, per_device(): lax.ppermute(from_left[-1], 'tensor', right)  9.51 us
    dot_general x4, matrix products, per_device(): jnp.dot(rows, w_gate[0, cols], preferred_element_type=jnp.float32)  9.04 us
    ppermute x12, waiting for transfers between devices, per_device(): lax.ppermute(from_right[-1], 'tensor', left)  8.64 us
  transfers between devices with their start and end apart: 50, of which 35 were waited for; matrix products, arithmetic and copies ran while one was open for 13% of the time, Pallas kernels for 0%

profile of v2, /device:TPU:0, one launch (start us, length us, event | category | flops | bytes accessed | tf_op | source)
XLA Modules:
  0.0 134.3 jit_solution(2360561808370128907)
XLA Ops:
  0.2 0.8 compare_reduce_fusion
  2.3 1.2 collective-permute-done
  3.5 2.9 %collective-permute-start.10 = (bf16[48,1536]{1,0:T(8,128)(2,1)S(1)}, bf16[48,1536]{1,0:T(8,128)(2,1)S(1)}, u32[]{:S(2)}, u32[]{:S(2)}) collective-permute-start(bf16[48,1536]{1,0:T(8,128)(2,1)S(1)} %get-tuple-element.106), channel_id=1, source_target_pairs={{2,0},{4,2},{6,4},{7,6},{5,7},{3,5},{1,3},{0,1},{10,8},{12,10},{14... | collective-permute-start | bytes 442376 | tf_op jit(solution)/shard_map/ppermute | solution.py:60
  6.6 2.0 %collective-permute-start.1 = (bf16[48,1536]{1,0:T(8,128)(2,1)S(1)}, bf16[48,1536]{1,0:T(8,128)(2,1)S(1)}, u32[]{:S(2)}, u32[]{:S(2)}) collective-permute-start(bf16[48,1536]{1,0:T(8,128)(2,1)S(1)} %get-tuple-element.134), channel_id=1, source_target_pairs={{0,2},{2,4},{4,6},{6,7},{7,5},{5,3},{3,1},{1,0},{8,10},{10,12},{12... | collective-permute-start | bytes 442376 | tf_op jit(solution)/shard_map/ppermute | solution.py:59
  8.6 2.2 %collective-permute-done.10 = bf16[48,1536]{1,0:T(8,128)(2,1)S(1)} collective-permute-done((bf16[48,1536]{1,0:T(8,128)(2,1)S(1)}, bf16[48,1536]{1,0:T(8,128)(2,1)S(1)}, u32[]{:S(2)}, u32[]{:S(2)}) %collective-permute-start.10) | collective-permute-done | bytes 147488 | tf_op jit(solution)/shard_map/ppermute | solution.py:60
  10.8 2.4 %collective-permute-done.9 = bf16[48,1536]{1,0:T(8,128)(2,1)S(1)} collective-permute-done((bf16[48,1536]{1,0:T(8,128)(2,1)S(1)}, bf16[48,1536]{1,0:T(8,128)(2,1)S(1)}, u32[]{:S(2)}, u32[]{:S(2)}) %collective-permute-start.9) | collective-permute-done | bytes 147488 | tf_op jit(solution)/shard_map/ppermute | solution.py:59
  13.3 1.9 %collective-permute-start.12 = (bf16[48,1536]{1,0:T(8,128)(2,1)S(1)}, bf16[48,1536]{1,0:T(8,128)(2,1)S(1)}, u32[]{:S(2)}, u32[]{:S(2)}) collective-permute-start(bf16[48,1536]{1,0:T(8,128)(2,1)S(1)} %collective-permute-done.10), channel_id=1, source_target_pairs={{2,0},{4,2},{6,4},{7,6},{5,7},{3,5},{1,3},{0,1},{10,8},{12,10},{14... | collective-permute-start | bytes 442376 | tf_op jit(solution)/shard_map/ppermute | solution.py:60
  15.2 1.1 collective-permute-done.1
  16.4 1.9 %collective-permute-start.4 = (bf16[48,1536]{1,0:T(8,128)(2,1)S(1)}, bf16[48,1536]{1,0:T(8,128)(2,1)S(1)}, u32[]{:S(2)}, u32[]{:S(2)}) collective-permute-start(bf16[48,1536]{1,0:T(8,128)(2,1)S(1)} %collective-permute-done.2), channel_id=1, source_target_pairs={{2,0},{4,2},{6,4},{7,6},{5,7},{3,5},{1,3},{0,1},{10,8},{12,10},{14... | collective-permute-start | bytes 442376 | tf_op jit(solution)/shard_map/ppermute | solution.py:60
  18.4 1.6 %collective-permute-done.11 = bf16[48,1536]{1,0:T(8,128)(2,1)S(1)} collective-permute-done((bf16[48,1536]{1,0:T(8,128)(2,1)S(1)}, bf16[48,1536]{1,0:T(8,128)(2,1)S(1)}, u32[]{:S(2)}, u32[]{:S(2)}) %collective-permute-start.11) | collective-permute-done | bytes 147488 | tf_op jit(solution)/shard_map/ppermute | solution.py:59
  20.0 2.0 %collective-permute-start.13 = (bf16[48,1536]{1,0:T(8,128)(2,1)S(1)}, bf16[48,1536]{1,0:T(8,128)(2,1)S(1)}, u32[]{:S(2)}, u32[]{:S(2)}) collective-permute-start(bf16[48,1536]{1,0:T(8,128)(2,1)S(1)} %collective-permute-done.11), channel_id=1, source_target_pairs={{0,2},{2,4},{4,6},{6,7},{7,5},{5,3},{3,1},{1,0},{8,10},{10,12},{12... | collective-permute-start | bytes 442376 | tf_op jit(solution)/shard_map/ppermute | solution.py:59
  22.0 1.1 collective-permute-done.3
  23.2 1.8 %collective-permute-start.5 = (bf16[48,1536]{1,0:T(8,128)(2,1)S(1)}, bf16[48,1536]{1,0:T(8,128)(2,1)S(1)}, u32[]{:S(2)}, u32[]{:S(2)}) collective-permute-start(bf16[48,1536]{1,0:T(8,128)(2,1)S(1)} %collective-permute-done.3), channel_id=1, source_target_pairs={{0,2},{2,4},{4,6},{6,7},{7,5},{5,3},{3,1},{1,0},{8,10},{10,12},{12... | collective-permute-start | bytes 442376 | tf_op jit(solution)/shard_map/ppermute | solution.py:59
  25.2 1.1 collective-permute-done.13
  26.3 1.6 %collective-permute-done.14 = bf16[48,1536]{1,0:T(8,128)(2,1)S(1)} collective-permute-done((bf16[48,1536]{1,0:T(8,128)(2,1)S(1)}, bf16[48,1536]{1,0:T(8,128)(2,1)S(1)}, u32[]{:S(2)}, u32[]{:S(2)}) %collective-permute-start.14) | collective-permute-done | bytes 147488 | tf_op jit(solution)/shard_map/ppermute | solution.py:60
  28.6 1.5 %collective-permute-start.15 = (bf16[24,1536]{1,0:T(8,128)(2,1)S(1)}, bf16[24,1536]{1,0:T(8,128)(2,1)S(1)}, u32[]{:S(2)}, u32[]{:S(2)}) collective-permute-start(bf16[24,1536]{1,0:T(8,128)(2,1)S(1)} %slice.203), channel_id=1, source_target_pairs={{0,2},{2,4},{4,6},{6,7},{7,5},{5,3},{3,1},{1,0},{8,10},{10,12},{12... | collective-permute-start | bytes 221192 | tf_op jit(solution)/shard_map/ppermute | solution.py:66
  30.1 0.8 collective-permute-done.6
  31.3 2.0 %collective-permute-start.7 = (bf16[24,1536]{1,0:T(8,128)(2,1)S(1)}, bf16[24,1536]{1,0:T(8,128)(2,1)S(1)}, u32[]{:S(2)}, u32[]{:S(2)}) collective-permute-start(bf16[24,1536]{1,0:T(8,128)(2,1)S(1)} %slice.199), channel_id=1, source_target_pairs={{0,2},{2,4},{4,6},{6,7},{7,5},{5,3},{3,1},{1,0},{8,10},{10,12},{12... | collective-permute-start | bytes 221192 | tf_op jit(solution)/shard_map/ppermute | solution.py:66
  33.3 1.4 %collective-permute-start.26 = (bf16[48,1536]{1,0:T(8,128)(2,1)S(1)}, bf16[48,1536]{1,0:T(8,128)(2,1)S(1)}, u32[]{:S(2)}, u32[]{:S(2)}) collective-permute-start(bf16[48,1536]{1,0:T(8,128)(2,1)S(1)} %get-tuple-element.80), channel_id=1, source_target_pairs={{2,0},{4,2},{6,4},{7,6},{5,7},{3,5},{1,3},{0,1},{10,8},{12,10},{14... | collective-permute-start | bytes 442376 | tf_op jit(solution)/shard_map/ppermute | solution.py:60
  35.4 0.9 collective-permute-done.8
  36.5 2.0 %collective-permute-start.18 = (bf16[48,1536]{1,0:T(8,128)(2,1)S(1)}, bf16[48,1536]{1,0:T(8,128)(2,1)S(1)}, u32[]{:S(2)}, u32[]{:S(2)}) collective-permute-start(bf16[48,1536]{1,0:T(8,128)(2,1)S(1)} %get-tuple-element.71), channel_id=1, source_target_pairs={{2,0},{4,2},{6,4},{7,6},{5,7},{3,5},{1,3},{0,1},{10,8},{12,10},{14... | collective-permute-start | bytes 442376 | tf_op jit(solution)/shard_map/ppermute | solution.py:60
  38.5 3.3 %fusion.17 = f32[384,1024]{1,0:T(8,128)S(1)} fusion(bf16[384,1536]{1,0:T(8,128)(2,1)S(1)} %constant_dynamic-update-slice_fusion, bf16[1,6144,1024]{2,1,0:T(8,128)(2,1)} %param.10), kind=kOutput, calls=%fused_computation.15 | convolution fusion | flops 1207959552 | bytes 5898240 | tf_op jit(solution)/shard_map/dot_general | solution.py:73
  41.8 1.4 %fusion.25 = f32[384,1024]{1,0:T(8,128)S(1)} fusion(bf16[384,1536]{1,0:T(8,128)(2,1)S(1)} %constant_dynamic-update-slice_fusion, bf16[1,6144,1024]{2,1,0:T(8,128)(2,1)S(1)} %copy-done.4), kind=kOutput, calls=%fused_computation.23 | convolution fusion | flops 1207959552 | bytes 5898240 | tf_op jit(solution)/shard_map/dot_general | solution.py:72
  43.3 3.4 %fusion.15 = f32[384,1024]{1,0:T(8,128)S(1)} fusion(bf16[384,1536]{1,0:T(8,128)(2,1)S(1)} %constant_dynamic-update-slice_fusion.9, bf16[1,6144,1024]{2,1,0:T(8,128)(2,1)} %param.10), kind=kOutput, calls=%fused_computation.13 | convolution fusion | flops 1207959552 | bytes 5898240 | tf_op jit(solution)/shard_map/dot_general | solution.py:73
  46.7 2.6 %fusion.23 = f32[384,1024]{1,0:T(8,128)} fusion(bf16[384,1536]{1,0:T(8,128)(2,1)S(1)} %constant_dynamic-update-slice_fusion.9, bf16[1,6144,1024]{2,1,0:T(8,128)(2,1)S(1)} %copy-done.4), kind=kOutput, calls=%fused_computation.21 | convolution fusion | flops 1207959552 | bytes 5898240 | tf_op jit(solution)/shard_map/dot_general | solution.py:72
  49.3 1.6 %collective-permute-start.27 = (bf16[48,1536]{1,0:T(8,128)(2,1)S(1)}, bf16[48,1536]{1,0:T(8,128)(2,1)S(1)}, u32[]{:S(2)}, u32[]{:S(2)}) collective-permute-start(bf16[48,1536]{1,0:T(8,128)(2,1)S(1)} %collective-permute-done.25), channel_id=1, source_target_pairs={{0,2},{2,4},{4,6},{6,7},{7,5},{5,3},{3,1},{1,0},{8,10},{10,12},{12... | collective-permute-start | bytes 442376 | tf_op jit(solution)/shard_map/ppermute | solution.py:59
  51.4 1.5 %collective-permute-start.19 = (bf16[48,1536]{1,0:T(8,128)(2,1)S(1)}, bf16[48,1536]{1,0:T(8,128)(2,1)S(1)}, u32[]{:S(2)}, u32[]{:S(2)}) collective-permute-start(bf16[48,1536]{1,0:T(8,128)(2,1)S(1)} %collective-permute-done.17), channel_id=1, source_target_pairs={{0,2},{2,4},{4,6},{6,7},{7,5},{5,3},{3,1},{1,0},{8,10},{10,12},{12... | collective-permute-start | bytes 442376 | tf_op jit(solution)/shard_map/ppermute | solution.py:59
  53.5 1.7 %collective-permute-done.27 = bf16[48,1536]{1,0:T(8,128)(2,1)S(1)} collective-permute-done((bf16[48,1536]{1,0:T(8,128)(2,1)S(1)}, bf16[48,1536]{1,0:T(8,128)(2,1)S(1)}, u32[]{:S(2)}, u32[]{:S(2)}) %collective-permute-start.27) | collective-permute-done | bytes 147488 | tf_op jit(solution)/shard_map/ppermute | solution.py:59
  55.2 1.8 %collective-permute-done.28 = bf16[48,1536]{1,0:T(8,128)(2,1)S(1)} collective-permute-done((bf16[48,1536]{1,0:T(8,128)(2,1)S(1)}, bf16[48,1536]{1,0:T(8,128)(2,1)S(1)}, u32[]{:S(2)}, u32[]{:S(2)}) %collective-permute-start.28) | collective-permute-done | bytes 147488 | tf_op jit(solution)/shard_map/ppermute | solution.py:60
  57.0 1.3 collective-permute-start.29
  59.5 1.3 collective-permute-start.21
  62.1 1.3 collective-permute-done.30
  64.2 1.3 collective-permute-start.31
  65.9 0.8 collective-permute-start.24
  66.7 1.3 collective-permute-start.23
  68.2 2.2 %collective-permute-done.24 = bf16[24,1536]{1,0:T(8,128)(2,1)S(1)} collective-permute-done((bf16[24,1536]{1,0:T(8,128)(2,1)S(1)}, bf16[24,1536]{1,0:T(8,128)(2,1)S(1)}, u32[]{:S(2)}, u32[]{:S(2)}) %collective-permute-start.24) | collective-permute-done | bytes 73760 | tf_op jit(solution)/shard_map/ppermute | solution.py:67
  70.3 0.7 collective-permute-done.23
  71.1 2.6 %fusion.13 = f32[384,1024]{1,0:T(8,128)} fusion(bf16[384,1536]{1,0:T(8,128)(2,1)S(1)} %constant_dynamic-update-slice_fusion.18, bf16[1,6144,1024]{2,1,0:T(8,128)(2,1)S(1)} %bitcast.62), kind=kOutput, calls=%fused_computation.11 | convolution fusion | flops 1207959552 | bytes 5898240 | tf_op jit(solution)/shard_map/dot_general | solution.py:73
  73.7 2.6 %fusion.21 = f32[384,1024]{1,0:T(8,128)} fusion(bf16[384,1536]{1,0:T(8,128)(2,1)S(1)} %constant_dynamic-update-slice_fusion.18, bf16[1,6144,1024]{2,1,0:T(8,128)(2,1)S(1)} %copy-done.4), kind=kOutput, calls=%fused_computation.19 | convolution fusion | flops 1207959552 | bytes 5898240 | tf_op jit(solution)/shard_map/dot_general | solution.py:72
  76.3 2.5 %fusion.19 = f32[384,1024]{1,0:T(8,128)} fusion(bf16[384,1536]{1,0:T(8,128)(2,1)S(1)} %constant_dynamic-update-slice_fusion.27, bf16[1,6144,1024]{2,1,0:T(8,128)(2,1)S(1)} %copy-done.4), kind=kOutput, calls=%fused_computation.17 | convolution fusion | flops 1207959552 | bytes 5898240 | tf_op jit(solution)/shard_map/dot_general | solution.py:72
  78.9 4.9 %multiply_convert_fusion = bf16[384,1024]{1,0:T(8,128)(2,1)S(1)} fusion(f32[384,1024]{1,0:T(8,128)} %fusion.13, f32[384,1024]{1,0:T(8,128)S(1)} %fusion.17, f32[384,1024]{1,0:T(8,128)S(1)} %fusion.15, f32[384,1024]{1,0:T(8,128)} %fusion.19, f32[384,1024]{1,0:T(8,128)} %fusion.21, f32[384,1024]{1,0:T(8,128)S(1)} %fusion.25, f32[384,1024]{1,0:T(8,128)} %fusion.23, ...), kind=kOutput, calls=%fused_computation.33 | convolution fusion | flops 1212678144 | bytes 16121856 | tf_op jit(solution)/shard_map/dot_general | solution.py:73
  84.2 2.8 %fusion.8 = bf16[384,3072]{1,0:T(8,128)(2,1)S(1)} fusion(bf16[384,1024]{1,0:T(8,128)(2,1)S(1)} %multiply_convert_fusion, bf16[1024,6144]{1,0:T(8,128)(2,1)S(1)} %bitcast.65), kind=kOutput, calls=%fused_computation.8 | convolution fusion | flops 2417098752 | bytes 9437184 | tf_op jit(solution)/shard_map/dot_general | solution.py:80
  87.0 2.8 %fusion.5 = bf16[384,3072]{1,0:T(8,128)(2,1)S(1)} fusion(bf16[384,1024]{1,0:T(8,128)(2,1)S(1)} %multiply_convert_fusion, bf16[1024,6144]{1,0:T(8,128)(2,1)S(1)} %bitcast.66), kind=kOutput, calls=%fused_computation.7 | convolution fusion | flops 2417098752 | bytes 9437184 | tf_op jit(solution)/shard_map/dot_general | solution.py:80
  90.4 1.7 %collective-permute-start.41 = (bf16[24,3072]{1,0:T(8,128)(2,1)S(1)}, bf16[24,3072]{1,0:T(8,128)(2,1)S(1)}, u32[]{:S(2)}, u32[]{:S(2)}) collective-permute-start(bf16[24,3072]{1,0:T(8,128)(2,1)S(1)} %get-tuple-element.126), channel_id=1, source_target_pairs={{0,2},{2,4},{4,6},{6,7},{7,5},{5,3},{3,1},{1,0},{8,10},{10,12},{12... | collective-permute-start | bytes 442376 | tf_op jit(solution)/shard_map/ppermute | solution.py:85
  92.5 1.7 %collective-permute-start.33 = (bf16[24,3072]{1,0:T(8,128)(2,1)S(1)}, bf16[24,3072]{1,0:T(8,128)(2,1)S(1)}, u32[]{:S(2)}, u32[]{:S(2)}) collective-permute-start(bf16[24,3072]{1,0:T(8,128)(2,1)S(1)} %get-tuple-element.116), channel_id=1, source_target_pairs={{0,2},{2,4},{4,6},{6,7},{7,5},{5,3},{3,1},{1,0},{8,10},{10,12},{12... | collective-permute-start | bytes 442376 | tf_op jit(solution)/shard_map/ppermute | solution.py:85
  94.1 2.6 %collective-permute-done.42 = bf16[24,3072]{1,0:T(8,128)(2,1)S(1)} collective-permute-done((bf16[24,3072]{1,0:T(8,128)(2,1)S(1)}, bf16[24,3072]{1,0:T(8,128)(2,1)S(1)}, u32[]{:S(2)}, u32[]{:S(2)}) %collective-permute-start.42) | collective-permute-done | bytes 147488 | tf_op jit(solution)/shard_map/ppermute | solution.py:85
  97.2 1.7 %collective-permute-start.43 = (bf16[48,3072]{1,0:T(8,128)(2,1)S(1)}, bf16[48,3072]{1,0:T(8,128)(2,1)S(1)}, u32[]{:S(2)}, u32[]{:S(2)}) collective-permute-start(bf16[48,3072]{1,0:T(8,128)(2,1)S(1)} %pad_maximum_fusion.3), channel_id=1, source_target_pairs={{0,2},{2,4},{4,6},{6,7},{7,5},{5,3},{3,1},{1,0},{8,10},{10,12},{12... | collective-permute-start | bytes 884744 | tf_op jit(solution)/shard_map/ppermute | solution.py:97
  100.4 1.7 %collective-permute-start.35 = (bf16[48,3072]{1,0:T(8,128)(2,1)S(1)}, bf16[48,3072]{1,0:T(8,128)(2,1)S(1)}, u32[]{:S(2)}, u32[]{:S(2)}) collective-permute-start(bf16[48,3072]{1,0:T(8,128)(2,1)S(1)} %pad_maximum_fusion.1), channel_id=1, source_target_pairs={{0,2},{2,4},{4,6},{6,7},{7,5},{5,3},{3,1},{1,0},{8,10},{10,12},{12... | collective-permute-start | bytes 884744 | tf_op jit(solution)/shard_map/ppermute | solution.py:97
  102.6 4.7 %collective-permute-done.43 = bf16[48,3072]{1,0:T(8,128)(2,1)S(1)} collective-permute-done((bf16[48,3072]{1,0:T(8,128)(2,1)S(1)}, bf16[48,3072]{1,0:T(8,128)(2,1)S(1)}, u32[]{:S(2)}, u32[]{:S(2)}) %collective-permute-start.43) | collective-permute-done | bytes 294944 | tf_op jit(solution)/shard_map/ppermute | solution.py:97
  107.3 1.7 %collective-permute-done.44 = bf16[48,3072]{1,0:T(8,128)(2,1)S(1)} collective-permute-done((bf16[48,3072]{1,0:T(8,128)(2,1)S(1)}, bf16[48,3072]{1,0:T(8,128)(2,1)S(1)}, u32[]{:S(2)}, u32[]{:S(2)}) %collective-permute-start.44) | collective-permute-done | bytes 294944 | tf_op jit(solution)/shard_map/ppermute | solution.py:98
  109.6 1.6 %collective-permute-start.45 = (bf16[48,3072]{1,0:T(8,128)(2,1)S(1)}, bf16[48,3072]{1,0:T(8,128)(2,1)S(1)}, u32[]{:S(2)}, u32[]{:S(2)}) collective-permute-start(bf16[48,3072]{1,0:T(8,128)(2,1)S(1)} %get-tuple-element.122), channel_id=1, source_target_pairs={{0,2},{2,4},{4,6},{6,7},{7,5},{5,3},{3,1},{1,0},{8,10},{10,12},{12... | collective-permute-start | bytes 884744 | tf_op jit(solution)/shard_map/ppermute | solution.py:97
  111.2 2.4 %collective-permute-done.35 = bf16[48,3072]{1,0:T(8,128)(2,1)S(1)} collective-permute-done((bf16[48,3072]{1,0:T(8,128)(2,1)S(1)}, bf16[48,3072]{1,0:T(8,128)(2,1)S(1)}, u32[]{:S(2)}, u32[]{:S(2)}) %collective-permute-start.35) | collective-permute-done | bytes 294944 | tf_op jit(solution)/shard_map/ppermute | solution.py:97
  113.6 1.7 %collective-permute-done.36 = bf16[48,3072]{1,0:T(8,128)(2,1)S(1)} collective-permute-done((bf16[48,3072]{1,0:T(8,128)(2,1)S(1)}, bf16[48,3072]{1,0:T(8,128)(2,1)S(1)}, u32[]{:S(2)}, u32[]{:S(2)}) %collective-permute-start.36) | collective-permute-done | bytes 294944 | tf_op jit(solution)/shard_map/ppermute | solution.py:98
  115.8 1.7 %collective-permute-start.37 = (bf16[48,3072]{1,0:T(8,128)(2,1)S(1)}, bf16[48,3072]{1,0:T(8,128)(2,1)S(1)}, u32[]{:S(2)}, u32[]{:S(2)}) collective-permute-start(bf16[48,3072]{1,0:T(8,128)(2,1)S(1)} %get-tuple-element.112), channel_id=1, source_target_pairs={{0,2},{2,4},{4,6},{6,7},{7,5},{5,3},{3,1},{1,0},{8,10},{10,12},{12... | collective-permute-start | bytes 884744 | tf_op jit(solution)/shard_map/ppermute | solution.py:97
  117.5 0.9 collective-permute-done.46
  118.6 1.1 collective-permute-start.48
  119.7 1.0 collective-permute-start.47
  120.7 1.5 %collective-permute-done.38 = bf16[48,3072]{1,0:T(8,128)(2,1)S(1)} collective-permute-done((bf16[48,3072]{1,0:T(8,128)(2,1)S(1)}, bf16[48,3072]{1,0:T(8,128)(2,1)S(1)}, u32[]{:S(2)}, u32[]{:S(2)}) %collective-permute-start.38) | collective-permute-done | bytes 294944 | tf_op jit(solution)/shard_map/ppermute | solution.py:98
  122.7 1.6 %collective-permute-start.40 = (bf16[48,3072]{1,0:T(8,128)(2,1)S(1)}, bf16[48,3072]{1,0:T(8,128)(2,1)S(1)}, u32[]{:S(2)}, u32[]{:S(2)}) collective-permute-start(bf16[48,3072]{1,0:T(8,128)(2,1)S(1)} %get-tuple-element.109), channel_id=1, source_target_pairs={{2,0},{4,2},{6,4},{7,6},{5,7},{3,5},{1,3},{0,1},{10,8},{12,10},{14... | collective-permute-start | bytes 884744 | tf_op jit(solution)/shard_map/ppermute | solution.py:98
  125.4 1.0 collective-permute-done.47
  126.4 3.1 %collective-permute-done.40 = bf16[48,3072]{1,0:T(8,128)(2,1)S(1)} collective-permute-done((bf16[48,3072]{1,0:T(8,128)(2,1)S(1)}, bf16[48,3072]{1,0:T(8,128)(2,1)S(1)}, u32[]{:S(2)}, u32[]{:S(2)}) %collective-permute-start.40) | collective-permute-done | bytes 294944 | tf_op jit(solution)/shard_map/ppermute | solution.py:98
  129.5 1.5 %collective-permute-done.39 = bf16[48,3072]{1,0:T(8,128)(2,1)S(1)} collective-permute-done((bf16[48,3072]{1,0:T(8,128)(2,1)S(1)}, bf16[48,3072]{1,0:T(8,128)(2,1)S(1)}, u32[]{:S(2)}, u32[]{:S(2)}) %collective-permute-start.39) | collective-permute-done | bytes 294944 | tf_op jit(solution)/shard_map/ppermute | solution.py:97
  131.9 1.1 collective-permute-done.49
  133.0 1.3 fusion
  (142 shorter events, 16.6 us)
Async XLA Ops:
  0.0 1.4 %copy-start = (bf16[64,6144]{1,0:T(8,128)(2,1)S(1)}, bf16[64,6144]{1,0:T(8,128)(2,1)}, u32[]{:S(2)}) copy-start(bf16[64,6144]{1,0:T(8,128)(2,1)} %param.6) | copy-start | bytes 2359300
  1.7 1.7 %collective-permute-start = (bf16[24,6144]{1,0:T(8,128)(2,1)S(1)}, bf16[24,6144]{1,0:T(8,128)(2,1)S(1)}, u32[]{:S(2)}, u32[]{:S(2)}) collective-permute-start(bf16[24,6144]{1,0:T(8,128)(2,1)S(1)} %get-tuple-element.136), channel_id=1, source_target_pairs={{0,8},{8,0},{1,9},{9,1},{2,10},{10,2},{3,11},{11,3},{4,12},{12,4},... | collective-permute-start | bytes 884744 | tf_op jit(solution)/shard_map/ppermute | solution.py:43
  3.5 7.3 %collective-permute-start.10 = (bf16[48,1536]{1,0:T(8,128)(2,1)S(1)}, bf16[48,1536]{1,0:T(8,128)(2,1)S(1)}, u32[]{:S(2)}, u32[]{:S(2)}) collective-permute-start(bf16[48,1536]{1,0:T(8,128)(2,1)S(1)} %get-tuple-element.106), channel_id=1, source_target_pairs={{2,0},{4,2},{6,4},{7,6},{5,7},{3,5},{1,3},{0,1},{10,8},{12,10},{14... | collective-permute-start | bytes 442376 | tf_op jit(solution)/shard_map/ppermute | solution.py:60
  6.5 6.7 %collective-permute-start.9 = (bf16[48,1536]{1,0:T(8,128)(2,1)S(1)}, bf16[48,1536]{1,0:T(8,128)(2,1)S(1)}, u32[]{:S(2)}, u32[]{:S(2)}) collective-permute-start(bf16[48,1536]{1,0:T(8,128)(2,1)S(1)} %get-tuple-element.106), channel_id=1, source_target_pairs={{0,2},{2,4},{4,6},{6,7},{7,5},{5,3},{3,1},{1,0},{8,10},{10,12},{12... | collective-permute-start | bytes 442376 | tf_op jit(solution)/shard_map/ppermute | solution.py:59
  6.6 9.8 %collective-permute-start.1 = (bf16[48,1536]{1,0:T(8,128)(2,1)S(1)}, bf16[48,1536]{1,0:T(8,128)(2,1)S(1)}, u32[]{:S(2)}, u32[]{:S(2)}) collective-permute-start(bf16[48,1536]{1,0:T(8,128)(2,1)S(1)} %get-tuple-element.134), channel_id=1, source_target_pairs={{0,2},{2,4},{4,6},{6,7},{7,5},{5,3},{3,1},{1,0},{8,10},{10,12},{12... | collective-permute-start | bytes 442376 | tf_op jit(solution)/shard_map/ppermute | solution.py:59
  8.6 7.8 %collective-permute-start.2 = (bf16[48,1536]{1,0:T(8,128)(2,1)S(1)}, bf16[48,1536]{1,0:T(8,128)(2,1)S(1)}, u32[]{:S(2)}, u32[]{:S(2)}) collective-permute-start(bf16[48,1536]{1,0:T(8,128)(2,1)S(1)} %get-tuple-element.134), channel_id=1, source_target_pairs={{2,0},{4,2},{6,4},{7,6},{5,7},{3,5},{1,3},{0,1},{10,8},{12,10},{14... | collective-permute-start | bytes 442376 | tf_op jit(solution)/shard_map/ppermute | solution.py:60
  13.2 6.8 %collective-permute-start.11 = (bf16[48,1536]{1,0:T(8,128)(2,1)S(1)}, bf16[48,1536]{1,0:T(8,128)(2,1)S(1)}, u32[]{:S(2)}, u32[]{:S(2)}) collective-permute-start(bf16[48,1536]{1,0:T(8,128)(2,1)S(1)} %collective-permute-done.9), channel_id=1, source_target_pairs={{0,2},{2,4},{4,6},{6,7},{7,5},{5,3},{3,1},{1,0},{8,10},{10,12},{12... | collective-permute-start | bytes 442376 | tf_op jit(solution)/shard_map/ppermute | solution.py:59
  13.3 6.7 %collective-permute-start.12 = (bf16[48,1536]{1,0:T(8,128)(2,1)S(1)}, bf16[48,1536]{1,0:T(8,128)(2,1)S(1)}, u32[]{:S(2)}, u32[]{:S(2)}) collective-permute-start(bf16[48,1536]{1,0:T(8,128)(2,1)S(1)} %collective-permute-done.10), channel_id=1, source_target_pairs={{2,0},{4,2},{6,4},{7,6},{5,7},{3,5},{1,3},{0,1},{10,8},{12,10},{14... | collective-permute-start | bytes 442376 | tf_op jit(solution)/shard_map/ppermute | solution.py:60
  16.4 6.8 %collective-permute-start.3 = (bf16[48,1536]{1,0:T(8,128)(2,1)S(1)}, bf16[48,1536]{1,0:T(8,128)(2,1)S(1)}, u32[]{:S(2)}, u32[]{:S(2)}) collective-permute-start(bf16[48,1536]{1,0:T(8,128)(2,1)S(1)} %collective-permute-done.1), channel_id=1, source_target_pairs={{0,2},{2,4},{4,6},{6,7},{7,5},{5,3},{3,1},{1,0},{8,10},{10,12},{12... | collective-permute-start | bytes 442376 | tf_op jit(solution)/shard_map/ppermute | solution.py:59
  16.4 6.7 %collective-permute-start.4 = (bf16[48,1536]{1,0:T(8,128)(2,1)S(1)}, bf16[48,1536]{1,0:T(8,128)(2,1)S(1)}, u32[]{:S(2)}, u32[]{:S(2)}) collective-permute-start(bf16[48,1536]{1,0:T(8,128)(2,1)S(1)} %collective-permute-done.2), channel_id=1, source_target_pairs={{2,0},{4,2},{6,4},{7,6},{5,7},{3,5},{1,3},{0,1},{10,8},{12,10},{14... | collective-permute-start | bytes 442376 | tf_op jit(solution)/shard_map/ppermute | solution.py:60
  18.4 23.4 %copy-start.4 = (bf16[1,6144,1024]{2,1,0:T(8,128)(2,1)S(1)}, bf16[1,6144,1024]{2,1,0:T(8,128)(2,1)}, u32[]{:S(2)}) copy-start(bf16[1,6144,1024]{2,1,0:T(8,128)(2,1)} %param.9) | copy-start | bytes 37748740
  20.0 6.3 %collective-permute-start.13 = (bf16[48,1536]{1,0:T(8,128)(2,1)S(1)}, bf16[48,1536]{1,0:T(8,128)(2,1)S(1)}, u32[]{:S(2)}, u32[]{:S(2)}) collective-permute-start(bf16[48,1536]{1,0:T(8,128)(2,1)S(1)} %collective-permute-done.11), channel_id=1, source_target_pairs={{0,2},{2,4},{4,6},{6,7},{7,5},{5,3},{3,1},{1,0},{8,10},{10,12},{12... | collective-permute-start | bytes 442376 | tf_op jit(solution)/shard_map/ppermute | solution.py:59
  22.0 5.9 %collective-permute-start.14 = (bf16[48,1536]{1,0:T(8,128)(2,1)S(1)}, bf16[48,1536]{1,0:T(8,128)(2,1)S(1)}, u32[]{:S(2)}, u32[]{:S(2)}) collective-permute-start(bf16[48,1536]{1,0:T(8,128)(2,1)S(1)} %collective-permute-done.12), channel_id=1, source_target_pairs={{2,0},{4,2},{6,4},{7,6},{5,7},{3,5},{1,3},{0,1},{10,8},{12,10},{14... | collective-permute-start | bytes 442376 | tf_op jit(solution)/shard_map/ppermute | solution.py:60
  23.2 6.9 %collective-permute-start.5 = (bf16[48,1536]{1,0:T(8,128)(2,1)S(1)}, bf16[48,1536]{1,0:T(8,128)(2,1)S(1)}, u32[]{:S(2)}, u32[]{:S(2)}) collective-permute-start(bf16[48,1536]{1,0:T(8,128)(2,1)S(1)} %collective-permute-done.3), channel_id=1, source_target_pairs={{0,2},{2,4},{4,6},{6,7},{7,5},{5,3},{3,1},{1,0},{8,10},{10,12},{12... | collective-permute-start | bytes 442376 | tf_op jit(solution)/shard_map/ppermute | solution.py:59
  24.9 5.9 %collective-permute-start.6 = (bf16[48,1536]{1,0:T(8,128)(2,1)S(1)}, bf16[48,1536]{1,0:T(8,128)(2,1)S(1)}, u32[]{:S(2)}, u32[]{:S(2)}) collective-permute-start(bf16[48,1536]{1,0:T(8,128)(2,1)S(1)} %collective-permute-done.4), channel_id=1, source_target_pairs={{2,0},{4,2},{6,4},{7,6},{5,7},{3,5},{1,3},{0,1},{10,8},{12,10},{14... | collective-permute-start | bytes 442376 | tf_op jit(solution)/shard_map/ppermute | solution.py:60
  28.0 5.3 %collective-permute-start.16 = (bf16[24,1536]{1,0:T(8,128)(2,1)S(1)}, bf16[24,1536]{1,0:T(8,128)(2,1)S(1)}, u32[]{:S(2)}, u32[]{:S(2)}) collective-permute-start(bf16[24,1536]{1,0:T(8,128)(2,1)S(1)} %slice.204), channel_id=1, source_target_pairs={{2,0},{4,2},{6,4},{7,6},{5,7},{3,5},{1,3},{0,1},{10,8},{12,10},{14... | collective-permute-start | bytes 221192 | tf_op jit(solution)/shard_map/ppermute | solution.py:67
  28.6 4.7 %collective-permute-start.15 = (bf16[24,1536]{1,0:T(8,128)(2,1)S(1)}, bf16[24,1536]{1,0:T(8,128)(2,1)S(1)}, u32[]{:S(2)}, u32[]{:S(2)}) collective-permute-start(bf16[24,1536]{1,0:T(8,128)(2,1)S(1)} %slice.203), channel_id=1, source_target_pairs={{0,2},{2,4},{4,6},{6,7},{7,5},{5,3},{3,1},{1,0},{8,10},{10,12},{12... | collective-permute-start | bytes 221192 | tf_op jit(solution)/shard_map/ppermute | solution.py:66
  31.0 5.3 %collective-permute-start.8 = (bf16[24,1536]{1,0:T(8,128)(2,1)S(1)}, bf16[24,1536]{1,0:T(8,128)(2,1)S(1)}, u32[]{:S(2)}, u32[]{:S(2)}) collective-permute-start(bf16[24,1536]{1,0:T(8,128)(2,1)S(1)} %slice.200), channel_id=1, source_target_pairs={{2,0},{4,2},{6,4},{7,6},{5,7},{3,5},{1,3},{0,1},{10,8},{12,10},{14... | collective-permute-start | bytes 221192 | tf_op jit(solution)/shard_map/ppermute | solution.py:67
  31.3 5.2 %collective-permute-start.7 = (bf16[24,1536]{1,0:T(8,128)(2,1)S(1)}, bf16[24,1536]{1,0:T(8,128)(2,1)S(1)}, u32[]{:S(2)}, u32[]{:S(2)}) collective-permute-start(bf16[24,1536]{1,0:T(8,128)(2,1)S(1)} %slice.199), channel_id=1, source_target_pairs={{0,2},{2,4},{4,6},{6,7},{7,5},{5,3},{3,1},{1,0},{8,10},{10,12},{12... | collective-permute-start | bytes 221192 | tf_op jit(solution)/shard_map/ppermute | solution.py:66
  33.3 16.0 %collective-permute-start.26 = (bf16[48,1536]{1,0:T(8,128)(2,1)S(1)}, bf16[48,1536]{1,0:T(8,128)(2,1)S(1)}, u32[]{:S(2)}, u32[]{:S(2)}) collective-permute-start(bf16[48,1536]{1,0:T(8,128)(2,1)S(1)} %get-tuple-element.80), channel_id=1, source_target_pairs={{2,0},{4,2},{6,4},{7,6},{5,7},{3,5},{1,3},{0,1},{10,8},{12,10},{14... | collective-permute-start | bytes 442376 | tf_op jit(solution)/shard_map/ppermute | solution.py:60
  34.6 14.6 %collective-permute-start.25 = (bf16[48,1536]{1,0:T(8,128)(2,1)S(1)}, bf16[48,1536]{1,0:T(8,128)(2,1)S(1)}, u32[]{:S(2)}, u32[]{:S(2)}) collective-permute-start(bf16[48,1536]{1,0:T(8,128)(2,1)S(1)} %get-tuple-element.80), channel_id=1, source_target_pairs={{0,2},{2,4},{4,6},{6,7},{7,5},{5,3},{3,1},{1,0},{8,10},{10,12},{12... | collective-permute-start | bytes 442376 | tf_op jit(solution)/shard_map/ppermute | solution.py:59
  36.5 15.0 %collective-permute-start.18 = (bf16[48,1536]{1,0:T(8,128)(2,1)S(1)}, bf16[48,1536]{1,0:T(8,128)(2,1)S(1)}, u32[]{:S(2)}, u32[]{:S(2)}) collective-permute-start(bf16[48,1536]{1,0:T(8,128)(2,1)S(1)} %get-tuple-element.71), channel_id=1, source_target_pairs={{2,0},{4,2},{6,4},{7,6},{5,7},{3,5},{1,3},{0,1},{10,8},{12,10},{14... | collective-permute-start | bytes 442376 | tf_op jit(solution)/shard_map/ppermute | solution.py:60
  38.5 13.0 %collective-permute-start.17 = (bf16[48,1536]{1,0:T(8,128)(2,1)S(1)}, bf16[48,1536]{1,0:T(8,128)(2,1)S(1)}, u32[]{:S(2)}, u32[]{:S(2)}) collective-permute-start(bf16[48,1536]{1,0:T(8,128)(2,1)S(1)} %get-tuple-element.71), channel_id=1, source_target_pairs={{0,2},{2,4},{4,6},{6,7},{7,5},{5,3},{3,1},{1,0},{8,10},{10,12},{12... | collective-permute-start | bytes 442376 | tf_op jit(solution)/shard_map/ppermute | solution.py:59
  41.8 29.3 %slice-start = ((s8[12582912]{0:T(1024)(128)(4,1)}), s8[4194304]{0:T(1024)(128)(4,1)S(1)}, s32[]{:S(2)}) async-start(s8[12582912]{0:T(1024)(128)(4,1)} %bitcast.61), calls=%async_computation | async-start | bytes 8388608
  43.2 27.9 %slice-start.1 = ((s8[12582912]{0:T(1024)(128)(4,1)}), s8[4194304]{0:T(1024)(128)(4,1)S(1)}, s32[]{:S(2)}) async-start(s8[12582912]{0:T(1024)(128)(4,1)} %bitcast.61), calls=%async_computation.1 | async-start | bytes 8388608
  46.7 24.4 %slice-start.2 = ((s8[12582912]{0:T(1024)(128)(4,1)}), s8[4194304]{0:T(1024)(128)(4,1)S(1)}, s32[]{:S(2)}) async-start(s8[12582912]{0:T(1024)(128)(4,1)} %bitcast.61), calls=%async_computation.2 | async-start | bytes 8388608
  49.3 5.9 %collective-permute-start.27 = (bf16[48,1536]{1,0:T(8,128)(2,1)S(1)}, bf16[48,1536]{1,0:T(8,128)(2,1)S(1)}, u32[]{:S(2)}, u32[]{:S(2)}) collective-permute-start(bf16[48,1536]{1,0:T(8,128)(2,1)S(1)} %collective-permute-done.25), channel_id=1, source_target_pairs={{0,2},{2,4},{4,6},{6,7},{7,5},{5,3},{3,1},{1,0},{8,10},{10,12},{12... | collective-permute-start | bytes 442376 | tf_op jit(solution)/shard_map/ppermute | solution.py:59
  50.9 6.1 %collective-permute-start.28 = (bf16[48,1536]{1,0:T(8,128)(2,1)S(1)}, bf16[48,1536]{1,0:T(8,128)(2,1)S(1)}, u32[]{:S(2)}, u32[]{:S(2)}) collective-permute-start(bf16[48,1536]{1,0:T(8,128)(2,1)S(1)} %collective-permute-done.26), channel_id=1, source_target_pairs={{2,0},{4,2},{6,4},{7,6},{5,7},{3,5},{1,3},{0,1},{10,8},{12,10},{14... | collective-permute-start | bytes 442376 | tf_op jit(solution)/shard_map/ppermute | solution.py:60
  51.4 7.6 %collective-permute-start.19 = (bf16[48,1536]{1,0:T(8,128)(2,1)S(1)}, bf16[48,1536]{1,0:T(8,128)(2,1)S(1)}, u32[]{:S(2)}, u32[]{:S(2)}) collective-permute-start(bf16[48,1536]{1,0:T(8,128)(2,1)S(1)} %collective-permute-done.17), channel_id=1, source_target_pairs={{0,2},{2,4},{4,6},{6,7},{7,5},{5,3},{3,1},{1,0},{8,10},{10,12},{12... | collective-permute-start | bytes 442376 | tf_op jit(solution)/shard_map/ppermute | solution.py:59
  52.9 6.6 %collective-permute-start.20 = (bf16[48,1536]{1,0:T(8,128)(2,1)S(1)}, bf16[48,1536]{1,0:T(8,128)(2,1)S(1)}, u32[]{:S(2)}, u32[]{:S(2)}) collective-permute-start(bf16[48,1536]{1,0:T(8,128)(2,1)S(1)} %collective-permute-done.18), channel_id=1, source_target_pairs={{2,0},{4,2},{6,4},{7,6},{5,7},{3,5},{1,3},{0,1},{10,8},{12,10},{14... | collective-permute-start | bytes 442376 | tf_op jit(solution)/shard_map/ppermute | solution.py:60
  57.0 5.1 %collective-permute-start.29 = (bf16[48,1536]{1,0:T(8,128)(2,1)S(1)}, bf16[48,1536]{1,0:T(8,128)(2,1)S(1)}, u32[]{:S(2)}, u32[]{:S(2)}) collective-permute-start(bf16[48,1536]{1,0:T(8,128)(2,1)S(1)} %collective-permute-done.27), channel_id=1, source_target_pairs={{0,2},{2,4},{4,6},{6,7},{7,5},{5,3},{3,1},{1,0},{8,10},{10,12},{12... | collective-permute-start | bytes 442376 | tf_op jit(solution)/shard_map/ppermute | solution.py:59
  58.3 5.1 %collective-permute-start.30 = (bf16[48,1536]{1,0:T(8,128)(2,1)S(1)}, bf16[48,1536]{1,0:T(8,128)(2,1)S(1)}, u32[]{:S(2)}, u32[]{:S(2)}) collective-permute-start(bf16[48,1536]{1,0:T(8,128)(2,1)S(1)} %collective-permute-done.28), channel_id=1, source_target_pairs={{2,0},{4,2},{6,4},{7,6},{5,7},{3,5},{1,3},{0,1},{10,8},{12,10},{14... | collective-permute-start | bytes 442376 | tf_op jit(solution)/shard_map/ppermute | solution.py:60
  59.5 6.0 %collective-permute-start.21 = (bf16[48,1536]{1,0:T(8,128)(2,1)S(1)}, bf16[48,1536]{1,0:T(8,128)(2,1)S(1)}, u32[]{:S(2)}, u32[]{:S(2)}) collective-permute-start(bf16[48,1536]{1,0:T(8,128)(2,1)S(1)} %collective-permute-done.19), channel_id=1, source_target_pairs={{0,2},{2,4},{4,6},{6,7},{7,5},{5,3},{3,1},{1,0},{8,10},{10,12},{12... | collective-permute-start | bytes 442376 | tf_op jit(solution)/shard_map/ppermute | solution.py:59
  60.8 5.1 %collective-permute-start.22 = (bf16[48,1536]{1,0:T(8,128)(2,1)S(1)}, bf16[48,1536]{1,0:T(8,128)(2,1)S(1)}, u32[]{:S(2)}, u32[]{:S(2)}) collective-permute-start(bf16[48,1536]{1,0:T(8,128)(2,1)S(1)} %collective-permute-done.20), channel_id=1, source_target_pairs={{2,0},{4,2},{6,4},{7,6},{5,7},{3,5},{1,3},{0,1},{10,8},{12,10},{14... | collective-permute-start | bytes 442376 | tf_op jit(solution)/shard_map/ppermute | solution.py:60
  63.5 12.8 %collective-permute-start.32 = (bf16[24,1536]{1,0:T(8,128)(2,1)S(1)}, bf16[24,1536]{1,0:T(8,128)(2,1)S(1)}, u32[]{:S(2)}, u32[]{:S(2)}) collective-permute-start(bf16[24,1536]{1,0:T(8,128)(2,1)S(1)} %slice.212), channel_id=1, source_target_pairs={{2,0},{4,2},{6,4},{7,6},{5,7},{3,5},{1,3},{0,1},{10,8},{12,10},{14... | collective-permute-start | bytes 221192 | tf_op jit(solution)/shard_map/ppermute | solution.py:67
  64.2 12.1 %collective-permute-start.31 = (bf16[24,1536]{1,0:T(8,128)(2,1)S(1)}, bf16[24,1536]{1,0:T(8,128)(2,1)S(1)}, u32[]{:S(2)}, u32[]{:S(2)}) collective-permute-start(bf16[24,1536]{1,0:T(8,128)(2,1)S(1)} %slice.211), channel_id=1, source_target_pairs={{0,2},{2,4},{4,6},{6,7},{7,5},{5,3},{3,1},{1,0},{8,10},{10,12},{12... | collective-permute-start | bytes 221192 | tf_op jit(solution)/shard_map/ppermute | solution.py:66
  65.9 4.4 %collective-permute-start.24 = (bf16[24,1536]{1,0:T(8,128)(2,1)S(1)}, bf16[24,1536]{1,0:T(8,128)(2,1)S(1)}, u32[]{:S(2)}, u32[]{:S(2)}) collective-permute-start(bf16[24,1536]{1,0:T(8,128)(2,1)S(1)} %slice.208), channel_id=1, source_target_pairs={{2,0},{4,2},{6,4},{7,6},{5,7},{3,5},{1,3},{0,1},{10,8},{12,10},{14... | collective-permute-start | bytes 221192 | tf_op jit(solution)/shard_map/ppermute | solution.py:67
  66.7 4.4 %collective-permute-start.23 = (bf16[24,1536]{1,0:T(8,128)(2,1)S(1)}, bf16[24,1536]{1,0:T(8,128)(2,1)S(1)}, u32[]{:S(2)}, u32[]{:S(2)}) collective-permute-start(bf16[24,1536]{1,0:T(8,128)(2,1)S(1)} %slice.207), channel_id=1, source_target_pairs={{0,2},{2,4},{4,6},{6,7},{7,5},{5,3},{3,1},{1,0},{8,10},{10,12},{12... | collective-permute-start | bytes 221192 | tf_op jit(solution)/shard_map/ppermute | solution.py:66
  76.3 7.4 %slice-start.3 = ((s8[12582912]{0:T(1024)(128)(4,1)}), s8[4194304]{0:T(1024)(128)(4,1)S(1)}, s32[]{:S(2)}) async-start(s8[12582912]{0:T(1024)(128)(4,1)} %bitcast.63), calls=%async_computation.3 | async-start | bytes 8388608
  78.9 4.9 %slice-start.4 = ((s8[12582912]{0:T(1024)(128)(4,1)}), s8[4194304]{0:T(1024)(128)(4,1)S(1)}, s32[]{:S(2)}) async-start(s8[12582912]{0:T(1024)(128)(4,1)} %bitcast.63), calls=%async_computation.4 | async-start | bytes 8388608
  78.9 5.3 %slice-start.5 = ((s8[12582912]{0:T(1024)(128)(4,1)}), s8[4194304]{0:T(1024)(128)(4,1)S(1)}, s32[]{:S(2)}) async-start(s8[12582912]{0:T(1024)(128)(4,1)} %bitcast.63), calls=%async_computation.5 | async-start | bytes 8388608
  89.9 6.8 %collective-permute-start.42 = (bf16[24,3072]{1,0:T(8,128)(2,1)S(1)}, bf16[24,3072]{1,0:T(8,128)(2,1)S(1)}, u32[]{:S(2)}, u32[]{:S(2)}) collective-permute-start(bf16[24,3072]{1,0:T(8,128)(2,1)S(1)} %get-tuple-element.125), channel_id=1, source_target_pairs={{2,0},{4,2},{6,4},{7,6},{5,7},{3,5},{1,3},{0,1},{10,8},{12,10},{14... | collective-permute-start | bytes 442376 | tf_op jit(solution)/shard_map/ppermute | solution.py:85
  90.4 6.8 %collective-permute-start.41 = (bf16[24,3072]{1,0:T(8,128)(2,1)S(1)}, bf16[24,3072]{1,0:T(8,128)(2,1)S(1)}, u32[]{:S(2)}, u32[]{:S(2)}) collective-permute-start(bf16[24,3072]{1,0:T(8,128)(2,1)S(1)} %get-tuple-element.126), channel_id=1, source_target_pairs={{0,2},{2,4},{4,6},{6,7},{7,5},{5,3},{3,1},{1,0},{8,10},{10,12},{12... | collective-permute-start | bytes 442376 | tf_op jit(solution)/shard_map/ppermute | solution.py:85
  92.1 7.9 %collective-permute-start.34 = (bf16[24,3072]{1,0:T(8,128)(2,1)S(1)}, bf16[24,3072]{1,0:T(8,128)(2,1)S(1)}, u32[]{:S(2)}, u32[]{:S(2)}) collective-permute-start(bf16[24,3072]{1,0:T(8,128)(2,1)S(1)} %get-tuple-element.115), channel_id=1, source_target_pairs={{2,0},{4,2},{6,4},{7,6},{5,7},{3,5},{1,3},{0,1},{10,8},{12,10},{14... | collective-permute-start | bytes 442376 | tf_op jit(solution)/shard_map/ppermute | solution.py:85
  92.5 7.8 %collective-permute-start.33 = (bf16[24,3072]{1,0:T(8,128)(2,1)S(1)}, bf16[24,3072]{1,0:T(8,128)(2,1)S(1)}, u32[]{:S(2)}, u32[]{:S(2)}) collective-permute-start(bf16[24,3072]{1,0:T(8,128)(2,1)S(1)} %get-tuple-element.116), channel_id=1, source_target_pairs={{0,2},{2,4},{4,6},{6,7},{7,5},{5,3},{3,1},{1,0},{8,10},{10,12},{12... | collective-permute-start | bytes 442376 | tf_op jit(solution)/shard_map/ppermute | solution.py:85
  97.2 10.0 %collective-permute-start.43 = (bf16[48,3072]{1,0:T(8,128)(2,1)S(1)}, bf16[48,3072]{1,0:T(8,128)(2,1)S(1)}, u32[]{:S(2)}, u32[]{:S(2)}) collective-permute-start(bf16[48,3072]{1,0:T(8,128)(2,1)S(1)} %pad_maximum_fusion.3), channel_id=1, source_target_pairs={{0,2},{2,4},{4,6},{6,7},{7,5},{5,3},{3,1},{1,0},{8,10},{10,12},{12... | collective-permute-start | bytes 884744 | tf_op jit(solution)/shard_map/ppermute | solution.py:97
  99.0 10.0 %collective-permute-start.44 = (bf16[48,3072]{1,0:T(8,128)(2,1)S(1)}, bf16[48,3072]{1,0:T(8,128)(2,1)S(1)}, u32[]{:S(2)}, u32[]{:S(2)}) collective-permute-start(bf16[48,3072]{1,0:T(8,128)(2,1)S(1)} %pad_maximum_fusion.4), channel_id=1, source_target_pairs={{2,0},{4,2},{6,4},{7,6},{5,7},{3,5},{1,3},{0,1},{10,8},{12,10},{14... | collective-permute-start | bytes 884744 | tf_op jit(solution)/shard_map/ppermute | solution.py:98
  100.4 13.2 %collective-permute-start.35 = (bf16[48,3072]{1,0:T(8,128)(2,1)S(1)}, bf16[48,3072]{1,0:T(8,128)(2,1)S(1)}, u32[]{:S(2)}, u32[]{:S(2)}) collective-permute-start(bf16[48,3072]{1,0:T(8,128)(2,1)S(1)} %pad_maximum_fusion.1), channel_id=1, source_target_pairs={{0,2},{2,4},{4,6},{6,7},{7,5},{5,3},{3,1},{1,0},{8,10},{10,12},{12... | collective-permute-start | bytes 884744 | tf_op jit(solution)/shard_map/ppermute | solution.py:97
  102.1 13.2 %collective-permute-start.36 = (bf16[48,3072]{1,0:T(8,128)(2,1)S(1)}, bf16[48,3072]{1,0:T(8,128)(2,1)S(1)}, u32[]{:S(2)}, u32[]{:S(2)}) collective-permute-start(bf16[48,3072]{1,0:T(8,128)(2,1)S(1)} %pad_maximum_fusion.2), channel_id=1, source_target_pairs={{2,0},{4,2},{6,4},{7,6},{5,7},{3,5},{1,3},{0,1},{10,8},{12,10},{14... | collective-permute-start | bytes 884744 | tf_op jit(solution)/shard_map/ppermute | solution.py:98
  109.1 9.3 %collective-permute-start.46 = (bf16[48,3072]{1,0:T(8,128)(2,1)S(1)}, bf16[48,3072]{1,0:T(8,128)(2,1)S(1)}, u32[]{:S(2)}, u32[]{:S(2)}) collective-permute-start(bf16[48,3072]{1,0:T(8,128)(2,1)S(1)} %get-tuple-element.121), channel_id=1, source_target_pairs={{2,0},{4,2},{6,4},{7,6},{5,7},{3,5},{1,3},{0,1},{10,8},{12,10},{14... | collective-permute-start | bytes 884744 | tf_op jit(solution)/shard_map/ppermute | solution.py:98
  109.6 8.9 %collective-permute-start.45 = (bf16[48,3072]{1,0:T(8,128)(2,1)S(1)}, bf16[48,3072]{1,0:T(8,128)(2,1)S(1)}, u32[]{:S(2)}, u32[]{:S(2)}) collective-permute-start(bf16[48,3072]{1,0:T(8,128)(2,1)S(1)} %get-tuple-element.122), channel_id=1, source_target_pairs={{0,2},{2,4},{4,6},{6,7},{7,5},{5,3},{3,1},{1,0},{8,10},{10,12},{12... | collective-permute-start | bytes 884744 | tf_op jit(solution)/shard_map/ppermute | solution.py:97
  115.4 6.8 %collective-permute-start.38 = (bf16[48,3072]{1,0:T(8,128)(2,1)S(1)}, bf16[48,3072]{1,0:T(8,128)(2,1)S(1)}, u32[]{:S(2)}, u32[]{:S(2)}) collective-permute-start(bf16[48,3072]{1,0:T(8,128)(2,1)S(1)} %get-tuple-element.111), channel_id=1, source_target_pairs={{2,0},{4,2},{6,4},{7,6},{5,7},{3,5},{1,3},{0,1},{10,8},{12,10},{14... | collective-permute-start | bytes 884744 | tf_op jit(solution)/shard_map/ppermute | solution.py:98
  115.8 6.7 %collective-permute-start.37 = (bf16[48,3072]{1,0:T(8,128)(2,1)S(1)}, bf16[48,3072]{1,0:T(8,128)(2,1)S(1)}, u32[]{:S(2)}, u32[]{:S(2)}) collective-permute-start(bf16[48,3072]{1,0:T(8,128)(2,1)S(1)} %get-tuple-element.112), channel_id=1, source_target_pairs={{0,2},{2,4},{4,6},{6,7},{7,5},{5,3},{3,1},{1,0},{8,10},{10,12},{12... | collective-permute-start | bytes 884744 | tf_op jit(solution)/shard_map/ppermute | solution.py:97
  118.6 6.8 %collective-permute-start.48 = (bf16[48,3072]{1,0:T(8,128)(2,1)S(1)}, bf16[48,3072]{1,0:T(8,128)(2,1)S(1)}, u32[]{:S(2)}, u32[]{:S(2)}) collective-permute-start(bf16[48,3072]{1,0:T(8,128)(2,1)S(1)} %get-tuple-element.119), channel_id=1, source_target_pairs={{2,0},{4,2},{6,4},{7,6},{5,7},{3,5},{1,3},{0,1},{10,8},{12,10},{14... | collective-permute-start | bytes 884744 | tf_op jit(solution)/shard_map/ppermute | solution.py:98
  119.7 6.7 %collective-permute-start.47 = (bf16[48,3072]{1,0:T(8,128)(2,1)S(1)}, bf16[48,3072]{1,0:T(8,128)(2,1)S(1)}, u32[]{:S(2)}, u32[]{:S(2)}) collective-permute-start(bf16[48,3072]{1,0:T(8,128)(2,1)S(1)} %get-tuple-element.120), channel_id=1, source_target_pairs={{0,2},{2,4},{4,6},{6,7},{7,5},{5,3},{3,1},{1,0},{8,10},{10,12},{12... | collective-permute-start | bytes 884744 | tf_op jit(solution)/shard_map/ppermute | solution.py:97
  122.7 6.8 %collective-permute-start.40 = (bf16[48,3072]{1,0:T(8,128)(2,1)S(1)}, bf16[48,3072]{1,0:T(8,128)(2,1)S(1)}, u32[]{:S(2)}, u32[]{:S(2)}) collective-permute-start(bf16[48,3072]{1,0:T(8,128)(2,1)S(1)} %get-tuple-element.109), channel_id=1, source_target_pairs={{2,0},{4,2},{6,4},{7,6},{5,7},{3,5},{1,3},{0,1},{10,8},{12,10},{14... | collective-permute-start | bytes 884744 | tf_op jit(solution)/shard_map/ppermute | solution.py:98
  124.3 6.7 %collective-permute-start.39 = (bf16[48,3072]{1,0:T(8,128)(2,1)S(1)}, bf16[48,3072]{1,0:T(8,128)(2,1)S(1)}, u32[]{:S(2)}, u32[]{:S(2)}) collective-permute-start(bf16[48,3072]{1,0:T(8,128)(2,1)S(1)} %get-tuple-element.110), channel_id=1, source_target_pairs={{0,2},{2,4},{4,6},{6,7},{7,5},{5,3},{3,1},{1,0},{8,10},{10,12},{12... | collective-permute-start | bytes 884744 | tf_op jit(solution)/shard_map/ppermute | solution.py:97
  131.1 0.7 copy-start.2
  131.1 0.7 copy-start.3
  131.1 3.1 %copy-start.1 = (bf16[64,6144]{1,0:T(8,128)(2,1)S(1)}, bf16[64,6144]{1,0:T(8,128)(2,1)}, u32[]{:S(2)}) copy-start(bf16[64,6144]{1,0:T(8,128)(2,1)} %param.6) | copy-start | bytes 2359300
  131.3 1.6 %collective-permute-start.49 = (bf16[24,6144]{1,0:T(8,128)(2,1)S(1)}, bf16[24,6144]{1,0:T(8,128)(2,1)S(1)}, u32[]{:S(2)}, u32[]{:S(2)}) collective-permute-start(bf16[24,6144]{1,0:T(8,128)(2,1)S(1)} %get-tuple-element.130), channel_id=1, source_target_pairs={{0,8},{8,0},{1,9},{9,1},{2,10},{10,2},{3,11},{11,3},{4,12},{12,4},... | collective-permute-start | bytes 884744 | tf_op jit(solution)/shard_map/ppermute | solution.py:103

commit v3 on v0

v3 whole, which is shorter than its diff:
```python
import jax
import jax.numpy as jnp
from jax import lax
from jax.sharding import PartitionSpec as P

CAP = 24


def ring_of(count):
    return list(range(0, count, 2)) + list(range(count - 1, 0, -2))


def routing(expert_ids, gate_probs, experts, slots):
    matches = expert_ids[:, :, None] == experts[None, None, :]
    member = jnp.any(matches, axis=1).astype(jnp.int32)
    weight = jnp.sum(jnp.where(matches, gate_probs[:, :, None], jnp.float32(0.0)), axis=1)
    slot_index = jnp.cumsum(member, axis=0) - member
    column = jnp.arange(slots)
    dispatch_map = (member[None, :, :] == 1) & (slot_index[None, :, :] == column[:, None, None])
    return (jnp.transpose(dispatch_map, (2, 0, 1)), weight)


def per_device(tokens, expert_ids, gate_probs, w_gate, w_up, w_down):
    n_tensor = lax.axis_size("tensor")
    model_width = tokens.shape[1]
    mid_col = model_width // 2
    half = n_tensor // 2
    ring = ring_of(n_tensor)
    right = [(ring[i], ring[(i + 1) % n_tensor]) for i in range(n_tensor)]
    left = [(b, a) for a, b in right]
    swap = [(0, 1), (1, 0)]

    def step(to_right, to_left):
        pair = (lax.ppermute(to_right, "tensor", right), lax.ppermute(to_left, "tensor", left))
        return lax.optimization_barrier(pair)

    me = lax.axis_index("expert")
    experts = jnp.stack([me, 1 - me])
    dispatch_map, weight = routing(expert_ids, gate_probs, experts, CAP)
    outgoing = jnp.dot(
        dispatch_map.astype(jnp.bfloat16).reshape(2 * CAP, tokens.shape[0]),
        tokens,
        preferred_element_type=jnp.float32,
    ).astype(jnp.bfloat16)
    same, away = outgoing[:CAP], outgoing[CAP:]
    other = lax.ppermute(away, "expert", swap)

    def first(perm):
        across = [(e * n_tensor + a, (1 - e) * n_tensor + b) for e in range(2) for a, b in perm]
        return lax.ppermute(away, ("expert", "tensor"), across)

    blocks = [[same, other]]
    carried = [step(same, same), lax.optimization_barrier((first(right), first(left)))]
    blocks.append([pair[side] for side in range(2) for pair in carried])
    for _ in range(half - 2):
        carried = [step(*pair) for pair in carried]
        blocks.append([pair[side] for side in range(2) for pair in carried])
    far = []
    for from_left, from_right in carried:
        pair = step(from_left[:, :mid_col], from_right[:, mid_col:])
        far.append(jnp.concatenate(pair, axis=1))
    blocks.append(far)

    def hidden_of(rows):
        gate_part = jnp.dot(rows, w_gate[0], preferred_element_type=jnp.float32)
        up_part = jnp.dot(rows, w_up[0], preferred_element_type=jnp.float32)
        return lax.optimization_barrier((jax.nn.silu(gate_part) * up_part).astype(jnp.bfloat16))

    near_hidden = hidden_of(jnp.concatenate(sum(blocks[:half - 1], []), axis=0))
    mid_hidden = hidden_of(jnp.concatenate(blocks[half - 1], axis=0))
    far_hidden = hidden_of(jnp.concatenate(far, axis=0))

    sums = []
    for cols in (slice(0, mid_col), slice(mid_col, model_width)):

        def down_of(hidden):
            part = jnp.dot(hidden, w_down[0, :, cols], preferred_element_type=jnp.float32).astype(jnp.bfloat16)
            return [part[i * 2 * CAP:(i + 1) * 2 * CAP].astype(jnp.float32) for i in range(part.shape[0] // (2 * CAP))]

        far_part = down_of(far_hidden)[0].astype(jnp.bfloat16)
        mid_parts = down_of(mid_hidden)
        own, *near_parts = down_of(near_hidden)
        to_left = near_parts[0::2] + [mid_parts[0]]
        to_right = near_parts[1::2] + [mid_parts[1]]
        got_a, got_b = step(far_part[:CAP], far_part[CAP:])
        for k in range(half - 2, -1, -1):
            got_a, got_b = got_a.astype(jnp.float32), got_b.astype(jnp.float32)
            send_a, send_b = to_right[k], to_left[k]
            if k == half - 2:
                send_a = jnp.concatenate([send_a[:CAP] + got_a, send_a[CAP:]], axis=0)
                send_b = jnp.concatenate([send_b[:CAP], send_b[CAP:] + got_b], axis=0)
            else:
                send_a = send_a + got_a
                send_b = send_b + got_b
            got_a, got_b = step(send_a.astype(jnp.bfloat16), send_b.astype(jnp.bfloat16))
        total = (own + got_a.astype(jnp.float32) + got_b.astype(jnp.float32)).astype(jnp.bfloat16)
        sums.append(jnp.stack([total[:CAP], lax.ppermute(total[CAP:], "expert", swap)]))
    returned = jnp.concatenate(sums, axis=2)
    combine = dispatch_map.astype(jnp.float32) * jnp.transpose(weight)[:, None, :]
    mixed = jnp.einsum("wcr,wcd->rd", combine, returned.astype(jnp.float32))
    return mixed.astype(jnp.bfloat16)


def solution(mesh):
    in_specs = (
        P(("groups", "expert", "tensor"), None),
        P(("groups", "expert", "tensor"), None),
        P(("groups", "expert", "tensor"), None),
        P("expert", None, "tensor"),
        P("expert", None, "tensor"),
        P("expert", "tensor", None),
    )
    out_specs = P(("groups", "expert", "tensor"), None)
    return jax.shard_map(
        per_device, mesh=mesh, in_specs=in_specs, out_specs=out_specs, check_vma=False
    )
```

time: 234 us -> 140 us (0.60)
  waiting for transfers between devices: 176 us -> 55 us
  starting transfers between devices: 0.04 us -> 34.1 us
  between operations: 13.5 us -> 0.53 us
  matrix products: 32.7 us -> 45.3 us
  blocking collectives: 10.2 us -> 0 us
    reduce_scatter x1 -> x0, waiting for transfers between devices: 92.9 us -> none  [per_device(): lax.psum_scatter(jnp.dot(hidden, down_rows, preferred_element_type=jnp.fl...]
    all_gather x1 -> x0, waiting for transfers between devices: 82.7 us -> none  [per_device(): piece = lax.all_gather(arrived_rows, 'tensor', axis=0, tiled=True)]
    ppermute x0 -> x35, waiting for transfers between devices: none -> 55 us  [the longest x15 24.5 us: step(): lax.ppermute(to_right, 'tensor', right)]
    ppermute x0 -> x35, starting transfers between devices: none -> 34.1 us  [the longest x15 25.6 us: step(): lax.ppermute(to_right, 'tensor', right)]
    dot_general x3 -> x13, matrix products: 31.4 us -> 44.1 us  [the longest x6 25.1 us: down_of(): jnp.dot(hidden, w_down[0, :, cols], preferred_element_type=jnp.float32)]
    all_to_all x2 -> x0, blocking collectives: 10.2 us -> none  [the longest x1 5.27 us: per_device(): lax.all_to_all(expert_out, 'expert', split_axis=0, concat_axis=0, tiled=T...]
  transfers between devices with their start and end apart: 2 -> 35, of which waited for: 2 -> 26; matrix products, arithmetic and copies ran while one was open for 0% -> 15% of each run, Pallas kernels for 0% -> 0%
where the time goes in v3:
time: 140 us
  waiting for transfers between devices  55 us (39%)
  matrix products  45.3 us (32%)
  starting transfers between devices  34.1 us (24%)
  local copies, waits for them, and re-layouts  2.49 us (2%)
  other arithmetic  2.2 us (2%)
    ppermute x15, starting transfers between devices, step(): lax.ppermute(to_right, 'tensor', right)  25.6 us
    dot_general x6, matrix products, down_of(): jnp.dot(hidden, w_down[0, :, cols], preferred_element_type=jnp.float32)  25.1 us
    ppermute x15, waiting for transfers between devices, step(): lax.ppermute(to_right, 'tensor', right)  24.5 us
    ppermute x15, waiting for transfers between devices, step(): lax.ppermute(to_left, 'tensor', left)  22.8 us
    dot_general x3, matrix products, hidden_of(): gate_part = jnp.dot(rows, w_gate[0], preferred_element_type=jnp.float32)  10.9 us
    dot_general x3, matrix products, hidden_of(): up_part = jnp.dot(rows, w_up[0], preferred_element_type=jnp.float32)  7.76 us
    ppermute x2, waiting for transfers between devices, first(): return lax.ppermute(away, ('expert', 'tensor'), across)  6.41 us
    ppermute x15, starting transfers between devices, step(): lax.ppermute(to_left, 'tensor', left)  5.82 us
  transfers between devices with their start and end apart: 35, of which 26 were waited for; matrix products, arithmetic and copies ran while one was open for 15% of the time, Pallas kernels for 0%

profile of v3, /device:TPU:0, one launch (start us, length us, event | category | flops | bytes accessed | tf_op | source)
XLA Modules:
  0.0 139.6 jit_solution(17134374252392027128)
XLA Ops:
  0.1 0.8 compare_reduce_fusion
  1.7 2.5 %collective-permute-start.3 = (bf16[24,6144]{1,0:T(8,128)(2,1)S(1)}, bf16[24,6144]{1,0:T(8,128)(2,1)S(1)}, u32[]{:S(2)}, u32[]{:S(2)}) collective-permute-start(bf16[24,6144]{1,0:T(8,128)(2,1)S(1)} %get-tuple-element.82), channel_id=1, source_target_pairs={{0,10},{2,12},{4,14},{6,15},{7,13},{5,11},{3,9},{1,8},{8,2},{10,4}... | collective-permute-start | bytes 884744 | tf_op jit(solution)/shard_map/ppermute | solution.py:50
  4.3 2.3 %collective-permute-start.1 = (bf16[24,6144]{1,0:T(8,128)(2,1)S(1)}, bf16[24,6144]{1,0:T(8,128)(2,1)S(1)}, u32[]{:S(2)}, u32[]{:S(2)}) collective-permute-start(bf16[24,6144]{1,0:T(8,128)(2,1)S(1)} %get-tuple-element.83), channel_id=1, source_target_pairs={{0,2},{2,4},{4,6},{6,7},{7,5},{5,3},{3,1},{1,0},{8,10},{10,12},{12... | collective-permute-start | bytes 884744 | tf_op jit(solution)/shard_map/ppermute | solution.py:34
  6.6 5.1 %collective-permute-done.3 = bf16[24,6144]{1,0:T(8,128)(2,1)S(1)} collective-permute-done((bf16[24,6144]{1,0:T(8,128)(2,1)S(1)}, bf16[24,6144]{1,0:T(8,128)(2,1)S(1)}, u32[]{:S(2)}, u32[]{:S(2)}) %collective-permute-start.3) | collective-permute-done | bytes 294944 | tf_op jit(solution)/shard_map/ppermute | solution.py:50
  11.7 1.3 collective-permute-done.4
  13.0 1.6 %collective-permute-start.7 = (bf16[24,6144]{1,0:T(8,128)(2,1)S(1)}, bf16[24,6144]{1,0:T(8,128)(2,1)S(1)}, u32[]{:S(2)}, u32[]{:S(2)}) collective-permute-start(bf16[24,6144]{1,0:T(8,128)(2,1)S(1)} %collective-permute-done.3), channel_id=1, source_target_pairs={{0,2},{2,4},{4,6},{6,7},{7,5},{5,3},{3,1},{1,0},{8,10},{10,12},{12... | collective-permute-start | bytes 884744 | tf_op jit(solution)/shard_map/ppermute | solution.py:34
  14.6 0.5 collective-permute-start.8
  15.0 3.9 %collective-permute-done.1 = bf16[24,6144]{1,0:T(8,128)(2,1)S(1)} collective-permute-done((bf16[24,6144]{1,0:T(8,128)(2,1)S(1)}, bf16[24,6144]{1,0:T(8,128)(2,1)S(1)}, u32[]{:S(2)}, u32[]{:S(2)}) %collective-permute-start.1) | collective-permute-done | bytes 294944 | tf_op jit(solution)/shard_map/ppermute | solution.py:34
  18.9 1.8 %collective-permute-done.2 = bf16[24,6144]{1,0:T(8,128)(2,1)S(1)} collective-permute-done((bf16[24,6144]{1,0:T(8,128)(2,1)S(1)}, bf16[24,6144]{1,0:T(8,128)(2,1)S(1)}, u32[]{:S(2)}, u32[]{:S(2)}) %collective-permute-start.2) | collective-permute-done | bytes 294944 | tf_op jit(solution)/shard_map/ppermute | solution.py:34
  20.7 1.6 %collective-permute-start.5 = (bf16[24,6144]{1,0:T(8,128)(2,1)S(1)}, bf16[24,6144]{1,0:T(8,128)(2,1)S(1)}, u32[]{:S(2)}, u32[]{:S(2)}) collective-permute-start(bf16[24,6144]{1,0:T(8,128)(2,1)S(1)} %collective-permute-done.1), channel_id=1, source_target_pairs={{0,2},{2,4},{4,6},{6,7},{7,5},{5,3},{3,1},{1,0},{8,10},{10,12},{12... | collective-permute-start | bytes 884744 | tf_op jit(solution)/shard_map/ppermute | solution.py:34
  22.9 2.4 %collective-permute-done.7 = bf16[24,6144]{1,0:T(8,128)(2,1)S(1)} collective-permute-done((bf16[24,6144]{1,0:T(8,128)(2,1)S(1)}, bf16[24,6144]{1,0:T(8,128)(2,1)S(1)}, u32[]{:S(2)}, u32[]{:S(2)}) %collective-permute-start.7) | collective-permute-done | bytes 294944 | tf_op jit(solution)/shard_map/ppermute | solution.py:34
  25.2 1.8 %collective-permute-done.8 = bf16[24,6144]{1,0:T(8,128)(2,1)S(1)} collective-permute-done((bf16[24,6144]{1,0:T(8,128)(2,1)S(1)}, bf16[24,6144]{1,0:T(8,128)(2,1)S(1)}, u32[]{:S(2)}, u32[]{:S(2)}) %collective-permute-start.8) | collective-permute-done | bytes 294944 | tf_op jit(solution)/shard_map/ppermute | solution.py:34
  27.0 1.6 %collective-permute-start.11 = (bf16[24,6144]{1,0:T(8,128)(2,1)S(1)}, bf16[24,6144]{1,0:T(8,128)(2,1)S(1)}, u32[]{:S(2)}, u32[]{:S(2)}) collective-permute-start(bf16[24,6144]{1,0:T(8,128)(2,1)S(1)} %collective-permute-done.7), channel_id=1, source_target_pairs={{0,2},{2,4},{4,6},{6,7},{7,5},{5,3},{3,1},{1,0},{8,10},{10,12},{12... | collective-permute-start | bytes 884744 | tf_op jit(solution)/shard_map/ppermute | solution.py:34
  29.0 2.5 %collective-permute-done.5 = bf16[24,6144]{1,0:T(8,128)(2,1)S(1)} collective-permute-done((bf16[24,6144]{1,0:T(8,128)(2,1)S(1)}, bf16[24,6144]{1,0:T(8,128)(2,1)S(1)}, u32[]{:S(2)}, u32[]{:S(2)}) %collective-permute-start.5) | collective-permute-done | bytes 294944 | tf_op jit(solution)/shard_map/ppermute | solution.py:34
  31.6 1.8 %collective-permute-done.6 = bf16[24,6144]{1,0:T(8,128)(2,1)S(1)} collective-permute-done((bf16[24,6144]{1,0:T(8,128)(2,1)S(1)}, bf16[24,6144]{1,0:T(8,128)(2,1)S(1)}, u32[]{:S(2)}, u32[]{:S(2)}) %collective-permute-start.6) | collective-permute-done | bytes 294944 | tf_op jit(solution)/shard_map/ppermute | solution.py:34
  33.3 2.0 %collective-permute-start.9 = (bf16[24,6144]{1,0:T(8,128)(2,1)S(1)}, bf16[24,6144]{1,0:T(8,128)(2,1)S(1)}, u32[]{:S(2)}, u32[]{:S(2)}) collective-permute-start(bf16[24,6144]{1,0:T(8,128)(2,1)S(1)} %collective-permute-done.5), channel_id=1, source_target_pairs={{0,2},{2,4},{4,6},{6,7},{7,5},{5,3},{3,1},{1,0},{8,10},{10,12},{12... | collective-permute-start | bytes 884744 | tf_op jit(solution)/shard_map/ppermute | solution.py:34
  35.5 6.5 %fusion.10 = f32[240,1024]{1,0:T(8,128)S(1)} fusion(bf16[240,6144]{1,0:T(8,128)(2,1)S(1)} %constant_dynamic-update-slice_fusion, bf16[1,6144,1024]{2,1,0:T(8,128)(2,1)} %param.9), kind=kOutput, calls=%fused_computation.10 | convolution fusion | flops 3019898880 | bytes 16515072 | tf_op jit(solution)/shard_map/dot_general | solution.py:65
  42.1 0.5 slice-done.4
  42.5 1.2 slice-done.5
  43.7 3.3 %fusion.52 = bf16[240,1024]{1,0:T(8,128)(2,1)S(1)} fusion(bf16[240,6144]{1,0:T(8,128)(2,1)S(1)} %constant_dynamic-update-slice_fusion, bf16[1,6144,1024]{2,1,0:T(8,128)(2,1)S(1)} %bitcast.90, f32[240,1024]{1,0:T(8,128)S(1)} %fusion.10), kind=kOutput, calls=%fused_computation.40 | convolution fusion | flops 3021373440 | bytes 17006592 | tf_op jit(solution)/shard_map/dot_general | solution.py:66
  47.1 4.6 %fusion.31 = bf16[240,3072]{1,0:T(8,128)(2,1)S(1)} fusion(bf16[240,1024]{1,0:T(8,128)(2,1)S(1)} %fusion.52, bf16[1,1024,6144]{2,1,0:T(8,128)(2,1)} %param.11), kind=kOutput, calls=%fused_computation.33 | convolution fusion | flops 1510686720 | bytes 8257536 | tf_op jit(solution)/shard_map/dot_general | solution.py:77
  51.7 4.6 %fusion.34 = bf16[240,3072]{1,0:T(8,128)(2,1)S(1)} fusion(bf16[240,1024]{1,0:T(8,128)(2,1)S(1)} %fusion.52, bf16[1,1024,6144]{2,1,0:T(8,128)(2,1)} %param.11), kind=kOutput, calls=%fused_computation.34 | convolution fusion | flops 1510686720 | bytes 8257536 | tf_op jit(solution)/shard_map/dot_general | solution.py:77
  56.6 2.1 %fusion.8 = f32[96,1024]{1,0:T(8,128)S(1)} fusion(bf16[96,6144]{1,0:T(8,128)(2,1)S(1)} %constant_dynamic-update-slice_fusion.10, bf16[1,6144,1024]{2,1,0:T(8,128)(2,1)S(1)} %bitcast.88), kind=kOutput, calls=%fused_computation.8 | convolution fusion | flops 1207959552 | bytes 14155776 | tf_op jit(solution)/shard_map/dot_general | solution.py:65
  58.8 2.1 %fusion.58 = bf16[96,1024]{1,0:T(8,128)(2,1)S(1)} fusion(bf16[96,6144]{1,0:T(8,128)(2,1)S(1)} %constant_dynamic-update-slice_fusion.10, bf16[1,6144,1024]{2,1,0:T(8,128)(2,1)S(1)} %bitcast.90, f32[96,1024]{1,0:T(8,128)S(1)} %fusion.8), kind=kOutput, calls=%fused_computation.42 | convolution fusion | flops 1208549376 | bytes 14352384 | tf_op jit(solution)/shard_map/dot_general | solution.py:66
  60.9 3.9 %fusion.37 = bf16[96,3072]{1,0:T(8,128)(2,1)S(1)} fusion(bf16[96,1024]{1,0:T(8,128)(2,1)S(1)} %fusion.58, bf16[1,1024,6144]{2,1,0:T(8,128)(2,1)} %param.11), kind=kOutput, calls=%fused_computation.35 | convolution fusion | flops 604274688 | bytes 7077888 | tf_op jit(solution)/shard_map/dot_general | solution.py:77
  64.8 3.9 %fusion.40 = bf16[96,3072]{1,0:T(8,128)(2,1)S(1)} fusion(bf16[96,1024]{1,0:T(8,128)(2,1)S(1)} %fusion.58, bf16[1,1024,6144]{2,1,0:T(8,128)(2,1)} %param.11), kind=kOutput, calls=%fused_computation.36 | convolution fusion | flops 604274688 | bytes 7077888 | tf_op jit(solution)/shard_map/dot_general | solution.py:77
  68.7 1.8 %collective-permute-start.15 = (bf16[24,3072]{1,0:T(8,128)(2,1)S(1)}, bf16[24,3072]{1,0:T(8,128)(2,1)S(1)}, u32[]{:S(2)}, u32[]{:S(2)}) collective-permute-start(bf16[24,3072]{1,0:T(8,128)(2,1)S(1)} %slice.144), channel_id=1, source_target_pairs={{0,2},{2,4},{4,6},{6,7},{7,5},{5,3},{3,1},{1,0},{8,10},{10,12},{12... | collective-permute-start | bytes 442376 | tf_op jit(solution)/shard_map/ppermute | solution.py:34
  70.5 0.4 collective-permute-start.16
  71.0 1.6 %collective-permute-start.13 = (bf16[24,3072]{1,0:T(8,128)(2,1)S(1)}, bf16[24,3072]{1,0:T(8,128)(2,1)S(1)}, u32[]{:S(2)}, u32[]{:S(2)}) collective-permute-start(bf16[24,3072]{1,0:T(8,128)(2,1)S(1)} %slice.142), channel_id=1, source_target_pairs={{0,2},{2,4},{4,6},{6,7},{7,5},{5,3},{3,1},{1,0},{8,10},{10,12},{12... | collective-permute-start | bytes 442376 | tf_op jit(solution)/shard_map/ppermute | solution.py:34
  72.6 0.4 collective-permute-start.14
  73.1 1.4 collective-permute-done.15
  74.4 1.3 collective-permute-done.16
  76.1 1.6 %collective-permute-done.14 = bf16[24,3072]{1,0:T(8,128)(2,1)S(1)} collective-permute-done((bf16[24,3072]{1,0:T(8,128)(2,1)S(1)}, bf16[24,3072]{1,0:T(8,128)(2,1)S(1)}, u32[]{:S(2)}, u32[]{:S(2)}) %collective-permute-start.14) | collective-permute-done | bytes 147488 | tf_op jit(solution)/shard_map/ppermute | solution.py:34
  77.7 2.3 %fusion.6 = f32[48,1024]{1,0:T(8,128)S(1)} fusion(bf16[1,6144,1024]{2,1,0:T(8,128)(2,1)S(1)} %bitcast.88, bf16[24,3072]{1,0:T(8,128)(2,1)S(1)} %collective-permute-done.16, bf16[24,3072]{1,0:T(8,128)(2,1)S(1)} %collective-permute-done.15, bf16[24,3072]{1,0:T(8,128)(2,1)S(1)} %collective-permute-done.14, bf16[24,3072]{1,0:T(8,128)(2,1)S(1)} %collective-permute-done.13), kind=kOutput, calls=%fused_computation.6 | convolution fusion | flops 606339072 | bytes 13369344 | tf_op jit(solution)/shard_map/dot_general | solution.py:65
  80.0 2.3 %fusion.64 = bf16[48,1024]{1,0:T(8,128)(2,1)S(1)} fusion(bf16[1,6144,1024]{2,1,0:T(8,128)(2,1)S(1)} %bitcast.90, f32[48,1024]{1,0:T(8,128)S(1)} %fusion.6, bf16[24,3072]{1,0:T(8,128)(2,1)S(1)} %collective-permute-done.16, bf16[24,3072]{1,0:T(8,128)(2,1)S(1)} %collective-permute-done.15, bf16[24,3072]{1,0:T(8,128)(2,1)S(1)} %collective-permute-done.14, ...), kind=kOutput, calls=%fused_computation.44 | convolution fusion | flops 606633984 | bytes 13467648 | tf_op jit(solution)/shard_map/dot_general | solution.py:66
  82.3 4.0 %fusion.43 = bf16[48,3072]{1,0:T(8,128)(2,1)S(1)} fusion(bf16[48,1024]{1,0:T(8,128)(2,1)S(1)} %fusion.64, bf16[1,1024,6144]{2,1,0:T(8,128)(2,1)} %param.11), kind=kOutput, calls=%fused_computation.37 | convolution fusion | flops 302137344 | bytes 6684672 | tf_op jit(solution)/shard_map/dot_general | solution.py:77
  86.3 4.0 %fusion.46 = bf16[48,3072]{1,0:T(8,128)(2,1)S(1)} fusion(bf16[48,1024]{1,0:T(8,128)(2,1)S(1)} %fusion.64, bf16[1,1024,6144]{2,1,0:T(8,128)(2,1)} %param.11), kind=kOutput, calls=%fused_computation.38 | convolution fusion | flops 302137344 | bytes 6684672 | tf_op jit(solution)/shard_map/dot_general | solution.py:77
  90.3 1.6 %collective-permute-start.17 = (bf16[24,3072]{1,0:T(8,128)(2,1)S(1)}, bf16[24,3072]{1,0:T(8,128)(2,1)S(1)}, u32[]{:S(2)}, u32[]{:S(2)}) collective-permute-start(bf16[24,3072]{1,0:T(8,128)(2,1)S(1)} %get-tuple-element.91), channel_id=1, source_target_pairs={{0,2},{2,4},{4,6},{6,7},{7,5},{5,3},{3,1},{1,0},{8,10},{10,12},{12... | collective-permute-start | bytes 442376 | tf_op jit(solution)/shard_map/ppermute | solution.py:34
  92.0 0.4 collective-permute-start.18
  92.4 1.6 %collective-permute-start.26 = (bf16[24,3072]{1,0:T(8,128)(2,1)S(1)}, bf16[24,3072]{1,0:T(8,128)(2,1)S(1)}, u32[]{:S(2)}, u32[]{:S(2)}) collective-permute-start(bf16[24,3072]{1,0:T(8,128)(2,1)S(1)} %get-tuple-element.95), channel_id=1, source_target_pairs={{0,2},{2,4},{4,6},{6,7},{7,5},{5,3},{3,1},{1,0},{8,10},{10,12},{12... | collective-permute-start | bytes 442376 | tf_op jit(solution)/shard_map/ppermute | solution.py:34
  94.1 0.4 collective-permute-start.27
  94.5 1.3 collective-permute-done.17
  95.8 2.9 %collective-permute-done.18 = bf16[24,3072]{1,0:T(8,128)(2,1)S(1)} collective-permute-done((bf16[24,3072]{1,0:T(8,128)(2,1)S(1)}, bf16[24,3072]{1,0:T(8,128)(2,1)S(1)}, u32[]{:S(2)}, u32[]{:S(2)}) %collective-permute-start.18) | collective-permute-done | bytes 147488 | tf_op jit(solution)/shard_map/ppermute | solution.py:34
  98.7 0.5 collective-permute-start.20
  99.3 1.7 %collective-permute-start.19 = (bf16[48,3072]{1,0:T(8,128)(2,1)S(1)}, bf16[48,3072]{1,0:T(8,128)(2,1)S(1)}, u32[]{:S(2)}, u32[]{:S(2)}) collective-permute-start(bf16[48,3072]{1,0:T(8,128)(2,1)S(1)} %pad_maximum_fusion), channel_id=1, source_target_pairs={{0,2},{2,4},{4,6},{6,7},{7,5},{5,3},{3,1},{1,0},{8,10},{10,12},{12... | collective-permute-start | bytes 884744 | tf_op jit(solution)/shard_map/ppermute | solution.py:34
  100.9 0.9 collective-permute-done.27
  101.9 0.5 collective-permute-start.29
  102.4 1.7 %collective-permute-start.28 = (bf16[48,3072]{1,0:T(8,128)(2,1)S(1)}, bf16[48,3072]{1,0:T(8,128)(2,1)S(1)}, u32[]{:S(2)}, u32[]{:S(2)}) collective-permute-start(bf16[48,3072]{1,0:T(8,128)(2,1)S(1)} %pad_maximum_fusion.2), channel_id=1, source_target_pairs={{0,2},{2,4},{4,6},{6,7},{7,5},{5,3},{3,1},{1,0},{8,10},{10,12},{12... | collective-permute-start | bytes 884744 | tf_op jit(solution)/shard_map/ppermute | solution.py:34
  104.1 4.7 %collective-permute-done.20 = bf16[48,3072]{1,0:T(8,128)(2,1)S(1)} collective-permute-done((bf16[48,3072]{1,0:T(8,128)(2,1)S(1)}, bf16[48,3072]{1,0:T(8,128)(2,1)S(1)}, u32[]{:S(2)}, u32[]{:S(2)}) %collective-permute-start.20) | collective-permute-done | bytes 294944 | tf_op jit(solution)/shard_map/ppermute | solution.py:34
  108.7 0.5 collective-permute-done.19
  109.4 1.6 %collective-permute-start.21 = (bf16[48,3072]{1,0:T(8,128)(2,1)S(1)}, bf16[48,3072]{1,0:T(8,128)(2,1)S(1)}, u32[]{:S(2)}, u32[]{:S(2)}) collective-permute-start(bf16[48,3072]{1,0:T(8,128)(2,1)S(1)} %get-tuple-element.72), channel_id=1, source_target_pairs={{0,2},{2,4},{4,6},{6,7},{7,5},{5,3},{3,1},{1,0},{8,10},{10,12},{12... | collective-permute-start | bytes 884744 | tf_op jit(solution)/shard_map/ppermute | solution.py:34
  111.5 3.6 %collective-permute-done.29 = bf16[48,3072]{1,0:T(8,128)(2,1)S(1)} collective-permute-done((bf16[48,3072]{1,0:T(8,128)(2,1)S(1)}, bf16[48,3072]{1,0:T(8,128)(2,1)S(1)}, u32[]{:S(2)}, u32[]{:S(2)}) %collective-permute-start.29) | collective-permute-done | bytes 294944 | tf_op jit(solution)/shard_map/ppermute | solution.py:34
  115.1 0.5 collective-permute-done.28
  115.7 1.6 %collective-permute-start.30 = (bf16[48,3072]{1,0:T(8,128)(2,1)S(1)}, bf16[48,3072]{1,0:T(8,128)(2,1)S(1)}, u32[]{:S(2)}, u32[]{:S(2)}) collective-permute-start(bf16[48,3072]{1,0:T(8,128)(2,1)S(1)} %get-tuple-element.76), channel_id=1, source_target_pairs={{0,2},{2,4},{4,6},{6,7},{7,5},{5,3},{3,1},{1,0},{8,10},{10,12},{12... | collective-permute-start | bytes 884744 | tf_op jit(solution)/shard_map/ppermute | solution.py:34
  117.8 4.1 %collective-permute-done.21 = bf16[48,3072]{1,0:T(8,128)(2,1)S(1)} collective-permute-done((bf16[48,3072]{1,0:T(8,128)(2,1)S(1)}, bf16[48,3072]{1,0:T(8,128)(2,1)S(1)}, u32[]{:S(2)}, u32[]{:S(2)}) %collective-permute-start.21) | collective-permute-done | bytes 294944 | tf_op jit(solution)/shard_map/ppermute | solution.py:34
  122.1 1.6 %collective-permute-start.23 = (bf16[48,3072]{1,0:T(8,128)(2,1)S(1)}, bf16[48,3072]{1,0:T(8,128)(2,1)S(1)}, u32[]{:S(2)}, u32[]{:S(2)}) collective-permute-start(bf16[48,3072]{1,0:T(8,128)(2,1)S(1)} %get-tuple-element.70), channel_id=1, source_target_pairs={{0,2},{2,4},{4,6},{6,7},{7,5},{5,3},{3,1},{1,0},{8,10},{10,12},{12... | collective-permute-start | bytes 884744 | tf_op jit(solution)/shard_map/ppermute | solution.py:34
  124.2 4.1 %collective-permute-done.30 = bf16[48,3072]{1,0:T(8,128)(2,1)S(1)} collective-permute-done((bf16[48,3072]{1,0:T(8,128)(2,1)S(1)}, bf16[48,3072]{1,0:T(8,128)(2,1)S(1)}, u32[]{:S(2)}, u32[]{:S(2)}) %collective-permute-start.30) | collective-permute-done | bytes 294944 | tf_op jit(solution)/shard_map/ppermute | solution.py:34
  128.4 1.6 %collective-permute-start.32 = (bf16[48,3072]{1,0:T(8,128)(2,1)S(1)}, bf16[48,3072]{1,0:T(8,128)(2,1)S(1)}, u32[]{:S(2)}, u32[]{:S(2)}) collective-permute-start(bf16[48,3072]{1,0:T(8,128)(2,1)S(1)} %get-tuple-element.74), channel_id=1, source_target_pairs={{0,2},{2,4},{4,6},{6,7},{7,5},{5,3},{3,1},{1,0},{8,10},{10,12},{12... | collective-permute-start | bytes 884744 | tf_op jit(solution)/shard_map/ppermute | solution.py:34
  130.5 1.4 %collective-permute-done.23 = bf16[48,3072]{1,0:T(8,128)(2,1)S(1)} collective-permute-done((bf16[48,3072]{1,0:T(8,128)(2,1)S(1)}, bf16[48,3072]{1,0:T(8,128)(2,1)S(1)}, u32[]{:S(2)}, u32[]{:S(2)}) %collective-permute-start.23) | collective-permute-done | bytes 294944 | tf_op jit(solution)/shard_map/ppermute | solution.py:34
  131.9 0.9 collective-permute-done.24
  133.0 2.1 %collective-permute-done.32 = bf16[48,3072]{1,0:T(8,128)(2,1)S(1)} collective-permute-done((bf16[48,3072]{1,0:T(8,128)(2,1)S(1)}, bf16[48,3072]{1,0:T(8,128)(2,1)S(1)}, u32[]{:S(2)}, u32[]{:S(2)}) %collective-permute-start.32) | collective-permute-done | bytes 294944 | tf_op jit(solution)/shard_map/ppermute | solution.py:34
  135.1 1.6 %collective-permute-done.33 = bf16[48,3072]{1,0:T(8,128)(2,1)S(1)} collective-permute-done((bf16[48,3072]{1,0:T(8,128)(2,1)S(1)}, bf16[48,3072]{1,0:T(8,128)(2,1)S(1)}, u32[]{:S(2)}, u32[]{:S(2)}) %collective-permute-start.33) | collective-permute-done | bytes 294944 | tf_op jit(solution)/shard_map/ppermute | solution.py:34
  137.1 1.3 collective-permute-done.34
  138.3 1.3 fusion.12
  (89 shorter events, 5.7 us)
Async XLA Ops:
  0.0 1.4 copy-start
  1.7 9.9 %collective-permute-start.3 = (bf16[24,6144]{1,0:T(8,128)(2,1)S(1)}, bf16[24,6144]{1,0:T(8,128)(2,1)S(1)}, u32[]{:S(2)}, u32[]{:S(2)}) collective-permute-start(bf16[24,6144]{1,0:T(8,128)(2,1)S(1)} %get-tuple-element.82), channel_id=1, source_target_pairs={{0,10},{2,12},{4,14},{6,15},{7,13},{5,11},{3,9},{1,8},{8,2},{10,4}... | collective-permute-start | bytes 884744 | tf_op jit(solution)/shard_map/ppermute | solution.py:50
  4.3 8.7 %collective-permute-start.4 = (bf16[24,6144]{1,0:T(8,128)(2,1)S(1)}, bf16[24,6144]{1,0:T(8,128)(2,1)S(1)}, u32[]{:S(2)}, u32[]{:S(2)}) collective-permute-start(bf16[24,6144]{1,0:T(8,128)(2,1)S(1)} %get-tuple-element.82), channel_id=1, source_target_pairs={{2,8},{4,10},{6,12},{7,14},{5,15},{3,13},{1,11},{0,9},{10,0},{12,2... | collective-permute-start | bytes 884744 | tf_op jit(solution)/shard_map/ppermute | solution.py:50
  4.3 14.7 %collective-permute-start.1 = (bf16[24,6144]{1,0:T(8,128)(2,1)S(1)}, bf16[24,6144]{1,0:T(8,128)(2,1)S(1)}, u32[]{:S(2)}, u32[]{:S(2)}) collective-permute-start(bf16[24,6144]{1,0:T(8,128)(2,1)S(1)} %get-tuple-element.83), channel_id=1, source_target_pairs={{0,2},{2,4},{4,6},{6,7},{7,5},{5,3},{3,1},{1,0},{8,10},{10,12},{12... | collective-permute-start | bytes 884744 | tf_op jit(solution)/shard_map/ppermute | solution.py:34
  6.6 14.1 %collective-permute-start.2 = (bf16[24,6144]{1,0:T(8,128)(2,1)S(1)}, bf16[24,6144]{1,0:T(8,128)(2,1)S(1)}, u32[]{:S(2)}, u32[]{:S(2)}) collective-permute-start(bf16[24,6144]{1,0:T(8,128)(2,1)S(1)} %get-tuple-element.83), channel_id=1, source_target_pairs={{2,0},{4,2},{6,4},{7,6},{5,7},{3,5},{1,3},{0,1},{10,8},{12,10},{14... | collective-permute-start | bytes 884744 | tf_op jit(solution)/shard_map/ppermute | solution.py:34
  6.6 16.2 %collective-permute-start = (bf16[24,6144]{1,0:T(8,128)(2,1)S(1)}, bf16[24,6144]{1,0:T(8,128)(2,1)S(1)}, u32[]{:S(2)}, u32[]{:S(2)}) collective-permute-start(bf16[24,6144]{1,0:T(8,128)(2,1)S(1)} %get-tuple-element.82), channel_id=1, source_target_pairs={{0,8},{8,0},{1,9},{9,1},{2,10},{10,2},{3,11},{11,3},{4,12},{12,4},... | collective-permute-start | bytes 884744 | tf_op jit(solution)/shard_map/ppermute | solution.py:46
  13.0 12.3 %collective-permute-start.7 = (bf16[24,6144]{1,0:T(8,128)(2,1)S(1)}, bf16[24,6144]{1,0:T(8,128)(2,1)S(1)}, u32[]{:S(2)}, u32[]{:S(2)}) collective-permute-start(bf16[24,6144]{1,0:T(8,128)(2,1)S(1)} %collective-permute-done.3), channel_id=1, source_target_pairs={{0,2},{2,4},{4,6},{6,7},{7,5},{5,3},{3,1},{1,0},{8,10},{10,12},{12... | collective-permute-start | bytes 884744 | tf_op jit(solution)/shard_map/ppermute | solution.py:34
  14.6 12.5 %collective-permute-start.8 = (bf16[24,6144]{1,0:T(8,128)(2,1)S(1)}, bf16[24,6144]{1,0:T(8,128)(2,1)S(1)}, u32[]{:S(2)}, u32[]{:S(2)}) collective-permute-start(bf16[24,6144]{1,0:T(8,128)(2,1)S(1)} %collective-permute-done.4), channel_id=1, source_target_pairs={{2,0},{4,2},{6,4},{7,6},{5,7},{3,5},{1,3},{0,1},{10,8},{12,10},{14... | collective-permute-start | bytes 884744 | tf_op jit(solution)/shard_map/ppermute | solution.py:34
  20.7 10.9 %collective-permute-start.5 = (bf16[24,6144]{1,0:T(8,128)(2,1)S(1)}, bf16[24,6144]{1,0:T(8,128)(2,1)S(1)}, u32[]{:S(2)}, u32[]{:S(2)}) collective-permute-start(bf16[24,6144]{1,0:T(8,128)(2,1)S(1)} %collective-permute-done.1), channel_id=1, source_target_pairs={{0,2},{2,4},{4,6},{6,7},{7,5},{5,3},{3,1},{1,0},{8,10},{10,12},{12... | collective-permute-start | bytes 884744 | tf_op jit(solution)/shard_map/ppermute | solution.py:34
  22.3 11.1 %collective-permute-start.6 = (bf16[24,6144]{1,0:T(8,128)(2,1)S(1)}, bf16[24,6144]{1,0:T(8,128)(2,1)S(1)}, u32[]{:S(2)}, u32[]{:S(2)}) collective-permute-start(bf16[24,6144]{1,0:T(8,128)(2,1)S(1)} %collective-permute-done.2), channel_id=1, source_target_pairs={{2,0},{4,2},{6,4},{7,6},{5,7},{3,5},{1,3},{0,1},{10,8},{12,10},{14... | collective-permute-start | bytes 884744 | tf_op jit(solution)/shard_map/ppermute | solution.py:34
  27.0 29.4 %collective-permute-start.11 = (bf16[24,6144]{1,0:T(8,128)(2,1)S(1)}, bf16[24,6144]{1,0:T(8,128)(2,1)S(1)}, u32[]{:S(2)}, u32[]{:S(2)}) collective-permute-start(bf16[24,6144]{1,0:T(8,128)(2,1)S(1)} %collective-permute-done.7), channel_id=1, source_target_pairs={{0,2},{2,4},{4,6},{6,7},{7,5},{5,3},{3,1},{1,0},{8,10},{10,12},{12... | collective-permute-start | bytes 884744 | tf_op jit(solution)/shard_map/ppermute | solution.py:34
  28.6 27.8 %collective-permute-start.12 = (bf16[24,6144]{1,0:T(8,128)(2,1)S(1)}, bf16[24,6144]{1,0:T(8,128)(2,1)S(1)}, u32[]{:S(2)}, u32[]{:S(2)}) collective-permute-start(bf16[24,6144]{1,0:T(8,128)(2,1)S(1)} %collective-permute-done.8), channel_id=1, source_target_pairs={{2,0},{4,2},{6,4},{7,6},{5,7},{3,5},{1,3},{0,1},{10,8},{12,10},{14... | collective-permute-start | bytes 884744 | tf_op jit(solution)/shard_map/ppermute | solution.py:34
  33.3 23.0 %collective-permute-start.10 = (bf16[24,6144]{1,0:T(8,128)(2,1)S(1)}, bf16[24,6144]{1,0:T(8,128)(2,1)S(1)}, u32[]{:S(2)}, u32[]{:S(2)}) collective-permute-start(bf16[24,6144]{1,0:T(8,128)(2,1)S(1)} %collective-permute-done.6), channel_id=1, source_target_pairs={{2,0},{4,2},{6,4},{7,6},{5,7},{3,5},{1,3},{0,1},{10,8},{12,10},{14... | collective-permute-start | bytes 884744 | tf_op jit(solution)/shard_map/ppermute | solution.py:34
  33.3 23.0 %collective-permute-start.9 = (bf16[24,6144]{1,0:T(8,128)(2,1)S(1)}, bf16[24,6144]{1,0:T(8,128)(2,1)S(1)}, u32[]{:S(2)}, u32[]{:S(2)}) collective-permute-start(bf16[24,6144]{1,0:T(8,128)(2,1)S(1)} %collective-permute-done.5), channel_id=1, source_target_pairs={{0,2},{2,4},{4,6},{6,7},{7,5},{5,3},{3,1},{1,0},{8,10},{10,12},{12... | collective-permute-start | bytes 884744 | tf_op jit(solution)/shard_map/ppermute | solution.py:34
  35.5 6.6 %slice-start.3 = ((s8[12582912]{0:T(1024)(128)(4,1)}), s8[4194304]{0:T(1024)(128)(4,1)S(1)}, s32[]{:S(2)}) async-start(s8[12582912]{0:T(1024)(128)(4,1)} %bitcast.89), calls=%async_computation.3 | async-start | bytes 8388608
  35.5 7.0 %slice-start.4 = ((s8[12582912]{0:T(1024)(128)(4,1)}), s8[4194304]{0:T(1024)(128)(4,1)S(1)}, s32[]{:S(2)}) async-start(s8[12582912]{0:T(1024)(128)(4,1)} %bitcast.89), calls=%async_computation.4 | async-start | bytes 8388608
  35.5 8.2 %slice-start.5 = ((s8[12582912]{0:T(1024)(128)(4,1)}), s8[4194304]{0:T(1024)(128)(4,1)S(1)}, s32[]{:S(2)}) async-start(s8[12582912]{0:T(1024)(128)(4,1)} %bitcast.89), calls=%async_computation.5 | async-start | bytes 8388608
  47.1 9.6 %slice-start = ((s8[12582912]{0:T(1024)(128)(4,1)}), s8[4194304]{0:T(1024)(128)(4,1)S(1)}, s32[]{:S(2)}) async-start(s8[12582912]{0:T(1024)(128)(4,1)} %bitcast.87), calls=%async_computation | async-start | bytes 8388608
  47.1 9.5 %slice-start.1 = ((s8[12582912]{0:T(1024)(128)(4,1)}), s8[4194304]{0:T(1024)(128)(4,1)S(1)}, s32[]{:S(2)}) async-start(s8[12582912]{0:T(1024)(128)(4,1)} %bitcast.87), calls=%async_computation.1 | async-start | bytes 8388608
  51.7 4.9 %slice-start.2 = ((s8[12582912]{0:T(1024)(128)(4,1)}), s8[4194304]{0:T(1024)(128)(4,1)S(1)}, s32[]{:S(2)}) async-start(s8[12582912]{0:T(1024)(128)(4,1)} %bitcast.87), calls=%async_computation.2 | async-start | bytes 8388608
  68.7 5.7 %collective-permute-start.15 = (bf16[24,3072]{1,0:T(8,128)(2,1)S(1)}, bf16[24,3072]{1,0:T(8,128)(2,1)S(1)}, u32[]{:S(2)}, u32[]{:S(2)}) collective-permute-start(bf16[24,3072]{1,0:T(8,128)(2,1)S(1)} %slice.144), channel_id=1, source_target_pairs={{0,2},{2,4},{4,6},{6,7},{7,5},{5,3},{3,1},{1,0},{8,10},{10,12},{12... | collective-permute-start | bytes 442376 | tf_op jit(solution)/shard_map/ppermute | solution.py:34
  70.5 5.2 %collective-permute-start.16 = (bf16[24,3072]{1,0:T(8,128)(2,1)S(1)}, bf16[24,3072]{1,0:T(8,128)(2,1)S(1)}, u32[]{:S(2)}, u32[]{:S(2)}) collective-permute-start(bf16[24,3072]{1,0:T(8,128)(2,1)S(1)} %slice.145), channel_id=1, source_target_pairs={{2,0},{4,2},{6,4},{7,6},{5,7},{3,5},{1,3},{0,1},{10,8},{12,10},{14... | collective-permute-start | bytes 442376 | tf_op jit(solution)/shard_map/ppermute | solution.py:34
  71.0 5.1 %collective-permute-start.13 = (bf16[24,3072]{1,0:T(8,128)(2,1)S(1)}, bf16[24,3072]{1,0:T(8,128)(2,1)S(1)}, u32[]{:S(2)}, u32[]{:S(2)}) collective-permute-start(bf16[24,3072]{1,0:T(8,128)(2,1)S(1)} %slice.142), channel_id=1, source_target_pairs={{0,2},{2,4},{4,6},{6,7},{7,5},{5,3},{3,1},{1,0},{8,10},{10,12},{12... | collective-permute-start | bytes 442376 | tf_op jit(solution)/shard_map/ppermute | solution.py:34
  72.6 5.1 %collective-permute-start.14 = (bf16[24,3072]{1,0:T(8,128)(2,1)S(1)}, bf16[24,3072]{1,0:T(8,128)(2,1)S(1)}, u32[]{:S(2)}, u32[]{:S(2)}) collective-permute-start(bf16[24,3072]{1,0:T(8,128)(2,1)S(1)} %slice.143), channel_id=1, source_target_pairs={{2,0},{4,2},{6,4},{7,6},{5,7},{3,5},{1,3},{0,1},{10,8},{12,10},{14... | collective-permute-start | bytes 442376 | tf_op jit(solution)/shard_map/ppermute | solution.py:34
  90.3 5.4 %collective-permute-start.17 = (bf16[24,3072]{1,0:T(8,128)(2,1)S(1)}, bf16[24,3072]{1,0:T(8,128)(2,1)S(1)}, u32[]{:S(2)}, u32[]{:S(2)}) collective-permute-start(bf16[24,3072]{1,0:T(8,128)(2,1)S(1)} %get-tuple-element.91), channel_id=1, source_target_pairs={{0,2},{2,4},{4,6},{6,7},{7,5},{5,3},{3,1},{1,0},{8,10},{10,12},{12... | collective-permute-start | bytes 442376 | tf_op jit(solution)/shard_map/ppermute | solution.py:34
  92.0 6.7 %collective-permute-start.18 = (bf16[24,3072]{1,0:T(8,128)(2,1)S(1)}, bf16[24,3072]{1,0:T(8,128)(2,1)S(1)}, u32[]{:S(2)}, u32[]{:S(2)}) collective-permute-start(bf16[24,3072]{1,0:T(8,128)(2,1)S(1)} %get-tuple-element.90), channel_id=1, source_target_pairs={{2,0},{4,2},{6,4},{7,6},{5,7},{3,5},{1,3},{0,1},{10,8},{12,10},{14... | collective-permute-start | bytes 442376 | tf_op jit(solution)/shard_map/ppermute | solution.py:34
  92.4 8.5 %collective-permute-start.26 = (bf16[24,3072]{1,0:T(8,128)(2,1)S(1)}, bf16[24,3072]{1,0:T(8,128)(2,1)S(1)}, u32[]{:S(2)}, u32[]{:S(2)}) collective-permute-start(bf16[24,3072]{1,0:T(8,128)(2,1)S(1)} %get-tuple-element.95), channel_id=1, source_target_pairs={{0,2},{2,4},{4,6},{6,7},{7,5},{5,3},{3,1},{1,0},{8,10},{10,12},{12... | collective-permute-start | bytes 442376 | tf_op jit(solution)/shard_map/ppermute | solution.py:34
  94.1 7.7 %collective-permute-start.27 = (bf16[24,3072]{1,0:T(8,128)(2,1)S(1)}, bf16[24,3072]{1,0:T(8,128)(2,1)S(1)}, u32[]{:S(2)}, u32[]{:S(2)}) collective-permute-start(bf16[24,3072]{1,0:T(8,128)(2,1)S(1)} %get-tuple-element.94), channel_id=1, source_target_pairs={{2,0},{4,2},{6,4},{7,6},{5,7},{3,5},{1,3},{0,1},{10,8},{12,10},{14... | collective-permute-start | bytes 442376 | tf_op jit(solution)/shard_map/ppermute | solution.py:34
  98.7 10.0 %collective-permute-start.20 = (bf16[48,3072]{1,0:T(8,128)(2,1)S(1)}, bf16[48,3072]{1,0:T(8,128)(2,1)S(1)}, u32[]{:S(2)}, u32[]{:S(2)}) collective-permute-start(bf16[48,3072]{1,0:T(8,128)(2,1)S(1)} %pad_maximum_fusion.1), channel_id=1, source_target_pairs={{2,0},{4,2},{6,4},{7,6},{5,7},{3,5},{1,3},{0,1},{10,8},{12,10},{14... | collective-permute-start | bytes 884744 | tf_op jit(solution)/shard_map/ppermute | solution.py:34
  99.3 10.0 %collective-permute-start.19 = (bf16[48,3072]{1,0:T(8,128)(2,1)S(1)}, bf16[48,3072]{1,0:T(8,128)(2,1)S(1)}, u32[]{:S(2)}, u32[]{:S(2)}) collective-permute-start(bf16[48,3072]{1,0:T(8,128)(2,1)S(1)} %pad_maximum_fusion), channel_id=1, source_target_pairs={{0,2},{2,4},{4,6},{6,7},{7,5},{5,3},{3,1},{1,0},{8,10},{10,12},{12... | collective-permute-start | bytes 884744 | tf_op jit(solution)/shard_map/ppermute | solution.py:34
  101.9 13.2 %collective-permute-start.29 = (bf16[48,3072]{1,0:T(8,128)(2,1)S(1)}, bf16[48,3072]{1,0:T(8,128)(2,1)S(1)}, u32[]{:S(2)}, u32[]{:S(2)}) collective-permute-start(bf16[48,3072]{1,0:T(8,128)(2,1)S(1)} %pad_maximum_fusion.3), channel_id=1, source_target_pairs={{2,0},{4,2},{6,4},{7,6},{5,7},{3,5},{1,3},{0,1},{10,8},{12,10},{14... | collective-permute-start | bytes 884744 | tf_op jit(solution)/shard_map/ppermute | solution.py:34
  102.4 13.2 %collective-permute-start.28 = (bf16[48,3072]{1,0:T(8,128)(2,1)S(1)}, bf16[48,3072]{1,0:T(8,128)(2,1)S(1)}, u32[]{:S(2)}, u32[]{:S(2)}) collective-permute-start(bf16[48,3072]{1,0:T(8,128)(2,1)S(1)} %pad_maximum_fusion.2), channel_id=1, source_target_pairs={{0,2},{2,4},{4,6},{6,7},{7,5},{5,3},{3,1},{1,0},{8,10},{10,12},{12... | collective-permute-start | bytes 884744 | tf_op jit(solution)/shard_map/ppermute | solution.py:34
  109.4 12.5 %collective-permute-start.21 = (bf16[48,3072]{1,0:T(8,128)(2,1)S(1)}, bf16[48,3072]{1,0:T(8,128)(2,1)S(1)}, u32[]{:S(2)}, u32[]{:S(2)}) collective-permute-start(bf16[48,3072]{1,0:T(8,128)(2,1)S(1)} %get-tuple-element.72), channel_id=1, source_target_pairs={{0,2},{2,4},{4,6},{6,7},{7,5},{5,3},{3,1},{1,0},{8,10},{10,12},{12... | collective-permute-start | bytes 884744 | tf_op jit(solution)/shard_map/ppermute | solution.py:34
  111.1 10.8 %collective-permute-start.22 = (bf16[48,3072]{1,0:T(8,128)(2,1)S(1)}, bf16[48,3072]{1,0:T(8,128)(2,1)S(1)}, u32[]{:S(2)}, u32[]{:S(2)}) collective-permute-start(bf16[48,3072]{1,0:T(8,128)(2,1)S(1)} %get-tuple-element.71), channel_id=1, source_target_pairs={{2,0},{4,2},{6,4},{7,6},{5,7},{3,5},{1,3},{0,1},{10,8},{12,10},{14... | collective-permute-start | bytes 884744 | tf_op jit(solution)/shard_map/ppermute | solution.py:34
  115.7 12.5 %collective-permute-start.30 = (bf16[48,3072]{1,0:T(8,128)(2,1)S(1)}, bf16[48,3072]{1,0:T(8,128)(2,1)S(1)}, u32[]{:S(2)}, u32[]{:S(2)}) collective-permute-start(bf16[48,3072]{1,0:T(8,128)(2,1)S(1)} %get-tuple-element.76), channel_id=1, source_target_pairs={{0,2},{2,4},{4,6},{6,7},{7,5},{5,3},{3,1},{1,0},{8,10},{10,12},{12... | collective-permute-start | bytes 884744 | tf_op jit(solution)/shard_map/ppermute | solution.py:34
  117.4 10.8 %collective-permute-start.31 = (bf16[48,3072]{1,0:T(8,128)(2,1)S(1)}, bf16[48,3072]{1,0:T(8,128)(2,1)S(1)}, u32[]{:S(2)}, u32[]{:S(2)}) collective-permute-start(bf16[48,3072]{1,0:T(8,128)(2,1)S(1)} %get-tuple-element.75), channel_id=1, source_target_pairs={{2,0},{4,2},{6,4},{7,6},{5,7},{3,5},{1,3},{0,1},{10,8},{12,10},{14... | collective-permute-start | bytes 884744 | tf_op jit(solution)/shard_map/ppermute | solution.py:34
  122.0 14.9 %copy-start.2 = (s32[64,2]{0,1:T(2,128)S(1)}, s32[64,2]{0,1:T(2,128)}, u32[]{:S(2)}) copy-start(s32[64,2]{0,1:T(2,128)} %param.7) | copy-start | bytes 1540
  122.1 14.9 %copy-start.3 = (f32[64,2]{0,1:T(2,128)S(1)}, f32[64,2]{0,1:T(2,128)}, u32[]{:S(2)}) copy-start(f32[64,2]{0,1:T(2,128)} %param.8) | copy-start | bytes 1540
  122.1 9.8 %collective-permute-start.23 = (bf16[48,3072]{1,0:T(8,128)(2,1)S(1)}, bf16[48,3072]{1,0:T(8,128)(2,1)S(1)}, u32[]{:S(2)}, u32[]{:S(2)}) collective-permute-start(bf16[48,3072]{1,0:T(8,128)(2,1)S(1)} %get-tuple-element.70), channel_id=1, source_target_pairs={{0,2},{2,4},{4,6},{6,7},{7,5},{5,3},{3,1},{1,0},{8,10},{10,12},{12... | collective-permute-start | bytes 884744 | tf_op jit(solution)/shard_map/ppermute | solution.py:34
  123.7 9.1 %collective-permute-start.24 = (bf16[48,3072]{1,0:T(8,128)(2,1)S(1)}, bf16[48,3072]{1,0:T(8,128)(2,1)S(1)}, u32[]{:S(2)}, u32[]{:S(2)}) collective-permute-start(bf16[48,3072]{1,0:T(8,128)(2,1)S(1)} %get-tuple-element.69), channel_id=1, source_target_pairs={{2,0},{4,2},{6,4},{7,6},{5,7},{3,5},{1,3},{0,1},{10,8},{12,10},{14... | collective-permute-start | bytes 884744 | tf_op jit(solution)/shard_map/ppermute | solution.py:34
  128.2 11.4 %copy-start.1 = (bf16[64,6144]{1,0:T(8,128)(2,1)S(1)}, bf16[64,6144]{1,0:T(8,128)(2,1)}, u32[]{:S(2)}) copy-start(bf16[64,6144]{1,0:T(8,128)(2,1)} %param.6) | copy-start | bytes 2359300
  128.4 6.8 %collective-permute-start.32 = (bf16[48,3072]{1,0:T(8,128)(2,1)S(1)}, bf16[48,3072]{1,0:T(8,128)(2,1)S(1)}, u32[]{:S(2)}, u32[]{:S(2)}) collective-permute-start(bf16[48,3072]{1,0:T(8,128)(2,1)S(1)} %get-tuple-element.74), channel_id=1, source_target_pairs={{0,2},{2,4},{4,6},{6,7},{7,5},{5,3},{3,1},{1,0},{8,10},{10,12},{12... | collective-permute-start | bytes 884744 | tf_op jit(solution)/shard_map/ppermute | solution.py:34
  130.0 6.7 %collective-permute-start.33 = (bf16[48,3072]{1,0:T(8,128)(2,1)S(1)}, bf16[48,3072]{1,0:T(8,128)(2,1)S(1)}, u32[]{:S(2)}, u32[]{:S(2)}) collective-permute-start(bf16[48,3072]{1,0:T(8,128)(2,1)S(1)} %get-tuple-element.73), channel_id=1, source_target_pairs={{2,0},{4,2},{6,4},{7,6},{5,7},{3,5},{1,3},{0,1},{10,8},{12,10},{14... | collective-permute-start | bytes 884744 | tf_op jit(solution)/shard_map/ppermute | solution.py:34
  132.9 4.1 %collective-permute-start.25 = (bf16[24,3072]{1,0:T(8,128)(2,1)S(1)}, bf16[24,3072]{1,0:T(8,128)(2,1)S(1)}, u32[]{:S(2)}, u32[]{:S(2)}) collective-permute-start(bf16[24,3072]{1,0:T(8,128)(2,1)S(1)} %get-tuple-element.89), channel_id=1, source_target_pairs={{0,8},{8,0},{1,9},{9,1},{2,10},{10,2},{3,11},{11,3},{4,12},{12,4},... | collective-permute-start | bytes 442376 | tf_op jit(solution)/shard_map/ppermute | solution.py:97
  136.9 1.4 %collective-permute-start.34 = (bf16[24,3072]{1,0:T(8,128)(2,1)S(1)}, bf16[24,3072]{1,0:T(8,128)(2,1)S(1)}, u32[]{:S(2)}, u32[]{:S(2)}) collective-permute-start(bf16[24,3072]{1,0:T(8,128)(2,1)S(1)} %get-tuple-element.93), channel_id=1, source_target_pairs={{0,8},{8,0},{1,9},{9,1},{2,10},{10,2},{3,11},{11,3},{4,12},{12,4},... | collective-permute-start | bytes 442376 | tf_op jit(solution)/shard_map/ppermute | solution.py:97

commit v4 on v3

v4 whole, which is shorter than its diff:
```python
import jax
import jax.numpy as jnp
from jax import lax
from jax.experimental import pallas as pl
from jax.experimental.pallas import tpu as pltpu
from jax.sharding import PartitionSpec as P

CAP = 24


def ring_of(count):
    return list(range(0, count, 2)) + list(range(count - 1, 0, -2))


def routing(expert_ids, gate_probs, experts, slots):
    matches = expert_ids[:, :, None] == experts[None, None, :]
    member = jnp.any(matches, axis=1).astype(jnp.int32)
    weight = jnp.sum(jnp.where(matches, gate_probs[:, :, None], jnp.float32(0.0)), axis=1)
    slot_index = jnp.cumsum(member, axis=0) - member
    column = jnp.arange(slots)
    dispatch_map = (member[None, :, :] == 1) & (slot_index[None, :, :] == column[:, None, None])
    return (jnp.transpose(dispatch_map, (2, 0, 1)), weight)


CHEAP = pl.CostEstimate(flops=1024, bytes_accessed=1024, transcendentals=0)
PARAMS = pltpu.CompilerParams(dimension_semantics=("arbitrary",), vmem_limit_bytes=12 * 2**20)


def gate_kernel(rows, weights, out):
    part = jnp.dot(rows[...], weights[0], preferred_element_type=jnp.float32)

    @pl.when(pl.program_id(0) == 0)
    def _():
        out[...] = part

    @pl.when(pl.program_id(0) > 0)
    def _():
        out[...] += part


def up_kernel(rows, weights, gate, out, total):
    part = jnp.dot(rows[...], weights[0], preferred_element_type=jnp.float32)

    @pl.when(pl.program_id(0) == 0)
    def _():
        total[...] = part

    @pl.when(pl.program_id(0) > 0)
    def _():
        total[...] += part

    @pl.when(pl.program_id(0) == pl.num_programs(0) - 1)
    def _():
        value = gate[...]
        out[...] = (value / (1.0 + jnp.exp(-value)) * total[...]).astype(out.dtype)


def down_kernel(hidden, weights, out):
    out[...] = jnp.dot(hidden[...], weights[0], preferred_element_type=jnp.float32).astype(out.dtype)


def gate_product(rows, w_gate):
    count, depth = rows.shape
    units = w_gate.shape[2]
    return pl.pallas_call(
        gate_kernel,
        grid=(depth // 512,),
        in_specs=[
            pl.BlockSpec((count, 512), lambda k: (0, k)),
            pl.BlockSpec((1, 512, units), lambda k: (0, k, 0)),
        ],
        out_specs=pl.BlockSpec((count, units), lambda k: (0, 0)),
        out_shape=jax.ShapeDtypeStruct((count, units), jnp.float32),
        cost_estimate=CHEAP,
        compiler_params=PARAMS,
        name="gate_product",
    )(rows, pltpu.with_memory_space_constraint(w_gate, pltpu.HBM))


def up_product(rows, w_up, gate):
    count, depth = rows.shape
    units = w_up.shape[2]
    return pl.pallas_call(
        up_kernel,
        grid=(depth // 512,),
        in_specs=[
            pl.BlockSpec((count, 512), lambda k: (0, k)),
            pl.BlockSpec((1, 512, units), lambda k: (0, k, 0)),
            pl.BlockSpec((count, units), lambda k: (0, 0)),
        ],
        out_specs=pl.BlockSpec((count, units), lambda k: (0, 0)),
        out_shape=jax.ShapeDtypeStruct((count, units), jnp.bfloat16),
        scratch_shapes=[pltpu.VMEM((count, units), jnp.float32)],
        cost_estimate=CHEAP,
        compiler_params=PARAMS,
        name="up_product",
    )(rows, pltpu.with_memory_space_constraint(w_up, pltpu.HBM), gate)


def down_product(hidden, w_down, start, width):
    count, units = hidden.shape
    return pl.pallas_call(
        down_kernel,
        grid=(width // 512,),
        in_specs=[
            pl.BlockSpec((count, units), lambda j: (0, 0)),
            pl.BlockSpec((1, units, 512), lambda j: (0, 0, j + start // 512)),
        ],
        out_specs=pl.BlockSpec((count, 512), lambda j: (0, j)),
        out_shape=jax.ShapeDtypeStruct((count, width), jnp.bfloat16),
        cost_estimate=CHEAP,
        compiler_params=PARAMS,
        name="down_product",
    )(hidden, pltpu.with_memory_space_constraint(w_down, pltpu.HBM))


def per_device(tokens, expert_ids, gate_probs, w_gate, w_up, w_down):
    n_tensor = lax.axis_size("tensor")
    model_width = tokens.shape[1]
    mid_col = model_width // 2
    half = n_tensor // 2
    ring = ring_of(n_tensor)
    right = [(ring[i], ring[(i + 1) % n_tensor]) for i in range(n_tensor)]
    left = [(b, a) for a, b in right]
    swap = [(0, 1), (1, 0)]

    def step(to_right, to_left):
        pair = (lax.ppermute(to_right, "tensor", right), lax.ppermute(to_left, "tensor", left))
        return lax.optimization_barrier(pair)

    me = lax.axis_index("expert")
    experts = jnp.stack([me, 1 - me])
    dispatch_map, weight = routing(expert_ids, gate_probs, experts, CAP)
    outgoing = jnp.dot(
        dispatch_map.astype(jnp.bfloat16).reshape(2 * CAP, tokens.shape[0]),
        tokens,
        preferred_element_type=jnp.float32,
    ).astype(jnp.bfloat16)
    same, away = outgoing[:CAP], outgoing[CAP:]
    other = lax.ppermute(away, "expert", swap)

    def first(perm):
        across = [(e * n_tensor + a, (1 - e) * n_tensor + b) for e in range(2) for a, b in perm]
        return lax.ppermute(away, ("expert", "tensor"), across)

    blocks = [[same, other]]
    carried = [step(same, same), lax.optimization_barrier((first(right), first(left)))]
    blocks.append([pair[side] for side in range(2) for pair in carried])
    for _ in range(half - 3):
        carried = [step(*pair) for pair in carried]
        blocks.append([pair[side] for side in range(2) for pair in carried])

    near = jnp.concatenate(sum(blocks, []), axis=0)
    near_gate = gate_product(near, w_gate)
    held, near_gate = lax.optimization_barrier((carried[1], near_gate))
    carried = [step(*carried[0]), step(*held)]
    blocks.append([pair[side] for side in range(2) for pair in carried])
    near, held = lax.optimization_barrier((near, carried[1]))
    near_hidden = up_product(near, w_up, near_gate)
    far = []
    for from_left, from_right in (carried[0], held):
        pair = step(from_left[:, :mid_col], from_right[:, mid_col:])
        far.append(jnp.concatenate(pair, axis=1))

    rest = jnp.concatenate(blocks[half - 1] + far, axis=0)
    rest, near_hidden = lax.optimization_barrier((rest, near_hidden))
    rest_gate = jnp.dot(rest, w_gate[0], preferred_element_type=jnp.float32)
    rest_up = jnp.dot(rest, w_up[0], preferred_element_type=jnp.float32)
    rest_hidden = lax.optimization_barrier((jax.nn.silu(rest_gate) * rest_up).astype(jnp.bfloat16))

    def block_of(part, index):
        return part[index * 2 * CAP:(index + 1) * 2 * CAP]

    rest_part, near_part, got = [], [], []
    for start in (0, mid_col):
        part = down_product(rest_hidden, w_down, start, mid_col)
        rest_part.append(part)
        far_part = block_of(part, 2)
        got.append(step(far_part[:CAP], far_part[CAP:]))

    def sending(chunk, distance):
        got_a, got_b = (part.astype(jnp.float32) for part in got[chunk])
        if distance == half - 1:
            send_b, send_a = (block_of(rest_part[chunk], side).astype(jnp.float32) for side in range(2))
            send_a = jnp.concatenate([send_a[:CAP] + got_a, send_a[CAP:]], axis=0)
            send_b = jnp.concatenate([send_b[:CAP], send_b[CAP:] + got_b], axis=0)
        else:
            send_b, send_a = (block_of(near_part[chunk], 2 * distance - 1 + side).astype(jnp.float32) for side in range(2))
            send_a = send_a + got_a
            send_b = send_b + got_b
        return send_a.astype(jnp.bfloat16), send_b.astype(jnp.bfloat16)

    def near_down(chunk, after):
        hidden, after = lax.optimization_barrier((near_hidden, after))
        near_part.append(down_product(hidden, w_down, chunk * mid_col, mid_col))
        return after

    got[0] = step(*sending(0, half - 1))
    got[1] = near_down(0, got[1])
    second = sending(1, half - 1)
    second, near_part[0] = lax.optimization_barrier((second, near_part[0]))
    got[1] = step(*second)
    got[0] = near_down(1, got[0])
    for distance in range(half - 2, 0, -1):
        first_pair = sending(0, distance)
        if distance == half - 2:
            first_pair, near_part[1] = lax.optimization_barrier((first_pair, near_part[1]))
        got[0] = step(*first_pair)
        got[1] = step(*sending(1, distance))
    sums = []
    for chunk in range(2):
        got_a, got_b = (part.astype(jnp.float32) for part in got[chunk])
        total = (block_of(near_part[chunk], 0).astype(jnp.float32) + got_a + got_b).astype(jnp.bfloat16)
        sums.append(jnp.stack([total[:CAP], lax.ppermute(total[CAP:], "expert", swap)]))
    returned = jnp.concatenate(sums, axis=2)
    combine = dispatch_map.astype(jnp.float32) * jnp.transpose(weight)[:, None, :]
    mixed = jnp.einsum("wcr,wcd->rd", combine, returned.astype(jnp.float32))
    return mixed.astype(jnp.bfloat16)


def solution(mesh):
    in_specs = (
        P(("groups", "expert", "tensor"), None),
        P(("groups", "expert", "tensor"), None),
        P(("groups", "expert", "tensor"), None),
        P("expert", None, "tensor"),
        P("expert", None, "tensor"),
        P("expert", "tensor", None),
    )
    out_specs = P(("groups", "expert", "tensor"), None)
    return jax.shard_map(
        per_device, mesh=mesh, in_specs=in_specs, out_specs=out_specs, check_vma=False
    )
```

time: 140 us -> 147 us (1.050)
  Pallas kernels: 0 us -> 46 us
  matrix products: 45.3 us -> 5.75 us
    pallas_call x0 -> x6, Pallas kernels: none -> 46 us  [the longest x4 21.7 us: down_product(): pl.pallas_call(down_kernel, grid=(width // 512,), in_specs=[pl.BlockSpec(...]
    dot_general x12 -> x2, matrix products: 43.8 us -> 4.18 us  [the longest x1 2.15 us: per_device(): rest_up = jnp.dot(rest, w_up[0], preferred_element_type=jnp.float32)]
    ppermute x2, waiting for transfers between devices: 6.41 us -> 2.17 us  [first(): return lax.ppermute(away, ('expert', 'tensor'), across)]
    ppermute x15, starting transfers between devices: 5.82 us -> 9.69 us  [step(): lax.ppermute(to_left, 'tensor', left)]
    ppermute x15, starting transfers between devices: 25.6 us -> 22.6 us  [step(): lax.ppermute(to_right, 'tensor', right)]
    ppermute x15, waiting for transfers between devices: 24.5 us -> 27.2 us  [step(): lax.ppermute(to_right, 'tensor', right)]
  transfers between devices with their start and end apart: 35 -> 35, of which waited for: 26 -> 21; matrix products, arithmetic and copies ran while one was open for 15% -> 1% of each run, Pallas kernels for 0% -> 24%
where the time goes in v4:
time: 147 us; the launch traced here: 146 us
  waiting for transfers between devices  53.8 us (37%)
  Pallas kernels  46 us (31%)
  starting transfers between devices  34.6 us (24%)
  matrix products  5.75 us (4%)
  local copies, waits for them, and re-layouts  3.32 us (2%)
  other arithmetic  2.24 us (2%)
    ppermute x15, waiting for transfers between devices, step(): lax.ppermute(to_right, 'tensor', right)  27.2 us
    ppermute x15, waiting for transfers between devices, step(): lax.ppermute(to_left, 'tensor', left)  23.2 us
    ppermute x15, starting transfers between devices, step(): lax.ppermute(to_right, 'tensor', right)  22.6 us
    pallas_call x4, Pallas kernels, down_product(): pl.pallas_call(down_kernel, grid=(width // 512,), in_specs=[pl.BlockSpec(...  21.7 us
    pallas_call x1, Pallas kernels, gate_product(): pl.pallas_call(gate_kernel, grid=(depth // 512,), in_specs=[pl.BlockSpec(...  12.3 us
    pallas_call x1, Pallas kernels, up_product(): pl.pallas_call(up_kernel, grid=(depth // 512,), in_specs=[pl.BlockSpec((c...  11.9 us
    ppermute x15, starting transfers between devices, step(): lax.ppermute(to_left, 'tensor', left)  9.69 us
  transfers between devices with their start and end apart: 35, of which 21 were waited for; matrix products, arithmetic and copies ran while one was open for 1% of the time, Pallas kernels for 24%

profile of v4, /device:TPU:0, one launch (start us, length us, event | category | flops | bytes accessed | tf_op | source)
XLA Modules:
  0.0 146.2 jit_solution(2998938021688442712)
XLA Ops:
  0.1 0.8 compare_reduce_fusion
  1.4 0.3 convolution_convert_fusion
  1.7 3.1 %collective-permute-start = (bf16[24,6144]{1,0:T(8,128)(2,1)S(1)}, bf16[24,6144]{1,0:T(8,128)(2,1)S(1)}, u32[]{:S(2)}, u32[]{:S(2)}) collective-permute-start(bf16[24,6144]{1,0:T(8,128)(2,1)S(1)} %get-tuple-element.131), channel_id=1, source_target_pairs={{0,2},{2,4},{4,6},{6,7},{7,5},{5,3},{3,1},{1,0},{8,10},{10,12},{12... | collective-permute-start | bytes 884744 | tf_op jit(solution)/shard_map/ppermute | solution.py:128
  4.8 2.1 %collective-permute-start.6 = (bf16[24,6144]{1,0:T(8,128)(2,1)S(1)}, bf16[24,6144]{1,0:T(8,128)(2,1)S(1)}, u32[]{:S(2)}, u32[]{:S(2)}) collective-permute-start(bf16[24,6144]{1,0:T(8,128)(2,1)S(1)} %get-tuple-element.130), channel_id=1, source_target_pairs={{0,10},{2,12},{4,14},{6,15},{7,13},{5,11},{3,9},{1,8},{8,2},{10,4}... | collective-permute-start | bytes 884744 | tf_op jit(solution)/shard_map/ppermute | solution.py:144
  7.0 5.6 %collective-permute-done = bf16[24,6144]{1,0:T(8,128)(2,1)S(1)} collective-permute-done((bf16[24,6144]{1,0:T(8,128)(2,1)S(1)}, bf16[24,6144]{1,0:T(8,128)(2,1)S(1)}, u32[]{:S(2)}, u32[]{:S(2)}) %collective-permute-start) | collective-permute-done | bytes 294944 | tf_op jit(solution)/shard_map/ppermute | solution.py:128
  12.6 2.2 %collective-permute-done.1 = bf16[24,6144]{1,0:T(8,128)(2,1)S(1)} collective-permute-done((bf16[24,6144]{1,0:T(8,128)(2,1)S(1)}, bf16[24,6144]{1,0:T(8,128)(2,1)S(1)}, u32[]{:S(2)}, u32[]{:S(2)}) %collective-permute-start.1) | collective-permute-done | bytes 294944 | tf_op jit(solution)/shard_map/ppermute | solution.py:128
  14.8 1.6 %collective-permute-start.2 = (bf16[24,6144]{1,0:T(8,128)(2,1)S(1)}, bf16[24,6144]{1,0:T(8,128)(2,1)S(1)}, u32[]{:S(2)}, u32[]{:S(2)}) collective-permute-start(bf16[24,6144]{1,0:T(8,128)(2,1)S(1)} %collective-permute-done), channel_id=1, source_target_pairs={{0,2},{2,4},{4,6},{6,7},{7,5},{5,3},{3,1},{1,0},{8,10},{10,12},{12... | collective-permute-start | bytes 884744 | tf_op jit(solution)/shard_map/ppermute | solution.py:128
  16.4 2.2 %collective-permute-done.6 = bf16[24,6144]{1,0:T(8,128)(2,1)S(1)} collective-permute-done((bf16[24,6144]{1,0:T(8,128)(2,1)S(1)}, bf16[24,6144]{1,0:T(8,128)(2,1)S(1)}, u32[]{:S(2)}, u32[]{:S(2)}) %collective-permute-start.6) | collective-permute-done | bytes 294944 | tf_op jit(solution)/shard_map/ppermute | solution.py:144
  18.6 1.6 %collective-permute-start.8 = (bf16[24,6144]{1,0:T(8,128)(2,1)S(1)}, bf16[24,6144]{1,0:T(8,128)(2,1)S(1)}, u32[]{:S(2)}, u32[]{:S(2)}) collective-permute-start(bf16[24,6144]{1,0:T(8,128)(2,1)S(1)} %collective-permute-done.6), channel_id=1, source_target_pairs={{0,2},{2,4},{4,6},{6,7},{7,5},{5,3},{3,1},{1,0},{8,10},{10,12},{12... | collective-permute-start | bytes 884744 | tf_op jit(solution)/shard_map/ppermute | solution.py:128
  20.2 0.5 collective-permute-start.3
  20.7 0.6 collective-permute-start.9
  21.3 3.9 %collective-permute-done.2 = bf16[24,6144]{1,0:T(8,128)(2,1)S(1)} collective-permute-done((bf16[24,6144]{1,0:T(8,128)(2,1)S(1)}, bf16[24,6144]{1,0:T(8,128)(2,1)S(1)}, u32[]{:S(2)}, u32[]{:S(2)}) %collective-permute-start.2) | collective-permute-done | bytes 294944 | tf_op jit(solution)/shard_map/ppermute | solution.py:128
  25.2 4.9 %collective-permute-done.3 = bf16[24,6144]{1,0:T(8,128)(2,1)S(1)} collective-permute-done((bf16[24,6144]{1,0:T(8,128)(2,1)S(1)}, bf16[24,6144]{1,0:T(8,128)(2,1)S(1)}, u32[]{:S(2)}, u32[]{:S(2)}) %collective-permute-start.3) | collective-permute-done | bytes 294944 | tf_op jit(solution)/shard_map/ppermute | solution.py:128
  30.1 1.6 %collective-permute-start.4 = (bf16[24,6144]{1,0:T(8,128)(2,1)S(1)}, bf16[24,6144]{1,0:T(8,128)(2,1)S(1)}, u32[]{:S(2)}, u32[]{:S(2)}) collective-permute-start(bf16[24,6144]{1,0:T(8,128)(2,1)S(1)} %collective-permute-done.2), channel_id=1, source_target_pairs={{0,2},{2,4},{4,6},{6,7},{7,5},{5,3},{3,1},{1,0},{8,10},{10,12},{12... | collective-permute-start | bytes 884744 | tf_op jit(solution)/shard_map/ppermute | solution.py:128
  31.7 4.6 %collective-permute-done.9 = bf16[24,6144]{1,0:T(8,128)(2,1)S(1)} collective-permute-done((bf16[24,6144]{1,0:T(8,128)(2,1)S(1)}, bf16[24,6144]{1,0:T(8,128)(2,1)S(1)}, u32[]{:S(2)}, u32[]{:S(2)}) %collective-permute-start.9) | collective-permute-done | bytes 294944 | tf_op jit(solution)/shard_map/ppermute | solution.py:128
  36.3 0.4 collective-permute-start.5
  36.9 12.3 %gate_product.1.gate = f32[240,1024]{1,0:T(8,128)S(1)} custom-call(bf16[240,6144]{1,0:T(8,128)(2,1)S(1)} %constant_dynamic-update-slice_fusion.rows, bf16[1,6144,1024]{2,1,0:T(8,128)(2,1)} %weights.6), custom_call_target="tpu_custom_call" | custom-call | flops 1024 | bytes 1024 | tf_op jit(solution)/shard_map/gate_product/pallas_call | solution.py:65
  49.2 1.6 %collective-permute-start.11 = (bf16[24,6144]{1,0:T(8,128)(2,1)S(1)}, bf16[24,6144]{1,0:T(8,128)(2,1)S(1)}, u32[]{:S(2)}, u32[]{:S(2)}) collective-permute-start(bf16[24,6144]{1,0:T(8,128)(2,1)S(1)} %collective-permute-done.8), channel_id=1, source_target_pairs={{0,2},{2,4},{4,6},{6,7},{7,5},{5,3},{3,1},{1,0},{8,10},{10,12},{12... | collective-permute-start | bytes 884744 | tf_op jit(solution)/shard_map/ppermute | solution.py:128
  50.9 0.4 collective-permute-start.12
  51.4 6.6 %collective-permute-done.11 = bf16[24,6144]{1,0:T(8,128)(2,1)S(1)} collective-permute-done((bf16[24,6144]{1,0:T(8,128)(2,1)S(1)}, bf16[24,6144]{1,0:T(8,128)(2,1)S(1)}, u32[]{:S(2)}, u32[]{:S(2)}) %collective-permute-start.11) | collective-permute-done | bytes 294944 | tf_op jit(solution)/shard_map/ppermute | solution.py:128
  57.9 1.3 collective-permute-done.12
  59.2 1.6 %collective-permute-start.15 = (bf16[24,3072]{1,0:T(8,128)(2,1)S(1)}, bf16[24,3072]{1,0:T(8,128)(2,1)S(1)}, u32[]{:S(2)}, u32[]{:S(2)}) collective-permute-start(bf16[24,3072]{1,0:T(8,128)(2,1)S(1)} %slice.134), channel_id=1, source_target_pairs={{0,2},{2,4},{4,6},{6,7},{7,5},{5,3},{3,1},{1,0},{8,10},{10,12},{12... | collective-permute-start | bytes 442376 | tf_op jit(solution)/shard_map/ppermute | solution.py:128
  60.9 0.5 collective-permute-start.16
  61.5 1.6 %collective-permute-start.13 = (bf16[24,3072]{1,0:T(8,128)(2,1)S(1)}, bf16[24,3072]{1,0:T(8,128)(2,1)S(1)}, u32[]{:S(2)}, u32[]{:S(2)}) collective-permute-start(bf16[24,3072]{1,0:T(8,128)(2,1)S(1)} %slice.132), channel_id=1, source_target_pairs={{0,2},{2,4},{4,6},{6,7},{7,5},{5,3},{3,1},{1,0},{8,10},{10,12},{12... | collective-permute-start | bytes 442376 | tf_op jit(solution)/shard_map/ppermute | solution.py:128
  63.1 0.4 collective-permute-start.14
  63.6 11.9 %up_product.1.hidden = bf16[240,1024]{1,0:T(8,128)(2,1)S(1)} custom-call(bf16[240,6144]{1,0:T(8,128)(2,1)S(1)} %constant_dynamic-update-slice_fusion.rows, bf16[1,6144,1024]{2,1,0:T(8,128)(2,1)} %weights.7, f32[240,1024]{1,0:T(8,128)S(1)} %gate_product.1.gate), custom_call_target="tpu_custom_call" | custom-call | flops 1024 | bytes 1024 | tf_op jit(solution)/shard_map/up_product/pallas_call | solution.py:83
  75.7 2.0 %fusion.2 = f32[144,1024]{1,0:T(8,128)S(1)} fusion(bf16[144,6144]{1,0:T(8,128)(2,1)S(1)} %maximum_dynamic-update-slice_fusion, bf16[1,6144,1024]{2,1,0:T(8,128)(2,1)S(1)} %bitcast.38), kind=kOutput, calls=%fused_computation.2 | convolution fusion | flops 1811939328 | bytes 14942208 | tf_op jit(solution)/shard_map/dot_general | solution.py:167
  77.8 1.3 slice-done.4
  79.1 1.2 slice-done.5
  80.3 2.1 %fusion.8.hidden = bf16[144,1024]{1,0:T(8,128)(2,1)S(1)} fusion(bf16[144,6144]{1,0:T(8,128)(2,1)S(1)} %maximum_dynamic-update-slice_fusion, bf16[1,6144,1024]{2,1,0:T(8,128)(2,1)S(1)} %bitcast.40, f32[144,1024]{1,0:T(8,128)S(1)} %fusion.2), kind=kOutput, calls=%fused_computation.8 | convolution fusion | flops 1812824064 | bytes 15237120 | tf_op jit(solution)/shard_map/dot_general | solution.py:168
  82.4 5.2 %down_product.6 = bf16[144,3072]{1,0:T(8,128)(2,1)S(1)} custom-call(bf16[144,1024]{1,0:T(8,128)(2,1)S(1)} %fusion.8.hidden, bf16[1,1024,6144]{2,1,0:T(8,128)(2,1)} %weights.11), custom_call_target="tpu_custom_call" | custom-call | flops 1024 | bytes 1024 | tf_op jit(solution)/shard_map/down_product/pallas_call | solution.py:102
  87.7 5.3 %down_product.4 = bf16[144,3072]{1,0:T(8,128)(2,1)S(1)} custom-call(bf16[144,1024]{1,0:T(8,128)(2,1)S(1)} %fusion.8.hidden, bf16[1,1024,6144]{2,1,0:T(8,128)(2,1)} %weights.11), custom_call_target="tpu_custom_call" | custom-call | flops 1024 | bytes 1024 | tf_op jit(solution)/shard_map/down_product/pallas_call | solution.py:102
  93.0 1.6 %collective-permute-start.19 = (bf16[24,3072]{1,0:T(8,128)(2,1)S(1)}, bf16[24,3072]{1,0:T(8,128)(2,1)S(1)}, u32[]{:S(2)}, u32[]{:S(2)}) collective-permute-start(bf16[24,3072]{1,0:T(8,128)(2,1)S(1)} %get-tuple-element.120), channel_id=1, source_target_pairs={{0,2},{2,4},{4,6},{6,7},{7,5},{5,3},{3,1},{1,0},{8,10},{10,12},{12... | collective-permute-start | bytes 442376 | tf_op jit(solution)/shard_map/ppermute | solution.py:128
  94.6 0.4 collective-permute-start.20
  95.1 1.6 %collective-permute-start.17 = (bf16[24,3072]{1,0:T(8,128)(2,1)S(1)}, bf16[24,3072]{1,0:T(8,128)(2,1)S(1)}, u32[]{:S(2)}, u32[]{:S(2)}) collective-permute-start(bf16[24,3072]{1,0:T(8,128)(2,1)S(1)} %get-tuple-element.126), channel_id=1, source_target_pairs={{0,2},{2,4},{4,6},{6,7},{7,5},{5,3},{3,1},{1,0},{8,10},{10,12},{12... | collective-permute-start | bytes 442376 | tf_op jit(solution)/shard_map/ppermute | solution.py:128
  96.7 0.4 collective-permute-start.18
  97.2 1.0 collective-permute-done.19
  98.2 2.8 %collective-permute-done.20 = bf16[24,3072]{1,0:T(8,128)(2,1)S(1)} collective-permute-done((bf16[24,3072]{1,0:T(8,128)(2,1)S(1)}, bf16[24,3072]{1,0:T(8,128)(2,1)S(1)}, u32[]{:S(2)}, u32[]{:S(2)}) %collective-permute-start.20) | collective-permute-done | bytes 147488 | tf_op jit(solution)/shard_map/ppermute | solution.py:128
  101.1 0.5 collective-permute-start.22
  101.6 1.6 %collective-permute-start.21 = (bf16[48,3072]{1,0:T(8,128)(2,1)S(1)}, bf16[48,3072]{1,0:T(8,128)(2,1)S(1)}, u32[]{:S(2)}, u32[]{:S(2)}) collective-permute-start(bf16[48,3072]{1,0:T(8,128)(2,1)S(1)} %pad_maximum_fusion.2), channel_id=1, source_target_pairs={{0,2},{2,4},{4,6},{6,7},{7,5},{5,3},{3,1},{1,0},{8,10},{10,12},{12... | collective-permute-start | bytes 884744 | tf_op jit(solution)/shard_map/ppermute | solution.py:128
  103.3 0.9 collective-permute-done.18
  104.2 5.6 %down_product.5 = bf16[240,3072]{1,0:T(8,128)(2,1)S(1)} custom-call(bf16[240,1024]{1,0:T(8,128)(2,1)S(1)} %up_product.1.hidden, bf16[1,1024,6144]{2,1,0:T(8,128)(2,1)} %weights.11), custom_call_target="tpu_custom_call" | custom-call | flops 1024 | bytes 1024 | tf_op jit(solution)/shard_map/down_product/pallas_call | solution.py:102
  109.9 1.6 %collective-permute-start.28 = (bf16[48,3072]{1,0:T(8,128)(2,1)S(1)}, bf16[48,3072]{1,0:T(8,128)(2,1)S(1)}, u32[]{:S(2)}, u32[]{:S(2)}) collective-permute-start(bf16[48,3072]{1,0:T(8,128)(2,1)S(1)} %get-tuple-element.101), channel_id=1, source_target_pairs={{0,2},{2,4},{4,6},{6,7},{7,5},{5,3},{3,1},{1,0},{8,10},{10,12},{12... | collective-permute-start | bytes 884744 | tf_op jit(solution)/shard_map/ppermute | solution.py:128
  111.4 0.5 collective-permute-start.29
  112.0 0.1 add_convert_fusion.8
  112.1 5.6 %down_product.7 = bf16[240,3072]{1,0:T(8,128)(2,1)S(1)} custom-call(bf16[240,1024]{1,0:T(8,128)(2,1)S(1)} %up_product.1.hidden, bf16[1,1024,6144]{2,1,0:T(8,128)(2,1)} %weights.11), custom_call_target="tpu_custom_call" | custom-call | flops 1024 | bytes 1024 | tf_op jit(solution)/shard_map/down_product/pallas_call | solution.py:102
  117.7 1.6 %collective-permute-start.23 = (bf16[48,3072]{1,0:T(8,128)(2,1)S(1)}, bf16[48,3072]{1,0:T(8,128)(2,1)S(1)}, u32[]{:S(2)}, u32[]{:S(2)}) collective-permute-start(bf16[48,3072]{1,0:T(8,128)(2,1)S(1)} %get-tuple-element.94), channel_id=1, source_target_pairs={{0,2},{2,4},{4,6},{6,7},{7,5},{5,3},{3,1},{1,0},{8,10},{10,12},{12... | collective-permute-start | bytes 884744 | tf_op jit(solution)/shard_map/ppermute | solution.py:128
  119.3 0.5 collective-permute-start.24
  119.8 1.4 collective-permute-done.29
  121.5 1.9 %collective-permute-start.31 = (bf16[48,3072]{1,0:T(8,128)(2,1)S(1)}, bf16[48,3072]{1,0:T(8,128)(2,1)S(1)}, u32[]{:S(2)}, u32[]{:S(2)}) collective-permute-start(bf16[48,3072]{1,0:T(8,128)(2,1)S(1)} %get-tuple-element.113), channel_id=1, source_target_pairs={{2,0},{4,2},{6,4},{7,6},{5,7},{3,5},{1,3},{0,1},{10,8},{12,10},{14... | collective-permute-start | bytes 884744 | tf_op jit(solution)/shard_map/ppermute | solution.py:128
  123.5 4.3 %collective-permute-done.23 = bf16[48,3072]{1,0:T(8,128)(2,1)S(1)} collective-permute-done((bf16[48,3072]{1,0:T(8,128)(2,1)S(1)}, bf16[48,3072]{1,0:T(8,128)(2,1)S(1)}, u32[]{:S(2)}, u32[]{:S(2)}) %collective-permute-start.23) | collective-permute-done | bytes 294944 | tf_op jit(solution)/shard_map/ppermute | solution.py:128
  127.7 1.5 %collective-permute-done.24 = bf16[48,3072]{1,0:T(8,128)(2,1)S(1)} collective-permute-done((bf16[48,3072]{1,0:T(8,128)(2,1)S(1)}, bf16[48,3072]{1,0:T(8,128)(2,1)S(1)}, u32[]{:S(2)}, u32[]{:S(2)}) %collective-permute-start.24) | collective-permute-done | bytes 294944 | tf_op jit(solution)/shard_map/ppermute | solution.py:128
  129.4 0.9 collective-permute-start.25
  130.3 1.2 collective-permute-start.26
  131.5 2.6 %collective-permute-done.30 = bf16[48,3072]{1,0:T(8,128)(2,1)S(1)} collective-permute-done((bf16[48,3072]{1,0:T(8,128)(2,1)S(1)}, bf16[48,3072]{1,0:T(8,128)(2,1)S(1)}, u32[]{:S(2)}, u32[]{:S(2)}) %collective-permute-start.30) | collective-permute-done | bytes 294944 | tf_op jit(solution)/shard_map/ppermute | solution.py:128
  134.1 1.5 %collective-permute-done.31 = bf16[48,3072]{1,0:T(8,128)(2,1)S(1)} collective-permute-done((bf16[48,3072]{1,0:T(8,128)(2,1)S(1)}, bf16[48,3072]{1,0:T(8,128)(2,1)S(1)}, u32[]{:S(2)}, u32[]{:S(2)}) %collective-permute-start.31) | collective-permute-done | bytes 294944 | tf_op jit(solution)/shard_map/ppermute | solution.py:128
  135.7 0.9 collective-permute-start.32
  136.6 1.2 collective-permute-start.33
  137.8 0.8 collective-permute-done.25
  138.6 1.2 collective-permute-done.26
  140.0 2.5 %collective-permute-done.32 = bf16[48,3072]{1,0:T(8,128)(2,1)S(1)} collective-permute-done((bf16[48,3072]{1,0:T(8,128)(2,1)S(1)}, bf16[48,3072]{1,0:T(8,128)(2,1)S(1)}, u32[]{:S(2)}, u32[]{:S(2)}) %collective-permute-start.32) | collective-permute-done | bytes 294944 | tf_op jit(solution)/shard_map/ppermute | solution.py:128
  142.5 0.8 collective-permute-done.33
  143.7 1.3 collective-permute-done.34
  144.9 1.3 fusion.4
  (84 shorter events, 2.4 us)
Async XLA Ops:
  0.0 1.4 copy-start
  1.7 10.9 %collective-permute-start = (bf16[24,6144]{1,0:T(8,128)(2,1)S(1)}, bf16[24,6144]{1,0:T(8,128)(2,1)S(1)}, u32[]{:S(2)}, u32[]{:S(2)}) collective-permute-start(bf16[24,6144]{1,0:T(8,128)(2,1)S(1)} %get-tuple-element.131), channel_id=1, source_target_pairs={{0,2},{2,4},{4,6},{6,7},{7,5},{5,3},{3,1},{1,0},{8,10},{10,12},{12... | collective-permute-start | bytes 884744 | tf_op jit(solution)/shard_map/ppermute | solution.py:128
  4.8 9.9 %collective-permute-start.1 = (bf16[24,6144]{1,0:T(8,128)(2,1)S(1)}, bf16[24,6144]{1,0:T(8,128)(2,1)S(1)}, u32[]{:S(2)}, u32[]{:S(2)}) collective-permute-start(bf16[24,6144]{1,0:T(8,128)(2,1)S(1)} %get-tuple-element.131), channel_id=1, source_target_pairs={{2,0},{4,2},{6,4},{7,6},{5,7},{3,5},{1,3},{0,1},{10,8},{12,10},{14... | collective-permute-start | bytes 884744 | tf_op jit(solution)/shard_map/ppermute | solution.py:128
  4.8 11.5 %collective-permute-start.10 = (bf16[24,6144]{1,0:T(8,128)(2,1)S(1)}, bf16[24,6144]{1,0:T(8,128)(2,1)S(1)}, u32[]{:S(2)}, u32[]{:S(2)}) collective-permute-start(bf16[24,6144]{1,0:T(8,128)(2,1)S(1)} %get-tuple-element.130), channel_id=1, source_target_pairs={{0,8},{8,0},{1,9},{9,1},{2,10},{10,2},{3,11},{11,3},{4,12},{12,4},... | collective-permute-start | bytes 884744 | tf_op jit(solution)/shard_map/ppermute | solution.py:140
  4.8 13.7 %collective-permute-start.6 = (bf16[24,6144]{1,0:T(8,128)(2,1)S(1)}, bf16[24,6144]{1,0:T(8,128)(2,1)S(1)}, u32[]{:S(2)}, u32[]{:S(2)}) collective-permute-start(bf16[24,6144]{1,0:T(8,128)(2,1)S(1)} %get-tuple-element.130), channel_id=1, source_target_pairs={{0,10},{2,12},{4,14},{6,15},{7,13},{5,11},{3,9},{1,8},{8,2},{10,4}... | collective-permute-start | bytes 884744 | tf_op jit(solution)/shard_map/ppermute | solution.py:144
  7.0 11.6 %collective-permute-start.7 = (bf16[24,6144]{1,0:T(8,128)(2,1)S(1)}, bf16[24,6144]{1,0:T(8,128)(2,1)S(1)}, u32[]{:S(2)}, u32[]{:S(2)}) collective-permute-start(bf16[24,6144]{1,0:T(8,128)(2,1)S(1)} %get-tuple-element.130), channel_id=1, source_target_pairs={{2,8},{4,10},{6,12},{7,14},{5,15},{3,13},{1,11},{0,9},{10,0},{12,2... | collective-permute-start | bytes 884744 | tf_op jit(solution)/shard_map/ppermute | solution.py:144
  14.8 10.5 %collective-permute-start.2 = (bf16[24,6144]{1,0:T(8,128)(2,1)S(1)}, bf16[24,6144]{1,0:T(8,128)(2,1)S(1)}, u32[]{:S(2)}, u32[]{:S(2)}) collective-permute-start(bf16[24,6144]{1,0:T(8,128)(2,1)S(1)} %collective-permute-done), channel_id=1, source_target_pairs={{0,2},{2,4},{4,6},{6,7},{7,5},{5,3},{3,1},{1,0},{8,10},{10,12},{12... | collective-permute-start | bytes 884744 | tf_op jit(solution)/shard_map/ppermute | solution.py:128
  18.6 13.1 %collective-permute-start.8 = (bf16[24,6144]{1,0:T(8,128)(2,1)S(1)}, bf16[24,6144]{1,0:T(8,128)(2,1)S(1)}, u32[]{:S(2)}, u32[]{:S(2)}) collective-permute-start(bf16[24,6144]{1,0:T(8,128)(2,1)S(1)} %collective-permute-done.6), channel_id=1, source_target_pairs={{0,2},{2,4},{4,6},{6,7},{7,5},{5,3},{3,1},{1,0},{8,10},{10,12},{12... | collective-permute-start | bytes 884744 | tf_op jit(solution)/shard_map/ppermute | solution.py:128
  20.2 9.9 %collective-permute-start.3 = (bf16[24,6144]{1,0:T(8,128)(2,1)S(1)}, bf16[24,6144]{1,0:T(8,128)(2,1)S(1)}, u32[]{:S(2)}, u32[]{:S(2)}) collective-permute-start(bf16[24,6144]{1,0:T(8,128)(2,1)S(1)} %collective-permute-done.1), channel_id=1, source_target_pairs={{2,0},{4,2},{6,4},{7,6},{5,7},{3,5},{1,3},{0,1},{10,8},{12,10},{14... | collective-permute-start | bytes 884744 | tf_op jit(solution)/shard_map/ppermute | solution.py:128
  20.7 15.6 %collective-permute-start.9 = (bf16[24,6144]{1,0:T(8,128)(2,1)S(1)}, bf16[24,6144]{1,0:T(8,128)(2,1)S(1)}, u32[]{:S(2)}, u32[]{:S(2)}) collective-permute-start(bf16[24,6144]{1,0:T(8,128)(2,1)S(1)} %collective-permute-done.7), channel_id=1, source_target_pairs={{2,0},{4,2},{6,4},{7,6},{5,7},{3,5},{1,3},{0,1},{10,8},{12,10},{14... | collective-permute-start | bytes 884744 | tf_op jit(solution)/shard_map/ppermute | solution.py:128
  30.1 21.2 %collective-permute-start.4 = (bf16[24,6144]{1,0:T(8,128)(2,1)S(1)}, bf16[24,6144]{1,0:T(8,128)(2,1)S(1)}, u32[]{:S(2)}, u32[]{:S(2)}) collective-permute-start(bf16[24,6144]{1,0:T(8,128)(2,1)S(1)} %collective-permute-done.2), channel_id=1, source_target_pairs={{0,2},{2,4},{4,6},{6,7},{7,5},{5,3},{3,1},{1,0},{8,10},{10,12},{12... | collective-permute-start | bytes 884744 | tf_op jit(solution)/shard_map/ppermute | solution.py:128
  36.3 15.0 %collective-permute-start.5 = (bf16[24,6144]{1,0:T(8,128)(2,1)S(1)}, bf16[24,6144]{1,0:T(8,128)(2,1)S(1)}, u32[]{:S(2)}, u32[]{:S(2)}) collective-permute-start(bf16[24,6144]{1,0:T(8,128)(2,1)S(1)} %collective-permute-done.3), channel_id=1, source_target_pairs={{2,0},{4,2},{6,4},{7,6},{5,7},{3,5},{1,3},{0,1},{10,8},{12,10},{14... | collective-permute-start | bytes 884744 | tf_op jit(solution)/shard_map/ppermute | solution.py:128
  36.9 38.8 %slice-start = ((s8[12582912]{0:T(1024)(128)(4,1)}), s8[4194304]{0:T(1024)(128)(4,1)S(1)}, s32[]{:S(2)}) async-start(s8[12582912]{0:T(1024)(128)(4,1)} %bitcast.37), calls=%async_computation | async-start | bytes 8388608
  36.9 38.8 %slice-start.1 = ((s8[12582912]{0:T(1024)(128)(4,1)}), s8[4194304]{0:T(1024)(128)(4,1)S(1)}, s32[]{:S(2)}) async-start(s8[12582912]{0:T(1024)(128)(4,1)} %bitcast.37), calls=%async_computation.1 | async-start | bytes 8388608
  49.2 8.7 %collective-permute-start.11 = (bf16[24,6144]{1,0:T(8,128)(2,1)S(1)}, bf16[24,6144]{1,0:T(8,128)(2,1)S(1)}, u32[]{:S(2)}, u32[]{:S(2)}) collective-permute-start(bf16[24,6144]{1,0:T(8,128)(2,1)S(1)} %collective-permute-done.8), channel_id=1, source_target_pairs={{0,2},{2,4},{4,6},{6,7},{7,5},{5,3},{3,1},{1,0},{8,10},{10,12},{12... | collective-permute-start | bytes 884744 | tf_op jit(solution)/shard_map/ppermute | solution.py:128
  50.9 8.4 %collective-permute-start.12 = (bf16[24,6144]{1,0:T(8,128)(2,1)S(1)}, bf16[24,6144]{1,0:T(8,128)(2,1)S(1)}, u32[]{:S(2)}, u32[]{:S(2)}) collective-permute-start(bf16[24,6144]{1,0:T(8,128)(2,1)S(1)} %collective-permute-done.9), channel_id=1, source_target_pairs={{2,0},{4,2},{6,4},{7,6},{5,7},{3,5},{1,3},{0,1},{10,8},{12,10},{14... | collective-permute-start | bytes 884744 | tf_op jit(solution)/shard_map/ppermute | solution.py:128
  59.2 16.3 %collective-permute-start.15 = (bf16[24,3072]{1,0:T(8,128)(2,1)S(1)}, bf16[24,3072]{1,0:T(8,128)(2,1)S(1)}, u32[]{:S(2)}, u32[]{:S(2)}) collective-permute-start(bf16[24,3072]{1,0:T(8,128)(2,1)S(1)} %slice.134), channel_id=1, source_target_pairs={{0,2},{2,4},{4,6},{6,7},{7,5},{5,3},{3,1},{1,0},{8,10},{10,12},{12... | collective-permute-start | bytes 442376 | tf_op jit(solution)/shard_map/ppermute | solution.py:128
  60.9 14.6 %collective-permute-start.16 = (bf16[24,3072]{1,0:T(8,128)(2,1)S(1)}, bf16[24,3072]{1,0:T(8,128)(2,1)S(1)}, u32[]{:S(2)}, u32[]{:S(2)}) collective-permute-start(bf16[24,3072]{1,0:T(8,128)(2,1)S(1)} %slice.135), channel_id=1, source_target_pairs={{2,0},{4,2},{6,4},{7,6},{5,7},{3,5},{1,3},{0,1},{10,8},{12,10},{14... | collective-permute-start | bytes 442376 | tf_op jit(solution)/shard_map/ppermute | solution.py:128
  61.5 14.1 %collective-permute-start.13 = (bf16[24,3072]{1,0:T(8,128)(2,1)S(1)}, bf16[24,3072]{1,0:T(8,128)(2,1)S(1)}, u32[]{:S(2)}, u32[]{:S(2)}) collective-permute-start(bf16[24,3072]{1,0:T(8,128)(2,1)S(1)} %slice.132), channel_id=1, source_target_pairs={{0,2},{2,4},{4,6},{6,7},{7,5},{5,3},{3,1},{1,0},{8,10},{10,12},{12... | collective-permute-start | bytes 442376 | tf_op jit(solution)/shard_map/ppermute | solution.py:128
  63.1 12.5 %collective-permute-start.14 = (bf16[24,3072]{1,0:T(8,128)(2,1)S(1)}, bf16[24,3072]{1,0:T(8,128)(2,1)S(1)}, u32[]{:S(2)}, u32[]{:S(2)}) collective-permute-start(bf16[24,3072]{1,0:T(8,128)(2,1)S(1)} %slice.133), channel_id=1, source_target_pairs={{2,0},{4,2},{6,4},{7,6},{5,7},{3,5},{1,3},{0,1},{10,8},{12,10},{14... | collective-permute-start | bytes 442376 | tf_op jit(solution)/shard_map/ppermute | solution.py:128
  63.6 12.1 %slice-start.2 = ((s8[12582912]{0:T(1024)(128)(4,1)}), s8[4194304]{0:T(1024)(128)(4,1)S(1)}, s32[]{:S(2)}) async-start(s8[12582912]{0:T(1024)(128)(4,1)} %bitcast.37), calls=%async_computation.2 | async-start | bytes 8388608
  75.6 2.2 %slice-start.3 = ((s8[12582912]{0:T(1024)(128)(4,1)}), s8[4194304]{0:T(1024)(128)(4,1)S(1)}, s32[]{:S(2)}) async-start(s8[12582912]{0:T(1024)(128)(4,1)} %bitcast.39), calls=%async_computation.3 | async-start | bytes 8388608
  75.7 3.4 %slice-start.4 = ((s8[12582912]{0:T(1024)(128)(4,1)}), s8[4194304]{0:T(1024)(128)(4,1)S(1)}, s32[]{:S(2)}) async-start(s8[12582912]{0:T(1024)(128)(4,1)} %bitcast.39), calls=%async_computation.4 | async-start | bytes 8388608
  75.7 4.6 %slice-start.5 = ((s8[12582912]{0:T(1024)(128)(4,1)}), s8[4194304]{0:T(1024)(128)(4,1)S(1)}, s32[]{:S(2)}) async-start(s8[12582912]{0:T(1024)(128)(4,1)} %bitcast.39), calls=%async_computation.5 | async-start | bytes 8388608
  93.0 5.2 %collective-permute-start.19 = (bf16[24,3072]{1,0:T(8,128)(2,1)S(1)}, bf16[24,3072]{1,0:T(8,128)(2,1)S(1)}, u32[]{:S(2)}, u32[]{:S(2)}) collective-permute-start(bf16[24,3072]{1,0:T(8,128)(2,1)S(1)} %get-tuple-element.120), channel_id=1, source_target_pairs={{0,2},{2,4},{4,6},{6,7},{7,5},{5,3},{3,1},{1,0},{8,10},{10,12},{12... | collective-permute-start | bytes 442376 | tf_op jit(solution)/shard_map/ppermute | solution.py:128
  94.6 6.4 %collective-permute-start.20 = (bf16[24,3072]{1,0:T(8,128)(2,1)S(1)}, bf16[24,3072]{1,0:T(8,128)(2,1)S(1)}, u32[]{:S(2)}, u32[]{:S(2)}) collective-permute-start(bf16[24,3072]{1,0:T(8,128)(2,1)S(1)} %get-tuple-element.119), channel_id=1, source_target_pairs={{2,0},{4,2},{6,4},{7,6},{5,7},{3,5},{1,3},{0,1},{10,8},{12,10},{14... | collective-permute-start | bytes 442376 | tf_op jit(solution)/shard_map/ppermute | solution.py:128
  95.1 8.2 %collective-permute-start.17 = (bf16[24,3072]{1,0:T(8,128)(2,1)S(1)}, bf16[24,3072]{1,0:T(8,128)(2,1)S(1)}, u32[]{:S(2)}, u32[]{:S(2)}) collective-permute-start(bf16[24,3072]{1,0:T(8,128)(2,1)S(1)} %get-tuple-element.126), channel_id=1, source_target_pairs={{0,2},{2,4},{4,6},{6,7},{7,5},{5,3},{3,1},{1,0},{8,10},{10,12},{12... | collective-permute-start | bytes 442376 | tf_op jit(solution)/shard_map/ppermute | solution.py:128
  96.7 7.4 %collective-permute-start.18 = (bf16[24,3072]{1,0:T(8,128)(2,1)S(1)}, bf16[24,3072]{1,0:T(8,128)(2,1)S(1)}, u32[]{:S(2)}, u32[]{:S(2)}) collective-permute-start(bf16[24,3072]{1,0:T(8,128)(2,1)S(1)} %get-tuple-element.125), channel_id=1, source_target_pairs={{2,0},{4,2},{6,4},{7,6},{5,7},{3,5},{1,3},{0,1},{10,8},{12,10},{14... | collective-permute-start | bytes 442376 | tf_op jit(solution)/shard_map/ppermute | solution.py:128
  101.1 10.8 %collective-permute-start.22 = (bf16[48,3072]{1,0:T(8,128)(2,1)S(1)}, bf16[48,3072]{1,0:T(8,128)(2,1)S(1)}, u32[]{:S(2)}, u32[]{:S(2)}) collective-permute-start(bf16[48,3072]{1,0:T(8,128)(2,1)S(1)} %pad_maximum_fusion.3), channel_id=1, source_target_pairs={{2,0},{4,2},{6,4},{7,6},{5,7},{3,5},{1,3},{0,1},{10,8},{12,10},{14... | collective-permute-start | bytes 884744 | tf_op jit(solution)/shard_map/ppermute | solution.py:128
  101.6 10.3 %collective-permute-start.21 = (bf16[48,3072]{1,0:T(8,128)(2,1)S(1)}, bf16[48,3072]{1,0:T(8,128)(2,1)S(1)}, u32[]{:S(2)}, u32[]{:S(2)}) collective-permute-start(bf16[48,3072]{1,0:T(8,128)(2,1)S(1)} %pad_maximum_fusion.2), channel_id=1, source_target_pairs={{0,2},{2,4},{4,6},{6,7},{7,5},{5,3},{3,1},{1,0},{8,10},{10,12},{12... | collective-permute-start | bytes 884744 | tf_op jit(solution)/shard_map/ppermute | solution.py:128
  109.9 9.9 %collective-permute-start.28 = (bf16[48,3072]{1,0:T(8,128)(2,1)S(1)}, bf16[48,3072]{1,0:T(8,128)(2,1)S(1)}, u32[]{:S(2)}, u32[]{:S(2)}) collective-permute-start(bf16[48,3072]{1,0:T(8,128)(2,1)S(1)} %get-tuple-element.101), channel_id=1, source_target_pairs={{0,2},{2,4},{4,6},{6,7},{7,5},{5,3},{3,1},{1,0},{8,10},{10,12},{12... | collective-permute-start | bytes 884744 | tf_op jit(solution)/shard_map/ppermute | solution.py:128
  111.4 9.8 %collective-permute-start.29 = (bf16[48,3072]{1,0:T(8,128)(2,1)S(1)}, bf16[48,3072]{1,0:T(8,128)(2,1)S(1)}, u32[]{:S(2)}, u32[]{:S(2)}) collective-permute-start(bf16[48,3072]{1,0:T(8,128)(2,1)S(1)} %get-tuple-element.102), channel_id=1, source_target_pairs={{2,0},{4,2},{6,4},{7,6},{5,7},{3,5},{1,3},{0,1},{10,8},{12,10},{14... | collective-permute-start | bytes 884744 | tf_op jit(solution)/shard_map/ppermute | solution.py:128
  117.7 10.0 %collective-permute-start.23 = (bf16[48,3072]{1,0:T(8,128)(2,1)S(1)}, bf16[48,3072]{1,0:T(8,128)(2,1)S(1)}, u32[]{:S(2)}, u32[]{:S(2)}) collective-permute-start(bf16[48,3072]{1,0:T(8,128)(2,1)S(1)} %get-tuple-element.94), channel_id=1, source_target_pairs={{0,2},{2,4},{4,6},{6,7},{7,5},{5,3},{3,1},{1,0},{8,10},{10,12},{12... | collective-permute-start | bytes 884744 | tf_op jit(solution)/shard_map/ppermute | solution.py:128
  119.3 9.9 %collective-permute-start.24 = (bf16[48,3072]{1,0:T(8,128)(2,1)S(1)}, bf16[48,3072]{1,0:T(8,128)(2,1)S(1)}, u32[]{:S(2)}, u32[]{:S(2)}) collective-permute-start(bf16[48,3072]{1,0:T(8,128)(2,1)S(1)} %get-tuple-element.95), channel_id=1, source_target_pairs={{2,0},{4,2},{6,4},{7,6},{5,7},{3,5},{1,3},{0,1},{10,8},{12,10},{14... | collective-permute-start | bytes 884744 | tf_op jit(solution)/shard_map/ppermute | solution.py:128
  121.4 12.7 %collective-permute-start.30 = (bf16[48,3072]{1,0:T(8,128)(2,1)S(1)}, bf16[48,3072]{1,0:T(8,128)(2,1)S(1)}, u32[]{:S(2)}, u32[]{:S(2)}) collective-permute-start(bf16[48,3072]{1,0:T(8,128)(2,1)S(1)} %get-tuple-element.114), channel_id=1, source_target_pairs={{0,2},{2,4},{4,6},{6,7},{7,5},{5,3},{3,1},{1,0},{8,10},{10,12},{12... | collective-permute-start | bytes 884744 | tf_op jit(solution)/shard_map/ppermute | solution.py:128
  121.5 14.0 %collective-permute-start.31 = (bf16[48,3072]{1,0:T(8,128)(2,1)S(1)}, bf16[48,3072]{1,0:T(8,128)(2,1)S(1)}, u32[]{:S(2)}, u32[]{:S(2)}) collective-permute-start(bf16[48,3072]{1,0:T(8,128)(2,1)S(1)} %get-tuple-element.113), channel_id=1, source_target_pairs={{2,0},{4,2},{6,4},{7,6},{5,7},{3,5},{1,3},{0,1},{10,8},{12,10},{14... | collective-permute-start | bytes 884744 | tf_op jit(solution)/shard_map/ppermute | solution.py:128
  129.4 9.2 %collective-permute-start.25 = (bf16[48,3072]{1,0:T(8,128)(2,1)S(1)}, bf16[48,3072]{1,0:T(8,128)(2,1)S(1)}, u32[]{:S(2)}, u32[]{:S(2)}) collective-permute-start(bf16[48,3072]{1,0:T(8,128)(2,1)S(1)} %get-tuple-element.110), channel_id=1, source_target_pairs={{0,2},{2,4},{4,6},{6,7},{7,5},{5,3},{3,1},{1,0},{8,10},{10,12},{12... | collective-permute-start | bytes 884744 | tf_op jit(solution)/shard_map/ppermute | solution.py:128
  130.3 9.5 %collective-permute-start.26 = (bf16[48,3072]{1,0:T(8,128)(2,1)S(1)}, bf16[48,3072]{1,0:T(8,128)(2,1)S(1)}, u32[]{:S(2)}, u32[]{:S(2)}) collective-permute-start(bf16[48,3072]{1,0:T(8,128)(2,1)S(1)} %get-tuple-element.109), channel_id=1, source_target_pairs={{2,0},{4,2},{6,4},{7,6},{5,7},{3,5},{1,3},{0,1},{10,8},{12,10},{14... | collective-permute-start | bytes 884744 | tf_op jit(solution)/shard_map/ppermute | solution.py:128
  135.7 6.8 %collective-permute-start.32 = (bf16[48,3072]{1,0:T(8,128)(2,1)S(1)}, bf16[48,3072]{1,0:T(8,128)(2,1)S(1)}, u32[]{:S(2)}, u32[]{:S(2)}) collective-permute-start(bf16[48,3072]{1,0:T(8,128)(2,1)S(1)} %get-tuple-element.112), channel_id=1, source_target_pairs={{0,2},{2,4},{4,6},{6,7},{7,5},{5,3},{3,1},{1,0},{8,10},{10,12},{12... | collective-permute-start | bytes 884744 | tf_op jit(solution)/shard_map/ppermute | solution.py:128
  136.6 7.0 %copy-start.2 = (s32[64,2]{0,1:T(2,128)S(1)}, s32[64,2]{0,1:T(2,128)}, u32[]{:S(2)}) copy-start(s32[64,2]{0,1:T(2,128)} %param.7) | copy-start | bytes 1540
  136.6 7.0 %copy-start.3 = (f32[64,2]{0,1:T(2,128)S(1)}, f32[64,2]{0,1:T(2,128)}, u32[]{:S(2)}) copy-start(f32[64,2]{0,1:T(2,128)} %param.8) | copy-start | bytes 1540
  136.6 6.7 %collective-permute-start.33 = (bf16[48,3072]{1,0:T(8,128)(2,1)S(1)}, bf16[48,3072]{1,0:T(8,128)(2,1)S(1)}, u32[]{:S(2)}, u32[]{:S(2)}) collective-permute-start(bf16[48,3072]{1,0:T(8,128)(2,1)S(1)} %get-tuple-element.111), channel_id=1, source_target_pairs={{2,0},{4,2},{6,4},{7,6},{5,7},{3,5},{1,3},{0,1},{10,8},{12,10},{14... | collective-permute-start | bytes 884744 | tf_op jit(solution)/shard_map/ppermute | solution.py:128
  139.9 6.3 %copy-start.1 = (bf16[64,6144]{1,0:T(8,128)(2,1)S(1)}, bf16[64,6144]{1,0:T(8,128)(2,1)}, u32[]{:S(2)}) copy-start(bf16[64,6144]{1,0:T(8,128)(2,1)} %param.6) | copy-start | bytes 2359300
  139.9 3.7 %collective-permute-start.27 = (bf16[24,3072]{1,0:T(8,128)(2,1)S(1)}, bf16[24,3072]{1,0:T(8,128)(2,1)S(1)}, u32[]{:S(2)}, u32[]{:S(2)}) collective-permute-start(bf16[24,3072]{1,0:T(8,128)(2,1)S(1)} %get-tuple-element.133), channel_id=1, source_target_pairs={{0,8},{8,0},{1,9},{9,1},{2,10},{10,2},{3,11},{11,3},{4,12},{12,4},... | collective-permute-start | bytes 442376 | tf_op jit(solution)/shard_map/ppermute | solution.py:214
  143.5 1.4 collective-permute-start.34

commit v5 on v3

--- a/solution.py
+++ b/solution.py
@@ -18,6 +18,14 @@
     column = jnp.arange(slots)
     dispatch_map = (member[None, :, :] == 1) & (slot_index[None, :, :] == column[:, None, None])
     return (jnp.transpose(dispatch_map, (2, 0, 1)), weight)
+
+
+def product(rows, weights):
+    return jnp.dot(rows, weights, preferred_element_type=jnp.float32)
+
+
+def activated(gate, up):
+    return (jax.nn.silu(gate) * up).astype(jnp.bfloat16)
 
 
 def per_device(tokens, expert_ids, gate_probs, w_gate, w_up, w_down):
@@ -59,41 +67,38 @@
     for from_left, from_right in carried:
         pair = step(from_left[:, :mid_col], from_right[:, mid_col:])
         far.append(jnp.concatenate(pair, axis=1))
-    blocks.append(far)
 
-    def hidden_of(rows):
-        gate_part = jnp.dot(rows, w_gate[0], preferred_element_type=jnp.float32)
-        up_part = jnp.dot(rows, w_up[0], preferred_element_type=jnp.float32)
-        return lax.optimization_barrier((jax.nn.silu(gate_part) * up_part).astype(jnp.bfloat16))
+    rows = jnp.concatenate(sum(blocks, []) + far, axis=0)
+    hidden = lax.optimization_barrier(activated(product(rows, w_gate[0]), product(rows, w_up[0])))
 
-    near_hidden = hidden_of(jnp.concatenate(sum(blocks[:half - 1], []), axis=0))
-    mid_hidden = hidden_of(jnp.concatenate(blocks[half - 1], axis=0))
-    far_hidden = hidden_of(jnp.concatenate(far, axis=0))
+    def block_of(part, index):
+        return part[index * 2 * CAP:(index + 1) * 2 * CAP]
 
+    down, got = [], []
+    for start in (0, mid_col):
+        part = product(hidden, w_down[0, :, start:start + mid_col]).astype(jnp.bfloat16)
+        down.append(part)
+        far_part = block_of(part, n_tensor - 1)
+        got.append(step(far_part[:CAP], far_part[CAP:]))
+
+    def sending(chunk, distance):
+        got_a, got_b = (part.astype(jnp.float32) for part in got[chunk])
+        send_b, send_a = (block_of(down[chunk], 2 * distance - 1 + side).astype(jnp.float32) for side in range(2))
+        if distance == half - 1:
+            send_a = jnp.concatenate([send_a[:CAP] + got_a, send_a[CAP:]], axis=0)
+            send_b = jnp.concatenate([send_b[:CAP], send_b[CAP:] + got_b], axis=0)
+        else:
+            send_a = send_a + got_a
+            send_b = send_b + got_b
+        return send_a.astype(jnp.bfloat16), send_b.astype(jnp.bfloat16)
+
+    for distance in range(half - 1, 0, -1):
+        for chunk in range(2):
+            got[chunk] = step(*sending(chunk, distance))
     sums = []
-    for cols in (slice(0, mid_col), slice(mid_col, model_width)):
-
-        def down_of(hidden):
-            part = jnp.dot(hidden, w_down[0, :, cols], preferred_element_type=jnp.float32).astype(jnp.bfloat16)
-            return [part[i * 2 * CAP:(i + 1) * 2 * CAP].astype(jnp.float32) for i in range(part.shape[0] // (2 * CAP))]
-
-        far_part = down_of(far_hidden)[0].astype(jnp.bfloat16)
-        mid_parts = down_of(mid_hidden)
-        own, *near_parts = down_of(near_hidden)
-        to_left = near_parts[0::2] + [mid_parts[0]]
-        to_right = near_parts[1::2] + [mid_parts[1]]
-        got_a, got_b = step(far_part[:CAP], far_part[CAP:])
-        for k in range(half - 2, -1, -1):
-            got_a, got_b = got_a.astype(jnp.float32), got_b.astype(jnp.float32)
-            send_a, send_b = to_right[k], to_left[k]
-            if k == half - 2:
-                send_a = jnp.concatenate([send_a[:CAP] + got_a, send_a[CAP:]], axis=0)
-                send_b = jnp.concatenate([send_b[:CAP], send_b[CAP:] + got_b], axis=0)
-            else:
-                send_a = send_a + got_a
-                send_b = send_b + got_b
-            got_a, got_b = step(send_a.astype(jnp.bfloat16), send_b.astype(jnp.bfloat16))
-        total = (own + got_a.astype(jnp.float32) + got_b.astype(jnp.float32)).astype(jnp.bfloat16)
+    for chunk in range(2):
+        got_a, got_b = (part.astype(jnp.float32) for part in got[chunk])
+        total = (block_of(down[chunk], 0).astype(jnp.float32) + got_a + got_b).astype(jnp.bfloat16)
         sums.append(jnp.stack([total[:CAP], lax.ppermute(total[CAP:], "expert", swap)]))
     returned = jnp.concatenate(sums, axis=2)
     combine = dispatch_map.astype(jnp.float32) * jnp.transpose(weight)[:, None, :]

time: 140 us -> 133 us (0.950)
  matrix products: 45.3 us -> 23.1 us
  waiting for transfers between devices: 55 us -> 71.8 us
  local copies, waits for them, and re-layouts: 2.49 us -> 0.79 us
    dot_general x12 -> x4, matrix products: 43.8 us -> 21.6 us  [product(): return jnp.dot(rows, weights, preferred_element_type=jnp.float32)]
    ppermute x15, waiting for transfers between devices: 22.8 us -> 35 us  [step(): lax.ppermute(to_left, 'tensor', left)]
    ppermute x15, waiting for transfers between devices: 24.5 us -> 33.3 us  [step(): lax.ppermute(to_right, 'tensor', right)]
    ppermute x15, starting transfers between devices: 5.82 us -> 14.3 us  [step(): lax.ppermute(to_left, 'tensor', left)]
    ppermute x15, starting transfers between devices: 25.6 us -> 18.2 us  [step(): lax.ppermute(to_right, 'tensor', right)]
    ppermute x2, waiting for transfers between devices: 6.41 us -> 2.17 us  [first(): return lax.ppermute(away, ('expert', 'tensor'), across)]
    unnamed x32 -> x29, local copies, waits for them, and re-layouts: 2.02 us -> 0.31 us
  transfers between devices with their start and end apart: 35 -> 35, of which waited for: 26 -> 28; matrix products, arithmetic and copies ran while one was open for 15% -> 1% of each run, Pallas kernels for 0% -> 0%
where the time goes in v5:
time: 133 us
  waiting for transfers between devices  71.8 us (54%)
  starting transfers between devices  34.8 us (26%)
  matrix products  23.1 us (17%)
  other arithmetic  2.27 us (2%)
    ppermute x15, waiting for transfers between devices, step(): lax.ppermute(to_left, 'tensor', left)  35 us
    ppermute x15, waiting for transfers between devices, step(): lax.ppermute(to_right, 'tensor', right)  33.3 us
    dot_general x4, matrix products, product(): return jnp.dot(rows, weights, preferred_element_type=jnp.float32)  21.6 us
    ppermute x15, starting transfers between devices, step(): lax.ppermute(to_right, 'tensor', right)  18.2 us
    ppermute x15, starting transfers between devices, step(): lax.ppermute(to_left, 'tensor', left)  14.3 us
  transfers between devices with their start and end apart: 35, of which 28 were waited for; matrix products, arithmetic and copies ran while one was open for 1% of the time, Pallas kernels for 0%

profile of v5, /device:TPU:0, one launch (start us, length us, event | category | flops | bytes accessed | tf_op | source)
XLA Modules:
  0.0 133.2 jit_solution(15328251586421108705)
XLA Ops:
  0.2 0.8 compare_reduce_fusion
  1.4 0.3 convolution_convert_fusion
  1.8 3.1 %collective-permute-start.1 = (bf16[24,6144]{1,0:T(8,128)(2,1)S(1)}, bf16[24,6144]{1,0:T(8,128)(2,1)S(1)}, u32[]{:S(2)}, u32[]{:S(2)}) collective-permute-start(bf16[24,6144]{1,0:T(8,128)(2,1)S(1)} %get-tuple-element.89), channel_id=1, source_target_pairs={{0,2},{2,4},{4,6},{6,7},{7,5},{5,3},{3,1},{1,0},{8,10},{10,12},{12... | collective-permute-start | bytes 884744 | tf_op jit(solution)/shard_map/ppermute | solution.py:42
  4.9 2.1 %collective-permute-start.3 = (bf16[24,6144]{1,0:T(8,128)(2,1)S(1)}, bf16[24,6144]{1,0:T(8,128)(2,1)S(1)}, u32[]{:S(2)}, u32[]{:S(2)}) collective-permute-start(bf16[24,6144]{1,0:T(8,128)(2,1)S(1)} %get-tuple-element.91), channel_id=1, source_target_pairs={{0,10},{2,12},{4,14},{6,15},{7,13},{5,11},{3,9},{1,8},{8,2},{10,4}... | collective-permute-start | bytes 884744 | tf_op jit(solution)/shard_map/ppermute | solution.py:58
  7.0 5.6 %collective-permute-done.1 = bf16[24,6144]{1,0:T(8,128)(2,1)S(1)} collective-permute-done((bf16[24,6144]{1,0:T(8,128)(2,1)S(1)}, bf16[24,6144]{1,0:T(8,128)(2,1)S(1)}, u32[]{:S(2)}, u32[]{:S(2)}) %collective-permute-start.1) | collective-permute-done | bytes 294944 | tf_op jit(solution)/shard_map/ppermute | solution.py:42
  12.6 2.2 %collective-permute-done.2 = bf16[24,6144]{1,0:T(8,128)(2,1)S(1)} collective-permute-done((bf16[24,6144]{1,0:T(8,128)(2,1)S(1)}, bf16[24,6144]{1,0:T(8,128)(2,1)S(1)}, u32[]{:S(2)}, u32[]{:S(2)}) %collective-permute-start.2) | collective-permute-done | bytes 294944 | tf_op jit(solution)/shard_map/ppermute | solution.py:42
  14.8 1.6 %collective-permute-start.5 = (bf16[24,6144]{1,0:T(8,128)(2,1)S(1)}, bf16[24,6144]{1,0:T(8,128)(2,1)S(1)}, u32[]{:S(2)}, u32[]{:S(2)}) collective-permute-start(bf16[24,6144]{1,0:T(8,128)(2,1)S(1)} %collective-permute-done.1), channel_id=1, source_target_pairs={{0,2},{2,4},{4,6},{6,7},{7,5},{5,3},{3,1},{1,0},{8,10},{10,12},{12... | collective-permute-start | bytes 884744 | tf_op jit(solution)/shard_map/ppermute | solution.py:42
  16.4 2.2 %collective-permute-done.3 = bf16[24,6144]{1,0:T(8,128)(2,1)S(1)} collective-permute-done((bf16[24,6144]{1,0:T(8,128)(2,1)S(1)}, bf16[24,6144]{1,0:T(8,128)(2,1)S(1)}, u32[]{:S(2)}, u32[]{:S(2)}) %collective-permute-start.3) | collective-permute-done | bytes 294944 | tf_op jit(solution)/shard_map/ppermute | solution.py:58
  18.6 1.6 %collective-permute-start.7 = (bf16[24,6144]{1,0:T(8,128)(2,1)S(1)}, bf16[24,6144]{1,0:T(8,128)(2,1)S(1)}, u32[]{:S(2)}, u32[]{:S(2)}) collective-permute-start(bf16[24,6144]{1,0:T(8,128)(2,1)S(1)} %collective-permute-done.3), channel_id=1, source_target_pairs={{0,2},{2,4},{4,6},{6,7},{7,5},{5,3},{3,1},{1,0},{8,10},{10,12},{12... | collective-permute-start | bytes 884744 | tf_op jit(solution)/shard_map/ppermute | solution.py:42
  20.2 0.5 collective-permute-start.6
  20.7 0.6 collective-permute-start.8
  21.3 3.9 %collective-permute-done.5 = bf16[24,6144]{1,0:T(8,128)(2,1)S(1)} collective-permute-done((bf16[24,6144]{1,0:T(8,128)(2,1)S(1)}, bf16[24,6144]{1,0:T(8,128)(2,1)S(1)}, u32[]{:S(2)}, u32[]{:S(2)}) %collective-permute-start.5) | collective-permute-done | bytes 294944 | tf_op jit(solution)/shard_map/ppermute | solution.py:42
  25.3 4.9 %collective-permute-done.6 = bf16[24,6144]{1,0:T(8,128)(2,1)S(1)} collective-permute-done((bf16[24,6144]{1,0:T(8,128)(2,1)S(1)}, bf16[24,6144]{1,0:T(8,128)(2,1)S(1)}, u32[]{:S(2)}, u32[]{:S(2)}) %collective-permute-start.6) | collective-permute-done | bytes 294944 | tf_op jit(solution)/shard_map/ppermute | solution.py:42
  30.1 1.6 %collective-permute-start.9 = (bf16[24,6144]{1,0:T(8,128)(2,1)S(1)}, bf16[24,6144]{1,0:T(8,128)(2,1)S(1)}, u32[]{:S(2)}, u32[]{:S(2)}) collective-permute-start(bf16[24,6144]{1,0:T(8,128)(2,1)S(1)} %collective-permute-done.5), channel_id=1, source_target_pairs={{0,2},{2,4},{4,6},{6,7},{7,5},{5,3},{3,1},{1,0},{8,10},{10,12},{12... | collective-permute-start | bytes 884744 | tf_op jit(solution)/shard_map/ppermute | solution.py:42
  31.7 4.6 %collective-permute-done.8 = bf16[24,6144]{1,0:T(8,128)(2,1)S(1)} collective-permute-done((bf16[24,6144]{1,0:T(8,128)(2,1)S(1)}, bf16[24,6144]{1,0:T(8,128)(2,1)S(1)}, u32[]{:S(2)}, u32[]{:S(2)}) %collective-permute-start.8) | collective-permute-done | bytes 294944 | tf_op jit(solution)/shard_map/ppermute | solution.py:42
  36.4 1.6 %collective-permute-start.11 = (bf16[24,6144]{1,0:T(8,128)(2,1)S(1)}, bf16[24,6144]{1,0:T(8,128)(2,1)S(1)}, u32[]{:S(2)}, u32[]{:S(2)}) collective-permute-start(bf16[24,6144]{1,0:T(8,128)(2,1)S(1)} %collective-permute-done.7), channel_id=1, source_target_pairs={{0,2},{2,4},{4,6},{6,7},{7,5},{5,3},{3,1},{1,0},{8,10},{10,12},{12... | collective-permute-start | bytes 884744 | tf_op jit(solution)/shard_map/ppermute | solution.py:42
  38.0 0.5 collective-permute-start.10
  38.5 0.5 collective-permute-start.12
  39.0 8.9 %collective-permute-done.10 = bf16[24,6144]{1,0:T(8,128)(2,1)S(1)} collective-permute-done((bf16[24,6144]{1,0:T(8,128)(2,1)S(1)}, bf16[24,6144]{1,0:T(8,128)(2,1)S(1)}, u32[]{:S(2)}, u32[]{:S(2)}) %collective-permute-start.10) | collective-permute-done | bytes 294944 | tf_op jit(solution)/shard_map/ppermute | solution.py:42
  48.0 5.0 %collective-permute-done.12 = bf16[24,6144]{1,0:T(8,128)(2,1)S(1)} collective-permute-done((bf16[24,6144]{1,0:T(8,128)(2,1)S(1)}, bf16[24,6144]{1,0:T(8,128)(2,1)S(1)}, u32[]{:S(2)}, u32[]{:S(2)}) %collective-permute-start.12) | collective-permute-done | bytes 294944 | tf_op jit(solution)/shard_map/ppermute | solution.py:42
  53.1 1.6 %collective-permute-start.13 = (bf16[24,3072]{1,0:T(8,128)(2,1)S(1)}, bf16[24,3072]{1,0:T(8,128)(2,1)S(1)}, u32[]{:S(2)}, u32[]{:S(2)}) collective-permute-start(bf16[24,3072]{1,0:T(8,128)(2,1)S(1)} %slice.138), channel_id=1, source_target_pairs={{0,2},{2,4},{4,6},{6,7},{7,5},{5,3},{3,1},{1,0},{8,10},{10,12},{12... | collective-permute-start | bytes 442376 | tf_op jit(solution)/shard_map/ppermute | solution.py:42
  54.7 0.5 collective-permute-start.14
  55.2 1.5 %collective-permute-start.15 = (bf16[24,3072]{1,0:T(8,128)(2,1)S(1)}, bf16[24,3072]{1,0:T(8,128)(2,1)S(1)}, u32[]{:S(2)}, u32[]{:S(2)}) collective-permute-start(bf16[24,3072]{1,0:T(8,128)(2,1)S(1)} %slice.140), channel_id=1, source_target_pairs={{0,2},{2,4},{4,6},{6,7},{7,5},{5,3},{3,1},{1,0},{8,10},{10,12},{12... | collective-permute-start | bytes 442376 | tf_op jit(solution)/shard_map/ppermute | solution.py:42
  56.7 0.7 collective-permute-start.16
  57.5 1.9 %collective-permute-done.13 = bf16[24,3072]{1,0:T(8,128)(2,1)S(1)} collective-permute-done((bf16[24,3072]{1,0:T(8,128)(2,1)S(1)}, bf16[24,3072]{1,0:T(8,128)(2,1)S(1)}, u32[]{:S(2)}, u32[]{:S(2)}) %collective-permute-start.13) | collective-permute-done | bytes 147488 | tf_op jit(solution)/shard_map/ppermute | solution.py:42
  59.3 1.4 %collective-permute-done.14 = bf16[24,3072]{1,0:T(8,128)(2,1)S(1)} collective-permute-done((bf16[24,3072]{1,0:T(8,128)(2,1)S(1)}, bf16[24,3072]{1,0:T(8,128)(2,1)S(1)}, u32[]{:S(2)}, u32[]{:S(2)}) %collective-permute-start.14) | collective-permute-done | bytes 147488 | tf_op jit(solution)/shard_map/ppermute | solution.py:42
  60.9 1.4 %collective-permute-done.16 = bf16[24,3072]{1,0:T(8,128)(2,1)S(1)} collective-permute-done((bf16[24,3072]{1,0:T(8,128)(2,1)S(1)}, bf16[24,3072]{1,0:T(8,128)(2,1)S(1)}, u32[]{:S(2)}, u32[]{:S(2)}) %collective-permute-start.16) | collective-permute-done | bytes 147488 | tf_op jit(solution)/shard_map/ppermute | solution.py:42
  62.4 5.1 %fusion.2 = f32[384,1024]{1,0:T(8,128)S(1)} fusion(bf16[384,6144]{1,0:T(8,128)(2,1)S(1)} %maximum_dynamic-update-slice_fusion, bf16[1,6144,1024]{2,1,0:T(8,128)(2,1)S(1)} %copy-done.4), kind=kOutput, calls=%fused_computation.2 | convolution fusion | flops 4831838208 | bytes 18874368 | tf_op jit(solution)/shard_map/dot_general | solution.py:24
  67.5 5.2 %multiply_convert_fusion = bf16[384,1024]{1,0:T(8,128)(2,1)S(1)} fusion(f32[384,1024]{1,0:T(8,128)S(1)} %fusion.2, bf16[384,6144]{1,0:T(8,128)(2,1)S(1)} %maximum_dynamic-update-slice_fusion, bf16[1,6144,1024]{2,1,0:T(8,128)(2,1)S(1)} %bitcast.49), kind=kOutput, calls=%fused_computation.15 | convolution fusion | flops 4834197504 | bytes 19660800 | tf_op jit(solution)/shard_map/dot_general | solution.py:24
  72.8 5.6 %fusion.14 = bf16[384,3072]{1,0:T(8,128)(2,1)S(1)} fusion(bf16[384,1024]{1,0:T(8,128)(2,1)S(1)} %multiply_convert_fusion, bf16[1,1024,6144]{2,1,0:T(8,128)(2,1)} %param.11), kind=kOutput, calls=%fused_computation.14 | convolution fusion | flops 2417098752 | bytes 9437184 | tf_op jit(solution)/shard_map/dot_general | solution.py:24
  78.4 5.6 %fusion.11 = bf16[384,3072]{1,0:T(8,128)(2,1)S(1)} fusion(bf16[384,1024]{1,0:T(8,128)(2,1)S(1)} %multiply_convert_fusion, bf16[1,1024,6144]{2,1,0:T(8,128)(2,1)} %param.11), kind=kOutput, calls=%fused_computation.13 | convolution fusion | flops 2417098752 | bytes 9437184 | tf_op jit(solution)/shard_map/dot_general | solution.py:24
  84.1 1.4 %collective-permute-start.26 = (bf16[24,3072]{1,0:T(8,128)(2,1)S(1)}, bf16[24,3072]{1,0:T(8,128)(2,1)S(1)}, u32[]{:S(2)}, u32[]{:S(2)}) collective-permute-start(bf16[24,3072]{1,0:T(8,128)(2,1)S(1)} %get-tuple-element.86), channel_id=1, source_target_pairs={{0,2},{2,4},{4,6},{6,7},{7,5},{5,3},{3,1},{1,0},{8,10},{10,12},{12... | collective-permute-start | bytes 442376 | tf_op jit(solution)/shard_map/ppermute | solution.py:42
  85.4 0.7 collective-permute-start.27
  86.2 1.4 %collective-permute-start.17 = (bf16[24,3072]{1,0:T(8,128)(2,1)S(1)}, bf16[24,3072]{1,0:T(8,128)(2,1)S(1)}, u32[]{:S(2)}, u32[]{:S(2)}) collective-permute-start(bf16[24,3072]{1,0:T(8,128)(2,1)S(1)} %get-tuple-element.76), channel_id=1, source_target_pairs={{0,2},{2,4},{4,6},{6,7},{7,5},{5,3},{3,1},{1,0},{8,10},{10,12},{12... | collective-permute-start | bytes 442376 | tf_op jit(solution)/shard_map/ppermute | solution.py:42
  87.6 0.7 collective-permute-start.18
  88.3 1.1 collective-permute-done.26
  89.4 1.8 %collective-permute-done.27 = bf16[24,3072]{1,0:T(8,128)(2,1)S(1)} collective-permute-done((bf16[24,3072]{1,0:T(8,128)(2,1)S(1)}, bf16[24,3072]{1,0:T(8,128)(2,1)S(1)}, u32[]{:S(2)}, u32[]{:S(2)}) %collective-permute-start.27) | collective-permute-done | bytes 147488 | tf_op jit(solution)/shard_map/ppermute | solution.py:42
  91.3 0.5 collective-permute-start.28
  91.8 1.6 %collective-permute-start.29 = (bf16[48,3072]{1,0:T(8,128)(2,1)S(1)}, bf16[48,3072]{1,0:T(8,128)(2,1)S(1)}, u32[]{:S(2)}, u32[]{:S(2)}) collective-permute-start(bf16[48,3072]{1,0:T(8,128)(2,1)S(1)} %pad_maximum_fusion.3), channel_id=1, source_target_pairs={{2,0},{4,2},{6,4},{7,6},{5,7},{3,5},{1,3},{0,1},{10,8},{12,10},{14... | collective-permute-start | bytes 884744 | tf_op jit(solution)/shard_map/ppermute | solution.py:42
  93.4 0.9 collective-permute-done.18
  94.4 0.5 collective-permute-start.19
  95.0 1.6 %collective-permute-start.20 = (bf16[48,3072]{1,0:T(8,128)(2,1)S(1)}, bf16[48,3072]{1,0:T(8,128)(2,1)S(1)}, u32[]{:S(2)}, u32[]{:S(2)}) collective-permute-start(bf16[48,3072]{1,0:T(8,128)(2,1)S(1)} %pad_maximum_fusion.1), channel_id=1, source_target_pairs={{2,0},{4,2},{6,4},{7,6},{5,7},{3,5},{1,3},{0,1},{10,8},{12,10},{14... | collective-permute-start | bytes 884744 | tf_op jit(solution)/shard_map/ppermute | solution.py:42
  96.6 4.7 %collective-permute-done.28 = bf16[48,3072]{1,0:T(8,128)(2,1)S(1)} collective-permute-done((bf16[48,3072]{1,0:T(8,128)(2,1)S(1)}, bf16[48,3072]{1,0:T(8,128)(2,1)S(1)}, u32[]{:S(2)}, u32[]{:S(2)}) %collective-permute-start.28) | collective-permute-done | bytes 294944 | tf_op jit(solution)/shard_map/ppermute | solution.py:42
  101.3 0.5 collective-permute-done.29
  102.0 0.5 collective-permute-start.30
  102.5 1.6 %collective-permute-start.31 = (bf16[48,3072]{1,0:T(8,128)(2,1)S(1)}, bf16[48,3072]{1,0:T(8,128)(2,1)S(1)}, u32[]{:S(2)}, u32[]{:S(2)}) collective-permute-start(bf16[48,3072]{1,0:T(8,128)(2,1)S(1)} %get-tuple-element.81), channel_id=1, source_target_pairs={{2,0},{4,2},{6,4},{7,6},{5,7},{3,5},{1,3},{0,1},{10,8},{12,10},{14... | collective-permute-start | bytes 884744 | tf_op jit(solution)/shard_map/ppermute | solution.py:42
  104.0 3.5 %collective-permute-done.19 = bf16[48,3072]{1,0:T(8,128)(2,1)S(1)} collective-permute-done((bf16[48,3072]{1,0:T(8,128)(2,1)S(1)}, bf16[48,3072]{1,0:T(8,128)(2,1)S(1)}, u32[]{:S(2)}, u32[]{:S(2)}) %collective-permute-start.19) | collective-permute-done | bytes 294944 | tf_op jit(solution)/shard_map/ppermute | solution.py:42
  107.6 0.5 collective-permute-done.20
  108.3 0.5 collective-permute-start.21
  108.8 1.6 %collective-permute-start.22 = (bf16[48,3072]{1,0:T(8,128)(2,1)S(1)}, bf16[48,3072]{1,0:T(8,128)(2,1)S(1)}, u32[]{:S(2)}, u32[]{:S(2)}) collective-permute-start(bf16[48,3072]{1,0:T(8,128)(2,1)S(1)} %get-tuple-element.71), channel_id=1, source_target_pairs={{2,0},{4,2},{6,4},{7,6},{5,7},{3,5},{1,3},{0,1},{10,8},{12,10},{14... | collective-permute-start | bytes 884744 | tf_op jit(solution)/shard_map/ppermute | solution.py:42
  110.3 3.6 %collective-permute-done.30 = bf16[48,3072]{1,0:T(8,128)(2,1)S(1)} collective-permute-done((bf16[48,3072]{1,0:T(8,128)(2,1)S(1)}, bf16[48,3072]{1,0:T(8,128)(2,1)S(1)}, u32[]{:S(2)}, u32[]{:S(2)}) %collective-permute-start.30) | collective-permute-done | bytes 294944 | tf_op jit(solution)/shard_map/ppermute | solution.py:42
  113.9 0.5 collective-permute-done.31
  114.6 0.5 collective-permute-start.32
  115.1 1.6 %collective-permute-start.33 = (bf16[48,3072]{1,0:T(8,128)(2,1)S(1)}, bf16[48,3072]{1,0:T(8,128)(2,1)S(1)}, u32[]{:S(2)}, u32[]{:S(2)}) collective-permute-start(bf16[48,3072]{1,0:T(8,128)(2,1)S(1)} %get-tuple-element.79), channel_id=1, source_target_pairs={{2,0},{4,2},{6,4},{7,6},{5,7},{3,5},{1,3},{0,1},{10,8},{12,10},{14... | collective-permute-start | bytes 884744 | tf_op jit(solution)/shard_map/ppermute | solution.py:42
  116.7 3.6 %collective-permute-done.21 = bf16[48,3072]{1,0:T(8,128)(2,1)S(1)} collective-permute-done((bf16[48,3072]{1,0:T(8,128)(2,1)S(1)}, bf16[48,3072]{1,0:T(8,128)(2,1)S(1)}, u32[]{:S(2)}, u32[]{:S(2)}) %collective-permute-start.21) | collective-permute-done | bytes 294944 | tf_op jit(solution)/shard_map/ppermute | solution.py:42
  120.2 0.5 collective-permute-done.22
  120.9 0.5 collective-permute-start.23
  121.4 1.6 %collective-permute-start.24 = (bf16[48,3072]{1,0:T(8,128)(2,1)S(1)}, bf16[48,3072]{1,0:T(8,128)(2,1)S(1)}, u32[]{:S(2)}, u32[]{:S(2)}) collective-permute-start(bf16[48,3072]{1,0:T(8,128)(2,1)S(1)} %get-tuple-element.69), channel_id=1, source_target_pairs={{2,0},{4,2},{6,4},{7,6},{5,7},{3,5},{1,3},{0,1},{10,8},{12,10},{14... | collective-permute-start | bytes 884744 | tf_op jit(solution)/shard_map/ppermute | solution.py:42
  123.0 3.2 %collective-permute-done.32 = bf16[48,3072]{1,0:T(8,128)(2,1)S(1)} collective-permute-done((bf16[48,3072]{1,0:T(8,128)(2,1)S(1)}, bf16[48,3072]{1,0:T(8,128)(2,1)S(1)}, u32[]{:S(2)}, u32[]{:S(2)}) %collective-permute-start.32) | collective-permute-done | bytes 294944 | tf_op jit(solution)/shard_map/ppermute | solution.py:42
  126.2 0.9 collective-permute-done.33
  127.3 2.0 %collective-permute-done.23 = bf16[48,3072]{1,0:T(8,128)(2,1)S(1)} collective-permute-done((bf16[48,3072]{1,0:T(8,128)(2,1)S(1)}, bf16[48,3072]{1,0:T(8,128)(2,1)S(1)}, u32[]{:S(2)}, u32[]{:S(2)}) %collective-permute-start.23) | collective-permute-done | bytes 294944 | tf_op jit(solution)/shard_map/ppermute | solution.py:42
  129.3 1.1 collective-permute-done.24
  130.7 1.3 collective-permute-done.25
  132.0 1.3 fusion.4
  (76 shorter events, 2.6 us)
Async XLA Ops:
  0.0 1.4 %copy-start = (bf16[64,6144]{1,0:T(8,128)(2,1)S(1)}, bf16[64,6144]{1,0:T(8,128)(2,1)}, u32[]{:S(2)}) copy-start(bf16[64,6144]{1,0:T(8,128)(2,1)} %param.6) | copy-start | bytes 2359300
  1.4 61.0 %copy-start.4 = (bf16[1,6144,1024]{2,1,0:T(8,128)(2,1)S(1)}, bf16[1,6144,1024]{2,1,0:T(8,128)(2,1)}, u32[]{:S(2)}) copy-start(bf16[1,6144,1024]{2,1,0:T(8,128)(2,1)} %param.9) | copy-start | bytes 37748740
  1.8 10.9 %collective-permute-start.1 = (bf16[24,6144]{1,0:T(8,128)(2,1)S(1)}, bf16[24,6144]{1,0:T(8,128)(2,1)S(1)}, u32[]{:S(2)}, u32[]{:S(2)}) collective-permute-start(bf16[24,6144]{1,0:T(8,128)(2,1)S(1)} %get-tuple-element.89), channel_id=1, source_target_pairs={{0,2},{2,4},{4,6},{6,7},{7,5},{5,3},{3,1},{1,0},{8,10},{10,12},{12... | collective-permute-start | bytes 884744 | tf_op jit(solution)/shard_map/ppermute | solution.py:42
  4.8 9.9 %collective-permute-start.2 = (bf16[24,6144]{1,0:T(8,128)(2,1)S(1)}, bf16[24,6144]{1,0:T(8,128)(2,1)S(1)}, u32[]{:S(2)}, u32[]{:S(2)}) collective-permute-start(bf16[24,6144]{1,0:T(8,128)(2,1)S(1)} %get-tuple-element.89), channel_id=1, source_target_pairs={{2,0},{4,2},{6,4},{7,6},{5,7},{3,5},{1,3},{0,1},{10,8},{12,10},{14... | collective-permute-start | bytes 884744 | tf_op jit(solution)/shard_map/ppermute | solution.py:42
  4.9 11.5 %collective-permute-start = (bf16[24,6144]{1,0:T(8,128)(2,1)S(1)}, bf16[24,6144]{1,0:T(8,128)(2,1)S(1)}, u32[]{:S(2)}, u32[]{:S(2)}) collective-permute-start(bf16[24,6144]{1,0:T(8,128)(2,1)S(1)} %get-tuple-element.91), channel_id=1, source_target_pairs={{0,8},{8,0},{1,9},{9,1},{2,10},{10,2},{3,11},{11,3},{4,12},{12,4},... | collective-permute-start | bytes 884744 | tf_op jit(solution)/shard_map/ppermute | solution.py:54
  4.9 13.7 %collective-permute-start.3 = (bf16[24,6144]{1,0:T(8,128)(2,1)S(1)}, bf16[24,6144]{1,0:T(8,128)(2,1)S(1)}, u32[]{:S(2)}, u32[]{:S(2)}) collective-permute-start(bf16[24,6144]{1,0:T(8,128)(2,1)S(1)} %get-tuple-element.91), channel_id=1, source_target_pairs={{0,10},{2,12},{4,14},{6,15},{7,13},{5,11},{3,9},{1,8},{8,2},{10,4}... | collective-permute-start | bytes 884744 | tf_op jit(solution)/shard_map/ppermute | solution.py:58
  7.0 11.6 %collective-permute-start.4 = (bf16[24,6144]{1,0:T(8,128)(2,1)S(1)}, bf16[24,6144]{1,0:T(8,128)(2,1)S(1)}, u32[]{:S(2)}, u32[]{:S(2)}) collective-permute-start(bf16[24,6144]{1,0:T(8,128)(2,1)S(1)} %get-tuple-element.91), channel_id=1, source_target_pairs={{2,8},{4,10},{6,12},{7,14},{5,15},{3,13},{1,11},{0,9},{10,0},{12,2... | collective-permute-start | bytes 884744 | tf_op jit(solution)/shard_map/ppermute | solution.py:58
  14.8 10.5 %collective-permute-start.5 = (bf16[24,6144]{1,0:T(8,128)(2,1)S(1)}, bf16[24,6144]{1,0:T(8,128)(2,1)S(1)}, u32[]{:S(2)}, u32[]{:S(2)}) collective-permute-start(bf16[24,6144]{1,0:T(8,128)(2,1)S(1)} %collective-permute-done.1), channel_id=1, source_target_pairs={{0,2},{2,4},{4,6},{6,7},{7,5},{5,3},{3,1},{1,0},{8,10},{10,12},{12... | collective-permute-start | bytes 884744 | tf_op jit(solution)/shard_map/ppermute | solution.py:42
  18.6 13.1 %collective-permute-start.7 = (bf16[24,6144]{1,0:T(8,128)(2,1)S(1)}, bf16[24,6144]{1,0:T(8,128)(2,1)S(1)}, u32[]{:S(2)}, u32[]{:S(2)}) collective-permute-start(bf16[24,6144]{1,0:T(8,128)(2,1)S(1)} %collective-permute-done.3), channel_id=1, source_target_pairs={{0,2},{2,4},{4,6},{6,7},{7,5},{5,3},{3,1},{1,0},{8,10},{10,12},{12... | collective-permute-start | bytes 884744 | tf_op jit(solution)/shard_map/ppermute | solution.py:42
  20.2 9.9 %collective-permute-start.6 = (bf16[24,6144]{1,0:T(8,128)(2,1)S(1)}, bf16[24,6144]{1,0:T(8,128)(2,1)S(1)}, u32[]{:S(2)}, u32[]{:S(2)}) collective-permute-start(bf16[24,6144]{1,0:T(8,128)(2,1)S(1)} %collective-permute-done.2), channel_id=1, source_target_pairs={{2,0},{4,2},{6,4},{7,6},{5,7},{3,5},{1,3},{0,1},{10,8},{12,10},{14... | collective-permute-start | bytes 884744 | tf_op jit(solution)/shard_map/ppermute | solution.py:42
  20.7 15.6 %collective-permute-start.8 = (bf16[24,6144]{1,0:T(8,128)(2,1)S(1)}, bf16[24,6144]{1,0:T(8,128)(2,1)S(1)}, u32[]{:S(2)}, u32[]{:S(2)}) collective-permute-start(bf16[24,6144]{1,0:T(8,128)(2,1)S(1)} %collective-permute-done.4), channel_id=1, source_target_pairs={{2,0},{4,2},{6,4},{7,6},{5,7},{3,5},{1,3},{0,1},{10,8},{12,10},{14... | collective-permute-start | bytes 884744 | tf_op jit(solution)/shard_map/ppermute | solution.py:42
  30.1 8.9 %collective-permute-start.9 = (bf16[24,6144]{1,0:T(8,128)(2,1)S(1)}, bf16[24,6144]{1,0:T(8,128)(2,1)S(1)}, u32[]{:S(2)}, u32[]{:S(2)}) collective-permute-start(bf16[24,6144]{1,0:T(8,128)(2,1)S(1)} %collective-permute-done.5), channel_id=1, source_target_pairs={{0,2},{2,4},{4,6},{6,7},{7,5},{5,3},{3,1},{1,0},{8,10},{10,12},{12... | collective-permute-start | bytes 884744 | tf_op jit(solution)/shard_map/ppermute | solution.py:42
  36.4 11.6 %collective-permute-start.11 = (bf16[24,6144]{1,0:T(8,128)(2,1)S(1)}, bf16[24,6144]{1,0:T(8,128)(2,1)S(1)}, u32[]{:S(2)}, u32[]{:S(2)}) collective-permute-start(bf16[24,6144]{1,0:T(8,128)(2,1)S(1)} %collective-permute-done.7), channel_id=1, source_target_pairs={{0,2},{2,4},{4,6},{6,7},{7,5},{5,3},{3,1},{1,0},{8,10},{10,12},{12... | collective-permute-start | bytes 884744 | tf_op jit(solution)/shard_map/ppermute | solution.py:42
  38.0 10.0 %collective-permute-start.10 = (bf16[24,6144]{1,0:T(8,128)(2,1)S(1)}, bf16[24,6144]{1,0:T(8,128)(2,1)S(1)}, u32[]{:S(2)}, u32[]{:S(2)}) collective-permute-start(bf16[24,6144]{1,0:T(8,128)(2,1)S(1)} %collective-permute-done.6), channel_id=1, source_target_pairs={{2,0},{4,2},{6,4},{7,6},{5,7},{3,5},{1,3},{0,1},{10,8},{12,10},{14... | collective-permute-start | bytes 884744 | tf_op jit(solution)/shard_map/ppermute | solution.py:42
  38.5 14.5 %collective-permute-start.12 = (bf16[24,6144]{1,0:T(8,128)(2,1)S(1)}, bf16[24,6144]{1,0:T(8,128)(2,1)S(1)}, u32[]{:S(2)}, u32[]{:S(2)}) collective-permute-start(bf16[24,6144]{1,0:T(8,128)(2,1)S(1)} %collective-permute-done.8), channel_id=1, source_target_pairs={{2,0},{4,2},{6,4},{7,6},{5,7},{3,5},{1,3},{0,1},{10,8},{12,10},{14... | collective-permute-start | bytes 884744 | tf_op jit(solution)/shard_map/ppermute | solution.py:42
  53.1 6.2 %collective-permute-start.13 = (bf16[24,3072]{1,0:T(8,128)(2,1)S(1)}, bf16[24,3072]{1,0:T(8,128)(2,1)S(1)}, u32[]{:S(2)}, u32[]{:S(2)}) collective-permute-start(bf16[24,3072]{1,0:T(8,128)(2,1)S(1)} %slice.138), channel_id=1, source_target_pairs={{0,2},{2,4},{4,6},{6,7},{7,5},{5,3},{3,1},{1,0},{8,10},{10,12},{12... | collective-permute-start | bytes 442376 | tf_op jit(solution)/shard_map/ppermute | solution.py:42
  54.7 6.1 %collective-permute-start.14 = (bf16[24,3072]{1,0:T(8,128)(2,1)S(1)}, bf16[24,3072]{1,0:T(8,128)(2,1)S(1)}, u32[]{:S(2)}, u32[]{:S(2)}) collective-permute-start(bf16[24,3072]{1,0:T(8,128)(2,1)S(1)} %slice.139), channel_id=1, source_target_pairs={{2,0},{4,2},{6,4},{7,6},{5,7},{3,5},{1,3},{0,1},{10,8},{12,10},{14... | collective-permute-start | bytes 442376 | tf_op jit(solution)/shard_map/ppermute | solution.py:42
  55.2 5.8 %collective-permute-start.15 = (bf16[24,3072]{1,0:T(8,128)(2,1)S(1)}, bf16[24,3072]{1,0:T(8,128)(2,1)S(1)}, u32[]{:S(2)}, u32[]{:S(2)}) collective-permute-start(bf16[24,3072]{1,0:T(8,128)(2,1)S(1)} %slice.140), channel_id=1, source_target_pairs={{0,2},{2,4},{4,6},{6,7},{7,5},{5,3},{3,1},{1,0},{8,10},{10,12},{12... | collective-permute-start | bytes 442376 | tf_op jit(solution)/shard_map/ppermute | solution.py:42
  56.7 5.6 %collective-permute-start.16 = (bf16[24,3072]{1,0:T(8,128)(2,1)S(1)}, bf16[24,3072]{1,0:T(8,128)(2,1)S(1)}, u32[]{:S(2)}, u32[]{:S(2)}) collective-permute-start(bf16[24,3072]{1,0:T(8,128)(2,1)S(1)} %slice.141), channel_id=1, source_target_pairs={{2,0},{4,2},{6,4},{7,6},{5,7},{3,5},{1,3},{0,1},{10,8},{12,10},{14... | collective-permute-start | bytes 442376 | tf_op jit(solution)/shard_map/ppermute | solution.py:42
  62.3 5.2 %slice-start = ((s8[12582912]{0:T(1024)(128)(4,1)}), s8[4194304]{0:T(1024)(128)(4,1)S(1)}, s32[]{:S(2)}) async-start(s8[12582912]{0:T(1024)(128)(4,1)} %bitcast.48), calls=%async_computation | async-start | bytes 8388608
  62.4 5.1 %slice-start.1 = ((s8[12582912]{0:T(1024)(128)(4,1)}), s8[4194304]{0:T(1024)(128)(4,1)S(1)}, s32[]{:S(2)}) async-start(s8[12582912]{0:T(1024)(128)(4,1)} %bitcast.48), calls=%async_computation.1 | async-start | bytes 8388608
  62.4 5.1 %slice-start.2 = ((s8[12582912]{0:T(1024)(128)(4,1)}), s8[4194304]{0:T(1024)(128)(4,1)S(1)}, s32[]{:S(2)}) async-start(s8[12582912]{0:T(1024)(128)(4,1)} %bitcast.48), calls=%async_computation.2 | async-start | bytes 8388608
  84.1 5.3 %collective-permute-start.26 = (bf16[24,3072]{1,0:T(8,128)(2,1)S(1)}, bf16[24,3072]{1,0:T(8,128)(2,1)S(1)}, u32[]{:S(2)}, u32[]{:S(2)}) collective-permute-start(bf16[24,3072]{1,0:T(8,128)(2,1)S(1)} %get-tuple-element.86), channel_id=1, source_target_pairs={{0,2},{2,4},{4,6},{6,7},{7,5},{5,3},{3,1},{1,0},{8,10},{10,12},{12... | collective-permute-start | bytes 442376 | tf_op jit(solution)/shard_map/ppermute | solution.py:42
  85.4 5.7 %collective-permute-start.27 = (bf16[24,3072]{1,0:T(8,128)(2,1)S(1)}, bf16[24,3072]{1,0:T(8,128)(2,1)S(1)}, u32[]{:S(2)}, u32[]{:S(2)}) collective-permute-start(bf16[24,3072]{1,0:T(8,128)(2,1)S(1)} %get-tuple-element.85), channel_id=1, source_target_pairs={{2,0},{4,2},{6,4},{7,6},{5,7},{3,5},{1,3},{0,1},{10,8},{12,10},{14... | collective-permute-start | bytes 442376 | tf_op jit(solution)/shard_map/ppermute | solution.py:42
  86.2 7.2 %collective-permute-start.17 = (bf16[24,3072]{1,0:T(8,128)(2,1)S(1)}, bf16[24,3072]{1,0:T(8,128)(2,1)S(1)}, u32[]{:S(2)}, u32[]{:S(2)}) collective-permute-start(bf16[24,3072]{1,0:T(8,128)(2,1)S(1)} %get-tuple-element.76), channel_id=1, source_target_pairs={{0,2},{2,4},{4,6},{6,7},{7,5},{5,3},{3,1},{1,0},{8,10},{10,12},{12... | collective-permute-start | bytes 442376 | tf_op jit(solution)/shard_map/ppermute | solution.py:42
  87.6 6.8 %collective-permute-start.18 = (bf16[24,3072]{1,0:T(8,128)(2,1)S(1)}, bf16[24,3072]{1,0:T(8,128)(2,1)S(1)}, u32[]{:S(2)}, u32[]{:S(2)}) collective-permute-start(bf16[24,3072]{1,0:T(8,128)(2,1)S(1)} %get-tuple-element.75), channel_id=1, source_target_pairs={{2,0},{4,2},{6,4},{7,6},{5,7},{3,5},{1,3},{0,1},{10,8},{12,10},{14... | collective-permute-start | bytes 442376 | tf_op jit(solution)/shard_map/ppermute | solution.py:42
  91.3 10.0 %collective-permute-start.28 = (bf16[48,3072]{1,0:T(8,128)(2,1)S(1)}, bf16[48,3072]{1,0:T(8,128)(2,1)S(1)}, u32[]{:S(2)}, u32[]{:S(2)}) collective-permute-start(bf16[48,3072]{1,0:T(8,128)(2,1)S(1)} %pad_maximum_fusion.2), channel_id=1, source_target_pairs={{0,2},{2,4},{4,6},{6,7},{7,5},{5,3},{3,1},{1,0},{8,10},{10,12},{12... | collective-permute-start | bytes 884744 | tf_op jit(solution)/shard_map/ppermute | solution.py:42
  91.8 10.0 %collective-permute-start.29 = (bf16[48,3072]{1,0:T(8,128)(2,1)S(1)}, bf16[48,3072]{1,0:T(8,128)(2,1)S(1)}, u32[]{:S(2)}, u32[]{:S(2)}) collective-permute-start(bf16[48,3072]{1,0:T(8,128)(2,1)S(1)} %pad_maximum_fusion.3), channel_id=1, source_target_pairs={{2,0},{4,2},{6,4},{7,6},{5,7},{3,5},{1,3},{0,1},{10,8},{12,10},{14... | collective-permute-start | bytes 884744 | tf_op jit(solution)/shard_map/ppermute | solution.py:42
  94.4 13.2 %collective-permute-start.19 = (bf16[48,3072]{1,0:T(8,128)(2,1)S(1)}, bf16[48,3072]{1,0:T(8,128)(2,1)S(1)}, u32[]{:S(2)}, u32[]{:S(2)}) collective-permute-start(bf16[48,3072]{1,0:T(8,128)(2,1)S(1)} %pad_maximum_fusion), channel_id=1, source_target_pairs={{0,2},{2,4},{4,6},{6,7},{7,5},{5,3},{3,1},{1,0},{8,10},{10,12},{12... | collective-permute-start | bytes 884744 | tf_op jit(solution)/shard_map/ppermute | solution.py:42
  95.0 13.2 %collective-permute-start.20 = (bf16[48,3072]{1,0:T(8,128)(2,1)S(1)}, bf16[48,3072]{1,0:T(8,128)(2,1)S(1)}, u32[]{:S(2)}, u32[]{:S(2)}) collective-permute-start(bf16[48,3072]{1,0:T(8,128)(2,1)S(1)} %pad_maximum_fusion.1), channel_id=1, source_target_pairs={{2,0},{4,2},{6,4},{7,6},{5,7},{3,5},{1,3},{0,1},{10,8},{12,10},{14... | collective-permute-start | bytes 884744 | tf_op jit(solution)/shard_map/ppermute | solution.py:42
  101.9 28.7 %copy-start.2 = (s32[64,2]{0,1:T(2,128)S(1)}, s32[64,2]{0,1:T(2,128)}, u32[]{:S(2)}) copy-start(s32[64,2]{0,1:T(2,128)} %param.7) | copy-start | bytes 1540
  102.0 28.7 %copy-start.3 = (f32[64,2]{0,1:T(2,128)S(1)}, f32[64,2]{0,1:T(2,128)}, u32[]{:S(2)}) copy-start(f32[64,2]{0,1:T(2,128)} %param.8) | copy-start | bytes 1540
  102.0 11.9 %collective-permute-start.30 = (bf16[48,3072]{1,0:T(8,128)(2,1)S(1)}, bf16[48,3072]{1,0:T(8,128)(2,1)S(1)}, u32[]{:S(2)}, u32[]{:S(2)}) collective-permute-start(bf16[48,3072]{1,0:T(8,128)(2,1)S(1)} %get-tuple-element.82), channel_id=1, source_target_pairs={{0,2},{2,4},{4,6},{6,7},{7,5},{5,3},{3,1},{1,0},{8,10},{10,12},{12... | collective-permute-start | bytes 884744 | tf_op jit(solution)/shard_map/ppermute | solution.py:42
  102.5 12.0 %collective-permute-start.31 = (bf16[48,3072]{1,0:T(8,128)(2,1)S(1)}, bf16[48,3072]{1,0:T(8,128)(2,1)S(1)}, u32[]{:S(2)}, u32[]{:S(2)}) collective-permute-start(bf16[48,3072]{1,0:T(8,128)(2,1)S(1)} %get-tuple-element.81), channel_id=1, source_target_pairs={{2,0},{4,2},{6,4},{7,6},{5,7},{3,5},{1,3},{0,1},{10,8},{12,10},{14... | collective-permute-start | bytes 884744 | tf_op jit(solution)/shard_map/ppermute | solution.py:42
  108.1 25.1 %copy-start.1 = (bf16[64,6144]{1,0:T(8,128)(2,1)S(1)}, bf16[64,6144]{1,0:T(8,128)(2,1)}, u32[]{:S(2)}) copy-start(bf16[64,6144]{1,0:T(8,128)(2,1)} %param.6) | copy-start | bytes 2359300
  108.3 12.0 %collective-permute-start.21 = (bf16[48,3072]{1,0:T(8,128)(2,1)S(1)}, bf16[48,3072]{1,0:T(8,128)(2,1)S(1)}, u32[]{:S(2)}, u32[]{:S(2)}) collective-permute-start(bf16[48,3072]{1,0:T(8,128)(2,1)S(1)} %get-tuple-element.72), channel_id=1, source_target_pairs={{0,2},{2,4},{4,6},{6,7},{7,5},{5,3},{3,1},{1,0},{8,10},{10,12},{12... | collective-permute-start | bytes 884744 | tf_op jit(solution)/shard_map/ppermute | solution.py:42
  108.8 12.0 %collective-permute-start.22 = (bf16[48,3072]{1,0:T(8,128)(2,1)S(1)}, bf16[48,3072]{1,0:T(8,128)(2,1)S(1)}, u32[]{:S(2)}, u32[]{:S(2)}) collective-permute-start(bf16[48,3072]{1,0:T(8,128)(2,1)S(1)} %get-tuple-element.71), channel_id=1, source_target_pairs={{2,0},{4,2},{6,4},{7,6},{5,7},{3,5},{1,3},{0,1},{10,8},{12,10},{14... | collective-permute-start | bytes 884744 | tf_op jit(solution)/shard_map/ppermute | solution.py:42
  114.6 11.6 %collective-permute-start.32 = (bf16[48,3072]{1,0:T(8,128)(2,1)S(1)}, bf16[48,3072]{1,0:T(8,128)(2,1)S(1)}, u32[]{:S(2)}, u32[]{:S(2)}) collective-permute-start(bf16[48,3072]{1,0:T(8,128)(2,1)S(1)} %get-tuple-element.80), channel_id=1, source_target_pairs={{0,2},{2,4},{4,6},{6,7},{7,5},{5,3},{3,1},{1,0},{8,10},{10,12},{12... | collective-permute-start | bytes 884744 | tf_op jit(solution)/shard_map/ppermute | solution.py:42
  115.1 12.0 %collective-permute-start.33 = (bf16[48,3072]{1,0:T(8,128)(2,1)S(1)}, bf16[48,3072]{1,0:T(8,128)(2,1)S(1)}, u32[]{:S(2)}, u32[]{:S(2)}) collective-permute-start(bf16[48,3072]{1,0:T(8,128)(2,1)S(1)} %get-tuple-element.79), channel_id=1, source_target_pairs={{2,0},{4,2},{6,4},{7,6},{5,7},{3,5},{1,3},{0,1},{10,8},{12,10},{14... | collective-permute-start | bytes 884744 | tf_op jit(solution)/shard_map/ppermute | solution.py:42
  120.9 8.4 %collective-permute-start.23 = (bf16[48,3072]{1,0:T(8,128)(2,1)S(1)}, bf16[48,3072]{1,0:T(8,128)(2,1)S(1)}, u32[]{:S(2)}, u32[]{:S(2)}) collective-permute-start(bf16[48,3072]{1,0:T(8,128)(2,1)S(1)} %get-tuple-element.70), channel_id=1, source_target_pairs={{0,2},{2,4},{4,6},{6,7},{7,5},{5,3},{3,1},{1,0},{8,10},{10,12},{12... | collective-permute-start | bytes 884744 | tf_op jit(solution)/shard_map/ppermute | solution.py:42
  121.4 9.0 %collective-permute-start.24 = (bf16[48,3072]{1,0:T(8,128)(2,1)S(1)}, bf16[48,3072]{1,0:T(8,128)(2,1)S(1)}, u32[]{:S(2)}, u32[]{:S(2)}) collective-permute-start(bf16[48,3072]{1,0:T(8,128)(2,1)S(1)} %get-tuple-element.69), channel_id=1, source_target_pairs={{2,0},{4,2},{6,4},{7,6},{5,7},{3,5},{1,3},{0,1},{10,8},{12,10},{14... | collective-permute-start | bytes 884744 | tf_op jit(solution)/shard_map/ppermute | solution.py:42
  127.2 3.5 %collective-permute-start.34 = (bf16[24,3072]{1,0:T(8,128)(2,1)S(1)}, bf16[24,3072]{1,0:T(8,128)(2,1)S(1)}, u32[]{:S(2)}, u32[]{:S(2)}) collective-permute-start(bf16[24,3072]{1,0:T(8,128)(2,1)S(1)} %get-tuple-element.95), channel_id=1, source_target_pairs={{0,8},{8,0},{1,9},{9,1},{2,10},{10,2},{3,11},{11,3},{4,12},{12,4},... | collective-permute-start | bytes 442376 | tf_op jit(solution)/shard_map/ppermute | solution.py:102
  130.5 1.4 %collective-permute-start.25 = (bf16[24,3072]{1,0:T(8,128)(2,1)S(1)}, bf16[24,3072]{1,0:T(8,128)(2,1)S(1)}, u32[]{:S(2)}, u32[]{:S(2)}) collective-permute-start(bf16[24,3072]{1,0:T(8,128)(2,1)S(1)} %get-tuple-element.93), channel_id=1, source_target_pairs={{0,8},{8,0},{1,9},{9,1},{2,10},{10,2},{3,11},{11,3},{4,12},{12,4},... | collective-permute-start | bytes 442376 | tf_op jit(solution)/shard_map/ppermute | solution.py:102

commit v6 on v5

v6 whole, which is shorter than its diff:
```python
import jax
import jax.numpy as jnp
from jax import lax
from jax.experimental import pallas as pl
from jax.experimental.pallas import tpu as pltpu
from jax.sharding import PartitionSpec as P

CAP = 24
COPIES = 16


def ring_of(count):
    return list(range(0, count, 2)) + list(range(count - 1, 0, -2))


def fill_kernel(source, target, done):
    rows = source.shape[1] // COPIES
    copies = [
        pltpu.make_async_copy(
            source.at[:, pl.ds(i * rows, rows)], target.at[:, pl.ds(i * rows, rows)], done.at[i]
        )
        for i in range(COPIES)
    ]
    for copy in copies:
        copy.start()
    for copy in copies:
        copy.wait()


def fetched(weights):
    return pl.pallas_call(
        fill_kernel,
        in_specs=[pl.BlockSpec(memory_space=pltpu.HBM)],
        out_specs=pl.BlockSpec(memory_space=pltpu.VMEM),
        out_shape=pltpu.VMEM(weights.shape, weights.dtype),
        scratch_shapes=[pltpu.SemaphoreType.DMA((COPIES,))],
        cost_estimate=pl.CostEstimate(flops=1024, bytes_accessed=1024, transcendentals=0),
        compiler_params=pltpu.CompilerParams(vmem_limit_bytes=2**20),
        name="fetched",
    )(pltpu.with_memory_space_constraint(weights, pltpu.HBM))


def routing(expert_ids, gate_probs, experts, slots):
    matches = expert_ids[:, :, None] == experts[None, None, :]
    member = jnp.any(matches, axis=1).astype(jnp.int32)
    weight = jnp.sum(jnp.where(matches, gate_probs[:, :, None], jnp.float32(0.0)), axis=1)
    slot_index = jnp.cumsum(member, axis=0) - member
    column = jnp.arange(slots)
    dispatch_map = (member[None, :, :] == 1) & (slot_index[None, :, :] == column[:, None, None])
    return (jnp.transpose(dispatch_map, (2, 0, 1)), weight)


def product(rows, weights):
    return jnp.dot(rows, weights, preferred_element_type=jnp.float32)


def activated(gate, up):
    return (jax.nn.silu(gate) * up).astype(jnp.bfloat16)


def per_device(tokens, expert_ids, gate_probs, w_gate, w_up, w_down):
    n_tensor = lax.axis_size("tensor")
    half = n_tensor // 2
    block_rows = 2 * CAP
    ring = ring_of(n_tensor)
    right = [(ring[i], ring[(i + 1) % n_tensor]) for i in range(n_tensor)]
    left = [(b, a) for a, b in right]
    swap = [(0, 1), (1, 0)]

    def step(to_right, to_left):
        pair = (lax.ppermute(to_right, "tensor", right), lax.ppermute(to_left, "tensor", left))
        return lax.optimization_barrier(pair)

    def before(pair, *others):
        return lax.optimization_barrier((pair, *others))

    me = lax.axis_index("expert")
    experts = jnp.stack([me, 1 - me])
    dispatch_map, weight = routing(expert_ids, gate_probs, experts, CAP)
    outgoing = jnp.dot(
        dispatch_map.astype(jnp.bfloat16).reshape(block_rows, tokens.shape[0]),
        tokens,
        preferred_element_type=jnp.float32,
    ).astype(jnp.bfloat16)
    own = jnp.concatenate([outgoing[:CAP], lax.ppermute(outgoing[CAP:], "expert", swap)], axis=0)

    blocks = [[own]]
    own, w_gate, w_up = before(own, w_gate, w_up)
    pair = step(own, own)
    gate_here, up_here = fetched(w_gate), fetched(w_up)
    pair, gate_here, up_here = before(pair, gate_here, up_here)
    blocks.append(list(pair))
    for distance in range(2, half - 1):
        pair = step(*pair)
        blocks.append(list(pair))
    near = jnp.concatenate(sum(blocks, []), axis=0)
    pair = step(*pair)
    near_hidden = activated(product(near, gate_here[0]), product(near, up_here[0]))
    pair, near_hidden = before(pair, near_hidden)
    far = jnp.concatenate(step(pair[0][:CAP], pair[1][CAP:]), axis=0)
    rest = jnp.concatenate([*pair, far], axis=0)
    rest_hidden = lax.optimization_barrier(activated(product(rest, gate_here[0]), product(rest, up_here[0])))

    def block_of(part, index):
        return part[index * block_rows:(index + 1) * block_rows].astype(jnp.float32)

    rest_part = product(rest_hidden, w_down[0]).astype(jnp.bfloat16)
    far_part = rest_part[2 * block_rows:]
    pair = step(far_part[:CAP], far_part[CAP:])
    got_a, got_b = (part.astype(jnp.float32) for part in pair)
    send_b, send_a = block_of(rest_part, 0), block_of(rest_part, 1)
    send_a = jnp.concatenate([send_a[:CAP] + got_a, send_a[CAP:]], axis=0)
    send_b = jnp.concatenate([send_b[:CAP], send_b[CAP:] + got_b], axis=0)
    near_hidden, send_a, send_b = before(near_hidden, send_a.astype(jnp.bfloat16), send_b.astype(jnp.bfloat16))
    pair = step(send_a, send_b)
    near_part = product(near_hidden, w_down[0]).astype(jnp.bfloat16)
    for distance in range(half - 2, 0, -1):
        got_a, got_b = (part.astype(jnp.float32) for part in pair)
        send_b, send_a = (block_of(near_part, 2 * distance - 1 + side) for side in range(2))
        pair = step((send_a + got_a).astype(jnp.bfloat16), (send_b + got_b).astype(jnp.bfloat16))
    got_a, got_b = (part.astype(jnp.float32) for part in pair)
    total = (block_of(near_part, 0) + got_a + got_b).astype(jnp.bfloat16)

    returned = jnp.stack([total[:CAP], lax.ppermute(total[CAP:], "expert", swap)])
    combine = dispatch_map.astype(jnp.float32) * jnp.transpose(weight)[:, None, :]
    mixed = jnp.einsum("wcr,wcd->rd", combine, returned.astype(jnp.float32))
    return mixed.astype(jnp.bfloat16)


def solution(mesh):
    in_specs = (
        P(("groups", "expert", "tensor"), None),
        P(("groups", "expert", "tensor"), None),
        P(("groups", "expert", "tensor"), None),
        P("expert", None, "tensor"),
        P("expert", None, "tensor"),
        P("expert", "tensor", None),
    )
    out_specs = P(("groups", "expert", "tensor"), None)
    return jax.shard_map(
        per_device, mesh=mesh, in_specs=in_specs, out_specs=out_specs, check_vma=False
    )
```

time: 133 us -> 130 us (0.977)
  starting transfers between devices: 34.8 us -> 18.2 us
  Pallas kernels: 0 us -> 9.45 us
  waiting for transfers between devices: 71.8 us -> 76 us
    ppermute x15 -> x8, starting transfers between devices: 18.2 us -> 6.76 us  [step(): lax.ppermute(to_right, 'tensor', right)]
    pallas_call x0 -> x2, Pallas kernels: none -> 9.45 us  [fetched(): pl.pallas_call(fill_kernel, in_specs=[pl.BlockSpec(memory_space=pltpu.HBM...]
    ppermute x15 -> x8, waiting for transfers between devices: 35 us -> 41.5 us  [step(): lax.ppermute(to_left, 'tensor', left)]
    ppermute x15 -> x8, starting transfers between devices: 14.3 us -> 10.9 us  [step(): lax.ppermute(to_left, 'tensor', left)]
    ppermute x3 -> x1, starting transfers between devices: 2.13 us -> 0.52 us  [per_device(): lax.ppermute(outgoing[CAP:], 'expert', swap)]
    ppermute x15 -> x8, waiting for transfers between devices: 33.3 us -> 31.8 us  [step(): lax.ppermute(to_right, 'tensor', right)]
    dot_general x4 -> x6, matrix products: 21.6 us -> 21.2 us  [product(): return jnp.dot(rows, weights, preferred_element_type=jnp.float32)]
  transfers between devices with their start and end apart: 35 -> 18, of which waited for: 28 -> 18; matrix products, arithmetic and copies ran while one was open for 1% -> 8% of each run, Pallas kernels for 0% -> 7%
where the time goes in v6:
time: 130 us
  waiting for transfers between devices  76 us (58%)
  matrix products  22.8 us (18%)
  starting transfers between devices  18.2 us (14%)
  Pallas kernels  9.45 us (7%)
  other arithmetic  2.27 us (2%)
    ppermute x8, waiting for transfers between devices, step(): lax.ppermute(to_left, 'tensor', left)  41.5 us
    ppermute x8, waiting for transfers between devices, step(): lax.ppermute(to_right, 'tensor', right)  31.8 us
    dot_general x6, matrix products, product(): return jnp.dot(rows, weights, preferred_element_type=jnp.float32)  21.2 us
    ppermute x8, starting transfers between devices, step(): lax.ppermute(to_left, 'tensor', left)  10.9 us
    pallas_call x2, Pallas kernels, fetched(): pl.pallas_call(fill_kernel, in_specs=[pl.BlockSpec(memory_space=pltpu.HBM...  9.45 us
    ppermute x8, starting transfers between devices, step(): lax.ppermute(to_right, 'tensor', right)  6.76 us
  transfers between devices with their start and end apart: 18, of which 18 were waited for; matrix products, arithmetic and copies ran while one was open for 8% of the time, Pallas kernels for 7%

profile of v6, /device:TPU:0, one launch (start us, length us, event | category | flops | bytes accessed | tf_op | source)
XLA Modules:
  0.0 129.8 jit_solution(12756597399891377622)
XLA Ops:
  0.0 0.1 eq.64
  0.1 0.1 pad_add_fusion
  0.2 0.8 compare_reduce_fusion
  1.0 0.1 copy.17
  1.1 0.1 reduce_window_sum.11
  1.2 0.1 copy.18
  1.3 0.1 fusion.37
  1.4 0.3 convolution_convert_fusion
  1.7 0.1 constant_dynamic-update-slice_fusion.5
  1.8 0.5 collective-permute-start
  2.3 1.2 collective-permute-done
  3.5 2.9 %collective-permute-start.2 = (bf16[48,6144]{1,0:T(8,128)(2,1)S(1)}, bf16[48,6144]{1,0:T(8,128)(2,1)S(1)}, u32[]{:S(2)}, u32[]{:S(2)}) collective-permute-start(bf16[48,6144]{1,0:T(8,128)(2,1)S(1)} %pad_maximum_fusion), channel_id=1, source_target_pairs={{2,0},{4,2},{6,4},{7,6},{5,7},{3,5},{1,3},{0,1},{10,8},{12,10},{14... | collective-permute-start | bytes 1769480 | tf_op jit(solution)/shard_map/ppermute | solution.py:71
  6.5 0.1 collective-permute-start.1
  6.6 4.7 %fetched.2 = bf16[1,6144,1024]{2,1,0:T(8,128)(2,1)S(1)} custom-call(bf16[1,6144,1024]{2,1,0:T(8,128)(2,1)} %source), custom_call_target="tpu_custom_call" | custom-call | flops 1024 | bytes 1024 | tf_op jit(solution)/shard_map/fetched/pallas_call | solution.py:31
  11.3 4.7 %fetched.3 = bf16[1,6144,1024]{2,1,0:T(8,128)(2,1)S(1)} custom-call(bf16[1,6144,1024]{2,1,0:T(8,128)(2,1)} %source.1), custom_call_target="tpu_custom_call" | custom-call | flops 1024 | bytes 1024 | tf_op jit(solution)/shard_map/fetched/pallas_call | solution.py:31
  16.1 4.1 %collective-permute-done.2 = bf16[48,6144]{1,0:T(8,128)(2,1)S(1)} collective-permute-done((bf16[48,6144]{1,0:T(8,128)(2,1)S(1)}, bf16[48,6144]{1,0:T(8,128)(2,1)S(1)}, u32[]{:S(2)}, u32[]{:S(2)}) %collective-permute-start.2) | collective-permute-done | bytes 589856 | tf_op jit(solution)/shard_map/ppermute | solution.py:71
  20.2 1.4 %collective-permute-done.1 = bf16[48,6144]{1,0:T(8,128)(2,1)S(1)} collective-permute-done((bf16[48,6144]{1,0:T(8,128)(2,1)S(1)}, bf16[48,6144]{1,0:T(8,128)(2,1)S(1)}, u32[]{:S(2)}, u32[]{:S(2)}) %collective-permute-start.1) | collective-permute-done | bytes 589856 | tf_op jit(solution)/shard_map/ppermute | solution.py:71
  21.6 0.4 collective-permute-start.3
  22.0 1.7 %collective-permute-start.4 = (bf16[48,6144]{1,0:T(8,128)(2,1)S(1)}, bf16[48,6144]{1,0:T(8,128)(2,1)S(1)}, u32[]{:S(2)}, u32[]{:S(2)}) collective-permute-start(bf16[48,6144]{1,0:T(8,128)(2,1)S(1)} %collective-permute-done.2), channel_id=1, source_target_pairs={{2,0},{4,2},{6,4},{7,6},{5,7},{3,5},{1,3},{0,1},{10,8},{12,10},{14... | collective-permute-start | bytes 1769480 | tf_op jit(solution)/shard_map/ppermute | solution.py:71
  23.7 12.1 %collective-permute-done.3 = bf16[48,6144]{1,0:T(8,128)(2,1)S(1)} collective-permute-done((bf16[48,6144]{1,0:T(8,128)(2,1)S(1)}, bf16[48,6144]{1,0:T(8,128)(2,1)S(1)}, u32[]{:S(2)}, u32[]{:S(2)}) %collective-permute-start.3) | collective-permute-done | bytes 589856 | tf_op jit(solution)/shard_map/ppermute | solution.py:71
  35.8 0.5 collective-permute-done.4
  36.3 1.5 %collective-permute-start.5 = (bf16[48,6144]{1,0:T(8,128)(2,1)S(1)}, bf16[48,6144]{1,0:T(8,128)(2,1)S(1)}, u32[]{:S(2)}, u32[]{:S(2)}) collective-permute-start(bf16[48,6144]{1,0:T(8,128)(2,1)S(1)} %collective-permute-done.3), channel_id=1, source_target_pairs={{0,2},{2,4},{4,6},{6,7},{7,5},{5,3},{3,1},{1,0},{8,10},{10,12},{12... | collective-permute-start | bytes 1769480 | tf_op jit(solution)/shard_map/ppermute | solution.py:71
  37.9 0.6 collective-permute-start.6
  38.5 3.2 %fusion.10 = f32[240,1024]{1,0:T(8,128)S(1)} fusion(bf16[240,6144]{1,0:T(8,128)(2,1)S(1)} %constant_dynamic-update-slice_fusion, bf16[1,6144,1024]{2,1,0:T(8,128)(2,1)S(1)} %fetched.2), kind=kOutput, calls=%fused_computation.10 | convolution fusion | flops 3019898880 | bytes 16515072 | tf_op jit(solution)/shard_map/dot_general | solution.py:54
  41.7 3.4 %fusion.22 = bf16[240,1024]{1,0:T(8,128)(2,1)S(1)} fusion(bf16[240,6144]{1,0:T(8,128)(2,1)S(1)} %constant_dynamic-update-slice_fusion, bf16[1,6144,1024]{2,1,0:T(8,128)(2,1)S(1)} %fetched.3, f32[240,1024]{1,0:T(8,128)S(1)} %fusion.10), kind=kOutput, calls=%fused_computation.18 | convolution fusion | flops 3021373440 | bytes 17006592 | tf_op jit(solution)/shard_map/dot_general | solution.py:54
  45.1 4.5 %collective-permute-done.5 = bf16[48,6144]{1,0:T(8,128)(2,1)S(1)} collective-permute-done((bf16[48,6144]{1,0:T(8,128)(2,1)S(1)}, bf16[48,6144]{1,0:T(8,128)(2,1)S(1)}, u32[]{:S(2)}, u32[]{:S(2)}) %collective-permute-start.5) | collective-permute-done | bytes 589856 | tf_op jit(solution)/shard_map/ppermute | solution.py:71
  49.7 1.6 %collective-permute-done.6 = bf16[48,6144]{1,0:T(8,128)(2,1)S(1)} collective-permute-done((bf16[48,6144]{1,0:T(8,128)(2,1)S(1)}, bf16[48,6144]{1,0:T(8,128)(2,1)S(1)}, u32[]{:S(2)}, u32[]{:S(2)}) %collective-permute-start.6) | collective-permute-done | bytes 589856 | tf_op jit(solution)/shard_map/ppermute | solution.py:71
  51.4 0.6 collective-permute-start.8
  51.9 1.5 %collective-permute-start.7 = (bf16[24,6144]{1,0:T(8,128)(2,1)S(1)}, bf16[24,6144]{1,0:T(8,128)(2,1)S(1)}, u32[]{:S(2)}, u32[]{:S(2)}) collective-permute-start(bf16[24,6144]{1,0:T(8,128)(2,1)S(1)} %slice.70), channel_id=1, source_target_pairs={{0,2},{2,4},{4,6},{6,7},{7,5},{5,3},{3,1},{1,0},{8,10},{10,12},{12... | collective-permute-start | bytes 884744 | tf_op jit(solution)/shard_map/ppermute | solution.py:71
  53.5 4.7 %collective-permute-done.8 = bf16[24,6144]{1,0:T(8,128)(2,1)S(1)} collective-permute-done((bf16[24,6144]{1,0:T(8,128)(2,1)S(1)}, bf16[24,6144]{1,0:T(8,128)(2,1)S(1)}, u32[]{:S(2)}, u32[]{:S(2)}) %collective-permute-start.8) | collective-permute-done | bytes 294944 | tf_op jit(solution)/shard_map/ppermute | solution.py:71
  58.1 0.5 collective-permute-done.7
  58.7 2.0 %fusion.8 = f32[144,1024]{1,0:T(8,128)S(1)} fusion(bf16[144,6144]{1,0:T(8,128)(2,1)S(1)} %constant_dynamic-update-slice_fusion.6, bf16[1,6144,1024]{2,1,0:T(8,128)(2,1)S(1)} %fetched.2), kind=kOutput, calls=%fused_computation.8 | convolution fusion | flops 1811939328 | bytes 14942208 | tf_op jit(solution)/shard_map/dot_general | solution.py:54
  60.7 0.0 slice-start
  60.8 0.0 slice-start.1
  60.8 2.2 %fusion.28 = bf16[144,1024]{1,0:T(8,128)(2,1)S(1)} fusion(bf16[144,6144]{1,0:T(8,128)(2,1)S(1)} %constant_dynamic-update-slice_fusion.6, bf16[1,6144,1024]{2,1,0:T(8,128)(2,1)S(1)} %fetched.3, f32[144,1024]{1,0:T(8,128)S(1)} %fusion.8), kind=kOutput, calls=%fused_computation.20 | convolution fusion | flops 1812824064 | bytes 15237120 | tf_op jit(solution)/shard_map/dot_general | solution.py:54
  62.9 0.0 slice-start.2
  63.0 6.9 %fusion.15 = bf16[144,6144]{1,0:T(8,128)(2,1)S(1)} fusion(bf16[144,1024]{1,0:T(8,128)(2,1)S(1)} %fusion.28, bf16[1,1024,6144]{2,1,0:T(8,128)(2,1)} %param.11), kind=kOutput, calls=%fused_computation.13 | convolution fusion | flops 1812824064 | bytes 14647296 | tf_op jit(solution)/shard_map/dot_general | solution.py:54
  69.8 0.1 fusion.45
  69.9 1.3 %collective-permute-start.10 = (bf16[24,6144]{1,0:T(8,128)(2,1)S(1)}, bf16[24,6144]{1,0:T(8,128)(2,1)S(1)}, u32[]{:S(2)}, u32[]{:S(2)}) collective-permute-start(bf16[24,6144]{1,0:T(8,128)(2,1)S(1)} %get-tuple-element.69), channel_id=1, source_target_pairs={{2,0},{4,2},{6,4},{7,6},{5,7},{3,5},{1,3},{0,1},{10,8},{12,10},{14... | collective-permute-start | bytes 884744 | tf_op jit(solution)/shard_map/ppermute | solution.py:71
  71.2 0.8 collective-permute-start.9
  72.0 6.2 %collective-permute-done.10 = bf16[24,6144]{1,0:T(8,128)(2,1)S(1)} collective-permute-done((bf16[24,6144]{1,0:T(8,128)(2,1)S(1)}, bf16[24,6144]{1,0:T(8,128)(2,1)S(1)}, u32[]{:S(2)}, u32[]{:S(2)}) %collective-permute-start.10) | collective-permute-done | bytes 294944 | tf_op jit(solution)/shard_map/ppermute | solution.py:71
  78.2 2.9 %collective-permute-done.9 = bf16[24,6144]{1,0:T(8,128)(2,1)S(1)} collective-permute-done((bf16[24,6144]{1,0:T(8,128)(2,1)S(1)}, bf16[24,6144]{1,0:T(8,128)(2,1)S(1)}, u32[]{:S(2)}, u32[]{:S(2)}) %collective-permute-start.9) | collective-permute-done | bytes 294944 | tf_op jit(solution)/shard_map/ppermute | solution.py:71
  81.1 0.1 add_convert_fusion.5
  81.2 0.1 pad_maximum_fusion.1
  81.3 0.8 collective-permute-start.11
  82.2 1.2 collective-permute-start.12
  83.4 3.5 %fusion.12 = bf16[240,6144]{1,0:T(8,128)(2,1)S(1)} fusion(bf16[240,1024]{1,0:T(8,128)(2,1)S(1)} %fusion.22, bf16[1,1024,6144]{2,1,0:T(8,128)(2,1)S(1)} %bitcast.56), kind=kOutput, calls=%fused_computation.12 | convolution fusion | flops 3021373440 | bytes 16023552 | tf_op jit(solution)/shard_map/dot_general | solution.py:54
  87.0 7.9 %collective-permute-done.11 = bf16[48,6144]{1,0:T(8,128)(2,1)S(1)} collective-permute-done((bf16[48,6144]{1,0:T(8,128)(2,1)S(1)}, bf16[48,6144]{1,0:T(8,128)(2,1)S(1)}, u32[]{:S(2)}, u32[]{:S(2)}) %collective-permute-start.11) | collective-permute-done | bytes 589856 | tf_op jit(solution)/shard_map/ppermute | solution.py:71
  94.9 3.0 %collective-permute-done.12 = bf16[48,6144]{1,0:T(8,128)(2,1)S(1)} collective-permute-done((bf16[48,6144]{1,0:T(8,128)(2,1)S(1)}, bf16[48,6144]{1,0:T(8,128)(2,1)S(1)}, u32[]{:S(2)}, u32[]{:S(2)}) %collective-permute-start.12) | collective-permute-done | bytes 589856 | tf_op jit(solution)/shard_map/ppermute | solution.py:71
  97.9 0.3 add_convert_fusion.3
  98.2 0.9 collective-permute-start.14
  99.1 1.2 collective-permute-start.13
  100.3 13.6 %collective-permute-done.14 = bf16[48,6144]{1,0:T(8,128)(2,1)S(1)} collective-permute-done((bf16[48,6144]{1,0:T(8,128)(2,1)S(1)}, bf16[48,6144]{1,0:T(8,128)(2,1)S(1)}, u32[]{:S(2)}, u32[]{:S(2)}) %collective-permute-start.14) | collective-permute-done | bytes 589856 | tf_op jit(solution)/shard_map/ppermute | solution.py:71
  113.8 1.0 collective-permute-done.13
  114.8 0.3 add_convert_fusion.1
  115.1 1.6 %collective-permute-start.16 = (bf16[48,6144]{1,0:T(8,128)(2,1)S(1)}, bf16[48,6144]{1,0:T(8,128)(2,1)S(1)}, u32[]{:S(2)}, u32[]{:S(2)}) collective-permute-start(bf16[48,6144]{1,0:T(8,128)(2,1)S(1)} %get-tuple-element.63), channel_id=1, source_target_pairs={{2,0},{4,2},{6,4},{7,6},{5,7},{3,5},{1,3},{0,1},{10,8},{12,10},{14... | collective-permute-start | bytes 1769480 | tf_op jit(solution)/shard_map/ppermute | solution.py:71
  116.7 0.4 collective-permute-start.15
  117.2 7.9 %collective-permute-done.16 = bf16[48,6144]{1,0:T(8,128)(2,1)S(1)} collective-permute-done((bf16[48,6144]{1,0:T(8,128)(2,1)S(1)}, bf16[48,6144]{1,0:T(8,128)(2,1)S(1)}, u32[]{:S(2)}, u32[]{:S(2)}) %collective-permute-start.16) | collective-permute-done | bytes 589856 | tf_op jit(solution)/shard_map/ppermute | solution.py:71
  125.0 1.6 %collective-permute-done.15 = bf16[48,6144]{1,0:T(8,128)(2,1)S(1)} collective-permute-done((bf16[48,6144]{1,0:T(8,128)(2,1)S(1)}, bf16[48,6144]{1,0:T(8,128)(2,1)S(1)}, u32[]{:S(2)}, u32[]{:S(2)}) %collective-permute-start.15) | collective-permute-done | bytes 589856 | tf_op jit(solution)/shard_map/ppermute | solution.py:71
  126.6 0.2 add_convert_fusion
  126.9 0.1 collective-permute-start.17
  127.0 0.1 fusion.42
  127.1 1.5 %collective-permute-done.17 = bf16[24,6144]{1,0:T(8,128)(2,1)S(1)} collective-permute-done((bf16[24,6144]{1,0:T(8,128)(2,1)S(1)}, bf16[24,6144]{1,0:T(8,128)(2,1)S(1)}, u32[]{:S(2)}, u32[]{:S(2)}) %collective-permute-start.17) | collective-permute-done | bytes 294944 | tf_op jit(solution)/shard_map/ppermute | solution.py:124
  128.5 1.3 fusion.18
  (28 shorter events, 0.5 us)
Async XLA Ops:
  0.0 1.4 %copy-start = (bf16[64,6144]{1,0:T(8,128)(2,1)S(1)}, bf16[64,6144]{1,0:T(8,128)(2,1)}, u32[]{:S(2)}) copy-start(bf16[64,6144]{1,0:T(8,128)(2,1)} %param.6) | copy-start | bytes 2359300
  1.8 1.7 %collective-permute-start = (bf16[24,6144]{1,0:T(8,128)(2,1)S(1)}, bf16[24,6144]{1,0:T(8,128)(2,1)S(1)}, u32[]{:S(2)}, u32[]{:S(2)}) collective-permute-start(bf16[24,6144]{1,0:T(8,128)(2,1)S(1)} %get-tuple-element.76), channel_id=1, source_target_pairs={{0,8},{8,0},{1,9},{9,1},{2,10},{10,2},{3,11},{11,3},{4,12},{12,4},... | collective-permute-start | bytes 884744 | tf_op jit(solution)/shard_map/ppermute | solution.py:85
  3.5 16.6 %collective-permute-start.2 = (bf16[48,6144]{1,0:T(8,128)(2,1)S(1)}, bf16[48,6144]{1,0:T(8,128)(2,1)S(1)}, u32[]{:S(2)}, u32[]{:S(2)}) collective-permute-start(bf16[48,6144]{1,0:T(8,128)(2,1)S(1)} %pad_maximum_fusion), channel_id=1, source_target_pairs={{2,0},{4,2},{6,4},{7,6},{5,7},{3,5},{1,3},{0,1},{10,8},{12,10},{14... | collective-permute-start | bytes 1769480 | tf_op jit(solution)/shard_map/ppermute | solution.py:71
  6.5 15.1 %collective-permute-start.1 = (bf16[48,6144]{1,0:T(8,128)(2,1)S(1)}, bf16[48,6144]{1,0:T(8,128)(2,1)S(1)}, u32[]{:S(2)}, u32[]{:S(2)}) collective-permute-start(bf16[48,6144]{1,0:T(8,128)(2,1)S(1)} %pad_maximum_fusion), channel_id=1, source_target_pairs={{0,2},{2,4},{4,6},{6,7},{7,5},{5,3},{3,1},{1,0},{8,10},{10,12},{12... | collective-permute-start | bytes 1769480 | tf_op jit(solution)/shard_map/ppermute | solution.py:71
  21.6 14.2 %collective-permute-start.3 = (bf16[48,6144]{1,0:T(8,128)(2,1)S(1)}, bf16[48,6144]{1,0:T(8,128)(2,1)S(1)}, u32[]{:S(2)}, u32[]{:S(2)}) collective-permute-start(bf16[48,6144]{1,0:T(8,128)(2,1)S(1)} %collective-permute-done.1), channel_id=1, source_target_pairs={{0,2},{2,4},{4,6},{6,7},{7,5},{5,3},{3,1},{1,0},{8,10},{10,12},{12... | collective-permute-start | bytes 1769480 | tf_op jit(solution)/shard_map/ppermute | solution.py:71
  22.0 14.3 %collective-permute-start.4 = (bf16[48,6144]{1,0:T(8,128)(2,1)S(1)}, bf16[48,6144]{1,0:T(8,128)(2,1)S(1)}, u32[]{:S(2)}, u32[]{:S(2)}) collective-permute-start(bf16[48,6144]{1,0:T(8,128)(2,1)S(1)} %collective-permute-done.2), channel_id=1, source_target_pairs={{2,0},{4,2},{6,4},{7,6},{5,7},{3,5},{1,3},{0,1},{10,8},{12,10},{14... | collective-permute-start | bytes 1769480 | tf_op jit(solution)/shard_map/ppermute | solution.py:71
  36.3 13.3 %collective-permute-start.5 = (bf16[48,6144]{1,0:T(8,128)(2,1)S(1)}, bf16[48,6144]{1,0:T(8,128)(2,1)S(1)}, u32[]{:S(2)}, u32[]{:S(2)}) collective-permute-start(bf16[48,6144]{1,0:T(8,128)(2,1)S(1)} %collective-permute-done.3), channel_id=1, source_target_pairs={{0,2},{2,4},{4,6},{6,7},{7,5},{5,3},{3,1},{1,0},{8,10},{10,12},{12... | collective-permute-start | bytes 1769480 | tf_op jit(solution)/shard_map/ppermute | solution.py:71
  37.9 13.4 %collective-permute-start.6 = (bf16[48,6144]{1,0:T(8,128)(2,1)S(1)}, bf16[48,6144]{1,0:T(8,128)(2,1)S(1)}, u32[]{:S(2)}, u32[]{:S(2)}) collective-permute-start(bf16[48,6144]{1,0:T(8,128)(2,1)S(1)} %collective-permute-done.4), channel_id=1, source_target_pairs={{2,0},{4,2},{6,4},{7,6},{5,7},{3,5},{1,3},{0,1},{10,8},{12,10},{14... | collective-permute-start | bytes 1769480 | tf_op jit(solution)/shard_map/ppermute | solution.py:71
  51.4 6.8 %collective-permute-start.8 = (bf16[24,6144]{1,0:T(8,128)(2,1)S(1)}, bf16[24,6144]{1,0:T(8,128)(2,1)S(1)}, u32[]{:S(2)}, u32[]{:S(2)}) collective-permute-start(bf16[24,6144]{1,0:T(8,128)(2,1)S(1)} %slice.71), channel_id=1, source_target_pairs={{2,0},{4,2},{6,4},{7,6},{5,7},{3,5},{1,3},{0,1},{10,8},{12,10},{14... | collective-permute-start | bytes 884744 | tf_op jit(solution)/shard_map/ppermute | solution.py:71
  51.9 6.7 %collective-permute-start.7 = (bf16[24,6144]{1,0:T(8,128)(2,1)S(1)}, bf16[24,6144]{1,0:T(8,128)(2,1)S(1)}, u32[]{:S(2)}, u32[]{:S(2)}) collective-permute-start(bf16[24,6144]{1,0:T(8,128)(2,1)S(1)} %slice.70), channel_id=1, source_target_pairs={{0,2},{2,4},{4,6},{6,7},{7,5},{5,3},{3,1},{1,0},{8,10},{10,12},{12... | collective-permute-start | bytes 884744 | tf_op jit(solution)/shard_map/ppermute | solution.py:71
  60.7 22.7 %slice-start = ((s8[12582912]{0:T(1024)(128)(4,1)}), s8[4194304]{0:T(1024)(128)(4,1)S(1)}, s32[]{:S(2)}) async-start(s8[12582912]{0:T(1024)(128)(4,1)} %bitcast.55), calls=%async_computation | async-start | bytes 8388608
  60.8 22.7 %slice-start.1 = ((s8[12582912]{0:T(1024)(128)(4,1)}), s8[4194304]{0:T(1024)(128)(4,1)S(1)}, s32[]{:S(2)}) async-start(s8[12582912]{0:T(1024)(128)(4,1)} %bitcast.55), calls=%async_computation.1 | async-start | bytes 8388608
  62.9 20.5 %slice-start.2 = ((s8[12582912]{0:T(1024)(128)(4,1)}), s8[4194304]{0:T(1024)(128)(4,1)S(1)}, s32[]{:S(2)}) async-start(s8[12582912]{0:T(1024)(128)(4,1)} %bitcast.55), calls=%async_computation.2 | async-start | bytes 8388608
  69.9 8.3 %collective-permute-start.10 = (bf16[24,6144]{1,0:T(8,128)(2,1)S(1)}, bf16[24,6144]{1,0:T(8,128)(2,1)S(1)}, u32[]{:S(2)}, u32[]{:S(2)}) collective-permute-start(bf16[24,6144]{1,0:T(8,128)(2,1)S(1)} %get-tuple-element.69), channel_id=1, source_target_pairs={{2,0},{4,2},{6,4},{7,6},{5,7},{3,5},{1,3},{0,1},{10,8},{12,10},{14... | collective-permute-start | bytes 884744 | tf_op jit(solution)/shard_map/ppermute | solution.py:71
  71.2 9.8 %collective-permute-start.9 = (bf16[24,6144]{1,0:T(8,128)(2,1)S(1)}, bf16[24,6144]{1,0:T(8,128)(2,1)S(1)}, u32[]{:S(2)}, u32[]{:S(2)}) collective-permute-start(bf16[24,6144]{1,0:T(8,128)(2,1)S(1)} %get-tuple-element.70), channel_id=1, source_target_pairs={{0,2},{2,4},{4,6},{6,7},{7,5},{5,3},{3,1},{1,0},{8,10},{10,12},{12... | collective-permute-start | bytes 884744 | tf_op jit(solution)/shard_map/ppermute | solution.py:71
  81.3 13.5 %collective-permute-start.11 = (bf16[48,6144]{1,0:T(8,128)(2,1)S(1)}, bf16[48,6144]{1,0:T(8,128)(2,1)S(1)}, u32[]{:S(2)}, u32[]{:S(2)}) collective-permute-start(bf16[48,6144]{1,0:T(8,128)(2,1)S(1)} %get-tuple-element.55), channel_id=1, source_target_pairs={{0,2},{2,4},{4,6},{6,7},{7,5},{5,3},{3,1},{1,0},{8,10},{10,12},{12... | collective-permute-start | bytes 1769480 | tf_op jit(solution)/shard_map/ppermute | solution.py:71
  82.2 15.7 %collective-permute-start.12 = (bf16[48,6144]{1,0:T(8,128)(2,1)S(1)}, bf16[48,6144]{1,0:T(8,128)(2,1)S(1)}, u32[]{:S(2)}, u32[]{:S(2)}) collective-permute-start(bf16[48,6144]{1,0:T(8,128)(2,1)S(1)} %get-tuple-element.56), channel_id=1, source_target_pairs={{2,0},{4,2},{6,4},{7,6},{5,7},{3,5},{1,3},{0,1},{10,8},{12,10},{14... | collective-permute-start | bytes 1769480 | tf_op jit(solution)/shard_map/ppermute | solution.py:71
  98.2 15.6 %collective-permute-start.14 = (bf16[48,6144]{1,0:T(8,128)(2,1)S(1)}, bf16[48,6144]{1,0:T(8,128)(2,1)S(1)}, u32[]{:S(2)}, u32[]{:S(2)}) collective-permute-start(bf16[48,6144]{1,0:T(8,128)(2,1)S(1)} %get-tuple-element.65), channel_id=1, source_target_pairs={{2,0},{4,2},{6,4},{7,6},{5,7},{3,5},{1,3},{0,1},{10,8},{12,10},{14... | collective-permute-start | bytes 1769480 | tf_op jit(solution)/shard_map/ppermute | solution.py:71
  99.1 27.9 %copy-start.2 = (s32[64,2]{0,1:T(2,128)S(1)}, s32[64,2]{0,1:T(2,128)}, u32[]{:S(2)}) copy-start(s32[64,2]{0,1:T(2,128)} %param.7) | copy-start | bytes 1540
  99.1 27.9 %copy-start.3 = (f32[64,2]{0,1:T(2,128)S(1)}, f32[64,2]{0,1:T(2,128)}, u32[]{:S(2)}) copy-start(f32[64,2]{0,1:T(2,128)} %param.8) | copy-start | bytes 1540
  99.1 15.7 %collective-permute-start.13 = (bf16[48,6144]{1,0:T(8,128)(2,1)S(1)}, bf16[48,6144]{1,0:T(8,128)(2,1)S(1)}, u32[]{:S(2)}, u32[]{:S(2)}) collective-permute-start(bf16[48,6144]{1,0:T(8,128)(2,1)S(1)} %get-tuple-element.66), channel_id=1, source_target_pairs={{0,2},{2,4},{4,6},{6,7},{7,5},{5,3},{3,1},{1,0},{8,10},{10,12},{12... | collective-permute-start | bytes 1769480 | tf_op jit(solution)/shard_map/ppermute | solution.py:71
  114.8 15.1 %copy-start.1 = (bf16[64,6144]{1,0:T(8,128)(2,1)S(1)}, bf16[64,6144]{1,0:T(8,128)(2,1)}, u32[]{:S(2)}) copy-start(bf16[64,6144]{1,0:T(8,128)(2,1)} %param.6) | copy-start | bytes 2359300
  115.1 9.9 %collective-permute-start.16 = (bf16[48,6144]{1,0:T(8,128)(2,1)S(1)}, bf16[48,6144]{1,0:T(8,128)(2,1)S(1)}, u32[]{:S(2)}, u32[]{:S(2)}) collective-permute-start(bf16[48,6144]{1,0:T(8,128)(2,1)S(1)} %get-tuple-element.63), channel_id=1, source_target_pairs={{2,0},{4,2},{6,4},{7,6},{5,7},{3,5},{1,3},{0,1},{10,8},{12,10},{14... | collective-permute-start | bytes 1769480 | tf_op jit(solution)/shard_map/ppermute | solution.py:71
  116.7 9.9 %collective-permute-start.15 = (bf16[48,6144]{1,0:T(8,128)(2,1)S(1)}, bf16[48,6144]{1,0:T(8,128)(2,1)S(1)}, u32[]{:S(2)}, u32[]{:S(2)}) collective-permute-start(bf16[48,6144]{1,0:T(8,128)(2,1)S(1)} %get-tuple-element.64), channel_id=1, source_target_pairs={{0,2},{2,4},{4,6},{6,7},{7,5},{5,3},{3,1},{1,0},{8,10},{10,12},{12... | collective-permute-start | bytes 1769480 | tf_op jit(solution)/shard_map/ppermute | solution.py:71
  126.9 1.6 %collective-permute-start.17 = (bf16[24,6144]{1,0:T(8,128)(2,1)S(1)}, bf16[24,6144]{1,0:T(8,128)(2,1)S(1)}, u32[]{:S(2)}, u32[]{:S(2)}) collective-permute-start(bf16[24,6144]{1,0:T(8,128)(2,1)S(1)} %get-tuple-element.74), channel_id=1, source_target_pairs={{0,8},{8,0},{1,9},{9,1},{2,10},{10,2},{3,11},{11,3},{4,12},{12,4},... | collective-permute-start | bytes 884744 | tf_op jit(solution)/shard_map/ppermute | solution.py:124

commit v7 on v6

--- a/solution.py
+++ b/solution.py
@@ -62,6 +62,7 @@
     n_tensor = lax.axis_size("tensor")
     half = n_tensor // 2
     block_rows = 2 * CAP
+    mid_col = tokens.shape[1] // 2
     ring = ring_of(n_tensor)
     right = [(ring[i], ring[(i + 1) % n_tensor]) for i in range(n_tensor)]
     left = [(b, a) for a, b in right]
@@ -84,44 +85,82 @@
     ).astype(jnp.bfloat16)
     own = jnp.concatenate([outgoing[:CAP], lax.ppermute(outgoing[CAP:], "expert", swap)], axis=0)
 
-    blocks = [[own]]
-    own, w_gate, w_up = before(own, w_gate, w_up)
-    pair = step(own, own)
+    halves = [own[:, :mid_col], own[:, mid_col:]]
+    reached = [[[part] for part in halves]]
+    halves, w_gate, w_up = before(halves, w_gate, w_up)
+    ends = [[part, part] for part in halves]
+
+    def advance(chunk):
+        to_right, to_left = ends[chunk]
+        ends[chunk] = [lax.ppermute(to_right, "tensor", right), lax.ppermute(to_left, "tensor", left)]
+
+    def joined(distances):
+        return jnp.concatenate(
+            [jnp.concatenate([reached[d][chunk][side] for chunk in range(2)], axis=1)
+             for d in distances for side in range(len(reached[d][0]))], axis=0)
+
+    advance(0)
+    advance(1)
     gate_here, up_here = fetched(w_gate), fetched(w_up)
-    pair, gate_here, up_here = before(pair, gate_here, up_here)
-    blocks.append(list(pair))
-    for distance in range(2, half - 1):
-        pair = step(*pair)
-        blocks.append(list(pair))
-    near = jnp.concatenate(sum(blocks, []), axis=0)
-    pair = step(*pair)
-    near_hidden = activated(product(near, gate_here[0]), product(near, up_here[0]))
-    pair, near_hidden = before(pair, near_hidden)
-    far = jnp.concatenate(step(pair[0][:CAP], pair[1][CAP:]), axis=0)
-    rest = jnp.concatenate([*pair, far], axis=0)
+    ends[1], gate_here, up_here = before(ends[1], gate_here, up_here)
+    for _ in range(half - 2):
+        reached.append([list(ends[0]), list(ends[1])])
+        advance(0)
+        advance(1)
+    near = joined(range(half - 1))
+    near_gate = product(near, gate_here[0])
+    ends[0], near_gate = before(ends[0], near_gate)
+    near, after = before(near, ends[0])
+    near_hidden = activated(near_gate, product(near, up_here[0]))
+    ends[0] = list(after)
+    ends[1], near_hidden = before(ends[1], near_hidden)
+    reached.append([list(ends[0]), list(ends[1])])
+    far = []
+    for to_right, to_left in ends:
+        far.append([lax.ppermute(to_right[:CAP], "tensor", right), lax.ppermute(to_left[CAP:], "tensor", left)])
+    far = jnp.concatenate([jnp.concatenate([far[0][side], far[1][side]], axis=1) for side in range(2)], axis=0)
+    rest = jnp.concatenate([joined([half - 1]), far], axis=0)
+    near_hidden, w_down = before(near_hidden, w_down)
+    down_here = fetched(w_down)
+    rest, down_here = before(rest, down_here)
     rest_hidden = lax.optimization_barrier(activated(product(rest, gate_here[0]), product(rest, up_here[0])))
 
     def block_of(part, index):
-        return part[index * block_rows:(index + 1) * block_rows].astype(jnp.float32)
+        return part[index * block_rows:(index + 1) * block_rows]
 
-    rest_part = product(rest_hidden, w_down[0]).astype(jnp.bfloat16)
-    far_part = rest_part[2 * block_rows:]
-    pair = step(far_part[:CAP], far_part[CAP:])
-    got_a, got_b = (part.astype(jnp.float32) for part in pair)
-    send_b, send_a = block_of(rest_part, 0), block_of(rest_part, 1)
-    send_a = jnp.concatenate([send_a[:CAP] + got_a, send_a[CAP:]], axis=0)
-    send_b = jnp.concatenate([send_b[:CAP], send_b[CAP:] + got_b], axis=0)
-    near_hidden, send_a, send_b = before(near_hidden, send_a.astype(jnp.bfloat16), send_b.astype(jnp.bfloat16))
-    pair = step(send_a, send_b)
-    near_part = product(near_hidden, w_down[0]).astype(jnp.bfloat16)
+    def down_of(hidden, chunk):
+        return product(hidden, down_here[0, :, chunk * mid_col:(chunk + 1) * mid_col]).astype(jnp.bfloat16)
+
+    rest_part, got = [], []
+    for chunk in range(2):
+        rest_part.append(down_of(rest_hidden, chunk))
+        far_part = block_of(rest_part[chunk], 2)
+        got.append(step(far_part[:CAP], far_part[CAP:]))
+
+    def sending(chunk, distance):
+        got_a, got_b = (part.astype(jnp.float32) for part in got[chunk])
+        if distance == half - 1:
+            send_b, send_a = (block_of(rest_part[chunk], side).astype(jnp.float32) for side in range(2))
+            send_a = jnp.concatenate([send_a[:CAP] + got_a, send_a[CAP:]], axis=0)
+            send_b = jnp.concatenate([send_b[:CAP], send_b[CAP:] + got_b], axis=0)
+        else:
+            send_b, send_a = (block_of(near_part[chunk], 2 * distance - 1 + side).astype(jnp.float32) for side in range(2))
+            send_a = send_a + got_a
+            send_b = send_b + got_b
+        return send_a.astype(jnp.bfloat16), send_b.astype(jnp.bfloat16)
+
+    near_part = [down_of(near_hidden, chunk) for chunk in range(2)]
+    for chunk in range(2):
+        got[chunk] = step(*sending(chunk, half - 1))
     for distance in range(half - 2, 0, -1):
-        got_a, got_b = (part.astype(jnp.float32) for part in pair)
-        send_b, send_a = (block_of(near_part, 2 * distance - 1 + side) for side in range(2))
-        pair = step((send_a + got_a).astype(jnp.bfloat16), (send_b + got_b).astype(jnp.bfloat16))
-    got_a, got_b = (part.astype(jnp.float32) for part in pair)
-    total = (block_of(near_part, 0) + got_a + got_b).astype(jnp.bfloat16)
-
-    returned = jnp.stack([total[:CAP], lax.ppermute(total[CAP:], "expert", swap)])
+        for chunk in range(2):
+            got[chunk] = step(*sending(chunk, distance))
+    sums = []
+    for chunk in range(2):
+        got_a, got_b = (part.astype(jnp.float32) for part in got[chunk])
+        total = (block_of(near_part[chunk], 0).astype(jnp.float32) + got_a + got_b).astype(jnp.bfloat16)
+        sums.append(jnp.stack([total[:CAP], lax.ppermute(total[CAP:], "expert", swap)]))
+    returned = jnp.concatenate(sums, axis=2)
     combine = dispatch_map.astype(jnp.float32) * jnp.transpose(weight)[:, None, :]
     mixed = jnp.einsum("wcr,wcd->rd", combine, returned.astype(jnp.float32))
     return mixed.astype(jnp.bfloat16)

time: 130 us -> 137 us (1.054)
  waiting for transfers between devices: 76 us -> 43.4 us
  starting transfers between devices: 18.2 us -> 34.7 us
  other arithmetic: 2.27 us -> 15 us
  Pallas kernels: 9.45 us -> 14.2 us
  local copies, waits for them, and re-layouts: 0.81 us -> 5.1 us
    ppermute x8, waiting for transfers between devices: 41.5 us -> 11.6 us  [step(): lax.ppermute(to_left, 'tensor', left)]
    ppermute x8, waiting for transfers between devices: 31.8 us -> 14.1 us  [step(): lax.ppermute(to_right, 'tensor', right)]
    ppermute x0 -> x16, starting transfers between devices: none -> 17.3 us  [the longest x6 7.62 us: advance(): lax.ppermute(to_left, 'tensor', left)]
    ppermute x0 -> x16, waiting for transfers between devices: none -> 15.2 us  [the longest x6 11.4 us: advance(): lax.ppermute(to_left, 'tensor', left)]
    concatenate x1 -> x6, other arithmetic: 0.11 us -> 12.5 us  [the longest x1 12.4 us: per_device(): rest = jnp.concatenate([joined([half - 1]), far], axis=0)]
    pallas_call x2 -> x3, Pallas kernels: 9.45 us -> 14.2 us  [fetched(): pl.pallas_call(fill_kernel, in_specs=[pl.BlockSpec(memory_space=pltpu.HBM...]
    unnamed x22 -> x18, local copies, waits for them, and re-layouts: 0.33 us -> 4.67 us
    ppermute x8, starting transfers between devices: 6.76 us -> 3.86 us  [step(): lax.ppermute(to_right, 'tensor', right)]
  transfers between devices with their start and end apart: 18 -> 35, of which waited for: 18 -> 18; matrix products, arithmetic and copies ran while one was open for 8% -> 8% of each run, Pallas kernels for 7% -> 10%
where the time goes in v7:
time: 137 us
  waiting for transfers between devices  43.4 us (32%)
  starting transfers between devices  34.7 us (25%)
  matrix products  23.7 us (17%)
  other arithmetic  15 us (11%)
  Pallas kernels  14.2 us (10%)
  local copies, waits for them, and re-layouts  5.1 us (4%)
    dot_general x8, matrix products, product(): return jnp.dot(rows, weights, preferred_element_type=jnp.float32)  22.2 us
    pallas_call x3, Pallas kernels, fetched(): pl.pallas_call(fill_kernel, in_specs=[pl.BlockSpec(memory_space=pltpu.HBM...  14.2 us
    ppermute x8, waiting for transfers between devices, step(): lax.ppermute(to_right, 'tensor', right)  14.1 us
    ppermute x8, starting transfers between devices, step(): lax.ppermute(to_left, 'tensor', left)  12.9 us
    concatenate x1, other arithmetic, per_device(): rest = jnp.concatenate([joined([half - 1]), far], axis=0)  12.4 us
    ppermute x8, waiting for transfers between devices, step(): lax.ppermute(to_left, 'tensor', left)  11.6 us
    ppermute x6, waiting for transfers between devices, advance(): lax.ppermute(to_left, 'tensor', left)  11.4 us
    ppermute x6, starting transfers between devices, advance(): lax.ppermute(to_left, 'tensor', left)  7.62 us
  transfers between devices with their start and end apart: 35, of which 18 were waited for; matrix products, arithmetic and copies ran while one was open for 8% of the time, Pallas kernels for 10%

profile of v7, /device:TPU:0, one launch (start us, length us, event | category | flops | bytes accessed | tf_op | source)
XLA Modules:
  0.0 136.6 jit_solution(7015201541464274880)
XLA Ops:
  0.2 0.8 compare_reduce_fusion
  1.4 0.3 convolution_convert_fusion
  1.8 0.5 collective-permute-start
  2.3 1.2 collective-permute-done
  3.5 2.9 %collective-permute-start.2 = (bf16[48,3072]{1,0:T(8,128)(2,1)S(1)}, bf16[48,3072]{1,0:T(8,128)(2,1)S(1)}, u32[]{:S(2)}, u32[]{:S(2)}) collective-permute-start(bf16[48,3072]{1,0:T(8,128)(2,1)S(1)} %get-tuple-element.42), channel_id=1, source_target_pairs={{2,0},{4,2},{6,4},{7,6},{5,7},{3,5},{1,3},{0,1},{10,8},{12,10},{14... | collective-permute-start | bytes 884744 | tf_op jit(solution)/shard_map/ppermute | solution.py:95
  6.6 1.9 %collective-permute-start.10 = (bf16[48,3072]{1,0:T(8,128)(2,1)S(1)}, bf16[48,3072]{1,0:T(8,128)(2,1)S(1)}, u32[]{:S(2)}, u32[]{:S(2)}) collective-permute-start(bf16[48,3072]{1,0:T(8,128)(2,1)S(1)} %get-tuple-element.47), channel_id=1, source_target_pairs={{2,0},{4,2},{6,4},{7,6},{5,7},{3,5},{1,3},{0,1},{10,8},{12,10},{14... | collective-permute-start | bytes 884744 | tf_op jit(solution)/shard_map/ppermute | solution.py:95
  8.6 4.7 %fetched.3 = bf16[1,6144,1024]{2,1,0:T(8,128)(2,1)S(1)} custom-call(bf16[1,6144,1024]{2,1,0:T(8,128)(2,1)} %source), custom_call_target="tpu_custom_call" | custom-call | flops 1024 | bytes 1024 | tf_op jit(solution)/shard_map/fetched/pallas_call | solution.py:31
  13.4 4.7 %fetched.4 = bf16[1,6144,1024]{2,1,0:T(8,128)(2,1)S(1)} custom-call(bf16[1,6144,1024]{2,1,0:T(8,128)(2,1)} %source.1), custom_call_target="tpu_custom_call" | custom-call | flops 1024 | bytes 1024 | tf_op jit(solution)/shard_map/fetched/pallas_call | solution.py:31
  18.1 2.0 %collective-permute-start.3 = (bf16[48,3072]{1,0:T(8,128)(2,1)S(1)}, bf16[48,3072]{1,0:T(8,128)(2,1)S(1)}, u32[]{:S(2)}, u32[]{:S(2)}) collective-permute-start(bf16[48,3072]{1,0:T(8,128)(2,1)S(1)} %collective-permute-done.1), channel_id=1, source_target_pairs={{0,2},{2,4},{4,6},{6,7},{7,5},{5,3},{3,1},{1,0},{8,10},{10,12},{12... | collective-permute-start | bytes 884744 | tf_op jit(solution)/shard_map/ppermute | solution.py:95
  20.2 1.9 %collective-permute-start.11 = (bf16[48,3072]{1,0:T(8,128)(2,1)S(1)}, bf16[48,3072]{1,0:T(8,128)(2,1)S(1)}, u32[]{:S(2)}, u32[]{:S(2)}) collective-permute-start(bf16[48,3072]{1,0:T(8,128)(2,1)S(1)} %collective-permute-done.10), channel_id=1, source_target_pairs={{2,0},{4,2},{6,4},{7,6},{5,7},{3,5},{1,3},{0,1},{10,8},{12,10},{14... | collective-permute-start | bytes 884744 | tf_op jit(solution)/shard_map/ppermute | solution.py:95
  22.1 0.6 collective-permute-done.7
  22.8 11.3 %collective-permute-done.11 = bf16[48,3072]{1,0:T(8,128)(2,1)S(1)} collective-permute-done((bf16[48,3072]{1,0:T(8,128)(2,1)S(1)}, bf16[48,3072]{1,0:T(8,128)(2,1)S(1)}, u32[]{:S(2)}, u32[]{:S(2)}) %collective-permute-start.11) | collective-permute-done | bytes 294944 | tf_op jit(solution)/shard_map/ppermute | solution.py:95
  34.1 0.4 collective-permute-start.12
  34.5 1.7 %collective-permute-start.9 = (bf16[48,3072]{1,0:T(8,128)(2,1)S(1)}, bf16[48,3072]{1,0:T(8,128)(2,1)S(1)}, u32[]{:S(2)}, u32[]{:S(2)}) collective-permute-start(bf16[48,3072]{1,0:T(8,128)(2,1)S(1)} %collective-permute-done.8), channel_id=1, source_target_pairs={{0,2},{2,4},{4,6},{6,7},{7,5},{5,3},{3,1},{1,0},{8,10},{10,12},{12... | collective-permute-start | bytes 884744 | tf_op jit(solution)/shard_map/ppermute | solution.py:95
  36.3 3.2 %fusion.6 = f32[240,1024]{1,0:T(8,128)S(1)} fusion(bf16[240,6144]{1,0:T(8,128)(2,1)S(1)} %maximum_dynamic-update-slice_fusion, bf16[1,6144,1024]{2,1,0:T(8,128)(2,1)S(1)} %fetched.3), kind=kOutput, calls=%fused_computation.6 | convolution fusion | flops 3019898880 | bytes 16515072 | tf_op jit(solution)/shard_map/dot_general | solution.py:54
  39.5 1.6 %collective-permute-start.4 = (bf16[48,3072]{1,0:T(8,128)(2,1)S(1)}, bf16[48,3072]{1,0:T(8,128)(2,1)S(1)}, u32[]{:S(2)}, u32[]{:S(2)}) collective-permute-start(bf16[48,3072]{1,0:T(8,128)(2,1)S(1)} %collective-permute-done.3), channel_id=1, source_target_pairs={{0,2},{2,4},{4,6},{6,7},{7,5},{5,3},{3,1},{1,0},{8,10},{10,12},{12... | collective-permute-start | bytes 884744 | tf_op jit(solution)/shard_map/ppermute | solution.py:95
  41.1 0.4 collective-permute-start.6
  41.6 2.8 %collective-permute-done.9 = bf16[48,3072]{1,0:T(8,128)(2,1)S(1)} collective-permute-done((bf16[48,3072]{1,0:T(8,128)(2,1)S(1)}, bf16[48,3072]{1,0:T(8,128)(2,1)S(1)}, u32[]{:S(2)}, u32[]{:S(2)}) %collective-permute-start.9) | collective-permute-done | bytes 294944 | tf_op jit(solution)/shard_map/ppermute | solution.py:95
  44.4 3.2 %fusion.2 = f32[240,1024]{1,0:T(8,128)S(1)} fusion(bf16[240,6144]{1,0:T(8,128)(2,1)S(1)} %maximum_dynamic-update-slice_fusion, bf16[1,6144,1024]{2,1,0:T(8,128)(2,1)S(1)} %fetched.4), kind=kOutput, calls=%fused_computation.2 | convolution fusion | flops 3019898880 | bytes 16515072 | tf_op jit(solution)/shard_map/dot_general | solution.py:54
  47.7 0.3 multiply_convert_fusion
  48.0 0.5 collective-permute-done.4
  48.5 1.6 %collective-permute-start.15 = (bf16[24,3072]{1,0:T(8,128)(2,1)S(1)}, bf16[24,3072]{1,0:T(8,128)(2,1)S(1)}, u32[]{:S(2)}, u32[]{:S(2)}) collective-permute-start(bf16[24,3072]{1,0:T(8,128)(2,1)S(1)} %slice.151), channel_id=1, source_target_pairs={{2,0},{4,2},{6,4},{7,6},{5,7},{3,5},{1,3},{0,1},{10,8},{12,10},{14... | collective-permute-start | bytes 442376 | tf_op jit(solution)/shard_map/ppermute | solution.py:120
  50.1 0.4 collective-permute-start.13
  50.6 1.6 %collective-permute-start.16 = (bf16[24,3072]{1,0:T(8,128)(2,1)S(1)}, bf16[24,3072]{1,0:T(8,128)(2,1)S(1)}, u32[]{:S(2)}, u32[]{:S(2)}) collective-permute-start(bf16[24,3072]{1,0:T(8,128)(2,1)S(1)} %slice.152), channel_id=1, source_target_pairs={{2,0},{4,2},{6,4},{7,6},{5,7},{3,5},{1,3},{0,1},{10,8},{12,10},{14... | collective-permute-start | bytes 442376 | tf_op jit(solution)/shard_map/ppermute | solution.py:120
  52.1 0.5 collective-permute-start.14
  52.6 4.7 %fetched.5 = bf16[1,1024,6144]{2,1,0:T(8,128)(2,1)S(1)} custom-call(bf16[1,1024,6144]{2,1,0:T(8,128)(2,1)} %source.2), custom_call_target="tpu_custom_call" | custom-call | flops 1024 | bytes 1024 | tf_op jit(solution)/shard_map/fetched/pallas_call | solution.py:31
  57.3 4.6 %copy-done.2 = bf16[1,1024,6144]{2,1,0:T(8,128)(2,1)} copy-done((bf16[1,1024,6144]{2,1,0:T(8,128)(2,1)}, bf16[1,1024,6144]{2,1,0:T(8,128)(2,1)S(1)}, u32[]{:S(2)}) %copy-start.2) | copy-done | bytes 12582936
  61.9 12.4 %maximum_maximum_fusion = bf16[144,6144]{1,0:T(8,128)(2,1)S(1)} fusion(bf16[24,3072]{1,0:T(8,128)(2,1)S(1)} %collective-permute-done.16, bf16[24,3072]{1,0:T(8,128)(2,1)S(1)} %collective-permute-done.15, bf16[24,3072]{1,0:T(8,128)(2,1)S(1)} %collective-permute-done.14, bf16[24,3072]{1,0:T(8,128)(2,1)S(1)} %collective-permute-done.13, ...), kind=kLoop, calls=%fused_computation.27 | loop fusion | flops 14155776 | bytes 3538944 | tf_op jit(solution)/shard_map/concatenate | solution.py:122
  74.3 2.0 %fusion.4 = f32[144,1024]{1,0:T(8,128)S(1)} fusion(bf16[144,6144]{1,0:T(8,128)(2,1)S(1)} %maximum_maximum_fusion, bf16[1,6144,1024]{2,1,0:T(8,128)(2,1)S(1)} %fetched.3), kind=kOutput, calls=%fused_computation.4 | convolution fusion | flops 1811939328 | bytes 14942208 | tf_op jit(solution)/shard_map/dot_general | solution.py:54
  76.4 2.2 %multiply_convert_fusion.1 = bf16[144,1024]{1,0:T(8,128)(2,1)S(1)} fusion(f32[144,1024]{1,0:T(8,128)S(1)} %fusion.4, bf16[144,6144]{1,0:T(8,128)(2,1)S(1)} %maximum_maximum_fusion, bf16[1,6144,1024]{2,1,0:T(8,128)(2,1)S(1)} %fetched.4), kind=kOutput, calls=%fused_computation.52 | convolution fusion | flops 1812824064 | bytes 15237120 | tf_op jit(solution)/shard_map/dot_general | solution.py:54
  78.5 4.2 %fusion.30 = bf16[144,3072]{1,0:T(8,128)(2,1)S(1)} fusion(bf16[144,1024]{1,0:T(8,128)(2,1)S(1)} %multiply_convert_fusion.1, bf16[1,1024,6144]{2,1,0:T(8,128)(2,1)} %copy-done.2), kind=kOutput, calls=%fused_computation.26 | convolution fusion | flops 906412032 | bytes 7471104 | tf_op jit(solution)/shard_map/dot_general | solution.py:54
  82.7 3.9 %fusion.27 = bf16[144,3072]{1,0:T(8,128)(2,1)S(1)} fusion(bf16[144,1024]{1,0:T(8,128)(2,1)S(1)} %multiply_convert_fusion.1, bf16[1,1024,6144]{2,1,0:T(8,128)(2,1)} %copy-done.2), kind=kOutput, calls=%fused_computation.25 | convolution fusion | flops 906412032 | bytes 7471104 | tf_op jit(solution)/shard_map/dot_general | solution.py:54
  86.7 1.6 %collective-permute-start.18 = (bf16[24,3072]{1,0:T(8,128)(2,1)S(1)}, bf16[24,3072]{1,0:T(8,128)(2,1)S(1)}, u32[]{:S(2)}, u32[]{:S(2)}) collective-permute-start(bf16[24,3072]{1,0:T(8,128)(2,1)S(1)} %get-tuple-element.89), channel_id=1, source_target_pairs={{2,0},{4,2},{6,4},{7,6},{5,7},{3,5},{1,3},{0,1},{10,8},{12,10},{14... | collective-permute-start | bytes 442376 | tf_op jit(solution)/shard_map/ppermute | solution.py:72
  88.3 0.5 collective-permute-start.17
  88.8 1.6 %collective-permute-start.27 = (bf16[24,3072]{1,0:T(8,128)(2,1)S(1)}, bf16[24,3072]{1,0:T(8,128)(2,1)S(1)}, u32[]{:S(2)}, u32[]{:S(2)}) collective-permute-start(bf16[24,3072]{1,0:T(8,128)(2,1)S(1)} %get-tuple-element.95), channel_id=1, source_target_pairs={{2,0},{4,2},{6,4},{7,6},{5,7},{3,5},{1,3},{0,1},{10,8},{12,10},{14... | collective-permute-start | bytes 442376 | tf_op jit(solution)/shard_map/ppermute | solution.py:72
  90.4 0.5 collective-permute-start.26
  90.9 1.7 %fusion.24 = bf16[240,3072]{1,0:T(8,128)(2,1)S(1)} fusion(bf16[240,1024]{1,0:T(8,128)(2,1)S(1)} %multiply_convert_fusion, bf16[1,1024,6144]{2,1,0:T(8,128)(2,1)S(1)} %bitcast.64), kind=kOutput, calls=%fused_computation.24 | convolution fusion | flops 1510686720 | bytes 8257536 | tf_op jit(solution)/shard_map/dot_general | solution.py:54
  92.6 2.3 %collective-permute-done.17 = bf16[24,3072]{1,0:T(8,128)(2,1)S(1)} collective-permute-done((bf16[24,3072]{1,0:T(8,128)(2,1)S(1)}, bf16[24,3072]{1,0:T(8,128)(2,1)S(1)}, u32[]{:S(2)}, u32[]{:S(2)}) %collective-permute-start.17) | collective-permute-done | bytes 147488 | tf_op jit(solution)/shard_map/ppermute | solution.py:72
  95.0 0.6 collective-permute-start.19
  95.6 1.6 %collective-permute-start.20 = (bf16[48,3072]{1,0:T(8,128)(2,1)S(1)}, bf16[48,3072]{1,0:T(8,128)(2,1)S(1)}, u32[]{:S(2)}, u32[]{:S(2)}) collective-permute-start(bf16[48,3072]{1,0:T(8,128)(2,1)S(1)} %pad_maximum_fusion.2), channel_id=1, source_target_pairs={{2,0},{4,2},{6,4},{7,6},{5,7},{3,5},{1,3},{0,1},{10,8},{12,10},{14... | collective-permute-start | bytes 884744 | tf_op jit(solution)/shard_map/ppermute | solution.py:72
  97.2 0.9 collective-permute-done.26
  98.2 0.6 collective-permute-start.28
  98.8 1.6 %collective-permute-start.29 = (bf16[48,3072]{1,0:T(8,128)(2,1)S(1)}, bf16[48,3072]{1,0:T(8,128)(2,1)S(1)}, u32[]{:S(2)}, u32[]{:S(2)}) collective-permute-start(bf16[48,3072]{1,0:T(8,128)(2,1)S(1)} %pad_maximum_fusion.4), channel_id=1, source_target_pairs={{2,0},{4,2},{6,4},{7,6},{5,7},{3,5},{1,3},{0,1},{10,8},{12,10},{14... | collective-permute-start | bytes 884744 | tf_op jit(solution)/shard_map/ppermute | solution.py:72
  100.3 1.7 %fusion.21 = bf16[240,3072]{1,0:T(8,128)(2,1)S(1)} fusion(bf16[240,1024]{1,0:T(8,128)(2,1)S(1)} %multiply_convert_fusion, bf16[1,1024,6144]{2,1,0:T(8,128)(2,1)S(1)} %bitcast.64), kind=kOutput, calls=%fused_computation.23 | convolution fusion | flops 1510686720 | bytes 8257536 | tf_op jit(solution)/shard_map/dot_general | solution.py:54
  102.1 1.9 %collective-permute-done.19 = bf16[48,3072]{1,0:T(8,128)(2,1)S(1)} collective-permute-done((bf16[48,3072]{1,0:T(8,128)(2,1)S(1)}, bf16[48,3072]{1,0:T(8,128)(2,1)S(1)}, u32[]{:S(2)}, u32[]{:S(2)}) %collective-permute-start.19) | collective-permute-done | bytes 294944 | tf_op jit(solution)/shard_map/ppermute | solution.py:72
  104.0 3.2 %collective-permute-done.28 = bf16[48,3072]{1,0:T(8,128)(2,1)S(1)} collective-permute-done((bf16[48,3072]{1,0:T(8,128)(2,1)S(1)}, bf16[48,3072]{1,0:T(8,128)(2,1)S(1)}, u32[]{:S(2)}, u32[]{:S(2)}) %collective-permute-start.28) | collective-permute-done | bytes 294944 | tf_op jit(solution)/shard_map/ppermute | solution.py:72
  107.3 1.6 %collective-permute-start.31 = (bf16[48,3072]{1,0:T(8,128)(2,1)S(1)}, bf16[48,3072]{1,0:T(8,128)(2,1)S(1)}, u32[]{:S(2)}, u32[]{:S(2)}) collective-permute-start(bf16[48,3072]{1,0:T(8,128)(2,1)S(1)} %get-tuple-element.85), channel_id=1, source_target_pairs={{2,0},{4,2},{6,4},{7,6},{5,7},{3,5},{1,3},{0,1},{10,8},{12,10},{14... | collective-permute-start | bytes 884744 | tf_op jit(solution)/shard_map/ppermute | solution.py:72
  109.0 0.4 collective-permute-start.30
  109.6 1.6 %collective-permute-start.22 = (bf16[48,3072]{1,0:T(8,128)(2,1)S(1)}, bf16[48,3072]{1,0:T(8,128)(2,1)S(1)}, u32[]{:S(2)}, u32[]{:S(2)}) collective-permute-start(bf16[48,3072]{1,0:T(8,128)(2,1)S(1)} %get-tuple-element.81), channel_id=1, source_target_pairs={{2,0},{4,2},{6,4},{7,6},{5,7},{3,5},{1,3},{0,1},{10,8},{12,10},{14... | collective-permute-start | bytes 884744 | tf_op jit(solution)/shard_map/ppermute | solution.py:72
  111.2 0.4 collective-permute-start.21
  111.6 5.7 %collective-permute-done.31 = bf16[48,3072]{1,0:T(8,128)(2,1)S(1)} collective-permute-done((bf16[48,3072]{1,0:T(8,128)(2,1)S(1)}, bf16[48,3072]{1,0:T(8,128)(2,1)S(1)}, u32[]{:S(2)}, u32[]{:S(2)}) %collective-permute-start.31) | collective-permute-done | bytes 294944 | tf_op jit(solution)/shard_map/ppermute | solution.py:72
  117.3 1.6 %collective-permute-done.30 = bf16[48,3072]{1,0:T(8,128)(2,1)S(1)} collective-permute-done((bf16[48,3072]{1,0:T(8,128)(2,1)S(1)}, bf16[48,3072]{1,0:T(8,128)(2,1)S(1)}, u32[]{:S(2)}, u32[]{:S(2)}) %collective-permute-start.30) | collective-permute-done | bytes 294944 | tf_op jit(solution)/shard_map/ppermute | solution.py:72
  119.1 1.6 %collective-permute-start.33 = (bf16[48,3072]{1,0:T(8,128)(2,1)S(1)}, bf16[48,3072]{1,0:T(8,128)(2,1)S(1)}, u32[]{:S(2)}, u32[]{:S(2)}) collective-permute-start(bf16[48,3072]{1,0:T(8,128)(2,1)S(1)} %get-tuple-element.83), channel_id=1, source_target_pairs={{2,0},{4,2},{6,4},{7,6},{5,7},{3,5},{1,3},{0,1},{10,8},{12,10},{14... | collective-permute-start | bytes 884744 | tf_op jit(solution)/shard_map/ppermute | solution.py:72
  120.7 0.4 collective-permute-start.32
  121.2 2.5 %collective-permute-done.22 = bf16[48,3072]{1,0:T(8,128)(2,1)S(1)} collective-permute-done((bf16[48,3072]{1,0:T(8,128)(2,1)S(1)}, bf16[48,3072]{1,0:T(8,128)(2,1)S(1)}, u32[]{:S(2)}, u32[]{:S(2)}) %collective-permute-start.22) | collective-permute-done | bytes 294944 | tf_op jit(solution)/shard_map/ppermute | solution.py:72
  123.6 1.6 %collective-permute-done.21 = bf16[48,3072]{1,0:T(8,128)(2,1)S(1)} collective-permute-done((bf16[48,3072]{1,0:T(8,128)(2,1)S(1)}, bf16[48,3072]{1,0:T(8,128)(2,1)S(1)}, u32[]{:S(2)}, u32[]{:S(2)}) %collective-permute-start.21) | collective-permute-done | bytes 294944 | tf_op jit(solution)/shard_map/ppermute | solution.py:72
  125.4 1.6 %collective-permute-start.24 = (bf16[48,3072]{1,0:T(8,128)(2,1)S(1)}, bf16[48,3072]{1,0:T(8,128)(2,1)S(1)}, u32[]{:S(2)}, u32[]{:S(2)}) collective-permute-start(bf16[48,3072]{1,0:T(8,128)(2,1)S(1)} %get-tuple-element.79), channel_id=1, source_target_pairs={{2,0},{4,2},{6,4},{7,6},{5,7},{3,5},{1,3},{0,1},{10,8},{12,10},{14... | collective-permute-start | bytes 884744 | tf_op jit(solution)/shard_map/ppermute | solution.py:72
  127.0 0.4 collective-permute-start.23
  127.5 0.8 collective-permute-done.33
  128.3 1.0 collective-permute-done.32
  129.6 2.6 %collective-permute-done.24 = bf16[48,3072]{1,0:T(8,128)(2,1)S(1)} collective-permute-done((bf16[48,3072]{1,0:T(8,128)(2,1)S(1)}, bf16[48,3072]{1,0:T(8,128)(2,1)S(1)}, u32[]{:S(2)}, u32[]{:S(2)}) %collective-permute-start.24) | collective-permute-done | bytes 294944 | tf_op jit(solution)/shard_map/ppermute | solution.py:72
  132.2 1.6 %collective-permute-done.23 = bf16[48,3072]{1,0:T(8,128)(2,1)S(1)} collective-permute-done((bf16[48,3072]{1,0:T(8,128)(2,1)S(1)}, bf16[48,3072]{1,0:T(8,128)(2,1)S(1)}, u32[]{:S(2)}, u32[]{:S(2)}) %collective-permute-start.23) | collective-permute-done | bytes 294944 | tf_op jit(solution)/shard_map/ppermute | solution.py:72
  134.1 1.3 collective-permute-done.25
  135.3 1.3 fusion.8
  (76 shorter events, 2.6 us)
Async XLA Ops:
  0.0 1.4 %copy-start = (bf16[64,6144]{1,0:T(8,128)(2,1)S(1)}, bf16[64,6144]{1,0:T(8,128)(2,1)}, u32[]{:S(2)}) copy-start(bf16[64,6144]{1,0:T(8,128)(2,1)} %param.6) | copy-start | bytes 2359300
  1.8 1.7 %collective-permute-start = (bf16[24,6144]{1,0:T(8,128)(2,1)S(1)}, bf16[24,6144]{1,0:T(8,128)(2,1)S(1)}, u32[]{:S(2)}, u32[]{:S(2)}) collective-permute-start(bf16[24,6144]{1,0:T(8,128)(2,1)S(1)} %get-tuple-element.100), channel_id=1, source_target_pairs={{0,8},{8,0},{1,9},{9,1},{2,10},{10,2},{3,11},{11,3},{4,12},{12,4},... | collective-permute-start | bytes 884744 | tf_op jit(solution)/shard_map/ppermute | solution.py:86
  3.5 14.6 %collective-permute-start.2 = (bf16[48,3072]{1,0:T(8,128)(2,1)S(1)}, bf16[48,3072]{1,0:T(8,128)(2,1)S(1)}, u32[]{:S(2)}, u32[]{:S(2)}) collective-permute-start(bf16[48,3072]{1,0:T(8,128)(2,1)S(1)} %get-tuple-element.42), channel_id=1, source_target_pairs={{2,0},{4,2},{6,4},{7,6},{5,7},{3,5},{1,3},{0,1},{10,8},{12,10},{14... | collective-permute-start | bytes 884744 | tf_op jit(solution)/shard_map/ppermute | solution.py:95
  6.5 11.7 %collective-permute-start.1 = (bf16[48,3072]{1,0:T(8,128)(2,1)S(1)}, bf16[48,3072]{1,0:T(8,128)(2,1)S(1)}, u32[]{:S(2)}, u32[]{:S(2)}) collective-permute-start(bf16[48,3072]{1,0:T(8,128)(2,1)S(1)} %get-tuple-element.42), channel_id=1, source_target_pairs={{0,2},{2,4},{4,6},{6,7},{7,5},{5,3},{3,1},{1,0},{8,10},{10,12},{12... | collective-permute-start | bytes 884744 | tf_op jit(solution)/shard_map/ppermute | solution.py:95
  6.6 13.6 %collective-permute-start.10 = (bf16[48,3072]{1,0:T(8,128)(2,1)S(1)}, bf16[48,3072]{1,0:T(8,128)(2,1)S(1)}, u32[]{:S(2)}, u32[]{:S(2)}) collective-permute-start(bf16[48,3072]{1,0:T(8,128)(2,1)S(1)} %get-tuple-element.47), channel_id=1, source_target_pairs={{2,0},{4,2},{6,4},{7,6},{5,7},{3,5},{1,3},{0,1},{10,8},{12,10},{14... | collective-permute-start | bytes 884744 | tf_op jit(solution)/shard_map/ppermute | solution.py:95
  8.5 14.2 %collective-permute-start.7 = (bf16[48,3072]{1,0:T(8,128)(2,1)S(1)}, bf16[48,3072]{1,0:T(8,128)(2,1)S(1)}, u32[]{:S(2)}, u32[]{:S(2)}) collective-permute-start(bf16[48,3072]{1,0:T(8,128)(2,1)S(1)} %get-tuple-element.47), channel_id=1, source_target_pairs={{0,2},{2,4},{4,6},{6,7},{7,5},{5,3},{3,1},{1,0},{8,10},{10,12},{12... | collective-permute-start | bytes 884744 | tf_op jit(solution)/shard_map/ppermute | solution.py:95
  18.1 18.0 %collective-permute-start.3 = (bf16[48,3072]{1,0:T(8,128)(2,1)S(1)}, bf16[48,3072]{1,0:T(8,128)(2,1)S(1)}, u32[]{:S(2)}, u32[]{:S(2)}) collective-permute-start(bf16[48,3072]{1,0:T(8,128)(2,1)S(1)} %collective-permute-done.1), channel_id=1, source_target_pairs={{0,2},{2,4},{4,6},{6,7},{7,5},{5,3},{3,1},{1,0},{8,10},{10,12},{12... | collective-permute-start | bytes 884744 | tf_op jit(solution)/shard_map/ppermute | solution.py:95
  20.1 16.0 %collective-permute-start.5 = (bf16[48,3072]{1,0:T(8,128)(2,1)S(1)}, bf16[48,3072]{1,0:T(8,128)(2,1)S(1)}, u32[]{:S(2)}, u32[]{:S(2)}) collective-permute-start(bf16[48,3072]{1,0:T(8,128)(2,1)S(1)} %collective-permute-done.2), channel_id=1, source_target_pairs={{2,0},{4,2},{6,4},{7,6},{5,7},{3,5},{1,3},{0,1},{10,8},{12,10},{14... | collective-permute-start | bytes 884744 | tf_op jit(solution)/shard_map/ppermute | solution.py:95
  20.2 13.9 %collective-permute-start.11 = (bf16[48,3072]{1,0:T(8,128)(2,1)S(1)}, bf16[48,3072]{1,0:T(8,128)(2,1)S(1)}, u32[]{:S(2)}, u32[]{:S(2)}) collective-permute-start(bf16[48,3072]{1,0:T(8,128)(2,1)S(1)} %collective-permute-done.10), channel_id=1, source_target_pairs={{2,0},{4,2},{6,4},{7,6},{5,7},{3,5},{1,3},{0,1},{10,8},{12,10},{14... | collective-permute-start | bytes 884744 | tf_op jit(solution)/shard_map/ppermute | solution.py:95
  22.7 11.8 %collective-permute-start.8 = (bf16[48,3072]{1,0:T(8,128)(2,1)S(1)}, bf16[48,3072]{1,0:T(8,128)(2,1)S(1)}, u32[]{:S(2)}, u32[]{:S(2)}) collective-permute-start(bf16[48,3072]{1,0:T(8,128)(2,1)S(1)} %collective-permute-done.7), channel_id=1, source_target_pairs={{0,2},{2,4},{4,6},{6,7},{7,5},{5,3},{3,1},{1,0},{8,10},{10,12},{12... | collective-permute-start | bytes 884744 | tf_op jit(solution)/shard_map/ppermute | solution.py:95
  34.1 7.5 %collective-permute-start.12 = (bf16[48,3072]{1,0:T(8,128)(2,1)S(1)}, bf16[48,3072]{1,0:T(8,128)(2,1)S(1)}, u32[]{:S(2)}, u32[]{:S(2)}) collective-permute-start(bf16[48,3072]{1,0:T(8,128)(2,1)S(1)} %collective-permute-done.11), channel_id=1, source_target_pairs={{2,0},{4,2},{6,4},{7,6},{5,7},{3,5},{1,3},{0,1},{10,8},{12,10},{14... | collective-permute-start | bytes 884744 | tf_op jit(solution)/shard_map/ppermute | solution.py:95
  34.5 9.9 %collective-permute-start.9 = (bf16[48,3072]{1,0:T(8,128)(2,1)S(1)}, bf16[48,3072]{1,0:T(8,128)(2,1)S(1)}, u32[]{:S(2)}, u32[]{:S(2)}) collective-permute-start(bf16[48,3072]{1,0:T(8,128)(2,1)S(1)} %collective-permute-done.8), channel_id=1, source_target_pairs={{0,2},{2,4},{4,6},{6,7},{7,5},{5,3},{3,1},{1,0},{8,10},{10,12},{12... | collective-permute-start | bytes 884744 | tf_op jit(solution)/shard_map/ppermute | solution.py:95
  39.5 8.9 %collective-permute-start.4 = (bf16[48,3072]{1,0:T(8,128)(2,1)S(1)}, bf16[48,3072]{1,0:T(8,128)(2,1)S(1)}, u32[]{:S(2)}, u32[]{:S(2)}) collective-permute-start(bf16[48,3072]{1,0:T(8,128)(2,1)S(1)} %collective-permute-done.3), channel_id=1, source_target_pairs={{0,2},{2,4},{4,6},{6,7},{7,5},{5,3},{3,1},{1,0},{8,10},{10,12},{12... | collective-permute-start | bytes 884744 | tf_op jit(solution)/shard_map/ppermute | solution.py:95
  41.1 7.3 %collective-permute-start.6 = (bf16[48,3072]{1,0:T(8,128)(2,1)S(1)}, bf16[48,3072]{1,0:T(8,128)(2,1)S(1)}, u32[]{:S(2)}, u32[]{:S(2)}) collective-permute-start(bf16[48,3072]{1,0:T(8,128)(2,1)S(1)} %collective-permute-done.5), channel_id=1, source_target_pairs={{2,0},{4,2},{6,4},{7,6},{5,7},{3,5},{1,3},{0,1},{10,8},{12,10},{14... | collective-permute-start | bytes 884744 | tf_op jit(solution)/shard_map/ppermute | solution.py:95
  48.5 13.4 %collective-permute-start.15 = (bf16[24,3072]{1,0:T(8,128)(2,1)S(1)}, bf16[24,3072]{1,0:T(8,128)(2,1)S(1)}, u32[]{:S(2)}, u32[]{:S(2)}) collective-permute-start(bf16[24,3072]{1,0:T(8,128)(2,1)S(1)} %slice.151), channel_id=1, source_target_pairs={{2,0},{4,2},{6,4},{7,6},{5,7},{3,5},{1,3},{0,1},{10,8},{12,10},{14... | collective-permute-start | bytes 442376 | tf_op jit(solution)/shard_map/ppermute | solution.py:120
  50.1 11.8 %collective-permute-start.13 = (bf16[24,3072]{1,0:T(8,128)(2,1)S(1)}, bf16[24,3072]{1,0:T(8,128)(2,1)S(1)}, u32[]{:S(2)}, u32[]{:S(2)}) collective-permute-start(bf16[24,3072]{1,0:T(8,128)(2,1)S(1)} %slice.149), channel_id=1, source_target_pairs={{0,2},{2,4},{4,6},{6,7},{7,5},{5,3},{3,1},{1,0},{8,10},{10,12},{12... | collective-permute-start | bytes 442376 | tf_op jit(solution)/shard_map/ppermute | solution.py:120
  50.6 11.3 %collective-permute-start.16 = (bf16[24,3072]{1,0:T(8,128)(2,1)S(1)}, bf16[24,3072]{1,0:T(8,128)(2,1)S(1)}, u32[]{:S(2)}, u32[]{:S(2)}) collective-permute-start(bf16[24,3072]{1,0:T(8,128)(2,1)S(1)} %slice.152), channel_id=1, source_target_pairs={{2,0},{4,2},{6,4},{7,6},{5,7},{3,5},{1,3},{0,1},{10,8},{12,10},{14... | collective-permute-start | bytes 442376 | tf_op jit(solution)/shard_map/ppermute | solution.py:120
  52.1 9.8 %collective-permute-start.14 = (bf16[24,3072]{1,0:T(8,128)(2,1)S(1)}, bf16[24,3072]{1,0:T(8,128)(2,1)S(1)}, u32[]{:S(2)}, u32[]{:S(2)}) collective-permute-start(bf16[24,3072]{1,0:T(8,128)(2,1)S(1)} %slice.150), channel_id=1, source_target_pairs={{0,2},{2,4},{4,6},{6,7},{7,5},{5,3},{3,1},{1,0},{8,10},{10,12},{12... | collective-permute-start | bytes 442376 | tf_op jit(solution)/shard_map/ppermute | solution.py:120
  57.3 4.6 %copy-start.2 = (bf16[1,1024,6144]{2,1,0:T(8,128)(2,1)}, bf16[1,1024,6144]{2,1,0:T(8,128)(2,1)S(1)}, u32[]{:S(2)}) copy-start(bf16[1,1024,6144]{2,1,0:T(8,128)(2,1)S(1)} %fetched.5) | copy-start | bytes 37748740
  76.3 14.5 %slice-start = ((s8[12582912]{0:T(1024)(128)(4,1)}), s8[4194304]{0:T(1024)(128)(4,1)S(1)}, s32[]{:S(2)}) async-start(s8[12582912]{0:T(1024)(128)(4,1)} %bitcast.63), calls=%async_computation | async-start | bytes 8388608
  76.3 14.5 %slice-start.1 = ((s8[12582912]{0:T(1024)(128)(4,1)}), s8[4194304]{0:T(1024)(128)(4,1)S(1)}, s32[]{:S(2)}) async-start(s8[12582912]{0:T(1024)(128)(4,1)} %bitcast.63), calls=%async_computation.1 | async-start | bytes 8388608
  78.5 12.3 %slice-start.2 = ((s8[12582912]{0:T(1024)(128)(4,1)}), s8[4194304]{0:T(1024)(128)(4,1)S(1)}, s32[]{:S(2)}) async-start(s8[12582912]{0:T(1024)(128)(4,1)} %bitcast.63), calls=%async_computation.2 | async-start | bytes 8388608
  86.7 5.9 %collective-permute-start.18 = (bf16[24,3072]{1,0:T(8,128)(2,1)S(1)}, bf16[24,3072]{1,0:T(8,128)(2,1)S(1)}, u32[]{:S(2)}, u32[]{:S(2)}) collective-permute-start(bf16[24,3072]{1,0:T(8,128)(2,1)S(1)} %get-tuple-element.89), channel_id=1, source_target_pairs={{2,0},{4,2},{6,4},{7,6},{5,7},{3,5},{1,3},{0,1},{10,8},{12,10},{14... | collective-permute-start | bytes 442376 | tf_op jit(solution)/shard_map/ppermute | solution.py:72
  88.3 6.6 %collective-permute-start.17 = (bf16[24,3072]{1,0:T(8,128)(2,1)S(1)}, bf16[24,3072]{1,0:T(8,128)(2,1)S(1)}, u32[]{:S(2)}, u32[]{:S(2)}) collective-permute-start(bf16[24,3072]{1,0:T(8,128)(2,1)S(1)} %get-tuple-element.90), channel_id=1, source_target_pairs={{0,2},{2,4},{4,6},{6,7},{7,5},{5,3},{3,1},{1,0},{8,10},{10,12},{12... | collective-permute-start | bytes 442376 | tf_op jit(solution)/shard_map/ppermute | solution.py:72
  88.8 8.4 %collective-permute-start.27 = (bf16[24,3072]{1,0:T(8,128)(2,1)S(1)}, bf16[24,3072]{1,0:T(8,128)(2,1)S(1)}, u32[]{:S(2)}, u32[]{:S(2)}) collective-permute-start(bf16[24,3072]{1,0:T(8,128)(2,1)S(1)} %get-tuple-element.95), channel_id=1, source_target_pairs={{2,0},{4,2},{6,4},{7,6},{5,7},{3,5},{1,3},{0,1},{10,8},{12,10},{14... | collective-permute-start | bytes 442376 | tf_op jit(solution)/shard_map/ppermute | solution.py:72
  90.4 7.7 %collective-permute-start.26 = (bf16[24,3072]{1,0:T(8,128)(2,1)S(1)}, bf16[24,3072]{1,0:T(8,128)(2,1)S(1)}, u32[]{:S(2)}, u32[]{:S(2)}) collective-permute-start(bf16[24,3072]{1,0:T(8,128)(2,1)S(1)} %get-tuple-element.96), channel_id=1, source_target_pairs={{0,2},{2,4},{4,6},{6,7},{7,5},{5,3},{3,1},{1,0},{8,10},{10,12},{12... | collective-permute-start | bytes 442376 | tf_op jit(solution)/shard_map/ppermute | solution.py:72
  95.0 9.0 %collective-permute-start.19 = (bf16[48,3072]{1,0:T(8,128)(2,1)S(1)}, bf16[48,3072]{1,0:T(8,128)(2,1)S(1)}, u32[]{:S(2)}, u32[]{:S(2)}) collective-permute-start(bf16[48,3072]{1,0:T(8,128)(2,1)S(1)} %pad_maximum_fusion.1), channel_id=1, source_target_pairs={{0,2},{2,4},{4,6},{6,7},{7,5},{5,3},{3,1},{1,0},{8,10},{10,12},{12... | collective-permute-start | bytes 884744 | tf_op jit(solution)/shard_map/ppermute | solution.py:72
  95.6 8.4 %collective-permute-start.20 = (bf16[48,3072]{1,0:T(8,128)(2,1)S(1)}, bf16[48,3072]{1,0:T(8,128)(2,1)S(1)}, u32[]{:S(2)}, u32[]{:S(2)}) collective-permute-start(bf16[48,3072]{1,0:T(8,128)(2,1)S(1)} %pad_maximum_fusion.2), channel_id=1, source_target_pairs={{2,0},{4,2},{6,4},{7,6},{5,7},{3,5},{1,3},{0,1},{10,8},{12,10},{14... | collective-permute-start | bytes 884744 | tf_op jit(solution)/shard_map/ppermute | solution.py:72
  98.2 9.0 %collective-permute-start.28 = (bf16[48,3072]{1,0:T(8,128)(2,1)S(1)}, bf16[48,3072]{1,0:T(8,128)(2,1)S(1)}, u32[]{:S(2)}, u32[]{:S(2)}) collective-permute-start(bf16[48,3072]{1,0:T(8,128)(2,1)S(1)} %pad_maximum_fusion.3), channel_id=1, source_target_pairs={{0,2},{2,4},{4,6},{6,7},{7,5},{5,3},{3,1},{1,0},{8,10},{10,12},{12... | collective-permute-start | bytes 884744 | tf_op jit(solution)/shard_map/ppermute | solution.py:72
  98.8 8.4 %collective-permute-start.29 = (bf16[48,3072]{1,0:T(8,128)(2,1)S(1)}, bf16[48,3072]{1,0:T(8,128)(2,1)S(1)}, u32[]{:S(2)}, u32[]{:S(2)}) collective-permute-start(bf16[48,3072]{1,0:T(8,128)(2,1)S(1)} %pad_maximum_fusion.4), channel_id=1, source_target_pairs={{2,0},{4,2},{6,4},{7,6},{5,7},{3,5},{1,3},{0,1},{10,8},{12,10},{14... | collective-permute-start | bytes 884744 | tf_op jit(solution)/shard_map/ppermute | solution.py:72
  107.3 10.0 %collective-permute-start.31 = (bf16[48,3072]{1,0:T(8,128)(2,1)S(1)}, bf16[48,3072]{1,0:T(8,128)(2,1)S(1)}, u32[]{:S(2)}, u32[]{:S(2)}) collective-permute-start(bf16[48,3072]{1,0:T(8,128)(2,1)S(1)} %get-tuple-element.85), channel_id=1, source_target_pairs={{2,0},{4,2},{6,4},{7,6},{5,7},{3,5},{1,3},{0,1},{10,8},{12,10},{14... | collective-permute-start | bytes 884744 | tf_op jit(solution)/shard_map/ppermute | solution.py:72
  109.0 9.9 %collective-permute-start.30 = (bf16[48,3072]{1,0:T(8,128)(2,1)S(1)}, bf16[48,3072]{1,0:T(8,128)(2,1)S(1)}, u32[]{:S(2)}, u32[]{:S(2)}) collective-permute-start(bf16[48,3072]{1,0:T(8,128)(2,1)S(1)} %get-tuple-element.86), channel_id=1, source_target_pairs={{0,2},{2,4},{4,6},{6,7},{7,5},{5,3},{3,1},{1,0},{8,10},{10,12},{12... | collective-permute-start | bytes 884744 | tf_op jit(solution)/shard_map/ppermute | solution.py:72
  109.6 14.1 %collective-permute-start.22 = (bf16[48,3072]{1,0:T(8,128)(2,1)S(1)}, bf16[48,3072]{1,0:T(8,128)(2,1)S(1)}, u32[]{:S(2)}, u32[]{:S(2)}) collective-permute-start(bf16[48,3072]{1,0:T(8,128)(2,1)S(1)} %get-tuple-element.81), channel_id=1, source_target_pairs={{2,0},{4,2},{6,4},{7,6},{5,7},{3,5},{1,3},{0,1},{10,8},{12,10},{14... | collective-permute-start | bytes 884744 | tf_op jit(solution)/shard_map/ppermute | solution.py:72
  111.2 14.0 %collective-permute-start.21 = (bf16[48,3072]{1,0:T(8,128)(2,1)S(1)}, bf16[48,3072]{1,0:T(8,128)(2,1)S(1)}, u32[]{:S(2)}, u32[]{:S(2)}) collective-permute-start(bf16[48,3072]{1,0:T(8,128)(2,1)S(1)} %get-tuple-element.82), channel_id=1, source_target_pairs={{0,2},{2,4},{4,6},{6,7},{7,5},{5,3},{3,1},{1,0},{8,10},{10,12},{12... | collective-permute-start | bytes 884744 | tf_op jit(solution)/shard_map/ppermute | solution.py:72
  119.1 14.9 %copy-start.3 = (s32[64,2]{0,1:T(2,128)S(1)}, s32[64,2]{0,1:T(2,128)}, u32[]{:S(2)}) copy-start(s32[64,2]{0,1:T(2,128)} %param.7) | copy-start | bytes 1540
  119.1 14.9 %copy-start.4 = (f32[64,2]{0,1:T(2,128)S(1)}, f32[64,2]{0,1:T(2,128)}, u32[]{:S(2)}) copy-start(f32[64,2]{0,1:T(2,128)} %param.8) | copy-start | bytes 1540
  119.1 9.2 %collective-permute-start.33 = (bf16[48,3072]{1,0:T(8,128)(2,1)S(1)}, bf16[48,3072]{1,0:T(8,128)(2,1)S(1)}, u32[]{:S(2)}, u32[]{:S(2)}) collective-permute-start(bf16[48,3072]{1,0:T(8,128)(2,1)S(1)} %get-tuple-element.83), channel_id=1, source_target_pairs={{2,0},{4,2},{6,4},{7,6},{5,7},{3,5},{1,3},{0,1},{10,8},{12,10},{14... | collective-permute-start | bytes 884744 | tf_op jit(solution)/shard_map/ppermute | solution.py:72
  120.7 8.6 %collective-permute-start.32 = (bf16[48,3072]{1,0:T(8,128)(2,1)S(1)}, bf16[48,3072]{1,0:T(8,128)(2,1)S(1)}, u32[]{:S(2)}, u32[]{:S(2)}) collective-permute-start(bf16[48,3072]{1,0:T(8,128)(2,1)S(1)} %get-tuple-element.84), channel_id=1, source_target_pairs={{0,2},{2,4},{4,6},{6,7},{7,5},{5,3},{3,1},{1,0},{8,10},{10,12},{12... | collective-permute-start | bytes 884744 | tf_op jit(solution)/shard_map/ppermute | solution.py:72
  125.2 11.4 %copy-start.1 = (bf16[64,6144]{1,0:T(8,128)(2,1)S(1)}, bf16[64,6144]{1,0:T(8,128)(2,1)}, u32[]{:S(2)}) copy-start(bf16[64,6144]{1,0:T(8,128)(2,1)} %param.6) | copy-start | bytes 2359300
  125.4 6.8 %collective-permute-start.24 = (bf16[48,3072]{1,0:T(8,128)(2,1)S(1)}, bf16[48,3072]{1,0:T(8,128)(2,1)S(1)}, u32[]{:S(2)}, u32[]{:S(2)}) collective-permute-start(bf16[48,3072]{1,0:T(8,128)(2,1)S(1)} %get-tuple-element.79), channel_id=1, source_target_pairs={{2,0},{4,2},{6,4},{7,6},{5,7},{3,5},{1,3},{0,1},{10,8},{12,10},{14... | collective-permute-start | bytes 884744 | tf_op jit(solution)/shard_map/ppermute | solution.py:72
  127.0 6.7 %collective-permute-start.23 = (bf16[48,3072]{1,0:T(8,128)(2,1)S(1)}, bf16[48,3072]{1,0:T(8,128)(2,1)S(1)}, u32[]{:S(2)}, u32[]{:S(2)}) collective-permute-start(bf16[48,3072]{1,0:T(8,128)(2,1)S(1)} %get-tuple-element.80), channel_id=1, source_target_pairs={{0,2},{2,4},{4,6},{6,7},{7,5},{5,3},{3,1},{1,0},{8,10},{10,12},{12... | collective-permute-start | bytes 884744 | tf_op jit(solution)/shard_map/ppermute | solution.py:72
  129.5 4.6 %collective-permute-start.34 = (bf16[24,3072]{1,0:T(8,128)(2,1)S(1)}, bf16[24,3072]{1,0:T(8,128)(2,1)S(1)}, u32[]{:S(2)}, u32[]{:S(2)}) collective-permute-start(bf16[24,3072]{1,0:T(8,128)(2,1)S(1)} %get-tuple-element.107), channel_id=1, source_target_pairs={{0,8},{8,0},{1,9},{9,1},{2,10},{10,2},{3,11},{11,3},{4,12},{12,4},... | collective-permute-start | bytes 442376 | tf_op jit(solution)/shard_map/ppermute | solution.py:162
  133.9 1.4 %collective-permute-start.25 = (bf16[24,3072]{1,0:T(8,128)(2,1)S(1)}, bf16[24,3072]{1,0:T(8,128)(2,1)S(1)}, u32[]{:S(2)}, u32[]{:S(2)}) collective-permute-start(bf16[24,3072]{1,0:T(8,128)(2,1)S(1)} %get-tuple-element.105), channel_id=1, source_target_pairs={{0,8},{8,0},{1,9},{9,1},{2,10},{10,2},{3,11},{11,3},{4,12},{12,4},... | collective-permute-start | bytes 442376 | tf_op jit(solution)/shard_map/ppermute | solution.py:162

commit v8 on v6

v8 whole, which is shorter than its diff:
```python
import functools
import jax
import jax.numpy as jnp
from jax import lax
from jax.experimental import pallas as pl
from jax.experimental.pallas import tpu as pltpu
from jax.sharding import PartitionSpec as P

CAP = 24
COPIES = 16
TILE = 512
MARGIN = 3 * 2**20
CHEAP = pl.CostEstimate(flops=1024, bytes_accessed=1024, transcendentals=0)


def ring_of(count):
    return list(range(0, count, 2)) + list(range(count - 1, 0, -2))


def in_vmem(array):
    return pltpu.with_memory_space_constraint(array, pltpu.VMEM)


def in_hbm(array):
    return pltpu.with_memory_space_constraint(array, pltpu.HBM)


def call(kernel, name, operands, outs, scratch, room):
    return pl.pallas_call(
        kernel,
        in_specs=[pl.BlockSpec(memory_space=memory) for _, memory in operands],
        out_specs=[pl.BlockSpec(memory_space=pltpu.VMEM)] * len(outs),
        out_shape=[pltpu.VMEM(*out) for out in outs],
        scratch_shapes=scratch,
        cost_estimate=CHEAP,
        compiler_params=pltpu.CompilerParams(vmem_limit_bytes=room + MARGIN),
        name=name,
    )(*[in_vmem(array) if memory == pltpu.VMEM else in_hbm(array) for array, memory in operands])


def fill_kernel(source, target, done):
    rows = source.shape[1] // COPIES
    copies = [
        pltpu.make_async_copy(
            source.at[:, pl.ds(i * rows, rows)], target.at[:, pl.ds(i * rows, rows)], done.at[i]
        )
        for i in range(COPIES)
    ]
    for copy in copies:
        copy.start()
    for copy in copies:
        copy.wait()


def fetched(weights):
    operands = [(weights, pltpu.HBM)]
    outs = [(weights.shape, weights.dtype)]
    return call(fill_kernel, "fetched", operands, outs, [pltpu.SemaphoreType.DMA((COPIES,))], 0)[0]


def accumulate(chunks, products):
    for _, total in products:
        total[...] = jnp.zeros_like(total)
    for c, blocks in enumerate(chunks):
        width = blocks[0].shape[1]

        @pl.loop(0, width // TILE)
        def _(i):
            at = pl.multiple_of(i * TILE, TILE)
            rows = jnp.concatenate([block[:, pl.ds(at, TILE)] for block in blocks], axis=0)
            for weights, total in products:
                below = weights[0, pl.ds(pl.multiple_of(c * width + at, TILE), TILE), :]
                total[...] += jnp.dot(rows, below, preferred_element_type=jnp.float32)


def activated(gate, up):
    return (gate / (1.0 + jnp.exp(-gate)) * up).astype(jnp.bfloat16)


def gate_kernel(count, *refs):
    chunks, (weights, out) = (refs[:count], refs[count:2 * count]), refs[2 * count:]
    accumulate(chunks, [(weights, out)])


def up_kernel(count, *refs):
    chunks, (weights, gate, out, total) = (refs[:count], refs[count:2 * count]), refs[2 * count:]
    accumulate(chunks, [(weights, total)])
    out[...] = activated(gate[...], total[...])


def down_copies(source, target, done):
    return [
        pltpu.make_async_copy(
            source.at[:, :, pl.ds(i * TILE, TILE)], target.at[:, :, pl.ds(i * TILE, TILE)], done.at[i]
        )
        for i in range(source.shape[2] // TILE)
    ]


def rest_kernel(*refs):
    chunks, (w_gate, w_up, w_down), outs = (refs[:3], refs[3:6]), refs[6:9], refs[9:15]
    gate, up, hidden, down, done = refs[15:]
    copies = down_copies(w_down, down, done)
    for copy in copies:
        copy.start()
    accumulate(chunks, [(w_gate, gate), (w_up, up)])
    hidden[...] = activated(gate[...], up[...])
    size = outs[0].shape[0]
    for i, copy in enumerate(copies):
        copy.wait()
        part = jnp.dot(hidden[...], down[0, :, i * TILE:(i + 1) * TILE], preferred_element_type=jnp.float32)
        chunk, at = divmod(i * TILE, outs[0].shape[1])
        for b in range(3):
            outs[3 * chunk + b][:, at:at + TILE] = part[b * size:(b + 1) * size].astype(jnp.bfloat16)


def near_down_kernel(hidden, w_down, *refs):
    outs, (down, done) = refs[:-2], refs[-2:]
    size, width = outs[0].shape
    count = len(outs) // 2
    copies = down_copies(w_down, down, done)
    for copy in copies:
        copy.start()
    for i, copy in enumerate(copies):
        copy.wait()
        part = jnp.dot(hidden[...], down[0, :, i * TILE:(i + 1) * TILE], preferred_element_type=jnp.float32)
        chunk, at = divmod(i * TILE, width)
        for b in range(count):
            outs[count * chunk + b][:, at:at + TILE] = part[b * size:(b + 1) * size].astype(jnp.bfloat16)


def routing(expert_ids, gate_probs, experts, slots):
    matches = expert_ids[:, :, None] == experts[None, None, :]
    member = jnp.any(matches, axis=1).astype(jnp.int32)
    weight = jnp.sum(jnp.where(matches, gate_probs[:, :, None], jnp.float32(0.0)), axis=1)
    slot_index = jnp.cumsum(member, axis=0) - member
    column = jnp.arange(slots)
    dispatch_map = (member[None, :, :] == 1) & (slot_index[None, :, :] == column[:, None, None])
    return (jnp.transpose(dispatch_map, (2, 0, 1)), weight)


def per_device(tokens, expert_ids, gate_probs, w_gate, w_up, w_down):
    n_tensor = lax.axis_size("tensor")
    half = n_tensor // 2
    size = 2 * CAP
    width = tokens.shape[1]
    mid_col = width // 2
    units = w_gate.shape[2]
    ring = ring_of(n_tensor)
    right = [(ring[i], ring[(i + 1) % n_tensor]) for i in range(n_tensor)]
    left = [(b, a) for a, b in right]
    swap = [(0, 1), (1, 0)]

    def step(to_right, to_left):
        pair = (lax.ppermute(to_right, "tensor", right), lax.ppermute(to_left, "tensor", left))
        return lax.optimization_barrier(pair)

    def tied(*values):
        return lax.optimization_barrier(values)

    me = lax.axis_index("expert")
    experts = jnp.stack([me, 1 - me])
    dispatch_map, weight = routing(expert_ids, gate_probs, experts, CAP)
    outgoing = jnp.dot(
        dispatch_map.astype(jnp.bfloat16).reshape(size, tokens.shape[0]),
        tokens,
        preferred_element_type=jnp.float32,
    ).astype(jnp.bfloat16)
    own = jnp.concatenate([outgoing[:CAP], lax.ppermute(outgoing[CAP:], "expert", swap)], axis=0)

    own, w_gate = tied(own, w_gate)
    halves = [own[:, :mid_col], own[:, mid_col:]]
    blocks = [[halves[0]], [halves[1]]]

    def arrived(a, b):
        blocks[0].extend([a[0], b[1]])
        blocks[1].extend([b[0], a[1]])

    a = step(halves[0], halves[1])
    b = step(halves[1], halves[0])
    gate_here = fetched(w_gate)
    a, gate_here = tied(a, gate_here)
    b, w_up = tied(b, w_up)
    up_here = fetched(w_up)
    b, up_here = tied(b, up_here)
    arrived(a, b)
    for _ in range(half - 3):
        a = step(*a)
        b = step(*b)
        arrived(a, b)
    near = [(block, pltpu.VMEM) for chunk in blocks for block in chunk]
    count = len(blocks[0])
    rows = count * size
    product = ((rows, units), jnp.float32)
    near_gate, = call(
        functools.partial(gate_kernel, count), "near_gate", near + [(gate_here, pltpu.VMEM)], [product], [],
        rows * units * 8,
    )
    b, near_gate = tied(b, near_gate)
    a = step(*a)
    b = step(*b)
    rest = [[a[0], b[1]], [b[0], a[1]]]
    a, near_gate = tied(a, near_gate)
    far = step(*a)
    near_hidden, = call(
        functools.partial(up_kernel, count), "near_up",
        near + [(up_here, pltpu.VMEM), (near_gate, pltpu.VMEM)], [((rows, units), jnp.bfloat16)],
        [pltpu.VMEM((rows, units), jnp.float32)], rows * units * 16,
    )
    rest = [rest[chunk] + [far[chunk]] for chunk in range(2)]
    rest, near_hidden = tied(rest, near_hidden)
    down_scratch = [pltpu.VMEM(w_down.shape, jnp.bfloat16), pltpu.SemaphoreType.DMA((width // TILE,))]
    down_room = units * width * 2
    rest_parts = call(
        rest_kernel, "rest",
        [(block, pltpu.VMEM) for chunk in rest for block in chunk]
        + [(gate_here, pltpu.VMEM), (up_here, pltpu.VMEM), (w_down, pltpu.HBM)],
        [((size, mid_col), jnp.bfloat16)] * 6,
        [pltpu.VMEM((3 * size, units), jnp.float32)] * 2 + [pltpu.VMEM((3 * size, units), jnp.bfloat16)] + down_scratch,
        down_room + 3 * size * units * 24,
    )
    near_parts = call(
        near_down_kernel, "near_down", [(near_hidden, pltpu.VMEM), (w_down, pltpu.HBM)],
        [((size, mid_col), jnp.bfloat16)] * (2 * count), down_scratch, down_room + rows * TILE * 8,
    )

    def part_of(chunk, distance, side):
        if distance == half - 1:
            return rest_parts[3 * chunk + side].astype(jnp.float32)
        index = 2 * distance - 1 + side if distance else 0
        return near_parts[count * chunk + index].astype(jnp.float32)

    def sent(stream, distance, got):
        to_right = part_of(stream, distance, 1) + got[0].astype(jnp.float32)
        to_left = part_of(1 - stream, distance, 0) + got[1].astype(jnp.float32)
        return step(to_right.astype(jnp.bfloat16), to_left.astype(jnp.bfloat16))

    a = step(rest_parts[2], rest_parts[5])
    b = step(rest_parts[4], rest_parts[0])
    a = sent(0, half - 1, a)
    for distance in range(half - 2, 0, -1):
        b = sent(1, distance, b)
        a = sent(0, distance, a)
    totals = [
        part_of(0, 0, 0) + a[0].astype(jnp.float32) + b[1].astype(jnp.float32),
        part_of(1, 0, 0) + b[0].astype(jnp.float32) + a[1].astype(jnp.float32),
    ]
    total = jnp.concatenate(totals, axis=1).astype(jnp.bfloat16)
    returned = jnp.stack([total[:CAP], lax.ppermute(total[CAP:], "expert", swap)])
    combine = dispatch_map.astype(jnp.float32) * jnp.transpose(weight)[:, None, :]
    mixed = jnp.einsum("wcr,wcd->rd", combine, returned.astype(jnp.float32))
    return mixed.astype(jnp.bfloat16)


def solution(mesh):
    in_specs = (
        P(("groups", "expert", "tensor"), None),
        P(("groups", "expert", "tensor"), None),
        P(("groups", "expert", "tensor"), None),
        P("expert", None, "tensor"),
        P("expert", None, "tensor"),
        P("expert", "tensor", None),
    )
    out_specs = P(("groups", "expert", "tensor"), None)
    return jax.shard_map(
        per_device, mesh=mesh, in_specs=in_specs, out_specs=out_specs, check_vma=False
    )
```

time: 130 us -> 112 us (0.86)
  waiting for transfers between devices: 76 us -> 39.9 us
  Pallas kernels: 9.45 us -> 36.7 us
  matrix products: 22.8 us -> 1.59 us
  starting transfers between devices: 18.2 us -> 30.6 us
    pallas_call x2 -> x6, Pallas kernels: 9.45 us -> 36.7 us  [call(): pl.pallas_call(kernel, in_specs=[pl.BlockSpec(memory_space=memory) for _,...]
    dot_general x7 -> x1, matrix products: 21.5 us -> 0.3 us  [per_device(): jnp.dot(dispatch_map.astype(jnp.bfloat16).reshape(size, tokens.shape[0]),...]
    ppermute x8 -> x14, waiting for transfers between devices: 41.5 us -> 20.8 us  [step(): lax.ppermute(to_left, 'tensor', left)]
    ppermute x8 -> x14, waiting for transfers between devices: 31.8 us -> 16.5 us  [step(): lax.ppermute(to_right, 'tensor', right)]
    ppermute x8 -> x14, starting transfers between devices: 6.76 us -> 18.7 us  [step(): lax.ppermute(to_right, 'tensor', right)]
    ppermute x8 -> x14, starting transfers between devices: 10.9 us -> 11.3 us  [step(): lax.ppermute(to_left, 'tensor', left)]
  transfers between devices with their start and end apart: 18 -> 30, of which waited for: 18 -> 19; matrix products, arithmetic and copies ran while one was open for 8% -> 1% of each run, Pallas kernels for 7% -> 24%
where the time goes in v8:
time: 112 us
  waiting for transfers between devices  39.9 us (36%)
  Pallas kernels  36.7 us (33%)
  starting transfers between devices  30.6 us (27%)
  other arithmetic  2.19 us (2%)
  matrix products  1.59 us (1%)
    pallas_call x6, Pallas kernels, call(): pl.pallas_call(kernel, in_specs=[pl.BlockSpec(memory_space=memory) for _,...  36.7 us
    ppermute x14, waiting for transfers between devices, step(): lax.ppermute(to_left, 'tensor', left)  20.8 us
    ppermute x14, starting transfers between devices, step(): lax.ppermute(to_right, 'tensor', right)  18.7 us
    ppermute x14, waiting for transfers between devices, step(): lax.ppermute(to_right, 'tensor', right)  16.5 us
    ppermute x14, starting transfers between devices, step(): lax.ppermute(to_left, 'tensor', left)  11.3 us
  transfers between devices with their start and end apart: 30, of which 19 were waited for; matrix products, arithmetic and copies ran while one was open for 1% of the time, Pallas kernels for 24%

profile of v8, /device:TPU:0, one launch (start us, length us, event | category | flops | bytes accessed | tf_op | source)
XLA Modules:
  0.0 111.6 jit_solution(1085757400995460267)
XLA Ops:
  0.0 0.1 eq.64
  0.1 0.1 pad_add_fusion
  0.2 0.8 compare_reduce_fusion
  1.0 0.1 copy.17
  1.1 0.1 reduce_window_sum.11
  1.2 0.1 copy.18
  1.3 0.1 fusion.9
  1.4 0.3 convolution_convert_fusion
  1.7 0.5 collective-permute-start
  2.3 1.2 %collective-permute-done = bf16[24,6144]{1,0:T(8,128)(2,1)S(1)} collective-permute-done((bf16[24,6144]{1,0:T(8,128)(2,1)S(1)}, bf16[24,6144]{1,0:T(8,128)(2,1)S(1)}, u32[]{:S(2)}, u32[]{:S(2)}) %collective-permute-start) | collective-permute-done | bytes 294944 | tf_op jit(solution)/shard_map/ppermute | solution.py:169
  3.6 2.9 %collective-permute-start.2 = (bf16[48,3072]{1,0:T(8,128)(2,1)S(1)}, bf16[48,3072]{1,0:T(8,128)(2,1)S(1)}, u32[]{:S(2)}, u32[]{:S(2)}) collective-permute-start(bf16[48,3072]{1,0:T(8,128)(2,1)S(1)} %get-tuple-element.143.refs_5_), channel_id=1, source_target_pairs={{2,0},{4,2},{6,4},{7,6},{5,7},{3,5},{1,3},{0,1},{10,8},{12,10},{14... | collective-permute-start | bytes 884744 | tf_op jit(solution)/shard_map/ppermute | solution.py:155
  6.5 0.1 collective-permute-start.1
  6.6 2.0 %collective-permute-start.7 = (bf16[48,3072]{1,0:T(8,128)(2,1)S(1)}, bf16[48,3072]{1,0:T(8,128)(2,1)S(1)}, u32[]{:S(2)}, u32[]{:S(2)}) collective-permute-start(bf16[48,3072]{1,0:T(8,128)(2,1)S(1)} %get-tuple-element.143.refs_5_), channel_id=1, source_target_pairs={{0,2},{2,4},{4,6},{6,7},{7,5},{5,3},{3,1},{1,0},{8,10},{10,12},{12... | collective-permute-start | bytes 884744 | tf_op jit(solution)/shard_map/ppermute | solution.py:155
  8.6 4.7 %fetched.2.refs_10_.refs_6_ = bf16[1,6144,1024]{2,1,0:T(8,128)(2,1)S(1)} custom-call(bf16[1,6144,1024]{2,1,0:T(8,128)(2,1)} %source), custom_call_target="tpu_custom_call" | custom-call | flops 1024 | bytes 1024 | tf_op jit(solution)/shard_map/fetched/pallas_call | solution.py:29
  13.4 1.0 collective-permute-done.2.refs_7_
  14.3 2.0 %collective-permute-done.1.refs_1_ = bf16[48,3072]{1,0:T(8,128)(2,1)S(1)} collective-permute-done((bf16[48,3072]{1,0:T(8,128)(2,1)S(1)}, bf16[48,3072]{1,0:T(8,128)(2,1)S(1)}, u32[]{:S(2)}, u32[]{:S(2)}) %collective-permute-start.1) | collective-permute-done | bytes 294944 | tf_op jit(solution)/shard_map/ppermute | solution.py:155
  16.4 0.1 collective-permute-start.3
  16.5 1.9 %collective-permute-start.4 = (bf16[48,3072]{1,0:T(8,128)(2,1)S(1)}, bf16[48,3072]{1,0:T(8,128)(2,1)S(1)}, u32[]{:S(2)}, u32[]{:S(2)}) collective-permute-start(bf16[48,3072]{1,0:T(8,128)(2,1)S(1)} %collective-permute-done.2.refs_7_), channel_id=1, source_target_pairs={{2,0},{4,2},{6,4},{7,6},{5,7},{3,5},{1,3},{0,1},{10,8},{12,10},{14... | collective-permute-start | bytes 884744 | tf_op jit(solution)/shard_map/ppermute | solution.py:155
  18.4 4.3 %collective-permute-done.7.refs_6_ = bf16[48,3072]{1,0:T(8,128)(2,1)S(1)} collective-permute-done((bf16[48,3072]{1,0:T(8,128)(2,1)S(1)}, bf16[48,3072]{1,0:T(8,128)(2,1)S(1)}, u32[]{:S(2)}, u32[]{:S(2)}) %collective-permute-start.7) | collective-permute-done | bytes 294944 | tf_op jit(solution)/shard_map/ppermute | solution.py:155
  22.7 4.7 %fetched.3.refs_10_.refs_7_ = bf16[1,6144,1024]{2,1,0:T(8,128)(2,1)S(1)} custom-call(bf16[1,6144,1024]{2,1,0:T(8,128)(2,1)} %source.1), custom_call_target="tpu_custom_call" | custom-call | flops 1024 | bytes 1024 | tf_op jit(solution)/shard_map/fetched/pallas_call | solution.py:29
  27.4 0.1 collective-permute-start.9
  27.6 1.9 %collective-permute-start.10 = (bf16[48,3072]{1,0:T(8,128)(2,1)S(1)}, bf16[48,3072]{1,0:T(8,128)(2,1)S(1)}, u32[]{:S(2)}, u32[]{:S(2)}) collective-permute-start(bf16[48,3072]{1,0:T(8,128)(2,1)S(1)} %collective-permute-done.8.refs_2_), channel_id=1, source_target_pairs={{2,0},{4,2},{6,4},{7,6},{5,7},{3,5},{1,3},{0,1},{10,8},{12,10},{14... | collective-permute-start | bytes 884744 | tf_op jit(solution)/shard_map/ppermute | solution.py:155
  29.5 0.1 collective-permute-start.5
  29.6 1.9 %collective-permute-start.6 = (bf16[48,3072]{1,0:T(8,128)(2,1)S(1)}, bf16[48,3072]{1,0:T(8,128)(2,1)S(1)}, u32[]{:S(2)}, u32[]{:S(2)}) collective-permute-start(bf16[48,3072]{1,0:T(8,128)(2,1)S(1)} %collective-permute-done.4.refs_9_), channel_id=1, source_target_pairs={{2,0},{4,2},{6,4},{7,6},{5,7},{3,5},{1,3},{0,1},{10,8},{12,10},{14... | collective-permute-start | bytes 884744 | tf_op jit(solution)/shard_map/ppermute | solution.py:155
  31.6 5.9 %collective-permute-done.9.refs_8_ = bf16[48,3072]{1,0:T(8,128)(2,1)S(1)} collective-permute-done((bf16[48,3072]{1,0:T(8,128)(2,1)S(1)}, bf16[48,3072]{1,0:T(8,128)(2,1)S(1)}, u32[]{:S(2)}, u32[]{:S(2)}) %collective-permute-start.9) | collective-permute-done | bytes 294944 | tf_op jit(solution)/shard_map/ppermute | solution.py:155
  37.4 0.1 collective-permute-done.10.refs_4_
  37.5 5.2 %near_gate.1.refs_11_ = f32[240,1024]{1,0:T(8,128)S(1)} custom-call(bf16[48,3072]{1,0:T(8,128)(2,1)S(1)} %get-tuple-element.144.refs_0_, bf16[48,3072]{1,0:T(8,128)(2,1)S(1)} %collective-permute-done.1.refs_1_, bf16[48,3072]{1,0:T(8,128)(2,1)S(1)} %collective-permute-done.8.refs_2_, bf16[48,3072]{1,0:T(8,128)(2,1)S(1)} %collective-permute-done.3.refs_3_, ...), custom_call_target="tpu_custom_call" | custom-call | flops 1024 | bytes 1024 | tf_op jit(solution)/shard_map/near_gate/pallas_call | solution.py:29
  42.7 1.9 %collective-permute-start.11 = (bf16[48,3072]{1,0:T(8,128)(2,1)S(1)}, bf16[48,3072]{1,0:T(8,128)(2,1)S(1)}, u32[]{:S(2)}, u32[]{:S(2)}) collective-permute-start(bf16[48,3072]{1,0:T(8,128)(2,1)S(1)} %collective-permute-done.9.refs_8_), channel_id=1, source_target_pairs={{0,2},{2,4},{4,6},{6,7},{7,5},{5,3},{3,1},{1,0},{8,10},{10,12},{12... | collective-permute-start | bytes 884744 | tf_op jit(solution)/shard_map/ppermute | solution.py:155
  44.7 0.2 collective-permute-start.12
  44.8 1.9 %collective-permute-start.13 = (bf16[48,3072]{1,0:T(8,128)(2,1)S(1)}, bf16[48,3072]{1,0:T(8,128)(2,1)S(1)}, u32[]{:S(2)}, u32[]{:S(2)}) collective-permute-start(bf16[48,3072]{1,0:T(8,128)(2,1)S(1)} %collective-permute-done.5.refs_0_), channel_id=1, source_target_pairs={{0,2},{2,4},{4,6},{6,7},{7,5},{5,3},{3,1},{1,0},{8,10},{10,12},{12... | collective-permute-start | bytes 884744 | tf_op jit(solution)/shard_map/ppermute | solution.py:155
  46.7 0.2 collective-permute-start.14
  46.9 5.5 %near_up.1.hidden = bf16[240,1024]{1,0:T(8,128)(2,1)S(1)} custom-call(bf16[48,3072]{1,0:T(8,128)(2,1)S(1)} %get-tuple-element.144.refs_0_, bf16[48,3072]{1,0:T(8,128)(2,1)S(1)} %collective-permute-done.1.refs_1_, bf16[48,3072]{1,0:T(8,128)(2,1)S(1)} %collective-permute-done.8.refs_2_, bf16[48,3072]{1,0:T(8,128)(2,1)S(1)} %collective-permute-done.3.refs_3_, ...), custom_call_target="tpu_custom_call" | custom-call | flops 1024 | bytes 1024 | tf_op jit(solution)/shard_map/near_up/pallas_call | solution.py:29
  52.3 0.9 collective-permute-done.13.refs_2_
  53.2 1.3 %collective-permute-done.14.refs_5_ = bf16[48,3072]{1,0:T(8,128)(2,1)S(1)} collective-permute-done((bf16[48,3072]{1,0:T(8,128)(2,1)S(1)}, bf16[48,3072]{1,0:T(8,128)(2,1)S(1)}, u32[]{:S(2)}, u32[]{:S(2)}) %collective-permute-start.14) | collective-permute-done | bytes 294944 | tf_op jit(solution)/shard_map/ppermute | solution.py:155
  54.5 10.1 %rest.1 = (bf16[48,3072]{1,0:T(8,128)(2,1)S(1)}, bf16[48,3072]{1,0:T(8,128)(2,1)S(1)}, bf16[48,3072]{1,0:T(8,128)(2,1)S(1)}, bf16[48,3072]{1,0:T(8,128)(2,1)S(1)...) custom-call(bf16[48,3072]{1,0:T(8,128)(2,1)S(1)} %collective-permute-done.5.refs_0_, ...), custom_call_target="tpu_custom_call" | custom-call | flops 1024 | bytes 1024 | tf_op jit(solution)/shard_map/rest/pallas_call | solution.py:29
  64.7 1.6 %collective-permute-start.15 = (bf16[48,3072]{1,0:T(8,128)(2,1)S(1)}, bf16[48,3072]{1,0:T(8,128)(2,1)S(1)}, u32[]{:S(2)}, u32[]{:S(2)}) collective-permute-start(bf16[48,3072]{1,0:T(8,128)(2,1)S(1)} %get-tuple-element.115), channel_id=1, source_target_pairs={{0,2},{2,4},{4,6},{6,7},{7,5},{5,3},{3,1},{1,0},{8,10},{10,12},{12... | collective-permute-start | bytes 884744 | tf_op jit(solution)/shard_map/ppermute | solution.py:155
  66.3 0.4 collective-permute-start.16
  66.8 1.6 %collective-permute-start.23 = (bf16[48,3072]{1,0:T(8,128)(2,1)S(1)}, bf16[48,3072]{1,0:T(8,128)(2,1)S(1)}, u32[]{:S(2)}, u32[]{:S(2)}) collective-permute-start(bf16[48,3072]{1,0:T(8,128)(2,1)S(1)} %get-tuple-element.129), channel_id=1, source_target_pairs={{0,2},{2,4},{4,6},{6,7},{7,5},{5,3},{3,1},{1,0},{8,10},{10,12},{12... | collective-permute-start | bytes 884744 | tf_op jit(solution)/shard_map/ppermute | solution.py:155
  68.3 0.4 collective-permute-start.24
  68.8 6.4 %near_down.1 = (bf16[48,3072]{1,0:T(8,128)(2,1)S(1)}, bf16[48,3072]{1,0:T(8,128)(2,1)S(1)}, bf16[48,3072]{1,0:T(8,128)(2,1)S(1)}, bf16[48,3072]{1,0:T(8,128)(2,1...) custom-call(bf16[240,1024]{1,0:T(8,128)(2,1)S(1)} %near_up.1.hidden,, ...), custom_call_target="tpu_custom_call" | custom-call | flops 1024 | bytes 1024 | tf_op jit(solution)/shard_map/near_down/pallas_call | solution.py:29
  75.2 1.0 collective-permute-done.16
  76.4 2.1 %collective-permute-start.17 = (bf16[48,3072]{1,0:T(8,128)(2,1)S(1)}, bf16[48,3072]{1,0:T(8,128)(2,1)S(1)}, u32[]{:S(2)}, u32[]{:S(2)}) collective-permute-start(bf16[48,3072]{1,0:T(8,128)(2,1)S(1)} %add_convert_fusion.11), channel_id=1, source_target_pairs={{0,2},{2,4},{4,6},{6,7},{7,5},{5,3},{3,1},{1,0},{8,10},{10,12},{12... | collective-permute-start | bytes 884744 | tf_op jit(solution)/shard_map/ppermute | solution.py:155
  78.5 4.0 %collective-permute-done.24 = bf16[48,3072]{1,0:T(8,128)(2,1)S(1)} collective-permute-done((bf16[48,3072]{1,0:T(8,128)(2,1)S(1)}, bf16[48,3072]{1,0:T(8,128)(2,1)S(1)}, u32[]{:S(2)}, u32[]{:S(2)}) %collective-permute-start.24) | collective-permute-done | bytes 294944 | tf_op jit(solution)/shard_map/ppermute | solution.py:155
  82.6 1.6 %collective-permute-start.25 = (bf16[48,3072]{1,0:T(8,128)(2,1)S(1)}, bf16[48,3072]{1,0:T(8,128)(2,1)S(1)}, u32[]{:S(2)}, u32[]{:S(2)}) collective-permute-start(bf16[48,3072]{1,0:T(8,128)(2,1)S(1)} %add_convert_fusion.5), channel_id=1, source_target_pairs={{0,2},{2,4},{4,6},{6,7},{7,5},{5,3},{3,1},{1,0},{8,10},{10,12},{12... | collective-permute-start | bytes 884744 | tf_op jit(solution)/shard_map/ppermute | solution.py:155
  84.3 0.5 collective-permute-start.26
  84.8 4.0 %collective-permute-done.18 = bf16[48,3072]{1,0:T(8,128)(2,1)S(1)} collective-permute-done((bf16[48,3072]{1,0:T(8,128)(2,1)S(1)}, bf16[48,3072]{1,0:T(8,128)(2,1)S(1)}, u32[]{:S(2)}, u32[]{:S(2)}) %collective-permute-start.18) | collective-permute-done | bytes 294944 | tf_op jit(solution)/shard_map/ppermute | solution.py:155
  88.8 0.1 add_convert_fusion.9
  88.9 1.6 %collective-permute-start.19 = (bf16[48,3072]{1,0:T(8,128)(2,1)S(1)}, bf16[48,3072]{1,0:T(8,128)(2,1)S(1)}, u32[]{:S(2)}, u32[]{:S(2)}) collective-permute-start(bf16[48,3072]{1,0:T(8,128)(2,1)S(1)} %add_convert_fusion.9), channel_id=1, source_target_pairs={{0,2},{2,4},{4,6},{6,7},{7,5},{5,3},{3,1},{1,0},{8,10},{10,12},{12... | collective-permute-start | bytes 884744 | tf_op jit(solution)/shard_map/ppermute | solution.py:155
  90.6 0.5 collective-permute-start.20
  91.1 1.6 %collective-permute-done.25 = bf16[48,3072]{1,0:T(8,128)(2,1)S(1)} collective-permute-done((bf16[48,3072]{1,0:T(8,128)(2,1)S(1)}, bf16[48,3072]{1,0:T(8,128)(2,1)S(1)}, u32[]{:S(2)}, u32[]{:S(2)}) %collective-permute-start.25) | collective-permute-done | bytes 294944 | tf_op jit(solution)/shard_map/ppermute | solution.py:155
  92.7 2.4 %collective-permute-done.26 = bf16[48,3072]{1,0:T(8,128)(2,1)S(1)} collective-permute-done((bf16[48,3072]{1,0:T(8,128)(2,1)S(1)}, bf16[48,3072]{1,0:T(8,128)(2,1)S(1)}, u32[]{:S(2)}, u32[]{:S(2)}) %collective-permute-start.26) | collective-permute-done | bytes 294944 | tf_op jit(solution)/shard_map/ppermute | solution.py:155
  95.3 0.1 add_convert_fusion.3
  95.4 2.1 %collective-permute-start.27 = (bf16[48,3072]{1,0:T(8,128)(2,1)S(1)}, bf16[48,3072]{1,0:T(8,128)(2,1)S(1)}, u32[]{:S(2)}, u32[]{:S(2)}) collective-permute-start(bf16[48,3072]{1,0:T(8,128)(2,1)S(1)} %add_convert_fusion.3), channel_id=1, source_target_pairs={{0,2},{2,4},{4,6},{6,7},{7,5},{5,3},{3,1},{1,0},{8,10},{10,12},{12... | collective-permute-start | bytes 884744 | tf_op jit(solution)/shard_map/ppermute | solution.py:155
  97.4 1.6 %collective-permute-done.19 = bf16[48,3072]{1,0:T(8,128)(2,1)S(1)} collective-permute-done((bf16[48,3072]{1,0:T(8,128)(2,1)S(1)}, bf16[48,3072]{1,0:T(8,128)(2,1)S(1)}, u32[]{:S(2)}, u32[]{:S(2)}) %collective-permute-start.19) | collective-permute-done | bytes 294944 | tf_op jit(solution)/shard_map/ppermute | solution.py:155
  99.1 2.4 %collective-permute-done.20 = bf16[48,3072]{1,0:T(8,128)(2,1)S(1)} collective-permute-done((bf16[48,3072]{1,0:T(8,128)(2,1)S(1)}, bf16[48,3072]{1,0:T(8,128)(2,1)S(1)}, u32[]{:S(2)}, u32[]{:S(2)}) %collective-permute-start.20) | collective-permute-done | bytes 294944 | tf_op jit(solution)/shard_map/ppermute | solution.py:155
  101.4 0.1 add_convert_fusion.6
  101.7 2.1 %collective-permute-start.21 = (bf16[48,3072]{1,0:T(8,128)(2,1)S(1)}, bf16[48,3072]{1,0:T(8,128)(2,1)S(1)}, u32[]{:S(2)}, u32[]{:S(2)}) collective-permute-start(bf16[48,3072]{1,0:T(8,128)(2,1)S(1)} %add_convert_fusion.7), channel_id=1, source_target_pairs={{0,2},{2,4},{4,6},{6,7},{7,5},{5,3},{3,1},{1,0},{8,10},{10,12},{12... | collective-permute-start | bytes 884744 | tf_op jit(solution)/shard_map/ppermute | solution.py:155
  103.7 0.9 collective-permute-done.28
  104.6 3.7 %collective-permute-done.22 = bf16[48,3072]{1,0:T(8,128)(2,1)S(1)} collective-permute-done((bf16[48,3072]{1,0:T(8,128)(2,1)S(1)}, bf16[48,3072]{1,0:T(8,128)(2,1)S(1)}, u32[]{:S(2)}, u32[]{:S(2)}) %collective-permute-start.22) | collective-permute-done | bytes 294944 | tf_op jit(solution)/shard_map/ppermute | solution.py:155
  108.3 0.1 collective-permute-done.21
  108.4 0.2 add_convert_fusion
  108.8 0.1 fusion.14
  108.9 1.5 %collective-permute-done.29 = bf16[24,6144]{1,0:T(8,128)(2,1)S(1)} collective-permute-done((bf16[24,6144]{1,0:T(8,128)(2,1)S(1)}, bf16[24,6144]{1,0:T(8,128)(2,1)S(1)}, u32[]{:S(2)}, u32[]{:S(2)}) %collective-permute-start.29) | collective-permute-done | bytes 294944 | tf_op jit(solution)/shard_map/ppermute | solution.py:249
  110.3 1.3 %fusion = bf16[64,6144]{1,0:T(8,128)(2,1)} fusion(bf16[1,24,6144]{2,1,0:T(8,128)(2,1)S(1)} %bitcast.22, bf16[1,24,6144]{2,1,0:T(8,128)(2,1)S(1)} %get-tuple-element.141, bf16[2,64]{1,0:T(2,128)(2,1)S(1)} %bitcast.23, s32[2,64]{1,0:T(2,128)S(1)} %subtract_bitcast_fusion, pred[2,64]{1,0:T(4,128)(4,1)S(1)} %get-tuple-element.147), kind=kOutput, calls=%fused_computation.1 | convolution fusion | flops 38052864 | bytes 1377152 | tf_op jit(solution)/shard_map/wcr,wcd->rd/dot_general | solution.py:251
  (38 shorter events, 1.0 us)
Async XLA Ops:
  0.0 1.4 %copy-start = (bf16[64,6144]{1,0:T(8,128)(2,1)S(1)}, bf16[64,6144]{1,0:T(8,128)(2,1)}, u32[]{:S(2)}) copy-start(bf16[64,6144]{1,0:T(8,128)(2,1)} %param.6) | copy-start | bytes 2359300
  1.7 1.7 %collective-permute-start = (bf16[24,6144]{1,0:T(8,128)(2,1)S(1)}, bf16[24,6144]{1,0:T(8,128)(2,1)S(1)}, u32[]{:S(2)}, u32[]{:S(2)}) collective-permute-start(bf16[24,6144]{1,0:T(8,128)(2,1)S(1)} %get-tuple-element.146), channel_id=1, source_target_pairs={{0,8},{8,0},{1,9},{9,1},{2,10},{10,2},{3,11},{11,3},{4,12},{12,4},... | collective-permute-start | bytes 884744 | tf_op jit(solution)/shard_map/ppermute | solution.py:169
  3.6 10.8 %collective-permute-start.2 = (bf16[48,3072]{1,0:T(8,128)(2,1)S(1)}, bf16[48,3072]{1,0:T(8,128)(2,1)S(1)}, u32[]{:S(2)}, u32[]{:S(2)}) collective-permute-start(bf16[48,3072]{1,0:T(8,128)(2,1)S(1)} %get-tuple-element.143.refs_5_), channel_id=1, source_target_pairs={{2,0},{4,2},{6,4},{7,6},{5,7},{3,5},{1,3},{0,1},{10,8},{12,10},{14... | collective-permute-start | bytes 884744 | tf_op jit(solution)/shard_map/ppermute | solution.py:155
  6.5 9.9 %collective-permute-start.1 = (bf16[48,3072]{1,0:T(8,128)(2,1)S(1)}, bf16[48,3072]{1,0:T(8,128)(2,1)S(1)}, u32[]{:S(2)}, u32[]{:S(2)}) collective-permute-start(bf16[48,3072]{1,0:T(8,128)(2,1)S(1)} %get-tuple-element.144.refs_0_), channel_id=1, source_target_pairs={{0,2},{2,4},{4,6},{6,7},{7,5},{5,3},{3,1},{1,0},{8,10},{10,12},{12... | collective-permute-start | bytes 884744 | tf_op jit(solution)/shard_map/ppermute | solution.py:155
  6.6 16.1 %collective-permute-start.7 = (bf16[48,3072]{1,0:T(8,128)(2,1)S(1)}, bf16[48,3072]{1,0:T(8,128)(2,1)S(1)}, u32[]{:S(2)}, u32[]{:S(2)}) collective-permute-start(bf16[48,3072]{1,0:T(8,128)(2,1)S(1)} %get-tuple-element.143.refs_5_), channel_id=1, source_target_pairs={{0,2},{2,4},{4,6},{6,7},{7,5},{5,3},{3,1},{1,0},{8,10},{10,12},{12... | collective-permute-start | bytes 884744 | tf_op jit(solution)/shard_map/ppermute | solution.py:155
  8.6 14.1 %collective-permute-start.8 = (bf16[48,3072]{1,0:T(8,128)(2,1)S(1)}, bf16[48,3072]{1,0:T(8,128)(2,1)S(1)}, u32[]{:S(2)}, u32[]{:S(2)}) collective-permute-start(bf16[48,3072]{1,0:T(8,128)(2,1)S(1)} %get-tuple-element.144.refs_0_), channel_id=1, source_target_pairs={{2,0},{4,2},{6,4},{7,6},{5,7},{3,5},{1,3},{0,1},{10,8},{12,10},{14... | collective-permute-start | bytes 884744 | tf_op jit(solution)/shard_map/ppermute | solution.py:155
  16.4 13.1 %collective-permute-start.3 = (bf16[48,3072]{1,0:T(8,128)(2,1)S(1)}, bf16[48,3072]{1,0:T(8,128)(2,1)S(1)}, u32[]{:S(2)}, u32[]{:S(2)}) collective-permute-start(bf16[48,3072]{1,0:T(8,128)(2,1)S(1)} %collective-permute-done.1.refs_1_), channel_id=1, source_target_pairs={{0,2},{2,4},{4,6},{6,7},{7,5},{5,3},{3,1},{1,0},{8,10},{10,12},{12... | collective-permute-start | bytes 884744 | tf_op jit(solution)/shard_map/ppermute | solution.py:155
  16.5 13.1 %collective-permute-start.4 = (bf16[48,3072]{1,0:T(8,128)(2,1)S(1)}, bf16[48,3072]{1,0:T(8,128)(2,1)S(1)}, u32[]{:S(2)}, u32[]{:S(2)}) collective-permute-start(bf16[48,3072]{1,0:T(8,128)(2,1)S(1)} %collective-permute-done.2.refs_7_), channel_id=1, source_target_pairs={{2,0},{4,2},{6,4},{7,6},{5,7},{3,5},{1,3},{0,1},{10,8},{12,10},{14... | collective-permute-start | bytes 884744 | tf_op jit(solution)/shard_map/ppermute | solution.py:155
  27.4 10.0 %collective-permute-start.9 = (bf16[48,3072]{1,0:T(8,128)(2,1)S(1)}, bf16[48,3072]{1,0:T(8,128)(2,1)S(1)}, u32[]{:S(2)}, u32[]{:S(2)}) collective-permute-start(bf16[48,3072]{1,0:T(8,128)(2,1)S(1)} %collective-permute-done.7.refs_6_), channel_id=1, source_target_pairs={{0,2},{2,4},{4,6},{6,7},{7,5},{5,3},{3,1},{1,0},{8,10},{10,12},{12... | collective-permute-start | bytes 884744 | tf_op jit(solution)/shard_map/ppermute | solution.py:155
  27.6 9.9 %collective-permute-start.10 = (bf16[48,3072]{1,0:T(8,128)(2,1)S(1)}, bf16[48,3072]{1,0:T(8,128)(2,1)S(1)}, u32[]{:S(2)}, u32[]{:S(2)}) collective-permute-start(bf16[48,3072]{1,0:T(8,128)(2,1)S(1)} %collective-permute-done.8.refs_2_), channel_id=1, source_target_pairs={{2,0},{4,2},{6,4},{7,6},{5,7},{3,5},{1,3},{0,1},{10,8},{12,10},{14... | collective-permute-start | bytes 884744 | tf_op jit(solution)/shard_map/ppermute | solution.py:155
  29.5 15.3 %collective-permute-start.5 = (bf16[48,3072]{1,0:T(8,128)(2,1)S(1)}, bf16[48,3072]{1,0:T(8,128)(2,1)S(1)}, u32[]{:S(2)}, u32[]{:S(2)}) collective-permute-start(bf16[48,3072]{1,0:T(8,128)(2,1)S(1)} %collective-permute-done.3.refs_3_), channel_id=1, source_target_pairs={{0,2},{2,4},{4,6},{6,7},{7,5},{5,3},{3,1},{1,0},{8,10},{10,12},{12... | collective-permute-start | bytes 884744 | tf_op jit(solution)/shard_map/ppermute | solution.py:155
  29.6 15.2 %collective-permute-start.6 = (bf16[48,3072]{1,0:T(8,128)(2,1)S(1)}, bf16[48,3072]{1,0:T(8,128)(2,1)S(1)}, u32[]{:S(2)}, u32[]{:S(2)}) collective-permute-start(bf16[48,3072]{1,0:T(8,128)(2,1)S(1)} %collective-permute-done.4.refs_9_), channel_id=1, source_target_pairs={{2,0},{4,2},{6,4},{7,6},{5,7},{3,5},{1,3},{0,1},{10,8},{12,10},{14... | collective-permute-start | bytes 884744 | tf_op jit(solution)/shard_map/ppermute | solution.py:155
  42.7 9.6 %collective-permute-start.11 = (bf16[48,3072]{1,0:T(8,128)(2,1)S(1)}, bf16[48,3072]{1,0:T(8,128)(2,1)S(1)}, u32[]{:S(2)}, u32[]{:S(2)}) collective-permute-start(bf16[48,3072]{1,0:T(8,128)(2,1)S(1)} %collective-permute-done.9.refs_8_), channel_id=1, source_target_pairs={{0,2},{2,4},{4,6},{6,7},{7,5},{5,3},{3,1},{1,0},{8,10},{10,12},{12... | collective-permute-start | bytes 884744 | tf_op jit(solution)/shard_map/ppermute | solution.py:155
  44.7 7.7 %collective-permute-start.12 = (bf16[48,3072]{1,0:T(8,128)(2,1)S(1)}, bf16[48,3072]{1,0:T(8,128)(2,1)S(1)}, u32[]{:S(2)}, u32[]{:S(2)}) collective-permute-start(bf16[48,3072]{1,0:T(8,128)(2,1)S(1)} %collective-permute-done.10.refs_4_), channel_id=1, source_target_pairs={{2,0},{4,2},{6,4},{7,6},{5,7},{3,5},{1,3},{0,1},{10,8},{12,10},{14... | collective-permute-start | bytes 884744 | tf_op jit(solution)/shard_map/ppermute | solution.py:155
  44.8 8.4 %collective-permute-start.13 = (bf16[48,3072]{1,0:T(8,128)(2,1)S(1)}, bf16[48,3072]{1,0:T(8,128)(2,1)S(1)}, u32[]{:S(2)}, u32[]{:S(2)}) collective-permute-start(bf16[48,3072]{1,0:T(8,128)(2,1)S(1)} %collective-permute-done.5.refs_0_), channel_id=1, source_target_pairs={{0,2},{2,4},{4,6},{6,7},{7,5},{5,3},{3,1},{1,0},{8,10},{10,12},{12... | collective-permute-start | bytes 884744 | tf_op jit(solution)/shard_map/ppermute | solution.py:155
  46.7 7.8 %collective-permute-start.14 = (bf16[48,3072]{1,0:T(8,128)(2,1)S(1)}, bf16[48,3072]{1,0:T(8,128)(2,1)S(1)}, u32[]{:S(2)}, u32[]{:S(2)}) collective-permute-start(bf16[48,3072]{1,0:T(8,128)(2,1)S(1)} %collective-permute-done.6.refs_4_), channel_id=1, source_target_pairs={{2,0},{4,2},{6,4},{7,6},{5,7},{3,5},{1,3},{0,1},{10,8},{12,10},{14... | collective-permute-start | bytes 884744 | tf_op jit(solution)/shard_map/ppermute | solution.py:155
  64.7 10.5 %collective-permute-start.15 = (bf16[48,3072]{1,0:T(8,128)(2,1)S(1)}, bf16[48,3072]{1,0:T(8,128)(2,1)S(1)}, u32[]{:S(2)}, u32[]{:S(2)}) collective-permute-start(bf16[48,3072]{1,0:T(8,128)(2,1)S(1)} %get-tuple-element.115), channel_id=1, source_target_pairs={{0,2},{2,4},{4,6},{6,7},{7,5},{5,3},{3,1},{1,0},{8,10},{10,12},{12... | collective-permute-start | bytes 884744 | tf_op jit(solution)/shard_map/ppermute | solution.py:155
  66.3 9.9 %collective-permute-start.16 = (bf16[48,3072]{1,0:T(8,128)(2,1)S(1)}, bf16[48,3072]{1,0:T(8,128)(2,1)S(1)}, u32[]{:S(2)}, u32[]{:S(2)}) collective-permute-start(bf16[48,3072]{1,0:T(8,128)(2,1)S(1)} %get-tuple-element.116), channel_id=1, source_target_pairs={{2,0},{4,2},{6,4},{7,6},{5,7},{3,5},{1,3},{0,1},{10,8},{12,10},{14... | collective-permute-start | bytes 884744 | tf_op jit(solution)/shard_map/ppermute | solution.py:155
  66.8 11.7 %collective-permute-start.23 = (bf16[48,3072]{1,0:T(8,128)(2,1)S(1)}, bf16[48,3072]{1,0:T(8,128)(2,1)S(1)}, u32[]{:S(2)}, u32[]{:S(2)}) collective-permute-start(bf16[48,3072]{1,0:T(8,128)(2,1)S(1)} %get-tuple-element.129), channel_id=1, source_target_pairs={{0,2},{2,4},{4,6},{6,7},{7,5},{5,3},{3,1},{1,0},{8,10},{10,12},{12... | collective-permute-start | bytes 884744 | tf_op jit(solution)/shard_map/ppermute | solution.py:155
  68.3 43.3 %copy-start.1 = (bf16[64,6144]{1,0:T(8,128)(2,1)S(1)}, bf16[64,6144]{1,0:T(8,128)(2,1)}, u32[]{:S(2)}) copy-start(bf16[64,6144]{1,0:T(8,128)(2,1)} %param.6) | copy-start | bytes 2359300
  68.3 40.4 %copy-start.2 = (s32[64,2]{0,1:T(2,128)S(1)}, s32[64,2]{0,1:T(2,128)}, u32[]{:S(2)}) copy-start(s32[64,2]{0,1:T(2,128)} %param.7) | copy-start | bytes 1540
  68.3 40.4 %copy-start.3 = (f32[64,2]{0,1:T(2,128)S(1)}, f32[64,2]{0,1:T(2,128)}, u32[]{:S(2)}) copy-start(f32[64,2]{0,1:T(2,128)} %param.8) | copy-start | bytes 1540
  68.3 14.2 %collective-permute-start.24 = (bf16[48,3072]{1,0:T(8,128)(2,1)S(1)}, bf16[48,3072]{1,0:T(8,128)(2,1)S(1)}, u32[]{:S(2)}, u32[]{:S(2)}) collective-permute-start(bf16[48,3072]{1,0:T(8,128)(2,1)S(1)} %get-tuple-element.130), channel_id=1, source_target_pairs={{2,0},{4,2},{6,4},{7,6},{5,7},{3,5},{1,3},{0,1},{10,8},{12,10},{14... | collective-permute-start | bytes 884744 | tf_op jit(solution)/shard_map/ppermute | solution.py:155
  76.3 12.6 %collective-permute-start.18 = (bf16[48,3072]{1,0:T(8,128)(2,1)S(1)}, bf16[48,3072]{1,0:T(8,128)(2,1)S(1)}, u32[]{:S(2)}, u32[]{:S(2)}) collective-permute-start(bf16[48,3072]{1,0:T(8,128)(2,1)S(1)} %add_convert_fusion.10), channel_id=1, source_target_pairs={{2,0},{4,2},{6,4},{7,6},{5,7},{3,5},{1,3},{0,1},{10,8},{12,10},{14... | collective-permute-start | bytes 884744 | tf_op jit(solution)/shard_map/ppermute | solution.py:155
  76.4 12.4 %collective-permute-start.17 = (bf16[48,3072]{1,0:T(8,128)(2,1)S(1)}, bf16[48,3072]{1,0:T(8,128)(2,1)S(1)}, u32[]{:S(2)}, u32[]{:S(2)}) collective-permute-start(bf16[48,3072]{1,0:T(8,128)(2,1)S(1)} %add_convert_fusion.11), channel_id=1, source_target_pairs={{0,2},{2,4},{4,6},{6,7},{7,5},{5,3},{3,1},{1,0},{8,10},{10,12},{12... | collective-permute-start | bytes 884744 | tf_op jit(solution)/shard_map/ppermute | solution.py:155
  82.6 10.1 %collective-permute-start.25 = (bf16[48,3072]{1,0:T(8,128)(2,1)S(1)}, bf16[48,3072]{1,0:T(8,128)(2,1)S(1)}, u32[]{:S(2)}, u32[]{:S(2)}) collective-permute-start(bf16[48,3072]{1,0:T(8,128)(2,1)S(1)} %add_convert_fusion.5), channel_id=1, source_target_pairs={{0,2},{2,4},{4,6},{6,7},{7,5},{5,3},{3,1},{1,0},{8,10},{10,12},{12... | collective-permute-start | bytes 884744 | tf_op jit(solution)/shard_map/ppermute | solution.py:155
  84.3 10.9 %collective-permute-start.26 = (bf16[48,3072]{1,0:T(8,128)(2,1)S(1)}, bf16[48,3072]{1,0:T(8,128)(2,1)S(1)}, u32[]{:S(2)}, u32[]{:S(2)}) collective-permute-start(bf16[48,3072]{1,0:T(8,128)(2,1)S(1)} %add_convert_fusion.4), channel_id=1, source_target_pairs={{2,0},{4,2},{6,4},{7,6},{5,7},{3,5},{1,3},{0,1},{10,8},{12,10},{14... | collective-permute-start | bytes 884744 | tf_op jit(solution)/shard_map/ppermute | solution.py:155
  88.9 10.1 %collective-permute-start.19 = (bf16[48,3072]{1,0:T(8,128)(2,1)S(1)}, bf16[48,3072]{1,0:T(8,128)(2,1)S(1)}, u32[]{:S(2)}, u32[]{:S(2)}) collective-permute-start(bf16[48,3072]{1,0:T(8,128)(2,1)S(1)} %add_convert_fusion.9), channel_id=1, source_target_pairs={{0,2},{2,4},{4,6},{6,7},{7,5},{5,3},{3,1},{1,0},{8,10},{10,12},{12... | collective-permute-start | bytes 884744 | tf_op jit(solution)/shard_map/ppermute | solution.py:155
  90.6 10.9 %collective-permute-start.20 = (bf16[48,3072]{1,0:T(8,128)(2,1)S(1)}, bf16[48,3072]{1,0:T(8,128)(2,1)S(1)}, u32[]{:S(2)}, u32[]{:S(2)}) collective-permute-start(bf16[48,3072]{1,0:T(8,128)(2,1)S(1)} %add_convert_fusion.8), channel_id=1, source_target_pairs={{2,0},{4,2},{6,4},{7,6},{5,7},{3,5},{1,3},{0,1},{10,8},{12,10},{14... | collective-permute-start | bytes 884744 | tf_op jit(solution)/shard_map/ppermute | solution.py:155
  95.2 9.4 %collective-permute-start.28 = (bf16[48,3072]{1,0:T(8,128)(2,1)S(1)}, bf16[48,3072]{1,0:T(8,128)(2,1)S(1)}, u32[]{:S(2)}, u32[]{:S(2)}) collective-permute-start(bf16[48,3072]{1,0:T(8,128)(2,1)S(1)} %add_convert_fusion.2), channel_id=1, source_target_pairs={{2,0},{4,2},{6,4},{7,6},{5,7},{3,5},{1,3},{0,1},{10,8},{12,10},{14... | collective-permute-start | bytes 884744 | tf_op jit(solution)/shard_map/ppermute | solution.py:155
  95.4 9.2 %collective-permute-start.27 = (bf16[48,3072]{1,0:T(8,128)(2,1)S(1)}, bf16[48,3072]{1,0:T(8,128)(2,1)S(1)}, u32[]{:S(2)}, u32[]{:S(2)}) collective-permute-start(bf16[48,3072]{1,0:T(8,128)(2,1)S(1)} %add_convert_fusion.3), channel_id=1, source_target_pairs={{0,2},{2,4},{4,6},{6,7},{7,5},{5,3},{3,1},{1,0},{8,10},{10,12},{12... | collective-permute-start | bytes 884744 | tf_op jit(solution)/shard_map/ppermute | solution.py:155
  101.5 6.8 %collective-permute-start.22 = (bf16[48,3072]{1,0:T(8,128)(2,1)S(1)}, bf16[48,3072]{1,0:T(8,128)(2,1)S(1)}, u32[]{:S(2)}, u32[]{:S(2)}) collective-permute-start(bf16[48,3072]{1,0:T(8,128)(2,1)S(1)} %add_convert_fusion.6), channel_id=1, source_target_pairs={{2,0},{4,2},{6,4},{7,6},{5,7},{3,5},{1,3},{0,1},{10,8},{12,10},{14... | collective-permute-start | bytes 884744 | tf_op jit(solution)/shard_map/ppermute | solution.py:155
  101.7 6.8 %collective-permute-start.21 = (bf16[48,3072]{1,0:T(8,128)(2,1)S(1)}, bf16[48,3072]{1,0:T(8,128)(2,1)S(1)}, u32[]{:S(2)}, u32[]{:S(2)}) collective-permute-start(bf16[48,3072]{1,0:T(8,128)(2,1)S(1)} %add_convert_fusion.7), channel_id=1, source_target_pairs={{0,2},{2,4},{4,6},{6,7},{7,5},{5,3},{3,1},{1,0},{8,10},{10,12},{12... | collective-permute-start | bytes 884744 | tf_op jit(solution)/shard_map/ppermute | solution.py:155
  108.7 1.6 %collective-permute-start.29 = (bf16[24,6144]{1,0:T(8,128)(2,1)S(1)}, bf16[24,6144]{1,0:T(8,128)(2,1)S(1)}, u32[]{:S(2)}, u32[]{:S(2)}) collective-permute-start(bf16[24,6144]{1,0:T(8,128)(2,1)S(1)} %get-tuple-element.142), channel_id=1, source_target_pairs={{0,8},{8,0},{1,9},{9,1},{2,10},{10,2},{3,11},{11,3},{4,12},{12,4},... | collective-permute-start | bytes 884744 | tf_op jit(solution)/shard_map/ppermute | solution.py:249

commit v9 on v8

--- a/solution.py
+++ b/solution.py
@@ -59,18 +59,15 @@
 
 
 def accumulate(chunks, products):
-    for _, total in products:
-        total[...] = jnp.zeros_like(total)
+    size, width = chunks[0][0].shape
+    depth = width if size * len(chunks[0]) <= 512 else TILE
     for c, blocks in enumerate(chunks):
-        width = blocks[0].shape[1]
-
-        @pl.loop(0, width // TILE)
-        def _(i):
-            at = pl.multiple_of(i * TILE, TILE)
-            rows = jnp.concatenate([block[:, pl.ds(at, TILE)] for block in blocks], axis=0)
+        for at in range(0, width, depth):
+            rows = jnp.concatenate([block[:, at:at + depth] for block in blocks], axis=0)
+            above = c * width + at
             for weights, total in products:
-                below = weights[0, pl.ds(pl.multiple_of(c * width + at, TILE), TILE), :]
-                total[...] += jnp.dot(rows, below, preferred_element_type=jnp.float32)
+                part = jnp.dot(rows, weights[0, above:above + depth, :], preferred_element_type=jnp.float32)
+                total[...] = total[...] + part if above else part
 
 
 def activated(gate, up):
@@ -180,7 +177,7 @@
     b = step(halves[1], halves[0])
     gate_here = fetched(w_gate)
     a, gate_here = tied(a, gate_here)
-    b, w_up = tied(b, w_up)
+    a, w_up = tied(a, w_up)
     up_here = fetched(w_up)
     b, up_here = tied(b, up_here)
     arrived(a, b)

time: 112 us -> 111 us (level)
  Pallas kernels: 36.7 us -> 31.2 us
  waiting for transfers between devices: 39.9 us -> 44.9 us
    ppermute x14, starting transfers between devices: 11.3 us -> 21.6 us  [step(): lax.ppermute(to_left, 'tensor', left)]
    ppermute x14, starting transfers between devices: 18.7 us -> 8.44 us  [step(): lax.ppermute(to_right, 'tensor', right)]
    ppermute x14, waiting for transfers between devices: 16.5 us -> 26.4 us  [step(): lax.ppermute(to_right, 'tensor', right)]
    pallas_call x6, Pallas kernels: 36.7 us -> 31.2 us  [call(): pl.pallas_call(kernel, in_specs=[pl.BlockSpec(memory_space=memory) for _,...]
    ppermute x14, waiting for transfers between devices: 20.8 us -> 15.8 us  [step(): lax.ppermute(to_left, 'tensor', left)]
  transfers between devices with their start and end apart: 30 -> 30, of which waited for: 19 -> 19; matrix products, arithmetic and copies ran while one was open for 1% -> 1% of each run, Pallas kernels for 24% -> 20%
where the time goes in v9:
time: 111 us
  waiting for transfers between devices  44.9 us (40%)
  Pallas kernels  31.2 us (28%)
  starting transfers between devices  30.7 us (28%)
  other arithmetic  2.19 us (2%)
  matrix products  1.58 us (1%)
    pallas_call x6, Pallas kernels, call(): pl.pallas_call(kernel, in_specs=[pl.BlockSpec(memory_space=memory) for _,...  31.2 us
    ppermute x14, waiting for transfers between devices, step(): lax.ppermute(to_right, 'tensor', right)  26.4 us
    ppermute x14, starting transfers between devices, step(): lax.ppermute(to_left, 'tensor', left)  21.6 us
    ppermute x14, waiting for transfers between devices, step(): lax.ppermute(to_left, 'tensor', left)  15.8 us
    ppermute x14, starting transfers between devices, step(): lax.ppermute(to_right, 'tensor', right)  8.44 us
  transfers between devices with their start and end apart: 30, of which 19 were waited for; matrix products, arithmetic and copies ran while one was open for 1% of the time, Pallas kernels for 20%

profile of v9, /device:TPU:0, one launch (start us, length us, event | category | flops | bytes accessed | tf_op | source)
XLA Modules:
  0.0 111.1 jit_solution(3834539904056146519)
XLA Ops:
  0.0 0.1 eq.64
  0.1 0.1 pad_add_fusion
  0.2 0.8 compare_reduce_fusion
  1.0 0.1 copy.17
  1.1 0.1 reduce_window_sum.11
  1.3 0.1 fusion.9
  1.4 0.3 convolution_convert_fusion
  1.7 0.5 collective-permute-start
  2.3 1.2 %collective-permute-done = bf16[24,6144]{1,0:T(8,128)(2,1)S(1)} collective-permute-done((bf16[24,6144]{1,0:T(8,128)(2,1)S(1)}, bf16[24,6144]{1,0:T(8,128)(2,1)S(1)}, u32[]{:S(2)}, u32[]{:S(2)}) %collective-permute-start) | collective-permute-done | bytes 294944 | tf_op jit(solution)/shard_map/ppermute | solution.py:166
  3.6 2.9 %collective-permute-start.2 = (bf16[48,3072]{1,0:T(8,128)(2,1)S(1)}, bf16[48,3072]{1,0:T(8,128)(2,1)S(1)}, u32[]{:S(2)}, u32[]{:S(2)}) collective-permute-start(bf16[48,3072]{1,0:T(8,128)(2,1)S(1)} %get-tuple-element.143.refs_5_), channel_id=1, source_target_pairs={{2,0},{4,2},{6,4},{7,6},{5,7},{3,5},{1,3},{0,1},{10,8},{12,10},{14... | collective-permute-start | bytes 884744 | tf_op jit(solution)/shard_map/ppermute | solution.py:152
  6.5 0.1 collective-permute-start.1
  6.6 2.0 %collective-permute-start.7 = (bf16[48,3072]{1,0:T(8,128)(2,1)S(1)}, bf16[48,3072]{1,0:T(8,128)(2,1)S(1)}, u32[]{:S(2)}, u32[]{:S(2)}) collective-permute-start(bf16[48,3072]{1,0:T(8,128)(2,1)S(1)} %get-tuple-element.143.refs_5_), channel_id=1, source_target_pairs={{0,2},{2,4},{4,6},{6,7},{7,5},{5,3},{3,1},{1,0},{8,10},{10,12},{12... | collective-permute-start | bytes 884744 | tf_op jit(solution)/shard_map/ppermute | solution.py:152
  8.6 4.7 %fetched.2.refs_10_.refs_6_ = bf16[1,6144,1024]{2,1,0:T(8,128)(2,1)S(1)} custom-call(bf16[1,6144,1024]{2,1,0:T(8,128)(2,1)} %source), custom_call_target="tpu_custom_call" | custom-call | flops 1024 | bytes 1024 | tf_op jit(solution)/shard_map/fetched/pallas_call | solution.py:29
  13.4 1.0 collective-permute-done.2.refs_7_
  14.3 2.0 %collective-permute-done.1.refs_1_ = bf16[48,3072]{1,0:T(8,128)(2,1)S(1)} collective-permute-done((bf16[48,3072]{1,0:T(8,128)(2,1)S(1)}, bf16[48,3072]{1,0:T(8,128)(2,1)S(1)}, u32[]{:S(2)}, u32[]{:S(2)}) %collective-permute-start.1) | collective-permute-done | bytes 294944 | tf_op jit(solution)/shard_map/ppermute | solution.py:152
  16.4 0.1 collective-permute-start.3
  16.5 1.9 %collective-permute-start.4 = (bf16[48,3072]{1,0:T(8,128)(2,1)S(1)}, bf16[48,3072]{1,0:T(8,128)(2,1)S(1)}, u32[]{:S(2)}, u32[]{:S(2)}) collective-permute-start(bf16[48,3072]{1,0:T(8,128)(2,1)S(1)} %collective-permute-done.2.refs_7_), channel_id=1, source_target_pairs={{2,0},{4,2},{6,4},{7,6},{5,7},{3,5},{1,3},{0,1},{10,8},{12,10},{14... | collective-permute-start | bytes 884744 | tf_op jit(solution)/shard_map/ppermute | solution.py:152
  18.4 4.7 %fetched.3.refs_10_.refs_7_ = bf16[1,6144,1024]{2,1,0:T(8,128)(2,1)S(1)} custom-call(bf16[1,6144,1024]{2,1,0:T(8,128)(2,1)} %source.1), custom_call_target="tpu_custom_call" | custom-call | flops 1024 | bytes 1024 | tf_op jit(solution)/shard_map/fetched/pallas_call | solution.py:29
  23.2 0.1 collective-permute-start.9
  23.3 1.9 %collective-permute-start.10 = (bf16[48,3072]{1,0:T(8,128)(2,1)S(1)}, bf16[48,3072]{1,0:T(8,128)(2,1)S(1)}, u32[]{:S(2)}, u32[]{:S(2)}) collective-permute-start(bf16[48,3072]{1,0:T(8,128)(2,1)S(1)} %collective-permute-done.8.refs_2_), channel_id=1, source_target_pairs={{2,0},{4,2},{6,4},{7,6},{5,7},{3,5},{1,3},{0,1},{10,8},{12,10},{14... | collective-permute-start | bytes 884744 | tf_op jit(solution)/shard_map/ppermute | solution.py:152
  25.2 3.8 %collective-permute-done.3.refs_3_ = bf16[48,3072]{1,0:T(8,128)(2,1)S(1)} collective-permute-done((bf16[48,3072]{1,0:T(8,128)(2,1)S(1)}, bf16[48,3072]{1,0:T(8,128)(2,1)S(1)}, u32[]{:S(2)}, u32[]{:S(2)}) %collective-permute-start.3) | collective-permute-done | bytes 294944 | tf_op jit(solution)/shard_map/ppermute | solution.py:152
  29.0 0.1 collective-permute-start.5
  29.1 1.9 %collective-permute-start.6 = (bf16[48,3072]{1,0:T(8,128)(2,1)S(1)}, bf16[48,3072]{1,0:T(8,128)(2,1)S(1)}, u32[]{:S(2)}, u32[]{:S(2)}) collective-permute-start(bf16[48,3072]{1,0:T(8,128)(2,1)S(1)} %collective-permute-done.4.refs_9_), channel_id=1, source_target_pairs={{2,0},{4,2},{6,4},{7,6},{5,7},{3,5},{1,3},{0,1},{10,8},{12,10},{14... | collective-permute-start | bytes 884744 | tf_op jit(solution)/shard_map/ppermute | solution.py:152
  31.1 4.3 %collective-permute-done.9.refs_8_ = bf16[48,3072]{1,0:T(8,128)(2,1)S(1)} collective-permute-done((bf16[48,3072]{1,0:T(8,128)(2,1)S(1)}, bf16[48,3072]{1,0:T(8,128)(2,1)S(1)}, u32[]{:S(2)}, u32[]{:S(2)}) %collective-permute-start.9) | collective-permute-done | bytes 294944 | tf_op jit(solution)/shard_map/ppermute | solution.py:152
  35.4 3.2 %near_gate.1.refs_11_ = f32[240,1024]{1,0:T(8,128)S(1)} custom-call(bf16[48,3072]{1,0:T(8,128)(2,1)S(1)} %get-tuple-element.144.refs_0_, bf16[48,3072]{1,0:T(8,128)(2,1)S(1)} %collective-permute-done.1.refs_1_, bf16[48,3072]{1,0:T(8,128)(2,1)S(1)} %collective-permute-done.8.refs_2_, bf16[48,3072]{1,0:T(8,128)(2,1)S(1)} %collective-permute-done.3.refs_3_, ...), custom_call_target="tpu_custom_call" | custom-call | flops 1024 | bytes 1024 | tf_op jit(solution)/shard_map/near_gate/pallas_call | solution.py:29
  38.6 0.1 collective-permute-start.11
  38.7 1.9 %collective-permute-start.12 = (bf16[48,3072]{1,0:T(8,128)(2,1)S(1)}, bf16[48,3072]{1,0:T(8,128)(2,1)S(1)}, u32[]{:S(2)}, u32[]{:S(2)}) collective-permute-start(bf16[48,3072]{1,0:T(8,128)(2,1)S(1)} %collective-permute-done.10.refs_4_), channel_id=1, source_target_pairs={{2,0},{4,2},{6,4},{7,6},{5,7},{3,5},{1,3},{0,1},{10,8},{12,10},{14... | collective-permute-start | bytes 884744 | tf_op jit(solution)/shard_map/ppermute | solution.py:152
  40.6 1.0 collective-permute-done.5.refs_0_
  41.7 0.1 collective-permute-start.13
  41.8 1.9 %collective-permute-start.14 = (bf16[48,3072]{1,0:T(8,128)(2,1)S(1)}, bf16[48,3072]{1,0:T(8,128)(2,1)S(1)}, u32[]{:S(2)}, u32[]{:S(2)}) collective-permute-start(bf16[48,3072]{1,0:T(8,128)(2,1)S(1)} %collective-permute-done.6.refs_4_), channel_id=1, source_target_pairs={{2,0},{4,2},{6,4},{7,6},{5,7},{3,5},{1,3},{0,1},{10,8},{12,10},{14... | collective-permute-start | bytes 884744 | tf_op jit(solution)/shard_map/ppermute | solution.py:152
  43.7 3.2 %near_up.1.hidden = bf16[240,1024]{1,0:T(8,128)(2,1)S(1)} custom-call(bf16[48,3072]{1,0:T(8,128)(2,1)S(1)} %get-tuple-element.144.refs_0_, bf16[48,3072]{1,0:T(8,128)(2,1)S(1)} %collective-permute-done.1.refs_1_, bf16[48,3072]{1,0:T(8,128)(2,1)S(1)} %collective-permute-done.8.refs_2_, bf16[48,3072]{1,0:T(8,128)(2,1)S(1)} %collective-permute-done.3.refs_3_, ...), custom_call_target="tpu_custom_call" | custom-call | flops 1024 | bytes 1024 | tf_op jit(solution)/shard_map/near_up/pallas_call | solution.py:29
  46.9 1.6 %collective-permute-done.11.refs_3_ = bf16[48,3072]{1,0:T(8,128)(2,1)S(1)} collective-permute-done((bf16[48,3072]{1,0:T(8,128)(2,1)S(1)}, bf16[48,3072]{1,0:T(8,128)(2,1)S(1)}, u32[]{:S(2)}, u32[]{:S(2)}) %collective-permute-start.11) | collective-permute-done | bytes 294944 | tf_op jit(solution)/shard_map/ppermute | solution.py:152
  48.6 0.1 collective-permute-done.12.refs_1_
  48.6 4.6 %collective-permute-done.13.refs_2_ = bf16[48,3072]{1,0:T(8,128)(2,1)S(1)} collective-permute-done((bf16[48,3072]{1,0:T(8,128)(2,1)S(1)}, bf16[48,3072]{1,0:T(8,128)(2,1)S(1)}, u32[]{:S(2)}, u32[]{:S(2)}) %collective-permute-start.13) | collective-permute-done | bytes 294944 | tf_op jit(solution)/shard_map/ppermute | solution.py:152
  53.2 8.9 %rest.1 = (bf16[48,3072]{1,0:T(8,128)(2,1)S(1)}, bf16[48,3072]{1,0:T(8,128)(2,1)S(1)}, bf16[48,3072]{1,0:T(8,128)(2,1)S(1)}, bf16[48,3072]{1,0:T(8,128)(2,1)S(1)...) custom-call(bf16[48,3072]{1,0:T(8,128)(2,1)S(1)} %collective-permute-done.5.refs_0_, ...), custom_call_target="tpu_custom_call" | custom-call | flops 1024 | bytes 1024 | tf_op jit(solution)/shard_map/rest/pallas_call | solution.py:29
  62.1 0.5 collective-permute-start.15
  62.7 1.6 %collective-permute-start.16 = (bf16[48,3072]{1,0:T(8,128)(2,1)S(1)}, bf16[48,3072]{1,0:T(8,128)(2,1)S(1)}, u32[]{:S(2)}, u32[]{:S(2)}) collective-permute-start(bf16[48,3072]{1,0:T(8,128)(2,1)S(1)} %get-tuple-element.116), channel_id=1, source_target_pairs={{2,0},{4,2},{6,4},{7,6},{5,7},{3,5},{1,3},{0,1},{10,8},{12,10},{14... | collective-permute-start | bytes 884744 | tf_op jit(solution)/shard_map/ppermute | solution.py:152
  64.2 0.5 collective-permute-start.23
  64.7 1.6 %collective-permute-start.24 = (bf16[48,3072]{1,0:T(8,128)(2,1)S(1)}, bf16[48,3072]{1,0:T(8,128)(2,1)S(1)}, u32[]{:S(2)}, u32[]{:S(2)}) collective-permute-start(bf16[48,3072]{1,0:T(8,128)(2,1)S(1)} %get-tuple-element.130), channel_id=1, source_target_pairs={{2,0},{4,2},{6,4},{7,6},{5,7},{3,5},{1,3},{0,1},{10,8},{12,10},{14... | collective-permute-start | bytes 884744 | tf_op jit(solution)/shard_map/ppermute | solution.py:152
  66.3 6.4 %near_down.1 = (bf16[48,3072]{1,0:T(8,128)(2,1)S(1)}, bf16[48,3072]{1,0:T(8,128)(2,1)S(1)}, bf16[48,3072]{1,0:T(8,128)(2,1)S(1)}, bf16[48,3072]{1,0:T(8,128)(2,1...) custom-call(bf16[240,1024]{1,0:T(8,128)(2,1)S(1)} %near_up.1.hidden,, ...), custom_call_target="tpu_custom_call" | custom-call | flops 1024 | bytes 1024 | tf_op jit(solution)/shard_map/near_down/pallas_call | solution.py:29
  72.8 1.6 %collective-permute-start.18 = (bf16[48,3072]{1,0:T(8,128)(2,1)S(1)}, bf16[48,3072]{1,0:T(8,128)(2,1)S(1)}, u32[]{:S(2)}, u32[]{:S(2)}) collective-permute-start(bf16[48,3072]{1,0:T(8,128)(2,1)S(1)} %add_convert_fusion.10), channel_id=1, source_target_pairs={{2,0},{4,2},{6,4},{7,6},{5,7},{3,5},{1,3},{0,1},{10,8},{12,10},{14... | collective-permute-start | bytes 884744 | tf_op jit(solution)/shard_map/ppermute | solution.py:152
  74.5 0.5 collective-permute-start.17
  75.0 2.5 %collective-permute-done.23 = bf16[48,3072]{1,0:T(8,128)(2,1)S(1)} collective-permute-done((bf16[48,3072]{1,0:T(8,128)(2,1)S(1)}, bf16[48,3072]{1,0:T(8,128)(2,1)S(1)}, u32[]{:S(2)}, u32[]{:S(2)}) %collective-permute-start.23) | collective-permute-done | bytes 294944 | tf_op jit(solution)/shard_map/ppermute | solution.py:152
  77.5 1.5 %collective-permute-done.24 = bf16[48,3072]{1,0:T(8,128)(2,1)S(1)} collective-permute-done((bf16[48,3072]{1,0:T(8,128)(2,1)S(1)}, bf16[48,3072]{1,0:T(8,128)(2,1)S(1)}, u32[]{:S(2)}, u32[]{:S(2)}) %collective-permute-start.24) | collective-permute-done | bytes 294944 | tf_op jit(solution)/shard_map/ppermute | solution.py:152
  79.0 1.7 %collective-permute-start.25 = (bf16[48,3072]{1,0:T(8,128)(2,1)S(1)}, bf16[48,3072]{1,0:T(8,128)(2,1)S(1)}, u32[]{:S(2)}, u32[]{:S(2)}) collective-permute-start(bf16[48,3072]{1,0:T(8,128)(2,1)S(1)} %add_convert_fusion.5), channel_id=1, source_target_pairs={{0,2},{2,4},{4,6},{6,7},{7,5},{5,3},{3,1},{1,0},{8,10},{10,12},{12... | collective-permute-start | bytes 884744 | tf_op jit(solution)/shard_map/ppermute | solution.py:152
  80.7 0.5 collective-permute-start.26
  81.2 4.0 %collective-permute-done.18 = bf16[48,3072]{1,0:T(8,128)(2,1)S(1)} collective-permute-done((bf16[48,3072]{1,0:T(8,128)(2,1)S(1)}, bf16[48,3072]{1,0:T(8,128)(2,1)S(1)}, u32[]{:S(2)}, u32[]{:S(2)}) %collective-permute-start.18) | collective-permute-done | bytes 294944 | tf_op jit(solution)/shard_map/ppermute | solution.py:152
  85.3 0.1 add_convert_fusion.9
  85.3 1.7 %collective-permute-start.19 = (bf16[48,3072]{1,0:T(8,128)(2,1)S(1)}, bf16[48,3072]{1,0:T(8,128)(2,1)S(1)}, u32[]{:S(2)}, u32[]{:S(2)}) collective-permute-start(bf16[48,3072]{1,0:T(8,128)(2,1)S(1)} %add_convert_fusion.9), channel_id=1, source_target_pairs={{0,2},{2,4},{4,6},{6,7},{7,5},{5,3},{3,1},{1,0},{8,10},{10,12},{12... | collective-permute-start | bytes 884744 | tf_op jit(solution)/shard_map/ppermute | solution.py:152
  87.1 0.5 collective-permute-start.20
  87.5 3.3 %collective-permute-done.25 = bf16[48,3072]{1,0:T(8,128)(2,1)S(1)} collective-permute-done((bf16[48,3072]{1,0:T(8,128)(2,1)S(1)}, bf16[48,3072]{1,0:T(8,128)(2,1)S(1)}, u32[]{:S(2)}, u32[]{:S(2)}) %collective-permute-start.25) | collective-permute-done | bytes 294944 | tf_op jit(solution)/shard_map/ppermute | solution.py:152
  90.8 0.8 collective-permute-done.26
  91.6 1.6 %collective-permute-start.28 = (bf16[48,3072]{1,0:T(8,128)(2,1)S(1)}, bf16[48,3072]{1,0:T(8,128)(2,1)S(1)}, u32[]{:S(2)}, u32[]{:S(2)}) collective-permute-start(bf16[48,3072]{1,0:T(8,128)(2,1)S(1)} %add_convert_fusion.2), channel_id=1, source_target_pairs={{2,0},{4,2},{6,4},{7,6},{5,7},{3,5},{1,3},{0,1},{10,8},{12,10},{14... | collective-permute-start | bytes 884744 | tf_op jit(solution)/shard_map/ppermute | solution.py:152
  93.3 0.5 collective-permute-start.27
  93.9 3.3 %collective-permute-done.19 = bf16[48,3072]{1,0:T(8,128)(2,1)S(1)} collective-permute-done((bf16[48,3072]{1,0:T(8,128)(2,1)S(1)}, bf16[48,3072]{1,0:T(8,128)(2,1)S(1)}, u32[]{:S(2)}, u32[]{:S(2)}) %collective-permute-start.19) | collective-permute-done | bytes 294944 | tf_op jit(solution)/shard_map/ppermute | solution.py:152
  97.1 0.8 collective-permute-done.20
  98.0 1.6 %collective-permute-start.22 = (bf16[48,3072]{1,0:T(8,128)(2,1)S(1)}, bf16[48,3072]{1,0:T(8,128)(2,1)S(1)}, u32[]{:S(2)}, u32[]{:S(2)}) collective-permute-start(bf16[48,3072]{1,0:T(8,128)(2,1)S(1)} %add_convert_fusion.6), channel_id=1, source_target_pairs={{2,0},{4,2},{6,4},{7,6},{5,7},{3,5},{1,3},{0,1},{10,8},{12,10},{14... | collective-permute-start | bytes 884744 | tf_op jit(solution)/shard_map/ppermute | solution.py:152
  99.7 0.5 collective-permute-start.21
  100.2 4.0 %collective-permute-done.28 = bf16[48,3072]{1,0:T(8,128)(2,1)S(1)} collective-permute-done((bf16[48,3072]{1,0:T(8,128)(2,1)S(1)}, bf16[48,3072]{1,0:T(8,128)(2,1)S(1)}, u32[]{:S(2)}, u32[]{:S(2)}) %collective-permute-start.28) | collective-permute-done | bytes 294944 | tf_op jit(solution)/shard_map/ppermute | solution.py:152
  104.2 3.7 %collective-permute-done.22 = bf16[48,3072]{1,0:T(8,128)(2,1)S(1)} collective-permute-done((bf16[48,3072]{1,0:T(8,128)(2,1)S(1)}, bf16[48,3072]{1,0:T(8,128)(2,1)S(1)}, u32[]{:S(2)}, u32[]{:S(2)}) %collective-permute-start.22) | collective-permute-done | bytes 294944 | tf_op jit(solution)/shard_map/ppermute | solution.py:152
  107.9 0.2 add_convert_fusion
  108.3 0.1 fusion.14
  108.3 1.5 %collective-permute-done.29 = bf16[24,6144]{1,0:T(8,128)(2,1)S(1)} collective-permute-done((bf16[24,6144]{1,0:T(8,128)(2,1)S(1)}, bf16[24,6144]{1,0:T(8,128)(2,1)S(1)}, u32[]{:S(2)}, u32[]{:S(2)}) %collective-permute-start.29) | collective-permute-done | bytes 294944 | tf_op jit(solution)/shard_map/ppermute | solution.py:246
  109.8 1.3 %fusion = bf16[64,6144]{1,0:T(8,128)(2,1)} fusion(bf16[1,24,6144]{2,1,0:T(8,128)(2,1)S(1)} %bitcast.22, bf16[1,24,6144]{2,1,0:T(8,128)(2,1)S(1)} %get-tuple-element.141, bf16[2,64]{1,0:T(2,128)(2,1)S(1)} %bitcast.23, s32[2,64]{1,0:T(2,128)S(1)} %subtract_bitcast_fusion, pred[2,64]{1,0:T(4,128)(4,1)S(1)} %get-tuple-element.147), kind=kOutput, calls=%fused_computation.1 | convolution fusion | flops 38052864 | bytes 1377152 | tf_op jit(solution)/shard_map/wcr,wcd->rd/dot_general | solution.py:248
  (38 shorter events, 1.1 us)
Async XLA Ops:
  0.0 1.4 %copy-start = (bf16[64,6144]{1,0:T(8,128)(2,1)S(1)}, bf16[64,6144]{1,0:T(8,128)(2,1)}, u32[]{:S(2)}) copy-start(bf16[64,6144]{1,0:T(8,128)(2,1)} %param.6) | copy-start | bytes 2359300
  1.7 1.7 %collective-permute-start = (bf16[24,6144]{1,0:T(8,128)(2,1)S(1)}, bf16[24,6144]{1,0:T(8,128)(2,1)S(1)}, u32[]{:S(2)}, u32[]{:S(2)}) collective-permute-start(bf16[24,6144]{1,0:T(8,128)(2,1)S(1)} %get-tuple-element.146), channel_id=1, source_target_pairs={{0,8},{8,0},{1,9},{9,1},{2,10},{10,2},{3,11},{11,3},{4,12},{12,4},... | collective-permute-start | bytes 884744 | tf_op jit(solution)/shard_map/ppermute | solution.py:166
  3.6 10.8 %collective-permute-start.2 = (bf16[48,3072]{1,0:T(8,128)(2,1)S(1)}, bf16[48,3072]{1,0:T(8,128)(2,1)S(1)}, u32[]{:S(2)}, u32[]{:S(2)}) collective-permute-start(bf16[48,3072]{1,0:T(8,128)(2,1)S(1)} %get-tuple-element.143.refs_5_), channel_id=1, source_target_pairs={{2,0},{4,2},{6,4},{7,6},{5,7},{3,5},{1,3},{0,1},{10,8},{12,10},{14... | collective-permute-start | bytes 884744 | tf_op jit(solution)/shard_map/ppermute | solution.py:152
  6.5 9.9 %collective-permute-start.1 = (bf16[48,3072]{1,0:T(8,128)(2,1)S(1)}, bf16[48,3072]{1,0:T(8,128)(2,1)S(1)}, u32[]{:S(2)}, u32[]{:S(2)}) collective-permute-start(bf16[48,3072]{1,0:T(8,128)(2,1)S(1)} %get-tuple-element.144.refs_0_), channel_id=1, source_target_pairs={{0,2},{2,4},{4,6},{6,7},{7,5},{5,3},{3,1},{1,0},{8,10},{10,12},{12... | collective-permute-start | bytes 884744 | tf_op jit(solution)/shard_map/ppermute | solution.py:152
  6.6 16.5 %collective-permute-start.7 = (bf16[48,3072]{1,0:T(8,128)(2,1)S(1)}, bf16[48,3072]{1,0:T(8,128)(2,1)S(1)}, u32[]{:S(2)}, u32[]{:S(2)}) collective-permute-start(bf16[48,3072]{1,0:T(8,128)(2,1)S(1)} %get-tuple-element.143.refs_5_), channel_id=1, source_target_pairs={{0,2},{2,4},{4,6},{6,7},{7,5},{5,3},{3,1},{1,0},{8,10},{10,12},{12... | collective-permute-start | bytes 884744 | tf_op jit(solution)/shard_map/ppermute | solution.py:152
  8.6 14.6 %collective-permute-start.8 = (bf16[48,3072]{1,0:T(8,128)(2,1)S(1)}, bf16[48,3072]{1,0:T(8,128)(2,1)S(1)}, u32[]{:S(2)}, u32[]{:S(2)}) collective-permute-start(bf16[48,3072]{1,0:T(8,128)(2,1)S(1)} %get-tuple-element.144.refs_0_), channel_id=1, source_target_pairs={{2,0},{4,2},{6,4},{7,6},{5,7},{3,5},{1,3},{0,1},{10,8},{12,10},{14... | collective-permute-start | bytes 884744 | tf_op jit(solution)/shard_map/ppermute | solution.py:152
  16.4 12.6 %collective-permute-start.3 = (bf16[48,3072]{1,0:T(8,128)(2,1)S(1)}, bf16[48,3072]{1,0:T(8,128)(2,1)S(1)}, u32[]{:S(2)}, u32[]{:S(2)}) collective-permute-start(bf16[48,3072]{1,0:T(8,128)(2,1)S(1)} %collective-permute-done.1.refs_1_), channel_id=1, source_target_pairs={{0,2},{2,4},{4,6},{6,7},{7,5},{5,3},{3,1},{1,0},{8,10},{10,12},{12... | collective-permute-start | bytes 884744 | tf_op jit(solution)/shard_map/ppermute | solution.py:152
  16.5 12.6 %collective-permute-start.4 = (bf16[48,3072]{1,0:T(8,128)(2,1)S(1)}, bf16[48,3072]{1,0:T(8,128)(2,1)S(1)}, u32[]{:S(2)}, u32[]{:S(2)}) collective-permute-start(bf16[48,3072]{1,0:T(8,128)(2,1)S(1)} %collective-permute-done.2.refs_7_), channel_id=1, source_target_pairs={{2,0},{4,2},{6,4},{7,6},{5,7},{3,5},{1,3},{0,1},{10,8},{12,10},{14... | collective-permute-start | bytes 884744 | tf_op jit(solution)/shard_map/ppermute | solution.py:152
  23.2 12.2 %collective-permute-start.9 = (bf16[48,3072]{1,0:T(8,128)(2,1)S(1)}, bf16[48,3072]{1,0:T(8,128)(2,1)S(1)}, u32[]{:S(2)}, u32[]{:S(2)}) collective-permute-start(bf16[48,3072]{1,0:T(8,128)(2,1)S(1)} %collective-permute-done.7.refs_6_), channel_id=1, source_target_pairs={{0,2},{2,4},{4,6},{6,7},{7,5},{5,3},{3,1},{1,0},{8,10},{10,12},{12... | collective-permute-start | bytes 884744 | tf_op jit(solution)/shard_map/ppermute | solution.py:152
  23.3 12.1 %collective-permute-start.10 = (bf16[48,3072]{1,0:T(8,128)(2,1)S(1)}, bf16[48,3072]{1,0:T(8,128)(2,1)S(1)}, u32[]{:S(2)}, u32[]{:S(2)}) collective-permute-start(bf16[48,3072]{1,0:T(8,128)(2,1)S(1)} %collective-permute-done.8.refs_2_), channel_id=1, source_target_pairs={{2,0},{4,2},{6,4},{7,6},{5,7},{3,5},{1,3},{0,1},{10,8},{12,10},{14... | collective-permute-start | bytes 884744 | tf_op jit(solution)/shard_map/ppermute | solution.py:152
  29.0 12.6 %collective-permute-start.5 = (bf16[48,3072]{1,0:T(8,128)(2,1)S(1)}, bf16[48,3072]{1,0:T(8,128)(2,1)S(1)}, u32[]{:S(2)}, u32[]{:S(2)}) collective-permute-start(bf16[48,3072]{1,0:T(8,128)(2,1)S(1)} %collective-permute-done.3.refs_3_), channel_id=1, source_target_pairs={{0,2},{2,4},{4,6},{6,7},{7,5},{5,3},{3,1},{1,0},{8,10},{10,12},{12... | collective-permute-start | bytes 884744 | tf_op jit(solution)/shard_map/ppermute | solution.py:152
  29.1 12.6 %collective-permute-start.6 = (bf16[48,3072]{1,0:T(8,128)(2,1)S(1)}, bf16[48,3072]{1,0:T(8,128)(2,1)S(1)}, u32[]{:S(2)}, u32[]{:S(2)}) collective-permute-start(bf16[48,3072]{1,0:T(8,128)(2,1)S(1)} %collective-permute-done.4.refs_9_), channel_id=1, source_target_pairs={{2,0},{4,2},{6,4},{7,6},{5,7},{3,5},{1,3},{0,1},{10,8},{12,10},{14... | collective-permute-start | bytes 884744 | tf_op jit(solution)/shard_map/ppermute | solution.py:152
  38.6 10.0 %collective-permute-start.11 = (bf16[48,3072]{1,0:T(8,128)(2,1)S(1)}, bf16[48,3072]{1,0:T(8,128)(2,1)S(1)}, u32[]{:S(2)}, u32[]{:S(2)}) collective-permute-start(bf16[48,3072]{1,0:T(8,128)(2,1)S(1)} %collective-permute-done.9.refs_8_), channel_id=1, source_target_pairs={{0,2},{2,4},{4,6},{6,7},{7,5},{5,3},{3,1},{1,0},{8,10},{10,12},{12... | collective-permute-start | bytes 884744 | tf_op jit(solution)/shard_map/ppermute | solution.py:152
  38.7 9.9 %collective-permute-start.12 = (bf16[48,3072]{1,0:T(8,128)(2,1)S(1)}, bf16[48,3072]{1,0:T(8,128)(2,1)S(1)}, u32[]{:S(2)}, u32[]{:S(2)}) collective-permute-start(bf16[48,3072]{1,0:T(8,128)(2,1)S(1)} %collective-permute-done.10.refs_4_), channel_id=1, source_target_pairs={{2,0},{4,2},{6,4},{7,6},{5,7},{3,5},{1,3},{0,1},{10,8},{12,10},{14... | collective-permute-start | bytes 884744 | tf_op jit(solution)/shard_map/ppermute | solution.py:152
  41.7 11.5 %collective-permute-start.13 = (bf16[48,3072]{1,0:T(8,128)(2,1)S(1)}, bf16[48,3072]{1,0:T(8,128)(2,1)S(1)}, u32[]{:S(2)}, u32[]{:S(2)}) collective-permute-start(bf16[48,3072]{1,0:T(8,128)(2,1)S(1)} %collective-permute-done.5.refs_0_), channel_id=1, source_target_pairs={{0,2},{2,4},{4,6},{6,7},{7,5},{5,3},{3,1},{1,0},{8,10},{10,12},{12... | collective-permute-start | bytes 884744 | tf_op jit(solution)/shard_map/ppermute | solution.py:152
  41.8 11.4 %collective-permute-start.14 = (bf16[48,3072]{1,0:T(8,128)(2,1)S(1)}, bf16[48,3072]{1,0:T(8,128)(2,1)S(1)}, u32[]{:S(2)}, u32[]{:S(2)}) collective-permute-start(bf16[48,3072]{1,0:T(8,128)(2,1)S(1)} %collective-permute-done.6.refs_4_), channel_id=1, source_target_pairs={{2,0},{4,2},{6,4},{7,6},{5,7},{3,5},{1,3},{0,1},{10,8},{12,10},{14... | collective-permute-start | bytes 884744 | tf_op jit(solution)/shard_map/ppermute | solution.py:152
  62.1 10.5 %collective-permute-start.15 = (bf16[48,3072]{1,0:T(8,128)(2,1)S(1)}, bf16[48,3072]{1,0:T(8,128)(2,1)S(1)}, u32[]{:S(2)}, u32[]{:S(2)}) collective-permute-start(bf16[48,3072]{1,0:T(8,128)(2,1)S(1)} %get-tuple-element.115), channel_id=1, source_target_pairs={{0,2},{2,4},{4,6},{6,7},{7,5},{5,3},{3,1},{1,0},{8,10},{10,12},{12... | collective-permute-start | bytes 884744 | tf_op jit(solution)/shard_map/ppermute | solution.py:152
  62.7 10.0 %collective-permute-start.16 = (bf16[48,3072]{1,0:T(8,128)(2,1)S(1)}, bf16[48,3072]{1,0:T(8,128)(2,1)S(1)}, u32[]{:S(2)}, u32[]{:S(2)}) collective-permute-start(bf16[48,3072]{1,0:T(8,128)(2,1)S(1)} %get-tuple-element.116), channel_id=1, source_target_pairs={{2,0},{4,2},{6,4},{7,6},{5,7},{3,5},{1,3},{0,1},{10,8},{12,10},{14... | collective-permute-start | bytes 884744 | tf_op jit(solution)/shard_map/ppermute | solution.py:152
  64.2 13.2 %collective-permute-start.23 = (bf16[48,3072]{1,0:T(8,128)(2,1)S(1)}, bf16[48,3072]{1,0:T(8,128)(2,1)S(1)}, u32[]{:S(2)}, u32[]{:S(2)}) collective-permute-start(bf16[48,3072]{1,0:T(8,128)(2,1)S(1)} %get-tuple-element.129), channel_id=1, source_target_pairs={{0,2},{2,4},{4,6},{6,7},{7,5},{5,3},{3,1},{1,0},{8,10},{10,12},{12... | collective-permute-start | bytes 884744 | tf_op jit(solution)/shard_map/ppermute | solution.py:152
  64.7 46.4 %copy-start.1 = (bf16[64,6144]{1,0:T(8,128)(2,1)S(1)}, bf16[64,6144]{1,0:T(8,128)(2,1)}, u32[]{:S(2)}) copy-start(bf16[64,6144]{1,0:T(8,128)(2,1)} %param.6) | copy-start | bytes 2359300
  64.7 43.6 %copy-start.2 = (s32[64,2]{0,1:T(2,128)S(1)}, s32[64,2]{0,1:T(2,128)}, u32[]{:S(2)}) copy-start(s32[64,2]{0,1:T(2,128)} %param.7) | copy-start | bytes 1540
  64.7 43.6 %copy-start.3 = (f32[64,2]{0,1:T(2,128)S(1)}, f32[64,2]{0,1:T(2,128)}, u32[]{:S(2)}) copy-start(f32[64,2]{0,1:T(2,128)} %param.8) | copy-start | bytes 1540
  64.7 14.2 %collective-permute-start.24 = (bf16[48,3072]{1,0:T(8,128)(2,1)S(1)}, bf16[48,3072]{1,0:T(8,128)(2,1)S(1)}, u32[]{:S(2)}, u32[]{:S(2)}) collective-permute-start(bf16[48,3072]{1,0:T(8,128)(2,1)S(1)} %get-tuple-element.130), channel_id=1, source_target_pairs={{2,0},{4,2},{6,4},{7,6},{5,7},{3,5},{1,3},{0,1},{10,8},{12,10},{14... | collective-permute-start | bytes 884744 | tf_op jit(solution)/shard_map/ppermute | solution.py:152
  72.8 12.5 %collective-permute-start.18 = (bf16[48,3072]{1,0:T(8,128)(2,1)S(1)}, bf16[48,3072]{1,0:T(8,128)(2,1)S(1)}, u32[]{:S(2)}, u32[]{:S(2)}) collective-permute-start(bf16[48,3072]{1,0:T(8,128)(2,1)S(1)} %add_convert_fusion.10), channel_id=1, source_target_pairs={{2,0},{4,2},{6,4},{7,6},{5,7},{3,5},{1,3},{0,1},{10,8},{12,10},{14... | collective-permute-start | bytes 884744 | tf_op jit(solution)/shard_map/ppermute | solution.py:152
  74.5 10.8 %collective-permute-start.17 = (bf16[48,3072]{1,0:T(8,128)(2,1)S(1)}, bf16[48,3072]{1,0:T(8,128)(2,1)S(1)}, u32[]{:S(2)}, u32[]{:S(2)}) collective-permute-start(bf16[48,3072]{1,0:T(8,128)(2,1)S(1)} %add_convert_fusion.11), channel_id=1, source_target_pairs={{0,2},{2,4},{4,6},{6,7},{7,5},{5,3},{3,1},{1,0},{8,10},{10,12},{12... | collective-permute-start | bytes 884744 | tf_op jit(solution)/shard_map/ppermute | solution.py:152
  79.0 11.8 %collective-permute-start.25 = (bf16[48,3072]{1,0:T(8,128)(2,1)S(1)}, bf16[48,3072]{1,0:T(8,128)(2,1)S(1)}, u32[]{:S(2)}, u32[]{:S(2)}) collective-permute-start(bf16[48,3072]{1,0:T(8,128)(2,1)S(1)} %add_convert_fusion.5), channel_id=1, source_target_pairs={{0,2},{2,4},{4,6},{6,7},{7,5},{5,3},{3,1},{1,0},{8,10},{10,12},{12... | collective-permute-start | bytes 884744 | tf_op jit(solution)/shard_map/ppermute | solution.py:152
  80.7 10.8 %collective-permute-start.26 = (bf16[48,3072]{1,0:T(8,128)(2,1)S(1)}, bf16[48,3072]{1,0:T(8,128)(2,1)S(1)}, u32[]{:S(2)}, u32[]{:S(2)}) collective-permute-start(bf16[48,3072]{1,0:T(8,128)(2,1)S(1)} %add_convert_fusion.4), channel_id=1, source_target_pairs={{2,0},{4,2},{6,4},{7,6},{5,7},{3,5},{1,3},{0,1},{10,8},{12,10},{14... | collective-permute-start | bytes 884744 | tf_op jit(solution)/shard_map/ppermute | solution.py:152
  85.3 11.8 %collective-permute-start.19 = (bf16[48,3072]{1,0:T(8,128)(2,1)S(1)}, bf16[48,3072]{1,0:T(8,128)(2,1)S(1)}, u32[]{:S(2)}, u32[]{:S(2)}) collective-permute-start(bf16[48,3072]{1,0:T(8,128)(2,1)S(1)} %add_convert_fusion.9), channel_id=1, source_target_pairs={{0,2},{2,4},{4,6},{6,7},{7,5},{5,3},{3,1},{1,0},{8,10},{10,12},{12... | collective-permute-start | bytes 884744 | tf_op jit(solution)/shard_map/ppermute | solution.py:152
  87.1 10.8 %collective-permute-start.20 = (bf16[48,3072]{1,0:T(8,128)(2,1)S(1)}, bf16[48,3072]{1,0:T(8,128)(2,1)S(1)}, u32[]{:S(2)}, u32[]{:S(2)}) collective-permute-start(bf16[48,3072]{1,0:T(8,128)(2,1)S(1)} %add_convert_fusion.8), channel_id=1, source_target_pairs={{2,0},{4,2},{6,4},{7,6},{5,7},{3,5},{1,3},{0,1},{10,8},{12,10},{14... | collective-permute-start | bytes 884744 | tf_op jit(solution)/shard_map/ppermute | solution.py:152
  91.6 12.6 %collective-permute-start.28 = (bf16[48,3072]{1,0:T(8,128)(2,1)S(1)}, bf16[48,3072]{1,0:T(8,128)(2,1)S(1)}, u32[]{:S(2)}, u32[]{:S(2)}) collective-permute-start(bf16[48,3072]{1,0:T(8,128)(2,1)S(1)} %add_convert_fusion.2), channel_id=1, source_target_pairs={{2,0},{4,2},{6,4},{7,6},{5,7},{3,5},{1,3},{0,1},{10,8},{12,10},{14... | collective-permute-start | bytes 884744 | tf_op jit(solution)/shard_map/ppermute | solution.py:152
  93.3 10.9 %collective-permute-start.27 = (bf16[48,3072]{1,0:T(8,128)(2,1)S(1)}, bf16[48,3072]{1,0:T(8,128)(2,1)S(1)}, u32[]{:S(2)}, u32[]{:S(2)}) collective-permute-start(bf16[48,3072]{1,0:T(8,128)(2,1)S(1)} %add_convert_fusion.3), channel_id=1, source_target_pairs={{0,2},{2,4},{4,6},{6,7},{7,5},{5,3},{3,1},{1,0},{8,10},{10,12},{12... | collective-permute-start | bytes 884744 | tf_op jit(solution)/shard_map/ppermute | solution.py:152
  98.0 9.9 %collective-permute-start.22 = (bf16[48,3072]{1,0:T(8,128)(2,1)S(1)}, bf16[48,3072]{1,0:T(8,128)(2,1)S(1)}, u32[]{:S(2)}, u32[]{:S(2)}) collective-permute-start(bf16[48,3072]{1,0:T(8,128)(2,1)S(1)} %add_convert_fusion.6), channel_id=1, source_target_pairs={{2,0},{4,2},{6,4},{7,6},{5,7},{3,5},{1,3},{0,1},{10,8},{12,10},{14... | collective-permute-start | bytes 884744 | tf_op jit(solution)/shard_map/ppermute | solution.py:152
  99.7 8.2 %collective-permute-start.21 = (bf16[48,3072]{1,0:T(8,128)(2,1)S(1)}, bf16[48,3072]{1,0:T(8,128)(2,1)S(1)}, u32[]{:S(2)}, u32[]{:S(2)}) collective-permute-start(bf16[48,3072]{1,0:T(8,128)(2,1)S(1)} %add_convert_fusion.7), channel_id=1, source_target_pairs={{0,2},{2,4},{4,6},{6,7},{7,5},{5,3},{3,1},{1,0},{8,10},{10,12},{12... | collective-permute-start | bytes 884744 | tf_op jit(solution)/shard_map/ppermute | solution.py:152
  108.2 1.6 %collective-permute-start.29 = (bf16[24,6144]{1,0:T(8,128)(2,1)S(1)}, bf16[24,6144]{1,0:T(8,128)(2,1)S(1)}, u32[]{:S(2)}, u32[]{:S(2)}) collective-permute-start(bf16[24,6144]{1,0:T(8,128)(2,1)S(1)} %get-tuple-element.142), channel_id=1, source_target_pairs={{0,8},{8,0},{1,9},{9,1},{2,10},{10,2},{3,11},{11,3},{4,12},{12,4},... | collective-permute-start | bytes 884744 | tf_op jit(solution)/shard_map/ppermute | solution.py:246

commit v10 on v9

--- a/solution.py
+++ b/solution.py
@@ -38,14 +38,18 @@
     )(*[in_vmem(array) if memory == pltpu.VMEM else in_hbm(array) for array, memory in operands])
 
 
-def fill_kernel(source, target, done):
+def row_copies(source, target, done):
     rows = source.shape[1] // COPIES
-    copies = [
+    return [
         pltpu.make_async_copy(
             source.at[:, pl.ds(i * rows, rows)], target.at[:, pl.ds(i * rows, rows)], done.at[i]
         )
         for i in range(COPIES)
     ]
+
+
+def fill_kernel(source, target, done):
+    copies = row_copies(source, target, done)
     for copy in copies:
         copy.start()
     for copy in copies:
@@ -79,51 +83,40 @@
     accumulate(chunks, [(weights, out)])
 
 
-def up_kernel(count, *refs):
-    chunks, (weights, gate, out, total) = (refs[:count], refs[count:2 * count]), refs[2 * count:]
-    accumulate(chunks, [(weights, total)])
-    out[...] = activated(gate[...], total[...])
-
-
-def down_copies(source, target, done):
-    return [
-        pltpu.make_async_copy(
-            source.at[:, :, pl.ds(i * TILE, TILE)], target.at[:, :, pl.ds(i * TILE, TILE)], done.at[i]
-        )
-        for i in range(source.shape[2] // TILE)
-    ]
+def add_down(hidden, down, outs):
+    size, width = outs[0].shape
+    count = len(outs) // 2
+    for at in range(0, down.shape[2], TILE):
+        part = jnp.dot(hidden, down[0, :, at:at + TILE], preferred_element_type=jnp.float32).astype(jnp.bfloat16)
+        chunk, column = divmod(at, width)
+        for b in range(count):
+            outs[count * chunk + b][:, column:column + TILE] = part[b * size:(b + 1) * size]
+
+
+def near_kernel(count, *refs):
+    chunks, (w_up, gate, w_down) = (refs[:count], refs[count:2 * count]), refs[2 * count:2 * count + 3]
+    outs, (up, down, done) = refs[2 * count + 3:4 * count + 3], refs[4 * count + 3:]
+    copies = row_copies(w_down, down, done)
+    for copy in copies:
+        copy.start()
+    accumulate(chunks, [(w_up, up)])
+    hidden = activated(gate[...], up[...])
+    for copy in copies:
+        copy.wait()
+    add_down(hidden, down, outs)
 
 
 def rest_kernel(*refs):
     chunks, (w_gate, w_up, w_down), outs = (refs[:3], refs[3:6]), refs[6:9], refs[9:15]
-    gate, up, hidden, down, done = refs[15:]
-    copies = down_copies(w_down, down, done)
+    gate, up, down, done = refs[15:]
+    copies = row_copies(w_down, down, done)
     for copy in copies:
         copy.start()
     accumulate(chunks, [(w_gate, gate), (w_up, up)])
-    hidden[...] = activated(gate[...], up[...])
-    size = outs[0].shape[0]
-    for i, copy in enumerate(copies):
+    hidden = activated(gate[...], up[...])
+    for copy in copies:
         copy.wait()
-        part = jnp.dot(hidden[...], down[0, :, i * TILE:(i + 1) * TILE], preferred_element_type=jnp.float32)
-        chunk, at = divmod(i * TILE, outs[0].shape[1])
-        for b in range(3):
-            outs[3 * chunk + b][:, at:at + TILE] = part[b * size:(b + 1) * size].astype(jnp.bfloat16)
-
-
-def near_down_kernel(hidden, w_down, *refs):
-    outs, (down, done) = refs[:-2], refs[-2:]
-    size, width = outs[0].shape
-    count = len(outs) // 2
-    copies = down_copies(w_down, down, done)
-    for copy in copies:
-        copy.start()
-    for i, copy in enumerate(copies):
-        copy.wait()
-        part = jnp.dot(hidden[...], down[0, :, i * TILE:(i + 1) * TILE], preferred_element_type=jnp.float32)
-        chunk, at = divmod(i * TILE, width)
-        for b in range(count):
-            outs[count * chunk + b][:, at:at + TILE] = part[b * size:(b + 1) * size].astype(jnp.bfloat16)
+    add_down(hidden, down, outs)
 
 
 def routing(expert_ids, gate_probs, experts, slots):
@@ -199,26 +192,23 @@
     rest = [[a[0], b[1]], [b[0], a[1]]]
     a, near_gate = tied(a, near_gate)
     far = step(*a)
-    near_hidden, = call(
-        functools.partial(up_kernel, count), "near_up",
-        near + [(up_here, pltpu.VMEM), (near_gate, pltpu.VMEM)], [((rows, units), jnp.bfloat16)],
-        [pltpu.VMEM((rows, units), jnp.float32)], rows * units * 16,
+    down_scratch = [pltpu.VMEM(w_down.shape, jnp.bfloat16), pltpu.SemaphoreType.DMA((COPIES,))]
+    down_room = units * width * 2
+    near_parts = call(
+        functools.partial(near_kernel, count), "near_parts",
+        near + [(up_here, pltpu.VMEM), (near_gate, pltpu.VMEM), (w_down, pltpu.HBM)],
+        [((size, mid_col), jnp.bfloat16)] * (2 * count), [pltpu.VMEM((rows, units), jnp.float32)] + down_scratch,
+        down_room + rows * units * 16,
     )
     rest = [rest[chunk] + [far[chunk]] for chunk in range(2)]
-    rest, near_hidden = tied(rest, near_hidden)
-    down_scratch = [pltpu.VMEM(w_down.shape, jnp.bfloat16), pltpu.SemaphoreType.DMA((width // TILE,))]
-    down_room = units * width * 2
+    rest, near_parts = tied(rest, near_parts)
     rest_parts = call(
         rest_kernel, "rest",
         [(block, pltpu.VMEM) for chunk in rest for block in chunk]
         + [(gate_here, pltpu.VMEM), (up_here, pltpu.VMEM), (w_down, pltpu.HBM)],
         [((size, mid_col), jnp.bfloat16)] * 6,
-        [pltpu.VMEM((3 * size, units), jnp.float32)] * 2 + [pltpu.VMEM((3 * size, units), jnp.bfloat16)] + down_scratch,
-        down_room + 3 * size * units * 24,
-    )
-    near_parts = call(
-        near_down_kernel, "near_down", [(near_hidden, pltpu.VMEM), (w_down, pltpu.HBM)],
-        [((size, mid_col), jnp.bfloat16)] * (2 * count), down_scratch, down_room + rows * TILE * 8,
+        [pltpu.VMEM((3 * size, units), jnp.float32)] * 2 + down_scratch,
+        down_room + 3 * size * units * 16,
     )
 
     def part_of(chunk, distance, side):

time: 111 us -> 115 us (1.036)
  Pallas kernels: 31.2 us -> 33.8 us
    ppermute x14, starting transfers between devices: 8.44 us -> 24.6 us  [step(): lax.ppermute(to_right, 'tensor', right)]
    ppermute x14, waiting for transfers between devices: 15.8 us -> 31.6 us  [step(): lax.ppermute(to_left, 'tensor', left)]
    ppermute x14, starting transfers between devices: 21.6 us -> 5.91 us  [step(): lax.ppermute(to_left, 'tensor', left)]
    ppermute x14, waiting for transfers between devices: 26.4 us -> 11.4 us  [step(): lax.ppermute(to_right, 'tensor', right)]
    pallas_call x6 -> x5, Pallas kernels: 31.2 us -> 33.8 us  [call(): pl.pallas_call(kernel, in_specs=[pl.BlockSpec(memory_space=memory) for _,...]
  transfers between devices with their start and end apart: 30 -> 30, of which waited for: 19 -> 16; matrix products, arithmetic and copies ran while one was open for 1% -> 1% of each run, Pallas kernels for 20% -> 20%
where the time goes in v10:
time: 115 us
  waiting for transfers between devices  45.6 us (40%)
  Pallas kernels  33.8 us (29%)
  starting transfers between devices  31.1 us (27%)
  other arithmetic  2.17 us (2%)
  matrix products  1.59 us (1%)
    pallas_call x5, Pallas kernels, call(): pl.pallas_call(kernel, in_specs=[pl.BlockSpec(memory_space=memory) for _,...  33.8 us
    ppermute x14, waiting for transfers between devices, step(): lax.ppermute(to_left, 'tensor', left)  31.6 us
    ppermute x14, starting transfers between devices, step(): lax.ppermute(to_right, 'tensor', right)  24.6 us
    ppermute x14, waiting for transfers between devices, step(): lax.ppermute(to_right, 'tensor', right)  11.4 us
    ppermute x14, starting transfers between devices, step(): lax.ppermute(to_left, 'tensor', left)  5.91 us
  transfers between devices with their start and end apart: 30, of which 16 were waited for; matrix products, arithmetic and copies ran while one was open for 1% of the time, Pallas kernels for 20%

profile of v10, /device:TPU:0, one launch (start us, length us, event | category | flops | bytes accessed | tf_op | source)
XLA Modules:
  0.0 114.9 jit_solution(11730797715670708705)
XLA Ops:
  0.0 0.1 pad_add_fusion
  0.1 0.8 compare_reduce_fusion
  0.9 0.1 copy.17
  1.0 0.1 reduce_window_sum.11
  1.1 0.1 copy.18
  1.2 0.1 eq.64
  1.3 0.1 fusion.9
  1.4 0.3 convolution_convert_fusion
  1.7 0.5 collective-permute-start
  2.2 1.2 %collective-permute-done = bf16[24,6144]{1,0:T(8,128)(2,1)S(1)} collective-permute-done((bf16[24,6144]{1,0:T(8,128)(2,1)S(1)}, bf16[24,6144]{1,0:T(8,128)(2,1)S(1)}, u32[]{:S(2)}, u32[]{:S(2)}) %collective-permute-start) | collective-permute-done | bytes 294944 | tf_op jit(solution)/shard_map/ppermute | solution.py:159
  3.5 3.0 %collective-permute-start.1 = (bf16[48,3072]{1,0:T(8,128)(2,1)S(1)}, bf16[48,3072]{1,0:T(8,128)(2,1)S(1)}, u32[]{:S(2)}, u32[]{:S(2)}) collective-permute-start(bf16[48,3072]{1,0:T(8,128)(2,1)S(1)} %get-tuple-element.162.refs_0_), channel_id=1, source_target_pairs={{0,2},{2,4},{4,6},{6,7},{7,5},{5,3},{3,1},{1,0},{8,10},{10,12},{12... | collective-permute-start | bytes 884744 | tf_op jit(solution)/shard_map/ppermute | solution.py:145
  6.6 2.0 %collective-permute-start.7 = (bf16[48,3072]{1,0:T(8,128)(2,1)S(1)}, bf16[48,3072]{1,0:T(8,128)(2,1)S(1)}, u32[]{:S(2)}, u32[]{:S(2)}) collective-permute-start(bf16[48,3072]{1,0:T(8,128)(2,1)S(1)} %get-tuple-element.161.refs_5_), channel_id=1, source_target_pairs={{0,2},{2,4},{4,6},{6,7},{7,5},{5,3},{3,1},{1,0},{8,10},{10,12},{12... | collective-permute-start | bytes 884744 | tf_op jit(solution)/shard_map/ppermute | solution.py:145
  8.6 4.7 %fetched.2.refs_10_.refs_6_ = bf16[1,6144,1024]{2,1,0:T(8,128)(2,1)S(1)} custom-call(bf16[1,6144,1024]{2,1,0:T(8,128)(2,1)} %source), custom_call_target="tpu_custom_call" | custom-call | flops 1024 | bytes 1024 | tf_op jit(solution)/shard_map/fetched/pallas_call | solution.py:29
  13.3 1.0 collective-permute-done.1.refs_1_
  14.3 2.2 %collective-permute-done.2.refs_7_ = bf16[48,3072]{1,0:T(8,128)(2,1)S(1)} collective-permute-done((bf16[48,3072]{1,0:T(8,128)(2,1)S(1)}, bf16[48,3072]{1,0:T(8,128)(2,1)S(1)}, u32[]{:S(2)}, u32[]{:S(2)}) %collective-permute-start.2) | collective-permute-done | bytes 294944 | tf_op jit(solution)/shard_map/ppermute | solution.py:145
  16.4 1.6 %collective-permute-start.3 = (bf16[48,3072]{1,0:T(8,128)(2,1)S(1)}, bf16[48,3072]{1,0:T(8,128)(2,1)S(1)}, u32[]{:S(2)}, u32[]{:S(2)}) collective-permute-start(bf16[48,3072]{1,0:T(8,128)(2,1)S(1)} %collective-permute-done.1.refs_1_), channel_id=1, source_target_pairs={{0,2},{2,4},{4,6},{6,7},{7,5},{5,3},{3,1},{1,0},{8,10},{10,12},{12... | collective-permute-start | bytes 884744 | tf_op jit(solution)/shard_map/ppermute | solution.py:145
  18.0 0.4 collective-permute-start.4
  18.5 4.7 %fetched.3.refs_10_.refs_7_ = bf16[1,6144,1024]{2,1,0:T(8,128)(2,1)S(1)} custom-call(bf16[1,6144,1024]{2,1,0:T(8,128)(2,1)} %source.1), custom_call_target="tpu_custom_call" | custom-call | flops 1024 | bytes 1024 | tf_op jit(solution)/shard_map/fetched/pallas_call | solution.py:29
  23.2 1.1 collective-permute-start.10
  24.3 1.0 collective-permute-start.9
  25.3 1.6 %collective-permute-done.3.refs_3_ = bf16[48,3072]{1,0:T(8,128)(2,1)S(1)} collective-permute-done((bf16[48,3072]{1,0:T(8,128)(2,1)S(1)}, bf16[48,3072]{1,0:T(8,128)(2,1)S(1)}, u32[]{:S(2)}, u32[]{:S(2)}) %collective-permute-start.3) | collective-permute-done | bytes 294944 | tf_op jit(solution)/shard_map/ppermute | solution.py:145
  26.9 2.2 %collective-permute-done.4.refs_9_ = bf16[48,3072]{1,0:T(8,128)(2,1)S(1)} collective-permute-done((bf16[48,3072]{1,0:T(8,128)(2,1)S(1)}, bf16[48,3072]{1,0:T(8,128)(2,1)S(1)}, u32[]{:S(2)}, u32[]{:S(2)}) %collective-permute-start.4) | collective-permute-done | bytes 294944 | tf_op jit(solution)/shard_map/ppermute | solution.py:145
  29.1 1.6 %collective-permute-start.5 = (bf16[48,3072]{1,0:T(8,128)(2,1)S(1)}, bf16[48,3072]{1,0:T(8,128)(2,1)S(1)}, u32[]{:S(2)}, u32[]{:S(2)}) collective-permute-start(bf16[48,3072]{1,0:T(8,128)(2,1)S(1)} %collective-permute-done.3.refs_3_), channel_id=1, source_target_pairs={{0,2},{2,4},{4,6},{6,7},{7,5},{5,3},{3,1},{1,0},{8,10},{10,12},{12... | collective-permute-start | bytes 884744 | tf_op jit(solution)/shard_map/ppermute | solution.py:145
  30.7 0.4 collective-permute-start.6
  31.1 4.3 %collective-permute-done.10.refs_4_ = bf16[48,3072]{1,0:T(8,128)(2,1)S(1)} collective-permute-done((bf16[48,3072]{1,0:T(8,128)(2,1)S(1)}, bf16[48,3072]{1,0:T(8,128)(2,1)S(1)}, u32[]{:S(2)}, u32[]{:S(2)}) %collective-permute-start.10) | collective-permute-done | bytes 294944 | tf_op jit(solution)/shard_map/ppermute | solution.py:145
  35.4 3.2 %near_gate.1.refs_11_ = f32[240,1024]{1,0:T(8,128)S(1)} custom-call(bf16[48,3072]{1,0:T(8,128)(2,1)S(1)} %get-tuple-element.162.refs_0_, bf16[48,3072]{1,0:T(8,128)(2,1)S(1)} %collective-permute-done.1.refs_1_, bf16[48,3072]{1,0:T(8,128)(2,1)S(1)} %collective-permute-done.8.refs_2_, bf16[48,3072]{1,0:T(8,128)(2,1)S(1)} %collective-permute-done.3.refs_3_, ...), custom_call_target="tpu_custom_call" | custom-call | flops 1024 | bytes 1024 | tf_op jit(solution)/shard_map/near_gate/pallas_call | solution.py:29
  38.6 1.6 %collective-permute-start.11 = (bf16[48,3072]{1,0:T(8,128)(2,1)S(1)}, bf16[48,3072]{1,0:T(8,128)(2,1)S(1)}, u32[]{:S(2)}, u32[]{:S(2)}) collective-permute-start(bf16[48,3072]{1,0:T(8,128)(2,1)S(1)} %collective-permute-done.9.refs_8_), channel_id=1, source_target_pairs={{0,2},{2,4},{4,6},{6,7},{7,5},{5,3},{3,1},{1,0},{8,10},{10,12},{12... | collective-permute-start | bytes 884744 | tf_op jit(solution)/shard_map/ppermute | solution.py:145
  40.2 0.4 collective-permute-start.12
  40.7 1.6 %collective-permute-start.13 = (bf16[48,3072]{1,0:T(8,128)(2,1)S(1)}, bf16[48,3072]{1,0:T(8,128)(2,1)S(1)}, u32[]{:S(2)}, u32[]{:S(2)}) collective-permute-start(bf16[48,3072]{1,0:T(8,128)(2,1)S(1)} %collective-permute-done.5.refs_0_), channel_id=1, source_target_pairs={{0,2},{2,4},{4,6},{6,7},{7,5},{5,3},{3,1},{1,0},{8,10},{10,12},{12... | collective-permute-start | bytes 884744 | tf_op jit(solution)/shard_map/ppermute | solution.py:145
  42.3 0.4 collective-permute-start.14
  42.7 10.8 %near_parts.1 = (bf16[48,3072]{1,0:T(8,128)(2,1)S(1)}, bf16[48,3072]{1,0:T(8,128)(2,1)S(1)}, bf16[48,3072]{1,0:T(8,128)(2,1)S(1)}, bf16[48,3072]{1,0:T(8,128)(2,...) custom-call(bf16[48,3072]{1,0:T(8,128)(2,1)S(1)} %get-tuple-element., ...), custom_call_target="tpu_custom_call" | custom-call | flops 1024 | bytes 1024 | tf_op jit(solution)/shard_map/near_parts/pallas_call | solution.py:29
  53.6 10.4 %rest.1 = (bf16[48,3072]{1,0:T(8,128)(2,1)S(1)}, bf16[48,3072]{1,0:T(8,128)(2,1)S(1)}, bf16[48,3072]{1,0:T(8,128)(2,1)S(1)}, bf16[48,3072]{1,0:T(8,128)(2,1)S(1)...) custom-call(bf16[48,3072]{1,0:T(8,128)(2,1)S(1)} %collective-permute-done.5.refs_0_, ...), custom_call_target="tpu_custom_call" | custom-call | flops 1024 | bytes 1024 | tf_op jit(solution)/shard_map/rest/pallas_call | solution.py:29
  64.0 1.6 %collective-permute-start.23 = (bf16[48,3072]{1,0:T(8,128)(2,1)S(1)}, bf16[48,3072]{1,0:T(8,128)(2,1)S(1)}, u32[]{:S(2)}, u32[]{:S(2)}) collective-permute-start(bf16[48,3072]{1,0:T(8,128)(2,1)S(1)} %get-tuple-element.147), channel_id=1, source_target_pairs={{0,2},{2,4},{4,6},{6,7},{7,5},{5,3},{3,1},{1,0},{8,10},{10,12},{12... | collective-permute-start | bytes 884744 | tf_op jit(solution)/shard_map/ppermute | solution.py:145
  65.6 0.4 collective-permute-start.24
  66.1 1.6 %collective-permute-start.15 = (bf16[48,3072]{1,0:T(8,128)(2,1)S(1)}, bf16[48,3072]{1,0:T(8,128)(2,1)S(1)}, u32[]{:S(2)}, u32[]{:S(2)}) collective-permute-start(bf16[48,3072]{1,0:T(8,128)(2,1)S(1)} %get-tuple-element.133), channel_id=1, source_target_pairs={{0,2},{2,4},{4,6},{6,7},{7,5},{5,3},{3,1},{1,0},{8,10},{10,12},{12... | collective-permute-start | bytes 884744 | tf_op jit(solution)/shard_map/ppermute | solution.py:145
  67.7 0.4 collective-permute-start.16
  68.1 5.9 %collective-permute-done.23 = bf16[48,3072]{1,0:T(8,128)(2,1)S(1)} collective-permute-done((bf16[48,3072]{1,0:T(8,128)(2,1)S(1)}, bf16[48,3072]{1,0:T(8,128)(2,1)S(1)}, u32[]{:S(2)}, u32[]{:S(2)}) %collective-permute-start.23) | collective-permute-done | bytes 294944 | tf_op jit(solution)/shard_map/ppermute | solution.py:145
  74.0 1.6 %collective-permute-done.24 = bf16[48,3072]{1,0:T(8,128)(2,1)S(1)} collective-permute-done((bf16[48,3072]{1,0:T(8,128)(2,1)S(1)}, bf16[48,3072]{1,0:T(8,128)(2,1)S(1)}, u32[]{:S(2)}, u32[]{:S(2)}) %collective-permute-start.24) | collective-permute-done | bytes 294944 | tf_op jit(solution)/shard_map/ppermute | solution.py:145
  75.6 0.1 add_convert_fusion.4
  75.7 0.4 collective-permute-start.26
  76.2 0.1 add_convert_fusion.5
  76.2 1.7 %collective-permute-start.25 = (bf16[48,3072]{1,0:T(8,128)(2,1)S(1)}, bf16[48,3072]{1,0:T(8,128)(2,1)S(1)}, u32[]{:S(2)}, u32[]{:S(2)}) collective-permute-start(bf16[48,3072]{1,0:T(8,128)(2,1)S(1)} %add_convert_fusion.5), channel_id=1, source_target_pairs={{0,2},{2,4},{4,6},{6,7},{7,5},{5,3},{3,1},{1,0},{8,10},{10,12},{12... | collective-permute-start | bytes 884744 | tf_op jit(solution)/shard_map/ppermute | solution.py:145
  77.9 2.4 %collective-permute-done.15 = bf16[48,3072]{1,0:T(8,128)(2,1)S(1)} collective-permute-done((bf16[48,3072]{1,0:T(8,128)(2,1)S(1)}, bf16[48,3072]{1,0:T(8,128)(2,1)S(1)}, u32[]{:S(2)}, u32[]{:S(2)}) %collective-permute-start.15) | collective-permute-done | bytes 294944 | tf_op jit(solution)/shard_map/ppermute | solution.py:145
  80.3 1.6 %collective-permute-done.16 = bf16[48,3072]{1,0:T(8,128)(2,1)S(1)} collective-permute-done((bf16[48,3072]{1,0:T(8,128)(2,1)S(1)}, bf16[48,3072]{1,0:T(8,128)(2,1)S(1)}, u32[]{:S(2)}, u32[]{:S(2)}) %collective-permute-start.16) | collective-permute-done | bytes 294944 | tf_op jit(solution)/shard_map/ppermute | solution.py:145
  82.0 0.1 add_convert_fusion.10
  82.0 0.4 collective-permute-start.18
  82.5 1.7 %collective-permute-start.17 = (bf16[48,3072]{1,0:T(8,128)(2,1)S(1)}, bf16[48,3072]{1,0:T(8,128)(2,1)S(1)}, u32[]{:S(2)}, u32[]{:S(2)}) collective-permute-start(bf16[48,3072]{1,0:T(8,128)(2,1)S(1)} %add_convert_fusion.11), channel_id=1, source_target_pairs={{0,2},{2,4},{4,6},{6,7},{7,5},{5,3},{3,1},{1,0},{8,10},{10,12},{12... | collective-permute-start | bytes 884744 | tf_op jit(solution)/shard_map/ppermute | solution.py:145
  84.3 4.0 %collective-permute-done.26 = bf16[48,3072]{1,0:T(8,128)(2,1)S(1)} collective-permute-done((bf16[48,3072]{1,0:T(8,128)(2,1)S(1)}, bf16[48,3072]{1,0:T(8,128)(2,1)S(1)}, u32[]{:S(2)}, u32[]{:S(2)}) %collective-permute-start.26) | collective-permute-done | bytes 294944 | tf_op jit(solution)/shard_map/ppermute | solution.py:145
  88.4 0.4 collective-permute-start.28
  88.8 5.8 %collective-permute-done.18 = bf16[48,3072]{1,0:T(8,128)(2,1)S(1)} collective-permute-done((bf16[48,3072]{1,0:T(8,128)(2,1)S(1)}, bf16[48,3072]{1,0:T(8,128)(2,1)S(1)}, u32[]{:S(2)}, u32[]{:S(2)}) %collective-permute-start.18) | collective-permute-done | bytes 294944 | tf_op jit(solution)/shard_map/ppermute | solution.py:145
  94.7 0.4 collective-permute-start.20
  95.2 1.7 %collective-permute-start.19 = (bf16[48,3072]{1,0:T(8,128)(2,1)S(1)}, bf16[48,3072]{1,0:T(8,128)(2,1)S(1)}, u32[]{:S(2)}, u32[]{:S(2)}) collective-permute-start(bf16[48,3072]{1,0:T(8,128)(2,1)S(1)} %add_convert_fusion.9), channel_id=1, source_target_pairs={{0,2},{2,4},{4,6},{6,7},{7,5},{5,3},{3,1},{1,0},{8,10},{10,12},{12... | collective-permute-start | bytes 884744 | tf_op jit(solution)/shard_map/ppermute | solution.py:145
  97.0 2.1 %collective-permute-start.27 = (bf16[48,3072]{1,0:T(8,128)(2,1)S(1)}, bf16[48,3072]{1,0:T(8,128)(2,1)S(1)}, u32[]{:S(2)}, u32[]{:S(2)}) collective-permute-start(bf16[48,3072]{1,0:T(8,128)(2,1)S(1)} %add_convert_fusion.3), channel_id=1, source_target_pairs={{0,2},{2,4},{4,6},{6,7},{7,5},{5,3},{3,1},{1,0},{8,10},{10,12},{12... | collective-permute-start | bytes 884744 | tf_op jit(solution)/shard_map/ppermute | solution.py:145
  99.1 5.3 %collective-permute-done.20 = bf16[48,3072]{1,0:T(8,128)(2,1)S(1)} collective-permute-done((bf16[48,3072]{1,0:T(8,128)(2,1)S(1)}, bf16[48,3072]{1,0:T(8,128)(2,1)S(1)}, u32[]{:S(2)}, u32[]{:S(2)}) %collective-permute-start.20) | collective-permute-done | bytes 294944 | tf_op jit(solution)/shard_map/ppermute | solution.py:145
  104.4 0.4 collective-permute-start.22
  104.9 0.1 add_convert_fusion.7
  104.9 1.7 %collective-permute-start.21 = (bf16[48,3072]{1,0:T(8,128)(2,1)S(1)}, bf16[48,3072]{1,0:T(8,128)(2,1)S(1)}, u32[]{:S(2)}, u32[]{:S(2)}) collective-permute-start(bf16[48,3072]{1,0:T(8,128)(2,1)S(1)} %add_convert_fusion.7), channel_id=1, source_target_pairs={{0,2},{2,4},{4,6},{6,7},{7,5},{5,3},{3,1},{1,0},{8,10},{10,12},{12... | collective-permute-start | bytes 884744 | tf_op jit(solution)/shard_map/ppermute | solution.py:145
  106.7 4.6 %collective-permute-done.22 = bf16[48,3072]{1,0:T(8,128)(2,1)S(1)} collective-permute-done((bf16[48,3072]{1,0:T(8,128)(2,1)S(1)}, bf16[48,3072]{1,0:T(8,128)(2,1)S(1)}, u32[]{:S(2)}, u32[]{:S(2)}) %collective-permute-start.22) | collective-permute-done | bytes 294944 | tf_op jit(solution)/shard_map/ppermute | solution.py:145
  111.2 0.5 collective-permute-done.21
  111.7 0.2 add_convert_fusion
  112.0 0.1 collective-permute-start.29
  112.1 0.1 fusion.14
  112.2 1.5 %collective-permute-done.29 = bf16[24,6144]{1,0:T(8,128)(2,1)S(1)} collective-permute-done((bf16[24,6144]{1,0:T(8,128)(2,1)S(1)}, bf16[24,6144]{1,0:T(8,128)(2,1)S(1)}, u32[]{:S(2)}, u32[]{:S(2)}) %collective-permute-start.29) | collective-permute-done | bytes 294944 | tf_op jit(solution)/shard_map/ppermute | solution.py:236
  113.6 1.3 %fusion = bf16[64,6144]{1,0:T(8,128)(2,1)} fusion(bf16[1,24,6144]{2,1,0:T(8,128)(2,1)S(1)} %bitcast.22, bf16[1,24,6144]{2,1,0:T(8,128)(2,1)S(1)} %get-tuple-element.159, bf16[2,64]{1,0:T(2,128)(2,1)S(1)} %bitcast.23, s32[2,64]{1,0:T(2,128)S(1)} %subtract_bitcast_fusion, pred[2,64]{1,0:T(4,128)(4,1)S(1)} %get-tuple-element.165), kind=kOutput, calls=%fused_computation.1 | convolution fusion | flops 38052864 | bytes 1377152 | tf_op jit(solution)/shard_map/wcr,wcd->rd/dot_general | solution.py:238
  (41 shorter events, 0.7 us)
Async XLA Ops:
  0.0 1.4 %copy-start = (bf16[64,6144]{1,0:T(8,128)(2,1)S(1)}, bf16[64,6144]{1,0:T(8,128)(2,1)}, u32[]{:S(2)}) copy-start(bf16[64,6144]{1,0:T(8,128)(2,1)} %param.6) | copy-start | bytes 2359300
  1.7 1.7 %collective-permute-start = (bf16[24,6144]{1,0:T(8,128)(2,1)S(1)}, bf16[24,6144]{1,0:T(8,128)(2,1)S(1)}, u32[]{:S(2)}, u32[]{:S(2)}) collective-permute-start(bf16[24,6144]{1,0:T(8,128)(2,1)S(1)} %get-tuple-element.164), channel_id=1, source_target_pairs={{0,8},{8,0},{1,9},{9,1},{2,10},{10,2},{3,11},{11,3},{4,12},{12,4},... | collective-permute-start | bytes 884744 | tf_op jit(solution)/shard_map/ppermute | solution.py:159
  3.5 10.7 %collective-permute-start.1 = (bf16[48,3072]{1,0:T(8,128)(2,1)S(1)}, bf16[48,3072]{1,0:T(8,128)(2,1)S(1)}, u32[]{:S(2)}, u32[]{:S(2)}) collective-permute-start(bf16[48,3072]{1,0:T(8,128)(2,1)S(1)} %get-tuple-element.162.refs_0_), channel_id=1, source_target_pairs={{0,2},{2,4},{4,6},{6,7},{7,5},{5,3},{3,1},{1,0},{8,10},{10,12},{12... | collective-permute-start | bytes 884744 | tf_op jit(solution)/shard_map/ppermute | solution.py:145
  6.5 9.9 %collective-permute-start.2 = (bf16[48,3072]{1,0:T(8,128)(2,1)S(1)}, bf16[48,3072]{1,0:T(8,128)(2,1)S(1)}, u32[]{:S(2)}, u32[]{:S(2)}) collective-permute-start(bf16[48,3072]{1,0:T(8,128)(2,1)S(1)} %get-tuple-element.161.refs_5_), channel_id=1, source_target_pairs={{2,0},{4,2},{6,4},{7,6},{5,7},{3,5},{1,3},{0,1},{10,8},{12,10},{14... | collective-permute-start | bytes 884744 | tf_op jit(solution)/shard_map/ppermute | solution.py:145
  6.6 16.6 %collective-permute-start.7 = (bf16[48,3072]{1,0:T(8,128)(2,1)S(1)}, bf16[48,3072]{1,0:T(8,128)(2,1)S(1)}, u32[]{:S(2)}, u32[]{:S(2)}) collective-permute-start(bf16[48,3072]{1,0:T(8,128)(2,1)S(1)} %get-tuple-element.161.refs_5_), channel_id=1, source_target_pairs={{0,2},{2,4},{4,6},{6,7},{7,5},{5,3},{3,1},{1,0},{8,10},{10,12},{12... | collective-permute-start | bytes 884744 | tf_op jit(solution)/shard_map/ppermute | solution.py:145
  8.6 14.6 %collective-permute-start.8 = (bf16[48,3072]{1,0:T(8,128)(2,1)S(1)}, bf16[48,3072]{1,0:T(8,128)(2,1)S(1)}, u32[]{:S(2)}, u32[]{:S(2)}) collective-permute-start(bf16[48,3072]{1,0:T(8,128)(2,1)S(1)} %get-tuple-element.162.refs_0_), channel_id=1, source_target_pairs={{2,0},{4,2},{6,4},{7,6},{5,7},{3,5},{1,3},{0,1},{10,8},{12,10},{14... | collective-permute-start | bytes 884744 | tf_op jit(solution)/shard_map/ppermute | solution.py:145
  13.3 22.1 %copy-start.2 = (bf16[1,6144,1024]{2,1,0:T(8,128)(2,1)}, bf16[1,6144,1024]{2,1,0:T(8,128)(2,1)S(1)}, u32[]{:S(2)}) copy-start(bf16[1,6144,1024]{2,1,0:T(8,128)(2,1)S(1)} %fetched.2.refs_10_.refs_6_) | copy-start | bytes 37748740
  16.4 10.5 %collective-permute-start.3 = (bf16[48,3072]{1,0:T(8,128)(2,1)S(1)}, bf16[48,3072]{1,0:T(8,128)(2,1)S(1)}, u32[]{:S(2)}, u32[]{:S(2)}) collective-permute-start(bf16[48,3072]{1,0:T(8,128)(2,1)S(1)} %collective-permute-done.1.refs_1_), channel_id=1, source_target_pairs={{0,2},{2,4},{4,6},{6,7},{7,5},{5,3},{3,1},{1,0},{8,10},{10,12},{12... | collective-permute-start | bytes 884744 | tf_op jit(solution)/shard_map/ppermute | solution.py:145
  18.0 11.1 %collective-permute-start.4 = (bf16[48,3072]{1,0:T(8,128)(2,1)S(1)}, bf16[48,3072]{1,0:T(8,128)(2,1)S(1)}, u32[]{:S(2)}, u32[]{:S(2)}) collective-permute-start(bf16[48,3072]{1,0:T(8,128)(2,1)S(1)} %collective-permute-done.2.refs_7_), channel_id=1, source_target_pairs={{2,0},{4,2},{6,4},{7,6},{5,7},{3,5},{1,3},{0,1},{10,8},{12,10},{14... | collective-permute-start | bytes 884744 | tf_op jit(solution)/shard_map/ppermute | solution.py:145
  23.2 12.2 %collective-permute-start.10 = (bf16[48,3072]{1,0:T(8,128)(2,1)S(1)}, bf16[48,3072]{1,0:T(8,128)(2,1)S(1)}, u32[]{:S(2)}, u32[]{:S(2)}) collective-permute-start(bf16[48,3072]{1,0:T(8,128)(2,1)S(1)} %collective-permute-done.8.refs_2_), channel_id=1, source_target_pairs={{2,0},{4,2},{6,4},{7,6},{5,7},{3,5},{1,3},{0,1},{10,8},{12,10},{14... | collective-permute-start | bytes 884744 | tf_op jit(solution)/shard_map/ppermute | solution.py:145
  24.3 11.1 %collective-permute-start.9 = (bf16[48,3072]{1,0:T(8,128)(2,1)S(1)}, bf16[48,3072]{1,0:T(8,128)(2,1)S(1)}, u32[]{:S(2)}, u32[]{:S(2)}) collective-permute-start(bf16[48,3072]{1,0:T(8,128)(2,1)S(1)} %collective-permute-done.7.refs_6_), channel_id=1, source_target_pairs={{0,2},{2,4},{4,6},{6,7},{7,5},{5,3},{3,1},{1,0},{8,10},{10,12},{12... | collective-permute-start | bytes 884744 | tf_op jit(solution)/shard_map/ppermute | solution.py:145
  29.1 11.6 %collective-permute-start.5 = (bf16[48,3072]{1,0:T(8,128)(2,1)S(1)}, bf16[48,3072]{1,0:T(8,128)(2,1)S(1)}, u32[]{:S(2)}, u32[]{:S(2)}) collective-permute-start(bf16[48,3072]{1,0:T(8,128)(2,1)S(1)} %collective-permute-done.3.refs_3_), channel_id=1, source_target_pairs={{0,2},{2,4},{4,6},{6,7},{7,5},{5,3},{3,1},{1,0},{8,10},{10,12},{12... | collective-permute-start | bytes 884744 | tf_op jit(solution)/shard_map/ppermute | solution.py:145
  30.7 10.0 %collective-permute-start.6 = (bf16[48,3072]{1,0:T(8,128)(2,1)S(1)}, bf16[48,3072]{1,0:T(8,128)(2,1)S(1)}, u32[]{:S(2)}, u32[]{:S(2)}) collective-permute-start(bf16[48,3072]{1,0:T(8,128)(2,1)S(1)} %collective-permute-done.4.refs_9_), channel_id=1, source_target_pairs={{2,0},{4,2},{6,4},{7,6},{5,7},{3,5},{1,3},{0,1},{10,8},{12,10},{14... | collective-permute-start | bytes 884744 | tf_op jit(solution)/shard_map/ppermute | solution.py:145
  38.6 14.9 %copy-start.3 = (bf16[1,6144,1024]{2,1,0:T(8,128)(2,1)S(1)}, bf16[1,6144,1024]{2,1,0:T(8,128)(2,1)}, u32[]{:S(2)}) copy-start(bf16[1,6144,1024]{2,1,0:T(8,128)(2,1)} %copy-done.2) | copy-start | bytes 37748740
  38.6 14.9 %collective-permute-start.11 = (bf16[48,3072]{1,0:T(8,128)(2,1)S(1)}, bf16[48,3072]{1,0:T(8,128)(2,1)S(1)}, u32[]{:S(2)}, u32[]{:S(2)}) collective-permute-start(bf16[48,3072]{1,0:T(8,128)(2,1)S(1)} %collective-permute-done.9.refs_8_), channel_id=1, source_target_pairs={{0,2},{2,4},{4,6},{6,7},{7,5},{5,3},{3,1},{1,0},{8,10},{10,12},{12... | collective-permute-start | bytes 884744 | tf_op jit(solution)/shard_map/ppermute | solution.py:145
  40.2 13.3 %collective-permute-start.12 = (bf16[48,3072]{1,0:T(8,128)(2,1)S(1)}, bf16[48,3072]{1,0:T(8,128)(2,1)S(1)}, u32[]{:S(2)}, u32[]{:S(2)}) collective-permute-start(bf16[48,3072]{1,0:T(8,128)(2,1)S(1)} %collective-permute-done.10.refs_4_), channel_id=1, source_target_pairs={{2,0},{4,2},{6,4},{7,6},{5,7},{3,5},{1,3},{0,1},{10,8},{12,10},{14... | collective-permute-start | bytes 884744 | tf_op jit(solution)/shard_map/ppermute | solution.py:145
  40.7 12.8 %collective-permute-start.13 = (bf16[48,3072]{1,0:T(8,128)(2,1)S(1)}, bf16[48,3072]{1,0:T(8,128)(2,1)S(1)}, u32[]{:S(2)}, u32[]{:S(2)}) collective-permute-start(bf16[48,3072]{1,0:T(8,128)(2,1)S(1)} %collective-permute-done.5.refs_0_), channel_id=1, source_target_pairs={{0,2},{2,4},{4,6},{6,7},{7,5},{5,3},{3,1},{1,0},{8,10},{10,12},{12... | collective-permute-start | bytes 884744 | tf_op jit(solution)/shard_map/ppermute | solution.py:145
  42.3 11.3 %collective-permute-start.14 = (bf16[48,3072]{1,0:T(8,128)(2,1)S(1)}, bf16[48,3072]{1,0:T(8,128)(2,1)S(1)}, u32[]{:S(2)}, u32[]{:S(2)}) collective-permute-start(bf16[48,3072]{1,0:T(8,128)(2,1)S(1)} %collective-permute-done.6.refs_4_), channel_id=1, source_target_pairs={{2,0},{4,2},{6,4},{7,6},{5,7},{3,5},{1,3},{0,1},{10,8},{12,10},{14... | collective-permute-start | bytes 884744 | tf_op jit(solution)/shard_map/ppermute | solution.py:145
  53.5 58.5 %copy-start.4 = (s32[64,2]{0,1:T(2,128)S(1)}, s32[64,2]{0,1:T(2,128)}, u32[]{:S(2)}) copy-start(s32[64,2]{0,1:T(2,128)} %param.7) | copy-start | bytes 1540
  53.6 58.5 %copy-start.5 = (f32[64,2]{0,1:T(2,128)S(1)}, f32[64,2]{0,1:T(2,128)}, u32[]{:S(2)}) copy-start(f32[64,2]{0,1:T(2,128)} %param.8) | copy-start | bytes 1540
  53.6 61.3 %copy-start.1 = (bf16[64,6144]{1,0:T(8,128)(2,1)S(1)}, bf16[64,6144]{1,0:T(8,128)(2,1)}, u32[]{:S(2)}) copy-start(bf16[64,6144]{1,0:T(8,128)(2,1)} %param.6) | copy-start | bytes 2359300
  64.0 10.0 %collective-permute-start.23 = (bf16[48,3072]{1,0:T(8,128)(2,1)S(1)}, bf16[48,3072]{1,0:T(8,128)(2,1)S(1)}, u32[]{:S(2)}, u32[]{:S(2)}) collective-permute-start(bf16[48,3072]{1,0:T(8,128)(2,1)S(1)} %get-tuple-element.147), channel_id=1, source_target_pairs={{0,2},{2,4},{4,6},{6,7},{7,5},{5,3},{3,1},{1,0},{8,10},{10,12},{12... | collective-permute-start | bytes 884744 | tf_op jit(solution)/shard_map/ppermute | solution.py:145
  65.6 10.0 %collective-permute-start.24 = (bf16[48,3072]{1,0:T(8,128)(2,1)S(1)}, bf16[48,3072]{1,0:T(8,128)(2,1)S(1)}, u32[]{:S(2)}, u32[]{:S(2)}) collective-permute-start(bf16[48,3072]{1,0:T(8,128)(2,1)S(1)} %get-tuple-element.148), channel_id=1, source_target_pairs={{2,0},{4,2},{6,4},{7,6},{5,7},{3,5},{1,3},{0,1},{10,8},{12,10},{14... | collective-permute-start | bytes 884744 | tf_op jit(solution)/shard_map/ppermute | solution.py:145
  66.1 14.2 %collective-permute-start.15 = (bf16[48,3072]{1,0:T(8,128)(2,1)S(1)}, bf16[48,3072]{1,0:T(8,128)(2,1)S(1)}, u32[]{:S(2)}, u32[]{:S(2)}) collective-permute-start(bf16[48,3072]{1,0:T(8,128)(2,1)S(1)} %get-tuple-element.133), channel_id=1, source_target_pairs={{0,2},{2,4},{4,6},{6,7},{7,5},{5,3},{3,1},{1,0},{8,10},{10,12},{12... | collective-permute-start | bytes 884744 | tf_op jit(solution)/shard_map/ppermute | solution.py:145
  67.7 14.2 %collective-permute-start.16 = (bf16[48,3072]{1,0:T(8,128)(2,1)S(1)}, bf16[48,3072]{1,0:T(8,128)(2,1)S(1)}, u32[]{:S(2)}, u32[]{:S(2)}) collective-permute-start(bf16[48,3072]{1,0:T(8,128)(2,1)S(1)} %get-tuple-element.134), channel_id=1, source_target_pairs={{2,0},{4,2},{6,4},{7,6},{5,7},{3,5},{1,3},{0,1},{10,8},{12,10},{14... | collective-permute-start | bytes 884744 | tf_op jit(solution)/shard_map/ppermute | solution.py:145
  75.7 12.6 %collective-permute-start.26 = (bf16[48,3072]{1,0:T(8,128)(2,1)S(1)}, bf16[48,3072]{1,0:T(8,128)(2,1)S(1)}, u32[]{:S(2)}, u32[]{:S(2)}) collective-permute-start(bf16[48,3072]{1,0:T(8,128)(2,1)S(1)} %add_convert_fusion.4), channel_id=1, source_target_pairs={{2,0},{4,2},{6,4},{7,6},{5,7},{3,5},{1,3},{0,1},{10,8},{12,10},{14... | collective-permute-start | bytes 884744 | tf_op jit(solution)/shard_map/ppermute | solution.py:145
  76.2 12.1 %collective-permute-start.25 = (bf16[48,3072]{1,0:T(8,128)(2,1)S(1)}, bf16[48,3072]{1,0:T(8,128)(2,1)S(1)}, u32[]{:S(2)}, u32[]{:S(2)}) collective-permute-start(bf16[48,3072]{1,0:T(8,128)(2,1)S(1)} %add_convert_fusion.5), channel_id=1, source_target_pairs={{0,2},{2,4},{4,6},{6,7},{7,5},{5,3},{3,1},{1,0},{8,10},{10,12},{12... | collective-permute-start | bytes 884744 | tf_op jit(solution)/shard_map/ppermute | solution.py:145
  82.0 12.6 %collective-permute-start.18 = (bf16[48,3072]{1,0:T(8,128)(2,1)S(1)}, bf16[48,3072]{1,0:T(8,128)(2,1)S(1)}, u32[]{:S(2)}, u32[]{:S(2)}) collective-permute-start(bf16[48,3072]{1,0:T(8,128)(2,1)S(1)} %add_convert_fusion.10), channel_id=1, source_target_pairs={{2,0},{4,2},{6,4},{7,6},{5,7},{3,5},{1,3},{0,1},{10,8},{12,10},{14... | collective-permute-start | bytes 884744 | tf_op jit(solution)/shard_map/ppermute | solution.py:145
  82.5 12.1 %collective-permute-start.17 = (bf16[48,3072]{1,0:T(8,128)(2,1)S(1)}, bf16[48,3072]{1,0:T(8,128)(2,1)S(1)}, u32[]{:S(2)}, u32[]{:S(2)}) collective-permute-start(bf16[48,3072]{1,0:T(8,128)(2,1)S(1)} %add_convert_fusion.11), channel_id=1, source_target_pairs={{0,2},{2,4},{4,6},{6,7},{7,5},{5,3},{3,1},{1,0},{8,10},{10,12},{12... | collective-permute-start | bytes 884744 | tf_op jit(solution)/shard_map/ppermute | solution.py:145
  88.4 18.3 %collective-permute-start.28 = (bf16[48,3072]{1,0:T(8,128)(2,1)S(1)}, bf16[48,3072]{1,0:T(8,128)(2,1)S(1)}, u32[]{:S(2)}, u32[]{:S(2)}) collective-permute-start(bf16[48,3072]{1,0:T(8,128)(2,1)S(1)} %add_convert_fusion.2), channel_id=1, source_target_pairs={{2,0},{4,2},{6,4},{7,6},{5,7},{3,5},{1,3},{0,1},{10,8},{12,10},{14... | collective-permute-start | bytes 884744 | tf_op jit(solution)/shard_map/ppermute | solution.py:145
  94.7 9.7 %collective-permute-start.20 = (bf16[48,3072]{1,0:T(8,128)(2,1)S(1)}, bf16[48,3072]{1,0:T(8,128)(2,1)S(1)}, u32[]{:S(2)}, u32[]{:S(2)}) collective-permute-start(bf16[48,3072]{1,0:T(8,128)(2,1)S(1)} %add_convert_fusion.8), channel_id=1, source_target_pairs={{2,0},{4,2},{6,4},{7,6},{5,7},{3,5},{1,3},{0,1},{10,8},{12,10},{14... | collective-permute-start | bytes 884744 | tf_op jit(solution)/shard_map/ppermute | solution.py:145
  95.2 9.2 %collective-permute-start.19 = (bf16[48,3072]{1,0:T(8,128)(2,1)S(1)}, bf16[48,3072]{1,0:T(8,128)(2,1)S(1)}, u32[]{:S(2)}, u32[]{:S(2)}) collective-permute-start(bf16[48,3072]{1,0:T(8,128)(2,1)S(1)} %add_convert_fusion.9), channel_id=1, source_target_pairs={{0,2},{2,4},{4,6},{6,7},{7,5},{5,3},{3,1},{1,0},{8,10},{10,12},{12... | collective-permute-start | bytes 884744 | tf_op jit(solution)/shard_map/ppermute | solution.py:145
  97.0 9.7 %collective-permute-start.27 = (bf16[48,3072]{1,0:T(8,128)(2,1)S(1)}, bf16[48,3072]{1,0:T(8,128)(2,1)S(1)}, u32[]{:S(2)}, u32[]{:S(2)}) collective-permute-start(bf16[48,3072]{1,0:T(8,128)(2,1)S(1)} %add_convert_fusion.3), channel_id=1, source_target_pairs={{0,2},{2,4},{4,6},{6,7},{7,5},{5,3},{3,1},{1,0},{8,10},{10,12},{12... | collective-permute-start | bytes 884744 | tf_op jit(solution)/shard_map/ppermute | solution.py:145
  104.4 6.8 %collective-permute-start.22 = (bf16[48,3072]{1,0:T(8,128)(2,1)S(1)}, bf16[48,3072]{1,0:T(8,128)(2,1)S(1)}, u32[]{:S(2)}, u32[]{:S(2)}) collective-permute-start(bf16[48,3072]{1,0:T(8,128)(2,1)S(1)} %add_convert_fusion.6), channel_id=1, source_target_pairs={{2,0},{4,2},{6,4},{7,6},{5,7},{3,5},{1,3},{0,1},{10,8},{12,10},{14... | collective-permute-start | bytes 884744 | tf_op jit(solution)/shard_map/ppermute | solution.py:145
  104.9 6.8 %collective-permute-start.21 = (bf16[48,3072]{1,0:T(8,128)(2,1)S(1)}, bf16[48,3072]{1,0:T(8,128)(2,1)S(1)}, u32[]{:S(2)}, u32[]{:S(2)}) collective-permute-start(bf16[48,3072]{1,0:T(8,128)(2,1)S(1)} %add_convert_fusion.7), channel_id=1, source_target_pairs={{0,2},{2,4},{4,6},{6,7},{7,5},{5,3},{3,1},{1,0},{8,10},{10,12},{12... | collective-permute-start | bytes 884744 | tf_op jit(solution)/shard_map/ppermute | solution.py:145
  112.0 1.6 %collective-permute-start.29 = (bf16[24,6144]{1,0:T(8,128)(2,1)S(1)}, bf16[24,6144]{1,0:T(8,128)(2,1)S(1)}, u32[]{:S(2)}, u32[]{:S(2)}) collective-permute-start(bf16[24,6144]{1,0:T(8,128)(2,1)S(1)} %get-tuple-element.160), channel_id=1, source_target_pairs={{0,8},{8,0},{1,9},{9,1},{2,10},{10,2},{3,11},{11,3},{4,12},{12,4},... | collective-permute-start | bytes 884744 | tf_op jit(solution)/shard_map/ppermute | solution.py:236

commit v11 on v10

--- a/solution.py
+++ b/solution.py
@@ -86,11 +86,12 @@
 def add_down(hidden, down, outs):
     size, width = outs[0].shape
     count = len(outs) // 2
-    for at in range(0, down.shape[2], TILE):
-        part = jnp.dot(hidden, down[0, :, at:at + TILE], preferred_element_type=jnp.float32).astype(jnp.bfloat16)
+    depth = width if size * count <= 512 else TILE
+    for at in range(0, down.shape[2], depth):
+        part = jnp.dot(hidden, down[0, :, at:at + depth], preferred_element_type=jnp.float32).astype(jnp.bfloat16)
         chunk, column = divmod(at, width)
         for b in range(count):
-            outs[count * chunk + b][:, column:column + TILE] = part[b * size:(b + 1) * size]
+            outs[count * chunk + b][:, column:column + depth] = part[b * size:(b + 1) * size]
 
 
 def near_kernel(count, *refs):

time: 115 us -> 115 us (level)
  no operation moved by 1% of the time
where the time goes in v11:
time: 115 us
  waiting for transfers between devices  45.6 us (40%)
  Pallas kernels  33.8 us (29%)
  starting transfers between devices  31.1 us (27%)
  other arithmetic  2.17 us (2%)
  matrix products  1.59 us (1%)
    pallas_call x5, Pallas kernels, call(): pl.pallas_call(kernel, in_specs=[pl.BlockSpec(memory_space=memory) for _,...  33.8 us
    ppermute x14, waiting for transfers between devices, step(): lax.ppermute(to_left, 'tensor', left)  31.6 us
    ppermute x14, starting transfers between devices, step(): lax.ppermute(to_right, 'tensor', right)  24.6 us
    ppermute x14, waiting for transfers between devices, step(): lax.ppermute(to_right, 'tensor', right)  11.4 us
    ppermute x14, starting transfers between devices, step(): lax.ppermute(to_left, 'tensor', left)  5.91 us
  transfers between devices with their start and end apart: 30, of which 16 were waited for; matrix products, arithmetic and copies ran while one was open for 1% of the time, Pallas kernels for 20%

profile of v11, /device:TPU:0, one launch (start us, length us, event | category | flops | bytes accessed | tf_op | source)
XLA Modules:
  0.0 114.9 jit_solution(11730797715670708705)
XLA Ops:
  0.0 0.1 pad_add_fusion
  0.1 0.8 compare_reduce_fusion
  0.9 0.1 copy.17
  1.0 0.1 reduce_window_sum.11
  1.1 0.1 copy.18
  1.2 0.1 eq.64
  1.3 0.1 fusion.9
  1.4 0.3 convolution_convert_fusion
  1.7 0.5 collective-permute-start
  2.2 1.2 %collective-permute-done = bf16[24,6144]{1,0:T(8,128)(2,1)S(1)} collective-permute-done((bf16[24,6144]{1,0:T(8,128)(2,1)S(1)}, bf16[24,6144]{1,0:T(8,128)(2,1)S(1)}, u32[]{:S(2)}, u32[]{:S(2)}) %collective-permute-start) | collective-permute-done | bytes 294944 | tf_op jit(solution)/shard_map/ppermute | solution.py:160
  3.5 3.0 %collective-permute-start.1 = (bf16[48,3072]{1,0:T(8,128)(2,1)S(1)}, bf16[48,3072]{1,0:T(8,128)(2,1)S(1)}, u32[]{:S(2)}, u32[]{:S(2)}) collective-permute-start(bf16[48,3072]{1,0:T(8,128)(2,1)S(1)} %get-tuple-element.162.refs_0_), channel_id=1, source_target_pairs={{0,2},{2,4},{4,6},{6,7},{7,5},{5,3},{3,1},{1,0},{8,10},{10,12},{12... | collective-permute-start | bytes 884744 | tf_op jit(solution)/shard_map/ppermute | solution.py:146
  6.6 2.0 %collective-permute-start.7 = (bf16[48,3072]{1,0:T(8,128)(2,1)S(1)}, bf16[48,3072]{1,0:T(8,128)(2,1)S(1)}, u32[]{:S(2)}, u32[]{:S(2)}) collective-permute-start(bf16[48,3072]{1,0:T(8,128)(2,1)S(1)} %get-tuple-element.161.refs_5_), channel_id=1, source_target_pairs={{0,2},{2,4},{4,6},{6,7},{7,5},{5,3},{3,1},{1,0},{8,10},{10,12},{12... | collective-permute-start | bytes 884744 | tf_op jit(solution)/shard_map/ppermute | solution.py:146
  8.6 4.7 %fetched.2.refs_10_.refs_6_ = bf16[1,6144,1024]{2,1,0:T(8,128)(2,1)S(1)} custom-call(bf16[1,6144,1024]{2,1,0:T(8,128)(2,1)} %source), custom_call_target="tpu_custom_call" | custom-call | flops 1024 | bytes 1024 | tf_op jit(solution)/shard_map/fetched/pallas_call | solution.py:29
  13.3 1.0 collective-permute-done.1.refs_1_
  14.3 2.2 %collective-permute-done.2.refs_7_ = bf16[48,3072]{1,0:T(8,128)(2,1)S(1)} collective-permute-done((bf16[48,3072]{1,0:T(8,128)(2,1)S(1)}, bf16[48,3072]{1,0:T(8,128)(2,1)S(1)}, u32[]{:S(2)}, u32[]{:S(2)}) %collective-permute-start.2) | collective-permute-done | bytes 294944 | tf_op jit(solution)/shard_map/ppermute | solution.py:146
  16.4 1.6 %collective-permute-start.3 = (bf16[48,3072]{1,0:T(8,128)(2,1)S(1)}, bf16[48,3072]{1,0:T(8,128)(2,1)S(1)}, u32[]{:S(2)}, u32[]{:S(2)}) collective-permute-start(bf16[48,3072]{1,0:T(8,128)(2,1)S(1)} %collective-permute-done.1.refs_1_), channel_id=1, source_target_pairs={{0,2},{2,4},{4,6},{6,7},{7,5},{5,3},{3,1},{1,0},{8,10},{10,12},{12... | collective-permute-start | bytes 884744 | tf_op jit(solution)/shard_map/ppermute | solution.py:146
  18.0 0.4 collective-permute-start.4
  18.5 4.7 %fetched.3.refs_10_.refs_7_ = bf16[1,6144,1024]{2,1,0:T(8,128)(2,1)S(1)} custom-call(bf16[1,6144,1024]{2,1,0:T(8,128)(2,1)} %source.1), custom_call_target="tpu_custom_call" | custom-call | flops 1024 | bytes 1024 | tf_op jit(solution)/shard_map/fetched/pallas_call | solution.py:29
  23.2 1.1 collective-permute-start.10
  24.3 1.0 collective-permute-start.9
  25.3 1.6 %collective-permute-done.3.refs_3_ = bf16[48,3072]{1,0:T(8,128)(2,1)S(1)} collective-permute-done((bf16[48,3072]{1,0:T(8,128)(2,1)S(1)}, bf16[48,3072]{1,0:T(8,128)(2,1)S(1)}, u32[]{:S(2)}, u32[]{:S(2)}) %collective-permute-start.3) | collective-permute-done | bytes 294944 | tf_op jit(solution)/shard_map/ppermute | solution.py:146
  26.9 2.2 %collective-permute-done.4.refs_9_ = bf16[48,3072]{1,0:T(8,128)(2,1)S(1)} collective-permute-done((bf16[48,3072]{1,0:T(8,128)(2,1)S(1)}, bf16[48,3072]{1,0:T(8,128)(2,1)S(1)}, u32[]{:S(2)}, u32[]{:S(2)}) %collective-permute-start.4) | collective-permute-done | bytes 294944 | tf_op jit(solution)/shard_map/ppermute | solution.py:146
  29.1 1.6 %collective-permute-start.5 = (bf16[48,3072]{1,0:T(8,128)(2,1)S(1)}, bf16[48,3072]{1,0:T(8,128)(2,1)S(1)}, u32[]{:S(2)}, u32[]{:S(2)}) collective-permute-start(bf16[48,3072]{1,0:T(8,128)(2,1)S(1)} %collective-permute-done.3.refs_3_), channel_id=1, source_target_pairs={{0,2},{2,4},{4,6},{6,7},{7,5},{5,3},{3,1},{1,0},{8,10},{10,12},{12... | collective-permute-start | bytes 884744 | tf_op jit(solution)/shard_map/ppermute | solution.py:146
  30.7 0.4 collective-permute-start.6
  31.1 4.3 %collective-permute-done.10.refs_4_ = bf16[48,3072]{1,0:T(8,128)(2,1)S(1)} collective-permute-done((bf16[48,3072]{1,0:T(8,128)(2,1)S(1)}, bf16[48,3072]{1,0:T(8,128)(2,1)S(1)}, u32[]{:S(2)}, u32[]{:S(2)}) %collective-permute-start.10) | collective-permute-done | bytes 294944 | tf_op jit(solution)/shard_map/ppermute | solution.py:146
  35.4 3.2 %near_gate.1.refs_11_ = f32[240,1024]{1,0:T(8,128)S(1)} custom-call(bf16[48,3072]{1,0:T(8,128)(2,1)S(1)} %get-tuple-element.162.refs_0_, bf16[48,3072]{1,0:T(8,128)(2,1)S(1)} %collective-permute-done.1.refs_1_, bf16[48,3072]{1,0:T(8,128)(2,1)S(1)} %collective-permute-done.8.refs_2_, bf16[48,3072]{1,0:T(8,128)(2,1)S(1)} %collective-permute-done.3.refs_3_, ...), custom_call_target="tpu_custom_call" | custom-call | flops 1024 | bytes 1024 | tf_op jit(solution)/shard_map/near_gate/pallas_call | solution.py:29
  38.6 1.6 %collective-permute-start.11 = (bf16[48,3072]{1,0:T(8,128)(2,1)S(1)}, bf16[48,3072]{1,0:T(8,128)(2,1)S(1)}, u32[]{:S(2)}, u32[]{:S(2)}) collective-permute-start(bf16[48,3072]{1,0:T(8,128)(2,1)S(1)} %collective-permute-done.9.refs_8_), channel_id=1, source_target_pairs={{0,2},{2,4},{4,6},{6,7},{7,5},{5,3},{3,1},{1,0},{8,10},{10,12},{12... | collective-permute-start | bytes 884744 | tf_op jit(solution)/shard_map/ppermute | solution.py:146
  40.2 0.4 collective-permute-start.12
  40.7 1.6 %collective-permute-start.13 = (bf16[48,3072]{1,0:T(8,128)(2,1)S(1)}, bf16[48,3072]{1,0:T(8,128)(2,1)S(1)}, u32[]{:S(2)}, u32[]{:S(2)}) collective-permute-start(bf16[48,3072]{1,0:T(8,128)(2,1)S(1)} %collective-permute-done.5.refs_0_), channel_id=1, source_target_pairs={{0,2},{2,4},{4,6},{6,7},{7,5},{5,3},{3,1},{1,0},{8,10},{10,12},{12... | collective-permute-start | bytes 884744 | tf_op jit(solution)/shard_map/ppermute | solution.py:146
  42.3 0.4 collective-permute-start.14
  42.7 10.8 %near_parts.1 = (bf16[48,3072]{1,0:T(8,128)(2,1)S(1)}, bf16[48,3072]{1,0:T(8,128)(2,1)S(1)}, bf16[48,3072]{1,0:T(8,128)(2,1)S(1)}, bf16[48,3072]{1,0:T(8,128)(2,...) custom-call(bf16[48,3072]{1,0:T(8,128)(2,1)S(1)} %get-tuple-element., ...), custom_call_target="tpu_custom_call" | custom-call | flops 1024 | bytes 1024 | tf_op jit(solution)/shard_map/near_parts/pallas_call | solution.py:29
  53.6 10.4 %rest.1 = (bf16[48,3072]{1,0:T(8,128)(2,1)S(1)}, bf16[48,3072]{1,0:T(8,128)(2,1)S(1)}, bf16[48,3072]{1,0:T(8,128)(2,1)S(1)}, bf16[48,3072]{1,0:T(8,128)(2,1)S(1)...) custom-call(bf16[48,3072]{1,0:T(8,128)(2,1)S(1)} %collective-permute-done.5.refs_0_, ...), custom_call_target="tpu_custom_call" | custom-call | flops 1024 | bytes 1024 | tf_op jit(solution)/shard_map/rest/pallas_call | solution.py:29
  64.0 1.6 %collective-permute-start.23 = (bf16[48,3072]{1,0:T(8,128)(2,1)S(1)}, bf16[48,3072]{1,0:T(8,128)(2,1)S(1)}, u32[]{:S(2)}, u32[]{:S(2)}) collective-permute-start(bf16[48,3072]{1,0:T(8,128)(2,1)S(1)} %get-tuple-element.147), channel_id=1, source_target_pairs={{0,2},{2,4},{4,6},{6,7},{7,5},{5,3},{3,1},{1,0},{8,10},{10,12},{12... | collective-permute-start | bytes 884744 | tf_op jit(solution)/shard_map/ppermute | solution.py:146
  65.6 0.4 collective-permute-start.24
  66.1 1.6 %collective-permute-start.15 = (bf16[48,3072]{1,0:T(8,128)(2,1)S(1)}, bf16[48,3072]{1,0:T(8,128)(2,1)S(1)}, u32[]{:S(2)}, u32[]{:S(2)}) collective-permute-start(bf16[48,3072]{1,0:T(8,128)(2,1)S(1)} %get-tuple-element.133), channel_id=1, source_target_pairs={{0,2},{2,4},{4,6},{6,7},{7,5},{5,3},{3,1},{1,0},{8,10},{10,12},{12... | collective-permute-start | bytes 884744 | tf_op jit(solution)/shard_map/ppermute | solution.py:146
  67.7 0.4 collective-permute-start.16
  68.1 5.9 %collective-permute-done.23 = bf16[48,3072]{1,0:T(8,128)(2,1)S(1)} collective-permute-done((bf16[48,3072]{1,0:T(8,128)(2,1)S(1)}, bf16[48,3072]{1,0:T(8,128)(2,1)S(1)}, u32[]{:S(2)}, u32[]{:S(2)}) %collective-permute-start.23) | collective-permute-done | bytes 294944 | tf_op jit(solution)/shard_map/ppermute | solution.py:146
  74.0 1.6 %collective-permute-done.24 = bf16[48,3072]{1,0:T(8,128)(2,1)S(1)} collective-permute-done((bf16[48,3072]{1,0:T(8,128)(2,1)S(1)}, bf16[48,3072]{1,0:T(8,128)(2,1)S(1)}, u32[]{:S(2)}, u32[]{:S(2)}) %collective-permute-start.24) | collective-permute-done | bytes 294944 | tf_op jit(solution)/shard_map/ppermute | solution.py:146
  75.6 0.1 add_convert_fusion.4
  75.7 0.4 collective-permute-start.26
  76.2 0.1 add_convert_fusion.5
  76.2 1.7 %collective-permute-start.25 = (bf16[48,3072]{1,0:T(8,128)(2,1)S(1)}, bf16[48,3072]{1,0:T(8,128)(2,1)S(1)}, u32[]{:S(2)}, u32[]{:S(2)}) collective-permute-start(bf16[48,3072]{1,0:T(8,128)(2,1)S(1)} %add_convert_fusion.5), channel_id=1, source_target_pairs={{0,2},{2,4},{4,6},{6,7},{7,5},{5,3},{3,1},{1,0},{8,10},{10,12},{12... | collective-permute-start | bytes 884744 | tf_op jit(solution)/shard_map/ppermute | solution.py:146
  77.9 2.4 %collective-permute-done.15 = bf16[48,3072]{1,0:T(8,128)(2,1)S(1)} collective-permute-done((bf16[48,3072]{1,0:T(8,128)(2,1)S(1)}, bf16[48,3072]{1,0:T(8,128)(2,1)S(1)}, u32[]{:S(2)}, u32[]{:S(2)}) %collective-permute-start.15) | collective-permute-done | bytes 294944 | tf_op jit(solution)/shard_map/ppermute | solution.py:146
  80.3 1.6 %collective-permute-done.16 = bf16[48,3072]{1,0:T(8,128)(2,1)S(1)} collective-permute-done((bf16[48,3072]{1,0:T(8,128)(2,1)S(1)}, bf16[48,3072]{1,0:T(8,128)(2,1)S(1)}, u32[]{:S(2)}, u32[]{:S(2)}) %collective-permute-start.16) | collective-permute-done | bytes 294944 | tf_op jit(solution)/shard_map/ppermute | solution.py:146
  82.0 0.1 add_convert_fusion.10
  82.0 0.4 collective-permute-start.18
  82.5 1.7 %collective-permute-start.17 = (bf16[48,3072]{1,0:T(8,128)(2,1)S(1)}, bf16[48,3072]{1,0:T(8,128)(2,1)S(1)}, u32[]{:S(2)}, u32[]{:S(2)}) collective-permute-start(bf16[48,3072]{1,0:T(8,128)(2,1)S(1)} %add_convert_fusion.11), channel_id=1, source_target_pairs={{0,2},{2,4},{4,6},{6,7},{7,5},{5,3},{3,1},{1,0},{8,10},{10,12},{12... | collective-permute-start | bytes 884744 | tf_op jit(solution)/shard_map/ppermute | solution.py:146
  84.3 4.0 %collective-permute-done.26 = bf16[48,3072]{1,0:T(8,128)(2,1)S(1)} collective-permute-done((bf16[48,3072]{1,0:T(8,128)(2,1)S(1)}, bf16[48,3072]{1,0:T(8,128)(2,1)S(1)}, u32[]{:S(2)}, u32[]{:S(2)}) %collective-permute-start.26) | collective-permute-done | bytes 294944 | tf_op jit(solution)/shard_map/ppermute | solution.py:146
  88.4 0.4 collective-permute-start.28
  88.8 5.8 %collective-permute-done.18 = bf16[48,3072]{1,0:T(8,128)(2,1)S(1)} collective-permute-done((bf16[48,3072]{1,0:T(8,128)(2,1)S(1)}, bf16[48,3072]{1,0:T(8,128)(2,1)S(1)}, u32[]{:S(2)}, u32[]{:S(2)}) %collective-permute-start.18) | collective-permute-done | bytes 294944 | tf_op jit(solution)/shard_map/ppermute | solution.py:146
  94.7 0.4 collective-permute-start.20
  95.2 1.7 %collective-permute-start.19 = (bf16[48,3072]{1,0:T(8,128)(2,1)S(1)}, bf16[48,3072]{1,0:T(8,128)(2,1)S(1)}, u32[]{:S(2)}, u32[]{:S(2)}) collective-permute-start(bf16[48,3072]{1,0:T(8,128)(2,1)S(1)} %add_convert_fusion.9), channel_id=1, source_target_pairs={{0,2},{2,4},{4,6},{6,7},{7,5},{5,3},{3,1},{1,0},{8,10},{10,12},{12... | collective-permute-start | bytes 884744 | tf_op jit(solution)/shard_map/ppermute | solution.py:146
  97.0 2.1 %collective-permute-start.27 = (bf16[48,3072]{1,0:T(8,128)(2,1)S(1)}, bf16[48,3072]{1,0:T(8,128)(2,1)S(1)}, u32[]{:S(2)}, u32[]{:S(2)}) collective-permute-start(bf16[48,3072]{1,0:T(8,128)(2,1)S(1)} %add_convert_fusion.3), channel_id=1, source_target_pairs={{0,2},{2,4},{4,6},{6,7},{7,5},{5,3},{3,1},{1,0},{8,10},{10,12},{12... | collective-permute-start | bytes 884744 | tf_op jit(solution)/shard_map/ppermute | solution.py:146
  99.1 5.3 %collective-permute-done.20 = bf16[48,3072]{1,0:T(8,128)(2,1)S(1)} collective-permute-done((bf16[48,3072]{1,0:T(8,128)(2,1)S(1)}, bf16[48,3072]{1,0:T(8,128)(2,1)S(1)}, u32[]{:S(2)}, u32[]{:S(2)}) %collective-permute-start.20) | collective-permute-done | bytes 294944 | tf_op jit(solution)/shard_map/ppermute | solution.py:146
  104.4 0.4 collective-permute-start.22
  104.9 0.1 add_convert_fusion.7
  104.9 1.7 %collective-permute-start.21 = (bf16[48,3072]{1,0:T(8,128)(2,1)S(1)}, bf16[48,3072]{1,0:T(8,128)(2,1)S(1)}, u32[]{:S(2)}, u32[]{:S(2)}) collective-permute-start(bf16[48,3072]{1,0:T(8,128)(2,1)S(1)} %add_convert_fusion.7), channel_id=1, source_target_pairs={{0,2},{2,4},{4,6},{6,7},{7,5},{5,3},{3,1},{1,0},{8,10},{10,12},{12... | collective-permute-start | bytes 884744 | tf_op jit(solution)/shard_map/ppermute | solution.py:146
  106.7 4.6 %collective-permute-done.22 = bf16[48,3072]{1,0:T(8,128)(2,1)S(1)} collective-permute-done((bf16[48,3072]{1,0:T(8,128)(2,1)S(1)}, bf16[48,3072]{1,0:T(8,128)(2,1)S(1)}, u32[]{:S(2)}, u32[]{:S(2)}) %collective-permute-start.22) | collective-permute-done | bytes 294944 | tf_op jit(solution)/shard_map/ppermute | solution.py:146
  111.2 0.5 collective-permute-done.21
  111.7 0.2 add_convert_fusion
  112.0 0.1 collective-permute-start.29
  112.1 0.1 fusion.14
  112.2 1.5 %collective-permute-done.29 = bf16[24,6144]{1,0:T(8,128)(2,1)S(1)} collective-permute-done((bf16[24,6144]{1,0:T(8,128)(2,1)S(1)}, bf16[24,6144]{1,0:T(8,128)(2,1)S(1)}, u32[]{:S(2)}, u32[]{:S(2)}) %collective-permute-start.29) | collective-permute-done | bytes 294944 | tf_op jit(solution)/shard_map/ppermute | solution.py:237
  113.6 1.3 %fusion = bf16[64,6144]{1,0:T(8,128)(2,1)} fusion(bf16[1,24,6144]{2,1,0:T(8,128)(2,1)S(1)} %bitcast.22, bf16[1,24,6144]{2,1,0:T(8,128)(2,1)S(1)} %get-tuple-element.159, bf16[2,64]{1,0:T(2,128)(2,1)S(1)} %bitcast.23, s32[2,64]{1,0:T(2,128)S(1)} %subtract_bitcast_fusion, pred[2,64]{1,0:T(4,128)(4,1)S(1)} %get-tuple-element.165), kind=kOutput, calls=%fused_computation.1 | convolution fusion | flops 38052864 | bytes 1377152 | tf_op jit(solution)/shard_map/wcr,wcd->rd/dot_general | solution.py:239
  (41 shorter events, 0.7 us)
Async XLA Ops:
  0.0 1.4 %copy-start = (bf16[64,6144]{1,0:T(8,128)(2,1)S(1)}, bf16[64,6144]{1,0:T(8,128)(2,1)}, u32[]{:S(2)}) copy-start(bf16[64,6144]{1,0:T(8,128)(2,1)} %param.6) | copy-start | bytes 2359300
  1.7 1.7 %collective-permute-start = (bf16[24,6144]{1,0:T(8,128)(2,1)S(1)}, bf16[24,6144]{1,0:T(8,128)(2,1)S(1)}, u32[]{:S(2)}, u32[]{:S(2)}) collective-permute-start(bf16[24,6144]{1,0:T(8,128)(2,1)S(1)} %get-tuple-element.164), channel_id=1, source_target_pairs={{0,8},{8,0},{1,9},{9,1},{2,10},{10,2},{3,11},{11,3},{4,12},{12,4},... | collective-permute-start | bytes 884744 | tf_op jit(solution)/shard_map/ppermute | solution.py:160
  3.5 10.7 %collective-permute-start.1 = (bf16[48,3072]{1,0:T(8,128)(2,1)S(1)}, bf16[48,3072]{1,0:T(8,128)(2,1)S(1)}, u32[]{:S(2)}, u32[]{:S(2)}) collective-permute-start(bf16[48,3072]{1,0:T(8,128)(2,1)S(1)} %get-tuple-element.162.refs_0_), channel_id=1, source_target_pairs={{0,2},{2,4},{4,6},{6,7},{7,5},{5,3},{3,1},{1,0},{8,10},{10,12},{12... | collective-permute-start | bytes 884744 | tf_op jit(solution)/shard_map/ppermute | solution.py:146
  6.5 9.9 %collective-permute-start.2 = (bf16[48,3072]{1,0:T(8,128)(2,1)S(1)}, bf16[48,3072]{1,0:T(8,128)(2,1)S(1)}, u32[]{:S(2)}, u32[]{:S(2)}) collective-permute-start(bf16[48,3072]{1,0:T(8,128)(2,1)S(1)} %get-tuple-element.161.refs_5_), channel_id=1, source_target_pairs={{2,0},{4,2},{6,4},{7,6},{5,7},{3,5},{1,3},{0,1},{10,8},{12,10},{14... | collective-permute-start | bytes 884744 | tf_op jit(solution)/shard_map/ppermute | solution.py:146
  6.6 16.6 %collective-permute-start.7 = (bf16[48,3072]{1,0:T(8,128)(2,1)S(1)}, bf16[48,3072]{1,0:T(8,128)(2,1)S(1)}, u32[]{:S(2)}, u32[]{:S(2)}) collective-permute-start(bf16[48,3072]{1,0:T(8,128)(2,1)S(1)} %get-tuple-element.161.refs_5_), channel_id=1, source_target_pairs={{0,2},{2,4},{4,6},{6,7},{7,5},{5,3},{3,1},{1,0},{8,10},{10,12},{12... | collective-permute-start | bytes 884744 | tf_op jit(solution)/shard_map/ppermute | solution.py:146
  8.6 14.6 %collective-permute-start.8 = (bf16[48,3072]{1,0:T(8,128)(2,1)S(1)}, bf16[48,3072]{1,0:T(8,128)(2,1)S(1)}, u32[]{:S(2)}, u32[]{:S(2)}) collective-permute-start(bf16[48,3072]{1,0:T(8,128)(2,1)S(1)} %get-tuple-element.162.refs_0_), channel_id=1, source_target_pairs={{2,0},{4,2},{6,4},{7,6},{5,7},{3,5},{1,3},{0,1},{10,8},{12,10},{14... | collective-permute-start | bytes 884744 | tf_op jit(solution)/shard_map/ppermute | solution.py:146
  13.3 22.1 %copy-start.2 = (bf16[1,6144,1024]{2,1,0:T(8,128)(2,1)}, bf16[1,6144,1024]{2,1,0:T(8,128)(2,1)S(1)}, u32[]{:S(2)}) copy-start(bf16[1,6144,1024]{2,1,0:T(8,128)(2,1)S(1)} %fetched.2.refs_10_.refs_6_) | copy-start | bytes 37748740
  16.4 10.5 %collective-permute-start.3 = (bf16[48,3072]{1,0:T(8,128)(2,1)S(1)}, bf16[48,3072]{1,0:T(8,128)(2,1)S(1)}, u32[]{:S(2)}, u32[]{:S(2)}) collective-permute-start(bf16[48,3072]{1,0:T(8,128)(2,1)S(1)} %collective-permute-done.1.refs_1_), channel_id=1, source_target_pairs={{0,2},{2,4},{4,6},{6,7},{7,5},{5,3},{3,1},{1,0},{8,10},{10,12},{12... | collective-permute-start | bytes 884744 | tf_op jit(solution)/shard_map/ppermute | solution.py:146
  18.0 11.1 %collective-permute-start.4 = (bf16[48,3072]{1,0:T(8,128)(2,1)S(1)}, bf16[48,3072]{1,0:T(8,128)(2,1)S(1)}, u32[]{:S(2)}, u32[]{:S(2)}) collective-permute-start(bf16[48,3072]{1,0:T(8,128)(2,1)S(1)} %collective-permute-done.2.refs_7_), channel_id=1, source_target_pairs={{2,0},{4,2},{6,4},{7,6},{5,7},{3,5},{1,3},{0,1},{10,8},{12,10},{14... | collective-permute-start | bytes 884744 | tf_op jit(solution)/shard_map/ppermute | solution.py:146
  23.2 12.2 %collective-permute-start.10 = (bf16[48,3072]{1,0:T(8,128)(2,1)S(1)}, bf16[48,3072]{1,0:T(8,128)(2,1)S(1)}, u32[]{:S(2)}, u32[]{:S(2)}) collective-permute-start(bf16[48,3072]{1,0:T(8,128)(2,1)S(1)} %collective-permute-done.8.refs_2_), channel_id=1, source_target_pairs={{2,0},{4,2},{6,4},{7,6},{5,7},{3,5},{1,3},{0,1},{10,8},{12,10},{14... | collective-permute-start | bytes 884744 | tf_op jit(solution)/shard_map/ppermute | solution.py:146
  24.3 11.1 %collective-permute-start.9 = (bf16[48,3072]{1,0:T(8,128)(2,1)S(1)}, bf16[48,3072]{1,0:T(8,128)(2,1)S(1)}, u32[]{:S(2)}, u32[]{:S(2)}) collective-permute-start(bf16[48,3072]{1,0:T(8,128)(2,1)S(1)} %collective-permute-done.7.refs_6_), channel_id=1, source_target_pairs={{0,2},{2,4},{4,6},{6,7},{7,5},{5,3},{3,1},{1,0},{8,10},{10,12},{12... | collective-permute-start | bytes 884744 | tf_op jit(solution)/shard_map/ppermute | solution.py:146
  29.1 11.6 %collective-permute-start.5 = (bf16[48,3072]{1,0:T(8,128)(2,1)S(1)}, bf16[48,3072]{1,0:T(8,128)(2,1)S(1)}, u32[]{:S(2)}, u32[]{:S(2)}) collective-permute-start(bf16[48,3072]{1,0:T(8,128)(2,1)S(1)} %collective-permute-done.3.refs_3_), channel_id=1, source_target_pairs={{0,2},{2,4},{4,6},{6,7},{7,5},{5,3},{3,1},{1,0},{8,10},{10,12},{12... | collective-permute-start | bytes 884744 | tf_op jit(solution)/shard_map/ppermute | solution.py:146
  30.7 10.0 %collective-permute-start.6 = (bf16[48,3072]{1,0:T(8,128)(2,1)S(1)}, bf16[48,3072]{1,0:T(8,128)(2,1)S(1)}, u32[]{:S(2)}, u32[]{:S(2)}) collective-permute-start(bf16[48,3072]{1,0:T(8,128)(2,1)S(1)} %collective-permute-done.4.refs_9_), channel_id=1, source_target_pairs={{2,0},{4,2},{6,4},{7,6},{5,7},{3,5},{1,3},{0,1},{10,8},{12,10},{14... | collective-permute-start | bytes 884744 | tf_op jit(solution)/shard_map/ppermute | solution.py:146
  38.6 14.9 %copy-start.3 = (bf16[1,6144,1024]{2,1,0:T(8,128)(2,1)S(1)}, bf16[1,6144,1024]{2,1,0:T(8,128)(2,1)}, u32[]{:S(2)}) copy-start(bf16[1,6144,1024]{2,1,0:T(8,128)(2,1)} %copy-done.2) | copy-start | bytes 37748740
  38.6 14.9 %collective-permute-start.11 = (bf16[48,3072]{1,0:T(8,128)(2,1)S(1)}, bf16[48,3072]{1,0:T(8,128)(2,1)S(1)}, u32[]{:S(2)}, u32[]{:S(2)}) collective-permute-start(bf16[48,3072]{1,0:T(8,128)(2,1)S(1)} %collective-permute-done.9.refs_8_), channel_id=1, source_target_pairs={{0,2},{2,4},{4,6},{6,7},{7,5},{5,3},{3,1},{1,0},{8,10},{10,12},{12... | collective-permute-start | bytes 884744 | tf_op jit(solution)/shard_map/ppermute | solution.py:146
  40.2 13.3 %collective-permute-start.12 = (bf16[48,3072]{1,0:T(8,128)(2,1)S(1)}, bf16[48,3072]{1,0:T(8,128)(2,1)S(1)}, u32[]{:S(2)}, u32[]{:S(2)}) collective-permute-start(bf16[48,3072]{1,0:T(8,128)(2,1)S(1)} %collective-permute-done.10.refs_4_), channel_id=1, source_target_pairs={{2,0},{4,2},{6,4},{7,6},{5,7},{3,5},{1,3},{0,1},{10,8},{12,10},{14... | collective-permute-start | bytes 884744 | tf_op jit(solution)/shard_map/ppermute | solution.py:146
  40.7 12.8 %collective-permute-start.13 = (bf16[48,3072]{1,0:T(8,128)(2,1)S(1)}, bf16[48,3072]{1,0:T(8,128)(2,1)S(1)}, u32[]{:S(2)}, u32[]{:S(2)}) collective-permute-start(bf16[48,3072]{1,0:T(8,128)(2,1)S(1)} %collective-permute-done.5.refs_0_), channel_id=1, source_target_pairs={{0,2},{2,4},{4,6},{6,7},{7,5},{5,3},{3,1},{1,0},{8,10},{10,12},{12... | collective-permute-start | bytes 884744 | tf_op jit(solution)/shard_map/ppermute | solution.py:146
  42.3 11.3 %collective-permute-start.14 = (bf16[48,3072]{1,0:T(8,128)(2,1)S(1)}, bf16[48,3072]{1,0:T(8,128)(2,1)S(1)}, u32[]{:S(2)}, u32[]{:S(2)}) collective-permute-start(bf16[48,3072]{1,0:T(8,128)(2,1)S(1)} %collective-permute-done.6.refs_4_), channel_id=1, source_target_pairs={{2,0},{4,2},{6,4},{7,6},{5,7},{3,5},{1,3},{0,1},{10,8},{12,10},{14... | collective-permute-start | bytes 884744 | tf_op jit(solution)/shard_map/ppermute | solution.py:146
  53.5 58.5 %copy-start.4 = (s32[64,2]{0,1:T(2,128)S(1)}, s32[64,2]{0,1:T(2,128)}, u32[]{:S(2)}) copy-start(s32[64,2]{0,1:T(2,128)} %param.7) | copy-start | bytes 1540
  53.6 58.5 %copy-start.5 = (f32[64,2]{0,1:T(2,128)S(1)}, f32[64,2]{0,1:T(2,128)}, u32[]{:S(2)}) copy-start(f32[64,2]{0,1:T(2,128)} %param.8) | copy-start | bytes 1540
  53.6 61.3 %copy-start.1 = (bf16[64,6144]{1,0:T(8,128)(2,1)S(1)}, bf16[64,6144]{1,0:T(8,128)(2,1)}, u32[]{:S(2)}) copy-start(bf16[64,6144]{1,0:T(8,128)(2,1)} %param.6) | copy-start | bytes 2359300
  64.0 10.0 %collective-permute-start.23 = (bf16[48,3072]{1,0:T(8,128)(2,1)S(1)}, bf16[48,3072]{1,0:T(8,128)(2,1)S(1)}, u32[]{:S(2)}, u32[]{:S(2)}) collective-permute-start(bf16[48,3072]{1,0:T(8,128)(2,1)S(1)} %get-tuple-element.147), channel_id=1, source_target_pairs={{0,2},{2,4},{4,6},{6,7},{7,5},{5,3},{3,1},{1,0},{8,10},{10,12},{12... | collective-permute-start | bytes 884744 | tf_op jit(solution)/shard_map/ppermute | solution.py:146
  65.6 10.0 %collective-permute-start.24 = (bf16[48,3072]{1,0:T(8,128)(2,1)S(1)}, bf16[48,3072]{1,0:T(8,128)(2,1)S(1)}, u32[]{:S(2)}, u32[]{:S(2)}) collective-permute-start(bf16[48,3072]{1,0:T(8,128)(2,1)S(1)} %get-tuple-element.148), channel_id=1, source_target_pairs={{2,0},{4,2},{6,4},{7,6},{5,7},{3,5},{1,3},{0,1},{10,8},{12,10},{14... | collective-permute-start | bytes 884744 | tf_op jit(solution)/shard_map/ppermute | solution.py:146
  66.1 14.2 %collective-permute-start.15 = (bf16[48,3072]{1,0:T(8,128)(2,1)S(1)}, bf16[48,3072]{1,0:T(8,128)(2,1)S(1)}, u32[]{:S(2)}, u32[]{:S(2)}) collective-permute-start(bf16[48,3072]{1,0:T(8,128)(2,1)S(1)} %get-tuple-element.133), channel_id=1, source_target_pairs={{0,2},{2,4},{4,6},{6,7},{7,5},{5,3},{3,1},{1,0},{8,10},{10,12},{12... | collective-permute-start | bytes 884744 | tf_op jit(solution)/shard_map/ppermute | solution.py:146
  67.7 14.2 %collective-permute-start.16 = (bf16[48,3072]{1,0:T(8,128)(2,1)S(1)}, bf16[48,3072]{1,0:T(8,128)(2,1)S(1)}, u32[]{:S(2)}, u32[]{:S(2)}) collective-permute-start(bf16[48,3072]{1,0:T(8,128)(2,1)S(1)} %get-tuple-element.134), channel_id=1, source_target_pairs={{2,0},{4,2},{6,4},{7,6},{5,7},{3,5},{1,3},{0,1},{10,8},{12,10},{14... | collective-permute-start | bytes 884744 | tf_op jit(solution)/shard_map/ppermute | solution.py:146
  75.7 12.6 %collective-permute-start.26 = (bf16[48,3072]{1,0:T(8,128)(2,1)S(1)}, bf16[48,3072]{1,0:T(8,128)(2,1)S(1)}, u32[]{:S(2)}, u32[]{:S(2)}) collective-permute-start(bf16[48,3072]{1,0:T(8,128)(2,1)S(1)} %add_convert_fusion.4), channel_id=1, source_target_pairs={{2,0},{4,2},{6,4},{7,6},{5,7},{3,5},{1,3},{0,1},{10,8},{12,10},{14... | collective-permute-start | bytes 884744 | tf_op jit(solution)/shard_map/ppermute | solution.py:146
  76.2 12.1 %collective-permute-start.25 = (bf16[48,3072]{1,0:T(8,128)(2,1)S(1)}, bf16[48,3072]{1,0:T(8,128)(2,1)S(1)}, u32[]{:S(2)}, u32[]{:S(2)}) collective-permute-start(bf16[48,3072]{1,0:T(8,128)(2,1)S(1)} %add_convert_fusion.5), channel_id=1, source_target_pairs={{0,2},{2,4},{4,6},{6,7},{7,5},{5,3},{3,1},{1,0},{8,10},{10,12},{12... | collective-permute-start | bytes 884744 | tf_op jit(solution)/shard_map/ppermute | solution.py:146
  82.0 12.6 %collective-permute-start.18 = (bf16[48,3072]{1,0:T(8,128)(2,1)S(1)}, bf16[48,3072]{1,0:T(8,128)(2,1)S(1)}, u32[]{:S(2)}, u32[]{:S(2)}) collective-permute-start(bf16[48,3072]{1,0:T(8,128)(2,1)S(1)} %add_convert_fusion.10), channel_id=1, source_target_pairs={{2,0},{4,2},{6,4},{7,6},{5,7},{3,5},{1,3},{0,1},{10,8},{12,10},{14... | collective-permute-start | bytes 884744 | tf_op jit(solution)/shard_map/ppermute | solution.py:146
  82.5 12.1 %collective-permute-start.17 = (bf16[48,3072]{1,0:T(8,128)(2,1)S(1)}, bf16[48,3072]{1,0:T(8,128)(2,1)S(1)}, u32[]{:S(2)}, u32[]{:S(2)}) collective-permute-start(bf16[48,3072]{1,0:T(8,128)(2,1)S(1)} %add_convert_fusion.11), channel_id=1, source_target_pairs={{0,2},{2,4},{4,6},{6,7},{7,5},{5,3},{3,1},{1,0},{8,10},{10,12},{12... | collective-permute-start | bytes 884744 | tf_op jit(solution)/shard_map/ppermute | solution.py:146
  88.4 18.3 %collective-permute-start.28 = (bf16[48,3072]{1,0:T(8,128)(2,1)S(1)}, bf16[48,3072]{1,0:T(8,128)(2,1)S(1)}, u32[]{:S(2)}, u32[]{:S(2)}) collective-permute-start(bf16[48,3072]{1,0:T(8,128)(2,1)S(1)} %add_convert_fusion.2), channel_id=1, source_target_pairs={{2,0},{4,2},{6,4},{7,6},{5,7},{3,5},{1,3},{0,1},{10,8},{12,10},{14... | collective-permute-start | bytes 884744 | tf_op jit(solution)/shard_map/ppermute | solution.py:146
  94.7 9.7 %collective-permute-start.20 = (bf16[48,3072]{1,0:T(8,128)(2,1)S(1)}, bf16[48,3072]{1,0:T(8,128)(2,1)S(1)}, u32[]{:S(2)}, u32[]{:S(2)}) collective-permute-start(bf16[48,3072]{1,0:T(8,128)(2,1)S(1)} %add_convert_fusion.8), channel_id=1, source_target_pairs={{2,0},{4,2},{6,4},{7,6},{5,7},{3,5},{1,3},{0,1},{10,8},{12,10},{14... | collective-permute-start | bytes 884744 | tf_op jit(solution)/shard_map/ppermute | solution.py:146
  95.2 9.2 %collective-permute-start.19 = (bf16[48,3072]{1,0:T(8,128)(2,1)S(1)}, bf16[48,3072]{1,0:T(8,128)(2,1)S(1)}, u32[]{:S(2)}, u32[]{:S(2)}) collective-permute-start(bf16[48,3072]{1,0:T(8,128)(2,1)S(1)} %add_convert_fusion.9), channel_id=1, source_target_pairs={{0,2},{2,4},{4,6},{6,7},{7,5},{5,3},{3,1},{1,0},{8,10},{10,12},{12... | collective-permute-start | bytes 884744 | tf_op jit(solution)/shard_map/ppermute | solution.py:146
  97.0 9.7 %collective-permute-start.27 = (bf16[48,3072]{1,0:T(8,128)(2,1)S(1)}, bf16[48,3072]{1,0:T(8,128)(2,1)S(1)}, u32[]{:S(2)}, u32[]{:S(2)}) collective-permute-start(bf16[48,3072]{1,0:T(8,128)(2,1)S(1)} %add_convert_fusion.3), channel_id=1, source_target_pairs={{0,2},{2,4},{4,6},{6,7},{7,5},{5,3},{3,1},{1,0},{8,10},{10,12},{12... | collective-permute-start | bytes 884744 | tf_op jit(solution)/shard_map/ppermute | solution.py:146
  104.4 6.8 %collective-permute-start.22 = (bf16[48,3072]{1,0:T(8,128)(2,1)S(1)}, bf16[48,3072]{1,0:T(8,128)(2,1)S(1)}, u32[]{:S(2)}, u32[]{:S(2)}) collective-permute-start(bf16[48,3072]{1,0:T(8,128)(2,1)S(1)} %add_convert_fusion.6), channel_id=1, source_target_pairs={{2,0},{4,2},{6,4},{7,6},{5,7},{3,5},{1,3},{0,1},{10,8},{12,10},{14... | collective-permute-start | bytes 884744 | tf_op jit(solution)/shard_map/ppermute | solution.py:146
  104.9 6.8 %collective-permute-start.21 = (bf16[48,3072]{1,0:T(8,128)(2,1)S(1)}, bf16[48,3072]{1,0:T(8,128)(2,1)S(1)}, u32[]{:S(2)}, u32[]{:S(2)}) collective-permute-start(bf16[48,3072]{1,0:T(8,128)(2,1)S(1)} %add_convert_fusion.7), channel_id=1, source_target_pairs={{0,2},{2,4},{4,6},{6,7},{7,5},{5,3},{3,1},{1,0},{8,10},{10,12},{12... | collective-permute-start | bytes 884744 | tf_op jit(solution)/shard_map/ppermute | solution.py:146
  112.0 1.6 %collective-permute-start.29 = (bf16[24,6144]{1,0:T(8,128)(2,1)S(1)}, bf16[24,6144]{1,0:T(8,128)(2,1)S(1)}, u32[]{:S(2)}, u32[]{:S(2)}) collective-permute-start(bf16[24,6144]{1,0:T(8,128)(2,1)S(1)} %get-tuple-element.160), channel_id=1, source_target_pairs={{0,8},{8,0},{1,9},{9,1},{2,10},{10,2},{3,11},{11,3},{4,12},{12,4},... | collective-permute-start | bytes 884744 | tf_op jit(solution)/shard_map/ppermute | solution.py:237

commit v12 on v11

--- a/solution.py
+++ b/solution.py
@@ -38,11 +38,11 @@
     )(*[in_vmem(array) if memory == pltpu.VMEM else in_hbm(array) for array, memory in operands])
 
 
-def row_copies(source, target, done):
-    rows = source.shape[1] // COPIES
+def row_copies(source, target, done, column=0):
+    rows, width = source.shape[1] // COPIES, target.shape[2]
     return [
         pltpu.make_async_copy(
-            source.at[:, pl.ds(i * rows, rows)], target.at[:, pl.ds(i * rows, rows)], done.at[i]
+            source.at[:, pl.ds(i * rows, rows), pl.ds(column, width)], target.at[:, pl.ds(i * rows, rows)], done.at[i]
         )
         for i in range(COPIES)
     ]
@@ -56,9 +56,9 @@
         copy.wait()
 
 
-def fetched(weights):
+def fetched(weights, width):
     operands = [(weights, pltpu.HBM)]
-    outs = [(weights.shape, weights.dtype)]
+    outs = [((*weights.shape[:2], width), weights.dtype)]
     return call(fill_kernel, "fetched", operands, outs, [pltpu.SemaphoreType.DMA((COPIES,))], 0)[0]
 
 
@@ -85,39 +85,43 @@
 
 def add_down(hidden, down, outs):
     size, width = outs[0].shape
-    count = len(outs) // 2
-    depth = width if size * count <= 512 else TILE
-    for at in range(0, down.shape[2], depth):
+    depth = width if size * len(outs) <= 512 else TILE
+    for at in range(0, width, depth):
         part = jnp.dot(hidden, down[0, :, at:at + depth], preferred_element_type=jnp.float32).astype(jnp.bfloat16)
-        chunk, column = divmod(at, width)
-        for b in range(count):
-            outs[count * chunk + b][:, column:column + depth] = part[b * size:(b + 1) * size]
-
-
-def near_kernel(count, *refs):
-    chunks, (w_up, gate, w_down) = (refs[:count], refs[count:2 * count]), refs[2 * count:2 * count + 3]
-    outs, (up, down, done) = refs[2 * count + 3:4 * count + 3], refs[4 * count + 3:]
-    copies = row_copies(w_down, down, done)
-    for copy in copies:
-        copy.start()
-    accumulate(chunks, [(w_up, up)])
-    hidden = activated(gate[...], up[...])
-    for copy in copies:
-        copy.wait()
-    add_down(hidden, down, outs)
+        for b, out in enumerate(outs):
+            out[:, at:at + depth] = part[b * size:(b + 1) * size]
+
+
+def up_kernel(count, *refs):
+    chunks, (weights, gate, out, total) = (refs[:count], refs[count:2 * count]), refs[2 * count:]
+    accumulate(chunks, [(weights, total)])
+    out[...] = activated(gate[...], total[...])
 
 
 def rest_kernel(*refs):
-    chunks, (w_gate, w_up, w_down), outs = (refs[:3], refs[3:6]), refs[6:9], refs[9:15]
-    gate, up, down, done = refs[15:]
-    copies = row_copies(w_down, down, done)
+    chunks, (w_gate, w_up, down_0, w_down), outs = (refs[:3], refs[3:6]), refs[6:10], refs[10:16]
+    gate, up, down_1, done = refs[16:]
+    copies = row_copies(w_down, down_1, done, down_1.shape[2])
     for copy in copies:
         copy.start()
     accumulate(chunks, [(w_gate, gate), (w_up, up)])
     hidden = activated(gate[...], up[...])
+    add_down(hidden, down_0, outs[:3])
     for copy in copies:
         copy.wait()
-    add_down(hidden, down, outs)
+    add_down(hidden, down_1, outs[3:])
+
+
+def near_down_kernel(hidden, down_0, w_down, *refs):
+    outs, (down_1, done) = refs[:-2], refs[-2:]
+    count = len(outs) // 2
+    copies = row_copies(w_down, down_1, done, down_1.shape[2])
+    for copy in copies:
+        copy.start()
+    add_down(hidden[...], down_0, outs[:count])
+    for copy in copies:
+        copy.wait()
+    add_down(hidden[...], down_1, outs[count:])
 
 
 def routing(expert_ids, gate_probs, experts, slots):
@@ -169,10 +173,10 @@
 
     a = step(halves[0], halves[1])
     b = step(halves[1], halves[0])
-    gate_here = fetched(w_gate)
+    gate_here = fetched(w_gate, units)
     a, gate_here = tied(a, gate_here)
     a, w_up = tied(a, w_up)
-    up_here = fetched(w_up)
+    up_here = fetched(w_up, units)
     b, up_here = tied(b, up_here)
     arrived(a, b)
     for _ in range(half - 3):
@@ -193,23 +197,28 @@
     rest = [[a[0], b[1]], [b[0], a[1]]]
     a, near_gate = tied(a, near_gate)
     far = step(*a)
-    down_scratch = [pltpu.VMEM(w_down.shape, jnp.bfloat16), pltpu.SemaphoreType.DMA((COPIES,))]
-    down_room = units * width * 2
-    near_parts = call(
-        functools.partial(near_kernel, count), "near_parts",
-        near + [(up_here, pltpu.VMEM), (near_gate, pltpu.VMEM), (w_down, pltpu.HBM)],
-        [((size, mid_col), jnp.bfloat16)] * (2 * count), [pltpu.VMEM((rows, units), jnp.float32)] + down_scratch,
-        down_room + rows * units * 16,
-    )
+    near_hidden, = call(
+        functools.partial(up_kernel, count), "near_up",
+        near + [(up_here, pltpu.VMEM), (near_gate, pltpu.VMEM)], [((rows, units), jnp.bfloat16)],
+        [pltpu.VMEM((rows, units), jnp.float32)], rows * units * 16,
+    )
+    near_hidden, w_down = tied(near_hidden, w_down)
+    down_here = fetched(w_down, mid_col)
     rest = [rest[chunk] + [far[chunk]] for chunk in range(2)]
-    rest, near_parts = tied(rest, near_parts)
+    rest, down_here = tied(rest, down_here)
+    down_scratch = [pltpu.VMEM(down_here.shape, jnp.bfloat16), pltpu.SemaphoreType.DMA((COPIES,))]
+    down_room = units * width
     rest_parts = call(
         rest_kernel, "rest",
         [(block, pltpu.VMEM) for chunk in rest for block in chunk]
-        + [(gate_here, pltpu.VMEM), (up_here, pltpu.VMEM), (w_down, pltpu.HBM)],
+        + [(gate_here, pltpu.VMEM), (up_here, pltpu.VMEM), (down_here, pltpu.VMEM), (w_down, pltpu.HBM)],
         [((size, mid_col), jnp.bfloat16)] * 6,
         [pltpu.VMEM((3 * size, units), jnp.float32)] * 2 + down_scratch,
         down_room + 3 * size * units * 16,
+    )
+    near_parts = call(
+        near_down_kernel, "near_down", [(near_hidden, pltpu.VMEM), (down_here, pltpu.VMEM), (w_down, pltpu.HBM)],
+        [((size, mid_col), jnp.bfloat16)] * (2 * count), down_scratch, down_room + rows * TILE * 12,
     )
 
     def part_of(chunk, distance, side):

time: 115 us -> 112 us (0.974)
  waiting for transfers between devices: 45.6 us -> 43.5 us
    ppermute x14, starting transfers between devices: 24.6 us -> 6.48 us  [step(): lax.ppermute(to_right, 'tensor', right)]
    ppermute x14, starting transfers between devices: 5.91 us -> 23.7 us  [step(): lax.ppermute(to_left, 'tensor', left)]
    ppermute x14, waiting for transfers between devices: 31.6 us -> 23 us  [step(): lax.ppermute(to_left, 'tensor', left)]
    ppermute x14, waiting for transfers between devices: 11.4 us -> 17.9 us  [step(): lax.ppermute(to_right, 'tensor', right)]
    pallas_call x5 -> x7, Pallas kernels: 33.8 us -> 33.3 us  [call(): pl.pallas_call(kernel, in_specs=[pl.BlockSpec(memory_space=memory) for _,...]
  transfers between devices with their start and end apart: 30 -> 30, of which waited for: 16 -> 16; matrix products, arithmetic and copies ran while one was open for 1% -> 1% of each run, Pallas kernels for 20% -> 22%
where the time goes in v12:
time: 112 us
  waiting for transfers between devices  43.5 us (39%)
  Pallas kernels  33.3 us (30%)
  starting transfers between devices  30.7 us (27%)
  other arithmetic  2.18 us (2%)
  matrix products  1.58 us (1%)
    pallas_call x7, Pallas kernels, call(): pl.pallas_call(kernel, in_specs=[pl.BlockSpec(memory_space=memory) for _,...  33.3 us
    ppermute x14, starting transfers between devices, step(): lax.ppermute(to_left, 'tensor', left)  23.7 us
    ppermute x14, waiting for transfers between devices, step(): lax.ppermute(to_left, 'tensor', left)  23 us
    ppermute x14, waiting for transfers between devices, step(): lax.ppermute(to_right, 'tensor', right)  17.9 us
    ppermute x14, starting transfers between devices, step(): lax.ppermute(to_right, 'tensor', right)  6.48 us
  transfers between devices with their start and end apart: 30, of which 16 were waited for; matrix products, arithmetic and copies ran while one was open for 1% of the time, Pallas kernels for 22%

profile of v12, /device:TPU:0, one launch (start us, length us, event | category | flops | bytes accessed | tf_op | source)
XLA Modules:
  0.0 111.9 jit_solution(4091843588581568375)
XLA Ops:
  0.0 0.1 eq.64
  0.1 0.1 pad_add_fusion
  0.2 0.8 compare_reduce_fusion
  1.0 0.1 copy.17
  1.1 0.1 reduce_window_sum.11
  1.2 0.1 copy.18
  1.3 0.1 fusion.9
  1.4 0.3 convolution_convert_fusion
  1.7 0.5 collective-permute-start
  2.3 1.2 %collective-permute-done = bf16[24,6144]{1,0:T(8,128)(2,1)S(1)} collective-permute-done((bf16[24,6144]{1,0:T(8,128)(2,1)S(1)}, bf16[24,6144]{1,0:T(8,128)(2,1)S(1)}, u32[]{:S(2)}, u32[]{:S(2)}) %collective-permute-start) | collective-permute-done | bytes 294944 | tf_op jit(solution)/shard_map/ppermute | solution.py:164
  3.6 2.9 %collective-permute-start.2 = (bf16[48,3072]{1,0:T(8,128)(2,1)S(1)}, bf16[48,3072]{1,0:T(8,128)(2,1)S(1)}, u32[]{:S(2)}, u32[]{:S(2)}) collective-permute-start(bf16[48,3072]{1,0:T(8,128)(2,1)S(1)} %get-tuple-element.147.refs_5_), channel_id=1, source_target_pairs={{2,0},{4,2},{6,4},{7,6},{5,7},{3,5},{1,3},{0,1},{10,8},{12,10},{14... | collective-permute-start | bytes 884744 | tf_op jit(solution)/shard_map/ppermute | solution.py:150
  6.5 0.1 collective-permute-start.1
  6.6 2.0 %collective-permute-start.3 = (bf16[48,3072]{1,0:T(8,128)(2,1)S(1)}, bf16[48,3072]{1,0:T(8,128)(2,1)S(1)}, u32[]{:S(2)}, u32[]{:S(2)}) collective-permute-start(bf16[48,3072]{1,0:T(8,128)(2,1)S(1)} %get-tuple-element.147.refs_5_), channel_id=1, source_target_pairs={{0,2},{2,4},{4,6},{6,7},{7,5},{5,3},{3,1},{1,0},{8,10},{10,12},{12... | collective-permute-start | bytes 884744 | tf_op jit(solution)/shard_map/ppermute | solution.py:150
  8.6 4.7 %fetched.3.refs_10_.refs_6_ = bf16[1,6144,1024]{2,1,0:T(8,128)(2,1)S(1)} custom-call(bf16[1,6144,1024]{2,1,0:T(8,128)(2,1)} %source), custom_call_target="tpu_custom_call" | custom-call | flops 1024 | bytes 1024 | tf_op jit(solution)/shard_map/fetched/pallas_call | solution.py:29
  13.4 1.0 collective-permute-done.2.refs_7_
  14.3 2.0 %collective-permute-done.1.refs_1_ = bf16[48,3072]{1,0:T(8,128)(2,1)S(1)} collective-permute-done((bf16[48,3072]{1,0:T(8,128)(2,1)S(1)}, bf16[48,3072]{1,0:T(8,128)(2,1)S(1)}, u32[]{:S(2)}, u32[]{:S(2)}) %collective-permute-start.1) | collective-permute-done | bytes 294944 | tf_op jit(solution)/shard_map/ppermute | solution.py:150
  16.4 0.1 collective-permute-start.5
  16.5 1.9 %collective-permute-start.6 = (bf16[48,3072]{1,0:T(8,128)(2,1)S(1)}, bf16[48,3072]{1,0:T(8,128)(2,1)S(1)}, u32[]{:S(2)}, u32[]{:S(2)}) collective-permute-start(bf16[48,3072]{1,0:T(8,128)(2,1)S(1)} %collective-permute-done.2.refs_7_), channel_id=1, source_target_pairs={{2,0},{4,2},{6,4},{7,6},{5,7},{3,5},{1,3},{0,1},{10,8},{12,10},{14... | collective-permute-start | bytes 884744 | tf_op jit(solution)/shard_map/ppermute | solution.py:150
  18.4 4.7 %fetched.4.refs_10_.refs_7_ = bf16[1,6144,1024]{2,1,0:T(8,128)(2,1)S(1)} custom-call(bf16[1,6144,1024]{2,1,0:T(8,128)(2,1)} %source.1), custom_call_target="tpu_custom_call" | custom-call | flops 1024 | bytes 1024 | tf_op jit(solution)/shard_map/fetched/pallas_call | solution.py:29
  23.2 1.6 %collective-permute-start.8 = (bf16[48,3072]{1,0:T(8,128)(2,1)S(1)}, bf16[48,3072]{1,0:T(8,128)(2,1)S(1)}, u32[]{:S(2)}, u32[]{:S(2)}) collective-permute-start(bf16[48,3072]{1,0:T(8,128)(2,1)S(1)} %collective-permute-done.4.refs_2_), channel_id=1, source_target_pairs={{2,0},{4,2},{6,4},{7,6},{5,7},{3,5},{1,3},{0,1},{10,8},{12,10},{14... | collective-permute-start | bytes 884744 | tf_op jit(solution)/shard_map/ppermute | solution.py:150
  24.8 0.4 collective-permute-start.7
  25.2 3.8 %collective-permute-done.5.refs_3_ = bf16[48,3072]{1,0:T(8,128)(2,1)S(1)} collective-permute-done((bf16[48,3072]{1,0:T(8,128)(2,1)S(1)}, bf16[48,3072]{1,0:T(8,128)(2,1)S(1)}, u32[]{:S(2)}, u32[]{:S(2)}) %collective-permute-start.5) | collective-permute-done | bytes 294944 | tf_op jit(solution)/shard_map/ppermute | solution.py:150
  29.0 0.1 collective-permute-start.9
  29.1 1.9 %collective-permute-start.10 = (bf16[48,3072]{1,0:T(8,128)(2,1)S(1)}, bf16[48,3072]{1,0:T(8,128)(2,1)S(1)}, u32[]{:S(2)}, u32[]{:S(2)}) collective-permute-start(bf16[48,3072]{1,0:T(8,128)(2,1)S(1)} %collective-permute-done.6.refs_9_), channel_id=1, source_target_pairs={{2,0},{4,2},{6,4},{7,6},{5,7},{3,5},{1,3},{0,1},{10,8},{12,10},{14... | collective-permute-start | bytes 884744 | tf_op jit(solution)/shard_map/ppermute | solution.py:150
  31.1 2.2 %collective-permute-done.8.refs_4_ = bf16[48,3072]{1,0:T(8,128)(2,1)S(1)} collective-permute-done((bf16[48,3072]{1,0:T(8,128)(2,1)S(1)}, bf16[48,3072]{1,0:T(8,128)(2,1)S(1)}, u32[]{:S(2)}, u32[]{:S(2)}) %collective-permute-start.8) | collective-permute-done | bytes 294944 | tf_op jit(solution)/shard_map/ppermute | solution.py:150
  33.3 2.0 %collective-permute-done.7.refs_8_ = bf16[48,3072]{1,0:T(8,128)(2,1)S(1)} collective-permute-done((bf16[48,3072]{1,0:T(8,128)(2,1)S(1)}, bf16[48,3072]{1,0:T(8,128)(2,1)S(1)}, u32[]{:S(2)}, u32[]{:S(2)}) %collective-permute-start.7) | collective-permute-done | bytes 294944 | tf_op jit(solution)/shard_map/ppermute | solution.py:150
  35.4 3.2 %near_gate.1.refs_11_ = f32[240,1024]{1,0:T(8,128)S(1)} custom-call(bf16[48,3072]{1,0:T(8,128)(2,1)S(1)} %get-tuple-element.148.refs_0_, bf16[48,3072]{1,0:T(8,128)(2,1)S(1)} %collective-permute-done.1.refs_1_, bf16[48,3072]{1,0:T(8,128)(2,1)S(1)} %collective-permute-done.4.refs_2_, bf16[48,3072]{1,0:T(8,128)(2,1)S(1)} %collective-permute-done.5.refs_3_, ...), custom_call_target="tpu_custom_call" | custom-call | flops 1024 | bytes 1024 | tf_op jit(solution)/shard_map/near_gate/pallas_call | solution.py:29
  38.6 0.1 collective-permute-start.11
  38.7 1.9 %collective-permute-start.12 = (bf16[48,3072]{1,0:T(8,128)(2,1)S(1)}, bf16[48,3072]{1,0:T(8,128)(2,1)S(1)}, u32[]{:S(2)}, u32[]{:S(2)}) collective-permute-start(bf16[48,3072]{1,0:T(8,128)(2,1)S(1)} %collective-permute-done.8.refs_4_), channel_id=1, source_target_pairs={{2,0},{4,2},{6,4},{7,6},{5,7},{3,5},{1,3},{0,1},{10,8},{12,10},{14... | collective-permute-start | bytes 884744 | tf_op jit(solution)/shard_map/ppermute | solution.py:150
  40.6 1.0 collective-permute-done.9.refs_0_
  41.7 0.1 collective-permute-start.13
  41.8 1.9 %collective-permute-start.14 = (bf16[48,3072]{1,0:T(8,128)(2,1)S(1)}, bf16[48,3072]{1,0:T(8,128)(2,1)S(1)}, u32[]{:S(2)}, u32[]{:S(2)}) collective-permute-start(bf16[48,3072]{1,0:T(8,128)(2,1)S(1)} %collective-permute-done.10.refs_4_), channel_id=1, source_target_pairs={{2,0},{4,2},{6,4},{7,6},{5,7},{3,5},{1,3},{0,1},{10,8},{12,10},{14... | collective-permute-start | bytes 884744 | tf_op jit(solution)/shard_map/ppermute | solution.py:150
  43.7 3.2 %near_up.1.hidden = bf16[240,1024]{1,0:T(8,128)(2,1)S(1)} custom-call(bf16[48,3072]{1,0:T(8,128)(2,1)S(1)} %get-tuple-element.148.refs_0_, bf16[48,3072]{1,0:T(8,128)(2,1)S(1)} %collective-permute-done.1.refs_1_, bf16[48,3072]{1,0:T(8,128)(2,1)S(1)} %collective-permute-done.4.refs_2_, bf16[48,3072]{1,0:T(8,128)(2,1)S(1)} %collective-permute-done.5.refs_3_, ...), custom_call_target="tpu_custom_call" | custom-call | flops 1024 | bytes 1024 | tf_op jit(solution)/shard_map/near_up/pallas_call | solution.py:29
  46.9 2.9 %fetched.5.down_0.refs_8_ = bf16[1,1024,3072]{2,1,0:T(8,128)(2,1)S(1)} custom-call(bf16[1,1024,6144]{2,1,0:T(8,128)(2,1)} %refs_9_), custom_call_target="tpu_custom_call" | custom-call | flops 1024 | bytes 1024 | tf_op jit(solution)/shard_map/fetched/pallas_call | solution.py:29
  49.9 3.3 %collective-permute-done.13.refs_2_ = bf16[48,3072]{1,0:T(8,128)(2,1)S(1)} collective-permute-done((bf16[48,3072]{1,0:T(8,128)(2,1)S(1)}, bf16[48,3072]{1,0:T(8,128)(2,1)S(1)}, u32[]{:S(2)}, u32[]{:S(2)}) %collective-permute-start.13) | collective-permute-done | bytes 294944 | tf_op jit(solution)/shard_map/ppermute | solution.py:150
  53.2 8.5 %rest.1 = (bf16[48,3072]{1,0:T(8,128)(2,1)S(1)}, bf16[48,3072]{1,0:T(8,128)(2,1)S(1)}, bf16[48,3072]{1,0:T(8,128)(2,1)S(1)}, bf16[48,3072]{1,0:T(8,128)(2,1)S(1)...) custom-call(bf16[48,3072]{1,0:T(8,128)(2,1)S(1)} %collective-permute-done.9.refs_0_, ...), custom_call_target="tpu_custom_call" | custom-call | flops 1024 | bytes 1024 | tf_op jit(solution)/shard_map/rest/pallas_call | solution.py:29
  61.7 0.5 collective-permute-start.15
  62.2 1.6 %collective-permute-start.16 = (bf16[48,3072]{1,0:T(8,128)(2,1)S(1)}, bf16[48,3072]{1,0:T(8,128)(2,1)S(1)}, u32[]{:S(2)}, u32[]{:S(2)}) collective-permute-start(bf16[48,3072]{1,0:T(8,128)(2,1)S(1)} %get-tuple-element.120), channel_id=1, source_target_pairs={{2,0},{4,2},{6,4},{7,6},{5,7},{3,5},{1,3},{0,1},{10,8},{12,10},{14... | collective-permute-start | bytes 884744 | tf_op jit(solution)/shard_map/ppermute | solution.py:150
  63.8 6.1 %near_down.1 = (bf16[48,3072]{1,0:T(8,128)(2,1)S(1)}, bf16[48,3072]{1,0:T(8,128)(2,1)S(1)}, bf16[48,3072]{1,0:T(8,128)(2,1)S(1)}, bf16[48,3072]{1,0:T(8,128)(2,1...) custom-call(bf16[240,1024]{1,0:T(8,128)(2,1)S(1)} %near_up.1.hidden,, ...), custom_call_target="tpu_custom_call" | custom-call | flops 1024 | bytes 1024 | tf_op jit(solution)/shard_map/near_down/pallas_call | solution.py:29
  69.9 0.5 collective-permute-start.23
  70.4 1.6 %collective-permute-start.24 = (bf16[48,3072]{1,0:T(8,128)(2,1)S(1)}, bf16[48,3072]{1,0:T(8,128)(2,1)S(1)}, u32[]{:S(2)}, u32[]{:S(2)}) collective-permute-start(bf16[48,3072]{1,0:T(8,128)(2,1)S(1)} %get-tuple-element.134), channel_id=1, source_target_pairs={{2,0},{4,2},{6,4},{7,6},{5,7},{3,5},{1,3},{0,1},{10,8},{12,10},{14... | collective-permute-start | bytes 884744 | tf_op jit(solution)/shard_map/ppermute | solution.py:150
  71.9 0.1 add_convert_fusion.10
  72.0 1.6 %collective-permute-start.18 = (bf16[48,3072]{1,0:T(8,128)(2,1)S(1)}, bf16[48,3072]{1,0:T(8,128)(2,1)S(1)}, u32[]{:S(2)}, u32[]{:S(2)}) collective-permute-start(bf16[48,3072]{1,0:T(8,128)(2,1)S(1)} %add_convert_fusion.10), channel_id=1, source_target_pairs={{2,0},{4,2},{6,4},{7,6},{5,7},{3,5},{1,3},{0,1},{10,8},{12,10},{14... | collective-permute-start | bytes 884744 | tf_op jit(solution)/shard_map/ppermute | solution.py:150
  73.7 0.5 collective-permute-start.17
  74.2 5.6 %collective-permute-done.23 = bf16[48,3072]{1,0:T(8,128)(2,1)S(1)} collective-permute-done((bf16[48,3072]{1,0:T(8,128)(2,1)S(1)}, bf16[48,3072]{1,0:T(8,128)(2,1)S(1)}, u32[]{:S(2)}, u32[]{:S(2)}) %collective-permute-start.23) | collective-permute-done | bytes 294944 | tf_op jit(solution)/shard_map/ppermute | solution.py:150
  79.9 0.5 collective-permute-done.24
  80.4 1.6 %collective-permute-start.26 = (bf16[48,3072]{1,0:T(8,128)(2,1)S(1)}, bf16[48,3072]{1,0:T(8,128)(2,1)S(1)}, u32[]{:S(2)}, u32[]{:S(2)}) collective-permute-start(bf16[48,3072]{1,0:T(8,128)(2,1)S(1)} %add_convert_fusion.4), channel_id=1, source_target_pairs={{2,0},{4,2},{6,4},{7,6},{5,7},{3,5},{1,3},{0,1},{10,8},{12,10},{14... | collective-permute-start | bytes 884744 | tf_op jit(solution)/shard_map/ppermute | solution.py:150
  82.1 0.5 collective-permute-start.25
  82.6 4.0 %collective-permute-done.18 = bf16[48,3072]{1,0:T(8,128)(2,1)S(1)} collective-permute-done((bf16[48,3072]{1,0:T(8,128)(2,1)S(1)}, bf16[48,3072]{1,0:T(8,128)(2,1)S(1)}, u32[]{:S(2)}, u32[]{:S(2)}) %collective-permute-start.18) | collective-permute-done | bytes 294944 | tf_op jit(solution)/shard_map/ppermute | solution.py:150
  86.7 1.6 %collective-permute-start.20 = (bf16[48,3072]{1,0:T(8,128)(2,1)S(1)}, bf16[48,3072]{1,0:T(8,128)(2,1)S(1)}, u32[]{:S(2)}, u32[]{:S(2)}) collective-permute-start(bf16[48,3072]{1,0:T(8,128)(2,1)S(1)} %add_convert_fusion.8), channel_id=1, source_target_pairs={{2,0},{4,2},{6,4},{7,6},{5,7},{3,5},{1,3},{0,1},{10,8},{12,10},{14... | collective-permute-start | bytes 884744 | tf_op jit(solution)/shard_map/ppermute | solution.py:150
  88.4 0.5 collective-permute-start.19
  88.9 4.0 %collective-permute-done.26 = bf16[48,3072]{1,0:T(8,128)(2,1)S(1)} collective-permute-done((bf16[48,3072]{1,0:T(8,128)(2,1)S(1)}, bf16[48,3072]{1,0:T(8,128)(2,1)S(1)}, u32[]{:S(2)}, u32[]{:S(2)}) %collective-permute-start.26) | collective-permute-done | bytes 294944 | tf_op jit(solution)/shard_map/ppermute | solution.py:150
  93.0 1.6 %collective-permute-start.28 = (bf16[48,3072]{1,0:T(8,128)(2,1)S(1)}, bf16[48,3072]{1,0:T(8,128)(2,1)S(1)}, u32[]{:S(2)}, u32[]{:S(2)}) collective-permute-start(bf16[48,3072]{1,0:T(8,128)(2,1)S(1)} %add_convert_fusion.2), channel_id=1, source_target_pairs={{2,0},{4,2},{6,4},{7,6},{5,7},{3,5},{1,3},{0,1},{10,8},{12,10},{14... | collective-permute-start | bytes 884744 | tf_op jit(solution)/shard_map/ppermute | solution.py:150
  94.7 0.5 collective-permute-start.27
  95.2 4.0 %collective-permute-done.20 = bf16[48,3072]{1,0:T(8,128)(2,1)S(1)} collective-permute-done((bf16[48,3072]{1,0:T(8,128)(2,1)S(1)}, bf16[48,3072]{1,0:T(8,128)(2,1)S(1)}, u32[]{:S(2)}, u32[]{:S(2)}) %collective-permute-start.20) | collective-permute-done | bytes 294944 | tf_op jit(solution)/shard_map/ppermute | solution.py:150
  99.4 1.6 %collective-permute-start.22 = (bf16[48,3072]{1,0:T(8,128)(2,1)S(1)}, bf16[48,3072]{1,0:T(8,128)(2,1)S(1)}, u32[]{:S(2)}, u32[]{:S(2)}) collective-permute-start(bf16[48,3072]{1,0:T(8,128)(2,1)S(1)} %add_convert_fusion.6), channel_id=1, source_target_pairs={{2,0},{4,2},{6,4},{7,6},{5,7},{3,5},{1,3},{0,1},{10,8},{12,10},{14... | collective-permute-start | bytes 884744 | tf_op jit(solution)/shard_map/ppermute | solution.py:150
  101.1 0.5 collective-permute-start.21
  101.6 4.0 %collective-permute-done.28 = bf16[48,3072]{1,0:T(8,128)(2,1)S(1)} collective-permute-done((bf16[48,3072]{1,0:T(8,128)(2,1)S(1)}, bf16[48,3072]{1,0:T(8,128)(2,1)S(1)}, u32[]{:S(2)}, u32[]{:S(2)}) %collective-permute-start.28) | collective-permute-done | bytes 294944 | tf_op jit(solution)/shard_map/ppermute | solution.py:150
  105.6 3.2 %collective-permute-done.22 = bf16[48,3072]{1,0:T(8,128)(2,1)S(1)} collective-permute-done((bf16[48,3072]{1,0:T(8,128)(2,1)S(1)}, bf16[48,3072]{1,0:T(8,128)(2,1)S(1)}, u32[]{:S(2)}, u32[]{:S(2)}) %collective-permute-start.22) | collective-permute-done | bytes 294944 | tf_op jit(solution)/shard_map/ppermute | solution.py:150
  108.7 0.2 add_convert_fusion
  109.0 0.1 collective-permute-start.29
  109.1 0.1 fusion.14
  109.2 1.5 %collective-permute-done.29 = bf16[24,6144]{1,0:T(8,128)(2,1)S(1)} collective-permute-done((bf16[24,6144]{1,0:T(8,128)(2,1)S(1)}, bf16[24,6144]{1,0:T(8,128)(2,1)S(1)}, u32[]{:S(2)}, u32[]{:S(2)}) %collective-permute-start.29) | collective-permute-done | bytes 294944 | tf_op jit(solution)/shard_map/ppermute | solution.py:246
  110.7 1.3 %fusion = bf16[64,6144]{1,0:T(8,128)(2,1)} fusion(bf16[1,24,6144]{2,1,0:T(8,128)(2,1)S(1)} %bitcast.22, bf16[1,24,6144]{2,1,0:T(8,128)(2,1)S(1)} %get-tuple-element.145, bf16[2,64]{1,0:T(2,128)(2,1)S(1)} %bitcast.23, s32[2,64]{1,0:T(2,128)S(1)} %subtract_bitcast_fusion, pred[2,64]{1,0:T(4,128)(4,1)S(1)} %get-tuple-element.151), kind=kOutput, calls=%fused_computation.1 | convolution fusion | flops 38052864 | bytes 1377152 | tf_op jit(solution)/shard_map/wcr,wcd->rd/dot_general | solution.py:248
  (39 shorter events, 0.9 us)
Async XLA Ops:
  0.0 1.4 %copy-start = (bf16[64,6144]{1,0:T(8,128)(2,1)S(1)}, bf16[64,6144]{1,0:T(8,128)(2,1)}, u32[]{:S(2)}) copy-start(bf16[64,6144]{1,0:T(8,128)(2,1)} %param.6) | copy-start | bytes 2359300
  1.7 1.7 %collective-permute-start = (bf16[24,6144]{1,0:T(8,128)(2,1)S(1)}, bf16[24,6144]{1,0:T(8,128)(2,1)S(1)}, u32[]{:S(2)}, u32[]{:S(2)}) collective-permute-start(bf16[24,6144]{1,0:T(8,128)(2,1)S(1)} %get-tuple-element.150), channel_id=1, source_target_pairs={{0,8},{8,0},{1,9},{9,1},{2,10},{10,2},{3,11},{11,3},{4,12},{12,4},... | collective-permute-start | bytes 884744 | tf_op jit(solution)/shard_map/ppermute | solution.py:164
  3.6 10.8 %collective-permute-start.2 = (bf16[48,3072]{1,0:T(8,128)(2,1)S(1)}, bf16[48,3072]{1,0:T(8,128)(2,1)S(1)}, u32[]{:S(2)}, u32[]{:S(2)}) collective-permute-start(bf16[48,3072]{1,0:T(8,128)(2,1)S(1)} %get-tuple-element.147.refs_5_), channel_id=1, source_target_pairs={{2,0},{4,2},{6,4},{7,6},{5,7},{3,5},{1,3},{0,1},{10,8},{12,10},{14... | collective-permute-start | bytes 884744 | tf_op jit(solution)/shard_map/ppermute | solution.py:150
  6.5 9.9 %collective-permute-start.1 = (bf16[48,3072]{1,0:T(8,128)(2,1)S(1)}, bf16[48,3072]{1,0:T(8,128)(2,1)S(1)}, u32[]{:S(2)}, u32[]{:S(2)}) collective-permute-start(bf16[48,3072]{1,0:T(8,128)(2,1)S(1)} %get-tuple-element.148.refs_0_), channel_id=1, source_target_pairs={{0,2},{2,4},{4,6},{6,7},{7,5},{5,3},{3,1},{1,0},{8,10},{10,12},{12... | collective-permute-start | bytes 884744 | tf_op jit(solution)/shard_map/ppermute | solution.py:150
  6.6 16.5 %collective-permute-start.3 = (bf16[48,3072]{1,0:T(8,128)(2,1)S(1)}, bf16[48,3072]{1,0:T(8,128)(2,1)S(1)}, u32[]{:S(2)}, u32[]{:S(2)}) collective-permute-start(bf16[48,3072]{1,0:T(8,128)(2,1)S(1)} %get-tuple-element.147.refs_5_), channel_id=1, source_target_pairs={{0,2},{2,4},{4,6},{6,7},{7,5},{5,3},{3,1},{1,0},{8,10},{10,12},{12... | collective-permute-start | bytes 884744 | tf_op jit(solution)/shard_map/ppermute | solution.py:150
  8.6 14.6 %collective-permute-start.4 = (bf16[48,3072]{1,0:T(8,128)(2,1)S(1)}, bf16[48,3072]{1,0:T(8,128)(2,1)S(1)}, u32[]{:S(2)}, u32[]{:S(2)}) collective-permute-start(bf16[48,3072]{1,0:T(8,128)(2,1)S(1)} %get-tuple-element.148.refs_0_), channel_id=1, source_target_pairs={{2,0},{4,2},{6,4},{7,6},{5,7},{3,5},{1,3},{0,1},{10,8},{12,10},{14... | collective-permute-start | bytes 884744 | tf_op jit(solution)/shard_map/ppermute | solution.py:150
  16.4 12.6 %collective-permute-start.5 = (bf16[48,3072]{1,0:T(8,128)(2,1)S(1)}, bf16[48,3072]{1,0:T(8,128)(2,1)S(1)}, u32[]{:S(2)}, u32[]{:S(2)}) collective-permute-start(bf16[48,3072]{1,0:T(8,128)(2,1)S(1)} %collective-permute-done.1.refs_1_), channel_id=1, source_target_pairs={{0,2},{2,4},{4,6},{6,7},{7,5},{5,3},{3,1},{1,0},{8,10},{10,12},{12... | collective-permute-start | bytes 884744 | tf_op jit(solution)/shard_map/ppermute | solution.py:150
  16.5 12.6 %collective-permute-start.6 = (bf16[48,3072]{1,0:T(8,128)(2,1)S(1)}, bf16[48,3072]{1,0:T(8,128)(2,1)S(1)}, u32[]{:S(2)}, u32[]{:S(2)}) collective-permute-start(bf16[48,3072]{1,0:T(8,128)(2,1)S(1)} %collective-permute-done.2.refs_7_), channel_id=1, source_target_pairs={{2,0},{4,2},{6,4},{7,6},{5,7},{3,5},{1,3},{0,1},{10,8},{12,10},{14... | collective-permute-start | bytes 884744 | tf_op jit(solution)/shard_map/ppermute | solution.py:150
  23.2 10.1 %collective-permute-start.8 = (bf16[48,3072]{1,0:T(8,128)(2,1)S(1)}, bf16[48,3072]{1,0:T(8,128)(2,1)S(1)}, u32[]{:S(2)}, u32[]{:S(2)}) collective-permute-start(bf16[48,3072]{1,0:T(8,128)(2,1)S(1)} %collective-permute-done.4.refs_2_), channel_id=1, source_target_pairs={{2,0},{4,2},{6,4},{7,6},{5,7},{3,5},{1,3},{0,1},{10,8},{12,10},{14... | collective-permute-start | bytes 884744 | tf_op jit(solution)/shard_map/ppermute | solution.py:150
  24.8 10.6 %collective-permute-start.7 = (bf16[48,3072]{1,0:T(8,128)(2,1)S(1)}, bf16[48,3072]{1,0:T(8,128)(2,1)S(1)}, u32[]{:S(2)}, u32[]{:S(2)}) collective-permute-start(bf16[48,3072]{1,0:T(8,128)(2,1)S(1)} %collective-permute-done.3.refs_6_), channel_id=1, source_target_pairs={{0,2},{2,4},{4,6},{6,7},{7,5},{5,3},{3,1},{1,0},{8,10},{10,12},{12... | collective-permute-start | bytes 884744 | tf_op jit(solution)/shard_map/ppermute | solution.py:150
  29.0 12.6 %collective-permute-start.9 = (bf16[48,3072]{1,0:T(8,128)(2,1)S(1)}, bf16[48,3072]{1,0:T(8,128)(2,1)S(1)}, u32[]{:S(2)}, u32[]{:S(2)}) collective-permute-start(bf16[48,3072]{1,0:T(8,128)(2,1)S(1)} %collective-permute-done.5.refs_3_), channel_id=1, source_target_pairs={{0,2},{2,4},{4,6},{6,7},{7,5},{5,3},{3,1},{1,0},{8,10},{10,12},{12... | collective-permute-start | bytes 884744 | tf_op jit(solution)/shard_map/ppermute | solution.py:150
  29.1 12.6 %collective-permute-start.10 = (bf16[48,3072]{1,0:T(8,128)(2,1)S(1)}, bf16[48,3072]{1,0:T(8,128)(2,1)S(1)}, u32[]{:S(2)}, u32[]{:S(2)}) collective-permute-start(bf16[48,3072]{1,0:T(8,128)(2,1)S(1)} %collective-permute-done.6.refs_9_), channel_id=1, source_target_pairs={{2,0},{4,2},{6,4},{7,6},{5,7},{3,5},{1,3},{0,1},{10,8},{12,10},{14... | collective-permute-start | bytes 884744 | tf_op jit(solution)/shard_map/ppermute | solution.py:150
  38.6 11.3 %collective-permute-start.11 = (bf16[48,3072]{1,0:T(8,128)(2,1)S(1)}, bf16[48,3072]{1,0:T(8,128)(2,1)S(1)}, u32[]{:S(2)}, u32[]{:S(2)}) collective-permute-start(bf16[48,3072]{1,0:T(8,128)(2,1)S(1)} %collective-permute-done.7.refs_8_), channel_id=1, source_target_pairs={{0,2},{2,4},{4,6},{6,7},{7,5},{5,3},{3,1},{1,0},{8,10},{10,12},{12... | collective-permute-start | bytes 884744 | tf_op jit(solution)/shard_map/ppermute | solution.py:150
  38.7 11.2 %collective-permute-start.12 = (bf16[48,3072]{1,0:T(8,128)(2,1)S(1)}, bf16[48,3072]{1,0:T(8,128)(2,1)S(1)}, u32[]{:S(2)}, u32[]{:S(2)}) collective-permute-start(bf16[48,3072]{1,0:T(8,128)(2,1)S(1)} %collective-permute-done.8.refs_4_), channel_id=1, source_target_pairs={{2,0},{4,2},{6,4},{7,6},{5,7},{3,5},{1,3},{0,1},{10,8},{12,10},{14... | collective-permute-start | bytes 884744 | tf_op jit(solution)/shard_map/ppermute | solution.py:150
  41.7 11.5 %collective-permute-start.13 = (bf16[48,3072]{1,0:T(8,128)(2,1)S(1)}, bf16[48,3072]{1,0:T(8,128)(2,1)S(1)}, u32[]{:S(2)}, u32[]{:S(2)}) collective-permute-start(bf16[48,3072]{1,0:T(8,128)(2,1)S(1)} %collective-permute-done.9.refs_0_), channel_id=1, source_target_pairs={{0,2},{2,4},{4,6},{6,7},{7,5},{5,3},{3,1},{1,0},{8,10},{10,12},{12... | collective-permute-start | bytes 884744 | tf_op jit(solution)/shard_map/ppermute | solution.py:150
  41.8 11.4 %collective-permute-start.14 = (bf16[48,3072]{1,0:T(8,128)(2,1)S(1)}, bf16[48,3072]{1,0:T(8,128)(2,1)S(1)}, u32[]{:S(2)}, u32[]{:S(2)}) collective-permute-start(bf16[48,3072]{1,0:T(8,128)(2,1)S(1)} %collective-permute-done.10.refs_4_), channel_id=1, source_target_pairs={{2,0},{4,2},{6,4},{7,6},{5,7},{3,5},{1,3},{0,1},{10,8},{12,10},{14... | collective-permute-start | bytes 884744 | tf_op jit(solution)/shard_map/ppermute | solution.py:150
  61.7 10.3 %collective-permute-start.15 = (bf16[48,3072]{1,0:T(8,128)(2,1)S(1)}, bf16[48,3072]{1,0:T(8,128)(2,1)S(1)}, u32[]{:S(2)}, u32[]{:S(2)}) collective-permute-start(bf16[48,3072]{1,0:T(8,128)(2,1)S(1)} %get-tuple-element.119), channel_id=1, source_target_pairs={{0,2},{2,4},{4,6},{6,7},{7,5},{5,3},{3,1},{1,0},{8,10},{10,12},{12... | collective-permute-start | bytes 884744 | tf_op jit(solution)/shard_map/ppermute | solution.py:150
  62.2 49.7 %copy-start.1 = (bf16[64,6144]{1,0:T(8,128)(2,1)S(1)}, bf16[64,6144]{1,0:T(8,128)(2,1)}, u32[]{:S(2)}) copy-start(bf16[64,6144]{1,0:T(8,128)(2,1)} %param.6) | copy-start | bytes 2359300
  62.2 46.9 %copy-start.2 = (s32[64,2]{0,1:T(2,128)S(1)}, s32[64,2]{0,1:T(2,128)}, u32[]{:S(2)}) copy-start(s32[64,2]{0,1:T(2,128)} %param.7) | copy-start | bytes 1540
  62.2 46.9 %copy-start.3 = (f32[64,2]{0,1:T(2,128)S(1)}, f32[64,2]{0,1:T(2,128)}, u32[]{:S(2)}) copy-start(f32[64,2]{0,1:T(2,128)} %param.8) | copy-start | bytes 1540
  62.2 9.7 %collective-permute-start.16 = (bf16[48,3072]{1,0:T(8,128)(2,1)S(1)}, bf16[48,3072]{1,0:T(8,128)(2,1)S(1)}, u32[]{:S(2)}, u32[]{:S(2)}) collective-permute-start(bf16[48,3072]{1,0:T(8,128)(2,1)S(1)} %get-tuple-element.120), channel_id=1, source_target_pairs={{2,0},{4,2},{6,4},{7,6},{5,7},{3,5},{1,3},{0,1},{10,8},{12,10},{14... | collective-permute-start | bytes 884744 | tf_op jit(solution)/shard_map/ppermute | solution.py:150
  69.9 10.0 %collective-permute-start.23 = (bf16[48,3072]{1,0:T(8,128)(2,1)S(1)}, bf16[48,3072]{1,0:T(8,128)(2,1)S(1)}, u32[]{:S(2)}, u32[]{:S(2)}) collective-permute-start(bf16[48,3072]{1,0:T(8,128)(2,1)S(1)} %get-tuple-element.133), channel_id=1, source_target_pairs={{0,2},{2,4},{4,6},{6,7},{7,5},{5,3},{3,1},{1,0},{8,10},{10,12},{12... | collective-permute-start | bytes 884744 | tf_op jit(solution)/shard_map/ppermute | solution.py:150
  70.4 9.9 %collective-permute-start.24 = (bf16[48,3072]{1,0:T(8,128)(2,1)S(1)}, bf16[48,3072]{1,0:T(8,128)(2,1)S(1)}, u32[]{:S(2)}, u32[]{:S(2)}) collective-permute-start(bf16[48,3072]{1,0:T(8,128)(2,1)S(1)} %get-tuple-element.134), channel_id=1, source_target_pairs={{2,0},{4,2},{6,4},{7,6},{5,7},{3,5},{1,3},{0,1},{10,8},{12,10},{14... | collective-permute-start | bytes 884744 | tf_op jit(solution)/shard_map/ppermute | solution.py:150
  72.0 14.6 %collective-permute-start.18 = (bf16[48,3072]{1,0:T(8,128)(2,1)S(1)}, bf16[48,3072]{1,0:T(8,128)(2,1)S(1)}, u32[]{:S(2)}, u32[]{:S(2)}) collective-permute-start(bf16[48,3072]{1,0:T(8,128)(2,1)S(1)} %add_convert_fusion.10), channel_id=1, source_target_pairs={{2,0},{4,2},{6,4},{7,6},{5,7},{3,5},{1,3},{0,1},{10,8},{12,10},{14... | collective-permute-start | bytes 884744 | tf_op jit(solution)/shard_map/ppermute | solution.py:150
  73.7 12.9 %collective-permute-start.17 = (bf16[48,3072]{1,0:T(8,128)(2,1)S(1)}, bf16[48,3072]{1,0:T(8,128)(2,1)S(1)}, u32[]{:S(2)}, u32[]{:S(2)}) collective-permute-start(bf16[48,3072]{1,0:T(8,128)(2,1)S(1)} %add_convert_fusion.11), channel_id=1, source_target_pairs={{0,2},{2,4},{4,6},{6,7},{7,5},{5,3},{3,1},{1,0},{8,10},{10,12},{12... | collective-permute-start | bytes 884744 | tf_op jit(solution)/shard_map/ppermute | solution.py:150
  80.4 12.6 %collective-permute-start.26 = (bf16[48,3072]{1,0:T(8,128)(2,1)S(1)}, bf16[48,3072]{1,0:T(8,128)(2,1)S(1)}, u32[]{:S(2)}, u32[]{:S(2)}) collective-permute-start(bf16[48,3072]{1,0:T(8,128)(2,1)S(1)} %add_convert_fusion.4), channel_id=1, source_target_pairs={{2,0},{4,2},{6,4},{7,6},{5,7},{3,5},{1,3},{0,1},{10,8},{12,10},{14... | collective-permute-start | bytes 884744 | tf_op jit(solution)/shard_map/ppermute | solution.py:150
  82.1 10.9 %collective-permute-start.25 = (bf16[48,3072]{1,0:T(8,128)(2,1)S(1)}, bf16[48,3072]{1,0:T(8,128)(2,1)S(1)}, u32[]{:S(2)}, u32[]{:S(2)}) collective-permute-start(bf16[48,3072]{1,0:T(8,128)(2,1)S(1)} %add_convert_fusion.5), channel_id=1, source_target_pairs={{0,2},{2,4},{4,6},{6,7},{7,5},{5,3},{3,1},{1,0},{8,10},{10,12},{12... | collective-permute-start | bytes 884744 | tf_op jit(solution)/shard_map/ppermute | solution.py:150
  86.7 12.6 %collective-permute-start.20 = (bf16[48,3072]{1,0:T(8,128)(2,1)S(1)}, bf16[48,3072]{1,0:T(8,128)(2,1)S(1)}, u32[]{:S(2)}, u32[]{:S(2)}) collective-permute-start(bf16[48,3072]{1,0:T(8,128)(2,1)S(1)} %add_convert_fusion.8), channel_id=1, source_target_pairs={{2,0},{4,2},{6,4},{7,6},{5,7},{3,5},{1,3},{0,1},{10,8},{12,10},{14... | collective-permute-start | bytes 884744 | tf_op jit(solution)/shard_map/ppermute | solution.py:150
  88.4 10.9 %collective-permute-start.19 = (bf16[48,3072]{1,0:T(8,128)(2,1)S(1)}, bf16[48,3072]{1,0:T(8,128)(2,1)S(1)}, u32[]{:S(2)}, u32[]{:S(2)}) collective-permute-start(bf16[48,3072]{1,0:T(8,128)(2,1)S(1)} %add_convert_fusion.9), channel_id=1, source_target_pairs={{0,2},{2,4},{4,6},{6,7},{7,5},{5,3},{3,1},{1,0},{8,10},{10,12},{12... | collective-permute-start | bytes 884744 | tf_op jit(solution)/shard_map/ppermute | solution.py:150
  93.0 12.5 %collective-permute-start.28 = (bf16[48,3072]{1,0:T(8,128)(2,1)S(1)}, bf16[48,3072]{1,0:T(8,128)(2,1)S(1)}, u32[]{:S(2)}, u32[]{:S(2)}) collective-permute-start(bf16[48,3072]{1,0:T(8,128)(2,1)S(1)} %add_convert_fusion.2), channel_id=1, source_target_pairs={{2,0},{4,2},{6,4},{7,6},{5,7},{3,5},{1,3},{0,1},{10,8},{12,10},{14... | collective-permute-start | bytes 884744 | tf_op jit(solution)/shard_map/ppermute | solution.py:150
  94.7 10.8 %collective-permute-start.27 = (bf16[48,3072]{1,0:T(8,128)(2,1)S(1)}, bf16[48,3072]{1,0:T(8,128)(2,1)S(1)}, u32[]{:S(2)}, u32[]{:S(2)}) collective-permute-start(bf16[48,3072]{1,0:T(8,128)(2,1)S(1)} %add_convert_fusion.3), channel_id=1, source_target_pairs={{0,2},{2,4},{4,6},{6,7},{7,5},{5,3},{3,1},{1,0},{8,10},{10,12},{12... | collective-permute-start | bytes 884744 | tf_op jit(solution)/shard_map/ppermute | solution.py:150
  99.4 9.4 %collective-permute-start.22 = (bf16[48,3072]{1,0:T(8,128)(2,1)S(1)}, bf16[48,3072]{1,0:T(8,128)(2,1)S(1)}, u32[]{:S(2)}, u32[]{:S(2)}) collective-permute-start(bf16[48,3072]{1,0:T(8,128)(2,1)S(1)} %add_convert_fusion.6), channel_id=1, source_target_pairs={{2,0},{4,2},{6,4},{7,6},{5,7},{3,5},{1,3},{0,1},{10,8},{12,10},{14... | collective-permute-start | bytes 884744 | tf_op jit(solution)/shard_map/ppermute | solution.py:150
  101.1 7.7 %collective-permute-start.21 = (bf16[48,3072]{1,0:T(8,128)(2,1)S(1)}, bf16[48,3072]{1,0:T(8,128)(2,1)S(1)}, u32[]{:S(2)}, u32[]{:S(2)}) collective-permute-start(bf16[48,3072]{1,0:T(8,128)(2,1)S(1)} %add_convert_fusion.7), channel_id=1, source_target_pairs={{0,2},{2,4},{4,6},{6,7},{7,5},{5,3},{3,1},{1,0},{8,10},{10,12},{12... | collective-permute-start | bytes 884744 | tf_op jit(solution)/shard_map/ppermute | solution.py:150
  109.0 1.6 %collective-permute-start.29 = (bf16[24,6144]{1,0:T(8,128)(2,1)S(1)}, bf16[24,6144]{1,0:T(8,128)(2,1)S(1)}, u32[]{:S(2)}, u32[]{:S(2)}) collective-permute-start(bf16[24,6144]{1,0:T(8,128)(2,1)S(1)} %get-tuple-element.146), channel_id=1, source_target_pairs={{0,8},{8,0},{1,9},{9,1},{2,10},{10,2},{3,11},{11,3},{4,12},{12,4},... | collective-permute-start | bytes 884744 | tf_op jit(solution)/shard_map/ppermute | solution.py:246

commit v13 on v12

--- a/solution.py
+++ b/solution.py
@@ -17,25 +17,22 @@
     return list(range(0, count, 2)) + list(range(count - 1, 0, -2))
 
 
-def in_vmem(array):
-    return pltpu.with_memory_space_constraint(array, pltpu.VMEM)
-
-
-def in_hbm(array):
-    return pltpu.with_memory_space_constraint(array, pltpu.HBM)
-
-
-def call(kernel, name, operands, outs, scratch, room):
+def placed(array, memory):
+    return array if memory == pltpu.SMEM else pltpu.with_memory_space_constraint(array, memory)
+
+
+def call(kernel, name, operands, outs, scratch, room, aliases=None):
     return pl.pallas_call(
         kernel,
         in_specs=[pl.BlockSpec(memory_space=memory) for _, memory in operands],
         out_specs=[pl.BlockSpec(memory_space=pltpu.VMEM)] * len(outs),
         out_shape=[pltpu.VMEM(*out) for out in outs],
         scratch_shapes=scratch,
+        input_output_aliases=aliases or {},
         cost_estimate=CHEAP,
         compiler_params=pltpu.CompilerParams(vmem_limit_bytes=room + MARGIN),
         name=name,
-    )(*[in_vmem(array) if memory == pltpu.VMEM else in_hbm(array) for array, memory in operands])
+    )(*[placed(array, memory) for array, memory in operands])
 
 
 def row_copies(source, target, done, column=0):
@@ -56,10 +53,26 @@
         copy.wait()
 
 
+def fill_some_kernel(which, core, source, *refs):
+    target, done = refs[-2:]
+
+    @pl.when(core[0] == which)
+    def _():
+        fill_kernel(source, target, done)
+
+
 def fetched(weights, width):
     operands = [(weights, pltpu.HBM)]
     outs = [((*weights.shape[:2], width), weights.dtype)]
     return call(fill_kernel, "fetched", operands, outs, [pltpu.SemaphoreType.DMA((COPIES,))], 0)[0]
+
+
+def fetched_by(which, core, weights, target=None):
+    operands = [(core, pltpu.SMEM), (weights, pltpu.HBM)] + ([] if target is None else [(target, pltpu.VMEM)])
+    outs = [(weights.shape, weights.dtype)]
+    scratch = [pltpu.SemaphoreType.DMA((COPIES,))]
+    kernel = functools.partial(fill_some_kernel, which)
+    return call(kernel, "fetched_by", operands, outs, scratch, 0, {} if target is None else {2: 0})[0]
 
 
 def accumulate(chunks, products):
@@ -161,9 +174,15 @@
         tokens,
         preferred_element_type=jnp.float32,
     ).astype(jnp.bfloat16)
-    own = jnp.concatenate([outgoing[:CAP], lax.ppermute(outgoing[CAP:], "expert", swap)], axis=0)
-
-    own, w_gate = tied(own, w_gate)
+    core = jnp.reshape(me, (1,)).astype(jnp.int32)
+    outgoing, w_gate = tied(outgoing, w_gate)
+    gate_here = fetched_by(0, core, w_gate)
+    gate_here, w_up = tied(gate_here, w_up)
+    up_here = fetched_by(0, core, w_up)
+    swapped = lax.ppermute(outgoing[CAP:], "expert", swap)
+    own = jnp.concatenate([outgoing[:CAP], swapped], axis=0)
+
+    own, gate_here, up_here = tied(own, gate_here, up_here)
     halves = [own[:, :mid_col], own[:, mid_col:]]
     blocks = [[halves[0]], [halves[1]]]
 
@@ -173,10 +192,10 @@
 
     a = step(halves[0], halves[1])
     b = step(halves[1], halves[0])
-    gate_here = fetched(w_gate, units)
+    gate_here = fetched_by(1, core, w_gate, gate_here)
     a, gate_here = tied(a, gate_here)
-    a, w_up = tied(a, w_up)
-    up_here = fetched(w_up, units)
+    a, up_here = tied(a, up_here)
+    up_here = fetched_by(1, core, w_up, up_here)
     b, up_here = tied(b, up_here)
     arrived(a, b)
     for _ in range(half - 3):
@@ -216,6 +235,7 @@
         [pltpu.VMEM((3 * size, units), jnp.float32)] * 2 + down_scratch,
         down_room + 3 * size * units * 16,
     )
+    near_hidden, _ = tied(near_hidden, rest_parts)
     near_parts = call(
         near_down_kernel, "near_down", [(near_hidden, pltpu.VMEM), (down_here, pltpu.VMEM), (w_down, pltpu.HBM)],
         [((size, mid_col), jnp.bfloat16)] * (2 * count), down_scratch, down_room + rows * TILE * 12,

time: 112 us -> 115 us (1.027)
  waiting for transfers between devices: 43.5 us -> 47.1 us
    ppermute x14, starting transfers between devices: 23.7 us -> 3.99 us  [step(): lax.ppermute(to_left, 'tensor', left)]
    ppermute x14, starting transfers between devices: 6.48 us -> 25.3 us  [step(): lax.ppermute(to_right, 'tensor', right)]
    ppermute x14, waiting for transfers between devices: 23 us -> 30.8 us  [step(): lax.ppermute(to_left, 'tensor', left)]
    ppermute x14, waiting for transfers between devices: 17.9 us -> 14.8 us  [step(): lax.ppermute(to_right, 'tensor', right)]
    ppermute x1, waiting for transfers between devices: 1.21 us -> 0.01 us  [per_device(): swapped = lax.ppermute(outgoing[CAP:], 'expert', swap)]
    pallas_call x7 -> x9, Pallas kernels: 33.3 us -> 33.6 us  [call(): pl.pallas_call(kernel, in_specs=[pl.BlockSpec(memory_space=memory) for _,...]
  transfers between devices with their start and end apart: 30 -> 30, of which waited for: 16 -> 20; matrix products, arithmetic and copies ran while one was open for 1% -> 1% of each run, Pallas kernels for 22% -> 22%
where the time goes in v13:
time: 115 us
  waiting for transfers between devices  47.1 us (41%)
  Pallas kernels  33.6 us (29%)
  starting transfers between devices  29.9 us (26%)
  other arithmetic  2.17 us (2%)
  matrix products  1.59 us (1%)
    pallas_call x9, Pallas kernels, call(): pl.pallas_call(kernel, in_specs=[pl.BlockSpec(memory_space=memory) for _,...  33.6 us
    ppermute x14, waiting for transfers between devices, step(): lax.ppermute(to_left, 'tensor', left)  30.8 us
    ppermute x14, starting transfers between devices, step(): lax.ppermute(to_right, 'tensor', right)  25.3 us
    ppermute x14, waiting for transfers between devices, step(): lax.ppermute(to_right, 'tensor', right)  14.8 us
    ppermute x14, starting transfers between devices, step(): lax.ppermute(to_left, 'tensor', left)  3.99 us
  transfers between devices with their start and end apart: 30, of which 20 were waited for; matrix products, arithmetic and copies ran while one was open for 1% of the time, Pallas kernels for 22%

profile of v13, /device:TPU:0, one launch (start us, length us, event | category | flops | bytes accessed | tf_op | source)
XLA Modules:
  0.0 115.0 jit_solution(18345716348139432988)
XLA Ops:
  0.0 0.1 pad_add_fusion
  0.1 0.8 compare_reduce_fusion
  0.9 0.1 copy.19
  1.0 0.1 reduce_window_sum.11
  1.1 0.1 copy.20
  1.2 0.1 eq.64
  1.3 0.1 fusion.9
  1.4 0.3 convolution_convert_fusion
  1.7 0.5 collective-permute-start
  2.2 4.7 %fetched_by.4.refs_0_ = bf16[1,6144,1024]{2,1,0:T(8,128)(2,1)S(1)} custom-call(s32[1]{0:T(128)} %bitcast.core, bf16[1,6144,1024]{2,1,0:T(8,128)(2,1)} %source.2), custom_call_target="tpu_custom_call" | custom-call | flops 1024 | bytes 1024 | tf_op jit(solution)/shard_map/fetched_by/pallas_call | solution.py:25
  7.0 4.7 %fetched_by.5.refs_0_ = bf16[1,6144,1024]{2,1,0:T(8,128)(2,1)S(1)} custom-call(s32[1]{0:T(128)} %bitcast.core, bf16[1,6144,1024]{2,1,0:T(8,128)(2,1)} %source.3), custom_call_target="tpu_custom_call" | custom-call | flops 1024 | bytes 1024 | tf_op jit(solution)/shard_map/fetched_by/pallas_call | solution.py:25
  11.8 2.6 %collective-permute-start.1 = (bf16[48,3072]{1,0:T(8,128)(2,1)S(1)}, bf16[48,3072]{1,0:T(8,128)(2,1)S(1)}, u32[]{:S(2)}, u32[]{:S(2)}) collective-permute-start(bf16[48,3072]{1,0:T(8,128)(2,1)S(1)} %get-tuple-element.160.refs_0_), channel_id=1, source_target_pairs={{0,2},{2,4},{4,6},{6,7},{7,5},{5,3},{3,1},{1,0},{8,10},{10,12},{12... | collective-permute-start | bytes 884744 | tf_op jit(solution)/shard_map/ppermute | solution.py:163
  14.5 2.0 %collective-permute-start.3 = (bf16[48,3072]{1,0:T(8,128)(2,1)S(1)}, bf16[48,3072]{1,0:T(8,128)(2,1)S(1)}, u32[]{:S(2)}, u32[]{:S(2)}) collective-permute-start(bf16[48,3072]{1,0:T(8,128)(2,1)S(1)} %get-tuple-element.159.refs_5_), channel_id=1, source_target_pairs={{0,2},{2,4},{4,6},{6,7},{7,5},{5,3},{3,1},{1,0},{8,10},{10,12},{12... | collective-permute-start | bytes 884744 | tf_op jit(solution)/shard_map/ppermute | solution.py:163
  16.5 0.1 fetched_by.6.refs_10_.refs_6_
  16.7 4.9 %collective-permute-done.1.refs_1_ = bf16[48,3072]{1,0:T(8,128)(2,1)S(1)} collective-permute-done((bf16[48,3072]{1,0:T(8,128)(2,1)S(1)}, bf16[48,3072]{1,0:T(8,128)(2,1)S(1)}, u32[]{:S(2)}, u32[]{:S(2)}) %collective-permute-start.1) | collective-permute-done | bytes 294944 | tf_op jit(solution)/shard_map/ppermute | solution.py:163
  21.6 1.5 %collective-permute-done.2.refs_7_ = bf16[48,3072]{1,0:T(8,128)(2,1)S(1)} collective-permute-done((bf16[48,3072]{1,0:T(8,128)(2,1)S(1)}, bf16[48,3072]{1,0:T(8,128)(2,1)S(1)}, u32[]{:S(2)}, u32[]{:S(2)}) %collective-permute-start.2) | collective-permute-done | bytes 294944 | tf_op jit(solution)/shard_map/ppermute | solution.py:163
  23.0 1.6 %collective-permute-start.5 = (bf16[48,3072]{1,0:T(8,128)(2,1)S(1)}, bf16[48,3072]{1,0:T(8,128)(2,1)S(1)}, u32[]{:S(2)}, u32[]{:S(2)}) collective-permute-start(bf16[48,3072]{1,0:T(8,128)(2,1)S(1)} %collective-permute-done.1.refs_1_), channel_id=1, source_target_pairs={{0,2},{2,4},{4,6},{6,7},{7,5},{5,3},{3,1},{1,0},{8,10},{10,12},{12... | collective-permute-start | bytes 884744 | tf_op jit(solution)/shard_map/ppermute | solution.py:163
  24.6 0.4 collective-permute-start.6
  25.1 0.1 fetched_by.7.refs_10_.refs_7_
  25.2 2.7 %collective-permute-done.3.refs_6_ = bf16[48,3072]{1,0:T(8,128)(2,1)S(1)} collective-permute-done((bf16[48,3072]{1,0:T(8,128)(2,1)S(1)}, bf16[48,3072]{1,0:T(8,128)(2,1)S(1)}, u32[]{:S(2)}, u32[]{:S(2)}) %collective-permute-start.3) | collective-permute-done | bytes 294944 | tf_op jit(solution)/shard_map/ppermute | solution.py:163
  27.9 1.5 %collective-permute-done.4.refs_2_ = bf16[48,3072]{1,0:T(8,128)(2,1)S(1)} collective-permute-done((bf16[48,3072]{1,0:T(8,128)(2,1)S(1)}, bf16[48,3072]{1,0:T(8,128)(2,1)S(1)}, u32[]{:S(2)}, u32[]{:S(2)}) %collective-permute-start.4) | collective-permute-done | bytes 294944 | tf_op jit(solution)/shard_map/ppermute | solution.py:163
  29.3 1.6 %collective-permute-start.7 = (bf16[48,3072]{1,0:T(8,128)(2,1)S(1)}, bf16[48,3072]{1,0:T(8,128)(2,1)S(1)}, u32[]{:S(2)}, u32[]{:S(2)}) collective-permute-start(bf16[48,3072]{1,0:T(8,128)(2,1)S(1)} %collective-permute-done.3.refs_6_), channel_id=1, source_target_pairs={{0,2},{2,4},{4,6},{6,7},{7,5},{5,3},{3,1},{1,0},{8,10},{10,12},{12... | collective-permute-start | bytes 884744 | tf_op jit(solution)/shard_map/ppermute | solution.py:163
  30.9 0.4 collective-permute-start.8
  31.4 2.8 %collective-permute-done.5.refs_3_ = bf16[48,3072]{1,0:T(8,128)(2,1)S(1)} collective-permute-done((bf16[48,3072]{1,0:T(8,128)(2,1)S(1)}, bf16[48,3072]{1,0:T(8,128)(2,1)S(1)}, u32[]{:S(2)}, u32[]{:S(2)}) %collective-permute-start.5) | collective-permute-done | bytes 294944 | tf_op jit(solution)/shard_map/ppermute | solution.py:163
  34.2 1.5 %collective-permute-done.6.refs_9_ = bf16[48,3072]{1,0:T(8,128)(2,1)S(1)} collective-permute-done((bf16[48,3072]{1,0:T(8,128)(2,1)S(1)}, bf16[48,3072]{1,0:T(8,128)(2,1)S(1)}, u32[]{:S(2)}, u32[]{:S(2)}) %collective-permute-start.6) | collective-permute-done | bytes 294944 | tf_op jit(solution)/shard_map/ppermute | solution.py:163
  35.7 0.3 collective-permute-start.10
  36.0 1.7 %collective-permute-start.9 = (bf16[48,3072]{1,0:T(8,128)(2,1)S(1)}, bf16[48,3072]{1,0:T(8,128)(2,1)S(1)}, u32[]{:S(2)}, u32[]{:S(2)}) collective-permute-start(bf16[48,3072]{1,0:T(8,128)(2,1)S(1)} %collective-permute-done.5.refs_3_), channel_id=1, source_target_pairs={{0,2},{2,4},{4,6},{6,7},{7,5},{5,3},{3,1},{1,0},{8,10},{10,12},{12... | collective-permute-start | bytes 884744 | tf_op jit(solution)/shard_map/ppermute | solution.py:163
  37.7 1.7 %collective-permute-done.7.refs_8_ = bf16[48,3072]{1,0:T(8,128)(2,1)S(1)} collective-permute-done((bf16[48,3072]{1,0:T(8,128)(2,1)S(1)}, bf16[48,3072]{1,0:T(8,128)(2,1)S(1)}, u32[]{:S(2)}, u32[]{:S(2)}) %collective-permute-start.7) | collective-permute-done | bytes 294944 | tf_op jit(solution)/shard_map/ppermute | solution.py:163
  39.4 1.6 %collective-permute-done.8.refs_4_ = bf16[48,3072]{1,0:T(8,128)(2,1)S(1)} collective-permute-done((bf16[48,3072]{1,0:T(8,128)(2,1)S(1)}, bf16[48,3072]{1,0:T(8,128)(2,1)S(1)}, u32[]{:S(2)}, u32[]{:S(2)}) %collective-permute-start.8) | collective-permute-done | bytes 294944 | tf_op jit(solution)/shard_map/ppermute | solution.py:163
  41.0 3.2 %near_gate.1.refs_11_ = f32[240,1024]{1,0:T(8,128)S(1)} custom-call(bf16[48,3072]{1,0:T(8,128)(2,1)S(1)} %get-tuple-element.160.refs_0_, bf16[48,3072]{1,0:T(8,128)(2,1)S(1)} %collective-permute-done.1.refs_1_, bf16[48,3072]{1,0:T(8,128)(2,1)S(1)} %collective-permute-done.4.refs_2_, bf16[48,3072]{1,0:T(8,128)(2,1)S(1)} %collective-permute-done.5.refs_3_, ...), custom_call_target="tpu_custom_call" | custom-call | flops 1024 | bytes 1024 | tf_op jit(solution)/shard_map/near_gate/pallas_call | solution.py:25
  44.2 1.6 %collective-permute-start.11 = (bf16[48,3072]{1,0:T(8,128)(2,1)S(1)}, bf16[48,3072]{1,0:T(8,128)(2,1)S(1)}, u32[]{:S(2)}, u32[]{:S(2)}) collective-permute-start(bf16[48,3072]{1,0:T(8,128)(2,1)S(1)} %collective-permute-done.7.refs_8_), channel_id=1, source_target_pairs={{0,2},{2,4},{4,6},{6,7},{7,5},{5,3},{3,1},{1,0},{8,10},{10,12},{12... | collective-permute-start | bytes 884744 | tf_op jit(solution)/shard_map/ppermute | solution.py:163
  45.8 0.4 collective-permute-start.12
  46.3 1.0 collective-permute-done.10.refs_4_
  47.3 1.6 %collective-permute-start.13 = (bf16[48,3072]{1,0:T(8,128)(2,1)S(1)}, bf16[48,3072]{1,0:T(8,128)(2,1)S(1)}, u32[]{:S(2)}, u32[]{:S(2)}) collective-permute-start(bf16[48,3072]{1,0:T(8,128)(2,1)S(1)} %collective-permute-done.9.refs_0_), channel_id=1, source_target_pairs={{0,2},{2,4},{4,6},{6,7},{7,5},{5,3},{3,1},{1,0},{8,10},{10,12},{12... | collective-permute-start | bytes 884744 | tf_op jit(solution)/shard_map/ppermute | solution.py:163
  48.9 0.4 collective-permute-start.14
  49.3 3.2 %near_up.1.hidden = bf16[240,1024]{1,0:T(8,128)(2,1)S(1)} custom-call(bf16[48,3072]{1,0:T(8,128)(2,1)S(1)} %get-tuple-element.160.refs_0_, bf16[48,3072]{1,0:T(8,128)(2,1)S(1)} %collective-permute-done.1.refs_1_, bf16[48,3072]{1,0:T(8,128)(2,1)S(1)} %collective-permute-done.4.refs_2_, bf16[48,3072]{1,0:T(8,128)(2,1)S(1)} %collective-permute-done.5.refs_3_, ...), custom_call_target="tpu_custom_call" | custom-call | flops 1024 | bytes 1024 | tf_op jit(solution)/shard_map/near_up/pallas_call | solution.py:25
  52.6 2.9 %fetched.1.refs_8_.down_0 = bf16[1,1024,3072]{2,1,0:T(8,128)(2,1)S(1)} custom-call(bf16[1,1024,6144]{2,1,0:T(8,128)(2,1)} %w_down), custom_call_target="tpu_custom_call" | custom-call | flops 1024 | bytes 1024 | tf_op jit(solution)/shard_map/fetched/pallas_call | solution.py:25
  55.5 0.2 collective-permute-done.14.refs_5_
  55.7 8.5 %rest.1 = (bf16[48,3072]{1,0:T(8,128)(2,1)S(1)}, bf16[48,3072]{1,0:T(8,128)(2,1)S(1)}, bf16[48,3072]{1,0:T(8,128)(2,1)S(1)}, bf16[48,3072]{1,0:T(8,128)(2,1)S(1)...) custom-call(bf16[48,3072]{1,0:T(8,128)(2,1)S(1)} %collective-permute-done.9.refs_0_, ...), custom_call_target="tpu_custom_call" | custom-call | flops 1024 | bytes 1024 | tf_op jit(solution)/shard_map/rest/pallas_call | solution.py:25
  64.2 2.1 %collective-permute-start.23 = (bf16[48,3072]{1,0:T(8,128)(2,1)S(1)}, bf16[48,3072]{1,0:T(8,128)(2,1)S(1)}, u32[]{:S(2)}, u32[]{:S(2)}) collective-permute-start(bf16[48,3072]{1,0:T(8,128)(2,1)S(1)} %get-tuple-element.130), channel_id=1, source_target_pairs={{0,2},{2,4},{4,6},{6,7},{7,5},{5,3},{3,1},{1,0},{8,10},{10,12},{12... | collective-permute-start | bytes 884744 | tf_op jit(solution)/shard_map/ppermute | solution.py:163
  66.3 2.0 %collective-permute-start.15 = (bf16[48,3072]{1,0:T(8,128)(2,1)S(1)}, bf16[48,3072]{1,0:T(8,128)(2,1)S(1)}, u32[]{:S(2)}, u32[]{:S(2)}) collective-permute-start(bf16[48,3072]{1,0:T(8,128)(2,1)S(1)} %get-tuple-element.128), channel_id=1, source_target_pairs={{0,2},{2,4},{4,6},{6,7},{7,5},{5,3},{3,1},{1,0},{8,10},{10,12},{12... | collective-permute-start | bytes 884744 | tf_op jit(solution)/shard_map/ppermute | solution.py:163
  68.4 6.1 %near_down.1 = (bf16[48,3072]{1,0:T(8,128)(2,1)S(1)}, bf16[48,3072]{1,0:T(8,128)(2,1)S(1)}, bf16[48,3072]{1,0:T(8,128)(2,1)S(1)}, bf16[48,3072]{1,0:T(8,128)(2,1...) custom-call(bf16[240,1024]{1,0:T(8,128)(2,1)S(1)} %near_up.1.hidden,, ...), custom_call_target="tpu_custom_call" | custom-call | flops 1024 | bytes 1024 | tf_op jit(solution)/shard_map/near_down/pallas_call | solution.py:25
  74.5 1.7 %collective-permute-done.24 = bf16[48,3072]{1,0:T(8,128)(2,1)S(1)} collective-permute-done((bf16[48,3072]{1,0:T(8,128)(2,1)S(1)}, bf16[48,3072]{1,0:T(8,128)(2,1)S(1)}, u32[]{:S(2)}, u32[]{:S(2)}) %collective-permute-start.24) | collective-permute-done | bytes 294944 | tf_op jit(solution)/shard_map/ppermute | solution.py:163
  76.4 0.1 add_convert_fusion.5
  76.4 2.1 %collective-permute-start.25 = (bf16[48,3072]{1,0:T(8,128)(2,1)S(1)}, bf16[48,3072]{1,0:T(8,128)(2,1)S(1)}, u32[]{:S(2)}, u32[]{:S(2)}) collective-permute-start(bf16[48,3072]{1,0:T(8,128)(2,1)S(1)} %add_convert_fusion.5), channel_id=1, source_target_pairs={{0,2},{2,4},{4,6},{6,7},{7,5},{5,3},{3,1},{1,0},{8,10},{10,12},{12... | collective-permute-start | bytes 884744 | tf_op jit(solution)/shard_map/ppermute | solution.py:163
  78.6 0.8 collective-permute-done.15
  79.3 3.2 %collective-permute-done.16 = bf16[48,3072]{1,0:T(8,128)(2,1)S(1)} collective-permute-done((bf16[48,3072]{1,0:T(8,128)(2,1)S(1)}, bf16[48,3072]{1,0:T(8,128)(2,1)S(1)}, u32[]{:S(2)}, u32[]{:S(2)}) %collective-permute-start.16) | collective-permute-done | bytes 294944 | tf_op jit(solution)/shard_map/ppermute | solution.py:163
  82.7 0.1 add_convert_fusion.11
  82.8 2.1 %collective-permute-start.17 = (bf16[48,3072]{1,0:T(8,128)(2,1)S(1)}, bf16[48,3072]{1,0:T(8,128)(2,1)S(1)}, u32[]{:S(2)}, u32[]{:S(2)}) collective-permute-start(bf16[48,3072]{1,0:T(8,128)(2,1)S(1)} %add_convert_fusion.11), channel_id=1, source_target_pairs={{0,2},{2,4},{4,6},{6,7},{7,5},{5,3},{3,1},{1,0},{8,10},{10,12},{12... | collective-permute-start | bytes 884744 | tf_op jit(solution)/shard_map/ppermute | solution.py:163
  84.9 4.0 %collective-permute-done.26 = bf16[48,3072]{1,0:T(8,128)(2,1)S(1)} collective-permute-done((bf16[48,3072]{1,0:T(8,128)(2,1)S(1)}, bf16[48,3072]{1,0:T(8,128)(2,1)S(1)}, u32[]{:S(2)}, u32[]{:S(2)}) %collective-permute-start.26) | collective-permute-done | bytes 294944 | tf_op jit(solution)/shard_map/ppermute | solution.py:163
  89.0 5.0 %collective-permute-done.18 = bf16[48,3072]{1,0:T(8,128)(2,1)S(1)} collective-permute-done((bf16[48,3072]{1,0:T(8,128)(2,1)S(1)}, bf16[48,3072]{1,0:T(8,128)(2,1)S(1)}, u32[]{:S(2)}, u32[]{:S(2)}) %collective-permute-start.18) | collective-permute-done | bytes 294944 | tf_op jit(solution)/shard_map/ppermute | solution.py:163
  94.1 0.4 collective-permute-start.20
  94.5 1.8 %collective-permute-start.19 = (bf16[48,3072]{1,0:T(8,128)(2,1)S(1)}, bf16[48,3072]{1,0:T(8,128)(2,1)S(1)}, u32[]{:S(2)}, u32[]{:S(2)}) collective-permute-start(bf16[48,3072]{1,0:T(8,128)(2,1)S(1)} %add_convert_fusion.9), channel_id=1, source_target_pairs={{0,2},{2,4},{4,6},{6,7},{7,5},{5,3},{3,1},{1,0},{8,10},{10,12},{12... | collective-permute-start | bytes 884744 | tf_op jit(solution)/shard_map/ppermute | solution.py:163
  96.4 1.6 %collective-permute-start.27 = (bf16[48,3072]{1,0:T(8,128)(2,1)S(1)}, bf16[48,3072]{1,0:T(8,128)(2,1)S(1)}, u32[]{:S(2)}, u32[]{:S(2)}) collective-permute-start(bf16[48,3072]{1,0:T(8,128)(2,1)S(1)} %add_convert_fusion.3), channel_id=1, source_target_pairs={{0,2},{2,4},{4,6},{6,7},{7,5},{5,3},{3,1},{1,0},{8,10},{10,12},{12... | collective-permute-start | bytes 884744 | tf_op jit(solution)/shard_map/ppermute | solution.py:163
  98.0 5.5 %collective-permute-done.20 = bf16[48,3072]{1,0:T(8,128)(2,1)S(1)} collective-permute-done((bf16[48,3072]{1,0:T(8,128)(2,1)S(1)}, bf16[48,3072]{1,0:T(8,128)(2,1)S(1)}, u32[]{:S(2)}, u32[]{:S(2)}) %collective-permute-start.20) | collective-permute-done | bytes 294944 | tf_op jit(solution)/shard_map/ppermute | solution.py:163
  103.6 1.4 %collective-permute-start.22 = (bf16[48,3072]{1,0:T(8,128)(2,1)S(1)}, bf16[48,3072]{1,0:T(8,128)(2,1)S(1)}, u32[]{:S(2)}, u32[]{:S(2)}) collective-permute-start(bf16[48,3072]{1,0:T(8,128)(2,1)S(1)} %add_convert_fusion.6), channel_id=1, source_target_pairs={{2,0},{4,2},{6,4},{7,6},{5,7},{3,5},{1,3},{0,1},{10,8},{12,10},{14... | collective-permute-start | bytes 884744 | tf_op jit(solution)/shard_map/ppermute | solution.py:163
  105.0 0.8 collective-permute-start.21
  105.8 0.4 collective-permute-done.27
  106.3 4.1 %collective-permute-done.22 = bf16[48,3072]{1,0:T(8,128)(2,1)S(1)} collective-permute-done((bf16[48,3072]{1,0:T(8,128)(2,1)S(1)}, bf16[48,3072]{1,0:T(8,128)(2,1)S(1)}, u32[]{:S(2)}, u32[]{:S(2)}) %collective-permute-start.22) | collective-permute-done | bytes 294944 | tf_op jit(solution)/shard_map/ppermute | solution.py:163
  110.4 1.4 %collective-permute-done.21 = bf16[48,3072]{1,0:T(8,128)(2,1)S(1)} collective-permute-done((bf16[48,3072]{1,0:T(8,128)(2,1)S(1)}, bf16[48,3072]{1,0:T(8,128)(2,1)S(1)}, u32[]{:S(2)}, u32[]{:S(2)}) %collective-permute-start.21) | collective-permute-done | bytes 294944 | tf_op jit(solution)/shard_map/ppermute | solution.py:163
  111.8 0.2 add_convert_fusion
  112.2 0.1 fusion.14
  112.3 1.5 %collective-permute-done.29 = bf16[24,6144]{1,0:T(8,128)(2,1)S(1)} collective-permute-done((bf16[24,6144]{1,0:T(8,128)(2,1)S(1)}, bf16[24,6144]{1,0:T(8,128)(2,1)S(1)}, u32[]{:S(2)}, u32[]{:S(2)}) %collective-permute-start.29) | collective-permute-done | bytes 294944 | tf_op jit(solution)/shard_map/ppermute | solution.py:266
  113.7 1.3 %fusion = bf16[64,6144]{1,0:T(8,128)(2,1)} fusion(bf16[1,24,6144]{2,1,0:T(8,128)(2,1)S(1)} %bitcast.22, bf16[1,24,6144]{2,1,0:T(8,128)(2,1)S(1)} %get-tuple-element.157, bf16[2,64]{1,0:T(2,128)(2,1)S(1)} %bitcast.23, s32[2,64]{1,0:T(2,128)S(1)} %subtract_bitcast_fusion, pred[2,64]{1,0:T(4,128)(4,1)S(1)} %get-tuple-element.163), kind=kOutput, calls=%fused_computation.1 | convolution fusion | flops 38052864 | bytes 1377152 | tf_op jit(solution)/shard_map/wcr,wcd->rd/dot_general | solution.py:268
  (41 shorter events, 1.1 us)
Async XLA Ops:
  0.0 1.4 %copy-start = (bf16[64,6144]{1,0:T(8,128)(2,1)S(1)}, bf16[64,6144]{1,0:T(8,128)(2,1)}, u32[]{:S(2)}) copy-start(bf16[64,6144]{1,0:T(8,128)(2,1)} %param.6) | copy-start | bytes 2359300
  1.7 10.0 %collective-permute-start = (bf16[24,6144]{1,0:T(8,128)(2,1)S(1)}, bf16[24,6144]{1,0:T(8,128)(2,1)S(1)}, u32[]{:S(2)}, u32[]{:S(2)}) collective-permute-start(bf16[24,6144]{1,0:T(8,128)(2,1)S(1)} %get-tuple-element.162), channel_id=1, source_target_pairs={{0,8},{8,0},{1,9},{9,1},{2,10},{10,2},{3,11},{11,3},{4,12},{12,4},... | collective-permute-start | bytes 884744 | tf_op jit(solution)/shard_map/ppermute | solution.py:182
  11.8 9.8 %collective-permute-start.1 = (bf16[48,3072]{1,0:T(8,128)(2,1)S(1)}, bf16[48,3072]{1,0:T(8,128)(2,1)S(1)}, u32[]{:S(2)}, u32[]{:S(2)}) collective-permute-start(bf16[48,3072]{1,0:T(8,128)(2,1)S(1)} %get-tuple-element.160.refs_0_), channel_id=1, source_target_pairs={{0,2},{2,4},{4,6},{6,7},{7,5},{5,3},{3,1},{1,0},{8,10},{10,12},{12... | collective-permute-start | bytes 884744 | tf_op jit(solution)/shard_map/ppermute | solution.py:163
  14.5 8.6 %collective-permute-start.2 = (bf16[48,3072]{1,0:T(8,128)(2,1)S(1)}, bf16[48,3072]{1,0:T(8,128)(2,1)S(1)}, u32[]{:S(2)}, u32[]{:S(2)}) collective-permute-start(bf16[48,3072]{1,0:T(8,128)(2,1)S(1)} %get-tuple-element.159.refs_5_), channel_id=1, source_target_pairs={{2,0},{4,2},{6,4},{7,6},{5,7},{3,5},{1,3},{0,1},{10,8},{12,10},{14... | collective-permute-start | bytes 884744 | tf_op jit(solution)/shard_map/ppermute | solution.py:163
  14.5 13.4 %collective-permute-start.3 = (bf16[48,3072]{1,0:T(8,128)(2,1)S(1)}, bf16[48,3072]{1,0:T(8,128)(2,1)S(1)}, u32[]{:S(2)}, u32[]{:S(2)}) collective-permute-start(bf16[48,3072]{1,0:T(8,128)(2,1)S(1)} %get-tuple-element.159.refs_5_), channel_id=1, source_target_pairs={{0,2},{2,4},{4,6},{6,7},{7,5},{5,3},{3,1},{1,0},{8,10},{10,12},{12... | collective-permute-start | bytes 884744 | tf_op jit(solution)/shard_map/ppermute | solution.py:163
  16.5 12.9 %collective-permute-start.4 = (bf16[48,3072]{1,0:T(8,128)(2,1)S(1)}, bf16[48,3072]{1,0:T(8,128)(2,1)S(1)}, u32[]{:S(2)}, u32[]{:S(2)}) collective-permute-start(bf16[48,3072]{1,0:T(8,128)(2,1)S(1)} %get-tuple-element.160.refs_0_), channel_id=1, source_target_pairs={{2,0},{4,2},{6,4},{7,6},{5,7},{3,5},{1,3},{0,1},{10,8},{12,10},{14... | collective-permute-start | bytes 884744 | tf_op jit(solution)/shard_map/ppermute | solution.py:163
  23.0 11.2 %collective-permute-start.5 = (bf16[48,3072]{1,0:T(8,128)(2,1)S(1)}, bf16[48,3072]{1,0:T(8,128)(2,1)S(1)}, u32[]{:S(2)}, u32[]{:S(2)}) collective-permute-start(bf16[48,3072]{1,0:T(8,128)(2,1)S(1)} %collective-permute-done.1.refs_1_), channel_id=1, source_target_pairs={{0,2},{2,4},{4,6},{6,7},{7,5},{5,3},{3,1},{1,0},{8,10},{10,12},{12... | collective-permute-start | bytes 884744 | tf_op jit(solution)/shard_map/ppermute | solution.py:163
  24.6 11.0 %collective-permute-start.6 = (bf16[48,3072]{1,0:T(8,128)(2,1)S(1)}, bf16[48,3072]{1,0:T(8,128)(2,1)S(1)}, u32[]{:S(2)}, u32[]{:S(2)}) collective-permute-start(bf16[48,3072]{1,0:T(8,128)(2,1)S(1)} %collective-permute-done.2.refs_7_), channel_id=1, source_target_pairs={{2,0},{4,2},{6,4},{7,6},{5,7},{3,5},{1,3},{0,1},{10,8},{12,10},{14... | collective-permute-start | bytes 884744 | tf_op jit(solution)/shard_map/ppermute | solution.py:163
  29.3 10.0 %collective-permute-start.7 = (bf16[48,3072]{1,0:T(8,128)(2,1)S(1)}, bf16[48,3072]{1,0:T(8,128)(2,1)S(1)}, u32[]{:S(2)}, u32[]{:S(2)}) collective-permute-start(bf16[48,3072]{1,0:T(8,128)(2,1)S(1)} %collective-permute-done.3.refs_6_), channel_id=1, source_target_pairs={{0,2},{2,4},{4,6},{6,7},{7,5},{5,3},{3,1},{1,0},{8,10},{10,12},{12... | collective-permute-start | bytes 884744 | tf_op jit(solution)/shard_map/ppermute | solution.py:163
  30.9 10.1 %collective-permute-start.8 = (bf16[48,3072]{1,0:T(8,128)(2,1)S(1)}, bf16[48,3072]{1,0:T(8,128)(2,1)S(1)}, u32[]{:S(2)}, u32[]{:S(2)}) collective-permute-start(bf16[48,3072]{1,0:T(8,128)(2,1)S(1)} %collective-permute-done.4.refs_2_), channel_id=1, source_target_pairs={{2,0},{4,2},{6,4},{7,6},{5,7},{3,5},{1,3},{0,1},{10,8},{12,10},{14... | collective-permute-start | bytes 884744 | tf_op jit(solution)/shard_map/ppermute | solution.py:163
  35.7 11.6 %collective-permute-start.10 = (bf16[48,3072]{1,0:T(8,128)(2,1)S(1)}, bf16[48,3072]{1,0:T(8,128)(2,1)S(1)}, u32[]{:S(2)}, u32[]{:S(2)}) collective-permute-start(bf16[48,3072]{1,0:T(8,128)(2,1)S(1)} %collective-permute-done.6.refs_9_), channel_id=1, source_target_pairs={{2,0},{4,2},{6,4},{7,6},{5,7},{3,5},{1,3},{0,1},{10,8},{12,10},{14... | collective-permute-start | bytes 884744 | tf_op jit(solution)/shard_map/ppermute | solution.py:163
  36.0 11.3 %collective-permute-start.9 = (bf16[48,3072]{1,0:T(8,128)(2,1)S(1)}, bf16[48,3072]{1,0:T(8,128)(2,1)S(1)}, u32[]{:S(2)}, u32[]{:S(2)}) collective-permute-start(bf16[48,3072]{1,0:T(8,128)(2,1)S(1)} %collective-permute-done.5.refs_3_), channel_id=1, source_target_pairs={{0,2},{2,4},{4,6},{6,7},{7,5},{5,3},{3,1},{1,0},{8,10},{10,12},{12... | collective-permute-start | bytes 884744 | tf_op jit(solution)/shard_map/ppermute | solution.py:163
  44.2 11.3 %collective-permute-start.11 = (bf16[48,3072]{1,0:T(8,128)(2,1)S(1)}, bf16[48,3072]{1,0:T(8,128)(2,1)S(1)}, u32[]{:S(2)}, u32[]{:S(2)}) collective-permute-start(bf16[48,3072]{1,0:T(8,128)(2,1)S(1)} %collective-permute-done.7.refs_8_), channel_id=1, source_target_pairs={{0,2},{2,4},{4,6},{6,7},{7,5},{5,3},{3,1},{1,0},{8,10},{10,12},{12... | collective-permute-start | bytes 884744 | tf_op jit(solution)/shard_map/ppermute | solution.py:163
  45.8 9.7 %collective-permute-start.12 = (bf16[48,3072]{1,0:T(8,128)(2,1)S(1)}, bf16[48,3072]{1,0:T(8,128)(2,1)S(1)}, u32[]{:S(2)}, u32[]{:S(2)}) collective-permute-start(bf16[48,3072]{1,0:T(8,128)(2,1)S(1)} %collective-permute-done.8.refs_4_), channel_id=1, source_target_pairs={{2,0},{4,2},{6,4},{7,6},{5,7},{3,5},{1,3},{0,1},{10,8},{12,10},{14... | collective-permute-start | bytes 884744 | tf_op jit(solution)/shard_map/ppermute | solution.py:163
  47.3 8.2 %collective-permute-start.13 = (bf16[48,3072]{1,0:T(8,128)(2,1)S(1)}, bf16[48,3072]{1,0:T(8,128)(2,1)S(1)}, u32[]{:S(2)}, u32[]{:S(2)}) collective-permute-start(bf16[48,3072]{1,0:T(8,128)(2,1)S(1)} %collective-permute-done.9.refs_0_), channel_id=1, source_target_pairs={{0,2},{2,4},{4,6},{6,7},{7,5},{5,3},{3,1},{1,0},{8,10},{10,12},{12... | collective-permute-start | bytes 884744 | tf_op jit(solution)/shard_map/ppermute | solution.py:163
  48.9 6.8 %collective-permute-start.14 = (bf16[48,3072]{1,0:T(8,128)(2,1)S(1)}, bf16[48,3072]{1,0:T(8,128)(2,1)S(1)}, u32[]{:S(2)}, u32[]{:S(2)}) collective-permute-start(bf16[48,3072]{1,0:T(8,128)(2,1)S(1)} %collective-permute-done.10.refs_4_), channel_id=1, source_target_pairs={{2,0},{4,2},{6,4},{7,6},{5,7},{3,5},{1,3},{0,1},{10,8},{12,10},{14... | collective-permute-start | bytes 884744 | tf_op jit(solution)/shard_map/ppermute | solution.py:163
  64.2 10.3 %collective-permute-start.23 = (bf16[48,3072]{1,0:T(8,128)(2,1)S(1)}, bf16[48,3072]{1,0:T(8,128)(2,1)S(1)}, u32[]{:S(2)}, u32[]{:S(2)}) collective-permute-start(bf16[48,3072]{1,0:T(8,128)(2,1)S(1)} %get-tuple-element.130), channel_id=1, source_target_pairs={{0,2},{2,4},{4,6},{6,7},{7,5},{5,3},{3,1},{1,0},{8,10},{10,12},{12... | collective-permute-start | bytes 884744 | tf_op jit(solution)/shard_map/ppermute | solution.py:163
  66.3 9.9 %collective-permute-start.24 = (bf16[48,3072]{1,0:T(8,128)(2,1)S(1)}, bf16[48,3072]{1,0:T(8,128)(2,1)S(1)}, u32[]{:S(2)}, u32[]{:S(2)}) collective-permute-start(bf16[48,3072]{1,0:T(8,128)(2,1)S(1)} %get-tuple-element.126), channel_id=1, source_target_pairs={{2,0},{4,2},{6,4},{7,6},{5,7},{3,5},{1,3},{0,1},{10,8},{12,10},{14... | collective-permute-start | bytes 884744 | tf_op jit(solution)/shard_map/ppermute | solution.py:163
  66.3 13.0 %collective-permute-start.15 = (bf16[48,3072]{1,0:T(8,128)(2,1)S(1)}, bf16[48,3072]{1,0:T(8,128)(2,1)S(1)}, u32[]{:S(2)}, u32[]{:S(2)}) collective-permute-start(bf16[48,3072]{1,0:T(8,128)(2,1)S(1)} %get-tuple-element.128), channel_id=1, source_target_pairs={{0,2},{2,4},{4,6},{6,7},{7,5},{5,3},{3,1},{1,0},{8,10},{10,12},{12... | collective-permute-start | bytes 884744 | tf_op jit(solution)/shard_map/ppermute | solution.py:163
  68.3 14.2 %collective-permute-start.16 = (bf16[48,3072]{1,0:T(8,128)(2,1)S(1)}, bf16[48,3072]{1,0:T(8,128)(2,1)S(1)}, u32[]{:S(2)}, u32[]{:S(2)}) collective-permute-start(bf16[48,3072]{1,0:T(8,128)(2,1)S(1)} %get-tuple-element.131), channel_id=1, source_target_pairs={{2,0},{4,2},{6,4},{7,6},{5,7},{3,5},{1,3},{0,1},{10,8},{12,10},{14... | collective-permute-start | bytes 884744 | tf_op jit(solution)/shard_map/ppermute | solution.py:163
  68.3 46.7 %copy-start.1 = (bf16[64,6144]{1,0:T(8,128)(2,1)S(1)}, bf16[64,6144]{1,0:T(8,128)(2,1)}, u32[]{:S(2)}) copy-start(bf16[64,6144]{1,0:T(8,128)(2,1)} %param.6) | copy-start | bytes 2359300
  68.3 43.8 %copy-start.2 = (s32[64,2]{0,1:T(2,128)S(1)}, s32[64,2]{0,1:T(2,128)}, u32[]{:S(2)}) copy-start(s32[64,2]{0,1:T(2,128)} %param.7) | copy-start | bytes 1540
  68.3 43.8 %copy-start.3 = (f32[64,2]{0,1:T(2,128)S(1)}, f32[64,2]{0,1:T(2,128)}, u32[]{:S(2)}) copy-start(f32[64,2]{0,1:T(2,128)} %param.8) | copy-start | bytes 1540
  76.3 12.6 %collective-permute-start.26 = (bf16[48,3072]{1,0:T(8,128)(2,1)S(1)}, bf16[48,3072]{1,0:T(8,128)(2,1)S(1)}, u32[]{:S(2)}, u32[]{:S(2)}) collective-permute-start(bf16[48,3072]{1,0:T(8,128)(2,1)S(1)} %add_convert_fusion.4), channel_id=1, source_target_pairs={{2,0},{4,2},{6,4},{7,6},{5,7},{3,5},{1,3},{0,1},{10,8},{12,10},{14... | collective-permute-start | bytes 884744 | tf_op jit(solution)/shard_map/ppermute | solution.py:163
  76.4 12.4 %collective-permute-start.25 = (bf16[48,3072]{1,0:T(8,128)(2,1)S(1)}, bf16[48,3072]{1,0:T(8,128)(2,1)S(1)}, u32[]{:S(2)}, u32[]{:S(2)}) collective-permute-start(bf16[48,3072]{1,0:T(8,128)(2,1)S(1)} %add_convert_fusion.5), channel_id=1, source_target_pairs={{0,2},{2,4},{4,6},{6,7},{7,5},{5,3},{3,1},{1,0},{8,10},{10,12},{12... | collective-permute-start | bytes 884744 | tf_op jit(solution)/shard_map/ppermute | solution.py:163
  82.6 11.4 %collective-permute-start.18 = (bf16[48,3072]{1,0:T(8,128)(2,1)S(1)}, bf16[48,3072]{1,0:T(8,128)(2,1)S(1)}, u32[]{:S(2)}, u32[]{:S(2)}) collective-permute-start(bf16[48,3072]{1,0:T(8,128)(2,1)S(1)} %add_convert_fusion.10), channel_id=1, source_target_pairs={{2,0},{4,2},{6,4},{7,6},{5,7},{3,5},{1,3},{0,1},{10,8},{12,10},{14... | collective-permute-start | bytes 884744 | tf_op jit(solution)/shard_map/ppermute | solution.py:163
  82.8 11.3 %collective-permute-start.17 = (bf16[48,3072]{1,0:T(8,128)(2,1)S(1)}, bf16[48,3072]{1,0:T(8,128)(2,1)S(1)}, u32[]{:S(2)}, u32[]{:S(2)}) collective-permute-start(bf16[48,3072]{1,0:T(8,128)(2,1)S(1)} %add_convert_fusion.11), channel_id=1, source_target_pairs={{0,2},{2,4},{4,6},{6,7},{7,5},{5,3},{3,1},{1,0},{8,10},{10,12},{12... | collective-permute-start | bytes 884744 | tf_op jit(solution)/shard_map/ppermute | solution.py:163
  88.9 16.9 %collective-permute-start.28 = (bf16[48,3072]{1,0:T(8,128)(2,1)S(1)}, bf16[48,3072]{1,0:T(8,128)(2,1)S(1)}, u32[]{:S(2)}, u32[]{:S(2)}) collective-permute-start(bf16[48,3072]{1,0:T(8,128)(2,1)S(1)} %add_convert_fusion.2), channel_id=1, source_target_pairs={{2,0},{4,2},{6,4},{7,6},{5,7},{3,5},{1,3},{0,1},{10,8},{12,10},{14... | collective-permute-start | bytes 884744 | tf_op jit(solution)/shard_map/ppermute | solution.py:163
  94.1 9.4 %collective-permute-start.20 = (bf16[48,3072]{1,0:T(8,128)(2,1)S(1)}, bf16[48,3072]{1,0:T(8,128)(2,1)S(1)}, u32[]{:S(2)}, u32[]{:S(2)}) collective-permute-start(bf16[48,3072]{1,0:T(8,128)(2,1)S(1)} %add_convert_fusion.8), channel_id=1, source_target_pairs={{2,0},{4,2},{6,4},{7,6},{5,7},{3,5},{1,3},{0,1},{10,8},{12,10},{14... | collective-permute-start | bytes 884744 | tf_op jit(solution)/shard_map/ppermute | solution.py:163
  94.5 9.0 %collective-permute-start.19 = (bf16[48,3072]{1,0:T(8,128)(2,1)S(1)}, bf16[48,3072]{1,0:T(8,128)(2,1)S(1)}, u32[]{:S(2)}, u32[]{:S(2)}) collective-permute-start(bf16[48,3072]{1,0:T(8,128)(2,1)S(1)} %add_convert_fusion.9), channel_id=1, source_target_pairs={{0,2},{2,4},{4,6},{6,7},{7,5},{5,3},{3,1},{1,0},{8,10},{10,12},{12... | collective-permute-start | bytes 884744 | tf_op jit(solution)/shard_map/ppermute | solution.py:163
  96.4 9.9 %collective-permute-start.27 = (bf16[48,3072]{1,0:T(8,128)(2,1)S(1)}, bf16[48,3072]{1,0:T(8,128)(2,1)S(1)}, u32[]{:S(2)}, u32[]{:S(2)}) collective-permute-start(bf16[48,3072]{1,0:T(8,128)(2,1)S(1)} %add_convert_fusion.3), channel_id=1, source_target_pairs={{0,2},{2,4},{4,6},{6,7},{7,5},{5,3},{3,1},{1,0},{8,10},{10,12},{12... | collective-permute-start | bytes 884744 | tf_op jit(solution)/shard_map/ppermute | solution.py:163
  103.6 6.8 %collective-permute-start.22 = (bf16[48,3072]{1,0:T(8,128)(2,1)S(1)}, bf16[48,3072]{1,0:T(8,128)(2,1)S(1)}, u32[]{:S(2)}, u32[]{:S(2)}) collective-permute-start(bf16[48,3072]{1,0:T(8,128)(2,1)S(1)} %add_convert_fusion.6), channel_id=1, source_target_pairs={{2,0},{4,2},{6,4},{7,6},{5,7},{3,5},{1,3},{0,1},{10,8},{12,10},{14... | collective-permute-start | bytes 884744 | tf_op jit(solution)/shard_map/ppermute | solution.py:163
  105.0 6.8 %collective-permute-start.21 = (bf16[48,3072]{1,0:T(8,128)(2,1)S(1)}, bf16[48,3072]{1,0:T(8,128)(2,1)S(1)}, u32[]{:S(2)}, u32[]{:S(2)}) collective-permute-start(bf16[48,3072]{1,0:T(8,128)(2,1)S(1)} %add_convert_fusion.7), channel_id=1, source_target_pairs={{0,2},{2,4},{4,6},{6,7},{7,5},{5,3},{3,1},{1,0},{8,10},{10,12},{12... | collective-permute-start | bytes 884744 | tf_op jit(solution)/shard_map/ppermute | solution.py:163
  112.1 1.6 %collective-permute-start.29 = (bf16[24,6144]{1,0:T(8,128)(2,1)S(1)}, bf16[24,6144]{1,0:T(8,128)(2,1)S(1)}, u32[]{:S(2)}, u32[]{:S(2)}) collective-permute-start(bf16[24,6144]{1,0:T(8,128)(2,1)S(1)} %get-tuple-element.158), channel_id=1, source_target_pairs={{0,8},{8,0},{1,9},{9,1},{2,10},{10,2},{3,11},{11,3},{4,12},{12,4},... | collective-permute-start | bytes 884744 | tf_op jit(solution)/shard_map/ppermute | solution.py:266

commit v14 on v12

--- a/solution.py
+++ b/solution.py
@@ -216,6 +216,7 @@
         [pltpu.VMEM((3 * size, units), jnp.float32)] * 2 + down_scratch,
         down_room + 3 * size * units * 16,
     )
+    near_hidden, _, _ = tied(near_hidden, rest_parts[4], rest_parts[0])
     near_parts = call(
         near_down_kernel, "near_down", [(near_hidden, pltpu.VMEM), (down_here, pltpu.VMEM), (w_down, pltpu.HBM)],
         [((size, mid_col), jnp.bfloat16)] * (2 * count), down_scratch, down_room + rows * TILE * 12,

time: 112 us -> 111 us (level)
  waiting for transfers between devices: 43.5 us -> 42.3 us
    ppermute x14, waiting for transfers between devices: 17.9 us -> 15.2 us  [step(): lax.ppermute(to_right, 'tensor', right)]
    ppermute x14, waiting for transfers between devices: 23 us -> 24.4 us  [step(): lax.ppermute(to_left, 'tensor', left)]
  transfers between devices with their start and end apart: 30 -> 30, of which waited for: 16 -> 17; matrix products, arithmetic and copies ran while one was open for 1% -> 1% of each run, Pallas kernels for 22% -> 22%
where the time goes in v14:
time: 111 us
  waiting for transfers between devices  42.3 us (38%)
  Pallas kernels  33.3 us (30%)
  starting transfers between devices  30.7 us (28%)
  other arithmetic  2.18 us (2%)
  matrix products  1.59 us (1%)
    pallas_call x7, Pallas kernels, call(): pl.pallas_call(kernel, in_specs=[pl.BlockSpec(memory_space=memory) for _,...  33.3 us
    ppermute x14, waiting for transfers between devices, step(): lax.ppermute(to_left, 'tensor', left)  24.4 us
    ppermute x14, starting transfers between devices, step(): lax.ppermute(to_left, 'tensor', left)  23.7 us
    ppermute x14, waiting for transfers between devices, step(): lax.ppermute(to_right, 'tensor', right)  15.2 us
    ppermute x14, starting transfers between devices, step(): lax.ppermute(to_right, 'tensor', right)  6.4 us
  transfers between devices with their start and end apart: 30, of which 17 were waited for; matrix products, arithmetic and copies ran while one was open for 1% of the time, Pallas kernels for 22%

profile of v14, /device:TPU:0, one launch (start us, length us, event | category | flops | bytes accessed | tf_op | source)
XLA Modules:
  0.0 110.6 jit_solution(15485078057199478694)
XLA Ops:
  0.0 0.1 eq.64
  0.1 0.1 pad_add_fusion
  0.2 0.8 compare_reduce_fusion
  1.0 0.1 copy.17
  1.1 0.1 reduce_window_sum.11
  1.2 0.1 copy.18
  1.3 0.1 fusion.9
  1.4 0.3 convolution_convert_fusion
  1.7 0.5 collective-permute-start
  2.3 1.2 %collective-permute-done = bf16[24,6144]{1,0:T(8,128)(2,1)S(1)} collective-permute-done((bf16[24,6144]{1,0:T(8,128)(2,1)S(1)}, bf16[24,6144]{1,0:T(8,128)(2,1)S(1)}, u32[]{:S(2)}, u32[]{:S(2)}) %collective-permute-start) | collective-permute-done | bytes 294944 | tf_op jit(solution)/shard_map/ppermute | solution.py:164
  3.6 2.9 %collective-permute-start.2 = (bf16[48,3072]{1,0:T(8,128)(2,1)S(1)}, bf16[48,3072]{1,0:T(8,128)(2,1)S(1)}, u32[]{:S(2)}, u32[]{:S(2)}) collective-permute-start(bf16[48,3072]{1,0:T(8,128)(2,1)S(1)} %get-tuple-element.149.refs_5_), channel_id=1, source_target_pairs={{2,0},{4,2},{6,4},{7,6},{5,7},{3,5},{1,3},{0,1},{10,8},{12,10},{14... | collective-permute-start | bytes 884744 | tf_op jit(solution)/shard_map/ppermute | solution.py:150
  6.5 0.1 collective-permute-start.1
  6.6 2.0 %collective-permute-start.3 = (bf16[48,3072]{1,0:T(8,128)(2,1)S(1)}, bf16[48,3072]{1,0:T(8,128)(2,1)S(1)}, u32[]{:S(2)}, u32[]{:S(2)}) collective-permute-start(bf16[48,3072]{1,0:T(8,128)(2,1)S(1)} %get-tuple-element.149.refs_5_), channel_id=1, source_target_pairs={{0,2},{2,4},{4,6},{6,7},{7,5},{5,3},{3,1},{1,0},{8,10},{10,12},{12... | collective-permute-start | bytes 884744 | tf_op jit(solution)/shard_map/ppermute | solution.py:150
  8.6 4.7 %fetched.3.refs_10_.refs_6_ = bf16[1,6144,1024]{2,1,0:T(8,128)(2,1)S(1)} custom-call(bf16[1,6144,1024]{2,1,0:T(8,128)(2,1)} %source), custom_call_target="tpu_custom_call" | custom-call | flops 1024 | bytes 1024 | tf_op jit(solution)/shard_map/fetched/pallas_call | solution.py:29
  13.4 1.0 collective-permute-done.2.refs_7_
  14.3 2.0 %collective-permute-done.1.refs_1_ = bf16[48,3072]{1,0:T(8,128)(2,1)S(1)} collective-permute-done((bf16[48,3072]{1,0:T(8,128)(2,1)S(1)}, bf16[48,3072]{1,0:T(8,128)(2,1)S(1)}, u32[]{:S(2)}, u32[]{:S(2)}) %collective-permute-start.1) | collective-permute-done | bytes 294944 | tf_op jit(solution)/shard_map/ppermute | solution.py:150
  16.4 0.1 collective-permute-start.5
  16.5 1.9 %collective-permute-start.6 = (bf16[48,3072]{1,0:T(8,128)(2,1)S(1)}, bf16[48,3072]{1,0:T(8,128)(2,1)S(1)}, u32[]{:S(2)}, u32[]{:S(2)}) collective-permute-start(bf16[48,3072]{1,0:T(8,128)(2,1)S(1)} %collective-permute-done.2.refs_7_), channel_id=1, source_target_pairs={{2,0},{4,2},{6,4},{7,6},{5,7},{3,5},{1,3},{0,1},{10,8},{12,10},{14... | collective-permute-start | bytes 884744 | tf_op jit(solution)/shard_map/ppermute | solution.py:150
  18.4 4.7 %fetched.4.refs_10_.refs_7_ = bf16[1,6144,1024]{2,1,0:T(8,128)(2,1)S(1)} custom-call(bf16[1,6144,1024]{2,1,0:T(8,128)(2,1)} %source.1), custom_call_target="tpu_custom_call" | custom-call | flops 1024 | bytes 1024 | tf_op jit(solution)/shard_map/fetched/pallas_call | solution.py:29
  23.2 1.6 %collective-permute-start.8 = (bf16[48,3072]{1,0:T(8,128)(2,1)S(1)}, bf16[48,3072]{1,0:T(8,128)(2,1)S(1)}, u32[]{:S(2)}, u32[]{:S(2)}) collective-permute-start(bf16[48,3072]{1,0:T(8,128)(2,1)S(1)} %collective-permute-done.4.refs_2_), channel_id=1, source_target_pairs={{2,0},{4,2},{6,4},{7,6},{5,7},{3,5},{1,3},{0,1},{10,8},{12,10},{14... | collective-permute-start | bytes 884744 | tf_op jit(solution)/shard_map/ppermute | solution.py:150
  24.8 0.4 collective-permute-start.7
  25.2 3.8 %collective-permute-done.5.refs_3_ = bf16[48,3072]{1,0:T(8,128)(2,1)S(1)} collective-permute-done((bf16[48,3072]{1,0:T(8,128)(2,1)S(1)}, bf16[48,3072]{1,0:T(8,128)(2,1)S(1)}, u32[]{:S(2)}, u32[]{:S(2)}) %collective-permute-start.5) | collective-permute-done | bytes 294944 | tf_op jit(solution)/shard_map/ppermute | solution.py:150
  29.0 0.1 collective-permute-start.9
  29.1 1.9 %collective-permute-start.10 = (bf16[48,3072]{1,0:T(8,128)(2,1)S(1)}, bf16[48,3072]{1,0:T(8,128)(2,1)S(1)}, u32[]{:S(2)}, u32[]{:S(2)}) collective-permute-start(bf16[48,3072]{1,0:T(8,128)(2,1)S(1)} %collective-permute-done.6.refs_9_), channel_id=1, source_target_pairs={{2,0},{4,2},{6,4},{7,6},{5,7},{3,5},{1,3},{0,1},{10,8},{12,10},{14... | collective-permute-start | bytes 884744 | tf_op jit(solution)/shard_map/ppermute | solution.py:150
  31.1 2.2 %collective-permute-done.8.refs_4_ = bf16[48,3072]{1,0:T(8,128)(2,1)S(1)} collective-permute-done((bf16[48,3072]{1,0:T(8,128)(2,1)S(1)}, bf16[48,3072]{1,0:T(8,128)(2,1)S(1)}, u32[]{:S(2)}, u32[]{:S(2)}) %collective-permute-start.8) | collective-permute-done | bytes 294944 | tf_op jit(solution)/shard_map/ppermute | solution.py:150
  33.3 2.0 %collective-permute-done.7.refs_8_ = bf16[48,3072]{1,0:T(8,128)(2,1)S(1)} collective-permute-done((bf16[48,3072]{1,0:T(8,128)(2,1)S(1)}, bf16[48,3072]{1,0:T(8,128)(2,1)S(1)}, u32[]{:S(2)}, u32[]{:S(2)}) %collective-permute-start.7) | collective-permute-done | bytes 294944 | tf_op jit(solution)/shard_map/ppermute | solution.py:150
  35.4 3.2 %near_gate.1.refs_11_ = f32[240,1024]{1,0:T(8,128)S(1)} custom-call(bf16[48,3072]{1,0:T(8,128)(2,1)S(1)} %get-tuple-element.150.refs_0_, bf16[48,3072]{1,0:T(8,128)(2,1)S(1)} %collective-permute-done.1.refs_1_, bf16[48,3072]{1,0:T(8,128)(2,1)S(1)} %collective-permute-done.4.refs_2_, bf16[48,3072]{1,0:T(8,128)(2,1)S(1)} %collective-permute-done.5.refs_3_, ...), custom_call_target="tpu_custom_call" | custom-call | flops 1024 | bytes 1024 | tf_op jit(solution)/shard_map/near_gate/pallas_call | solution.py:29
  38.6 0.1 collective-permute-start.11
  38.7 1.9 %collective-permute-start.12 = (bf16[48,3072]{1,0:T(8,128)(2,1)S(1)}, bf16[48,3072]{1,0:T(8,128)(2,1)S(1)}, u32[]{:S(2)}, u32[]{:S(2)}) collective-permute-start(bf16[48,3072]{1,0:T(8,128)(2,1)S(1)} %collective-permute-done.8.refs_4_), channel_id=1, source_target_pairs={{2,0},{4,2},{6,4},{7,6},{5,7},{3,5},{1,3},{0,1},{10,8},{12,10},{14... | collective-permute-start | bytes 884744 | tf_op jit(solution)/shard_map/ppermute | solution.py:150
  40.6 1.0 collective-permute-done.9.refs_0_
  41.7 0.1 collective-permute-start.13
  41.8 1.9 %collective-permute-start.14 = (bf16[48,3072]{1,0:T(8,128)(2,1)S(1)}, bf16[48,3072]{1,0:T(8,128)(2,1)S(1)}, u32[]{:S(2)}, u32[]{:S(2)}) collective-permute-start(bf16[48,3072]{1,0:T(8,128)(2,1)S(1)} %collective-permute-done.10.refs_4_), channel_id=1, source_target_pairs={{2,0},{4,2},{6,4},{7,6},{5,7},{3,5},{1,3},{0,1},{10,8},{12,10},{14... | collective-permute-start | bytes 884744 | tf_op jit(solution)/shard_map/ppermute | solution.py:150
  43.7 3.2 %near_up.1.hidden = bf16[240,1024]{1,0:T(8,128)(2,1)S(1)} custom-call(bf16[48,3072]{1,0:T(8,128)(2,1)S(1)} %get-tuple-element.150.refs_0_, bf16[48,3072]{1,0:T(8,128)(2,1)S(1)} %collective-permute-done.1.refs_1_, bf16[48,3072]{1,0:T(8,128)(2,1)S(1)} %collective-permute-done.4.refs_2_, bf16[48,3072]{1,0:T(8,128)(2,1)S(1)} %collective-permute-done.5.refs_3_, ...), custom_call_target="tpu_custom_call" | custom-call | flops 1024 | bytes 1024 | tf_op jit(solution)/shard_map/near_up/pallas_call | solution.py:29
  46.9 2.9 %fetched.5.refs_8_.down_0 = bf16[1,1024,3072]{2,1,0:T(8,128)(2,1)S(1)} custom-call(bf16[1,1024,6144]{2,1,0:T(8,128)(2,1)} %w_down), custom_call_target="tpu_custom_call" | custom-call | flops 1024 | bytes 1024 | tf_op jit(solution)/shard_map/fetched/pallas_call | solution.py:29
  49.9 3.3 %collective-permute-done.13.refs_2_ = bf16[48,3072]{1,0:T(8,128)(2,1)S(1)} collective-permute-done((bf16[48,3072]{1,0:T(8,128)(2,1)S(1)}, bf16[48,3072]{1,0:T(8,128)(2,1)S(1)}, u32[]{:S(2)}, u32[]{:S(2)}) %collective-permute-start.13) | collective-permute-done | bytes 294944 | tf_op jit(solution)/shard_map/ppermute | solution.py:150
  53.2 8.5 %rest.1 = (bf16[48,3072]{1,0:T(8,128)(2,1)S(1)}, bf16[48,3072]{1,0:T(8,128)(2,1)S(1)}, bf16[48,3072]{1,0:T(8,128)(2,1)S(1)}, bf16[48,3072]{1,0:T(8,128)(2,1)S(1)...) custom-call(bf16[48,3072]{1,0:T(8,128)(2,1)S(1)} %collective-permute-done.9.refs_0_, ...), custom_call_target="tpu_custom_call" | custom-call | flops 1024 | bytes 1024 | tf_op jit(solution)/shard_map/rest/pallas_call | solution.py:29
  61.7 0.5 collective-permute-start.15
  62.2 1.6 %collective-permute-start.16 = (bf16[48,3072]{1,0:T(8,128)(2,1)S(1)}, bf16[48,3072]{1,0:T(8,128)(2,1)S(1)}, u32[]{:S(2)}, u32[]{:S(2)}) collective-permute-start(bf16[48,3072]{1,0:T(8,128)(2,1)S(1)} %get-tuple-element.124), channel_id=1, source_target_pairs={{2,0},{4,2},{6,4},{7,6},{5,7},{3,5},{1,3},{0,1},{10,8},{12,10},{14... | collective-permute-start | bytes 884744 | tf_op jit(solution)/shard_map/ppermute | solution.py:150
  63.8 0.5 collective-permute-start.23
  64.2 1.6 %collective-permute-start.24 = (bf16[48,3072]{1,0:T(8,128)(2,1)S(1)}, bf16[48,3072]{1,0:T(8,128)(2,1)S(1)}, u32[]{:S(2)}, u32[]{:S(2)}) collective-permute-start(bf16[48,3072]{1,0:T(8,128)(2,1)S(1)} %get-tuple-element.117), channel_id=1, source_target_pairs={{2,0},{4,2},{6,4},{7,6},{5,7},{3,5},{1,3},{0,1},{10,8},{12,10},{14... | collective-permute-start | bytes 884744 | tf_op jit(solution)/shard_map/ppermute | solution.py:150
  65.8 6.1 %near_down.1 = (bf16[48,3072]{1,0:T(8,128)(2,1)S(1)}, bf16[48,3072]{1,0:T(8,128)(2,1)S(1)}, bf16[48,3072]{1,0:T(8,128)(2,1)S(1)}, bf16[48,3072]{1,0:T(8,128)(2,1...) custom-call(bf16[240,1024]{1,0:T(8,128)(2,1)S(1)} %near_up.1.hidden,, ...), custom_call_target="tpu_custom_call" | custom-call | flops 1024 | bytes 1024 | tf_op jit(solution)/shard_map/near_down/pallas_call | solution.py:29
  71.9 0.2 collective-permute-done.16
  72.2 1.6 %collective-permute-start.18 = (bf16[48,3072]{1,0:T(8,128)(2,1)S(1)}, bf16[48,3072]{1,0:T(8,128)(2,1)S(1)}, u32[]{:S(2)}, u32[]{:S(2)}) collective-permute-start(bf16[48,3072]{1,0:T(8,128)(2,1)S(1)} %add_convert_fusion.10), channel_id=1, source_target_pairs={{2,0},{4,2},{6,4},{7,6},{5,7},{3,5},{1,3},{0,1},{10,8},{12,10},{14... | collective-permute-start | bytes 884744 | tf_op jit(solution)/shard_map/ppermute | solution.py:150
  73.9 0.5 collective-permute-start.17
  74.4 2.9 %collective-permute-done.23 = bf16[48,3072]{1,0:T(8,128)(2,1)S(1)} collective-permute-done((bf16[48,3072]{1,0:T(8,128)(2,1)S(1)}, bf16[48,3072]{1,0:T(8,128)(2,1)S(1)}, u32[]{:S(2)}, u32[]{:S(2)}) %collective-permute-start.23) | collective-permute-done | bytes 294944 | tf_op jit(solution)/shard_map/ppermute | solution.py:150
  77.3 1.1 %collective-permute-done.24 = bf16[48,3072]{1,0:T(8,128)(2,1)S(1)} collective-permute-done((bf16[48,3072]{1,0:T(8,128)(2,1)S(1)}, bf16[48,3072]{1,0:T(8,128)(2,1)S(1)}, u32[]{:S(2)}, u32[]{:S(2)}) %collective-permute-start.24) | collective-permute-done | bytes 294944 | tf_op jit(solution)/shard_map/ppermute | solution.py:150
  78.5 1.6 %collective-permute-start.26 = (bf16[48,3072]{1,0:T(8,128)(2,1)S(1)}, bf16[48,3072]{1,0:T(8,128)(2,1)S(1)}, u32[]{:S(2)}, u32[]{:S(2)}) collective-permute-start(bf16[48,3072]{1,0:T(8,128)(2,1)S(1)} %add_convert_fusion.4), channel_id=1, source_target_pairs={{2,0},{4,2},{6,4},{7,6},{5,7},{3,5},{1,3},{0,1},{10,8},{12,10},{14... | collective-permute-start | bytes 884744 | tf_op jit(solution)/shard_map/ppermute | solution.py:150
  80.2 0.5 collective-permute-start.25
  80.7 4.0 %collective-permute-done.18 = bf16[48,3072]{1,0:T(8,128)(2,1)S(1)} collective-permute-done((bf16[48,3072]{1,0:T(8,128)(2,1)S(1)}, bf16[48,3072]{1,0:T(8,128)(2,1)S(1)}, u32[]{:S(2)}, u32[]{:S(2)}) %collective-permute-start.18) | collective-permute-done | bytes 294944 | tf_op jit(solution)/shard_map/ppermute | solution.py:150
  84.9 1.6 %collective-permute-start.20 = (bf16[48,3072]{1,0:T(8,128)(2,1)S(1)}, bf16[48,3072]{1,0:T(8,128)(2,1)S(1)}, u32[]{:S(2)}, u32[]{:S(2)}) collective-permute-start(bf16[48,3072]{1,0:T(8,128)(2,1)S(1)} %add_convert_fusion.8), channel_id=1, source_target_pairs={{2,0},{4,2},{6,4},{7,6},{5,7},{3,5},{1,3},{0,1},{10,8},{12,10},{14... | collective-permute-start | bytes 884744 | tf_op jit(solution)/shard_map/ppermute | solution.py:150
  86.6 0.5 collective-permute-start.19
  87.1 4.0 %collective-permute-done.26 = bf16[48,3072]{1,0:T(8,128)(2,1)S(1)} collective-permute-done((bf16[48,3072]{1,0:T(8,128)(2,1)S(1)}, bf16[48,3072]{1,0:T(8,128)(2,1)S(1)}, u32[]{:S(2)}, u32[]{:S(2)}) %collective-permute-start.26) | collective-permute-done | bytes 294944 | tf_op jit(solution)/shard_map/ppermute | solution.py:150
  91.2 1.6 %collective-permute-start.28 = (bf16[48,3072]{1,0:T(8,128)(2,1)S(1)}, bf16[48,3072]{1,0:T(8,128)(2,1)S(1)}, u32[]{:S(2)}, u32[]{:S(2)}) collective-permute-start(bf16[48,3072]{1,0:T(8,128)(2,1)S(1)} %add_convert_fusion.2), channel_id=1, source_target_pairs={{2,0},{4,2},{6,4},{7,6},{5,7},{3,5},{1,3},{0,1},{10,8},{12,10},{14... | collective-permute-start | bytes 884744 | tf_op jit(solution)/shard_map/ppermute | solution.py:150
  92.9 0.5 collective-permute-start.27
  93.4 4.0 %collective-permute-done.20 = bf16[48,3072]{1,0:T(8,128)(2,1)S(1)} collective-permute-done((bf16[48,3072]{1,0:T(8,128)(2,1)S(1)}, bf16[48,3072]{1,0:T(8,128)(2,1)S(1)}, u32[]{:S(2)}, u32[]{:S(2)}) %collective-permute-start.20) | collective-permute-done | bytes 294944 | tf_op jit(solution)/shard_map/ppermute | solution.py:150
  97.5 1.6 %collective-permute-start.22 = (bf16[48,3072]{1,0:T(8,128)(2,1)S(1)}, bf16[48,3072]{1,0:T(8,128)(2,1)S(1)}, u32[]{:S(2)}, u32[]{:S(2)}) collective-permute-start(bf16[48,3072]{1,0:T(8,128)(2,1)S(1)} %add_convert_fusion.6), channel_id=1, source_target_pairs={{2,0},{4,2},{6,4},{7,6},{5,7},{3,5},{1,3},{0,1},{10,8},{12,10},{14... | collective-permute-start | bytes 884744 | tf_op jit(solution)/shard_map/ppermute | solution.py:150
  99.2 0.5 collective-permute-start.21
  99.7 4.0 %collective-permute-done.28 = bf16[48,3072]{1,0:T(8,128)(2,1)S(1)} collective-permute-done((bf16[48,3072]{1,0:T(8,128)(2,1)S(1)}, bf16[48,3072]{1,0:T(8,128)(2,1)S(1)}, u32[]{:S(2)}, u32[]{:S(2)}) %collective-permute-start.28) | collective-permute-done | bytes 294944 | tf_op jit(solution)/shard_map/ppermute | solution.py:150
  103.7 3.7 %collective-permute-done.22 = bf16[48,3072]{1,0:T(8,128)(2,1)S(1)} collective-permute-done((bf16[48,3072]{1,0:T(8,128)(2,1)S(1)}, bf16[48,3072]{1,0:T(8,128)(2,1)S(1)}, u32[]{:S(2)}, u32[]{:S(2)}) %collective-permute-start.22) | collective-permute-done | bytes 294944 | tf_op jit(solution)/shard_map/ppermute | solution.py:150
  107.4 0.2 add_convert_fusion
  107.7 0.1 collective-permute-start.29
  107.8 0.1 fusion.14
  107.9 1.5 %collective-permute-done.29 = bf16[24,6144]{1,0:T(8,128)(2,1)S(1)} collective-permute-done((bf16[24,6144]{1,0:T(8,128)(2,1)S(1)}, bf16[24,6144]{1,0:T(8,128)(2,1)S(1)}, u32[]{:S(2)}, u32[]{:S(2)}) %collective-permute-start.29) | collective-permute-done | bytes 294944 | tf_op jit(solution)/shard_map/ppermute | solution.py:247
  109.4 1.3 %fusion = bf16[64,6144]{1,0:T(8,128)(2,1)} fusion(bf16[1,24,6144]{2,1,0:T(8,128)(2,1)S(1)} %bitcast.22, bf16[1,24,6144]{2,1,0:T(8,128)(2,1)S(1)} %get-tuple-element.147, bf16[2,64]{1,0:T(2,128)(2,1)S(1)} %bitcast.23, s32[2,64]{1,0:T(2,128)S(1)} %subtract_bitcast_fusion, pred[2,64]{1,0:T(4,128)(4,1)S(1)} %get-tuple-element.153), kind=kOutput, calls=%fused_computation.1 | convolution fusion | flops 38052864 | bytes 1377152 | tf_op jit(solution)/shard_map/wcr,wcd->rd/dot_general | solution.py:249
  (39 shorter events, 1.0 us)
Async XLA Ops:
  0.0 1.4 %copy-start = (bf16[64,6144]{1,0:T(8,128)(2,1)S(1)}, bf16[64,6144]{1,0:T(8,128)(2,1)}, u32[]{:S(2)}) copy-start(bf16[64,6144]{1,0:T(8,128)(2,1)} %param.6) | copy-start | bytes 2359300
  1.7 1.7 %collective-permute-start = (bf16[24,6144]{1,0:T(8,128)(2,1)S(1)}, bf16[24,6144]{1,0:T(8,128)(2,1)S(1)}, u32[]{:S(2)}, u32[]{:S(2)}) collective-permute-start(bf16[24,6144]{1,0:T(8,128)(2,1)S(1)} %get-tuple-element.152), channel_id=1, source_target_pairs={{0,8},{8,0},{1,9},{9,1},{2,10},{10,2},{3,11},{11,3},{4,12},{12,4},... | collective-permute-start | bytes 884744 | tf_op jit(solution)/shard_map/ppermute | solution.py:164
  3.6 10.8 %collective-permute-start.2 = (bf16[48,3072]{1,0:T(8,128)(2,1)S(1)}, bf16[48,3072]{1,0:T(8,128)(2,1)S(1)}, u32[]{:S(2)}, u32[]{:S(2)}) collective-permute-start(bf16[48,3072]{1,0:T(8,128)(2,1)S(1)} %get-tuple-element.149.refs_5_), channel_id=1, source_target_pairs={{2,0},{4,2},{6,4},{7,6},{5,7},{3,5},{1,3},{0,1},{10,8},{12,10},{14... | collective-permute-start | bytes 884744 | tf_op jit(solution)/shard_map/ppermute | solution.py:150
  6.5 9.9 %collective-permute-start.1 = (bf16[48,3072]{1,0:T(8,128)(2,1)S(1)}, bf16[48,3072]{1,0:T(8,128)(2,1)S(1)}, u32[]{:S(2)}, u32[]{:S(2)}) collective-permute-start(bf16[48,3072]{1,0:T(8,128)(2,1)S(1)} %get-tuple-element.150.refs_0_), channel_id=1, source_target_pairs={{0,2},{2,4},{4,6},{6,7},{7,5},{5,3},{3,1},{1,0},{8,10},{10,12},{12... | collective-permute-start | bytes 884744 | tf_op jit(solution)/shard_map/ppermute | solution.py:150
  6.6 16.5 %collective-permute-start.3 = (bf16[48,3072]{1,0:T(8,128)(2,1)S(1)}, bf16[48,3072]{1,0:T(8,128)(2,1)S(1)}, u32[]{:S(2)}, u32[]{:S(2)}) collective-permute-start(bf16[48,3072]{1,0:T(8,128)(2,1)S(1)} %get-tuple-element.149.refs_5_), channel_id=1, source_target_pairs={{0,2},{2,4},{4,6},{6,7},{7,5},{5,3},{3,1},{1,0},{8,10},{10,12},{12... | collective-permute-start | bytes 884744 | tf_op jit(solution)/shard_map/ppermute | solution.py:150
  8.6 14.6 %collective-permute-start.4 = (bf16[48,3072]{1,0:T(8,128)(2,1)S(1)}, bf16[48,3072]{1,0:T(8,128)(2,1)S(1)}, u32[]{:S(2)}, u32[]{:S(2)}) collective-permute-start(bf16[48,3072]{1,0:T(8,128)(2,1)S(1)} %get-tuple-element.150.refs_0_), channel_id=1, source_target_pairs={{2,0},{4,2},{6,4},{7,6},{5,7},{3,5},{1,3},{0,1},{10,8},{12,10},{14... | collective-permute-start | bytes 884744 | tf_op jit(solution)/shard_map/ppermute | solution.py:150
  16.4 12.6 %collective-permute-start.5 = (bf16[48,3072]{1,0:T(8,128)(2,1)S(1)}, bf16[48,3072]{1,0:T(8,128)(2,1)S(1)}, u32[]{:S(2)}, u32[]{:S(2)}) collective-permute-start(bf16[48,3072]{1,0:T(8,128)(2,1)S(1)} %collective-permute-done.1.refs_1_), channel_id=1, source_target_pairs={{0,2},{2,4},{4,6},{6,7},{7,5},{5,3},{3,1},{1,0},{8,10},{10,12},{12... | collective-permute-start | bytes 884744 | tf_op jit(solution)/shard_map/ppermute | solution.py:150
  16.5 12.6 %collective-permute-start.6 = (bf16[48,3072]{1,0:T(8,128)(2,1)S(1)}, bf16[48,3072]{1,0:T(8,128)(2,1)S(1)}, u32[]{:S(2)}, u32[]{:S(2)}) collective-permute-start(bf16[48,3072]{1,0:T(8,128)(2,1)S(1)} %collective-permute-done.2.refs_7_), channel_id=1, source_target_pairs={{2,0},{4,2},{6,4},{7,6},{5,7},{3,5},{1,3},{0,1},{10,8},{12,10},{14... | collective-permute-start | bytes 884744 | tf_op jit(solution)/shard_map/ppermute | solution.py:150
  23.2 10.1 %collective-permute-start.8 = (bf16[48,3072]{1,0:T(8,128)(2,1)S(1)}, bf16[48,3072]{1,0:T(8,128)(2,1)S(1)}, u32[]{:S(2)}, u32[]{:S(2)}) collective-permute-start(bf16[48,3072]{1,0:T(8,128)(2,1)S(1)} %collective-permute-done.4.refs_2_), channel_id=1, source_target_pairs={{2,0},{4,2},{6,4},{7,6},{5,7},{3,5},{1,3},{0,1},{10,8},{12,10},{14... | collective-permute-start | bytes 884744 | tf_op jit(solution)/shard_map/ppermute | solution.py:150
  24.8 10.6 %collective-permute-start.7 = (bf16[48,3072]{1,0:T(8,128)(2,1)S(1)}, bf16[48,3072]{1,0:T(8,128)(2,1)S(1)}, u32[]{:S(2)}, u32[]{:S(2)}) collective-permute-start(bf16[48,3072]{1,0:T(8,128)(2,1)S(1)} %collective-permute-done.3.refs_6_), channel_id=1, source_target_pairs={{0,2},{2,4},{4,6},{6,7},{7,5},{5,3},{3,1},{1,0},{8,10},{10,12},{12... | collective-permute-start | bytes 884744 | tf_op jit(solution)/shard_map/ppermute | solution.py:150
  29.0 12.6 %collective-permute-start.9 = (bf16[48,3072]{1,0:T(8,128)(2,1)S(1)}, bf16[48,3072]{1,0:T(8,128)(2,1)S(1)}, u32[]{:S(2)}, u32[]{:S(2)}) collective-permute-start(bf16[48,3072]{1,0:T(8,128)(2,1)S(1)} %collective-permute-done.5.refs_3_), channel_id=1, source_target_pairs={{0,2},{2,4},{4,6},{6,7},{7,5},{5,3},{3,1},{1,0},{8,10},{10,12},{12... | collective-permute-start | bytes 884744 | tf_op jit(solution)/shard_map/ppermute | solution.py:150
  29.1 12.6 %collective-permute-start.10 = (bf16[48,3072]{1,0:T(8,128)(2,1)S(1)}, bf16[48,3072]{1,0:T(8,128)(2,1)S(1)}, u32[]{:S(2)}, u32[]{:S(2)}) collective-permute-start(bf16[48,3072]{1,0:T(8,128)(2,1)S(1)} %collective-permute-done.6.refs_9_), channel_id=1, source_target_pairs={{2,0},{4,2},{6,4},{7,6},{5,7},{3,5},{1,3},{0,1},{10,8},{12,10},{14... | collective-permute-start | bytes 884744 | tf_op jit(solution)/shard_map/ppermute | solution.py:150
  38.6 11.3 %collective-permute-start.11 = (bf16[48,3072]{1,0:T(8,128)(2,1)S(1)}, bf16[48,3072]{1,0:T(8,128)(2,1)S(1)}, u32[]{:S(2)}, u32[]{:S(2)}) collective-permute-start(bf16[48,3072]{1,0:T(8,128)(2,1)S(1)} %collective-permute-done.7.refs_8_), channel_id=1, source_target_pairs={{0,2},{2,4},{4,6},{6,7},{7,5},{5,3},{3,1},{1,0},{8,10},{10,12},{12... | collective-permute-start | bytes 884744 | tf_op jit(solution)/shard_map/ppermute | solution.py:150
  38.7 11.2 %collective-permute-start.12 = (bf16[48,3072]{1,0:T(8,128)(2,1)S(1)}, bf16[48,3072]{1,0:T(8,128)(2,1)S(1)}, u32[]{:S(2)}, u32[]{:S(2)}) collective-permute-start(bf16[48,3072]{1,0:T(8,128)(2,1)S(1)} %collective-permute-done.8.refs_4_), channel_id=1, source_target_pairs={{2,0},{4,2},{6,4},{7,6},{5,7},{3,5},{1,3},{0,1},{10,8},{12,10},{14... | collective-permute-start | bytes 884744 | tf_op jit(solution)/shard_map/ppermute | solution.py:150
  41.7 11.5 %collective-permute-start.13 = (bf16[48,3072]{1,0:T(8,128)(2,1)S(1)}, bf16[48,3072]{1,0:T(8,128)(2,1)S(1)}, u32[]{:S(2)}, u32[]{:S(2)}) collective-permute-start(bf16[48,3072]{1,0:T(8,128)(2,1)S(1)} %collective-permute-done.9.refs_0_), channel_id=1, source_target_pairs={{0,2},{2,4},{4,6},{6,7},{7,5},{5,3},{3,1},{1,0},{8,10},{10,12},{12... | collective-permute-start | bytes 884744 | tf_op jit(solution)/shard_map/ppermute | solution.py:150
  41.8 11.4 %collective-permute-start.14 = (bf16[48,3072]{1,0:T(8,128)(2,1)S(1)}, bf16[48,3072]{1,0:T(8,128)(2,1)S(1)}, u32[]{:S(2)}, u32[]{:S(2)}) collective-permute-start(bf16[48,3072]{1,0:T(8,128)(2,1)S(1)} %collective-permute-done.10.refs_4_), channel_id=1, source_target_pairs={{2,0},{4,2},{6,4},{7,6},{5,7},{3,5},{1,3},{0,1},{10,8},{12,10},{14... | collective-permute-start | bytes 884744 | tf_op jit(solution)/shard_map/ppermute | solution.py:150
  61.7 10.2 %collective-permute-start.15 = (bf16[48,3072]{1,0:T(8,128)(2,1)S(1)}, bf16[48,3072]{1,0:T(8,128)(2,1)S(1)}, u32[]{:S(2)}, u32[]{:S(2)}) collective-permute-start(bf16[48,3072]{1,0:T(8,128)(2,1)S(1)} %get-tuple-element.123), channel_id=1, source_target_pairs={{0,2},{2,4},{4,6},{6,7},{7,5},{5,3},{3,1},{1,0},{8,10},{10,12},{12... | collective-permute-start | bytes 884744 | tf_op jit(solution)/shard_map/ppermute | solution.py:150
  62.2 9.9 %collective-permute-start.16 = (bf16[48,3072]{1,0:T(8,128)(2,1)S(1)}, bf16[48,3072]{1,0:T(8,128)(2,1)S(1)}, u32[]{:S(2)}, u32[]{:S(2)}) collective-permute-start(bf16[48,3072]{1,0:T(8,128)(2,1)S(1)} %get-tuple-element.124), channel_id=1, source_target_pairs={{2,0},{4,2},{6,4},{7,6},{5,7},{3,5},{1,3},{0,1},{10,8},{12,10},{14... | collective-permute-start | bytes 884744 | tf_op jit(solution)/shard_map/ppermute | solution.py:150
  63.8 13.6 %collective-permute-start.23 = (bf16[48,3072]{1,0:T(8,128)(2,1)S(1)}, bf16[48,3072]{1,0:T(8,128)(2,1)S(1)}, u32[]{:S(2)}, u32[]{:S(2)}) collective-permute-start(bf16[48,3072]{1,0:T(8,128)(2,1)S(1)} %get-tuple-element.116), channel_id=1, source_target_pairs={{0,2},{2,4},{4,6},{6,7},{7,5},{5,3},{3,1},{1,0},{8,10},{10,12},{12... | collective-permute-start | bytes 884744 | tf_op jit(solution)/shard_map/ppermute | solution.py:150
  64.2 46.4 %copy-start.1 = (bf16[64,6144]{1,0:T(8,128)(2,1)S(1)}, bf16[64,6144]{1,0:T(8,128)(2,1)}, u32[]{:S(2)}) copy-start(bf16[64,6144]{1,0:T(8,128)(2,1)} %param.6) | copy-start | bytes 2359300
  64.2 43.6 %copy-start.2 = (s32[64,2]{0,1:T(2,128)S(1)}, s32[64,2]{0,1:T(2,128)}, u32[]{:S(2)}) copy-start(s32[64,2]{0,1:T(2,128)} %param.7) | copy-start | bytes 1540
  64.2 43.6 %copy-start.3 = (f32[64,2]{0,1:T(2,128)S(1)}, f32[64,2]{0,1:T(2,128)}, u32[]{:S(2)}) copy-start(f32[64,2]{0,1:T(2,128)} %param.8) | copy-start | bytes 1540
  64.2 14.2 %collective-permute-start.24 = (bf16[48,3072]{1,0:T(8,128)(2,1)S(1)}, bf16[48,3072]{1,0:T(8,128)(2,1)S(1)}, u32[]{:S(2)}, u32[]{:S(2)}) collective-permute-start(bf16[48,3072]{1,0:T(8,128)(2,1)S(1)} %get-tuple-element.117), channel_id=1, source_target_pairs={{2,0},{4,2},{6,4},{7,6},{5,7},{3,5},{1,3},{0,1},{10,8},{12,10},{14... | collective-permute-start | bytes 884744 | tf_op jit(solution)/shard_map/ppermute | solution.py:150
  72.2 12.6 %collective-permute-start.18 = (bf16[48,3072]{1,0:T(8,128)(2,1)S(1)}, bf16[48,3072]{1,0:T(8,128)(2,1)S(1)}, u32[]{:S(2)}, u32[]{:S(2)}) collective-permute-start(bf16[48,3072]{1,0:T(8,128)(2,1)S(1)} %add_convert_fusion.10), channel_id=1, source_target_pairs={{2,0},{4,2},{6,4},{7,6},{5,7},{3,5},{1,3},{0,1},{10,8},{12,10},{14... | collective-permute-start | bytes 884744 | tf_op jit(solution)/shard_map/ppermute | solution.py:150
  73.9 10.9 %collective-permute-start.17 = (bf16[48,3072]{1,0:T(8,128)(2,1)S(1)}, bf16[48,3072]{1,0:T(8,128)(2,1)S(1)}, u32[]{:S(2)}, u32[]{:S(2)}) collective-permute-start(bf16[48,3072]{1,0:T(8,128)(2,1)S(1)} %add_convert_fusion.11), channel_id=1, source_target_pairs={{0,2},{2,4},{4,6},{6,7},{7,5},{5,3},{3,1},{1,0},{8,10},{10,12},{12... | collective-permute-start | bytes 884744 | tf_op jit(solution)/shard_map/ppermute | solution.py:150
  78.5 12.6 %collective-permute-start.26 = (bf16[48,3072]{1,0:T(8,128)(2,1)S(1)}, bf16[48,3072]{1,0:T(8,128)(2,1)S(1)}, u32[]{:S(2)}, u32[]{:S(2)}) collective-permute-start(bf16[48,3072]{1,0:T(8,128)(2,1)S(1)} %add_convert_fusion.4), channel_id=1, source_target_pairs={{2,0},{4,2},{6,4},{7,6},{5,7},{3,5},{1,3},{0,1},{10,8},{12,10},{14... | collective-permute-start | bytes 884744 | tf_op jit(solution)/shard_map/ppermute | solution.py:150
  80.2 10.9 %collective-permute-start.25 = (bf16[48,3072]{1,0:T(8,128)(2,1)S(1)}, bf16[48,3072]{1,0:T(8,128)(2,1)S(1)}, u32[]{:S(2)}, u32[]{:S(2)}) collective-permute-start(bf16[48,3072]{1,0:T(8,128)(2,1)S(1)} %add_convert_fusion.5), channel_id=1, source_target_pairs={{0,2},{2,4},{4,6},{6,7},{7,5},{5,3},{3,1},{1,0},{8,10},{10,12},{12... | collective-permute-start | bytes 884744 | tf_op jit(solution)/shard_map/ppermute | solution.py:150
  84.9 12.6 %collective-permute-start.20 = (bf16[48,3072]{1,0:T(8,128)(2,1)S(1)}, bf16[48,3072]{1,0:T(8,128)(2,1)S(1)}, u32[]{:S(2)}, u32[]{:S(2)}) collective-permute-start(bf16[48,3072]{1,0:T(8,128)(2,1)S(1)} %add_convert_fusion.8), channel_id=1, source_target_pairs={{2,0},{4,2},{6,4},{7,6},{5,7},{3,5},{1,3},{0,1},{10,8},{12,10},{14... | collective-permute-start | bytes 884744 | tf_op jit(solution)/shard_map/ppermute | solution.py:150
  86.6 10.9 %collective-permute-start.19 = (bf16[48,3072]{1,0:T(8,128)(2,1)S(1)}, bf16[48,3072]{1,0:T(8,128)(2,1)S(1)}, u32[]{:S(2)}, u32[]{:S(2)}) collective-permute-start(bf16[48,3072]{1,0:T(8,128)(2,1)S(1)} %add_convert_fusion.9), channel_id=1, source_target_pairs={{0,2},{2,4},{4,6},{6,7},{7,5},{5,3},{3,1},{1,0},{8,10},{10,12},{12... | collective-permute-start | bytes 884744 | tf_op jit(solution)/shard_map/ppermute | solution.py:150
  91.2 12.6 %collective-permute-start.28 = (bf16[48,3072]{1,0:T(8,128)(2,1)S(1)}, bf16[48,3072]{1,0:T(8,128)(2,1)S(1)}, u32[]{:S(2)}, u32[]{:S(2)}) collective-permute-start(bf16[48,3072]{1,0:T(8,128)(2,1)S(1)} %add_convert_fusion.2), channel_id=1, source_target_pairs={{2,0},{4,2},{6,4},{7,6},{5,7},{3,5},{1,3},{0,1},{10,8},{12,10},{14... | collective-permute-start | bytes 884744 | tf_op jit(solution)/shard_map/ppermute | solution.py:150
  92.9 10.9 %collective-permute-start.27 = (bf16[48,3072]{1,0:T(8,128)(2,1)S(1)}, bf16[48,3072]{1,0:T(8,128)(2,1)S(1)}, u32[]{:S(2)}, u32[]{:S(2)}) collective-permute-start(bf16[48,3072]{1,0:T(8,128)(2,1)S(1)} %add_convert_fusion.3), channel_id=1, source_target_pairs={{0,2},{2,4},{4,6},{6,7},{7,5},{5,3},{3,1},{1,0},{8,10},{10,12},{12... | collective-permute-start | bytes 884744 | tf_op jit(solution)/shard_map/ppermute | solution.py:150
  97.5 9.9 %collective-permute-start.22 = (bf16[48,3072]{1,0:T(8,128)(2,1)S(1)}, bf16[48,3072]{1,0:T(8,128)(2,1)S(1)}, u32[]{:S(2)}, u32[]{:S(2)}) collective-permute-start(bf16[48,3072]{1,0:T(8,128)(2,1)S(1)} %add_convert_fusion.6), channel_id=1, source_target_pairs={{2,0},{4,2},{6,4},{7,6},{5,7},{3,5},{1,3},{0,1},{10,8},{12,10},{14... | collective-permute-start | bytes 884744 | tf_op jit(solution)/shard_map/ppermute | solution.py:150
  99.2 8.2 %collective-permute-start.21 = (bf16[48,3072]{1,0:T(8,128)(2,1)S(1)}, bf16[48,3072]{1,0:T(8,128)(2,1)S(1)}, u32[]{:S(2)}, u32[]{:S(2)}) collective-permute-start(bf16[48,3072]{1,0:T(8,128)(2,1)S(1)} %add_convert_fusion.7), channel_id=1, source_target_pairs={{0,2},{2,4},{4,6},{6,7},{7,5},{5,3},{3,1},{1,0},{8,10},{10,12},{12... | collective-permute-start | bytes 884744 | tf_op jit(solution)/shard_map/ppermute | solution.py:150
  107.7 1.6 %collective-permute-start.29 = (bf16[24,6144]{1,0:T(8,128)(2,1)S(1)}, bf16[24,6144]{1,0:T(8,128)(2,1)S(1)}, u32[]{:S(2)}, u32[]{:S(2)}) collective-permute-start(bf16[24,6144]{1,0:T(8,128)(2,1)S(1)} %get-tuple-element.148), channel_id=1, source_target_pairs={{0,8},{8,0},{1,9},{9,1},{2,10},{10,2},{3,11},{11,3},{4,12},{12,4},... | collective-permute-start | bytes 884744 | tf_op jit(solution)/shard_map/ppermute | solution.py:247

commit v15 on v14

--- a/solution.py
+++ b/solution.py
@@ -149,6 +149,10 @@
     def step(to_right, to_left):
         pair = (lax.ppermute(to_right, "tensor", right), lax.ppermute(to_left, "tensor", left))
         return lax.optimization_barrier(pair)
+
+    def across(rows, perm):
+        pairs = [(e * n_tensor + source, (1 - e) * n_tensor + target) for e in range(2) for source, target in perm]
+        return lax.ppermute(rows, ("expert", "tensor"), pairs)
 
     def tied(*values):
         return lax.optimization_barrier(values)
@@ -228,23 +232,30 @@
         index = 2 * distance - 1 + side if distance else 0
         return near_parts[count * chunk + index].astype(jnp.float32)
 
-    def sent(stream, distance, got):
+    def sends(stream, distance, got):
         to_right = part_of(stream, distance, 1) + got[0].astype(jnp.float32)
         to_left = part_of(1 - stream, distance, 0) + got[1].astype(jnp.float32)
-        return step(to_right.astype(jnp.bfloat16), to_left.astype(jnp.bfloat16))
+        return to_right.astype(jnp.bfloat16), to_left.astype(jnp.bfloat16)
 
     a = step(rest_parts[2], rest_parts[5])
     b = step(rest_parts[4], rest_parts[0])
-    a = sent(0, half - 1, a)
+    a = step(*sends(0, half - 1, a))
     for distance in range(half - 2, 0, -1):
-        b = sent(1, distance, b)
-        a = sent(0, distance, a)
-    totals = [
-        part_of(0, 0, 0) + a[0].astype(jnp.float32) + b[1].astype(jnp.float32),
-        part_of(1, 0, 0) + b[0].astype(jnp.float32) + a[1].astype(jnp.float32),
+        b = step(*sends(1, distance, b))
+        to_right, to_left = sends(0, distance, a)
+        if distance > 1:
+            a = step(to_right, to_left)
+    kept = step(to_right[:CAP], to_left[:CAP])
+    crossed = lax.optimization_barrier((across(to_right[CAP:], right), across(to_left[CAP:], left)))
+    partial = jnp.concatenate(
+        [part_of(0, 0, 0) + b[1].astype(jnp.float32), part_of(1, 0, 0) + b[0].astype(jnp.float32)], axis=1
+    )
+    exchanged = lax.ppermute(partial[CAP:].astype(jnp.bfloat16), "expert", swap)
+    returned = [
+        (base.astype(jnp.float32) + jnp.concatenate(last, axis=1).astype(jnp.float32)).astype(jnp.bfloat16)
+        for base, last in ((partial[:CAP], kept), (exchanged, crossed))
     ]
-    total = jnp.concatenate(totals, axis=1).astype(jnp.bfloat16)
-    returned = jnp.stack([total[:CAP], lax.ppermute(total[CAP:], "expert", swap)])
+    returned = jnp.stack(returned)
     combine = dispatch_map.astype(jnp.float32) * jnp.transpose(weight)[:, None, :]
     mixed = jnp.einsum("wcr,wcd->rd", combine, returned.astype(jnp.float32))
     return mixed.astype(jnp.bfloat16)

time: 111 us -> 111 us (level)
  waiting for transfers between devices: 42.3 us -> 39.7 us
  starting transfers between devices: 30.7 us -> 33 us
    ppermute x14, waiting for transfers between devices: 24.4 us -> 20.2 us  [step(): lax.ppermute(to_left, 'tensor', left)]
    ppermute x1 -> x3, starting transfers between devices: 0.07 us -> 2.44 us  [the longest x1 2.43 us: per_device(): exchanged = lax.ppermute(partial[CAP:].astype(jnp.bfloat16), 'expert', swap)]
    ppermute x1 -> x3, waiting for transfers between devices: 1.47 us -> 3.28 us  [the longest x2 3.28 us: across(): return lax.ppermute(rows, ('expert', 'tensor'), pairs)]
  transfers between devices with their start and end apart: 30 -> 32, of which waited for: 17 -> 18; matrix products, arithmetic and copies ran while one was open for 1% -> 1% of each run, Pallas kernels for 22% -> 22%
where the time goes in v15:
time: 111 us
  waiting for transfers between devices  39.7 us (36%)
  Pallas kernels  33.3 us (30%)
  starting transfers between devices  33 us (30%)
  other arithmetic  2.21 us (2%)
  matrix products  1.58 us (1%)
    pallas_call x7, Pallas kernels, call(): pl.pallas_call(kernel, in_specs=[pl.BlockSpec(memory_space=memory) for _,...  33.3 us
    ppermute x14, starting transfers between devices, step(): lax.ppermute(to_left, 'tensor', left)  23.7 us
    ppermute x14, waiting for transfers between devices, step(): lax.ppermute(to_left, 'tensor', left)  20.2 us
    ppermute x14, waiting for transfers between devices, step(): lax.ppermute(to_right, 'tensor', right)  15.1 us
    ppermute x14, starting transfers between devices, step(): lax.ppermute(to_right, 'tensor', right)  6.4 us
    ppermute x2, waiting for transfers between devices, across(): return lax.ppermute(rows, ('expert', 'tensor'), pairs)  3.28 us
    ppermute x1, starting transfers between devices, per_device(): exchanged = lax.ppermute(partial[CAP:].astype(jnp.bfloat16), 'expert', swap)  2.43 us
  transfers between devices with their start and end apart: 32, of which 18 were waited for; matrix products, arithmetic and copies ran while one was open for 1% of the time, Pallas kernels for 22%

profile of v15, /device:TPU:0, one launch (start us, length us, event | category | flops | bytes accessed | tf_op | source)
XLA Modules:
  0.0 110.6 jit_solution(6014166524837689162)
XLA Ops:
  0.0 0.1 eq.64
  0.2 0.8 compare_reduce_fusion
  1.0 0.1 copy.17
  1.1 0.1 reduce_window_sum.11
  1.3 0.1 fusion.13
  1.4 0.3 convolution_convert_fusion
  1.7 0.5 collective-permute-start
  2.3 1.2 %collective-permute-done = bf16[24,6144]{1,0:T(8,128)(2,1)S(1)} collective-permute-done((bf16[24,6144]{1,0:T(8,128)(2,1)S(1)}, bf16[24,6144]{1,0:T(8,128)(2,1)S(1)}, u32[]{:S(2)}, u32[]{:S(2)}) %collective-permute-start) | collective-permute-done | bytes 294944 | tf_op jit(solution)/shard_map/ppermute | solution.py:168
  3.6 2.9 %collective-permute-start.2 = (bf16[48,3072]{1,0:T(8,128)(2,1)S(1)}, bf16[48,3072]{1,0:T(8,128)(2,1)S(1)}, u32[]{:S(2)}, u32[]{:S(2)}) collective-permute-start(bf16[48,3072]{1,0:T(8,128)(2,1)S(1)} %get-tuple-element.151.refs_5_), channel_id=1, source_target_pairs={{2,0},{4,2},{6,4},{7,6},{5,7},{3,5},{1,3},{0,1},{10,8},{12,10},{14... | collective-permute-start | bytes 884744 | tf_op jit(solution)/shard_map/ppermute | solution.py:150
  6.5 0.1 collective-permute-start.1
  6.6 2.0 %collective-permute-start.3 = (bf16[48,3072]{1,0:T(8,128)(2,1)S(1)}, bf16[48,3072]{1,0:T(8,128)(2,1)S(1)}, u32[]{:S(2)}, u32[]{:S(2)}) collective-permute-start(bf16[48,3072]{1,0:T(8,128)(2,1)S(1)} %get-tuple-element.151.refs_5_), channel_id=1, source_target_pairs={{0,2},{2,4},{4,6},{6,7},{7,5},{5,3},{3,1},{1,0},{8,10},{10,12},{12... | collective-permute-start | bytes 884744 | tf_op jit(solution)/shard_map/ppermute | solution.py:150
  8.6 4.7 %fetched.3.refs_10_.refs_6_ = bf16[1,6144,1024]{2,1,0:T(8,128)(2,1)S(1)} custom-call(bf16[1,6144,1024]{2,1,0:T(8,128)(2,1)} %source), custom_call_target="tpu_custom_call" | custom-call | flops 1024 | bytes 1024 | tf_op jit(solution)/shard_map/fetched/pallas_call | solution.py:29
  13.4 1.0 collective-permute-done.2.refs_7_
  14.3 2.0 %collective-permute-done.1.refs_1_ = bf16[48,3072]{1,0:T(8,128)(2,1)S(1)} collective-permute-done((bf16[48,3072]{1,0:T(8,128)(2,1)S(1)}, bf16[48,3072]{1,0:T(8,128)(2,1)S(1)}, u32[]{:S(2)}, u32[]{:S(2)}) %collective-permute-start.1) | collective-permute-done | bytes 294944 | tf_op jit(solution)/shard_map/ppermute | solution.py:150
  16.4 0.1 collective-permute-start.5
  16.5 1.9 %collective-permute-start.6 = (bf16[48,3072]{1,0:T(8,128)(2,1)S(1)}, bf16[48,3072]{1,0:T(8,128)(2,1)S(1)}, u32[]{:S(2)}, u32[]{:S(2)}) collective-permute-start(bf16[48,3072]{1,0:T(8,128)(2,1)S(1)} %collective-permute-done.2.refs_7_), channel_id=1, source_target_pairs={{2,0},{4,2},{6,4},{7,6},{5,7},{3,5},{1,3},{0,1},{10,8},{12,10},{14... | collective-permute-start | bytes 884744 | tf_op jit(solution)/shard_map/ppermute | solution.py:150
  18.4 4.7 %fetched.4.refs_10_.refs_7_ = bf16[1,6144,1024]{2,1,0:T(8,128)(2,1)S(1)} custom-call(bf16[1,6144,1024]{2,1,0:T(8,128)(2,1)} %source.1), custom_call_target="tpu_custom_call" | custom-call | flops 1024 | bytes 1024 | tf_op jit(solution)/shard_map/fetched/pallas_call | solution.py:29
  23.2 1.6 %collective-permute-start.8 = (bf16[48,3072]{1,0:T(8,128)(2,1)S(1)}, bf16[48,3072]{1,0:T(8,128)(2,1)S(1)}, u32[]{:S(2)}, u32[]{:S(2)}) collective-permute-start(bf16[48,3072]{1,0:T(8,128)(2,1)S(1)} %collective-permute-done.4.refs_2_), channel_id=1, source_target_pairs={{2,0},{4,2},{6,4},{7,6},{5,7},{3,5},{1,3},{0,1},{10,8},{12,10},{14... | collective-permute-start | bytes 884744 | tf_op jit(solution)/shard_map/ppermute | solution.py:150
  24.8 0.4 collective-permute-start.7
  25.2 3.8 %collective-permute-done.5.refs_3_ = bf16[48,3072]{1,0:T(8,128)(2,1)S(1)} collective-permute-done((bf16[48,3072]{1,0:T(8,128)(2,1)S(1)}, bf16[48,3072]{1,0:T(8,128)(2,1)S(1)}, u32[]{:S(2)}, u32[]{:S(2)}) %collective-permute-start.5) | collective-permute-done | bytes 294944 | tf_op jit(solution)/shard_map/ppermute | solution.py:150
  29.0 0.1 collective-permute-start.9
  29.1 1.9 %collective-permute-start.10 = (bf16[48,3072]{1,0:T(8,128)(2,1)S(1)}, bf16[48,3072]{1,0:T(8,128)(2,1)S(1)}, u32[]{:S(2)}, u32[]{:S(2)}) collective-permute-start(bf16[48,3072]{1,0:T(8,128)(2,1)S(1)} %collective-permute-done.6.refs_9_), channel_id=1, source_target_pairs={{2,0},{4,2},{6,4},{7,6},{5,7},{3,5},{1,3},{0,1},{10,8},{12,10},{14... | collective-permute-start | bytes 884744 | tf_op jit(solution)/shard_map/ppermute | solution.py:150
  31.1 2.2 %collective-permute-done.8.refs_4_ = bf16[48,3072]{1,0:T(8,128)(2,1)S(1)} collective-permute-done((bf16[48,3072]{1,0:T(8,128)(2,1)S(1)}, bf16[48,3072]{1,0:T(8,128)(2,1)S(1)}, u32[]{:S(2)}, u32[]{:S(2)}) %collective-permute-start.8) | collective-permute-done | bytes 294944 | tf_op jit(solution)/shard_map/ppermute | solution.py:150
  33.3 2.0 %collective-permute-done.7.refs_8_ = bf16[48,3072]{1,0:T(8,128)(2,1)S(1)} collective-permute-done((bf16[48,3072]{1,0:T(8,128)(2,1)S(1)}, bf16[48,3072]{1,0:T(8,128)(2,1)S(1)}, u32[]{:S(2)}, u32[]{:S(2)}) %collective-permute-start.7) | collective-permute-done | bytes 294944 | tf_op jit(solution)/shard_map/ppermute | solution.py:150
  35.4 3.2 %near_gate.1.refs_11_ = f32[240,1024]{1,0:T(8,128)S(1)} custom-call(bf16[48,3072]{1,0:T(8,128)(2,1)S(1)} %get-tuple-element.152.refs_0_, bf16[48,3072]{1,0:T(8,128)(2,1)S(1)} %collective-permute-done.1.refs_1_, bf16[48,3072]{1,0:T(8,128)(2,1)S(1)} %collective-permute-done.4.refs_2_, bf16[48,3072]{1,0:T(8,128)(2,1)S(1)} %collective-permute-done.5.refs_3_, ...), custom_call_target="tpu_custom_call" | custom-call | flops 1024 | bytes 1024 | tf_op jit(solution)/shard_map/near_gate/pallas_call | solution.py:29
  38.6 0.1 collective-permute-start.11
  38.7 1.9 %collective-permute-start.12 = (bf16[48,3072]{1,0:T(8,128)(2,1)S(1)}, bf16[48,3072]{1,0:T(8,128)(2,1)S(1)}, u32[]{:S(2)}, u32[]{:S(2)}) collective-permute-start(bf16[48,3072]{1,0:T(8,128)(2,1)S(1)} %collective-permute-done.8.refs_4_), channel_id=1, source_target_pairs={{2,0},{4,2},{6,4},{7,6},{5,7},{3,5},{1,3},{0,1},{10,8},{12,10},{14... | collective-permute-start | bytes 884744 | tf_op jit(solution)/shard_map/ppermute | solution.py:150
  40.6 1.0 collective-permute-done.9.refs_0_
  41.7 0.1 collective-permute-start.13
  41.8 1.9 %collective-permute-start.14 = (bf16[48,3072]{1,0:T(8,128)(2,1)S(1)}, bf16[48,3072]{1,0:T(8,128)(2,1)S(1)}, u32[]{:S(2)}, u32[]{:S(2)}) collective-permute-start(bf16[48,3072]{1,0:T(8,128)(2,1)S(1)} %collective-permute-done.10.refs_4_), channel_id=1, source_target_pairs={{2,0},{4,2},{6,4},{7,6},{5,7},{3,5},{1,3},{0,1},{10,8},{12,10},{14... | collective-permute-start | bytes 884744 | tf_op jit(solution)/shard_map/ppermute | solution.py:150
  43.7 3.2 %near_up.1.hidden = bf16[240,1024]{1,0:T(8,128)(2,1)S(1)} custom-call(bf16[48,3072]{1,0:T(8,128)(2,1)S(1)} %get-tuple-element.152.refs_0_, bf16[48,3072]{1,0:T(8,128)(2,1)S(1)} %collective-permute-done.1.refs_1_, bf16[48,3072]{1,0:T(8,128)(2,1)S(1)} %collective-permute-done.4.refs_2_, bf16[48,3072]{1,0:T(8,128)(2,1)S(1)} %collective-permute-done.5.refs_3_, ...), custom_call_target="tpu_custom_call" | custom-call | flops 1024 | bytes 1024 | tf_op jit(solution)/shard_map/near_up/pallas_call | solution.py:29
  46.9 2.9 %fetched.5.refs_8_.down_0 = bf16[1,1024,3072]{2,1,0:T(8,128)(2,1)S(1)} custom-call(bf16[1,1024,6144]{2,1,0:T(8,128)(2,1)} %w_down), custom_call_target="tpu_custom_call" | custom-call | flops 1024 | bytes 1024 | tf_op jit(solution)/shard_map/fetched/pallas_call | solution.py:29
  49.9 3.3 %collective-permute-done.13.refs_2_ = bf16[48,3072]{1,0:T(8,128)(2,1)S(1)} collective-permute-done((bf16[48,3072]{1,0:T(8,128)(2,1)S(1)}, bf16[48,3072]{1,0:T(8,128)(2,1)S(1)}, u32[]{:S(2)}, u32[]{:S(2)}) %collective-permute-start.13) | collective-permute-done | bytes 294944 | tf_op jit(solution)/shard_map/ppermute | solution.py:150
  53.2 8.5 %rest.1 = (bf16[48,3072]{1,0:T(8,128)(2,1)S(1)}, bf16[48,3072]{1,0:T(8,128)(2,1)S(1)}, bf16[48,3072]{1,0:T(8,128)(2,1)S(1)}, bf16[48,3072]{1,0:T(8,128)(2,1)S(1)...) custom-call(bf16[48,3072]{1,0:T(8,128)(2,1)S(1)} %collective-permute-done.9.refs_0_, ...), custom_call_target="tpu_custom_call" | custom-call | flops 1024 | bytes 1024 | tf_op jit(solution)/shard_map/rest/pallas_call | solution.py:29
  61.7 0.5 collective-permute-start.21
  62.2 1.6 %collective-permute-start.22 = (bf16[48,3072]{1,0:T(8,128)(2,1)S(1)}, bf16[48,3072]{1,0:T(8,128)(2,1)S(1)}, u32[]{:S(2)}, u32[]{:S(2)}) collective-permute-start(bf16[48,3072]{1,0:T(8,128)(2,1)S(1)} %get-tuple-element.137), channel_id=1, source_target_pairs={{2,0},{4,2},{6,4},{7,6},{5,7},{3,5},{1,3},{0,1},{10,8},{12,10},{14... | collective-permute-start | bytes 884744 | tf_op jit(solution)/shard_map/ppermute | solution.py:150
  63.8 0.1 fusion.18
  63.8 0.5 collective-permute-start.15
  64.3 1.6 %collective-permute-start.16 = (bf16[48,3072]{1,0:T(8,128)(2,1)S(1)}, bf16[48,3072]{1,0:T(8,128)(2,1)S(1)}, u32[]{:S(2)}, u32[]{:S(2)}) collective-permute-start(bf16[48,3072]{1,0:T(8,128)(2,1)S(1)} %get-tuple-element.119), channel_id=1, source_target_pairs={{2,0},{4,2},{6,4},{7,6},{5,7},{3,5},{1,3},{0,1},{10,8},{12,10},{14... | collective-permute-start | bytes 884744 | tf_op jit(solution)/shard_map/ppermute | solution.py:150
  65.9 6.1 %near_down.1 = (bf16[48,3072]{1,0:T(8,128)(2,1)S(1)}, bf16[48,3072]{1,0:T(8,128)(2,1)S(1)}, bf16[48,3072]{1,0:T(8,128)(2,1)S(1)}, bf16[48,3072]{1,0:T(8,128)(2,1...) custom-call(bf16[240,1024]{1,0:T(8,128)(2,1)S(1)} %near_up.1.hidden,, ...), custom_call_target="tpu_custom_call" | custom-call | flops 1024 | bytes 1024 | tf_op jit(solution)/shard_map/near_down/pallas_call | solution.py:29
  72.0 0.2 collective-permute-done.22
  72.2 1.6 %collective-permute-start.24 = (bf16[48,3072]{1,0:T(8,128)(2,1)S(1)}, bf16[48,3072]{1,0:T(8,128)(2,1)S(1)}, u32[]{:S(2)}, u32[]{:S(2)}) collective-permute-start(bf16[48,3072]{1,0:T(8,128)(2,1)S(1)} %add_convert_fusion.5), channel_id=1, source_target_pairs={{2,0},{4,2},{6,4},{7,6},{5,7},{3,5},{1,3},{0,1},{10,8},{12,10},{14... | collective-permute-start | bytes 884744 | tf_op jit(solution)/shard_map/ppermute | solution.py:150
  73.9 0.5 collective-permute-start.23
  74.4 2.9 %collective-permute-done.15 = bf16[48,3072]{1,0:T(8,128)(2,1)S(1)} collective-permute-done((bf16[48,3072]{1,0:T(8,128)(2,1)S(1)}, bf16[48,3072]{1,0:T(8,128)(2,1)S(1)}, u32[]{:S(2)}, u32[]{:S(2)}) %collective-permute-start.15) | collective-permute-done | bytes 294944 | tf_op jit(solution)/shard_map/ppermute | solution.py:150
  77.3 1.2 %collective-permute-done.16 = bf16[48,3072]{1,0:T(8,128)(2,1)S(1)} collective-permute-done((bf16[48,3072]{1,0:T(8,128)(2,1)S(1)}, bf16[48,3072]{1,0:T(8,128)(2,1)S(1)}, u32[]{:S(2)}, u32[]{:S(2)}) %collective-permute-start.16) | collective-permute-done | bytes 294944 | tf_op jit(solution)/shard_map/ppermute | solution.py:150
  78.5 1.6 %collective-permute-start.18 = (bf16[48,3072]{1,0:T(8,128)(2,1)S(1)}, bf16[48,3072]{1,0:T(8,128)(2,1)S(1)}, u32[]{:S(2)}, u32[]{:S(2)}) collective-permute-start(bf16[48,3072]{1,0:T(8,128)(2,1)S(1)} %add_convert_fusion.9), channel_id=1, source_target_pairs={{2,0},{4,2},{6,4},{7,6},{5,7},{3,5},{1,3},{0,1},{10,8},{12,10},{14... | collective-permute-start | bytes 884744 | tf_op jit(solution)/shard_map/ppermute | solution.py:150
  80.2 0.5 collective-permute-start.17
  80.7 4.0 %collective-permute-done.24 = bf16[48,3072]{1,0:T(8,128)(2,1)S(1)} collective-permute-done((bf16[48,3072]{1,0:T(8,128)(2,1)S(1)}, bf16[48,3072]{1,0:T(8,128)(2,1)S(1)}, u32[]{:S(2)}, u32[]{:S(2)}) %collective-permute-start.24) | collective-permute-done | bytes 294944 | tf_op jit(solution)/shard_map/ppermute | solution.py:150
  84.9 1.6 %collective-permute-start.26 = (bf16[48,3072]{1,0:T(8,128)(2,1)S(1)}, bf16[48,3072]{1,0:T(8,128)(2,1)S(1)}, u32[]{:S(2)}, u32[]{:S(2)}) collective-permute-start(bf16[48,3072]{1,0:T(8,128)(2,1)S(1)} %add_convert_fusion.3), channel_id=1, source_target_pairs={{2,0},{4,2},{6,4},{7,6},{5,7},{3,5},{1,3},{0,1},{10,8},{12,10},{14... | collective-permute-start | bytes 884744 | tf_op jit(solution)/shard_map/ppermute | solution.py:150
  86.6 0.5 collective-permute-start.25
  87.1 4.0 %collective-permute-done.18 = bf16[48,3072]{1,0:T(8,128)(2,1)S(1)} collective-permute-done((bf16[48,3072]{1,0:T(8,128)(2,1)S(1)}, bf16[48,3072]{1,0:T(8,128)(2,1)S(1)}, u32[]{:S(2)}, u32[]{:S(2)}) %collective-permute-start.18) | collective-permute-done | bytes 294944 | tf_op jit(solution)/shard_map/ppermute | solution.py:150
  91.2 1.6 %collective-permute-start.20 = (bf16[48,3072]{1,0:T(8,128)(2,1)S(1)}, bf16[48,3072]{1,0:T(8,128)(2,1)S(1)}, u32[]{:S(2)}, u32[]{:S(2)}) collective-permute-start(bf16[48,3072]{1,0:T(8,128)(2,1)S(1)} %add_convert_fusion.7), channel_id=1, source_target_pairs={{2,0},{4,2},{6,4},{7,6},{5,7},{3,5},{1,3},{0,1},{10,8},{12,10},{14... | collective-permute-start | bytes 884744 | tf_op jit(solution)/shard_map/ppermute | solution.py:150
  92.9 0.5 collective-permute-start.19
  93.4 4.0 %collective-permute-done.26 = bf16[48,3072]{1,0:T(8,128)(2,1)S(1)} collective-permute-done((bf16[48,3072]{1,0:T(8,128)(2,1)S(1)}, bf16[48,3072]{1,0:T(8,128)(2,1)S(1)}, u32[]{:S(2)}, u32[]{:S(2)}) %collective-permute-start.26) | collective-permute-done | bytes 294944 | tf_op jit(solution)/shard_map/ppermute | solution.py:150
  97.4 0.1 add_convert_fusion.1
  97.6 1.6 %collective-permute-start.28 = (bf16[24,3072]{1,0:T(8,128)(2,1)S(1)}, bf16[24,3072]{1,0:T(8,128)(2,1)S(1)}, u32[]{:S(2)}, u32[]{:S(2)}) collective-permute-start(bf16[24,3072]{1,0:T(8,128)(2,1)S(1)} %get-tuple-element.155), channel_id=1, source_target_pairs={{2,0},{4,2},{6,4},{7,6},{5,7},{3,5},{1,3},{0,1},{10,8},{12,10},{14... | collective-permute-start | bytes 442376 | tf_op jit(solution)/shard_map/ppermute | solution.py:150
  99.3 0.5 collective-permute-start.27
  99.8 3.3 %collective-permute-done.20 = bf16[48,3072]{1,0:T(8,128)(2,1)S(1)} collective-permute-done((bf16[48,3072]{1,0:T(8,128)(2,1)S(1)}, bf16[48,3072]{1,0:T(8,128)(2,1)S(1)}, u32[]{:S(2)}, u32[]{:S(2)}) %collective-permute-start.20) | collective-permute-done | bytes 294944 | tf_op jit(solution)/shard_map/ppermute | solution.py:150
  103.1 0.1 convert_add_fusion
  103.3 2.4 %collective-permute-start.29 = (bf16[24,6144]{1,0:T(8,128)(2,1)S(1)}, bf16[24,6144]{1,0:T(8,128)(2,1)S(1)}, u32[]{:S(2)}, u32[]{:S(2)}) collective-permute-start(bf16[24,6144]{1,0:T(8,128)(2,1)S(1)} %fusion.4), channel_id=1, source_target_pairs={{0,8},{8,0},{1,9},{9,1},{2,10},{10,2},{3,11},{11,3},{4,12},{12,4},... | collective-permute-start | bytes 884744 | tf_op jit(solution)/shard_map/ppermute | solution.py:253
  105.7 0.1 collective-permute-done.28
  105.9 0.3 collective-permute-done.31
  106.2 2.9 %collective-permute-done.30 = bf16[24,3072]{1,0:T(8,128)(2,1)S(1)} collective-permute-done((bf16[24,3072]{1,0:T(8,128)(2,1)S(1)}, bf16[24,3072]{1,0:T(8,128)(2,1)S(1)}, u32[]{:S(2)}, u32[]{:S(2)}) %collective-permute-start.30) | collective-permute-done | bytes 147488 | tf_op jit(solution)/shard_map/ppermute | solution.py:155
  109.3 1.3 %fusion = bf16[64,6144]{1,0:T(8,128)(2,1)} fusion(bf16[1,24,6144]{2,1,0:T(8,128)(2,1)S(1)} %fusion.8, bf16[1,24,6144]{2,1,0:T(8,128)(2,1)S(1)} %fusion.9, bf16[2,64]{1,0:T(2,128)(2,1)S(1)} %bitcast.23, s32[2,64]{1,0:T(2,128)S(1)} %subtract_bitcast_fusion, pred[2,64]{1,0:T(4,128)(4,1)S(1)} %get-tuple-element.159), kind=kOutput, calls=%fused_computation.1 | convolution fusion | flops 38052864 | bytes 1377152 | tf_op jit(solution)/shard_map/wcr,wcd->rd/dot_general | solution.py:260
  (46 shorter events, 1.2 us)
Async XLA Ops:
  0.0 1.4 %copy-start = (bf16[64,6144]{1,0:T(8,128)(2,1)S(1)}, bf16[64,6144]{1,0:T(8,128)(2,1)}, u32[]{:S(2)}) copy-start(bf16[64,6144]{1,0:T(8,128)(2,1)} %param.6) | copy-start | bytes 2359300
  1.7 1.7 %collective-permute-start = (bf16[24,6144]{1,0:T(8,128)(2,1)S(1)}, bf16[24,6144]{1,0:T(8,128)(2,1)S(1)}, u32[]{:S(2)}, u32[]{:S(2)}) collective-permute-start(bf16[24,6144]{1,0:T(8,128)(2,1)S(1)} %get-tuple-element.154), channel_id=1, source_target_pairs={{0,8},{8,0},{1,9},{9,1},{2,10},{10,2},{3,11},{11,3},{4,12},{12,4},... | collective-permute-start | bytes 884744 | tf_op jit(solution)/shard_map/ppermute | solution.py:168
  3.6 10.8 %collective-permute-start.2 = (bf16[48,3072]{1,0:T(8,128)(2,1)S(1)}, bf16[48,3072]{1,0:T(8,128)(2,1)S(1)}, u32[]{:S(2)}, u32[]{:S(2)}) collective-permute-start(bf16[48,3072]{1,0:T(8,128)(2,1)S(1)} %get-tuple-element.151.refs_5_), channel_id=1, source_target_pairs={{2,0},{4,2},{6,4},{7,6},{5,7},{3,5},{1,3},{0,1},{10,8},{12,10},{14... | collective-permute-start | bytes 884744 | tf_op jit(solution)/shard_map/ppermute | solution.py:150
  6.5 9.9 %collective-permute-start.1 = (bf16[48,3072]{1,0:T(8,128)(2,1)S(1)}, bf16[48,3072]{1,0:T(8,128)(2,1)S(1)}, u32[]{:S(2)}, u32[]{:S(2)}) collective-permute-start(bf16[48,3072]{1,0:T(8,128)(2,1)S(1)} %get-tuple-element.152.refs_0_), channel_id=1, source_target_pairs={{0,2},{2,4},{4,6},{6,7},{7,5},{5,3},{3,1},{1,0},{8,10},{10,12},{12... | collective-permute-start | bytes 884744 | tf_op jit(solution)/shard_map/ppermute | solution.py:150
  6.6 16.5 %collective-permute-start.3 = (bf16[48,3072]{1,0:T(8,128)(2,1)S(1)}, bf16[48,3072]{1,0:T(8,128)(2,1)S(1)}, u32[]{:S(2)}, u32[]{:S(2)}) collective-permute-start(bf16[48,3072]{1,0:T(8,128)(2,1)S(1)} %get-tuple-element.151.refs_5_), channel_id=1, source_target_pairs={{0,2},{2,4},{4,6},{6,7},{7,5},{5,3},{3,1},{1,0},{8,10},{10,12},{12... | collective-permute-start | bytes 884744 | tf_op jit(solution)/shard_map/ppermute | solution.py:150
  8.6 14.6 %collective-permute-start.4 = (bf16[48,3072]{1,0:T(8,128)(2,1)S(1)}, bf16[48,3072]{1,0:T(8,128)(2,1)S(1)}, u32[]{:S(2)}, u32[]{:S(2)}) collective-permute-start(bf16[48,3072]{1,0:T(8,128)(2,1)S(1)} %get-tuple-element.152.refs_0_), channel_id=1, source_target_pairs={{2,0},{4,2},{6,4},{7,6},{5,7},{3,5},{1,3},{0,1},{10,8},{12,10},{14... | collective-permute-start | bytes 884744 | tf_op jit(solution)/shard_map/ppermute | solution.py:150
  16.4 12.6 %collective-permute-start.5 = (bf16[48,3072]{1,0:T(8,128)(2,1)S(1)}, bf16[48,3072]{1,0:T(8,128)(2,1)S(1)}, u32[]{:S(2)}, u32[]{:S(2)}) collective-permute-start(bf16[48,3072]{1,0:T(8,128)(2,1)S(1)} %collective-permute-done.1.refs_1_), channel_id=1, source_target_pairs={{0,2},{2,4},{4,6},{6,7},{7,5},{5,3},{3,1},{1,0},{8,10},{10,12},{12... | collective-permute-start | bytes 884744 | tf_op jit(solution)/shard_map/ppermute | solution.py:150
  16.5 12.6 %collective-permute-start.6 = (bf16[48,3072]{1,0:T(8,128)(2,1)S(1)}, bf16[48,3072]{1,0:T(8,128)(2,1)S(1)}, u32[]{:S(2)}, u32[]{:S(2)}) collective-permute-start(bf16[48,3072]{1,0:T(8,128)(2,1)S(1)} %collective-permute-done.2.refs_7_), channel_id=1, source_target_pairs={{2,0},{4,2},{6,4},{7,6},{5,7},{3,5},{1,3},{0,1},{10,8},{12,10},{14... | collective-permute-start | bytes 884744 | tf_op jit(solution)/shard_map/ppermute | solution.py:150
  23.2 10.1 %collective-permute-start.8 = (bf16[48,3072]{1,0:T(8,128)(2,1)S(1)}, bf16[48,3072]{1,0:T(8,128)(2,1)S(1)}, u32[]{:S(2)}, u32[]{:S(2)}) collective-permute-start(bf16[48,3072]{1,0:T(8,128)(2,1)S(1)} %collective-permute-done.4.refs_2_), channel_id=1, source_target_pairs={{2,0},{4,2},{6,4},{7,6},{5,7},{3,5},{1,3},{0,1},{10,8},{12,10},{14... | collective-permute-start | bytes 884744 | tf_op jit(solution)/shard_map/ppermute | solution.py:150
  24.8 10.6 %collective-permute-start.7 = (bf16[48,3072]{1,0:T(8,128)(2,1)S(1)}, bf16[48,3072]{1,0:T(8,128)(2,1)S(1)}, u32[]{:S(2)}, u32[]{:S(2)}) collective-permute-start(bf16[48,3072]{1,0:T(8,128)(2,1)S(1)} %collective-permute-done.3.refs_6_), channel_id=1, source_target_pairs={{0,2},{2,4},{4,6},{6,7},{7,5},{5,3},{3,1},{1,0},{8,10},{10,12},{12... | collective-permute-start | bytes 884744 | tf_op jit(solution)/shard_map/ppermute | solution.py:150
  29.0 12.6 %collective-permute-start.9 = (bf16[48,3072]{1,0:T(8,128)(2,1)S(1)}, bf16[48,3072]{1,0:T(8,128)(2,1)S(1)}, u32[]{:S(2)}, u32[]{:S(2)}) collective-permute-start(bf16[48,3072]{1,0:T(8,128)(2,1)S(1)} %collective-permute-done.5.refs_3_), channel_id=1, source_target_pairs={{0,2},{2,4},{4,6},{6,7},{7,5},{5,3},{3,1},{1,0},{8,10},{10,12},{12... | collective-permute-start | bytes 884744 | tf_op jit(solution)/shard_map/ppermute | solution.py:150
  29.1 12.6 %collective-permute-start.10 = (bf16[48,3072]{1,0:T(8,128)(2,1)S(1)}, bf16[48,3072]{1,0:T(8,128)(2,1)S(1)}, u32[]{:S(2)}, u32[]{:S(2)}) collective-permute-start(bf16[48,3072]{1,0:T(8,128)(2,1)S(1)} %collective-permute-done.6.refs_9_), channel_id=1, source_target_pairs={{2,0},{4,2},{6,4},{7,6},{5,7},{3,5},{1,3},{0,1},{10,8},{12,10},{14... | collective-permute-start | bytes 884744 | tf_op jit(solution)/shard_map/ppermute | solution.py:150
  38.6 11.3 %collective-permute-start.11 = (bf16[48,3072]{1,0:T(8,128)(2,1)S(1)}, bf16[48,3072]{1,0:T(8,128)(2,1)S(1)}, u32[]{:S(2)}, u32[]{:S(2)}) collective-permute-start(bf16[48,3072]{1,0:T(8,128)(2,1)S(1)} %collective-permute-done.7.refs_8_), channel_id=1, source_target_pairs={{0,2},{2,4},{4,6},{6,7},{7,5},{5,3},{3,1},{1,0},{8,10},{10,12},{12... | collective-permute-start | bytes 884744 | tf_op jit(solution)/shard_map/ppermute | solution.py:150
  38.7 11.2 %collective-permute-start.12 = (bf16[48,3072]{1,0:T(8,128)(2,1)S(1)}, bf16[48,3072]{1,0:T(8,128)(2,1)S(1)}, u32[]{:S(2)}, u32[]{:S(2)}) collective-permute-start(bf16[48,3072]{1,0:T(8,128)(2,1)S(1)} %collective-permute-done.8.refs_4_), channel_id=1, source_target_pairs={{2,0},{4,2},{6,4},{7,6},{5,7},{3,5},{1,3},{0,1},{10,8},{12,10},{14... | collective-permute-start | bytes 884744 | tf_op jit(solution)/shard_map/ppermute | solution.py:150
  41.7 11.5 %collective-permute-start.13 = (bf16[48,3072]{1,0:T(8,128)(2,1)S(1)}, bf16[48,3072]{1,0:T(8,128)(2,1)S(1)}, u32[]{:S(2)}, u32[]{:S(2)}) collective-permute-start(bf16[48,3072]{1,0:T(8,128)(2,1)S(1)} %collective-permute-done.9.refs_0_), channel_id=1, source_target_pairs={{0,2},{2,4},{4,6},{6,7},{7,5},{5,3},{3,1},{1,0},{8,10},{10,12},{12... | collective-permute-start | bytes 884744 | tf_op jit(solution)/shard_map/ppermute | solution.py:150
  41.8 11.4 %collective-permute-start.14 = (bf16[48,3072]{1,0:T(8,128)(2,1)S(1)}, bf16[48,3072]{1,0:T(8,128)(2,1)S(1)}, u32[]{:S(2)}, u32[]{:S(2)}) collective-permute-start(bf16[48,3072]{1,0:T(8,128)(2,1)S(1)} %collective-permute-done.10.refs_4_), channel_id=1, source_target_pairs={{2,0},{4,2},{6,4},{7,6},{5,7},{3,5},{1,3},{0,1},{10,8},{12,10},{14... | collective-permute-start | bytes 884744 | tf_op jit(solution)/shard_map/ppermute | solution.py:150
  49.8 13.9 %copy-start.2 = (s32[64,2]{0,1:T(2,128)S(1)}, s32[64,2]{0,1:T(2,128)}, u32[]{:S(2)}) copy-start(s32[64,2]{0,1:T(2,128)} %param.7) | copy-start | bytes 1540
  49.9 13.9 %copy-start.3 = (f32[64,2]{0,1:T(2,128)S(1)}, f32[64,2]{0,1:T(2,128)}, u32[]{:S(2)}) copy-start(f32[64,2]{0,1:T(2,128)} %param.8) | copy-start | bytes 1540
  61.7 10.3 %collective-permute-start.21 = (bf16[48,3072]{1,0:T(8,128)(2,1)S(1)}, bf16[48,3072]{1,0:T(8,128)(2,1)S(1)}, u32[]{:S(2)}, u32[]{:S(2)}) collective-permute-start(bf16[48,3072]{1,0:T(8,128)(2,1)S(1)} %get-tuple-element.136), channel_id=1, source_target_pairs={{0,2},{2,4},{4,6},{6,7},{7,5},{5,3},{3,1},{1,0},{8,10},{10,12},{12... | collective-permute-start | bytes 884744 | tf_op jit(solution)/shard_map/ppermute | solution.py:150
  62.2 9.9 %collective-permute-start.22 = (bf16[48,3072]{1,0:T(8,128)(2,1)S(1)}, bf16[48,3072]{1,0:T(8,128)(2,1)S(1)}, u32[]{:S(2)}, u32[]{:S(2)}) collective-permute-start(bf16[48,3072]{1,0:T(8,128)(2,1)S(1)} %get-tuple-element.137), channel_id=1, source_target_pairs={{2,0},{4,2},{6,4},{7,6},{5,7},{3,5},{1,3},{0,1},{10,8},{12,10},{14... | collective-permute-start | bytes 884744 | tf_op jit(solution)/shard_map/ppermute | solution.py:150
  63.8 13.4 %collective-permute-start.15 = (bf16[48,3072]{1,0:T(8,128)(2,1)S(1)}, bf16[48,3072]{1,0:T(8,128)(2,1)S(1)}, u32[]{:S(2)}, u32[]{:S(2)}) collective-permute-start(bf16[48,3072]{1,0:T(8,128)(2,1)S(1)} %get-tuple-element.118), channel_id=1, source_target_pairs={{0,2},{2,4},{4,6},{6,7},{7,5},{5,3},{3,1},{1,0},{8,10},{10,12},{12... | collective-permute-start | bytes 884744 | tf_op jit(solution)/shard_map/ppermute | solution.py:150
  64.3 14.2 %collective-permute-start.16 = (bf16[48,3072]{1,0:T(8,128)(2,1)S(1)}, bf16[48,3072]{1,0:T(8,128)(2,1)S(1)}, u32[]{:S(2)}, u32[]{:S(2)}) collective-permute-start(bf16[48,3072]{1,0:T(8,128)(2,1)S(1)} %get-tuple-element.119), channel_id=1, source_target_pairs={{2,0},{4,2},{6,4},{7,6},{5,7},{3,5},{1,3},{0,1},{10,8},{12,10},{14... | collective-permute-start | bytes 884744 | tf_op jit(solution)/shard_map/ppermute | solution.py:150
  72.2 12.6 %collective-permute-start.24 = (bf16[48,3072]{1,0:T(8,128)(2,1)S(1)}, bf16[48,3072]{1,0:T(8,128)(2,1)S(1)}, u32[]{:S(2)}, u32[]{:S(2)}) collective-permute-start(bf16[48,3072]{1,0:T(8,128)(2,1)S(1)} %add_convert_fusion.5), channel_id=1, source_target_pairs={{2,0},{4,2},{6,4},{7,6},{5,7},{3,5},{1,3},{0,1},{10,8},{12,10},{14... | collective-permute-start | bytes 884744 | tf_op jit(solution)/shard_map/ppermute | solution.py:150
  73.9 10.9 %collective-permute-start.23 = (bf16[48,3072]{1,0:T(8,128)(2,1)S(1)}, bf16[48,3072]{1,0:T(8,128)(2,1)S(1)}, u32[]{:S(2)}, u32[]{:S(2)}) collective-permute-start(bf16[48,3072]{1,0:T(8,128)(2,1)S(1)} %add_convert_fusion.6), channel_id=1, source_target_pairs={{0,2},{2,4},{4,6},{6,7},{7,5},{5,3},{3,1},{1,0},{8,10},{10,12},{12... | collective-permute-start | bytes 884744 | tf_op jit(solution)/shard_map/ppermute | solution.py:150
  78.5 12.6 %collective-permute-start.18 = (bf16[48,3072]{1,0:T(8,128)(2,1)S(1)}, bf16[48,3072]{1,0:T(8,128)(2,1)S(1)}, u32[]{:S(2)}, u32[]{:S(2)}) collective-permute-start(bf16[48,3072]{1,0:T(8,128)(2,1)S(1)} %add_convert_fusion.9), channel_id=1, source_target_pairs={{2,0},{4,2},{6,4},{7,6},{5,7},{3,5},{1,3},{0,1},{10,8},{12,10},{14... | collective-permute-start | bytes 884744 | tf_op jit(solution)/shard_map/ppermute | solution.py:150
  80.2 10.9 %collective-permute-start.17 = (bf16[48,3072]{1,0:T(8,128)(2,1)S(1)}, bf16[48,3072]{1,0:T(8,128)(2,1)S(1)}, u32[]{:S(2)}, u32[]{:S(2)}) collective-permute-start(bf16[48,3072]{1,0:T(8,128)(2,1)S(1)} %add_convert_fusion.10), channel_id=1, source_target_pairs={{0,2},{2,4},{4,6},{6,7},{7,5},{5,3},{3,1},{1,0},{8,10},{10,12},{12... | collective-permute-start | bytes 884744 | tf_op jit(solution)/shard_map/ppermute | solution.py:150
  84.9 12.6 %collective-permute-start.26 = (bf16[48,3072]{1,0:T(8,128)(2,1)S(1)}, bf16[48,3072]{1,0:T(8,128)(2,1)S(1)}, u32[]{:S(2)}, u32[]{:S(2)}) collective-permute-start(bf16[48,3072]{1,0:T(8,128)(2,1)S(1)} %add_convert_fusion.3), channel_id=1, source_target_pairs={{2,0},{4,2},{6,4},{7,6},{5,7},{3,5},{1,3},{0,1},{10,8},{12,10},{14... | collective-permute-start | bytes 884744 | tf_op jit(solution)/shard_map/ppermute | solution.py:150
  86.6 10.9 %collective-permute-start.25 = (bf16[48,3072]{1,0:T(8,128)(2,1)S(1)}, bf16[48,3072]{1,0:T(8,128)(2,1)S(1)}, u32[]{:S(2)}, u32[]{:S(2)}) collective-permute-start(bf16[48,3072]{1,0:T(8,128)(2,1)S(1)} %add_convert_fusion.4), channel_id=1, source_target_pairs={{0,2},{2,4},{4,6},{6,7},{7,5},{5,3},{3,1},{1,0},{8,10},{10,12},{12... | collective-permute-start | bytes 884744 | tf_op jit(solution)/shard_map/ppermute | solution.py:150
  91.1 19.5 %copy-start.1 = (bf16[64,6144]{1,0:T(8,128)(2,1)S(1)}, bf16[64,6144]{1,0:T(8,128)(2,1)}, u32[]{:S(2)}) copy-start(bf16[64,6144]{1,0:T(8,128)(2,1)} %param.6) | copy-start | bytes 2359300
  91.2 11.9 %collective-permute-start.20 = (bf16[48,3072]{1,0:T(8,128)(2,1)S(1)}, bf16[48,3072]{1,0:T(8,128)(2,1)S(1)}, u32[]{:S(2)}, u32[]{:S(2)}) collective-permute-start(bf16[48,3072]{1,0:T(8,128)(2,1)S(1)} %add_convert_fusion.7), channel_id=1, source_target_pairs={{2,0},{4,2},{6,4},{7,6},{5,7},{3,5},{1,3},{0,1},{10,8},{12,10},{14... | collective-permute-start | bytes 884744 | tf_op jit(solution)/shard_map/ppermute | solution.py:150
  92.9 10.2 %collective-permute-start.19 = (bf16[48,3072]{1,0:T(8,128)(2,1)S(1)}, bf16[48,3072]{1,0:T(8,128)(2,1)S(1)}, u32[]{:S(2)}, u32[]{:S(2)}) collective-permute-start(bf16[48,3072]{1,0:T(8,128)(2,1)S(1)} %add_convert_fusion.8), channel_id=1, source_target_pairs={{0,2},{2,4},{4,6},{6,7},{7,5},{5,3},{3,1},{1,0},{8,10},{10,12},{12... | collective-permute-start | bytes 884744 | tf_op jit(solution)/shard_map/ppermute | solution.py:150
  97.6 8.2 %collective-permute-start.28 = (bf16[24,3072]{1,0:T(8,128)(2,1)S(1)}, bf16[24,3072]{1,0:T(8,128)(2,1)S(1)}, u32[]{:S(2)}, u32[]{:S(2)}) collective-permute-start(bf16[24,3072]{1,0:T(8,128)(2,1)S(1)} %get-tuple-element.155), channel_id=1, source_target_pairs={{2,0},{4,2},{6,4},{7,6},{5,7},{3,5},{1,3},{0,1},{10,8},{12,10},{14... | collective-permute-start | bytes 442376 | tf_op jit(solution)/shard_map/ppermute | solution.py:150
  99.2 7.0 %collective-permute-start.31 = (bf16[24,3072]{1,0:T(8,128)(2,1)S(1)}, bf16[24,3072]{1,0:T(8,128)(2,1)S(1)}, u32[]{:S(2)}, u32[]{:S(2)}) collective-permute-start(bf16[24,3072]{1,0:T(8,128)(2,1)S(1)} %get-tuple-element.156), channel_id=1, source_target_pairs={{2,8},{4,10},{6,12},{7,14},{5,15},{3,13},{1,11},{0,9},{10,0},{12,2... | collective-permute-start | bytes 442376 | tf_op jit(solution)/shard_map/ppermute | solution.py:155
  99.3 6.6 %collective-permute-start.27 = (bf16[24,3072]{1,0:T(8,128)(2,1)S(1)}, bf16[24,3072]{1,0:T(8,128)(2,1)S(1)}, u32[]{:S(2)}, u32[]{:S(2)}) collective-permute-start(bf16[24,3072]{1,0:T(8,128)(2,1)S(1)} %get-tuple-element.157), channel_id=1, source_target_pairs={{0,2},{2,4},{4,6},{6,7},{7,5},{5,3},{3,1},{1,0},{8,10},{10,12},{12... | collective-permute-start | bytes 442376 | tf_op jit(solution)/shard_map/ppermute | solution.py:150
  103.1 6.1 %collective-permute-start.30 = (bf16[24,3072]{1,0:T(8,128)(2,1)S(1)}, bf16[24,3072]{1,0:T(8,128)(2,1)S(1)}, u32[]{:S(2)}, u32[]{:S(2)}) collective-permute-start(bf16[24,3072]{1,0:T(8,128)(2,1)S(1)} %get-tuple-element.158), channel_id=1, source_target_pairs={{0,10},{2,12},{4,14},{6,15},{7,13},{5,11},{3,9},{1,8},{8,2},{10,4}... | collective-permute-start | bytes 442376 | tf_op jit(solution)/shard_map/ppermute | solution.py:155
  103.3 5.9 %collective-permute-start.29 = (bf16[24,6144]{1,0:T(8,128)(2,1)S(1)}, bf16[24,6144]{1,0:T(8,128)(2,1)S(1)}, u32[]{:S(2)}, u32[]{:S(2)}) collective-permute-start(bf16[24,6144]{1,0:T(8,128)(2,1)S(1)} %fusion.4), channel_id=1, source_target_pairs={{0,8},{8,0},{1,9},{9,1},{2,10},{10,2},{3,11},{11,3},{4,12},{12,4},... | collective-permute-start | bytes 884744 | tf_op jit(solution)/shard_map/ppermute | solution.py:253

commit v16 on v12

--- a/solution.py
+++ b/solution.py
@@ -99,29 +99,25 @@
 
 
 def rest_kernel(*refs):
-    chunks, (w_gate, w_up, down_0, w_down), outs = (refs[:3], refs[3:6]), refs[6:10], refs[10:16]
-    gate, up, down_1, done = refs[16:]
-    copies = row_copies(w_down, down_1, done, down_1.shape[2])
+    chunks, (w_gate, w_up, down), outs, hidden = (refs[:3], refs[3:6]), refs[6:9], refs[9:12], refs[12]
+    gate, up = refs[13:]
+    accumulate(chunks, [(w_gate, gate), (w_up, up)])
+    hidden[...] = activated(gate[...], up[...])
+    add_down(hidden[...], down, outs)
+
+
+def rest_second_kernel(hidden, w_down, *refs):
+    outs, down, done = refs[:3], refs[3], refs[4]
+    copies = row_copies(w_down, down, done, down.shape[2])
     for copy in copies:
         copy.start()
-    accumulate(chunks, [(w_gate, gate), (w_up, up)])
-    hidden = activated(gate[...], up[...])
-    add_down(hidden, down_0, outs[:3])
     for copy in copies:
         copy.wait()
-    add_down(hidden, down_1, outs[3:])
-
-
-def near_down_kernel(hidden, down_0, w_down, *refs):
-    outs, (down_1, done) = refs[:-2], refs[-2:]
-    count = len(outs) // 2
-    copies = row_copies(w_down, down_1, done, down_1.shape[2])
-    for copy in copies:
-        copy.start()
-    add_down(hidden[...], down_0, outs[:count])
-    for copy in copies:
-        copy.wait()
-    add_down(hidden[...], down_1, outs[count:])
+    add_down(hidden[...], down, outs)
+
+
+def near_down_kernel(hidden, down, *outs):
+    add_down(hidden[...], down, outs)
 
 
 def routing(expert_ids, gate_probs, experts, slots):
@@ -206,41 +202,50 @@
     down_here = fetched(w_down, mid_col)
     rest = [rest[chunk] + [far[chunk]] for chunk in range(2)]
     rest, down_here = tied(rest, down_here)
-    down_scratch = [pltpu.VMEM(down_here.shape, jnp.bfloat16), pltpu.SemaphoreType.DMA((COPIES,))]
-    down_room = units * width
-    rest_parts = call(
-        rest_kernel, "rest",
-        [(block, pltpu.VMEM) for chunk in rest for block in chunk]
-        + [(gate_here, pltpu.VMEM), (up_here, pltpu.VMEM), (down_here, pltpu.VMEM), (w_down, pltpu.HBM)],
-        [((size, mid_col), jnp.bfloat16)] * 6,
-        [pltpu.VMEM((3 * size, units), jnp.float32)] * 2 + down_scratch,
-        down_room + 3 * size * units * 16,
-    )
-    near_parts = call(
-        near_down_kernel, "near_down", [(near_hidden, pltpu.VMEM), (down_here, pltpu.VMEM), (w_down, pltpu.HBM)],
-        [((size, mid_col), jnp.bfloat16)] * (2 * count), down_scratch, down_room + rows * TILE * 12,
-    )
+    block = ((size, mid_col), jnp.bfloat16)
+    *rest_0, rest_hidden = call(
+        rest_kernel, "rest_first",
+        [(part, pltpu.VMEM) for chunk in rest for part in chunk]
+        + [(gate_here, pltpu.VMEM), (up_here, pltpu.VMEM), (down_here, pltpu.VMEM)],
+        [block] * 3 + [((3 * size, units), jnp.bfloat16)],
+        [pltpu.VMEM((3 * size, units), jnp.float32)] * 2,
+        3 * size * units * 16,
+    )
+    *rest_1, down_rest = call(
+        rest_second_kernel, "rest_second", [(rest_hidden, pltpu.VMEM), (w_down, pltpu.HBM)],
+        [block] * 3 + [(down_here.shape, jnp.bfloat16)], [pltpu.SemaphoreType.DMA((COPIES,))], 3 * size * TILE * 12,
+    )
+    rest_parts = [rest_0, rest_1]
+
+    def near_down(chunk, hidden):
+        down = (down_here, down_rest)[chunk]
+        return call(
+            near_down_kernel, "near_down", [(hidden, pltpu.VMEM), (down, pltpu.VMEM)],
+            [block] * count, [], rows * TILE * 12,
+        )
+
+    near_hidden, _, _ = tied(near_hidden, rest_1[1], rest_1[2])
+    near_parts = [near_down(0, near_hidden), near_down(1, near_hidden)]
 
     def part_of(chunk, distance, side):
         if distance == half - 1:
-            return rest_parts[3 * chunk + side].astype(jnp.float32)
-        index = 2 * distance - 1 + side if distance else 0
-        return near_parts[count * chunk + index].astype(jnp.float32)
-
-    def sent(stream, distance, got):
-        to_right = part_of(stream, distance, 1) + got[0].astype(jnp.float32)
-        to_left = part_of(1 - stream, distance, 0) + got[1].astype(jnp.float32)
-        return step(to_right.astype(jnp.bfloat16), to_left.astype(jnp.bfloat16))
-
-    a = step(rest_parts[2], rest_parts[5])
-    b = step(rest_parts[4], rest_parts[0])
-    a = sent(0, half - 1, a)
-    for distance in range(half - 2, 0, -1):
-        b = sent(1, distance, b)
-        a = sent(0, distance, a)
+            return rest_parts[chunk][side].astype(jnp.float32)
+        return near_parts[chunk][2 * distance - 1 + side if distance else 0].astype(jnp.float32)
+
+    def added(chunk, distance, side, got):
+        return (part_of(chunk, distance, side) + got.astype(jnp.float32)).astype(jnp.bfloat16)
+
+    flows = [step(rest_0[2], rest_0[0]), step(rest_1[1], rest_1[2])]
+    for distance in range(half - 1, 1, -1):
+        for chunk in range(2):
+            to_right = added(chunk, distance - chunk, 1, flows[chunk][0])
+            to_left = added(chunk, distance - 1 + chunk, 0, flows[chunk][1])
+            flows[chunk] = step(to_right, to_left)
+    last_right = lax.ppermute(added(0, 1, 1, flows[0][0]), "tensor", right)
+    last_left = lax.ppermute(added(1, 1, 0, flows[1][1]), "tensor", left)
     totals = [
-        part_of(0, 0, 0) + a[0].astype(jnp.float32) + b[1].astype(jnp.float32),
-        part_of(1, 0, 0) + b[0].astype(jnp.float32) + a[1].astype(jnp.float32),
+        part_of(0, 0, 0) + last_right.astype(jnp.float32) + flows[0][1].astype(jnp.float32),
+        part_of(1, 0, 0) + flows[1][0].astype(jnp.float32) + last_left.astype(jnp.float32),
     ]
     total = jnp.concatenate(totals, axis=1).astype(jnp.bfloat16)
     returned = jnp.stack([total[:CAP], lax.ppermute(total[CAP:], "expert", swap)])

time: 112 us -> 109 us (0.973)
  Pallas kernels: 33.3 us -> 30.9 us
  waiting for transfers between devices: 43.5 us -> 41.6 us
  starting transfers between devices: 30.7 us -> 31.9 us
    ppermute x14 -> x13, waiting for transfers between devices: 23 us -> 14.9 us  [step(): lax.ppermute(to_left, 'tensor', left)]
    ppermute x0 -> x2, waiting for transfers between devices: none -> 5.02 us  [the longest x1 2.7 us: per_device(): last_right = lax.ppermute(added(0, 1, 1, flows[0][0]), 'tensor', right)]
    ppermute x0 -> x2, starting transfers between devices: none -> 3.27 us  [the longest x1 1.64 us: per_device(): last_left = lax.ppermute(added(1, 1, 0, flows[1][1]), 'tensor', left)]
    pallas_call x7 -> x9, Pallas kernels: 33.3 us -> 30.9 us  [call(): pl.pallas_call(kernel, in_specs=[pl.BlockSpec(memory_space=memory) for _,...]
    ppermute x14 -> x13, starting transfers between devices: 23.7 us -> 21.8 us  [step(): lax.ppermute(to_left, 'tensor', left)]
    ppermute x14 -> x13, waiting for transfers between devices: 17.9 us -> 19 us  [step(): lax.ppermute(to_right, 'tensor', right)]
    ppermute x14 -> x13, starting transfers between devices: 6.48 us -> 6.25 us  [step(): lax.ppermute(to_right, 'tensor', right)]
  transfers between devices with their start and end apart: 30 -> 30, of which waited for: 16 -> 19; matrix products, arithmetic and copies ran while one was open for 1% -> 1% of each run, Pallas kernels for 22% -> 24%
where the time goes in v16:
time: 109 us
  waiting for transfers between devices  41.6 us (38%)
  starting transfers between devices  31.9 us (29%)
  Pallas kernels  30.9 us (28%)
  other arithmetic  2.18 us (2%)
  matrix products  1.58 us (1%)
    pallas_call x9, Pallas kernels, call(): pl.pallas_call(kernel, in_specs=[pl.BlockSpec(memory_space=memory) for _,...  30.9 us
    ppermute x13, starting transfers between devices, step(): lax.ppermute(to_left, 'tensor', left)  21.8 us
    ppermute x13, waiting for transfers between devices, step(): lax.ppermute(to_right, 'tensor', right)  19 us
    ppermute x13, waiting for transfers between devices, step(): lax.ppermute(to_left, 'tensor', left)  14.9 us
    ppermute x13, starting transfers between devices, step(): lax.ppermute(to_right, 'tensor', right)  6.25 us
    ppermute x1, waiting for transfers between devices, per_device(): last_right = lax.ppermute(added(0, 1, 1, flows[0][0]), 'tensor', right)  2.7 us
    ppermute x1, waiting for transfers between devices, per_device(): last_left = lax.ppermute(added(1, 1, 0, flows[1][1]), 'tensor', left)  2.32 us
  transfers between devices with their start and end apart: 30, of which 19 were waited for; matrix products, arithmetic and copies ran while one was open for 1% of the time, Pallas kernels for 24%

profile of v16, /device:TPU:0, one launch (start us, length us, event | category | flops | bytes accessed | tf_op | source)
XLA Modules:
  0.0 108.8 jit_solution(11982301797538719113)
XLA Ops:
  0.0 0.1 eq.64
  0.2 0.8 compare_reduce_fusion
  1.0 0.1 copy.17
  1.1 0.1 reduce_window_sum.11
  1.3 0.1 fusion.9
  1.4 0.3 convolution_convert_fusion
  1.7 0.5 collective-permute-start
  2.3 1.2 %collective-permute-done = bf16[24,6144]{1,0:T(8,128)(2,1)S(1)} collective-permute-done((bf16[24,6144]{1,0:T(8,128)(2,1)S(1)}, bf16[24,6144]{1,0:T(8,128)(2,1)S(1)}, u32[]{:S(2)}, u32[]{:S(2)}) %collective-permute-start) | collective-permute-done | bytes 294944 | tf_op jit(solution)/shard_map/ppermute | solution.py:160
  3.6 2.9 %collective-permute-start.2 = (bf16[48,3072]{1,0:T(8,128)(2,1)S(1)}, bf16[48,3072]{1,0:T(8,128)(2,1)S(1)}, u32[]{:S(2)}, u32[]{:S(2)}) collective-permute-start(bf16[48,3072]{1,0:T(8,128)(2,1)S(1)} %get-tuple-element.149.refs_5_), channel_id=1, source_target_pairs={{2,0},{4,2},{6,4},{7,6},{5,7},{3,5},{1,3},{0,1},{10,8},{12,10},{14... | collective-permute-start | bytes 884744 | tf_op jit(solution)/shard_map/ppermute | solution.py:146
  6.5 0.1 collective-permute-start.1
  6.6 2.0 %collective-permute-start.3 = (bf16[48,3072]{1,0:T(8,128)(2,1)S(1)}, bf16[48,3072]{1,0:T(8,128)(2,1)S(1)}, u32[]{:S(2)}, u32[]{:S(2)}) collective-permute-start(bf16[48,3072]{1,0:T(8,128)(2,1)S(1)} %get-tuple-element.149.refs_5_), channel_id=1, source_target_pairs={{0,2},{2,4},{4,6},{6,7},{7,5},{5,3},{3,1},{1,0},{8,10},{10,12},{12... | collective-permute-start | bytes 884744 | tf_op jit(solution)/shard_map/ppermute | solution.py:146
  8.6 4.7 %fetched.3.refs_10_.refs_6_ = bf16[1,6144,1024]{2,1,0:T(8,128)(2,1)S(1)} custom-call(bf16[1,6144,1024]{2,1,0:T(8,128)(2,1)} %source), custom_call_target="tpu_custom_call" | custom-call | flops 1024 | bytes 1024 | tf_op jit(solution)/shard_map/fetched/pallas_call | solution.py:29
  13.4 1.0 collective-permute-done.2.refs_7_
  14.3 2.0 %collective-permute-done.1.refs_1_ = bf16[48,3072]{1,0:T(8,128)(2,1)S(1)} collective-permute-done((bf16[48,3072]{1,0:T(8,128)(2,1)S(1)}, bf16[48,3072]{1,0:T(8,128)(2,1)S(1)}, u32[]{:S(2)}, u32[]{:S(2)}) %collective-permute-start.1) | collective-permute-done | bytes 294944 | tf_op jit(solution)/shard_map/ppermute | solution.py:146
  16.5 1.9 %collective-permute-start.6 = (bf16[48,3072]{1,0:T(8,128)(2,1)S(1)}, bf16[48,3072]{1,0:T(8,128)(2,1)S(1)}, u32[]{:S(2)}, u32[]{:S(2)}) collective-permute-start(bf16[48,3072]{1,0:T(8,128)(2,1)S(1)} %collective-permute-done.2.refs_7_), channel_id=1, source_target_pairs={{2,0},{4,2},{6,4},{7,6},{5,7},{3,5},{1,3},{0,1},{10,8},{12,10},{14... | collective-permute-start | bytes 884744 | tf_op jit(solution)/shard_map/ppermute | solution.py:146
  18.4 4.7 %fetched.4.refs_10_.refs_7_ = bf16[1,6144,1024]{2,1,0:T(8,128)(2,1)S(1)} custom-call(bf16[1,6144,1024]{2,1,0:T(8,128)(2,1)} %source.1), custom_call_target="tpu_custom_call" | custom-call | flops 1024 | bytes 1024 | tf_op jit(solution)/shard_map/fetched/pallas_call | solution.py:29
  23.2 1.6 %collective-permute-start.8 = (bf16[48,3072]{1,0:T(8,128)(2,1)S(1)}, bf16[48,3072]{1,0:T(8,128)(2,1)S(1)}, u32[]{:S(2)}, u32[]{:S(2)}) collective-permute-start(bf16[48,3072]{1,0:T(8,128)(2,1)S(1)} %collective-permute-done.4.refs_2_), channel_id=1, source_target_pairs={{2,0},{4,2},{6,4},{7,6},{5,7},{3,5},{1,3},{0,1},{10,8},{12,10},{14... | collective-permute-start | bytes 884744 | tf_op jit(solution)/shard_map/ppermute | solution.py:146
  24.8 0.4 collective-permute-start.7
  25.2 3.8 %collective-permute-done.5.refs_3_ = bf16[48,3072]{1,0:T(8,128)(2,1)S(1)} collective-permute-done((bf16[48,3072]{1,0:T(8,128)(2,1)S(1)}, bf16[48,3072]{1,0:T(8,128)(2,1)S(1)}, u32[]{:S(2)}, u32[]{:S(2)}) %collective-permute-start.5) | collective-permute-done | bytes 294944 | tf_op jit(solution)/shard_map/ppermute | solution.py:146
  29.0 0.1 collective-permute-start.9
  29.1 1.9 %collective-permute-start.10 = (bf16[48,3072]{1,0:T(8,128)(2,1)S(1)}, bf16[48,3072]{1,0:T(8,128)(2,1)S(1)}, u32[]{:S(2)}, u32[]{:S(2)}) collective-permute-start(bf16[48,3072]{1,0:T(8,128)(2,1)S(1)} %collective-permute-done.6.refs_9_), channel_id=1, source_target_pairs={{2,0},{4,2},{6,4},{7,6},{5,7},{3,5},{1,3},{0,1},{10,8},{12,10},{14... | collective-permute-start | bytes 884744 | tf_op jit(solution)/shard_map/ppermute | solution.py:146
  31.1 2.2 %collective-permute-done.8.refs_4_ = bf16[48,3072]{1,0:T(8,128)(2,1)S(1)} collective-permute-done((bf16[48,3072]{1,0:T(8,128)(2,1)S(1)}, bf16[48,3072]{1,0:T(8,128)(2,1)S(1)}, u32[]{:S(2)}, u32[]{:S(2)}) %collective-permute-start.8) | collective-permute-done | bytes 294944 | tf_op jit(solution)/shard_map/ppermute | solution.py:146
  33.3 2.0 %collective-permute-done.7.refs_8_ = bf16[48,3072]{1,0:T(8,128)(2,1)S(1)} collective-permute-done((bf16[48,3072]{1,0:T(8,128)(2,1)S(1)}, bf16[48,3072]{1,0:T(8,128)(2,1)S(1)}, u32[]{:S(2)}, u32[]{:S(2)}) %collective-permute-start.7) | collective-permute-done | bytes 294944 | tf_op jit(solution)/shard_map/ppermute | solution.py:146
  35.4 3.2 %near_gate.1.refs_11_ = f32[240,1024]{1,0:T(8,128)S(1)} custom-call(bf16[48,3072]{1,0:T(8,128)(2,1)S(1)} %get-tuple-element.150.refs_0_, bf16[48,3072]{1,0:T(8,128)(2,1)S(1)} %collective-permute-done.1.refs_1_, bf16[48,3072]{1,0:T(8,128)(2,1)S(1)} %collective-permute-done.4.refs_2_, bf16[48,3072]{1,0:T(8,128)(2,1)S(1)} %collective-permute-done.5.refs_3_, ...), custom_call_target="tpu_custom_call" | custom-call | flops 1024 | bytes 1024 | tf_op jit(solution)/shard_map/near_gate/pallas_call | solution.py:29
  38.6 0.1 collective-permute-start.11
  38.7 1.9 %collective-permute-start.12 = (bf16[48,3072]{1,0:T(8,128)(2,1)S(1)}, bf16[48,3072]{1,0:T(8,128)(2,1)S(1)}, u32[]{:S(2)}, u32[]{:S(2)}) collective-permute-start(bf16[48,3072]{1,0:T(8,128)(2,1)S(1)} %collective-permute-done.8.refs_4_), channel_id=1, source_target_pairs={{2,0},{4,2},{6,4},{7,6},{5,7},{3,5},{1,3},{0,1},{10,8},{12,10},{14... | collective-permute-start | bytes 884744 | tf_op jit(solution)/shard_map/ppermute | solution.py:146
  40.6 1.0 collective-permute-done.9.refs_0_
  41.7 0.1 collective-permute-start.13
  41.8 1.9 %collective-permute-start.14 = (bf16[48,3072]{1,0:T(8,128)(2,1)S(1)}, bf16[48,3072]{1,0:T(8,128)(2,1)S(1)}, u32[]{:S(2)}, u32[]{:S(2)}) collective-permute-start(bf16[48,3072]{1,0:T(8,128)(2,1)S(1)} %collective-permute-done.10.refs_4_), channel_id=1, source_target_pairs={{2,0},{4,2},{6,4},{7,6},{5,7},{3,5},{1,3},{0,1},{10,8},{12,10},{14... | collective-permute-start | bytes 884744 | tf_op jit(solution)/shard_map/ppermute | solution.py:146
  43.7 3.2 %near_up.1.hidden = bf16[240,1024]{1,0:T(8,128)(2,1)S(1)} custom-call(bf16[48,3072]{1,0:T(8,128)(2,1)S(1)} %get-tuple-element.150.refs_0_, bf16[48,3072]{1,0:T(8,128)(2,1)S(1)} %collective-permute-done.1.refs_1_, bf16[48,3072]{1,0:T(8,128)(2,1)S(1)} %collective-permute-done.4.refs_2_, bf16[48,3072]{1,0:T(8,128)(2,1)S(1)} %collective-permute-done.5.refs_3_, ...), custom_call_target="tpu_custom_call" | custom-call | flops 1024 | bytes 1024 | tf_op jit(solution)/shard_map/near_up/pallas_call | solution.py:29
  46.9 2.9 %fetched.5.refs_8_.down = bf16[1,1024,3072]{2,1,0:T(8,128)(2,1)S(1)} custom-call(bf16[1,1024,6144]{2,1,0:T(8,128)(2,1)} %w_down), custom_call_target="tpu_custom_call" | custom-call | flops 1024 | bytes 1024 | tf_op jit(solution)/shard_map/fetched/pallas_call | solution.py:29
  49.9 3.3 %collective-permute-done.13.refs_2_ = bf16[48,3072]{1,0:T(8,128)(2,1)S(1)} collective-permute-done((bf16[48,3072]{1,0:T(8,128)(2,1)S(1)}, bf16[48,3072]{1,0:T(8,128)(2,1)S(1)}, u32[]{:S(2)}, u32[]{:S(2)}) %collective-permute-start.13) | collective-permute-done | bytes 294944 | tf_op jit(solution)/shard_map/ppermute | solution.py:146
  53.2 4.8 %rest_first.1 = (bf16[48,3072]{1,0:T(8,128)(2,1)S(1)}, bf16[48,3072]{1,0:T(8,128)(2,1)S(1)}, bf16[48,3072]{1,0:T(8,128)(2,1)S(1)}, bf16[144,1024]{1,0:T(8,128)(2,1)S(1)}) custom-call(bf16[48,3072]{1,0:T(8,128)(2,1)S(1)} %collective-permute-done.9.refs_0_, bf16[48,3072]{1,0:T(8,128)(2,1)S(1)} %collective-permute-done.12.refs_1_, ...), custom_call_target="tpu_custom_call" | custom-call | flops 1024 | bytes 1024 | tf_op jit(solution)/shard_map/rest_first/pallas_call | solution.py:29
  58.0 0.5 collective-permute-start.15
  58.5 1.6 %collective-permute-start.16 = (bf16[48,3072]{1,0:T(8,128)(2,1)S(1)}, bf16[48,3072]{1,0:T(8,128)(2,1)S(1)}, u32[]{:S(2)}, u32[]{:S(2)}) collective-permute-start(bf16[48,3072]{1,0:T(8,128)(2,1)S(1)} %get-tuple-element.125), channel_id=1, source_target_pairs={{2,0},{4,2},{6,4},{7,6},{5,7},{3,5},{1,3},{0,1},{10,8},{12,10},{14... | collective-permute-start | bytes 884744 | tf_op jit(solution)/shard_map/ppermute | solution.py:146
  60.0 4.0 %rest_second.1 = (bf16[48,3072]{1,0:T(8,128)(2,1)S(1)}, bf16[48,3072]{1,0:T(8,128)(2,1)S(1)}, bf16[48,3072]{1,0:T(8,128)(2,1)S(1)}, bf16[1,1024,3072]{2,1,0:T(8,128)(2,1)S(1)}) custom-call(bf16[144,1024]{1,0:T(8,128)(2,1)S(1)} %get-tuple-element.116.hidden, bf16[1,1024,6144]{2,1,0:T(8,128)(2,1)} %w_down), custom_call_target="tpu_custom_call" | custom-call | flops 1024 | bytes 1024 | tf_op jit(solution)/shard_map/rest_second/pallas_call | solution.py:29
  64.1 0.5 collective-permute-start.22
  64.6 1.6 %collective-permute-start.23 = (bf16[48,3072]{1,0:T(8,128)(2,1)S(1)}, bf16[48,3072]{1,0:T(8,128)(2,1)S(1)}, u32[]{:S(2)}, u32[]{:S(2)}) collective-permute-start(bf16[48,3072]{1,0:T(8,128)(2,1)S(1)} %get-tuple-element.118), channel_id=1, source_target_pairs={{2,0},{4,2},{6,4},{7,6},{5,7},{3,5},{1,3},{0,1},{10,8},{12,10},{14... | collective-permute-start | bytes 884744 | tf_op jit(solution)/shard_map/ppermute | solution.py:146
  66.2 1.7 %near_down.2 = (bf16[48,3072]{1,0:T(8,128)(2,1)S(1)}, bf16[48,3072]{1,0:T(8,128)(2,1)S(1)}, bf16[48,3072]{1,0:T(8,128)(2,1)S(1)}, bf16[48,3072]{1,0:T(8,128)(2,1)S(1)}, bf16[48,3072]{1,0:T(8,128)(2,1)S(1)}) custom-call(bf16[240,1024]{1,0:T(8,128)(2,1)S(1)} %near_up.1.hidden, bf16[1,1024,3072]{2,1,0:T(8,128)(2,1)S(1)} %fetched.5.refs_8_.down), custom_call_target="tpu_custom_call" | custom-call | flops 1024 | bytes 1024 | tf_op jit(solution)/shard_map/near_down/pallas_call | solution.py:29
  67.8 1.7 %near_down.3 = (bf16[48,3072]{1,0:T(8,128)(2,1)S(1)}, bf16[48,3072]{1,0:T(8,128)(2,1)S(1)}, bf16[48,3072]{1,0:T(8,128)(2,1)S(1)}, bf16[48,3072]{1,0:T(8,128)(2,1)S(1)}, bf16[48,3072]{1,0:T(8,128)(2,1)S(1)}) custom-call(bf16[240,1024]{1,0:T(8,128)(2,1)S(1)} %near_up.1.hidden, bf16[1,1024,3072]{2,1,0:T(8,128)(2,1)S(1)} %get-tuple-element.134.down), custom_call_target="tpu_custom_call" | custom-call | flops 1024 | bytes 1024 | tf_op jit(solution)/shard_map/near_down/pallas_call | solution.py:29
  69.7 0.5 collective-permute-start.17
  70.3 1.6 %collective-permute-start.18 = (bf16[48,3072]{1,0:T(8,128)(2,1)S(1)}, bf16[48,3072]{1,0:T(8,128)(2,1)S(1)}, u32[]{:S(2)}, u32[]{:S(2)}) collective-permute-start(bf16[48,3072]{1,0:T(8,128)(2,1)S(1)} %add_convert_fusion.10), channel_id=1, source_target_pairs={{2,0},{4,2},{6,4},{7,6},{5,7},{3,5},{1,3},{0,1},{10,8},{12,10},{14... | collective-permute-start | bytes 884744 | tf_op jit(solution)/shard_map/ppermute | solution.py:146
  71.9 1.7 %collective-permute-done.22 = bf16[48,3072]{1,0:T(8,128)(2,1)S(1)} collective-permute-done((bf16[48,3072]{1,0:T(8,128)(2,1)S(1)}, bf16[48,3072]{1,0:T(8,128)(2,1)S(1)}, u32[]{:S(2)}, u32[]{:S(2)}) %collective-permute-start.22) | collective-permute-done | bytes 294944 | tf_op jit(solution)/shard_map/ppermute | solution.py:146
  73.6 0.4 collective-permute-done.23
  74.0 1.4 %collective-permute-start.25 = (bf16[48,3072]{1,0:T(8,128)(2,1)S(1)}, bf16[48,3072]{1,0:T(8,128)(2,1)S(1)}, u32[]{:S(2)}, u32[]{:S(2)}) collective-permute-start(bf16[48,3072]{1,0:T(8,128)(2,1)S(1)} %add_convert_fusion.4), channel_id=1, source_target_pairs={{2,0},{4,2},{6,4},{7,6},{5,7},{3,5},{1,3},{0,1},{10,8},{12,10},{14... | collective-permute-start | bytes 884744 | tf_op jit(solution)/shard_map/ppermute | solution.py:146
  75.5 0.7 collective-permute-start.24
  76.3 3.6 %collective-permute-done.17 = bf16[48,3072]{1,0:T(8,128)(2,1)S(1)} collective-permute-done((bf16[48,3072]{1,0:T(8,128)(2,1)S(1)}, bf16[48,3072]{1,0:T(8,128)(2,1)S(1)}, u32[]{:S(2)}, u32[]{:S(2)}) %collective-permute-start.17) | collective-permute-done | bytes 294944 | tf_op jit(solution)/shard_map/ppermute | solution.py:146
  79.9 0.4 collective-permute-done.18
  80.4 1.6 %collective-permute-start.20 = (bf16[48,3072]{1,0:T(8,128)(2,1)S(1)}, bf16[48,3072]{1,0:T(8,128)(2,1)S(1)}, u32[]{:S(2)}, u32[]{:S(2)}) collective-permute-start(bf16[48,3072]{1,0:T(8,128)(2,1)S(1)} %add_convert_fusion.8), channel_id=1, source_target_pairs={{2,0},{4,2},{6,4},{7,6},{5,7},{3,5},{1,3},{0,1},{10,8},{12,10},{14... | collective-permute-start | bytes 884744 | tf_op jit(solution)/shard_map/ppermute | solution.py:146
  82.0 0.5 collective-permute-start.19
  82.6 4.0 %collective-permute-done.25 = bf16[48,3072]{1,0:T(8,128)(2,1)S(1)} collective-permute-done((bf16[48,3072]{1,0:T(8,128)(2,1)S(1)}, bf16[48,3072]{1,0:T(8,128)(2,1)S(1)}, u32[]{:S(2)}, u32[]{:S(2)}) %collective-permute-start.25) | collective-permute-done | bytes 294944 | tf_op jit(solution)/shard_map/ppermute | solution.py:146
  86.7 1.6 %collective-permute-start.27 = (bf16[48,3072]{1,0:T(8,128)(2,1)S(1)}, bf16[48,3072]{1,0:T(8,128)(2,1)S(1)}, u32[]{:S(2)}, u32[]{:S(2)}) collective-permute-start(bf16[48,3072]{1,0:T(8,128)(2,1)S(1)} %add_convert_fusion.2), channel_id=1, source_target_pairs={{2,0},{4,2},{6,4},{7,6},{5,7},{3,5},{1,3},{0,1},{10,8},{12,10},{14... | collective-permute-start | bytes 884744 | tf_op jit(solution)/shard_map/ppermute | solution.py:146
  88.3 0.5 collective-permute-start.26
  88.9 4.0 %collective-permute-done.20 = bf16[48,3072]{1,0:T(8,128)(2,1)S(1)} collective-permute-done((bf16[48,3072]{1,0:T(8,128)(2,1)S(1)}, bf16[48,3072]{1,0:T(8,128)(2,1)S(1)}, u32[]{:S(2)}, u32[]{:S(2)}) %collective-permute-start.20) | collective-permute-done | bytes 294944 | tf_op jit(solution)/shard_map/ppermute | solution.py:146
  93.0 1.6 %collective-permute-start.21 = (bf16[48,3072]{1,0:T(8,128)(2,1)S(1)}, bf16[48,3072]{1,0:T(8,128)(2,1)S(1)}, u32[]{:S(2)}, u32[]{:S(2)}) collective-permute-start(bf16[48,3072]{1,0:T(8,128)(2,1)S(1)} %add_convert_fusion.7), channel_id=1, source_target_pairs={{0,2},{2,4},{4,6},{6,7},{7,5},{5,3},{3,1},{1,0},{8,10},{10,12},{12... | collective-permute-start | bytes 884744 | tf_op jit(solution)/shard_map/ppermute | solution.py:244
  94.6 2.7 %collective-permute-done.27 = bf16[48,3072]{1,0:T(8,128)(2,1)S(1)} collective-permute-done((bf16[48,3072]{1,0:T(8,128)(2,1)S(1)}, bf16[48,3072]{1,0:T(8,128)(2,1)S(1)}, u32[]{:S(2)}, u32[]{:S(2)}) %collective-permute-start.27) | collective-permute-done | bytes 294944 | tf_op jit(solution)/shard_map/ppermute | solution.py:146
  97.4 1.5 %collective-permute-done.26 = bf16[48,3072]{1,0:T(8,128)(2,1)S(1)} collective-permute-done((bf16[48,3072]{1,0:T(8,128)(2,1)S(1)}, bf16[48,3072]{1,0:T(8,128)(2,1)S(1)}, u32[]{:S(2)}, u32[]{:S(2)}) %collective-permute-start.26) | collective-permute-done | bytes 294944 | tf_op jit(solution)/shard_map/ppermute | solution.py:146
  98.9 1.6 %collective-permute-start.28 = (bf16[48,3072]{1,0:T(8,128)(2,1)S(1)}, bf16[48,3072]{1,0:T(8,128)(2,1)S(1)}, u32[]{:S(2)}, u32[]{:S(2)}) collective-permute-start(bf16[48,3072]{1,0:T(8,128)(2,1)S(1)} %add_convert_fusion.1), channel_id=1, source_target_pairs={{2,0},{4,2},{6,4},{7,6},{5,7},{3,5},{1,3},{0,1},{10,8},{12,10},{14... | collective-permute-start | bytes 884744 | tf_op jit(solution)/shard_map/ppermute | solution.py:245
  100.6 2.7 %collective-permute-done.21 = bf16[48,3072]{1,0:T(8,128)(2,1)S(1)} collective-permute-done((bf16[48,3072]{1,0:T(8,128)(2,1)S(1)}, bf16[48,3072]{1,0:T(8,128)(2,1)S(1)}, u32[]{:S(2)}, u32[]{:S(2)}) %collective-permute-start.21) | collective-permute-done | bytes 294944 | tf_op jit(solution)/shard_map/ppermute | solution.py:244
  103.3 0.1 add_convert_fusion.6
  103.4 2.3 %collective-permute-done.28 = bf16[48,3072]{1,0:T(8,128)(2,1)S(1)} collective-permute-done((bf16[48,3072]{1,0:T(8,128)(2,1)S(1)}, bf16[48,3072]{1,0:T(8,128)(2,1)S(1)}, u32[]{:S(2)}, u32[]{:S(2)}) %collective-permute-start.28) | collective-permute-done | bytes 294944 | tf_op jit(solution)/shard_map/ppermute | solution.py:245
  105.7 0.1 add_convert_fusion
  106.0 1.5 %collective-permute-done.29 = bf16[24,6144]{1,0:T(8,128)(2,1)S(1)} collective-permute-done((bf16[24,6144]{1,0:T(8,128)(2,1)S(1)}, bf16[24,6144]{1,0:T(8,128)(2,1)S(1)}, u32[]{:S(2)}, u32[]{:S(2)}) %collective-permute-start.29) | collective-permute-done | bytes 294944 | tf_op jit(solution)/shard_map/ppermute | solution.py:251
  107.5 1.3 %fusion = bf16[64,6144]{1,0:T(8,128)(2,1)} fusion(bf16[1,24,6144]{2,1,0:T(8,128)(2,1)S(1)} %bitcast.22, bf16[1,24,6144]{2,1,0:T(8,128)(2,1)S(1)} %get-tuple-element.147, bf16[2,64]{1,0:T(2,128)(2,1)S(1)} %bitcast.23, s32[2,64]{1,0:T(2,128)S(1)} %subtract_bitcast_fusion, pred[2,64]{1,0:T(4,128)(4,1)S(1)} %get-tuple-element.153), kind=kOutput, calls=%fused_computation.1 | convolution fusion | flops 38052864 | bytes 1377152 | tf_op jit(solution)/shard_map/wcr,wcd->rd/dot_general | solution.py:253
  (42 shorter events, 1.4 us)
Async XLA Ops:
  0.0 1.4 %copy-start = (bf16[64,6144]{1,0:T(8,128)(2,1)S(1)}, bf16[64,6144]{1,0:T(8,128)(2,1)}, u32[]{:S(2)}) copy-start(bf16[64,6144]{1,0:T(8,128)(2,1)} %param.6) | copy-start | bytes 2359300
  1.7 1.7 %collective-permute-start = (bf16[24,6144]{1,0:T(8,128)(2,1)S(1)}, bf16[24,6144]{1,0:T(8,128)(2,1)S(1)}, u32[]{:S(2)}, u32[]{:S(2)}) collective-permute-start(bf16[24,6144]{1,0:T(8,128)(2,1)S(1)} %get-tuple-element.152), channel_id=1, source_target_pairs={{0,8},{8,0},{1,9},{9,1},{2,10},{10,2},{3,11},{11,3},{4,12},{12,4},... | collective-permute-start | bytes 884744 | tf_op jit(solution)/shard_map/ppermute | solution.py:160
  3.6 10.8 %collective-permute-start.2 = (bf16[48,3072]{1,0:T(8,128)(2,1)S(1)}, bf16[48,3072]{1,0:T(8,128)(2,1)S(1)}, u32[]{:S(2)}, u32[]{:S(2)}) collective-permute-start(bf16[48,3072]{1,0:T(8,128)(2,1)S(1)} %get-tuple-element.149.refs_5_), channel_id=1, source_target_pairs={{2,0},{4,2},{6,4},{7,6},{5,7},{3,5},{1,3},{0,1},{10,8},{12,10},{14... | collective-permute-start | bytes 884744 | tf_op jit(solution)/shard_map/ppermute | solution.py:146
  6.5 9.9 %collective-permute-start.1 = (bf16[48,3072]{1,0:T(8,128)(2,1)S(1)}, bf16[48,3072]{1,0:T(8,128)(2,1)S(1)}, u32[]{:S(2)}, u32[]{:S(2)}) collective-permute-start(bf16[48,3072]{1,0:T(8,128)(2,1)S(1)} %get-tuple-element.150.refs_0_), channel_id=1, source_target_pairs={{0,2},{2,4},{4,6},{6,7},{7,5},{5,3},{3,1},{1,0},{8,10},{10,12},{12... | collective-permute-start | bytes 884744 | tf_op jit(solution)/shard_map/ppermute | solution.py:146
  6.6 16.5 %collective-permute-start.3 = (bf16[48,3072]{1,0:T(8,128)(2,1)S(1)}, bf16[48,3072]{1,0:T(8,128)(2,1)S(1)}, u32[]{:S(2)}, u32[]{:S(2)}) collective-permute-start(bf16[48,3072]{1,0:T(8,128)(2,1)S(1)} %get-tuple-element.149.refs_5_), channel_id=1, source_target_pairs={{0,2},{2,4},{4,6},{6,7},{7,5},{5,3},{3,1},{1,0},{8,10},{10,12},{12... | collective-permute-start | bytes 884744 | tf_op jit(solution)/shard_map/ppermute | solution.py:146
  8.6 14.6 %collective-permute-start.4 = (bf16[48,3072]{1,0:T(8,128)(2,1)S(1)}, bf16[48,3072]{1,0:T(8,128)(2,1)S(1)}, u32[]{:S(2)}, u32[]{:S(2)}) collective-permute-start(bf16[48,3072]{1,0:T(8,128)(2,1)S(1)} %get-tuple-element.150.refs_0_), channel_id=1, source_target_pairs={{2,0},{4,2},{6,4},{7,6},{5,7},{3,5},{1,3},{0,1},{10,8},{12,10},{14... | collective-permute-start | bytes 884744 | tf_op jit(solution)/shard_map/ppermute | solution.py:146
  16.4 12.6 %collective-permute-start.5 = (bf16[48,3072]{1,0:T(8,128)(2,1)S(1)}, bf16[48,3072]{1,0:T(8,128)(2,1)S(1)}, u32[]{:S(2)}, u32[]{:S(2)}) collective-permute-start(bf16[48,3072]{1,0:T(8,128)(2,1)S(1)} %collective-permute-done.1.refs_1_), channel_id=1, source_target_pairs={{0,2},{2,4},{4,6},{6,7},{7,5},{5,3},{3,1},{1,0},{8,10},{10,12},{12... | collective-permute-start | bytes 884744 | tf_op jit(solution)/shard_map/ppermute | solution.py:146
  16.5 12.6 %collective-permute-start.6 = (bf16[48,3072]{1,0:T(8,128)(2,1)S(1)}, bf16[48,3072]{1,0:T(8,128)(2,1)S(1)}, u32[]{:S(2)}, u32[]{:S(2)}) collective-permute-start(bf16[48,3072]{1,0:T(8,128)(2,1)S(1)} %collective-permute-done.2.refs_7_), channel_id=1, source_target_pairs={{2,0},{4,2},{6,4},{7,6},{5,7},{3,5},{1,3},{0,1},{10,8},{12,10},{14... | collective-permute-start | bytes 884744 | tf_op jit(solution)/shard_map/ppermute | solution.py:146
  23.2 10.1 %collective-permute-start.8 = (bf16[48,3072]{1,0:T(8,128)(2,1)S(1)}, bf16[48,3072]{1,0:T(8,128)(2,1)S(1)}, u32[]{:S(2)}, u32[]{:S(2)}) collective-permute-start(bf16[48,3072]{1,0:T(8,128)(2,1)S(1)} %collective-permute-done.4.refs_2_), channel_id=1, source_target_pairs={{2,0},{4,2},{6,4},{7,6},{5,7},{3,5},{1,3},{0,1},{10,8},{12,10},{14... | collective-permute-start | bytes 884744 | tf_op jit(solution)/shard_map/ppermute | solution.py:146
  24.8 10.6 %collective-permute-start.7 = (bf16[48,3072]{1,0:T(8,128)(2,1)S(1)}, bf16[48,3072]{1,0:T(8,128)(2,1)S(1)}, u32[]{:S(2)}, u32[]{:S(2)}) collective-permute-start(bf16[48,3072]{1,0:T(8,128)(2,1)S(1)} %collective-permute-done.3.refs_6_), channel_id=1, source_target_pairs={{0,2},{2,4},{4,6},{6,7},{7,5},{5,3},{3,1},{1,0},{8,10},{10,12},{12... | collective-permute-start | bytes 884744 | tf_op jit(solution)/shard_map/ppermute | solution.py:146
  29.0 12.6 %collective-permute-start.9 = (bf16[48,3072]{1,0:T(8,128)(2,1)S(1)}, bf16[48,3072]{1,0:T(8,128)(2,1)S(1)}, u32[]{:S(2)}, u32[]{:S(2)}) collective-permute-start(bf16[48,3072]{1,0:T(8,128)(2,1)S(1)} %collective-permute-done.5.refs_3_), channel_id=1, source_target_pairs={{0,2},{2,4},{4,6},{6,7},{7,5},{5,3},{3,1},{1,0},{8,10},{10,12},{12... | collective-permute-start | bytes 884744 | tf_op jit(solution)/shard_map/ppermute | solution.py:146
  29.1 12.6 %collective-permute-start.10 = (bf16[48,3072]{1,0:T(8,128)(2,1)S(1)}, bf16[48,3072]{1,0:T(8,128)(2,1)S(1)}, u32[]{:S(2)}, u32[]{:S(2)}) collective-permute-start(bf16[48,3072]{1,0:T(8,128)(2,1)S(1)} %collective-permute-done.6.refs_9_), channel_id=1, source_target_pairs={{2,0},{4,2},{6,4},{7,6},{5,7},{3,5},{1,3},{0,1},{10,8},{12,10},{14... | collective-permute-start | bytes 884744 | tf_op jit(solution)/shard_map/ppermute | solution.py:146
  38.6 11.3 %collective-permute-start.11 = (bf16[48,3072]{1,0:T(8,128)(2,1)S(1)}, bf16[48,3072]{1,0:T(8,128)(2,1)S(1)}, u32[]{:S(2)}, u32[]{:S(2)}) collective-permute-start(bf16[48,3072]{1,0:T(8,128)(2,1)S(1)} %collective-permute-done.7.refs_8_), channel_id=1, source_target_pairs={{0,2},{2,4},{4,6},{6,7},{7,5},{5,3},{3,1},{1,0},{8,10},{10,12},{12... | collective-permute-start | bytes 884744 | tf_op jit(solution)/shard_map/ppermute | solution.py:146
  38.7 11.2 %collective-permute-start.12 = (bf16[48,3072]{1,0:T(8,128)(2,1)S(1)}, bf16[48,3072]{1,0:T(8,128)(2,1)S(1)}, u32[]{:S(2)}, u32[]{:S(2)}) collective-permute-start(bf16[48,3072]{1,0:T(8,128)(2,1)S(1)} %collective-permute-done.8.refs_4_), channel_id=1, source_target_pairs={{2,0},{4,2},{6,4},{7,6},{5,7},{3,5},{1,3},{0,1},{10,8},{12,10},{14... | collective-permute-start | bytes 884744 | tf_op jit(solution)/shard_map/ppermute | solution.py:146
  41.7 11.5 %collective-permute-start.13 = (bf16[48,3072]{1,0:T(8,128)(2,1)S(1)}, bf16[48,3072]{1,0:T(8,128)(2,1)S(1)}, u32[]{:S(2)}, u32[]{:S(2)}) collective-permute-start(bf16[48,3072]{1,0:T(8,128)(2,1)S(1)} %collective-permute-done.9.refs_0_), channel_id=1, source_target_pairs={{0,2},{2,4},{4,6},{6,7},{7,5},{5,3},{3,1},{1,0},{8,10},{10,12},{12... | collective-permute-start | bytes 884744 | tf_op jit(solution)/shard_map/ppermute | solution.py:146
  41.8 11.4 %collective-permute-start.14 = (bf16[48,3072]{1,0:T(8,128)(2,1)S(1)}, bf16[48,3072]{1,0:T(8,128)(2,1)S(1)}, u32[]{:S(2)}, u32[]{:S(2)}) collective-permute-start(bf16[48,3072]{1,0:T(8,128)(2,1)S(1)} %collective-permute-done.10.refs_4_), channel_id=1, source_target_pairs={{2,0},{4,2},{6,4},{7,6},{5,7},{3,5},{1,3},{0,1},{10,8},{12,10},{14... | collective-permute-start | bytes 884744 | tf_op jit(solution)/shard_map/ppermute | solution.py:146
  58.0 11.6 %collective-permute-start.15 = (bf16[48,3072]{1,0:T(8,128)(2,1)S(1)}, bf16[48,3072]{1,0:T(8,128)(2,1)S(1)}, u32[]{:S(2)}, u32[]{:S(2)}) collective-permute-start(bf16[48,3072]{1,0:T(8,128)(2,1)S(1)} %get-tuple-element.124), channel_id=1, source_target_pairs={{0,2},{2,4},{4,6},{6,7},{7,5},{5,3},{3,1},{1,0},{8,10},{10,12},{12... | collective-permute-start | bytes 884744 | tf_op jit(solution)/shard_map/ppermute | solution.py:146
  58.5 11.1 %collective-permute-start.16 = (bf16[48,3072]{1,0:T(8,128)(2,1)S(1)}, bf16[48,3072]{1,0:T(8,128)(2,1)S(1)}, u32[]{:S(2)}, u32[]{:S(2)}) collective-permute-start(bf16[48,3072]{1,0:T(8,128)(2,1)S(1)} %get-tuple-element.125), channel_id=1, source_target_pairs={{2,0},{4,2},{6,4},{7,6},{5,7},{3,5},{1,3},{0,1},{10,8},{12,10},{14... | collective-permute-start | bytes 884744 | tf_op jit(solution)/shard_map/ppermute | solution.py:146
  64.1 9.5 %collective-permute-start.22 = (bf16[48,3072]{1,0:T(8,128)(2,1)S(1)}, bf16[48,3072]{1,0:T(8,128)(2,1)S(1)}, u32[]{:S(2)}, u32[]{:S(2)}) collective-permute-start(bf16[48,3072]{1,0:T(8,128)(2,1)S(1)} %get-tuple-element.117), channel_id=1, source_target_pairs={{0,2},{2,4},{4,6},{6,7},{7,5},{5,3},{3,1},{1,0},{8,10},{10,12},{12... | collective-permute-start | bytes 884744 | tf_op jit(solution)/shard_map/ppermute | solution.py:146
  64.6 9.4 %collective-permute-start.23 = (bf16[48,3072]{1,0:T(8,128)(2,1)S(1)}, bf16[48,3072]{1,0:T(8,128)(2,1)S(1)}, u32[]{:S(2)}, u32[]{:S(2)}) collective-permute-start(bf16[48,3072]{1,0:T(8,128)(2,1)S(1)} %get-tuple-element.118), channel_id=1, source_target_pairs={{2,0},{4,2},{6,4},{7,6},{5,7},{3,5},{1,3},{0,1},{10,8},{12,10},{14... | collective-permute-start | bytes 884744 | tf_op jit(solution)/shard_map/ppermute | solution.py:146
  69.5 36.4 %copy-start.2 = (s32[64,2]{0,1:T(2,128)S(1)}, s32[64,2]{0,1:T(2,128)}, u32[]{:S(2)}) copy-start(s32[64,2]{0,1:T(2,128)} %param.7) | copy-start | bytes 1540
  69.6 36.4 %copy-start.3 = (f32[64,2]{0,1:T(2,128)S(1)}, f32[64,2]{0,1:T(2,128)}, u32[]{:S(2)}) copy-start(f32[64,2]{0,1:T(2,128)} %param.8) | copy-start | bytes 1540
  69.7 10.2 %collective-permute-start.17 = (bf16[48,3072]{1,0:T(8,128)(2,1)S(1)}, bf16[48,3072]{1,0:T(8,128)(2,1)S(1)}, u32[]{:S(2)}, u32[]{:S(2)}) collective-permute-start(bf16[48,3072]{1,0:T(8,128)(2,1)S(1)} %add_convert_fusion.11), channel_id=1, source_target_pairs={{0,2},{2,4},{4,6},{6,7},{7,5},{5,3},{3,1},{1,0},{8,10},{10,12},{12... | collective-permute-start | bytes 884744 | tf_op jit(solution)/shard_map/ppermute | solution.py:146
  70.2 38.6 %copy-start.1 = (bf16[64,6144]{1,0:T(8,128)(2,1)S(1)}, bf16[64,6144]{1,0:T(8,128)(2,1)}, u32[]{:S(2)}) copy-start(bf16[64,6144]{1,0:T(8,128)(2,1)} %param.6) | copy-start | bytes 2359300
  70.3 10.0 %collective-permute-start.18 = (bf16[48,3072]{1,0:T(8,128)(2,1)S(1)}, bf16[48,3072]{1,0:T(8,128)(2,1)S(1)}, u32[]{:S(2)}, u32[]{:S(2)}) collective-permute-start(bf16[48,3072]{1,0:T(8,128)(2,1)S(1)} %add_convert_fusion.10), channel_id=1, source_target_pairs={{2,0},{4,2},{6,4},{7,6},{5,7},{3,5},{1,3},{0,1},{10,8},{12,10},{14... | collective-permute-start | bytes 884744 | tf_op jit(solution)/shard_map/ppermute | solution.py:146
  74.0 12.6 %collective-permute-start.25 = (bf16[48,3072]{1,0:T(8,128)(2,1)S(1)}, bf16[48,3072]{1,0:T(8,128)(2,1)S(1)}, u32[]{:S(2)}, u32[]{:S(2)}) collective-permute-start(bf16[48,3072]{1,0:T(8,128)(2,1)S(1)} %add_convert_fusion.4), channel_id=1, source_target_pairs={{2,0},{4,2},{6,4},{7,6},{5,7},{3,5},{1,3},{0,1},{10,8},{12,10},{14... | collective-permute-start | bytes 884744 | tf_op jit(solution)/shard_map/ppermute | solution.py:146
  75.5 11.1 %collective-permute-start.24 = (bf16[48,3072]{1,0:T(8,128)(2,1)S(1)}, bf16[48,3072]{1,0:T(8,128)(2,1)S(1)}, u32[]{:S(2)}, u32[]{:S(2)}) collective-permute-start(bf16[48,3072]{1,0:T(8,128)(2,1)S(1)} %add_convert_fusion.5), channel_id=1, source_target_pairs={{0,2},{2,4},{4,6},{6,7},{7,5},{5,3},{3,1},{1,0},{8,10},{10,12},{12... | collective-permute-start | bytes 884744 | tf_op jit(solution)/shard_map/ppermute | solution.py:146
  80.4 12.6 %collective-permute-start.20 = (bf16[48,3072]{1,0:T(8,128)(2,1)S(1)}, bf16[48,3072]{1,0:T(8,128)(2,1)S(1)}, u32[]{:S(2)}, u32[]{:S(2)}) collective-permute-start(bf16[48,3072]{1,0:T(8,128)(2,1)S(1)} %add_convert_fusion.8), channel_id=1, source_target_pairs={{2,0},{4,2},{6,4},{7,6},{5,7},{3,5},{1,3},{0,1},{10,8},{12,10},{14... | collective-permute-start | bytes 884744 | tf_op jit(solution)/shard_map/ppermute | solution.py:146
  82.0 10.9 %collective-permute-start.19 = (bf16[48,3072]{1,0:T(8,128)(2,1)S(1)}, bf16[48,3072]{1,0:T(8,128)(2,1)S(1)}, u32[]{:S(2)}, u32[]{:S(2)}) collective-permute-start(bf16[48,3072]{1,0:T(8,128)(2,1)S(1)} %add_convert_fusion.9), channel_id=1, source_target_pairs={{0,2},{2,4},{4,6},{6,7},{7,5},{5,3},{3,1},{1,0},{8,10},{10,12},{12... | collective-permute-start | bytes 884744 | tf_op jit(solution)/shard_map/ppermute | solution.py:146
  86.7 10.7 %collective-permute-start.27 = (bf16[48,3072]{1,0:T(8,128)(2,1)S(1)}, bf16[48,3072]{1,0:T(8,128)(2,1)S(1)}, u32[]{:S(2)}, u32[]{:S(2)}) collective-permute-start(bf16[48,3072]{1,0:T(8,128)(2,1)S(1)} %add_convert_fusion.2), channel_id=1, source_target_pairs={{2,0},{4,2},{6,4},{7,6},{5,7},{3,5},{1,3},{0,1},{10,8},{12,10},{14... | collective-permute-start | bytes 884744 | tf_op jit(solution)/shard_map/ppermute | solution.py:146
  88.3 10.5 %collective-permute-start.26 = (bf16[48,3072]{1,0:T(8,128)(2,1)S(1)}, bf16[48,3072]{1,0:T(8,128)(2,1)S(1)}, u32[]{:S(2)}, u32[]{:S(2)}) collective-permute-start(bf16[48,3072]{1,0:T(8,128)(2,1)S(1)} %add_convert_fusion.3), channel_id=1, source_target_pairs={{0,2},{2,4},{4,6},{6,7},{7,5},{5,3},{3,1},{1,0},{8,10},{10,12},{12... | collective-permute-start | bytes 884744 | tf_op jit(solution)/shard_map/ppermute | solution.py:146
  93.0 10.2 %collective-permute-start.21 = (bf16[48,3072]{1,0:T(8,128)(2,1)S(1)}, bf16[48,3072]{1,0:T(8,128)(2,1)S(1)}, u32[]{:S(2)}, u32[]{:S(2)}) collective-permute-start(bf16[48,3072]{1,0:T(8,128)(2,1)S(1)} %add_convert_fusion.7), channel_id=1, source_target_pairs={{0,2},{2,4},{4,6},{6,7},{7,5},{5,3},{3,1},{1,0},{8,10},{10,12},{12... | collective-permute-start | bytes 884744 | tf_op jit(solution)/shard_map/ppermute | solution.py:244
  98.9 6.8 %collective-permute-start.28 = (bf16[48,3072]{1,0:T(8,128)(2,1)S(1)}, bf16[48,3072]{1,0:T(8,128)(2,1)S(1)}, u32[]{:S(2)}, u32[]{:S(2)}) collective-permute-start(bf16[48,3072]{1,0:T(8,128)(2,1)S(1)} %add_convert_fusion.1), channel_id=1, source_target_pairs={{2,0},{4,2},{6,4},{7,6},{5,7},{3,5},{1,3},{0,1},{10,8},{12,10},{14... | collective-permute-start | bytes 884744 | tf_op jit(solution)/shard_map/ppermute | solution.py:245
  105.9 1.6 %collective-permute-start.29 = (bf16[24,6144]{1,0:T(8,128)(2,1)S(1)}, bf16[24,6144]{1,0:T(8,128)(2,1)S(1)}, u32[]{:S(2)}, u32[]{:S(2)}) collective-permute-start(bf16[24,6144]{1,0:T(8,128)(2,1)S(1)} %get-tuple-element.148), channel_id=1, source_target_pairs={{0,8},{8,0},{1,9},{9,1},{2,10},{10,2},{3,11},{11,3},{4,12},{12,4},... | collective-permute-start | bytes 884744 | tf_op jit(solution)/shard_map/ppermute | solution.py:251

commit v17 on v16

--- a/solution.py
+++ b/solution.py
@@ -17,25 +17,21 @@
     return list(range(0, count, 2)) + list(range(count - 1, 0, -2))
 
 
-def in_vmem(array):
-    return pltpu.with_memory_space_constraint(array, pltpu.VMEM)
-
-
-def in_hbm(array):
-    return pltpu.with_memory_space_constraint(array, pltpu.HBM)
+def placed(array, memory):
+    return array if memory in (pltpu.SMEM, None) else pltpu.with_memory_space_constraint(array, memory)
 
 
 def call(kernel, name, operands, outs, scratch, room):
     return pl.pallas_call(
         kernel,
-        in_specs=[pl.BlockSpec(memory_space=memory) for _, memory in operands],
+        in_specs=[pl.BlockSpec(memory_space=memory or pltpu.VMEM) for _, memory in operands],
         out_specs=[pl.BlockSpec(memory_space=pltpu.VMEM)] * len(outs),
         out_shape=[pltpu.VMEM(*out) for out in outs],
         scratch_shapes=scratch,
         cost_estimate=CHEAP,
         compiler_params=pltpu.CompilerParams(vmem_limit_bytes=room + MARGIN),
         name=name,
-    )(*[in_vmem(array) if memory == pltpu.VMEM else in_hbm(array) for array, memory in operands])
+    )(*[placed(array, memory) for array, memory in operands])
 
 
 def row_copies(source, target, done, column=0):
@@ -120,14 +116,27 @@
     add_down(hidden[...], down, outs)
 
 
-def routing(expert_ids, gate_probs, experts, slots):
-    matches = expert_ids[:, :, None] == experts[None, None, :]
-    member = jnp.any(matches, axis=1).astype(jnp.int32)
-    weight = jnp.sum(jnp.where(matches, gate_probs[:, :, None], jnp.float32(0.0)), axis=1)
-    slot_index = jnp.cumsum(member, axis=0) - member
-    column = jnp.arange(slots)
-    dispatch_map = (member[None, :, :] == 1) & (slot_index[None, :, :] == column[:, None, None])
-    return (jnp.transpose(dispatch_map, (2, 0, 1)), weight)
+def dispatch_kernel(core, ids, probs, source, same, away, combine_0, combine_1, tokens, done):
+    copy = pltpu.make_async_copy(source, tokens, done)
+    copy.start()
+    count = tokens.shape[0]
+    slots = same.shape[0]
+    earlier = lax.broadcasted_iota(jnp.int32, (count, count), 0) < lax.broadcasted_iota(jnp.int32, (count, count), 1)
+    column = lax.broadcasted_iota(jnp.int32, (slots, count), 0)
+    maps = []
+    for expert, combine in ((core[0], combine_0), (1 - core[0], combine_1)):
+        matches = (ids[...] == expert).astype(jnp.float32)
+        member = jnp.max(matches, axis=0, keepdims=True)
+        weight = jnp.sum(matches * probs[...], axis=0, keepdims=True)
+        slot = jnp.dot(
+            jnp.broadcast_to(member, (8, count)), earlier.astype(jnp.float32), preferred_element_type=jnp.float32
+        )[:1].astype(jnp.int32)
+        chosen = jnp.where(column == slot, member, 0.0)
+        combine[...] = chosen * weight
+        maps.append(chosen.astype(jnp.bfloat16))
+    copy.wait()
+    for chosen, rows in zip(maps, (same, away)):
+        rows[...] = jnp.dot(chosen, tokens[...], preferred_element_type=jnp.float32).astype(jnp.bfloat16)
 
 
 def per_device(tokens, expert_ids, gate_probs, w_gate, w_up, w_down):
@@ -150,14 +159,14 @@
         return lax.optimization_barrier(values)
 
     me = lax.axis_index("expert")
-    experts = jnp.stack([me, 1 - me])
-    dispatch_map, weight = routing(expert_ids, gate_probs, experts, CAP)
-    outgoing = jnp.dot(
-        dispatch_map.astype(jnp.bfloat16).reshape(size, tokens.shape[0]),
-        tokens,
-        preferred_element_type=jnp.float32,
-    ).astype(jnp.bfloat16)
-    own = jnp.concatenate([outgoing[:CAP], lax.ppermute(outgoing[CAP:], "expert", swap)], axis=0)
+    core = jnp.reshape(me, (1,)).astype(jnp.int32)
+    same, away, *combine = call(
+        dispatch_kernel, "dispatch",
+        [(core, pltpu.SMEM), (expert_ids.T, None), (gate_probs.T, None), (tokens, pltpu.HBM)],
+        [((CAP, width), jnp.bfloat16)] * 2 + [((CAP, tokens.shape[0]), jnp.float32)] * 2,
+        [pltpu.VMEM(tokens.shape, jnp.bfloat16), pltpu.SemaphoreType.DMA], 3 * 2**20,
+    )
+    own = jnp.concatenate([same, lax.ppermute(away, "expert", swap)], axis=0)
 
     own, w_gate = tied(own, w_gate)
     halves = [own[:, :mid_col], own[:, mid_col:]]
@@ -249,8 +258,7 @@
     ]
     total = jnp.concatenate(totals, axis=1).astype(jnp.bfloat16)
     returned = jnp.stack([total[:CAP], lax.ppermute(total[CAP:], "expert", swap)])
-    combine = dispatch_map.astype(jnp.float32) * jnp.transpose(weight)[:, None, :]
-    mixed = jnp.einsum("wcr,wcd->rd", combine, returned.astype(jnp.float32))
+    mixed = jnp.einsum("wcr,wcd->rd", jnp.stack(combine), returned.astype(jnp.float32))
     return mixed.astype(jnp.bfloat16)
 
 

time: 109 us -> 110 us (level)
  Pallas kernels: 30.9 us -> 32.4 us
  other arithmetic: 2.18 us -> 1 us
    pallas_call x9 -> x10, Pallas kernels: 30.9 us -> 32.4 us  [call(): pl.pallas_call(kernel, in_specs=[pl.BlockSpec(memory_space=memory or pltp...]
    unnamed x8 -> x4, local copies, waits for them, and re-layouts: 0.02 us -> 1.36 us
where the time goes in v17:
time: 110 us
  waiting for transfers between devices  41.8 us (38%)
  Pallas kernels  32.4 us (29%)
  starting transfers between devices  31.8 us (29%)
  local copies, waits for them, and re-layouts  1.4 us (1%)
  matrix products  1.27 us (1%)
    pallas_call x10, Pallas kernels, call(): pl.pallas_call(kernel, in_specs=[pl.BlockSpec(memory_space=memory or pltp...  32.4 us
    ppermute x13, starting transfers between devices, step(): lax.ppermute(to_left, 'tensor', left)  21.6 us
    ppermute x13, waiting for transfers between devices, step(): lax.ppermute(to_right, 'tensor', right)  19.1 us
    ppermute x13, waiting for transfers between devices, step(): lax.ppermute(to_left, 'tensor', left)  14.9 us
    ppermute x13, starting transfers between devices, step(): lax.ppermute(to_right, 'tensor', right)  6.43 us
    ppermute x1, waiting for transfers between devices, per_device(): last_right = lax.ppermute(added(0, 1, 1, flows[0][0]), 'tensor', right)  2.67 us
    ppermute x1, waiting for transfers between devices, per_device(): last_left = lax.ppermute(added(1, 1, 0, flows[1][1]), 'tensor', left)  2.35 us
  transfers between devices with their start and end apart: 30, of which 19 were waited for; matrix products, arithmetic and copies ran while one was open for 1% of the time, Pallas kernels for 24%

profile of v17, /device:TPU:0, one launch (start us, length us, event | category | flops | bytes accessed | tf_op | source)
XLA Modules:
  0.0 109.9 jit_solution(13746718893232839065)
XLA Ops:
  0.0 0.7 copy-done
  0.7 0.7 copy-done.1
  1.4 1.5 %dispatch.1 = (bf16[24,6144]{1,0:T(8,128)(2,1)S(1)}, bf16[24,6144]{1,0:T(8,128)(2,1)S(1)}, f32[24,64]{1,0:T(8,128)S(1)}, f32[24,64]{1,0:T(8,128)S(1)}) custom-call(s32[1]{0:T(128)} %bitcast.core, s32[2,64]{1,0:T(2,128)S(1)} %bitcast.14, f32[2,64]{1,0:T(2,128)S(1)} %bitcast.15, bf16[64,6144]{1,0:T(8,128)(2,1)} %source.1), custom_call_target="tpu_custom_call" | custom-call | flops 1024 | bytes 1024 | tf_op jit(solution)/shard_map/dispatch/pallas_call | solution.py:25
  2.9 0.5 collective-permute-start
  3.4 1.2 %collective-permute-done = bf16[24,6144]{1,0:T(8,128)(2,1)S(1)} collective-permute-done((bf16[24,6144]{1,0:T(8,128)(2,1)S(1)}, bf16[24,6144]{1,0:T(8,128)(2,1)S(1)}, u32[]{:S(2)}, u32[]{:S(2)}) %collective-permute-start) | collective-permute-done | bytes 294944 | tf_op jit(solution)/shard_map/ppermute | solution.py:169
  4.7 2.9 %collective-permute-start.2 = (bf16[48,3072]{1,0:T(8,128)(2,1)S(1)}, bf16[48,3072]{1,0:T(8,128)(2,1)S(1)}, u32[]{:S(2)}, u32[]{:S(2)}) collective-permute-start(bf16[48,3072]{1,0:T(8,128)(2,1)S(1)} %get-tuple-element.157.refs_5_), channel_id=1, source_target_pairs={{2,0},{4,2},{6,4},{7,6},{5,7},{3,5},{1,3},{0,1},{10,8},{12,10},{14... | collective-permute-start | bytes 884744 | tf_op jit(solution)/shard_map/ppermute | solution.py:155
  7.6 0.1 collective-permute-start.1
  7.7 2.0 %collective-permute-start.3 = (bf16[48,3072]{1,0:T(8,128)(2,1)S(1)}, bf16[48,3072]{1,0:T(8,128)(2,1)S(1)}, u32[]{:S(2)}, u32[]{:S(2)}) collective-permute-start(bf16[48,3072]{1,0:T(8,128)(2,1)S(1)} %get-tuple-element.157.refs_5_), channel_id=1, source_target_pairs={{0,2},{2,4},{4,6},{6,7},{7,5},{5,3},{3,1},{1,0},{8,10},{10,12},{12... | collective-permute-start | bytes 884744 | tf_op jit(solution)/shard_map/ppermute | solution.py:155
  9.8 4.7 %fetched.3.refs_10_.refs_6_ = bf16[1,6144,1024]{2,1,0:T(8,128)(2,1)S(1)} custom-call(bf16[1,6144,1024]{2,1,0:T(8,128)(2,1)} %source.2), custom_call_target="tpu_custom_call" | custom-call | flops 1024 | bytes 1024 | tf_op jit(solution)/shard_map/fetched/pallas_call | solution.py:25
  14.5 1.0 collective-permute-done.2.refs_7_
  15.5 2.0 %collective-permute-done.1.refs_1_ = bf16[48,3072]{1,0:T(8,128)(2,1)S(1)} collective-permute-done((bf16[48,3072]{1,0:T(8,128)(2,1)S(1)}, bf16[48,3072]{1,0:T(8,128)(2,1)S(1)}, u32[]{:S(2)}, u32[]{:S(2)}) %collective-permute-start.1) | collective-permute-done | bytes 294944 | tf_op jit(solution)/shard_map/ppermute | solution.py:155
  17.5 0.1 collective-permute-start.5
  17.6 1.9 %collective-permute-start.6 = (bf16[48,3072]{1,0:T(8,128)(2,1)S(1)}, bf16[48,3072]{1,0:T(8,128)(2,1)S(1)}, u32[]{:S(2)}, u32[]{:S(2)}) collective-permute-start(bf16[48,3072]{1,0:T(8,128)(2,1)S(1)} %collective-permute-done.2.refs_7_), channel_id=1, source_target_pairs={{2,0},{4,2},{6,4},{7,6},{5,7},{3,5},{1,3},{0,1},{10,8},{12,10},{14... | collective-permute-start | bytes 884744 | tf_op jit(solution)/shard_map/ppermute | solution.py:155
  19.5 4.7 %fetched.4.refs_10_.refs_7_ = bf16[1,6144,1024]{2,1,0:T(8,128)(2,1)S(1)} custom-call(bf16[1,6144,1024]{2,1,0:T(8,128)(2,1)} %source.3), custom_call_target="tpu_custom_call" | custom-call | flops 1024 | bytes 1024 | tf_op jit(solution)/shard_map/fetched/pallas_call | solution.py:25
  24.3 1.6 %collective-permute-start.8 = (bf16[48,3072]{1,0:T(8,128)(2,1)S(1)}, bf16[48,3072]{1,0:T(8,128)(2,1)S(1)}, u32[]{:S(2)}, u32[]{:S(2)}) collective-permute-start(bf16[48,3072]{1,0:T(8,128)(2,1)S(1)} %collective-permute-done.4.refs_2_), channel_id=1, source_target_pairs={{2,0},{4,2},{6,4},{7,6},{5,7},{3,5},{1,3},{0,1},{10,8},{12,10},{14... | collective-permute-start | bytes 884744 | tf_op jit(solution)/shard_map/ppermute | solution.py:155
  25.9 0.4 collective-permute-start.7
  26.4 3.8 %collective-permute-done.5.refs_3_ = bf16[48,3072]{1,0:T(8,128)(2,1)S(1)} collective-permute-done((bf16[48,3072]{1,0:T(8,128)(2,1)S(1)}, bf16[48,3072]{1,0:T(8,128)(2,1)S(1)}, u32[]{:S(2)}, u32[]{:S(2)}) %collective-permute-start.5) | collective-permute-done | bytes 294944 | tf_op jit(solution)/shard_map/ppermute | solution.py:155
  30.2 0.1 collective-permute-start.9
  30.2 1.9 %collective-permute-start.10 = (bf16[48,3072]{1,0:T(8,128)(2,1)S(1)}, bf16[48,3072]{1,0:T(8,128)(2,1)S(1)}, u32[]{:S(2)}, u32[]{:S(2)}) collective-permute-start(bf16[48,3072]{1,0:T(8,128)(2,1)S(1)} %collective-permute-done.6.refs_9_), channel_id=1, source_target_pairs={{2,0},{4,2},{6,4},{7,6},{5,7},{3,5},{1,3},{0,1},{10,8},{12,10},{14... | collective-permute-start | bytes 884744 | tf_op jit(solution)/shard_map/ppermute | solution.py:155
  32.2 2.2 %collective-permute-done.8.refs_4_ = bf16[48,3072]{1,0:T(8,128)(2,1)S(1)} collective-permute-done((bf16[48,3072]{1,0:T(8,128)(2,1)S(1)}, bf16[48,3072]{1,0:T(8,128)(2,1)S(1)}, u32[]{:S(2)}, u32[]{:S(2)}) %collective-permute-start.8) | collective-permute-done | bytes 294944 | tf_op jit(solution)/shard_map/ppermute | solution.py:155
  34.4 2.0 %collective-permute-done.7.refs_8_ = bf16[48,3072]{1,0:T(8,128)(2,1)S(1)} collective-permute-done((bf16[48,3072]{1,0:T(8,128)(2,1)S(1)}, bf16[48,3072]{1,0:T(8,128)(2,1)S(1)}, u32[]{:S(2)}, u32[]{:S(2)}) %collective-permute-start.7) | collective-permute-done | bytes 294944 | tf_op jit(solution)/shard_map/ppermute | solution.py:155
  36.5 3.2 %near_gate.1.refs_11_ = f32[240,1024]{1,0:T(8,128)S(1)} custom-call(bf16[48,3072]{1,0:T(8,128)(2,1)S(1)} %get-tuple-element.158.refs_0_, bf16[48,3072]{1,0:T(8,128)(2,1)S(1)} %collective-permute-done.1.refs_1_, bf16[48,3072]{1,0:T(8,128)(2,1)S(1)} %collective-permute-done.4.refs_2_, bf16[48,3072]{1,0:T(8,128)(2,1)S(1)} %collective-permute-done.5.refs_3_, ...), custom_call_target="tpu_custom_call" | custom-call | flops 1024 | bytes 1024 | tf_op jit(solution)/shard_map/near_gate/pallas_call | solution.py:25
  39.7 0.1 collective-permute-start.11
  39.8 1.9 %collective-permute-start.12 = (bf16[48,3072]{1,0:T(8,128)(2,1)S(1)}, bf16[48,3072]{1,0:T(8,128)(2,1)S(1)}, u32[]{:S(2)}, u32[]{:S(2)}) collective-permute-start(bf16[48,3072]{1,0:T(8,128)(2,1)S(1)} %collective-permute-done.8.refs_4_), channel_id=1, source_target_pairs={{2,0},{4,2},{6,4},{7,6},{5,7},{3,5},{1,3},{0,1},{10,8},{12,10},{14... | collective-permute-start | bytes 884744 | tf_op jit(solution)/shard_map/ppermute | solution.py:155
  41.8 1.0 collective-permute-done.9.refs_0_
  42.8 0.1 collective-permute-start.13
  42.9 1.9 %collective-permute-start.14 = (bf16[48,3072]{1,0:T(8,128)(2,1)S(1)}, bf16[48,3072]{1,0:T(8,128)(2,1)S(1)}, u32[]{:S(2)}, u32[]{:S(2)}) collective-permute-start(bf16[48,3072]{1,0:T(8,128)(2,1)S(1)} %collective-permute-done.10.refs_4_), channel_id=1, source_target_pairs={{2,0},{4,2},{6,4},{7,6},{5,7},{3,5},{1,3},{0,1},{10,8},{12,10},{14... | collective-permute-start | bytes 884744 | tf_op jit(solution)/shard_map/ppermute | solution.py:155
  44.8 3.2 %near_up.1.hidden = bf16[240,1024]{1,0:T(8,128)(2,1)S(1)} custom-call(bf16[48,3072]{1,0:T(8,128)(2,1)S(1)} %get-tuple-element.158.refs_0_, bf16[48,3072]{1,0:T(8,128)(2,1)S(1)} %collective-permute-done.1.refs_1_, bf16[48,3072]{1,0:T(8,128)(2,1)S(1)} %collective-permute-done.4.refs_2_, bf16[48,3072]{1,0:T(8,128)(2,1)S(1)} %collective-permute-done.5.refs_3_, ...), custom_call_target="tpu_custom_call" | custom-call | flops 1024 | bytes 1024 | tf_op jit(solution)/shard_map/near_up/pallas_call | solution.py:25
  48.1 2.9 %fetched.5.refs_8_.down = bf16[1,1024,3072]{2,1,0:T(8,128)(2,1)S(1)} custom-call(bf16[1,1024,6144]{2,1,0:T(8,128)(2,1)} %w_down), custom_call_target="tpu_custom_call" | custom-call | flops 1024 | bytes 1024 | tf_op jit(solution)/shard_map/fetched/pallas_call | solution.py:25
  51.0 3.3 %collective-permute-done.13.refs_2_ = bf16[48,3072]{1,0:T(8,128)(2,1)S(1)} collective-permute-done((bf16[48,3072]{1,0:T(8,128)(2,1)S(1)}, bf16[48,3072]{1,0:T(8,128)(2,1)S(1)}, u32[]{:S(2)}, u32[]{:S(2)}) %collective-permute-start.13) | collective-permute-done | bytes 294944 | tf_op jit(solution)/shard_map/ppermute | solution.py:155
  54.3 4.8 %rest_first.1 = (bf16[48,3072]{1,0:T(8,128)(2,1)S(1)}, bf16[48,3072]{1,0:T(8,128)(2,1)S(1)}, bf16[48,3072]{1,0:T(8,128)(2,1)S(1)}, bf16[144,1024]{1,0:T(8,128)(2,1)S(1)}) custom-call(bf16[48,3072]{1,0:T(8,128)(2,1)S(1)} %collective-permute-done.9.refs_0_, bf16[48,3072]{1,0:T(8,128)(2,1)S(1)} %collective-permute-done.12.refs_1_, ...), custom_call_target="tpu_custom_call" | custom-call | flops 1024 | bytes 1024 | tf_op jit(solution)/shard_map/rest_first/pallas_call | solution.py:25
  59.1 0.5 collective-permute-start.15
  59.6 1.6 %collective-permute-start.16 = (bf16[48,3072]{1,0:T(8,128)(2,1)S(1)}, bf16[48,3072]{1,0:T(8,128)(2,1)S(1)}, u32[]{:S(2)}, u32[]{:S(2)}) collective-permute-start(bf16[48,3072]{1,0:T(8,128)(2,1)S(1)} %get-tuple-element.133), channel_id=1, source_target_pairs={{2,0},{4,2},{6,4},{7,6},{5,7},{3,5},{1,3},{0,1},{10,8},{12,10},{14... | collective-permute-start | bytes 884744 | tf_op jit(solution)/shard_map/ppermute | solution.py:155
  61.2 4.0 %rest_second.1 = (bf16[48,3072]{1,0:T(8,128)(2,1)S(1)}, bf16[48,3072]{1,0:T(8,128)(2,1)S(1)}, bf16[48,3072]{1,0:T(8,128)(2,1)S(1)}, bf16[1,1024,3072]{2,1,0:T(8,128)(2,1)S(1)}) custom-call(bf16[144,1024]{1,0:T(8,128)(2,1)S(1)} %get-tuple-element.124.hidden, bf16[1,1024,6144]{2,1,0:T(8,128)(2,1)} %w_down), custom_call_target="tpu_custom_call" | custom-call | flops 1024 | bytes 1024 | tf_op jit(solution)/shard_map/rest_second/pallas_call | solution.py:25
  65.2 0.5 collective-permute-start.22
  65.7 1.6 %collective-permute-start.23 = (bf16[48,3072]{1,0:T(8,128)(2,1)S(1)}, bf16[48,3072]{1,0:T(8,128)(2,1)S(1)}, u32[]{:S(2)}, u32[]{:S(2)}) collective-permute-start(bf16[48,3072]{1,0:T(8,128)(2,1)S(1)} %get-tuple-element.126), channel_id=1, source_target_pairs={{2,0},{4,2},{6,4},{7,6},{5,7},{3,5},{1,3},{0,1},{10,8},{12,10},{14... | collective-permute-start | bytes 884744 | tf_op jit(solution)/shard_map/ppermute | solution.py:155
  67.3 1.7 %near_down.2 = (bf16[48,3072]{1,0:T(8,128)(2,1)S(1)}, bf16[48,3072]{1,0:T(8,128)(2,1)S(1)}, bf16[48,3072]{1,0:T(8,128)(2,1)S(1)}, bf16[48,3072]{1,0:T(8,128)(2,1)S(1)}, bf16[48,3072]{1,0:T(8,128)(2,1)S(1)}) custom-call(bf16[240,1024]{1,0:T(8,128)(2,1)S(1)} %near_up.1.hidden, bf16[1,1024,3072]{2,1,0:T(8,128)(2,1)S(1)} %fetched.5.refs_8_.down), custom_call_target="tpu_custom_call" | custom-call | flops 1024 | bytes 1024 | tf_op jit(solution)/shard_map/near_down/pallas_call | solution.py:25
  69.0 1.7 %near_down.3 = (bf16[48,3072]{1,0:T(8,128)(2,1)S(1)}, bf16[48,3072]{1,0:T(8,128)(2,1)S(1)}, bf16[48,3072]{1,0:T(8,128)(2,1)S(1)}, bf16[48,3072]{1,0:T(8,128)(2,1)S(1)}, bf16[48,3072]{1,0:T(8,128)(2,1)S(1)}) custom-call(bf16[240,1024]{1,0:T(8,128)(2,1)S(1)} %near_up.1.hidden, bf16[1,1024,3072]{2,1,0:T(8,128)(2,1)S(1)} %get-tuple-element.142.down), custom_call_target="tpu_custom_call" | custom-call | flops 1024 | bytes 1024 | tf_op jit(solution)/shard_map/near_down/pallas_call | solution.py:25
  70.7 0.1 add_convert_fusion.11
  70.8 0.5 collective-permute-start.17
  71.4 1.6 %collective-permute-start.18 = (bf16[48,3072]{1,0:T(8,128)(2,1)S(1)}, bf16[48,3072]{1,0:T(8,128)(2,1)S(1)}, u32[]{:S(2)}, u32[]{:S(2)}) collective-permute-start(bf16[48,3072]{1,0:T(8,128)(2,1)S(1)} %add_convert_fusion.10), channel_id=1, source_target_pairs={{2,0},{4,2},{6,4},{7,6},{5,7},{3,5},{1,3},{0,1},{10,8},{12,10},{14... | collective-permute-start | bytes 884744 | tf_op jit(solution)/shard_map/ppermute | solution.py:155
  73.0 1.8 %collective-permute-done.22 = bf16[48,3072]{1,0:T(8,128)(2,1)S(1)} collective-permute-done((bf16[48,3072]{1,0:T(8,128)(2,1)S(1)}, bf16[48,3072]{1,0:T(8,128)(2,1)S(1)}, u32[]{:S(2)}, u32[]{:S(2)}) %collective-permute-start.22) | collective-permute-done | bytes 294944 | tf_op jit(solution)/shard_map/ppermute | solution.py:155
  74.7 0.4 collective-permute-done.23
  75.2 1.4 %collective-permute-start.25 = (bf16[48,3072]{1,0:T(8,128)(2,1)S(1)}, bf16[48,3072]{1,0:T(8,128)(2,1)S(1)}, u32[]{:S(2)}, u32[]{:S(2)}) collective-permute-start(bf16[48,3072]{1,0:T(8,128)(2,1)S(1)} %add_convert_fusion.4), channel_id=1, source_target_pairs={{2,0},{4,2},{6,4},{7,6},{5,7},{3,5},{1,3},{0,1},{10,8},{12,10},{14... | collective-permute-start | bytes 884744 | tf_op jit(solution)/shard_map/ppermute | solution.py:155
  76.7 0.7 collective-permute-start.24
  77.4 3.6 %collective-permute-done.17 = bf16[48,3072]{1,0:T(8,128)(2,1)S(1)} collective-permute-done((bf16[48,3072]{1,0:T(8,128)(2,1)S(1)}, bf16[48,3072]{1,0:T(8,128)(2,1)S(1)}, u32[]{:S(2)}, u32[]{:S(2)}) %collective-permute-start.17) | collective-permute-done | bytes 294944 | tf_op jit(solution)/shard_map/ppermute | solution.py:155
  81.0 0.4 collective-permute-done.18
  81.5 1.5 %collective-permute-start.20 = (bf16[48,3072]{1,0:T(8,128)(2,1)S(1)}, bf16[48,3072]{1,0:T(8,128)(2,1)S(1)}, u32[]{:S(2)}, u32[]{:S(2)}) collective-permute-start(bf16[48,3072]{1,0:T(8,128)(2,1)S(1)} %add_convert_fusion.8), channel_id=1, source_target_pairs={{2,0},{4,2},{6,4},{7,6},{5,7},{3,5},{1,3},{0,1},{10,8},{12,10},{14... | collective-permute-start | bytes 884744 | tf_op jit(solution)/shard_map/ppermute | solution.py:155
  83.0 0.1 add_convert_fusion.9
  83.1 0.6 collective-permute-start.19
  83.7 4.0 %collective-permute-done.25 = bf16[48,3072]{1,0:T(8,128)(2,1)S(1)} collective-permute-done((bf16[48,3072]{1,0:T(8,128)(2,1)S(1)}, bf16[48,3072]{1,0:T(8,128)(2,1)S(1)}, u32[]{:S(2)}, u32[]{:S(2)}) %collective-permute-start.25) | collective-permute-done | bytes 294944 | tf_op jit(solution)/shard_map/ppermute | solution.py:155
  87.8 1.5 %collective-permute-start.27 = (bf16[48,3072]{1,0:T(8,128)(2,1)S(1)}, bf16[48,3072]{1,0:T(8,128)(2,1)S(1)}, u32[]{:S(2)}, u32[]{:S(2)}) collective-permute-start(bf16[48,3072]{1,0:T(8,128)(2,1)S(1)} %add_convert_fusion.2), channel_id=1, source_target_pairs={{2,0},{4,2},{6,4},{7,6},{5,7},{3,5},{1,3},{0,1},{10,8},{12,10},{14... | collective-permute-start | bytes 884744 | tf_op jit(solution)/shard_map/ppermute | solution.py:155
  89.4 0.6 collective-permute-start.26
  90.1 4.0 %collective-permute-done.20 = bf16[48,3072]{1,0:T(8,128)(2,1)S(1)} collective-permute-done((bf16[48,3072]{1,0:T(8,128)(2,1)S(1)}, bf16[48,3072]{1,0:T(8,128)(2,1)S(1)}, u32[]{:S(2)}, u32[]{:S(2)}) %collective-permute-start.20) | collective-permute-done | bytes 294944 | tf_op jit(solution)/shard_map/ppermute | solution.py:155
  94.2 1.6 %collective-permute-start.21 = (bf16[48,3072]{1,0:T(8,128)(2,1)S(1)}, bf16[48,3072]{1,0:T(8,128)(2,1)S(1)}, u32[]{:S(2)}, u32[]{:S(2)}) collective-permute-start(bf16[48,3072]{1,0:T(8,128)(2,1)S(1)} %add_convert_fusion.7), channel_id=1, source_target_pairs={{0,2},{2,4},{4,6},{6,7},{7,5},{5,3},{3,1},{1,0},{8,10},{10,12},{12... | collective-permute-start | bytes 884744 | tf_op jit(solution)/shard_map/ppermute | solution.py:253
  95.7 2.8 %collective-permute-done.27 = bf16[48,3072]{1,0:T(8,128)(2,1)S(1)} collective-permute-done((bf16[48,3072]{1,0:T(8,128)(2,1)S(1)}, bf16[48,3072]{1,0:T(8,128)(2,1)S(1)}, u32[]{:S(2)}, u32[]{:S(2)}) %collective-permute-start.27) | collective-permute-done | bytes 294944 | tf_op jit(solution)/shard_map/ppermute | solution.py:155
  98.5 1.5 %collective-permute-done.26 = bf16[48,3072]{1,0:T(8,128)(2,1)S(1)} collective-permute-done((bf16[48,3072]{1,0:T(8,128)(2,1)S(1)}, bf16[48,3072]{1,0:T(8,128)(2,1)S(1)}, u32[]{:S(2)}, u32[]{:S(2)}) %collective-permute-start.26) | collective-permute-done | bytes 294944 | tf_op jit(solution)/shard_map/ppermute | solution.py:155
  100.1 1.6 %collective-permute-start.28 = (bf16[48,3072]{1,0:T(8,128)(2,1)S(1)}, bf16[48,3072]{1,0:T(8,128)(2,1)S(1)}, u32[]{:S(2)}, u32[]{:S(2)}) collective-permute-start(bf16[48,3072]{1,0:T(8,128)(2,1)S(1)} %add_convert_fusion.1), channel_id=1, source_target_pairs={{2,0},{4,2},{6,4},{7,6},{5,7},{3,5},{1,3},{0,1},{10,8},{12,10},{14... | collective-permute-start | bytes 884744 | tf_op jit(solution)/shard_map/ppermute | solution.py:254
  101.7 2.7 %collective-permute-done.21 = bf16[48,3072]{1,0:T(8,128)(2,1)S(1)} collective-permute-done((bf16[48,3072]{1,0:T(8,128)(2,1)S(1)}, bf16[48,3072]{1,0:T(8,128)(2,1)S(1)}, u32[]{:S(2)}, u32[]{:S(2)}) %collective-permute-start.21) | collective-permute-done | bytes 294944 | tf_op jit(solution)/shard_map/ppermute | solution.py:253
  104.4 0.1 add_convert_fusion.6
  104.5 2.3 %collective-permute-done.28 = bf16[48,3072]{1,0:T(8,128)(2,1)S(1)} collective-permute-done((bf16[48,3072]{1,0:T(8,128)(2,1)S(1)}, bf16[48,3072]{1,0:T(8,128)(2,1)S(1)}, u32[]{:S(2)}, u32[]{:S(2)}) %collective-permute-start.28) | collective-permute-done | bytes 294944 | tf_op jit(solution)/shard_map/ppermute | solution.py:254
  106.9 0.1 add_convert_fusion
  107.1 1.6 %collective-permute-done.29 = bf16[24,6144]{1,0:T(8,128)(2,1)S(1)} collective-permute-done((bf16[24,6144]{1,0:T(8,128)(2,1)S(1)}, bf16[24,6144]{1,0:T(8,128)(2,1)S(1)}, u32[]{:S(2)}, u32[]{:S(2)}) %collective-permute-start.29) | collective-permute-done | bytes 294944 | tf_op jit(solution)/shard_map/ppermute | solution.py:260
  108.7 1.3 %fusion = bf16[64,6144]{1,0:T(8,128)(2,1)} fusion(bf16[1,24,6144]{2,1,0:T(8,128)(2,1)S(1)} %bitcast.16, bf16[1,24,6144]{2,1,0:T(8,128)(2,1)S(1)} %get-tuple-element.155, f32[1,24,64]{2,1,0:T(8,128)S(1)} %bitcast.13, f32[1,24,64]{2,1,0:T(8,128)S(1)} %bitcast.12), kind=kOutput, calls=%fused_computation.1 | convolution fusion | flops 38046720 | bytes 1388544 | tf_op jit(solution)/shard_map/wcr,wcd->rd/dot_general | solution.py:261
  (26 shorter events, 0.8 us)
Async XLA Ops:
  0.0 0.7 copy-start
  0.7 0.7 copy-start.1
  2.9 1.7 %collective-permute-start = (bf16[24,6144]{1,0:T(8,128)(2,1)S(1)}, bf16[24,6144]{1,0:T(8,128)(2,1)S(1)}, u32[]{:S(2)}, u32[]{:S(2)}) collective-permute-start(bf16[24,6144]{1,0:T(8,128)(2,1)S(1)} %get-tuple-element.83), channel_id=1, source_target_pairs={{0,8},{8,0},{1,9},{9,1},{2,10},{10,2},{3,11},{11,3},{4,12},{12,4},... | collective-permute-start | bytes 884744 | tf_op jit(solution)/shard_map/ppermute | solution.py:169
  4.7 10.8 %collective-permute-start.2 = (bf16[48,3072]{1,0:T(8,128)(2,1)S(1)}, bf16[48,3072]{1,0:T(8,128)(2,1)S(1)}, u32[]{:S(2)}, u32[]{:S(2)}) collective-permute-start(bf16[48,3072]{1,0:T(8,128)(2,1)S(1)} %get-tuple-element.157.refs_5_), channel_id=1, source_target_pairs={{2,0},{4,2},{6,4},{7,6},{5,7},{3,5},{1,3},{0,1},{10,8},{12,10},{14... | collective-permute-start | bytes 884744 | tf_op jit(solution)/shard_map/ppermute | solution.py:155
  7.6 9.9 %collective-permute-start.1 = (bf16[48,3072]{1,0:T(8,128)(2,1)S(1)}, bf16[48,3072]{1,0:T(8,128)(2,1)S(1)}, u32[]{:S(2)}, u32[]{:S(2)}) collective-permute-start(bf16[48,3072]{1,0:T(8,128)(2,1)S(1)} %get-tuple-element.158.refs_0_), channel_id=1, source_target_pairs={{0,2},{2,4},{4,6},{6,7},{7,5},{5,3},{3,1},{1,0},{8,10},{10,12},{12... | collective-permute-start | bytes 884744 | tf_op jit(solution)/shard_map/ppermute | solution.py:155
  7.7 16.5 %collective-permute-start.3 = (bf16[48,3072]{1,0:T(8,128)(2,1)S(1)}, bf16[48,3072]{1,0:T(8,128)(2,1)S(1)}, u32[]{:S(2)}, u32[]{:S(2)}) collective-permute-start(bf16[48,3072]{1,0:T(8,128)(2,1)S(1)} %get-tuple-element.157.refs_5_), channel_id=1, source_target_pairs={{0,2},{2,4},{4,6},{6,7},{7,5},{5,3},{3,1},{1,0},{8,10},{10,12},{12... | collective-permute-start | bytes 884744 | tf_op jit(solution)/shard_map/ppermute | solution.py:155
  9.7 14.6 %collective-permute-start.4 = (bf16[48,3072]{1,0:T(8,128)(2,1)S(1)}, bf16[48,3072]{1,0:T(8,128)(2,1)S(1)}, u32[]{:S(2)}, u32[]{:S(2)}) collective-permute-start(bf16[48,3072]{1,0:T(8,128)(2,1)S(1)} %get-tuple-element.158.refs_0_), channel_id=1, source_target_pairs={{2,0},{4,2},{6,4},{7,6},{5,7},{3,5},{1,3},{0,1},{10,8},{12,10},{14... | collective-permute-start | bytes 884744 | tf_op jit(solution)/shard_map/ppermute | solution.py:155
  17.5 12.6 %collective-permute-start.5 = (bf16[48,3072]{1,0:T(8,128)(2,1)S(1)}, bf16[48,3072]{1,0:T(8,128)(2,1)S(1)}, u32[]{:S(2)}, u32[]{:S(2)}) collective-permute-start(bf16[48,3072]{1,0:T(8,128)(2,1)S(1)} %collective-permute-done.1.refs_1_), channel_id=1, source_target_pairs={{0,2},{2,4},{4,6},{6,7},{7,5},{5,3},{3,1},{1,0},{8,10},{10,12},{12... | collective-permute-start | bytes 884744 | tf_op jit(solution)/shard_map/ppermute | solution.py:155
  17.6 12.6 %collective-permute-start.6 = (bf16[48,3072]{1,0:T(8,128)(2,1)S(1)}, bf16[48,3072]{1,0:T(8,128)(2,1)S(1)}, u32[]{:S(2)}, u32[]{:S(2)}) collective-permute-start(bf16[48,3072]{1,0:T(8,128)(2,1)S(1)} %collective-permute-done.2.refs_7_), channel_id=1, source_target_pairs={{2,0},{4,2},{6,4},{7,6},{5,7},{3,5},{1,3},{0,1},{10,8},{12,10},{14... | collective-permute-start | bytes 884744 | tf_op jit(solution)/shard_map/ppermute | solution.py:155
  24.3 10.1 %collective-permute-start.8 = (bf16[48,3072]{1,0:T(8,128)(2,1)S(1)}, bf16[48,3072]{1,0:T(8,128)(2,1)S(1)}, u32[]{:S(2)}, u32[]{:S(2)}) collective-permute-start(bf16[48,3072]{1,0:T(8,128)(2,1)S(1)} %collective-permute-done.4.refs_2_), channel_id=1, source_target_pairs={{2,0},{4,2},{6,4},{7,6},{5,7},{3,5},{1,3},{0,1},{10,8},{12,10},{14... | collective-permute-start | bytes 884744 | tf_op jit(solution)/shard_map/ppermute | solution.py:155
  25.9 10.6 %collective-permute-start.7 = (bf16[48,3072]{1,0:T(8,128)(2,1)S(1)}, bf16[48,3072]{1,0:T(8,128)(2,1)S(1)}, u32[]{:S(2)}, u32[]{:S(2)}) collective-permute-start(bf16[48,3072]{1,0:T(8,128)(2,1)S(1)} %collective-permute-done.3.refs_6_), channel_id=1, source_target_pairs={{0,2},{2,4},{4,6},{6,7},{7,5},{5,3},{3,1},{1,0},{8,10},{10,12},{12... | collective-permute-start | bytes 884744 | tf_op jit(solution)/shard_map/ppermute | solution.py:155
  30.2 12.6 %collective-permute-start.9 = (bf16[48,3072]{1,0:T(8,128)(2,1)S(1)}, bf16[48,3072]{1,0:T(8,128)(2,1)S(1)}, u32[]{:S(2)}, u32[]{:S(2)}) collective-permute-start(bf16[48,3072]{1,0:T(8,128)(2,1)S(1)} %collective-permute-done.5.refs_3_), channel_id=1, source_target_pairs={{0,2},{2,4},{4,6},{6,7},{7,5},{5,3},{3,1},{1,0},{8,10},{10,12},{12... | collective-permute-start | bytes 884744 | tf_op jit(solution)/shard_map/ppermute | solution.py:155
  30.2 12.6 %collective-permute-start.10 = (bf16[48,3072]{1,0:T(8,128)(2,1)S(1)}, bf16[48,3072]{1,0:T(8,128)(2,1)S(1)}, u32[]{:S(2)}, u32[]{:S(2)}) collective-permute-start(bf16[48,3072]{1,0:T(8,128)(2,1)S(1)} %collective-permute-done.6.refs_9_), channel_id=1, source_target_pairs={{2,0},{4,2},{6,4},{7,6},{5,7},{3,5},{1,3},{0,1},{10,8},{12,10},{14... | collective-permute-start | bytes 884744 | tf_op jit(solution)/shard_map/ppermute | solution.py:155
  39.7 11.3 %collective-permute-start.11 = (bf16[48,3072]{1,0:T(8,128)(2,1)S(1)}, bf16[48,3072]{1,0:T(8,128)(2,1)S(1)}, u32[]{:S(2)}, u32[]{:S(2)}) collective-permute-start(bf16[48,3072]{1,0:T(8,128)(2,1)S(1)} %collective-permute-done.7.refs_8_), channel_id=1, source_target_pairs={{0,2},{2,4},{4,6},{6,7},{7,5},{5,3},{3,1},{1,0},{8,10},{10,12},{12... | collective-permute-start | bytes 884744 | tf_op jit(solution)/shard_map/ppermute | solution.py:155
  39.8 11.2 %collective-permute-start.12 = (bf16[48,3072]{1,0:T(8,128)(2,1)S(1)}, bf16[48,3072]{1,0:T(8,128)(2,1)S(1)}, u32[]{:S(2)}, u32[]{:S(2)}) collective-permute-start(bf16[48,3072]{1,0:T(8,128)(2,1)S(1)} %collective-permute-done.8.refs_4_), channel_id=1, source_target_pairs={{2,0},{4,2},{6,4},{7,6},{5,7},{3,5},{1,3},{0,1},{10,8},{12,10},{14... | collective-permute-start | bytes 884744 | tf_op jit(solution)/shard_map/ppermute | solution.py:155
  42.8 11.5 %collective-permute-start.13 = (bf16[48,3072]{1,0:T(8,128)(2,1)S(1)}, bf16[48,3072]{1,0:T(8,128)(2,1)S(1)}, u32[]{:S(2)}, u32[]{:S(2)}) collective-permute-start(bf16[48,3072]{1,0:T(8,128)(2,1)S(1)} %collective-permute-done.9.refs_0_), channel_id=1, source_target_pairs={{0,2},{2,4},{4,6},{6,7},{7,5},{5,3},{3,1},{1,0},{8,10},{10,12},{12... | collective-permute-start | bytes 884744 | tf_op jit(solution)/shard_map/ppermute | solution.py:155
  42.9 11.4 %collective-permute-start.14 = (bf16[48,3072]{1,0:T(8,128)(2,1)S(1)}, bf16[48,3072]{1,0:T(8,128)(2,1)S(1)}, u32[]{:S(2)}, u32[]{:S(2)}) collective-permute-start(bf16[48,3072]{1,0:T(8,128)(2,1)S(1)} %collective-permute-done.10.refs_4_), channel_id=1, source_target_pairs={{2,0},{4,2},{6,4},{7,6},{5,7},{3,5},{1,3},{0,1},{10,8},{12,10},{14... | collective-permute-start | bytes 884744 | tf_op jit(solution)/shard_map/ppermute | solution.py:155
  59.1 11.6 %collective-permute-start.15 = (bf16[48,3072]{1,0:T(8,128)(2,1)S(1)}, bf16[48,3072]{1,0:T(8,128)(2,1)S(1)}, u32[]{:S(2)}, u32[]{:S(2)}) collective-permute-start(bf16[48,3072]{1,0:T(8,128)(2,1)S(1)} %get-tuple-element.132), channel_id=1, source_target_pairs={{0,2},{2,4},{4,6},{6,7},{7,5},{5,3},{3,1},{1,0},{8,10},{10,12},{12... | collective-permute-start | bytes 884744 | tf_op jit(solution)/shard_map/ppermute | solution.py:155
  59.6 11.1 %collective-permute-start.16 = (bf16[48,3072]{1,0:T(8,128)(2,1)S(1)}, bf16[48,3072]{1,0:T(8,128)(2,1)S(1)}, u32[]{:S(2)}, u32[]{:S(2)}) collective-permute-start(bf16[48,3072]{1,0:T(8,128)(2,1)S(1)} %get-tuple-element.133), channel_id=1, source_target_pairs={{2,0},{4,2},{6,4},{7,6},{5,7},{3,5},{1,3},{0,1},{10,8},{12,10},{14... | collective-permute-start | bytes 884744 | tf_op jit(solution)/shard_map/ppermute | solution.py:155
  65.2 9.5 %collective-permute-start.22 = (bf16[48,3072]{1,0:T(8,128)(2,1)S(1)}, bf16[48,3072]{1,0:T(8,128)(2,1)S(1)}, u32[]{:S(2)}, u32[]{:S(2)}) collective-permute-start(bf16[48,3072]{1,0:T(8,128)(2,1)S(1)} %get-tuple-element.125), channel_id=1, source_target_pairs={{0,2},{2,4},{4,6},{6,7},{7,5},{5,3},{3,1},{1,0},{8,10},{10,12},{12... | collective-permute-start | bytes 884744 | tf_op jit(solution)/shard_map/ppermute | solution.py:155
  65.7 9.4 %collective-permute-start.23 = (bf16[48,3072]{1,0:T(8,128)(2,1)S(1)}, bf16[48,3072]{1,0:T(8,128)(2,1)S(1)}, u32[]{:S(2)}, u32[]{:S(2)}) collective-permute-start(bf16[48,3072]{1,0:T(8,128)(2,1)S(1)} %get-tuple-element.126), channel_id=1, source_target_pairs={{2,0},{4,2},{6,4},{7,6},{5,7},{3,5},{1,3},{0,1},{10,8},{12,10},{14... | collective-permute-start | bytes 884744 | tf_op jit(solution)/shard_map/ppermute | solution.py:155
  70.8 10.3 %collective-permute-start.17 = (bf16[48,3072]{1,0:T(8,128)(2,1)S(1)}, bf16[48,3072]{1,0:T(8,128)(2,1)S(1)}, u32[]{:S(2)}, u32[]{:S(2)}) collective-permute-start(bf16[48,3072]{1,0:T(8,128)(2,1)S(1)} %add_convert_fusion.11), channel_id=1, source_target_pairs={{0,2},{2,4},{4,6},{6,7},{7,5},{5,3},{3,1},{1,0},{8,10},{10,12},{12... | collective-permute-start | bytes 884744 | tf_op jit(solution)/shard_map/ppermute | solution.py:155
  71.4 10.1 %collective-permute-start.18 = (bf16[48,3072]{1,0:T(8,128)(2,1)S(1)}, bf16[48,3072]{1,0:T(8,128)(2,1)S(1)}, u32[]{:S(2)}, u32[]{:S(2)}) collective-permute-start(bf16[48,3072]{1,0:T(8,128)(2,1)S(1)} %add_convert_fusion.10), channel_id=1, source_target_pairs={{2,0},{4,2},{6,4},{7,6},{5,7},{3,5},{1,3},{0,1},{10,8},{12,10},{14... | collective-permute-start | bytes 884744 | tf_op jit(solution)/shard_map/ppermute | solution.py:155
  75.2 12.6 %collective-permute-start.25 = (bf16[48,3072]{1,0:T(8,128)(2,1)S(1)}, bf16[48,3072]{1,0:T(8,128)(2,1)S(1)}, u32[]{:S(2)}, u32[]{:S(2)}) collective-permute-start(bf16[48,3072]{1,0:T(8,128)(2,1)S(1)} %add_convert_fusion.4), channel_id=1, source_target_pairs={{2,0},{4,2},{6,4},{7,6},{5,7},{3,5},{1,3},{0,1},{10,8},{12,10},{14... | collective-permute-start | bytes 884744 | tf_op jit(solution)/shard_map/ppermute | solution.py:155
  76.7 11.1 %collective-permute-start.24 = (bf16[48,3072]{1,0:T(8,128)(2,1)S(1)}, bf16[48,3072]{1,0:T(8,128)(2,1)S(1)}, u32[]{:S(2)}, u32[]{:S(2)}) collective-permute-start(bf16[48,3072]{1,0:T(8,128)(2,1)S(1)} %add_convert_fusion.5), channel_id=1, source_target_pairs={{0,2},{2,4},{4,6},{6,7},{7,5},{5,3},{3,1},{1,0},{8,10},{10,12},{12... | collective-permute-start | bytes 884744 | tf_op jit(solution)/shard_map/ppermute | solution.py:155
  81.5 12.6 %collective-permute-start.20 = (bf16[48,3072]{1,0:T(8,128)(2,1)S(1)}, bf16[48,3072]{1,0:T(8,128)(2,1)S(1)}, u32[]{:S(2)}, u32[]{:S(2)}) collective-permute-start(bf16[48,3072]{1,0:T(8,128)(2,1)S(1)} %add_convert_fusion.8), channel_id=1, source_target_pairs={{2,0},{4,2},{6,4},{7,6},{5,7},{3,5},{1,3},{0,1},{10,8},{12,10},{14... | collective-permute-start | bytes 884744 | tf_op jit(solution)/shard_map/ppermute | solution.py:155
  83.1 11.0 %collective-permute-start.19 = (bf16[48,3072]{1,0:T(8,128)(2,1)S(1)}, bf16[48,3072]{1,0:T(8,128)(2,1)S(1)}, u32[]{:S(2)}, u32[]{:S(2)}) collective-permute-start(bf16[48,3072]{1,0:T(8,128)(2,1)S(1)} %add_convert_fusion.9), channel_id=1, source_target_pairs={{0,2},{2,4},{4,6},{6,7},{7,5},{5,3},{3,1},{1,0},{8,10},{10,12},{12... | collective-permute-start | bytes 884744 | tf_op jit(solution)/shard_map/ppermute | solution.py:155
  87.8 10.7 %collective-permute-start.27 = (bf16[48,3072]{1,0:T(8,128)(2,1)S(1)}, bf16[48,3072]{1,0:T(8,128)(2,1)S(1)}, u32[]{:S(2)}, u32[]{:S(2)}) collective-permute-start(bf16[48,3072]{1,0:T(8,128)(2,1)S(1)} %add_convert_fusion.2), channel_id=1, source_target_pairs={{2,0},{4,2},{6,4},{7,6},{5,7},{3,5},{1,3},{0,1},{10,8},{12,10},{14... | collective-permute-start | bytes 884744 | tf_op jit(solution)/shard_map/ppermute | solution.py:155
  89.4 10.6 %collective-permute-start.26 = (bf16[48,3072]{1,0:T(8,128)(2,1)S(1)}, bf16[48,3072]{1,0:T(8,128)(2,1)S(1)}, u32[]{:S(2)}, u32[]{:S(2)}) collective-permute-start(bf16[48,3072]{1,0:T(8,128)(2,1)S(1)} %add_convert_fusion.3), channel_id=1, source_target_pairs={{0,2},{2,4},{4,6},{6,7},{7,5},{5,3},{3,1},{1,0},{8,10},{10,12},{12... | collective-permute-start | bytes 884744 | tf_op jit(solution)/shard_map/ppermute | solution.py:155
  94.2 10.2 %collective-permute-start.21 = (bf16[48,3072]{1,0:T(8,128)(2,1)S(1)}, bf16[48,3072]{1,0:T(8,128)(2,1)S(1)}, u32[]{:S(2)}, u32[]{:S(2)}) collective-permute-start(bf16[48,3072]{1,0:T(8,128)(2,1)S(1)} %add_convert_fusion.7), channel_id=1, source_target_pairs={{0,2},{2,4},{4,6},{6,7},{7,5},{5,3},{3,1},{1,0},{8,10},{10,12},{12... | collective-permute-start | bytes 884744 | tf_op jit(solution)/shard_map/ppermute | solution.py:253
  100.1 6.8 %collective-permute-start.28 = (bf16[48,3072]{1,0:T(8,128)(2,1)S(1)}, bf16[48,3072]{1,0:T(8,128)(2,1)S(1)}, u32[]{:S(2)}, u32[]{:S(2)}) collective-permute-start(bf16[48,3072]{1,0:T(8,128)(2,1)S(1)} %add_convert_fusion.1), channel_id=1, source_target_pairs={{2,0},{4,2},{6,4},{7,6},{5,7},{3,5},{1,3},{0,1},{10,8},{12,10},{14... | collective-permute-start | bytes 884744 | tf_op jit(solution)/shard_map/ppermute | solution.py:254
  107.0 1.6 %collective-permute-start.29 = (bf16[24,6144]{1,0:T(8,128)(2,1)S(1)}, bf16[24,6144]{1,0:T(8,128)(2,1)S(1)}, u32[]{:S(2)}, u32[]{:S(2)}) collective-permute-start(bf16[24,6144]{1,0:T(8,128)(2,1)S(1)} %get-tuple-element.156), channel_id=1, source_target_pairs={{0,8},{8,0},{1,9},{9,1},{2,10},{10,2},{3,11},{11,3},{4,12},{12,4},... | collective-permute-start | bytes 884744 | tf_op jit(solution)/shard_map/ppermute | solution.py:260

commit v18 on v16

--- a/solution.py
+++ b/solution.py
@@ -118,6 +118,30 @@
 
 def near_down_kernel(hidden, down, *outs):
     add_down(hidden[...], down, outs)
+
+
+def combine_kernel(weights, kept, swapped, *refs):
+    out = refs[-1]
+    part = jnp.dot(weights[0], kept[...], preferred_element_type=jnp.float32)
+    part += jnp.dot(weights[1], swapped[...], preferred_element_type=jnp.float32)
+    out[...] = part.astype(out.dtype)
+
+
+def combined(chunk, width, weights, kept, swapped, result=None):
+    rows, columns = weights.shape[1], kept.shape[1]
+    operands = [weights, kept, swapped] + ([] if result is None else [result])
+    in_specs = [pl.BlockSpec(memory_space=pltpu.VMEM)] * 3 + [pl.BlockSpec(memory_space=pl.ANY)] * (len(operands) - 3)
+    return pl.pallas_call(
+        combine_kernel,
+        grid=(1,),
+        in_specs=in_specs,
+        out_specs=pl.BlockSpec((rows, columns), lambda i: (0, chunk)),
+        out_shape=jax.ShapeDtypeStruct((rows, width), jnp.bfloat16),
+        input_output_aliases={} if result is None else {3: 0},
+        cost_estimate=CHEAP,
+        compiler_params=pltpu.CompilerParams(vmem_limit_bytes=8 * 2**20),
+        name="combined",
+    )(*operands)
 
 
 def routing(expert_ids, gate_probs, experts, slots):
@@ -243,15 +267,18 @@
             flows[chunk] = step(to_right, to_left)
     last_right = lax.ppermute(added(0, 1, 1, flows[0][0]), "tensor", right)
     last_left = lax.ppermute(added(1, 1, 0, flows[1][1]), "tensor", left)
-    totals = [
-        part_of(0, 0, 0) + last_right.astype(jnp.float32) + flows[0][1].astype(jnp.float32),
-        part_of(1, 0, 0) + flows[1][0].astype(jnp.float32) + last_left.astype(jnp.float32),
-    ]
-    total = jnp.concatenate(totals, axis=1).astype(jnp.bfloat16)
-    returned = jnp.stack([total[:CAP], lax.ppermute(total[CAP:], "expert", swap)])
     combine = dispatch_map.astype(jnp.float32) * jnp.transpose(weight)[:, None, :]
-    mixed = jnp.einsum("wcr,wcd->rd", combine, returned.astype(jnp.float32))
-    return mixed.astype(jnp.bfloat16)
+    combine = jnp.transpose(combine, (0, 2, 1)).astype(jnp.bfloat16)
+    pairs = [(last_right, flows[0][1]), (flows[1][0], last_left)]
+    mixed = None
+    for chunk, (from_left, from_right) in enumerate(pairs):
+        if chunk:
+            from_right, mixed = tied(from_right, mixed)
+        total = part_of(chunk, 0, 0) + from_left.astype(jnp.float32) + from_right.astype(jnp.float32)
+        total = total.astype(jnp.bfloat16)
+        swapped = lax.ppermute(total[CAP:], "expert", swap)
+        mixed = combined(chunk, width, combine, total[:CAP], swapped, mixed)
+    return mixed
 
 
 def solution(mesh):

time: 109 us -> 109 us (level)
  Pallas kernels: 30.9 us -> 33.1 us
  matrix products: 1.58 us -> 0.3 us
  waiting for transfers between devices: 41.6 us -> 40.5 us
    ppermute x13, starting transfers between devices: 21.8 us -> 4.03 us  [step(): lax.ppermute(to_left, 'tensor', left)]
    ppermute x13, starting transfers between devices: 6.25 us -> 23.9 us  [step(): lax.ppermute(to_right, 'tensor', right)]
    ppermute x13, waiting for transfers between devices: 14.9 us -> 26.5 us  [step(): lax.ppermute(to_left, 'tensor', left)]
    ppermute x13, waiting for transfers between devices: 19 us -> 7.68 us  [step(): lax.ppermute(to_right, 'tensor', right)]
    pallas_call x0 -> x2, Pallas kernels: none -> 2.18 us  [combined(): pl.pallas_call(combine_kernel, grid=(1,), in_specs=in_specs, out_specs=pl...]
    ppermute x1, waiting for transfers between devices: 2.32 us -> 0.63 us  [per_device(): last_left = lax.ppermute(added(1, 1, 0, flows[1][1]), 'tensor', left)]
    dot_general x1 -> x0, matrix products: 1.28 us -> none  [per_device(): mixed = jnp.einsum('wcr,wcd->rd', combine, returned.astype(jnp.float32))]
    ppermute x1 -> x2, waiting for transfers between devices: 1.47 us -> 2.59 us  [per_device(): swapped = lax.ppermute(total[CAP:], 'expert', swap)]
  transfers between devices with their start and end apart: 30 -> 31, of which waited for: 19 -> 21; matrix products, arithmetic and copies ran while one was open for 1% -> 1% of each run, Pallas kernels for 24% -> 25%
where the time goes in v18:
time: 109 us
  waiting for transfers between devices  40.5 us (37%)
  Pallas kernels  33.1 us (30%)
  starting transfers between devices  31.8 us (29%)
  other arithmetic  2.25 us (2%)
    pallas_call x9, Pallas kernels, call(): pl.pallas_call(kernel, in_specs=[pl.BlockSpec(memory_space=memory) for _,...  30.9 us
    ppermute x13, waiting for transfers between devices, step(): lax.ppermute(to_left, 'tensor', left)  26.5 us
    ppermute x13, starting transfers between devices, step(): lax.ppermute(to_right, 'tensor', right)  23.9 us
    ppermute x13, waiting for transfers between devices, step(): lax.ppermute(to_right, 'tensor', right)  7.68 us
    ppermute x13, starting transfers between devices, step(): lax.ppermute(to_left, 'tensor', left)  4.03 us
    ppermute x2, waiting for transfers between devices, per_device(): swapped = lax.ppermute(total[CAP:], 'expert', swap)  2.59 us
  transfers between devices with their start and end apart: 31, of which 21 were waited for; matrix products, arithmetic and copies ran while one was open for 1% of the time, Pallas kernels for 25%

profile of v18, /device:TPU:0, one launch (start us, length us, event | category | flops | bytes accessed | tf_op | source)
XLA Modules:
  0.0 108.7 jit_solution(3461180739478278780)
XLA Ops:
  0.1 0.8 compare_reduce_fusion
  0.9 0.1 copy.22
  1.4 0.3 convolution_convert_fusion
  1.7 0.5 collective-permute-start
  2.2 1.2 %collective-permute-done = bf16[24,6144]{1,0:T(8,128)(2,1)S(1)} collective-permute-done((bf16[24,6144]{1,0:T(8,128)(2,1)S(1)}, bf16[24,6144]{1,0:T(8,128)(2,1)S(1)}, u32[]{:S(2)}, u32[]{:S(2)}) %collective-permute-start) | collective-permute-done | bytes 294944 | tf_op jit(solution)/shard_map/ppermute | solution.py:184
  3.5 3.0 %collective-permute-start.1 = (bf16[48,3072]{1,0:T(8,128)(2,1)S(1)}, bf16[48,3072]{1,0:T(8,128)(2,1)S(1)}, u32[]{:S(2)}, u32[]{:S(2)}) collective-permute-start(bf16[48,3072]{1,0:T(8,128)(2,1)S(1)} %get-tuple-element.152.refs_0_), channel_id=1, source_target_pairs={{0,2},{2,4},{4,6},{6,7},{7,5},{5,3},{3,1},{1,0},{8,10},{10,12},{12... | collective-permute-start | bytes 884744 | tf_op jit(solution)/shard_map/ppermute | solution.py:170
  6.6 2.0 %collective-permute-start.3 = (bf16[48,3072]{1,0:T(8,128)(2,1)S(1)}, bf16[48,3072]{1,0:T(8,128)(2,1)S(1)}, u32[]{:S(2)}, u32[]{:S(2)}) collective-permute-start(bf16[48,3072]{1,0:T(8,128)(2,1)S(1)} %get-tuple-element.151.refs_5_), channel_id=1, source_target_pairs={{0,2},{2,4},{4,6},{6,7},{7,5},{5,3},{3,1},{1,0},{8,10},{10,12},{12... | collective-permute-start | bytes 884744 | tf_op jit(solution)/shard_map/ppermute | solution.py:170
  8.6 4.7 %fetched.3.refs_10_.refs_6_ = bf16[1,6144,1024]{2,1,0:T(8,128)(2,1)S(1)} custom-call(bf16[1,6144,1024]{2,1,0:T(8,128)(2,1)} %source), custom_call_target="tpu_custom_call" | custom-call | flops 1024 | bytes 1024 | tf_op jit(solution)/shard_map/fetched/pallas_call | solution.py:29
  13.3 1.0 collective-permute-done.1.refs_1_
  14.3 2.2 %collective-permute-done.2.refs_7_ = bf16[48,3072]{1,0:T(8,128)(2,1)S(1)} collective-permute-done((bf16[48,3072]{1,0:T(8,128)(2,1)S(1)}, bf16[48,3072]{1,0:T(8,128)(2,1)S(1)}, u32[]{:S(2)}, u32[]{:S(2)}) %collective-permute-start.2) | collective-permute-done | bytes 294944 | tf_op jit(solution)/shard_map/ppermute | solution.py:170
  16.4 1.6 %collective-permute-start.5 = (bf16[48,3072]{1,0:T(8,128)(2,1)S(1)}, bf16[48,3072]{1,0:T(8,128)(2,1)S(1)}, u32[]{:S(2)}, u32[]{:S(2)}) collective-permute-start(bf16[48,3072]{1,0:T(8,128)(2,1)S(1)} %collective-permute-done.1.refs_1_), channel_id=1, source_target_pairs={{0,2},{2,4},{4,6},{6,7},{7,5},{5,3},{3,1},{1,0},{8,10},{10,12},{12... | collective-permute-start | bytes 884744 | tf_op jit(solution)/shard_map/ppermute | solution.py:170
  18.0 0.4 collective-permute-start.6
  18.5 4.7 %fetched.4.refs_10_.refs_7_ = bf16[1,6144,1024]{2,1,0:T(8,128)(2,1)S(1)} custom-call(bf16[1,6144,1024]{2,1,0:T(8,128)(2,1)} %source.1), custom_call_target="tpu_custom_call" | custom-call | flops 1024 | bytes 1024 | tf_op jit(solution)/shard_map/fetched/pallas_call | solution.py:29
  23.2 1.6 %collective-permute-start.7 = (bf16[48,3072]{1,0:T(8,128)(2,1)S(1)}, bf16[48,3072]{1,0:T(8,128)(2,1)S(1)}, u32[]{:S(2)}, u32[]{:S(2)}) collective-permute-start(bf16[48,3072]{1,0:T(8,128)(2,1)S(1)} %collective-permute-done.3.refs_6_), channel_id=1, source_target_pairs={{0,2},{2,4},{4,6},{6,7},{7,5},{5,3},{3,1},{1,0},{8,10},{10,12},{12... | collective-permute-start | bytes 884744 | tf_op jit(solution)/shard_map/ppermute | solution.py:170
  24.8 0.4 collective-permute-start.8
  25.3 1.6 %collective-permute-done.5.refs_3_ = bf16[48,3072]{1,0:T(8,128)(2,1)S(1)} collective-permute-done((bf16[48,3072]{1,0:T(8,128)(2,1)S(1)}, bf16[48,3072]{1,0:T(8,128)(2,1)S(1)}, u32[]{:S(2)}, u32[]{:S(2)}) %collective-permute-start.5) | collective-permute-done | bytes 294944 | tf_op jit(solution)/shard_map/ppermute | solution.py:170
  26.9 2.2 %collective-permute-done.6.refs_9_ = bf16[48,3072]{1,0:T(8,128)(2,1)S(1)} collective-permute-done((bf16[48,3072]{1,0:T(8,128)(2,1)S(1)}, bf16[48,3072]{1,0:T(8,128)(2,1)S(1)}, u32[]{:S(2)}, u32[]{:S(2)}) %collective-permute-start.6) | collective-permute-done | bytes 294944 | tf_op jit(solution)/shard_map/ppermute | solution.py:170
  29.1 2.0 %collective-permute-start.9 = (bf16[48,3072]{1,0:T(8,128)(2,1)S(1)}, bf16[48,3072]{1,0:T(8,128)(2,1)S(1)}, u32[]{:S(2)}, u32[]{:S(2)}) collective-permute-start(bf16[48,3072]{1,0:T(8,128)(2,1)S(1)} %collective-permute-done.5.refs_3_), channel_id=1, source_target_pairs={{0,2},{2,4},{4,6},{6,7},{7,5},{5,3},{3,1},{1,0},{8,10},{10,12},{12... | collective-permute-start | bytes 884744 | tf_op jit(solution)/shard_map/ppermute | solution.py:170
  31.1 2.1 %collective-permute-done.7.refs_8_ = bf16[48,3072]{1,0:T(8,128)(2,1)S(1)} collective-permute-done((bf16[48,3072]{1,0:T(8,128)(2,1)S(1)}, bf16[48,3072]{1,0:T(8,128)(2,1)S(1)}, u32[]{:S(2)}, u32[]{:S(2)}) %collective-permute-start.7) | collective-permute-done | bytes 294944 | tf_op jit(solution)/shard_map/ppermute | solution.py:170
  33.2 2.2 %collective-permute-done.8.refs_4_ = bf16[48,3072]{1,0:T(8,128)(2,1)S(1)} collective-permute-done((bf16[48,3072]{1,0:T(8,128)(2,1)S(1)}, bf16[48,3072]{1,0:T(8,128)(2,1)S(1)}, u32[]{:S(2)}, u32[]{:S(2)}) %collective-permute-start.8) | collective-permute-done | bytes 294944 | tf_op jit(solution)/shard_map/ppermute | solution.py:170
  35.4 3.2 %near_gate.1.refs_11_ = f32[240,1024]{1,0:T(8,128)S(1)} custom-call(bf16[48,3072]{1,0:T(8,128)(2,1)S(1)} %get-tuple-element.152.refs_0_, bf16[48,3072]{1,0:T(8,128)(2,1)S(1)} %collective-permute-done.1.refs_1_, bf16[48,3072]{1,0:T(8,128)(2,1)S(1)} %collective-permute-done.4.refs_2_, bf16[48,3072]{1,0:T(8,128)(2,1)S(1)} %collective-permute-done.5.refs_3_, ...), custom_call_target="tpu_custom_call" | custom-call | flops 1024 | bytes 1024 | tf_op jit(solution)/shard_map/near_gate/pallas_call | solution.py:29
  38.6 1.6 %collective-permute-start.11 = (bf16[48,3072]{1,0:T(8,128)(2,1)S(1)}, bf16[48,3072]{1,0:T(8,128)(2,1)S(1)}, u32[]{:S(2)}, u32[]{:S(2)}) collective-permute-start(bf16[48,3072]{1,0:T(8,128)(2,1)S(1)} %collective-permute-done.7.refs_8_), channel_id=1, source_target_pairs={{0,2},{2,4},{4,6},{6,7},{7,5},{5,3},{3,1},{1,0},{8,10},{10,12},{12... | collective-permute-start | bytes 884744 | tf_op jit(solution)/shard_map/ppermute | solution.py:170
  40.2 0.4 collective-permute-start.12
  40.7 1.6 %collective-permute-start.13 = (bf16[48,3072]{1,0:T(8,128)(2,1)S(1)}, bf16[48,3072]{1,0:T(8,128)(2,1)S(1)}, u32[]{:S(2)}, u32[]{:S(2)}) collective-permute-start(bf16[48,3072]{1,0:T(8,128)(2,1)S(1)} %collective-permute-done.9.refs_0_), channel_id=1, source_target_pairs={{0,2},{2,4},{4,6},{6,7},{7,5},{5,3},{3,1},{1,0},{8,10},{10,12},{12... | collective-permute-start | bytes 884744 | tf_op jit(solution)/shard_map/ppermute | solution.py:170
  42.3 0.4 collective-permute-start.14
  42.7 3.2 %near_up.1.hidden = bf16[240,1024]{1,0:T(8,128)(2,1)S(1)} custom-call(bf16[48,3072]{1,0:T(8,128)(2,1)S(1)} %get-tuple-element.152.refs_0_, bf16[48,3072]{1,0:T(8,128)(2,1)S(1)} %collective-permute-done.1.refs_1_, bf16[48,3072]{1,0:T(8,128)(2,1)S(1)} %collective-permute-done.4.refs_2_, bf16[48,3072]{1,0:T(8,128)(2,1)S(1)} %collective-permute-done.5.refs_3_, ...), custom_call_target="tpu_custom_call" | custom-call | flops 1024 | bytes 1024 | tf_op jit(solution)/shard_map/near_up/pallas_call | solution.py:29
  46.0 2.9 %fetched.5.refs_8_.down = bf16[1,1024,3072]{2,1,0:T(8,128)(2,1)S(1)} custom-call(bf16[1,1024,6144]{2,1,0:T(8,128)(2,1)} %w_down), custom_call_target="tpu_custom_call" | custom-call | flops 1024 | bytes 1024 | tf_op jit(solution)/shard_map/fetched/pallas_call | solution.py:29
  48.9 1.2 %collective-permute-done.12.refs_1_ = bf16[48,3072]{1,0:T(8,128)(2,1)S(1)} collective-permute-done((bf16[48,3072]{1,0:T(8,128)(2,1)S(1)}, bf16[48,3072]{1,0:T(8,128)(2,1)S(1)}, u32[]{:S(2)}, u32[]{:S(2)}) %collective-permute-start.12) | collective-permute-done | bytes 294944 | tf_op jit(solution)/shard_map/ppermute | solution.py:170
  50.1 1.7 %collective-permute-done.13.refs_2_ = bf16[48,3072]{1,0:T(8,128)(2,1)S(1)} collective-permute-done((bf16[48,3072]{1,0:T(8,128)(2,1)S(1)}, bf16[48,3072]{1,0:T(8,128)(2,1)S(1)}, u32[]{:S(2)}, u32[]{:S(2)}) %collective-permute-start.13) | collective-permute-done | bytes 294944 | tf_op jit(solution)/shard_map/ppermute | solution.py:170
  51.7 1.5 %collective-permute-done.14.refs_5_ = bf16[48,3072]{1,0:T(8,128)(2,1)S(1)} collective-permute-done((bf16[48,3072]{1,0:T(8,128)(2,1)S(1)}, bf16[48,3072]{1,0:T(8,128)(2,1)S(1)}, u32[]{:S(2)}, u32[]{:S(2)}) %collective-permute-start.14) | collective-permute-done | bytes 294944 | tf_op jit(solution)/shard_map/ppermute | solution.py:170
  53.2 4.8 %rest_first.1 = (bf16[48,3072]{1,0:T(8,128)(2,1)S(1)}, bf16[48,3072]{1,0:T(8,128)(2,1)S(1)}, bf16[48,3072]{1,0:T(8,128)(2,1)S(1)}, bf16[144,1024]{1,0:T(8,128)(2,1)S(1)}) custom-call(bf16[48,3072]{1,0:T(8,128)(2,1)S(1)} %collective-permute-done.9.refs_0_, bf16[48,3072]{1,0:T(8,128)(2,1)S(1)} %collective-permute-done.12.refs_1_, ...), custom_call_target="tpu_custom_call" | custom-call | flops 1024 | bytes 1024 | tf_op jit(solution)/shard_map/rest_first/pallas_call | solution.py:29
  58.0 1.6 %collective-permute-start.22 = (bf16[48,3072]{1,0:T(8,128)(2,1)S(1)}, bf16[48,3072]{1,0:T(8,128)(2,1)S(1)}, u32[]{:S(2)}, u32[]{:S(2)}) collective-permute-start(bf16[48,3072]{1,0:T(8,128)(2,1)S(1)} %get-tuple-element.139), channel_id=1, source_target_pairs={{0,2},{2,4},{4,6},{6,7},{7,5},{5,3},{3,1},{1,0},{8,10},{10,12},{12... | collective-permute-start | bytes 884744 | tf_op jit(solution)/shard_map/ppermute | solution.py:170
  59.6 0.4 collective-permute-start.23
  60.2 4.0 %rest_second.1 = (bf16[48,3072]{1,0:T(8,128)(2,1)S(1)}, bf16[48,3072]{1,0:T(8,128)(2,1)S(1)}, bf16[48,3072]{1,0:T(8,128)(2,1)S(1)}, bf16[1,1024,3072]{2,1,0:T(8,128)(2,1)S(1)}) custom-call(bf16[144,1024]{1,0:T(8,128)(2,1)S(1)} %get-tuple-element.118.hidden, bf16[1,1024,6144]{2,1,0:T(8,128)(2,1)} %w_down), custom_call_target="tpu_custom_call" | custom-call | flops 1024 | bytes 1024 | tf_op jit(solution)/shard_map/rest_second/pallas_call | solution.py:29
  64.2 1.6 %collective-permute-start.15 = (bf16[48,3072]{1,0:T(8,128)(2,1)S(1)}, bf16[48,3072]{1,0:T(8,128)(2,1)S(1)}, u32[]{:S(2)}, u32[]{:S(2)}) collective-permute-start(bf16[48,3072]{1,0:T(8,128)(2,1)S(1)} %get-tuple-element.119), channel_id=1, source_target_pairs={{0,2},{2,4},{4,6},{6,7},{7,5},{5,3},{3,1},{1,0},{8,10},{10,12},{12... | collective-permute-start | bytes 884744 | tf_op jit(solution)/shard_map/ppermute | solution.py:170
  65.8 0.5 collective-permute-start.16
  66.3 1.7 %near_down.3 = (bf16[48,3072]{1,0:T(8,128)(2,1)S(1)}, bf16[48,3072]{1,0:T(8,128)(2,1)S(1)}, bf16[48,3072]{1,0:T(8,128)(2,1)S(1)}, bf16[48,3072]{1,0:T(8,128)(2,1)S(1)}, bf16[48,3072]{1,0:T(8,128)(2,1)S(1)}) custom-call(bf16[240,1024]{1,0:T(8,128)(2,1)S(1)} %near_up.1.hidden, bf16[1,1024,3072]{2,1,0:T(8,128)(2,1)S(1)} %fetched.5.refs_8_.down), custom_call_target="tpu_custom_call" | custom-call | flops 1024 | bytes 1024 | tf_op jit(solution)/shard_map/near_down/pallas_call | solution.py:29
  68.0 1.7 %near_down.2 = (bf16[48,3072]{1,0:T(8,128)(2,1)S(1)}, bf16[48,3072]{1,0:T(8,128)(2,1)S(1)}, bf16[48,3072]{1,0:T(8,128)(2,1)S(1)}, bf16[48,3072]{1,0:T(8,128)(2,1)S(1)}, bf16[48,3072]{1,0:T(8,128)(2,1)S(1)}) custom-call(bf16[240,1024]{1,0:T(8,128)(2,1)S(1)} %near_up.1.hidden, bf16[1,1024,3072]{2,1,0:T(8,128)(2,1)S(1)} %get-tuple-element.122.down), custom_call_target="tpu_custom_call" | custom-call | flops 1024 | bytes 1024 | tf_op jit(solution)/shard_map/near_down/pallas_call | solution.py:29
  69.8 0.3 collective-permute-start.25
  70.2 1.8 %collective-permute-start.24 = (bf16[48,3072]{1,0:T(8,128)(2,1)S(1)}, bf16[48,3072]{1,0:T(8,128)(2,1)S(1)}, u32[]{:S(2)}, u32[]{:S(2)}) collective-permute-start(bf16[48,3072]{1,0:T(8,128)(2,1)S(1)} %add_convert_fusion.6), channel_id=1, source_target_pairs={{0,2},{2,4},{4,6},{6,7},{7,5},{5,3},{3,1},{1,0},{8,10},{10,12},{12... | collective-permute-start | bytes 884744 | tf_op jit(solution)/shard_map/ppermute | solution.py:170
  72.0 0.3 collective-permute-done.15
  72.2 3.5 %collective-permute-done.16 = bf16[48,3072]{1,0:T(8,128)(2,1)S(1)} collective-permute-done((bf16[48,3072]{1,0:T(8,128)(2,1)S(1)}, bf16[48,3072]{1,0:T(8,128)(2,1)S(1)}, u32[]{:S(2)}, u32[]{:S(2)}) %collective-permute-start.16) | collective-permute-done | bytes 294944 | tf_op jit(solution)/shard_map/ppermute | solution.py:170
  75.8 0.3 collective-permute-start.18
  76.2 1.8 %collective-permute-start.17 = (bf16[48,3072]{1,0:T(8,128)(2,1)S(1)}, bf16[48,3072]{1,0:T(8,128)(2,1)S(1)}, u32[]{:S(2)}, u32[]{:S(2)}) collective-permute-start(bf16[48,3072]{1,0:T(8,128)(2,1)S(1)} %add_convert_fusion.11), channel_id=1, source_target_pairs={{0,2},{2,4},{4,6},{6,7},{7,5},{5,3},{3,1},{1,0},{8,10},{10,12},{12... | collective-permute-start | bytes 884744 | tf_op jit(solution)/shard_map/ppermute | solution.py:170
  78.0 4.0 %collective-permute-done.25 = bf16[48,3072]{1,0:T(8,128)(2,1)S(1)} collective-permute-done((bf16[48,3072]{1,0:T(8,128)(2,1)S(1)}, bf16[48,3072]{1,0:T(8,128)(2,1)S(1)}, u32[]{:S(2)}, u32[]{:S(2)}) %collective-permute-start.25) | collective-permute-done | bytes 294944 | tf_op jit(solution)/shard_map/ppermute | solution.py:170
  82.2 0.3 collective-permute-start.27
  82.6 1.8 %collective-permute-start.26 = (bf16[48,3072]{1,0:T(8,128)(2,1)S(1)}, bf16[48,3072]{1,0:T(8,128)(2,1)S(1)}, u32[]{:S(2)}, u32[]{:S(2)}) collective-permute-start(bf16[48,3072]{1,0:T(8,128)(2,1)S(1)} %add_convert_fusion.4), channel_id=1, source_target_pairs={{0,2},{2,4},{4,6},{6,7},{7,5},{5,3},{3,1},{1,0},{8,10},{10,12},{12... | collective-permute-start | bytes 884744 | tf_op jit(solution)/shard_map/ppermute | solution.py:170
  84.4 4.0 %collective-permute-done.18 = bf16[48,3072]{1,0:T(8,128)(2,1)S(1)} collective-permute-done((bf16[48,3072]{1,0:T(8,128)(2,1)S(1)}, bf16[48,3072]{1,0:T(8,128)(2,1)S(1)}, u32[]{:S(2)}, u32[]{:S(2)}) %collective-permute-start.18) | collective-permute-done | bytes 294944 | tf_op jit(solution)/shard_map/ppermute | solution.py:170
  88.5 0.3 collective-permute-start.20
  88.9 1.8 %collective-permute-start.19 = (bf16[48,3072]{1,0:T(8,128)(2,1)S(1)}, bf16[48,3072]{1,0:T(8,128)(2,1)S(1)}, u32[]{:S(2)}, u32[]{:S(2)}) collective-permute-start(bf16[48,3072]{1,0:T(8,128)(2,1)S(1)} %add_convert_fusion.9), channel_id=1, source_target_pairs={{0,2},{2,4},{4,6},{6,7},{7,5},{5,3},{3,1},{1,0},{8,10},{10,12},{12... | collective-permute-start | bytes 884744 | tf_op jit(solution)/shard_map/ppermute | solution.py:170
  90.7 4.0 %collective-permute-done.27 = bf16[48,3072]{1,0:T(8,128)(2,1)S(1)} collective-permute-done((bf16[48,3072]{1,0:T(8,128)(2,1)S(1)}, bf16[48,3072]{1,0:T(8,128)(2,1)S(1)}, u32[]{:S(2)}, u32[]{:S(2)}) %collective-permute-start.27) | collective-permute-done | bytes 294944 | tf_op jit(solution)/shard_map/ppermute | solution.py:170
  94.8 1.6 %collective-permute-start.28 = (bf16[48,3072]{1,0:T(8,128)(2,1)S(1)}, bf16[48,3072]{1,0:T(8,128)(2,1)S(1)}, u32[]{:S(2)}, u32[]{:S(2)}) collective-permute-start(bf16[48,3072]{1,0:T(8,128)(2,1)S(1)} %add_convert_fusion.2), channel_id=1, source_target_pairs={{0,2},{2,4},{4,6},{6,7},{7,5},{5,3},{3,1},{1,0},{8,10},{10,12},{12... | collective-permute-start | bytes 884744 | tf_op jit(solution)/shard_map/ppermute | solution.py:268
  96.4 1.7 %collective-permute-done.20 = bf16[48,3072]{1,0:T(8,128)(2,1)S(1)} collective-permute-done((bf16[48,3072]{1,0:T(8,128)(2,1)S(1)}, bf16[48,3072]{1,0:T(8,128)(2,1)S(1)}, u32[]{:S(2)}, u32[]{:S(2)}) %collective-permute-start.20) | collective-permute-done | bytes 294944 | tf_op jit(solution)/shard_map/ppermute | solution.py:170
  98.1 1.0 collective-permute-done.19
  99.2 1.5 %collective-permute-start.21 = (bf16[48,3072]{1,0:T(8,128)(2,1)S(1)}, bf16[48,3072]{1,0:T(8,128)(2,1)S(1)}, u32[]{:S(2)}, u32[]{:S(2)}) collective-permute-start(bf16[48,3072]{1,0:T(8,128)(2,1)S(1)} %add_convert_fusion.7), channel_id=1, source_target_pairs={{2,0},{4,2},{6,4},{7,6},{5,7},{3,5},{1,3},{0,1},{10,8},{12,10},{14... | collective-permute-start | bytes 884744 | tf_op jit(solution)/shard_map/ppermute | solution.py:269
  100.8 1.9 %collective-permute-done.28 = bf16[48,3072]{1,0:T(8,128)(2,1)S(1)} collective-permute-done((bf16[48,3072]{1,0:T(8,128)(2,1)S(1)}, bf16[48,3072]{1,0:T(8,128)(2,1)S(1)}, u32[]{:S(2)}, u32[]{:S(2)}) %collective-permute-start.28) | collective-permute-done | bytes 294944 | tf_op jit(solution)/shard_map/ppermute | solution.py:268
  102.7 0.1 add_convert_fusion.1
  102.9 0.1 select_convert_fusion.weights
  103.0 1.2 %collective-permute-done.29.swapped = bf16[24,3072]{1,0:T(8,128)(2,1)S(1)} collective-permute-done((bf16[24,3072]{1,0:T(8,128)(2,1)S(1)}, bf16[24,3072]{1,0:T(8,128)(2,1)S(1)}, u32[]{:S(2)}, u32[]{:S(2)}) %collective-permute-start.29) | collective-permute-done | bytes 147488 | tf_op jit(solution)/shard_map/ppermute | solution.py:279
  104.3 1.1 %combined.2.refs_0_ = bf16[64,6144]{1,0:T(8,128)(2,1)} custom-call(bf16[2,64,24]{2,1,0:T(8,128)(2,1)S(1)} %select_convert_fusion.weights, bf16[24,3072]{1,0:T(8,128)(2,1)S(1)} %get-tuple-element.158.kept, bf16[24,3072]{1,0:T(8,128)(2,1)S(1)} %collective-permute-done.29.swapped), custom_call_target="tpu_custom_call" | custom-call | flops 1024 | bytes 1024 | tf_op jit(solution)/shard_map/combined/pallas_call | solution.py:134
  105.4 0.6 collective-permute-done.21
  106.0 0.1 add_convert_fusion
  106.2 1.4 %collective-permute-done.30.swapped = bf16[24,3072]{1,0:T(8,128)(2,1)S(1)} collective-permute-done((bf16[24,3072]{1,0:T(8,128)(2,1)S(1)}, bf16[24,3072]{1,0:T(8,128)(2,1)S(1)}, u32[]{:S(2)}, u32[]{:S(2)}) %collective-permute-start.30) | collective-permute-done | bytes 147488 | tf_op jit(solution)/shard_map/ppermute | solution.py:279
  107.6 1.1 %combined.3 = bf16[64,6144]{1,0:T(8,128)(2,1)} custom-call(bf16[2,64,24]{2,1,0:T(8,128)(2,1)S(1)} %select_convert_fusion.weights, bf16[24,3072]{1,0:T(8,128)(2,1)S(1)} %get-tuple-element.156.kept, bf16[24,3072]{1,0:T(8,128)(2,1)S(1)} %collective-permute-done.30.swapped, bf16[64,6144]{1,0:T(8,128)(2,1)} %combined.2.refs_0_), custom_call_target="tpu_custom_call", output_to_operand_aliasing={{}: (3, {})} | custom-call | flops 1024 | bytes 1024 | tf_op jit(solution)/shard_map/combined/pallas_call | solution.py:134
  (47 shorter events, 1.6 us)
Async XLA Ops:
  0.0 1.4 %copy-start = (bf16[64,6144]{1,0:T(8,128)(2,1)S(1)}, bf16[64,6144]{1,0:T(8,128)(2,1)}, u32[]{:S(2)}) copy-start(bf16[64,6144]{1,0:T(8,128)(2,1)} %param.6) | copy-start | bytes 2359300
  1.7 1.7 %collective-permute-start = (bf16[24,6144]{1,0:T(8,128)(2,1)S(1)}, bf16[24,6144]{1,0:T(8,128)(2,1)S(1)}, u32[]{:S(2)}, u32[]{:S(2)}) collective-permute-start(bf16[24,6144]{1,0:T(8,128)(2,1)S(1)} %get-tuple-element.154), channel_id=1, source_target_pairs={{0,8},{8,0},{1,9},{9,1},{2,10},{10,2},{3,11},{11,3},{4,12},{12,4},... | collective-permute-start | bytes 884744 | tf_op jit(solution)/shard_map/ppermute | solution.py:184
  3.5 10.7 %collective-permute-start.1 = (bf16[48,3072]{1,0:T(8,128)(2,1)S(1)}, bf16[48,3072]{1,0:T(8,128)(2,1)S(1)}, u32[]{:S(2)}, u32[]{:S(2)}) collective-permute-start(bf16[48,3072]{1,0:T(8,128)(2,1)S(1)} %get-tuple-element.152.refs_0_), channel_id=1, source_target_pairs={{0,2},{2,4},{4,6},{6,7},{7,5},{5,3},{3,1},{1,0},{8,10},{10,12},{12... | collective-permute-start | bytes 884744 | tf_op jit(solution)/shard_map/ppermute | solution.py:170
  6.5 9.9 %collective-permute-start.2 = (bf16[48,3072]{1,0:T(8,128)(2,1)S(1)}, bf16[48,3072]{1,0:T(8,128)(2,1)S(1)}, u32[]{:S(2)}, u32[]{:S(2)}) collective-permute-start(bf16[48,3072]{1,0:T(8,128)(2,1)S(1)} %get-tuple-element.151.refs_5_), channel_id=1, source_target_pairs={{2,0},{4,2},{6,4},{7,6},{5,7},{3,5},{1,3},{0,1},{10,8},{12,10},{14... | collective-permute-start | bytes 884744 | tf_op jit(solution)/shard_map/ppermute | solution.py:170
  6.6 16.6 %collective-permute-start.3 = (bf16[48,3072]{1,0:T(8,128)(2,1)S(1)}, bf16[48,3072]{1,0:T(8,128)(2,1)S(1)}, u32[]{:S(2)}, u32[]{:S(2)}) collective-permute-start(bf16[48,3072]{1,0:T(8,128)(2,1)S(1)} %get-tuple-element.151.refs_5_), channel_id=1, source_target_pairs={{0,2},{2,4},{4,6},{6,7},{7,5},{5,3},{3,1},{1,0},{8,10},{10,12},{12... | collective-permute-start | bytes 884744 | tf_op jit(solution)/shard_map/ppermute | solution.py:170
  8.6 14.6 %collective-permute-start.4 = (bf16[48,3072]{1,0:T(8,128)(2,1)S(1)}, bf16[48,3072]{1,0:T(8,128)(2,1)S(1)}, u32[]{:S(2)}, u32[]{:S(2)}) collective-permute-start(bf16[48,3072]{1,0:T(8,128)(2,1)S(1)} %get-tuple-element.152.refs_0_), channel_id=1, source_target_pairs={{2,0},{4,2},{6,4},{7,6},{5,7},{3,5},{1,3},{0,1},{10,8},{12,10},{14... | collective-permute-start | bytes 884744 | tf_op jit(solution)/shard_map/ppermute | solution.py:170
  16.4 10.5 %collective-permute-start.5 = (bf16[48,3072]{1,0:T(8,128)(2,1)S(1)}, bf16[48,3072]{1,0:T(8,128)(2,1)S(1)}, u32[]{:S(2)}, u32[]{:S(2)}) collective-permute-start(bf16[48,3072]{1,0:T(8,128)(2,1)S(1)} %collective-permute-done.1.refs_1_), channel_id=1, source_target_pairs={{0,2},{2,4},{4,6},{6,7},{7,5},{5,3},{3,1},{1,0},{8,10},{10,12},{12... | collective-permute-start | bytes 884744 | tf_op jit(solution)/shard_map/ppermute | solution.py:170
  18.0 11.1 %collective-permute-start.6 = (bf16[48,3072]{1,0:T(8,128)(2,1)S(1)}, bf16[48,3072]{1,0:T(8,128)(2,1)S(1)}, u32[]{:S(2)}, u32[]{:S(2)}) collective-permute-start(bf16[48,3072]{1,0:T(8,128)(2,1)S(1)} %collective-permute-done.2.refs_7_), channel_id=1, source_target_pairs={{2,0},{4,2},{6,4},{7,6},{5,7},{3,5},{1,3},{0,1},{10,8},{12,10},{14... | collective-permute-start | bytes 884744 | tf_op jit(solution)/shard_map/ppermute | solution.py:170
  23.2 10.0 %collective-permute-start.7 = (bf16[48,3072]{1,0:T(8,128)(2,1)S(1)}, bf16[48,3072]{1,0:T(8,128)(2,1)S(1)}, u32[]{:S(2)}, u32[]{:S(2)}) collective-permute-start(bf16[48,3072]{1,0:T(8,128)(2,1)S(1)} %collective-permute-done.3.refs_6_), channel_id=1, source_target_pairs={{0,2},{2,4},{4,6},{6,7},{7,5},{5,3},{3,1},{1,0},{8,10},{10,12},{12... | collective-permute-start | bytes 884744 | tf_op jit(solution)/shard_map/ppermute | solution.py:170
  24.8 10.6 %collective-permute-start.8 = (bf16[48,3072]{1,0:T(8,128)(2,1)S(1)}, bf16[48,3072]{1,0:T(8,128)(2,1)S(1)}, u32[]{:S(2)}, u32[]{:S(2)}) collective-permute-start(bf16[48,3072]{1,0:T(8,128)(2,1)S(1)} %collective-permute-done.4.refs_2_), channel_id=1, source_target_pairs={{2,0},{4,2},{6,4},{7,6},{5,7},{3,5},{1,3},{0,1},{10,8},{12,10},{14... | collective-permute-start | bytes 884744 | tf_op jit(solution)/shard_map/ppermute | solution.py:170
  29.1 11.6 %collective-permute-start.10 = (bf16[48,3072]{1,0:T(8,128)(2,1)S(1)}, bf16[48,3072]{1,0:T(8,128)(2,1)S(1)}, u32[]{:S(2)}, u32[]{:S(2)}) collective-permute-start(bf16[48,3072]{1,0:T(8,128)(2,1)S(1)} %collective-permute-done.6.refs_9_), channel_id=1, source_target_pairs={{2,0},{4,2},{6,4},{7,6},{5,7},{3,5},{1,3},{0,1},{10,8},{12,10},{14... | collective-permute-start | bytes 884744 | tf_op jit(solution)/shard_map/ppermute | solution.py:170
  29.1 11.6 %collective-permute-start.9 = (bf16[48,3072]{1,0:T(8,128)(2,1)S(1)}, bf16[48,3072]{1,0:T(8,128)(2,1)S(1)}, u32[]{:S(2)}, u32[]{:S(2)}) collective-permute-start(bf16[48,3072]{1,0:T(8,128)(2,1)S(1)} %collective-permute-done.5.refs_3_), channel_id=1, source_target_pairs={{0,2},{2,4},{4,6},{6,7},{7,5},{5,3},{3,1},{1,0},{8,10},{10,12},{12... | collective-permute-start | bytes 884744 | tf_op jit(solution)/shard_map/ppermute | solution.py:170
  38.6 10.3 %collective-permute-start.11 = (bf16[48,3072]{1,0:T(8,128)(2,1)S(1)}, bf16[48,3072]{1,0:T(8,128)(2,1)S(1)}, u32[]{:S(2)}, u32[]{:S(2)}) collective-permute-start(bf16[48,3072]{1,0:T(8,128)(2,1)S(1)} %collective-permute-done.7.refs_8_), channel_id=1, source_target_pairs={{0,2},{2,4},{4,6},{6,7},{7,5},{5,3},{3,1},{1,0},{8,10},{10,12},{12... | collective-permute-start | bytes 884744 | tf_op jit(solution)/shard_map/ppermute | solution.py:170
  40.2 9.8 %collective-permute-start.12 = (bf16[48,3072]{1,0:T(8,128)(2,1)S(1)}, bf16[48,3072]{1,0:T(8,128)(2,1)S(1)}, u32[]{:S(2)}, u32[]{:S(2)}) collective-permute-start(bf16[48,3072]{1,0:T(8,128)(2,1)S(1)} %collective-permute-done.8.refs_4_), channel_id=1, source_target_pairs={{2,0},{4,2},{6,4},{7,6},{5,7},{3,5},{1,3},{0,1},{10,8},{12,10},{14... | collective-permute-start | bytes 884744 | tf_op jit(solution)/shard_map/ppermute | solution.py:170
  40.7 11.0 %collective-permute-start.13 = (bf16[48,3072]{1,0:T(8,128)(2,1)S(1)}, bf16[48,3072]{1,0:T(8,128)(2,1)S(1)}, u32[]{:S(2)}, u32[]{:S(2)}) collective-permute-start(bf16[48,3072]{1,0:T(8,128)(2,1)S(1)} %collective-permute-done.9.refs_0_), channel_id=1, source_target_pairs={{0,2},{2,4},{4,6},{6,7},{7,5},{5,3},{3,1},{1,0},{8,10},{10,12},{12... | collective-permute-start | bytes 884744 | tf_op jit(solution)/shard_map/ppermute | solution.py:170
  42.3 10.9 %collective-permute-start.14 = (bf16[48,3072]{1,0:T(8,128)(2,1)S(1)}, bf16[48,3072]{1,0:T(8,128)(2,1)S(1)}, u32[]{:S(2)}, u32[]{:S(2)}) collective-permute-start(bf16[48,3072]{1,0:T(8,128)(2,1)S(1)} %collective-permute-done.10.refs_4_), channel_id=1, source_target_pairs={{2,0},{4,2},{6,4},{7,6},{5,7},{3,5},{1,3},{0,1},{10,8},{12,10},{14... | collective-permute-start | bytes 884744 | tf_op jit(solution)/shard_map/ppermute | solution.py:170
  48.9 11.2 %copy-start.2 = (s32[64,2]{0,1:T(2,128)S(1)}, s32[64,2]{0,1:T(2,128)}, u32[]{:S(2)}) copy-start(s32[64,2]{0,1:T(2,128)} %param.7) | copy-start | bytes 1540
  48.9 11.2 %copy-start.3 = (f32[64,2]{0,1:T(2,128)S(1)}, f32[64,2]{0,1:T(2,128)}, u32[]{:S(2)}) copy-start(f32[64,2]{0,1:T(2,128)} %param.8) | copy-start | bytes 1540
  58.0 11.7 %collective-permute-start.22 = (bf16[48,3072]{1,0:T(8,128)(2,1)S(1)}, bf16[48,3072]{1,0:T(8,128)(2,1)S(1)}, u32[]{:S(2)}, u32[]{:S(2)}) collective-permute-start(bf16[48,3072]{1,0:T(8,128)(2,1)S(1)} %get-tuple-element.139), channel_id=1, source_target_pairs={{0,2},{2,4},{4,6},{6,7},{7,5},{5,3},{3,1},{1,0},{8,10},{10,12},{12... | collective-permute-start | bytes 884744 | tf_op jit(solution)/shard_map/ppermute | solution.py:170
  59.6 10.1 %collective-permute-start.23 = (bf16[48,3072]{1,0:T(8,128)(2,1)S(1)}, bf16[48,3072]{1,0:T(8,128)(2,1)S(1)}, u32[]{:S(2)}, u32[]{:S(2)}) collective-permute-start(bf16[48,3072]{1,0:T(8,128)(2,1)S(1)} %get-tuple-element.140), channel_id=1, source_target_pairs={{2,0},{4,2},{6,4},{7,6},{5,7},{3,5},{1,3},{0,1},{10,8},{12,10},{14... | collective-permute-start | bytes 884744 | tf_op jit(solution)/shard_map/ppermute | solution.py:170
  64.2 8.0 %collective-permute-start.15 = (bf16[48,3072]{1,0:T(8,128)(2,1)S(1)}, bf16[48,3072]{1,0:T(8,128)(2,1)S(1)}, u32[]{:S(2)}, u32[]{:S(2)}) collective-permute-start(bf16[48,3072]{1,0:T(8,128)(2,1)S(1)} %get-tuple-element.119), channel_id=1, source_target_pairs={{0,2},{2,4},{4,6},{6,7},{7,5},{5,3},{3,1},{1,0},{8,10},{10,12},{12... | collective-permute-start | bytes 884744 | tf_op jit(solution)/shard_map/ppermute | solution.py:170
  65.8 9.9 %collective-permute-start.16 = (bf16[48,3072]{1,0:T(8,128)(2,1)S(1)}, bf16[48,3072]{1,0:T(8,128)(2,1)S(1)}, u32[]{:S(2)}, u32[]{:S(2)}) collective-permute-start(bf16[48,3072]{1,0:T(8,128)(2,1)S(1)} %get-tuple-element.120), channel_id=1, source_target_pairs={{2,0},{4,2},{6,4},{7,6},{5,7},{3,5},{1,3},{0,1},{10,8},{12,10},{14... | collective-permute-start | bytes 884744 | tf_op jit(solution)/shard_map/ppermute | solution.py:170
  69.8 12.3 %collective-permute-start.25 = (bf16[48,3072]{1,0:T(8,128)(2,1)S(1)}, bf16[48,3072]{1,0:T(8,128)(2,1)S(1)}, u32[]{:S(2)}, u32[]{:S(2)}) collective-permute-start(bf16[48,3072]{1,0:T(8,128)(2,1)S(1)} %add_convert_fusion.5), channel_id=1, source_target_pairs={{2,0},{4,2},{6,4},{7,6},{5,7},{3,5},{1,3},{0,1},{10,8},{12,10},{14... | collective-permute-start | bytes 884744 | tf_op jit(solution)/shard_map/ppermute | solution.py:170
  70.2 11.9 %collective-permute-start.24 = (bf16[48,3072]{1,0:T(8,128)(2,1)S(1)}, bf16[48,3072]{1,0:T(8,128)(2,1)S(1)}, u32[]{:S(2)}, u32[]{:S(2)}) collective-permute-start(bf16[48,3072]{1,0:T(8,128)(2,1)S(1)} %add_convert_fusion.6), channel_id=1, source_target_pairs={{0,2},{2,4},{4,6},{6,7},{7,5},{5,3},{3,1},{1,0},{8,10},{10,12},{12... | collective-permute-start | bytes 884744 | tf_op jit(solution)/shard_map/ppermute | solution.py:170
  75.8 12.6 %collective-permute-start.18 = (bf16[48,3072]{1,0:T(8,128)(2,1)S(1)}, bf16[48,3072]{1,0:T(8,128)(2,1)S(1)}, u32[]{:S(2)}, u32[]{:S(2)}) collective-permute-start(bf16[48,3072]{1,0:T(8,128)(2,1)S(1)} %add_convert_fusion.10), channel_id=1, source_target_pairs={{2,0},{4,2},{6,4},{7,6},{5,7},{3,5},{1,3},{0,1},{10,8},{12,10},{14... | collective-permute-start | bytes 884744 | tf_op jit(solution)/shard_map/ppermute | solution.py:170
  76.2 32.5 %copy-start.1 = (bf16[64,6144]{1,0:T(8,128)(2,1)S(1)}, bf16[64,6144]{1,0:T(8,128)(2,1)}, u32[]{:S(2)}) copy-start(bf16[64,6144]{1,0:T(8,128)(2,1)} %param.6) | copy-start | bytes 2359300
  76.2 12.2 %collective-permute-start.17 = (bf16[48,3072]{1,0:T(8,128)(2,1)S(1)}, bf16[48,3072]{1,0:T(8,128)(2,1)S(1)}, u32[]{:S(2)}, u32[]{:S(2)}) collective-permute-start(bf16[48,3072]{1,0:T(8,128)(2,1)S(1)} %add_convert_fusion.11), channel_id=1, source_target_pairs={{0,2},{2,4},{4,6},{6,7},{7,5},{5,3},{3,1},{1,0},{8,10},{10,12},{12... | collective-permute-start | bytes 884744 | tf_op jit(solution)/shard_map/ppermute | solution.py:170
  82.2 12.6 %collective-permute-start.27 = (bf16[48,3072]{1,0:T(8,128)(2,1)S(1)}, bf16[48,3072]{1,0:T(8,128)(2,1)S(1)}, u32[]{:S(2)}, u32[]{:S(2)}) collective-permute-start(bf16[48,3072]{1,0:T(8,128)(2,1)S(1)} %add_convert_fusion.3), channel_id=1, source_target_pairs={{2,0},{4,2},{6,4},{7,6},{5,7},{3,5},{1,3},{0,1},{10,8},{12,10},{14... | collective-permute-start | bytes 884744 | tf_op jit(solution)/shard_map/ppermute | solution.py:170
  82.6 12.2 %collective-permute-start.26 = (bf16[48,3072]{1,0:T(8,128)(2,1)S(1)}, bf16[48,3072]{1,0:T(8,128)(2,1)S(1)}, u32[]{:S(2)}, u32[]{:S(2)}) collective-permute-start(bf16[48,3072]{1,0:T(8,128)(2,1)S(1)} %add_convert_fusion.4), channel_id=1, source_target_pairs={{0,2},{2,4},{4,6},{6,7},{7,5},{5,3},{3,1},{1,0},{8,10},{10,12},{12... | collective-permute-start | bytes 884744 | tf_op jit(solution)/shard_map/ppermute | solution.py:170
  88.5 9.7 %collective-permute-start.20 = (bf16[48,3072]{1,0:T(8,128)(2,1)S(1)}, bf16[48,3072]{1,0:T(8,128)(2,1)S(1)}, u32[]{:S(2)}, u32[]{:S(2)}) collective-permute-start(bf16[48,3072]{1,0:T(8,128)(2,1)S(1)} %add_convert_fusion.8), channel_id=1, source_target_pairs={{2,0},{4,2},{6,4},{7,6},{5,7},{3,5},{1,3},{0,1},{10,8},{12,10},{14... | collective-permute-start | bytes 884744 | tf_op jit(solution)/shard_map/ppermute | solution.py:170
  88.9 10.3 %collective-permute-start.19 = (bf16[48,3072]{1,0:T(8,128)(2,1)S(1)}, bf16[48,3072]{1,0:T(8,128)(2,1)S(1)}, u32[]{:S(2)}, u32[]{:S(2)}) collective-permute-start(bf16[48,3072]{1,0:T(8,128)(2,1)S(1)} %add_convert_fusion.9), channel_id=1, source_target_pairs={{0,2},{2,4},{4,6},{6,7},{7,5},{5,3},{3,1},{1,0},{8,10},{10,12},{12... | collective-permute-start | bytes 884744 | tf_op jit(solution)/shard_map/ppermute | solution.py:170
  94.8 7.9 %collective-permute-start.28 = (bf16[48,3072]{1,0:T(8,128)(2,1)S(1)}, bf16[48,3072]{1,0:T(8,128)(2,1)S(1)}, u32[]{:S(2)}, u32[]{:S(2)}) collective-permute-start(bf16[48,3072]{1,0:T(8,128)(2,1)S(1)} %add_convert_fusion.2), channel_id=1, source_target_pairs={{0,2},{2,4},{4,6},{6,7},{7,5},{5,3},{3,1},{1,0},{8,10},{10,12},{12... | collective-permute-start | bytes 884744 | tf_op jit(solution)/shard_map/ppermute | solution.py:268
  99.2 6.8 %collective-permute-start.21 = (bf16[48,3072]{1,0:T(8,128)(2,1)S(1)}, bf16[48,3072]{1,0:T(8,128)(2,1)S(1)}, u32[]{:S(2)}, u32[]{:S(2)}) collective-permute-start(bf16[48,3072]{1,0:T(8,128)(2,1)S(1)} %add_convert_fusion.7), channel_id=1, source_target_pairs={{2,0},{4,2},{6,4},{7,6},{5,7},{3,5},{1,3},{0,1},{10,8},{12,10},{14... | collective-permute-start | bytes 884744 | tf_op jit(solution)/shard_map/ppermute | solution.py:269
  102.8 1.4 %collective-permute-start.29 = (bf16[24,3072]{1,0:T(8,128)(2,1)S(1)}, bf16[24,3072]{1,0:T(8,128)(2,1)S(1)}, u32[]{:S(2)}, u32[]{:S(2)}) collective-permute-start(bf16[24,3072]{1,0:T(8,128)(2,1)S(1)} %get-tuple-element.157), channel_id=1, source_target_pairs={{0,8},{8,0},{1,9},{9,1},{2,10},{10,2},{3,11},{11,3},{4,12},{12,4},... | collective-permute-start | bytes 442376 | tf_op jit(solution)/shard_map/ppermute | solution.py:279
  106.1 1.4 %collective-permute-start.30 = (bf16[24,3072]{1,0:T(8,128)(2,1)S(1)}, bf16[24,3072]{1,0:T(8,128)(2,1)S(1)}, u32[]{:S(2)}, u32[]{:S(2)}) collective-permute-start(bf16[24,3072]{1,0:T(8,128)(2,1)S(1)} %get-tuple-element.155), channel_id=1, source_target_pairs={{0,8},{8,0},{1,9},{9,1},{2,10},{10,2},{3,11},{11,3},{4,12},{12,4},... | collective-permute-start | bytes 442376 | tf_op jit(solution)/shard_map/ppermute | solution.py:279

commit v19 on v18

--- a/solution.py
+++ b/solution.py
@@ -7,7 +7,7 @@
 from jax.sharding import PartitionSpec as P
 
 CAP = 24
-COPIES = 16
+COPIES = 32
 TILE = 512
 MARGIN = 3 * 2**20
 CHEAP = pl.CostEstimate(flops=1024, bytes_accessed=1024, transcendentals=0)
@@ -39,12 +39,12 @@
 
 
 def row_copies(source, target, done, column=0):
-    rows, width = source.shape[1] // COPIES, target.shape[2]
+    rows, width = max(16, source.shape[1] // COPIES), target.shape[2]
     return [
         pltpu.make_async_copy(
             source.at[:, pl.ds(i * rows, rows), pl.ds(column, width)], target.at[:, pl.ds(i * rows, rows)], done.at[i]
         )
-        for i in range(COPIES)
+        for i in range(source.shape[1] // rows)
     ]
 
 

time: 109 us -> 109 us (level)
  transfers between devices with their start and end apart: 31 -> 31, of which waited for: 21 -> 20; matrix products, arithmetic and copies ran while one was open for 1% -> 1% of each run, Pallas kernels for 25% -> 26%
where the time goes in v19:
time: 109 us
  waiting for transfers between devices  40.3 us (37%)
  Pallas kernels  33.8 us (31%)
  starting transfers between devices  31.7 us (29%)
  other arithmetic  2.25 us (2%)
    pallas_call x9, Pallas kernels, call(): pl.pallas_call(kernel, in_specs=[pl.BlockSpec(memory_space=memory) for _,...  31.6 us
    ppermute x13, waiting for transfers between devices, step(): lax.ppermute(to_left, 'tensor', left)  26.4 us
    ppermute x13, starting transfers between devices, step(): lax.ppermute(to_right, 'tensor', right)  24.6 us
    ppermute x13, waiting for transfers between devices, step(): lax.ppermute(to_right, 'tensor', right)  7.29 us
    ppermute x13, starting transfers between devices, step(): lax.ppermute(to_left, 'tensor', left)  3.51 us
    ppermute x2, waiting for transfers between devices, per_device(): swapped = lax.ppermute(total[CAP:], 'expert', swap)  2.59 us
  transfers between devices with their start and end apart: 31, of which 20 were waited for; matrix products, arithmetic and copies ran while one was open for 1% of the time, Pallas kernels for 26%

profile of v19, /device:TPU:0, one launch (start us, length us, event | category | flops | bytes accessed | tf_op | source)
XLA Modules:
  0.0 109.1 jit_solution(10621869067064175750)
XLA Ops:
  0.1 0.8 compare_reduce_fusion
  0.9 0.1 copy.22
  1.0 0.1 reduce_window_sum.11
  1.4 0.3 convolution_convert_fusion
  1.7 0.5 collective-permute-start
  2.2 1.2 %collective-permute-done = bf16[24,6144]{1,0:T(8,128)(2,1)S(1)} collective-permute-done((bf16[24,6144]{1,0:T(8,128)(2,1)S(1)}, bf16[24,6144]{1,0:T(8,128)(2,1)S(1)}, u32[]{:S(2)}, u32[]{:S(2)}) %collective-permute-start) | collective-permute-done | bytes 294944 | tf_op jit(solution)/shard_map/ppermute | solution.py:184
  3.5 3.0 %collective-permute-start.1 = (bf16[48,3072]{1,0:T(8,128)(2,1)S(1)}, bf16[48,3072]{1,0:T(8,128)(2,1)S(1)}, u32[]{:S(2)}, u32[]{:S(2)}) collective-permute-start(bf16[48,3072]{1,0:T(8,128)(2,1)S(1)} %get-tuple-element.152.refs_0_), channel_id=1, source_target_pairs={{0,2},{2,4},{4,6},{6,7},{7,5},{5,3},{3,1},{1,0},{8,10},{10,12},{12... | collective-permute-start | bytes 884744 | tf_op jit(solution)/shard_map/ppermute | solution.py:170
  6.6 2.0 %collective-permute-start.3 = (bf16[48,3072]{1,0:T(8,128)(2,1)S(1)}, bf16[48,3072]{1,0:T(8,128)(2,1)S(1)}, u32[]{:S(2)}, u32[]{:S(2)}) collective-permute-start(bf16[48,3072]{1,0:T(8,128)(2,1)S(1)} %get-tuple-element.151.refs_5_), channel_id=1, source_target_pairs={{0,2},{2,4},{4,6},{6,7},{7,5},{5,3},{3,1},{1,0},{8,10},{10,12},{12... | collective-permute-start | bytes 884744 | tf_op jit(solution)/shard_map/ppermute | solution.py:170
  8.6 4.8 %fetched.3.refs_10_.refs_6_ = bf16[1,6144,1024]{2,1,0:T(8,128)(2,1)S(1)} custom-call(bf16[1,6144,1024]{2,1,0:T(8,128)(2,1)} %source), custom_call_target="tpu_custom_call" | custom-call | flops 1024 | bytes 1024 | tf_op jit(solution)/shard_map/fetched/pallas_call | solution.py:29
  13.4 0.9 collective-permute-done.1.refs_1_
  14.3 2.2 %collective-permute-done.2.refs_7_ = bf16[48,3072]{1,0:T(8,128)(2,1)S(1)} collective-permute-done((bf16[48,3072]{1,0:T(8,128)(2,1)S(1)}, bf16[48,3072]{1,0:T(8,128)(2,1)S(1)}, u32[]{:S(2)}, u32[]{:S(2)}) %collective-permute-start.2) | collective-permute-done | bytes 294944 | tf_op jit(solution)/shard_map/ppermute | solution.py:170
  16.4 1.6 %collective-permute-start.5 = (bf16[48,3072]{1,0:T(8,128)(2,1)S(1)}, bf16[48,3072]{1,0:T(8,128)(2,1)S(1)}, u32[]{:S(2)}, u32[]{:S(2)}) collective-permute-start(bf16[48,3072]{1,0:T(8,128)(2,1)S(1)} %collective-permute-done.1.refs_1_), channel_id=1, source_target_pairs={{0,2},{2,4},{4,6},{6,7},{7,5},{5,3},{3,1},{1,0},{8,10},{10,12},{12... | collective-permute-start | bytes 884744 | tf_op jit(solution)/shard_map/ppermute | solution.py:170
  18.0 0.4 collective-permute-start.6
  18.5 4.8 %fetched.4.refs_10_.refs_7_ = bf16[1,6144,1024]{2,1,0:T(8,128)(2,1)S(1)} custom-call(bf16[1,6144,1024]{2,1,0:T(8,128)(2,1)} %source.1), custom_call_target="tpu_custom_call" | custom-call | flops 1024 | bytes 1024 | tf_op jit(solution)/shard_map/fetched/pallas_call | solution.py:29
  23.3 1.6 %collective-permute-start.7 = (bf16[48,3072]{1,0:T(8,128)(2,1)S(1)}, bf16[48,3072]{1,0:T(8,128)(2,1)S(1)}, u32[]{:S(2)}, u32[]{:S(2)}) collective-permute-start(bf16[48,3072]{1,0:T(8,128)(2,1)S(1)} %collective-permute-done.3.refs_6_), channel_id=1, source_target_pairs={{0,2},{2,4},{4,6},{6,7},{7,5},{5,3},{3,1},{1,0},{8,10},{10,12},{12... | collective-permute-start | bytes 884744 | tf_op jit(solution)/shard_map/ppermute | solution.py:170
  25.0 0.4 collective-permute-start.8
  25.4 1.5 %collective-permute-done.5.refs_3_ = bf16[48,3072]{1,0:T(8,128)(2,1)S(1)} collective-permute-done((bf16[48,3072]{1,0:T(8,128)(2,1)S(1)}, bf16[48,3072]{1,0:T(8,128)(2,1)S(1)}, u32[]{:S(2)}, u32[]{:S(2)}) %collective-permute-start.5) | collective-permute-done | bytes 294944 | tf_op jit(solution)/shard_map/ppermute | solution.py:170
  26.9 2.2 %collective-permute-done.6.refs_9_ = bf16[48,3072]{1,0:T(8,128)(2,1)S(1)} collective-permute-done((bf16[48,3072]{1,0:T(8,128)(2,1)S(1)}, bf16[48,3072]{1,0:T(8,128)(2,1)S(1)}, u32[]{:S(2)}, u32[]{:S(2)}) %collective-permute-start.6) | collective-permute-done | bytes 294944 | tf_op jit(solution)/shard_map/ppermute | solution.py:170
  29.1 2.0 %collective-permute-start.9 = (bf16[48,3072]{1,0:T(8,128)(2,1)S(1)}, bf16[48,3072]{1,0:T(8,128)(2,1)S(1)}, u32[]{:S(2)}, u32[]{:S(2)}) collective-permute-start(bf16[48,3072]{1,0:T(8,128)(2,1)S(1)} %collective-permute-done.5.refs_3_), channel_id=1, source_target_pairs={{0,2},{2,4},{4,6},{6,7},{7,5},{5,3},{3,1},{1,0},{8,10},{10,12},{12... | collective-permute-start | bytes 884744 | tf_op jit(solution)/shard_map/ppermute | solution.py:170
  31.1 2.2 %collective-permute-done.7.refs_8_ = bf16[48,3072]{1,0:T(8,128)(2,1)S(1)} collective-permute-done((bf16[48,3072]{1,0:T(8,128)(2,1)S(1)}, bf16[48,3072]{1,0:T(8,128)(2,1)S(1)}, u32[]{:S(2)}, u32[]{:S(2)}) %collective-permute-start.7) | collective-permute-done | bytes 294944 | tf_op jit(solution)/shard_map/ppermute | solution.py:170
  33.3 2.1 %collective-permute-done.8.refs_4_ = bf16[48,3072]{1,0:T(8,128)(2,1)S(1)} collective-permute-done((bf16[48,3072]{1,0:T(8,128)(2,1)S(1)}, bf16[48,3072]{1,0:T(8,128)(2,1)S(1)}, u32[]{:S(2)}, u32[]{:S(2)}) %collective-permute-start.8) | collective-permute-done | bytes 294944 | tf_op jit(solution)/shard_map/ppermute | solution.py:170
  35.4 3.2 %near_gate.1.refs_11_ = f32[240,1024]{1,0:T(8,128)S(1)} custom-call(bf16[48,3072]{1,0:T(8,128)(2,1)S(1)} %get-tuple-element.152.refs_0_, bf16[48,3072]{1,0:T(8,128)(2,1)S(1)} %collective-permute-done.1.refs_1_, bf16[48,3072]{1,0:T(8,128)(2,1)S(1)} %collective-permute-done.4.refs_2_, bf16[48,3072]{1,0:T(8,128)(2,1)S(1)} %collective-permute-done.5.refs_3_, ...), custom_call_target="tpu_custom_call" | custom-call | flops 1024 | bytes 1024 | tf_op jit(solution)/shard_map/near_gate/pallas_call | solution.py:29
  38.6 1.6 %collective-permute-start.11 = (bf16[48,3072]{1,0:T(8,128)(2,1)S(1)}, bf16[48,3072]{1,0:T(8,128)(2,1)S(1)}, u32[]{:S(2)}, u32[]{:S(2)}) collective-permute-start(bf16[48,3072]{1,0:T(8,128)(2,1)S(1)} %collective-permute-done.7.refs_8_), channel_id=1, source_target_pairs={{0,2},{2,4},{4,6},{6,7},{7,5},{5,3},{3,1},{1,0},{8,10},{10,12},{12... | collective-permute-start | bytes 884744 | tf_op jit(solution)/shard_map/ppermute | solution.py:170
  40.2 0.4 collective-permute-start.12
  40.7 1.6 %collective-permute-start.13 = (bf16[48,3072]{1,0:T(8,128)(2,1)S(1)}, bf16[48,3072]{1,0:T(8,128)(2,1)S(1)}, u32[]{:S(2)}, u32[]{:S(2)}) collective-permute-start(bf16[48,3072]{1,0:T(8,128)(2,1)S(1)} %collective-permute-done.9.refs_0_), channel_id=1, source_target_pairs={{0,2},{2,4},{4,6},{6,7},{7,5},{5,3},{3,1},{1,0},{8,10},{10,12},{12... | collective-permute-start | bytes 884744 | tf_op jit(solution)/shard_map/ppermute | solution.py:170
  42.3 0.4 collective-permute-start.14
  42.7 3.2 %near_up.1.hidden = bf16[240,1024]{1,0:T(8,128)(2,1)S(1)} custom-call(bf16[48,3072]{1,0:T(8,128)(2,1)S(1)} %get-tuple-element.152.refs_0_, bf16[48,3072]{1,0:T(8,128)(2,1)S(1)} %collective-permute-done.1.refs_1_, bf16[48,3072]{1,0:T(8,128)(2,1)S(1)} %collective-permute-done.4.refs_2_, bf16[48,3072]{1,0:T(8,128)(2,1)S(1)} %collective-permute-done.5.refs_3_, ...), custom_call_target="tpu_custom_call" | custom-call | flops 1024 | bytes 1024 | tf_op jit(solution)/shard_map/near_up/pallas_call | solution.py:29
  46.0 3.2 %fetched.5.refs_8_.down = bf16[1,1024,3072]{2,1,0:T(8,128)(2,1)S(1)} custom-call(bf16[1,1024,6144]{2,1,0:T(8,128)(2,1)} %w_down), custom_call_target="tpu_custom_call" | custom-call | flops 1024 | bytes 1024 | tf_op jit(solution)/shard_map/fetched/pallas_call | solution.py:29
  49.2 0.9 collective-permute-done.12.refs_1_
  50.1 1.7 %collective-permute-done.13.refs_2_ = bf16[48,3072]{1,0:T(8,128)(2,1)S(1)} collective-permute-done((bf16[48,3072]{1,0:T(8,128)(2,1)S(1)}, bf16[48,3072]{1,0:T(8,128)(2,1)S(1)}, u32[]{:S(2)}, u32[]{:S(2)}) %collective-permute-start.13) | collective-permute-done | bytes 294944 | tf_op jit(solution)/shard_map/ppermute | solution.py:170
  51.7 1.5 %collective-permute-done.14.refs_5_ = bf16[48,3072]{1,0:T(8,128)(2,1)S(1)} collective-permute-done((bf16[48,3072]{1,0:T(8,128)(2,1)S(1)}, bf16[48,3072]{1,0:T(8,128)(2,1)S(1)}, u32[]{:S(2)}, u32[]{:S(2)}) %collective-permute-start.14) | collective-permute-done | bytes 294944 | tf_op jit(solution)/shard_map/ppermute | solution.py:170
  53.2 4.8 %rest_first.1 = (bf16[48,3072]{1,0:T(8,128)(2,1)S(1)}, bf16[48,3072]{1,0:T(8,128)(2,1)S(1)}, bf16[48,3072]{1,0:T(8,128)(2,1)S(1)}, bf16[144,1024]{1,0:T(8,128)(2,1)S(1)}) custom-call(bf16[48,3072]{1,0:T(8,128)(2,1)S(1)} %collective-permute-done.9.refs_0_, bf16[48,3072]{1,0:T(8,128)(2,1)S(1)} %collective-permute-done.12.refs_1_, ...), custom_call_target="tpu_custom_call" | custom-call | flops 1024 | bytes 1024 | tf_op jit(solution)/shard_map/rest_first/pallas_call | solution.py:29
  58.0 1.8 %collective-permute-start.22 = (bf16[48,3072]{1,0:T(8,128)(2,1)S(1)}, bf16[48,3072]{1,0:T(8,128)(2,1)S(1)}, u32[]{:S(2)}, u32[]{:S(2)}) collective-permute-start(bf16[48,3072]{1,0:T(8,128)(2,1)S(1)} %get-tuple-element.139), channel_id=1, source_target_pairs={{0,2},{2,4},{4,6},{6,7},{7,5},{5,3},{3,1},{1,0},{8,10},{10,12},{12... | collective-permute-start | bytes 884744 | tf_op jit(solution)/shard_map/ppermute | solution.py:170
  59.8 0.4 collective-permute-start.23
  60.3 4.2 %rest_second.1 = (bf16[48,3072]{1,0:T(8,128)(2,1)S(1)}, bf16[48,3072]{1,0:T(8,128)(2,1)S(1)}, bf16[48,3072]{1,0:T(8,128)(2,1)S(1)}, bf16[1,1024,3072]{2,1,0:T(8,128)(2,1)S(1)}) custom-call(bf16[144,1024]{1,0:T(8,128)(2,1)S(1)} %get-tuple-element.118.hidden, bf16[1,1024,6144]{2,1,0:T(8,128)(2,1)} %w_down), custom_call_target="tpu_custom_call" | custom-call | flops 1024 | bytes 1024 | tf_op jit(solution)/shard_map/rest_second/pallas_call | solution.py:29
  64.6 1.6 %collective-permute-start.15 = (bf16[48,3072]{1,0:T(8,128)(2,1)S(1)}, bf16[48,3072]{1,0:T(8,128)(2,1)S(1)}, u32[]{:S(2)}, u32[]{:S(2)}) collective-permute-start(bf16[48,3072]{1,0:T(8,128)(2,1)S(1)} %get-tuple-element.119), channel_id=1, source_target_pairs={{0,2},{2,4},{4,6},{6,7},{7,5},{5,3},{3,1},{1,0},{8,10},{10,12},{12... | collective-permute-start | bytes 884744 | tf_op jit(solution)/shard_map/ppermute | solution.py:170
  66.2 0.4 collective-permute-start.16
  66.7 1.7 %near_down.3 = (bf16[48,3072]{1,0:T(8,128)(2,1)S(1)}, bf16[48,3072]{1,0:T(8,128)(2,1)S(1)}, bf16[48,3072]{1,0:T(8,128)(2,1)S(1)}, bf16[48,3072]{1,0:T(8,128)(2,1)S(1)}, bf16[48,3072]{1,0:T(8,128)(2,1)S(1)}) custom-call(bf16[240,1024]{1,0:T(8,128)(2,1)S(1)} %near_up.1.hidden, bf16[1,1024,3072]{2,1,0:T(8,128)(2,1)S(1)} %fetched.5.refs_8_.down), custom_call_target="tpu_custom_call" | custom-call | flops 1024 | bytes 1024 | tf_op jit(solution)/shard_map/near_down/pallas_call | solution.py:29
  68.4 1.7 %near_down.2 = (bf16[48,3072]{1,0:T(8,128)(2,1)S(1)}, bf16[48,3072]{1,0:T(8,128)(2,1)S(1)}, bf16[48,3072]{1,0:T(8,128)(2,1)S(1)}, bf16[48,3072]{1,0:T(8,128)(2,1)S(1)}, bf16[48,3072]{1,0:T(8,128)(2,1)S(1)}) custom-call(bf16[240,1024]{1,0:T(8,128)(2,1)S(1)} %near_up.1.hidden, bf16[1,1024,3072]{2,1,0:T(8,128)(2,1)S(1)} %get-tuple-element.122.down), custom_call_target="tpu_custom_call" | custom-call | flops 1024 | bytes 1024 | tf_op jit(solution)/shard_map/near_down/pallas_call | solution.py:29
  70.2 0.4 collective-permute-start.25
  70.6 1.8 %collective-permute-start.24 = (bf16[48,3072]{1,0:T(8,128)(2,1)S(1)}, bf16[48,3072]{1,0:T(8,128)(2,1)S(1)}, u32[]{:S(2)}, u32[]{:S(2)}) collective-permute-start(bf16[48,3072]{1,0:T(8,128)(2,1)S(1)} %add_convert_fusion.6), channel_id=1, source_target_pairs={{0,2},{2,4},{4,6},{6,7},{7,5},{5,3},{3,1},{1,0},{8,10},{10,12},{12... | collective-permute-start | bytes 884744 | tf_op jit(solution)/shard_map/ppermute | solution.py:170
  72.4 3.8 %collective-permute-done.16 = bf16[48,3072]{1,0:T(8,128)(2,1)S(1)} collective-permute-done((bf16[48,3072]{1,0:T(8,128)(2,1)S(1)}, bf16[48,3072]{1,0:T(8,128)(2,1)S(1)}, u32[]{:S(2)}, u32[]{:S(2)}) %collective-permute-start.16) | collective-permute-done | bytes 294944 | tf_op jit(solution)/shard_map/ppermute | solution.py:170
  76.2 0.2 collective-permute-start.18
  76.5 2.0 %collective-permute-start.17 = (bf16[48,3072]{1,0:T(8,128)(2,1)S(1)}, bf16[48,3072]{1,0:T(8,128)(2,1)S(1)}, u32[]{:S(2)}, u32[]{:S(2)}) collective-permute-start(bf16[48,3072]{1,0:T(8,128)(2,1)S(1)} %add_convert_fusion.11), channel_id=1, source_target_pairs={{0,2},{2,4},{4,6},{6,7},{7,5},{5,3},{3,1},{1,0},{8,10},{10,12},{12... | collective-permute-start | bytes 884744 | tf_op jit(solution)/shard_map/ppermute | solution.py:170
  78.5 4.0 %collective-permute-done.25 = bf16[48,3072]{1,0:T(8,128)(2,1)S(1)} collective-permute-done((bf16[48,3072]{1,0:T(8,128)(2,1)S(1)}, bf16[48,3072]{1,0:T(8,128)(2,1)S(1)}, u32[]{:S(2)}, u32[]{:S(2)}) %collective-permute-start.25) | collective-permute-done | bytes 294944 | tf_op jit(solution)/shard_map/ppermute | solution.py:170
  82.6 0.2 collective-permute-start.27
  82.8 2.0 %collective-permute-start.26 = (bf16[48,3072]{1,0:T(8,128)(2,1)S(1)}, bf16[48,3072]{1,0:T(8,128)(2,1)S(1)}, u32[]{:S(2)}, u32[]{:S(2)}) collective-permute-start(bf16[48,3072]{1,0:T(8,128)(2,1)S(1)} %add_convert_fusion.4), channel_id=1, source_target_pairs={{0,2},{2,4},{4,6},{6,7},{7,5},{5,3},{3,1},{1,0},{8,10},{10,12},{12... | collective-permute-start | bytes 884744 | tf_op jit(solution)/shard_map/ppermute | solution.py:170
  84.8 4.0 %collective-permute-done.18 = bf16[48,3072]{1,0:T(8,128)(2,1)S(1)} collective-permute-done((bf16[48,3072]{1,0:T(8,128)(2,1)S(1)}, bf16[48,3072]{1,0:T(8,128)(2,1)S(1)}, u32[]{:S(2)}, u32[]{:S(2)}) %collective-permute-start.18) | collective-permute-done | bytes 294944 | tf_op jit(solution)/shard_map/ppermute | solution.py:170
  88.9 0.2 collective-permute-start.20
  89.1 2.0 %collective-permute-start.19 = (bf16[48,3072]{1,0:T(8,128)(2,1)S(1)}, bf16[48,3072]{1,0:T(8,128)(2,1)S(1)}, u32[]{:S(2)}, u32[]{:S(2)}) collective-permute-start(bf16[48,3072]{1,0:T(8,128)(2,1)S(1)} %add_convert_fusion.9), channel_id=1, source_target_pairs={{0,2},{2,4},{4,6},{6,7},{7,5},{5,3},{3,1},{1,0},{8,10},{10,12},{12... | collective-permute-start | bytes 884744 | tf_op jit(solution)/shard_map/ppermute | solution.py:170
  91.1 3.9 %collective-permute-done.27 = bf16[48,3072]{1,0:T(8,128)(2,1)S(1)} collective-permute-done((bf16[48,3072]{1,0:T(8,128)(2,1)S(1)}, bf16[48,3072]{1,0:T(8,128)(2,1)S(1)}, u32[]{:S(2)}, u32[]{:S(2)}) %collective-permute-start.27) | collective-permute-done | bytes 294944 | tf_op jit(solution)/shard_map/ppermute | solution.py:170
  95.0 1.6 %collective-permute-start.28 = (bf16[48,3072]{1,0:T(8,128)(2,1)S(1)}, bf16[48,3072]{1,0:T(8,128)(2,1)S(1)}, u32[]{:S(2)}, u32[]{:S(2)}) collective-permute-start(bf16[48,3072]{1,0:T(8,128)(2,1)S(1)} %add_convert_fusion.2), channel_id=1, source_target_pairs={{0,2},{2,4},{4,6},{6,7},{7,5},{5,3},{3,1},{1,0},{8,10},{10,12},{12... | collective-permute-start | bytes 884744 | tf_op jit(solution)/shard_map/ppermute | solution.py:268
  96.7 1.9 %collective-permute-done.20 = bf16[48,3072]{1,0:T(8,128)(2,1)S(1)} collective-permute-done((bf16[48,3072]{1,0:T(8,128)(2,1)S(1)}, bf16[48,3072]{1,0:T(8,128)(2,1)S(1)}, u32[]{:S(2)}, u32[]{:S(2)}) %collective-permute-start.20) | collective-permute-done | bytes 294944 | tf_op jit(solution)/shard_map/ppermute | solution.py:170
  98.6 1.0 collective-permute-done.19
  99.6 1.3 %collective-permute-start.21 = (bf16[48,3072]{1,0:T(8,128)(2,1)S(1)}, bf16[48,3072]{1,0:T(8,128)(2,1)S(1)}, u32[]{:S(2)}, u32[]{:S(2)}) collective-permute-start(bf16[48,3072]{1,0:T(8,128)(2,1)S(1)} %add_convert_fusion.7), channel_id=1, source_target_pairs={{2,0},{4,2},{6,4},{7,6},{5,7},{3,5},{1,3},{0,1},{10,8},{12,10},{14... | collective-permute-start | bytes 884744 | tf_op jit(solution)/shard_map/ppermute | solution.py:269
  100.9 2.0 %collective-permute-done.28 = bf16[48,3072]{1,0:T(8,128)(2,1)S(1)} collective-permute-done((bf16[48,3072]{1,0:T(8,128)(2,1)S(1)}, bf16[48,3072]{1,0:T(8,128)(2,1)S(1)}, u32[]{:S(2)}, u32[]{:S(2)}) %collective-permute-start.28) | collective-permute-done | bytes 294944 | tf_op jit(solution)/shard_map/ppermute | solution.py:268
  103.0 0.1 add_convert_fusion.1
  103.2 0.1 select_convert_fusion.weights
  103.3 1.2 %collective-permute-done.29.swapped = bf16[24,3072]{1,0:T(8,128)(2,1)S(1)} collective-permute-done((bf16[24,3072]{1,0:T(8,128)(2,1)S(1)}, bf16[24,3072]{1,0:T(8,128)(2,1)S(1)}, u32[]{:S(2)}, u32[]{:S(2)}) %collective-permute-start.29) | collective-permute-done | bytes 147488 | tf_op jit(solution)/shard_map/ppermute | solution.py:279
  104.5 1.1 combined.2.refs_0_
  105.6 0.8 collective-permute-done.21
  106.4 0.1 add_convert_fusion
  106.6 1.4 %collective-permute-done.30.swapped = bf16[24,3072]{1,0:T(8,128)(2,1)S(1)} collective-permute-done((bf16[24,3072]{1,0:T(8,128)(2,1)S(1)}, bf16[24,3072]{1,0:T(8,128)(2,1)S(1)}, u32[]{:S(2)}, u32[]{:S(2)}) %collective-permute-start.30) | collective-permute-done | bytes 147488 | tf_op jit(solution)/shard_map/ppermute | solution.py:279
  108.0 1.1 combined.3
  (47 shorter events, 1.5 us)
Async XLA Ops:
  0.0 1.4 %copy-start = (bf16[64,6144]{1,0:T(8,128)(2,1)S(1)}, bf16[64,6144]{1,0:T(8,128)(2,1)}, u32[]{:S(2)}) copy-start(bf16[64,6144]{1,0:T(8,128)(2,1)} %param.6) | copy-start | bytes 2359300
  1.7 1.7 %collective-permute-start = (bf16[24,6144]{1,0:T(8,128)(2,1)S(1)}, bf16[24,6144]{1,0:T(8,128)(2,1)S(1)}, u32[]{:S(2)}, u32[]{:S(2)}) collective-permute-start(bf16[24,6144]{1,0:T(8,128)(2,1)S(1)} %get-tuple-element.154), channel_id=1, source_target_pairs={{0,8},{8,0},{1,9},{9,1},{2,10},{10,2},{3,11},{11,3},{4,12},{12,4},... | collective-permute-start | bytes 884744 | tf_op jit(solution)/shard_map/ppermute | solution.py:184
  3.5 10.7 %collective-permute-start.1 = (bf16[48,3072]{1,0:T(8,128)(2,1)S(1)}, bf16[48,3072]{1,0:T(8,128)(2,1)S(1)}, u32[]{:S(2)}, u32[]{:S(2)}) collective-permute-start(bf16[48,3072]{1,0:T(8,128)(2,1)S(1)} %get-tuple-element.152.refs_0_), channel_id=1, source_target_pairs={{0,2},{2,4},{4,6},{6,7},{7,5},{5,3},{3,1},{1,0},{8,10},{10,12},{12... | collective-permute-start | bytes 884744 | tf_op jit(solution)/shard_map/ppermute | solution.py:170
  6.5 9.9 %collective-permute-start.2 = (bf16[48,3072]{1,0:T(8,128)(2,1)S(1)}, bf16[48,3072]{1,0:T(8,128)(2,1)S(1)}, u32[]{:S(2)}, u32[]{:S(2)}) collective-permute-start(bf16[48,3072]{1,0:T(8,128)(2,1)S(1)} %get-tuple-element.151.refs_5_), channel_id=1, source_target_pairs={{2,0},{4,2},{6,4},{7,6},{5,7},{3,5},{1,3},{0,1},{10,8},{12,10},{14... | collective-permute-start | bytes 884744 | tf_op jit(solution)/shard_map/ppermute | solution.py:170
  6.6 16.8 %collective-permute-start.3 = (bf16[48,3072]{1,0:T(8,128)(2,1)S(1)}, bf16[48,3072]{1,0:T(8,128)(2,1)S(1)}, u32[]{:S(2)}, u32[]{:S(2)}) collective-permute-start(bf16[48,3072]{1,0:T(8,128)(2,1)S(1)} %get-tuple-element.151.refs_5_), channel_id=1, source_target_pairs={{0,2},{2,4},{4,6},{6,7},{7,5},{5,3},{3,1},{1,0},{8,10},{10,12},{12... | collective-permute-start | bytes 884744 | tf_op jit(solution)/shard_map/ppermute | solution.py:170
  8.6 14.8 %collective-permute-start.4 = (bf16[48,3072]{1,0:T(8,128)(2,1)S(1)}, bf16[48,3072]{1,0:T(8,128)(2,1)S(1)}, u32[]{:S(2)}, u32[]{:S(2)}) collective-permute-start(bf16[48,3072]{1,0:T(8,128)(2,1)S(1)} %get-tuple-element.152.refs_0_), channel_id=1, source_target_pairs={{2,0},{4,2},{6,4},{7,6},{5,7},{3,5},{1,3},{0,1},{10,8},{12,10},{14... | collective-permute-start | bytes 884744 | tf_op jit(solution)/shard_map/ppermute | solution.py:170
  16.4 10.5 %collective-permute-start.5 = (bf16[48,3072]{1,0:T(8,128)(2,1)S(1)}, bf16[48,3072]{1,0:T(8,128)(2,1)S(1)}, u32[]{:S(2)}, u32[]{:S(2)}) collective-permute-start(bf16[48,3072]{1,0:T(8,128)(2,1)S(1)} %collective-permute-done.1.refs_1_), channel_id=1, source_target_pairs={{0,2},{2,4},{4,6},{6,7},{7,5},{5,3},{3,1},{1,0},{8,10},{10,12},{12... | collective-permute-start | bytes 884744 | tf_op jit(solution)/shard_map/ppermute | solution.py:170
  18.0 11.1 %collective-permute-start.6 = (bf16[48,3072]{1,0:T(8,128)(2,1)S(1)}, bf16[48,3072]{1,0:T(8,128)(2,1)S(1)}, u32[]{:S(2)}, u32[]{:S(2)}) collective-permute-start(bf16[48,3072]{1,0:T(8,128)(2,1)S(1)} %collective-permute-done.2.refs_7_), channel_id=1, source_target_pairs={{2,0},{4,2},{6,4},{7,6},{5,7},{3,5},{1,3},{0,1},{10,8},{12,10},{14... | collective-permute-start | bytes 884744 | tf_op jit(solution)/shard_map/ppermute | solution.py:170
  23.3 10.0 %collective-permute-start.7 = (bf16[48,3072]{1,0:T(8,128)(2,1)S(1)}, bf16[48,3072]{1,0:T(8,128)(2,1)S(1)}, u32[]{:S(2)}, u32[]{:S(2)}) collective-permute-start(bf16[48,3072]{1,0:T(8,128)(2,1)S(1)} %collective-permute-done.3.refs_6_), channel_id=1, source_target_pairs={{0,2},{2,4},{4,6},{6,7},{7,5},{5,3},{3,1},{1,0},{8,10},{10,12},{12... | collective-permute-start | bytes 884744 | tf_op jit(solution)/shard_map/ppermute | solution.py:170
  25.0 10.4 %collective-permute-start.8 = (bf16[48,3072]{1,0:T(8,128)(2,1)S(1)}, bf16[48,3072]{1,0:T(8,128)(2,1)S(1)}, u32[]{:S(2)}, u32[]{:S(2)}) collective-permute-start(bf16[48,3072]{1,0:T(8,128)(2,1)S(1)} %collective-permute-done.4.refs_2_), channel_id=1, source_target_pairs={{2,0},{4,2},{6,4},{7,6},{5,7},{3,5},{1,3},{0,1},{10,8},{12,10},{14... | collective-permute-start | bytes 884744 | tf_op jit(solution)/shard_map/ppermute | solution.py:170
  29.1 11.6 %collective-permute-start.10 = (bf16[48,3072]{1,0:T(8,128)(2,1)S(1)}, bf16[48,3072]{1,0:T(8,128)(2,1)S(1)}, u32[]{:S(2)}, u32[]{:S(2)}) collective-permute-start(bf16[48,3072]{1,0:T(8,128)(2,1)S(1)} %collective-permute-done.6.refs_9_), channel_id=1, source_target_pairs={{2,0},{4,2},{6,4},{7,6},{5,7},{3,5},{1,3},{0,1},{10,8},{12,10},{14... | collective-permute-start | bytes 884744 | tf_op jit(solution)/shard_map/ppermute | solution.py:170
  29.1 11.6 %collective-permute-start.9 = (bf16[48,3072]{1,0:T(8,128)(2,1)S(1)}, bf16[48,3072]{1,0:T(8,128)(2,1)S(1)}, u32[]{:S(2)}, u32[]{:S(2)}) collective-permute-start(bf16[48,3072]{1,0:T(8,128)(2,1)S(1)} %collective-permute-done.5.refs_3_), channel_id=1, source_target_pairs={{0,2},{2,4},{4,6},{6,7},{7,5},{5,3},{3,1},{1,0},{8,10},{10,12},{12... | collective-permute-start | bytes 884744 | tf_op jit(solution)/shard_map/ppermute | solution.py:170
  38.6 10.6 %collective-permute-start.11 = (bf16[48,3072]{1,0:T(8,128)(2,1)S(1)}, bf16[48,3072]{1,0:T(8,128)(2,1)S(1)}, u32[]{:S(2)}, u32[]{:S(2)}) collective-permute-start(bf16[48,3072]{1,0:T(8,128)(2,1)S(1)} %collective-permute-done.7.refs_8_), channel_id=1, source_target_pairs={{0,2},{2,4},{4,6},{6,7},{7,5},{5,3},{3,1},{1,0},{8,10},{10,12},{12... | collective-permute-start | bytes 884744 | tf_op jit(solution)/shard_map/ppermute | solution.py:170
  40.2 9.8 %collective-permute-start.12 = (bf16[48,3072]{1,0:T(8,128)(2,1)S(1)}, bf16[48,3072]{1,0:T(8,128)(2,1)S(1)}, u32[]{:S(2)}, u32[]{:S(2)}) collective-permute-start(bf16[48,3072]{1,0:T(8,128)(2,1)S(1)} %collective-permute-done.8.refs_4_), channel_id=1, source_target_pairs={{2,0},{4,2},{6,4},{7,6},{5,7},{3,5},{1,3},{0,1},{10,8},{12,10},{14... | collective-permute-start | bytes 884744 | tf_op jit(solution)/shard_map/ppermute | solution.py:170
  40.7 11.0 %collective-permute-start.13 = (bf16[48,3072]{1,0:T(8,128)(2,1)S(1)}, bf16[48,3072]{1,0:T(8,128)(2,1)S(1)}, u32[]{:S(2)}, u32[]{:S(2)}) collective-permute-start(bf16[48,3072]{1,0:T(8,128)(2,1)S(1)} %collective-permute-done.9.refs_0_), channel_id=1, source_target_pairs={{0,2},{2,4},{4,6},{6,7},{7,5},{5,3},{3,1},{1,0},{8,10},{10,12},{12... | collective-permute-start | bytes 884744 | tf_op jit(solution)/shard_map/ppermute | solution.py:170
  42.3 10.9 %collective-permute-start.14 = (bf16[48,3072]{1,0:T(8,128)(2,1)S(1)}, bf16[48,3072]{1,0:T(8,128)(2,1)S(1)}, u32[]{:S(2)}, u32[]{:S(2)}) collective-permute-start(bf16[48,3072]{1,0:T(8,128)(2,1)S(1)} %collective-permute-done.10.refs_4_), channel_id=1, source_target_pairs={{2,0},{4,2},{6,4},{7,6},{5,7},{3,5},{1,3},{0,1},{10,8},{12,10},{14... | collective-permute-start | bytes 884744 | tf_op jit(solution)/shard_map/ppermute | solution.py:170
  49.1 11.1 %copy-start.2 = (s32[64,2]{0,1:T(2,128)S(1)}, s32[64,2]{0,1:T(2,128)}, u32[]{:S(2)}) copy-start(s32[64,2]{0,1:T(2,128)} %param.7) | copy-start | bytes 1540
  49.1 11.1 %copy-start.3 = (f32[64,2]{0,1:T(2,128)S(1)}, f32[64,2]{0,1:T(2,128)}, u32[]{:S(2)}) copy-start(f32[64,2]{0,1:T(2,128)} %param.8) | copy-start | bytes 1540
  58.0 12.1 %collective-permute-start.22 = (bf16[48,3072]{1,0:T(8,128)(2,1)S(1)}, bf16[48,3072]{1,0:T(8,128)(2,1)S(1)}, u32[]{:S(2)}, u32[]{:S(2)}) collective-permute-start(bf16[48,3072]{1,0:T(8,128)(2,1)S(1)} %get-tuple-element.139), channel_id=1, source_target_pairs={{0,2},{2,4},{4,6},{6,7},{7,5},{5,3},{3,1},{1,0},{8,10},{10,12},{12... | collective-permute-start | bytes 884744 | tf_op jit(solution)/shard_map/ppermute | solution.py:170
  59.8 10.3 %collective-permute-start.23 = (bf16[48,3072]{1,0:T(8,128)(2,1)S(1)}, bf16[48,3072]{1,0:T(8,128)(2,1)S(1)}, u32[]{:S(2)}, u32[]{:S(2)}) collective-permute-start(bf16[48,3072]{1,0:T(8,128)(2,1)S(1)} %get-tuple-element.140), channel_id=1, source_target_pairs={{2,0},{4,2},{6,4},{7,6},{5,7},{3,5},{1,3},{0,1},{10,8},{12,10},{14... | collective-permute-start | bytes 884744 | tf_op jit(solution)/shard_map/ppermute | solution.py:170
  64.6 7.8 %collective-permute-start.15 = (bf16[48,3072]{1,0:T(8,128)(2,1)S(1)}, bf16[48,3072]{1,0:T(8,128)(2,1)S(1)}, u32[]{:S(2)}, u32[]{:S(2)}) collective-permute-start(bf16[48,3072]{1,0:T(8,128)(2,1)S(1)} %get-tuple-element.119), channel_id=1, source_target_pairs={{0,2},{2,4},{4,6},{6,7},{7,5},{5,3},{3,1},{1,0},{8,10},{10,12},{12... | collective-permute-start | bytes 884744 | tf_op jit(solution)/shard_map/ppermute | solution.py:170
  66.2 9.9 %collective-permute-start.16 = (bf16[48,3072]{1,0:T(8,128)(2,1)S(1)}, bf16[48,3072]{1,0:T(8,128)(2,1)S(1)}, u32[]{:S(2)}, u32[]{:S(2)}) collective-permute-start(bf16[48,3072]{1,0:T(8,128)(2,1)S(1)} %get-tuple-element.120), channel_id=1, source_target_pairs={{2,0},{4,2},{6,4},{7,6},{5,7},{3,5},{1,3},{0,1},{10,8},{12,10},{14... | collective-permute-start | bytes 884744 | tf_op jit(solution)/shard_map/ppermute | solution.py:170
  70.2 12.3 %collective-permute-start.25 = (bf16[48,3072]{1,0:T(8,128)(2,1)S(1)}, bf16[48,3072]{1,0:T(8,128)(2,1)S(1)}, u32[]{:S(2)}, u32[]{:S(2)}) collective-permute-start(bf16[48,3072]{1,0:T(8,128)(2,1)S(1)} %add_convert_fusion.5), channel_id=1, source_target_pairs={{2,0},{4,2},{6,4},{7,6},{5,7},{3,5},{1,3},{0,1},{10,8},{12,10},{14... | collective-permute-start | bytes 884744 | tf_op jit(solution)/shard_map/ppermute | solution.py:170
  70.6 11.9 %collective-permute-start.24 = (bf16[48,3072]{1,0:T(8,128)(2,1)S(1)}, bf16[48,3072]{1,0:T(8,128)(2,1)S(1)}, u32[]{:S(2)}, u32[]{:S(2)}) collective-permute-start(bf16[48,3072]{1,0:T(8,128)(2,1)S(1)} %add_convert_fusion.6), channel_id=1, source_target_pairs={{0,2},{2,4},{4,6},{6,7},{7,5},{5,3},{3,1},{1,0},{8,10},{10,12},{12... | collective-permute-start | bytes 884744 | tf_op jit(solution)/shard_map/ppermute | solution.py:170
  76.2 12.6 %collective-permute-start.18 = (bf16[48,3072]{1,0:T(8,128)(2,1)S(1)}, bf16[48,3072]{1,0:T(8,128)(2,1)S(1)}, u32[]{:S(2)}, u32[]{:S(2)}) collective-permute-start(bf16[48,3072]{1,0:T(8,128)(2,1)S(1)} %add_convert_fusion.10), channel_id=1, source_target_pairs={{2,0},{4,2},{6,4},{7,6},{5,7},{3,5},{1,3},{0,1},{10,8},{12,10},{14... | collective-permute-start | bytes 884744 | tf_op jit(solution)/shard_map/ppermute | solution.py:170
  76.4 32.7 %copy-start.1 = (bf16[64,6144]{1,0:T(8,128)(2,1)S(1)}, bf16[64,6144]{1,0:T(8,128)(2,1)}, u32[]{:S(2)}) copy-start(bf16[64,6144]{1,0:T(8,128)(2,1)} %param.6) | copy-start | bytes 2359300
  76.5 12.3 %collective-permute-start.17 = (bf16[48,3072]{1,0:T(8,128)(2,1)S(1)}, bf16[48,3072]{1,0:T(8,128)(2,1)S(1)}, u32[]{:S(2)}, u32[]{:S(2)}) collective-permute-start(bf16[48,3072]{1,0:T(8,128)(2,1)S(1)} %add_convert_fusion.11), channel_id=1, source_target_pairs={{0,2},{2,4},{4,6},{6,7},{7,5},{5,3},{3,1},{1,0},{8,10},{10,12},{12... | collective-permute-start | bytes 884744 | tf_op jit(solution)/shard_map/ppermute | solution.py:170
  82.6 12.4 %collective-permute-start.27 = (bf16[48,3072]{1,0:T(8,128)(2,1)S(1)}, bf16[48,3072]{1,0:T(8,128)(2,1)S(1)}, u32[]{:S(2)}, u32[]{:S(2)}) collective-permute-start(bf16[48,3072]{1,0:T(8,128)(2,1)S(1)} %add_convert_fusion.3), channel_id=1, source_target_pairs={{2,0},{4,2},{6,4},{7,6},{5,7},{3,5},{1,3},{0,1},{10,8},{12,10},{14... | collective-permute-start | bytes 884744 | tf_op jit(solution)/shard_map/ppermute | solution.py:170
  82.8 12.2 %collective-permute-start.26 = (bf16[48,3072]{1,0:T(8,128)(2,1)S(1)}, bf16[48,3072]{1,0:T(8,128)(2,1)S(1)}, u32[]{:S(2)}, u32[]{:S(2)}) collective-permute-start(bf16[48,3072]{1,0:T(8,128)(2,1)S(1)} %add_convert_fusion.4), channel_id=1, source_target_pairs={{0,2},{2,4},{4,6},{6,7},{7,5},{5,3},{3,1},{1,0},{8,10},{10,12},{12... | collective-permute-start | bytes 884744 | tf_op jit(solution)/shard_map/ppermute | solution.py:170
  88.9 9.7 %collective-permute-start.20 = (bf16[48,3072]{1,0:T(8,128)(2,1)S(1)}, bf16[48,3072]{1,0:T(8,128)(2,1)S(1)}, u32[]{:S(2)}, u32[]{:S(2)}) collective-permute-start(bf16[48,3072]{1,0:T(8,128)(2,1)S(1)} %add_convert_fusion.8), channel_id=1, source_target_pairs={{2,0},{4,2},{6,4},{7,6},{5,7},{3,5},{1,3},{0,1},{10,8},{12,10},{14... | collective-permute-start | bytes 884744 | tf_op jit(solution)/shard_map/ppermute | solution.py:170
  89.1 10.4 %collective-permute-start.19 = (bf16[48,3072]{1,0:T(8,128)(2,1)S(1)}, bf16[48,3072]{1,0:T(8,128)(2,1)S(1)}, u32[]{:S(2)}, u32[]{:S(2)}) collective-permute-start(bf16[48,3072]{1,0:T(8,128)(2,1)S(1)} %add_convert_fusion.9), channel_id=1, source_target_pairs={{0,2},{2,4},{4,6},{6,7},{7,5},{5,3},{3,1},{1,0},{8,10},{10,12},{12... | collective-permute-start | bytes 884744 | tf_op jit(solution)/shard_map/ppermute | solution.py:170
  95.0 7.9 %collective-permute-start.28 = (bf16[48,3072]{1,0:T(8,128)(2,1)S(1)}, bf16[48,3072]{1,0:T(8,128)(2,1)S(1)}, u32[]{:S(2)}, u32[]{:S(2)}) collective-permute-start(bf16[48,3072]{1,0:T(8,128)(2,1)S(1)} %add_convert_fusion.2), channel_id=1, source_target_pairs={{0,2},{2,4},{4,6},{6,7},{7,5},{5,3},{3,1},{1,0},{8,10},{10,12},{12... | collective-permute-start | bytes 884744 | tf_op jit(solution)/shard_map/ppermute | solution.py:268
  99.6 6.8 %collective-permute-start.21 = (bf16[48,3072]{1,0:T(8,128)(2,1)S(1)}, bf16[48,3072]{1,0:T(8,128)(2,1)S(1)}, u32[]{:S(2)}, u32[]{:S(2)}) collective-permute-start(bf16[48,3072]{1,0:T(8,128)(2,1)S(1)} %add_convert_fusion.7), channel_id=1, source_target_pairs={{2,0},{4,2},{6,4},{7,6},{5,7},{3,5},{1,3},{0,1},{10,8},{12,10},{14... | collective-permute-start | bytes 884744 | tf_op jit(solution)/shard_map/ppermute | solution.py:269
  103.1 1.4 %collective-permute-start.29 = (bf16[24,3072]{1,0:T(8,128)(2,1)S(1)}, bf16[24,3072]{1,0:T(8,128)(2,1)S(1)}, u32[]{:S(2)}, u32[]{:S(2)}) collective-permute-start(bf16[24,3072]{1,0:T(8,128)(2,1)S(1)} %get-tuple-element.157), channel_id=1, source_target_pairs={{0,8},{8,0},{1,9},{9,1},{2,10},{10,2},{3,11},{11,3},{4,12},{12,4},... | collective-permute-start | bytes 442376 | tf_op jit(solution)/shard_map/ppermute | solution.py:279
  106.5 1.4 %collective-permute-start.30 = (bf16[24,3072]{1,0:T(8,128)(2,1)S(1)}, bf16[24,3072]{1,0:T(8,128)(2,1)S(1)}, u32[]{:S(2)}, u32[]{:S(2)}) collective-permute-start(bf16[24,3072]{1,0:T(8,128)(2,1)S(1)} %get-tuple-element.155), channel_id=1, source_target_pairs={{0,8},{8,0},{1,9},{9,1},{2,10},{10,2},{3,11},{11,3},{4,12},{12,4},... | collective-permute-start | bytes 442376 | tf_op jit(solution)/shard_map/ppermute | solution.py:279

commit v20 on v18

--- a/solution.py
+++ b/solution.py
@@ -259,7 +259,9 @@
     def added(chunk, distance, side, got):
         return (part_of(chunk, distance, side) + got.astype(jnp.float32)).astype(jnp.bfloat16)
 
-    flows = [step(rest_0[2], rest_0[0]), step(rest_1[1], rest_1[2])]
+    second_left = lax.optimization_barrier(lax.ppermute(rest_1[2], "tensor", left))
+    second_right = lax.optimization_barrier(lax.ppermute(rest_1[1], "tensor", right))
+    flows = [step(rest_0[2], rest_0[0]), (second_right, second_left)]
     for distance in range(half - 1, 1, -1):
         for chunk in range(2):
             to_right = added(chunk, distance - chunk, 1, flows[chunk][0])

time: 109 us -> 109 us (level)
    ppermute x0 -> x2, waiting for transfers between devices: none -> 3.43 us  [the longest x1 3.43 us: per_device(): lax.ppermute(rest_1[2], 'tensor', left)]
    ppermute x13 -> x12, waiting for transfers between devices: 26.5 us -> 23.3 us  [step(): lax.ppermute(to_left, 'tensor', left)]
    ppermute x0 -> x2, starting transfers between devices: none -> 2.08 us  [the longest x1 1.73 us: per_device(): lax.ppermute(rest_1[1], 'tensor', right)]
    ppermute x13 -> x12, starting transfers between devices: 23.9 us -> 22.8 us  [step(): lax.ppermute(to_right, 'tensor', right)]
    ppermute x13 -> x12, starting transfers between devices: 4.03 us -> 3.03 us  [step(): lax.ppermute(to_left, 'tensor', left)]
    ppermute x13 -> x12, waiting for transfers between devices: 7.68 us -> 7.61 us  [step(): lax.ppermute(to_right, 'tensor', right)]
  transfers between devices with their start and end apart: 31 -> 31, of which waited for: 21 -> 20; matrix products, arithmetic and copies ran while one was open for 1% -> 1% of each run, Pallas kernels for 25% -> 25%
where the time goes in v20:
time: 109 us
  waiting for transfers between devices  40.6 us (37%)
  Pallas kernels  33.1 us (30%)
  starting transfers between devices  31.7 us (29%)
  other arithmetic  2.25 us (2%)
    pallas_call x9, Pallas kernels, call(): pl.pallas_call(kernel, in_specs=[pl.BlockSpec(memory_space=memory) for _,...  30.9 us
    ppermute x12, waiting for transfers between devices, step(): lax.ppermute(to_left, 'tensor', left)  23.3 us
    ppermute x12, starting transfers between devices, step(): lax.ppermute(to_right, 'tensor', right)  22.8 us
    ppermute x12, waiting for transfers between devices, step(): lax.ppermute(to_right, 'tensor', right)  7.61 us
    ppermute x1, waiting for transfers between devices, per_device(): lax.ppermute(rest_1[2], 'tensor', left)  3.43 us
    ppermute x12, starting transfers between devices, step(): lax.ppermute(to_left, 'tensor', left)  3.03 us
    ppermute x2, waiting for transfers between devices, per_device(): swapped = lax.ppermute(total[CAP:], 'expert', swap)  2.59 us
  transfers between devices with their start and end apart: 31, of which 20 were waited for; matrix products, arithmetic and copies ran while one was open for 1% of the time, Pallas kernels for 25%

profile of v20, /device:TPU:0, one launch (start us, length us, event | category | flops | bytes accessed | tf_op | source)
XLA Modules:
  0.0 108.6 jit_solution(16416100135327695910)
XLA Ops:
  0.1 0.8 compare_reduce_fusion
  0.9 0.1 copy.22
  1.0 0.1 reduce_window_sum.11
  1.3 0.1 fusion.1
  1.4 0.3 convolution_convert_fusion
  1.7 0.5 collective-permute-start
  2.2 1.2 %collective-permute-done = bf16[24,6144]{1,0:T(8,128)(2,1)S(1)} collective-permute-done((bf16[24,6144]{1,0:T(8,128)(2,1)S(1)}, bf16[24,6144]{1,0:T(8,128)(2,1)S(1)}, u32[]{:S(2)}, u32[]{:S(2)}) %collective-permute-start) | collective-permute-done | bytes 294944 | tf_op jit(solution)/shard_map/ppermute | solution.py:184
  3.5 3.0 %collective-permute-start.1 = (bf16[48,3072]{1,0:T(8,128)(2,1)S(1)}, bf16[48,3072]{1,0:T(8,128)(2,1)S(1)}, u32[]{:S(2)}, u32[]{:S(2)}) collective-permute-start(bf16[48,3072]{1,0:T(8,128)(2,1)S(1)} %get-tuple-element.148.refs_0_), channel_id=1, source_target_pairs={{0,2},{2,4},{4,6},{6,7},{7,5},{5,3},{3,1},{1,0},{8,10},{10,12},{12... | collective-permute-start | bytes 884744 | tf_op jit(solution)/shard_map/ppermute | solution.py:170
  6.6 2.0 %collective-permute-start.3 = (bf16[48,3072]{1,0:T(8,128)(2,1)S(1)}, bf16[48,3072]{1,0:T(8,128)(2,1)S(1)}, u32[]{:S(2)}, u32[]{:S(2)}) collective-permute-start(bf16[48,3072]{1,0:T(8,128)(2,1)S(1)} %get-tuple-element.147.refs_5_), channel_id=1, source_target_pairs={{0,2},{2,4},{4,6},{6,7},{7,5},{5,3},{3,1},{1,0},{8,10},{10,12},{12... | collective-permute-start | bytes 884744 | tf_op jit(solution)/shard_map/ppermute | solution.py:170
  8.6 4.7 %fetched.3.refs_10_.refs_6_ = bf16[1,6144,1024]{2,1,0:T(8,128)(2,1)S(1)} custom-call(bf16[1,6144,1024]{2,1,0:T(8,128)(2,1)} %source), custom_call_target="tpu_custom_call" | custom-call | flops 1024 | bytes 1024 | tf_op jit(solution)/shard_map/fetched/pallas_call | solution.py:29
  13.3 1.0 collective-permute-done.1.refs_1_
  14.3 2.2 %collective-permute-done.2.refs_7_ = bf16[48,3072]{1,0:T(8,128)(2,1)S(1)} collective-permute-done((bf16[48,3072]{1,0:T(8,128)(2,1)S(1)}, bf16[48,3072]{1,0:T(8,128)(2,1)S(1)}, u32[]{:S(2)}, u32[]{:S(2)}) %collective-permute-start.2) | collective-permute-done | bytes 294944 | tf_op jit(solution)/shard_map/ppermute | solution.py:170
  16.4 1.6 %collective-permute-start.5 = (bf16[48,3072]{1,0:T(8,128)(2,1)S(1)}, bf16[48,3072]{1,0:T(8,128)(2,1)S(1)}, u32[]{:S(2)}, u32[]{:S(2)}) collective-permute-start(bf16[48,3072]{1,0:T(8,128)(2,1)S(1)} %collective-permute-done.1.refs_1_), channel_id=1, source_target_pairs={{0,2},{2,4},{4,6},{6,7},{7,5},{5,3},{3,1},{1,0},{8,10},{10,12},{12... | collective-permute-start | bytes 884744 | tf_op jit(solution)/shard_map/ppermute | solution.py:170
  18.0 0.4 collective-permute-start.6
  18.5 4.7 %fetched.4.refs_10_.refs_7_ = bf16[1,6144,1024]{2,1,0:T(8,128)(2,1)S(1)} custom-call(bf16[1,6144,1024]{2,1,0:T(8,128)(2,1)} %source.1), custom_call_target="tpu_custom_call" | custom-call | flops 1024 | bytes 1024 | tf_op jit(solution)/shard_map/fetched/pallas_call | solution.py:29
  23.2 1.6 %collective-permute-start.7 = (bf16[48,3072]{1,0:T(8,128)(2,1)S(1)}, bf16[48,3072]{1,0:T(8,128)(2,1)S(1)}, u32[]{:S(2)}, u32[]{:S(2)}) collective-permute-start(bf16[48,3072]{1,0:T(8,128)(2,1)S(1)} %collective-permute-done.3.refs_6_), channel_id=1, source_target_pairs={{0,2},{2,4},{4,6},{6,7},{7,5},{5,3},{3,1},{1,0},{8,10},{10,12},{12... | collective-permute-start | bytes 884744 | tf_op jit(solution)/shard_map/ppermute | solution.py:170
  24.8 0.4 collective-permute-start.8
  25.3 1.6 %collective-permute-done.5.refs_3_ = bf16[48,3072]{1,0:T(8,128)(2,1)S(1)} collective-permute-done((bf16[48,3072]{1,0:T(8,128)(2,1)S(1)}, bf16[48,3072]{1,0:T(8,128)(2,1)S(1)}, u32[]{:S(2)}, u32[]{:S(2)}) %collective-permute-start.5) | collective-permute-done | bytes 294944 | tf_op jit(solution)/shard_map/ppermute | solution.py:170
  26.9 2.2 %collective-permute-done.6.refs_9_ = bf16[48,3072]{1,0:T(8,128)(2,1)S(1)} collective-permute-done((bf16[48,3072]{1,0:T(8,128)(2,1)S(1)}, bf16[48,3072]{1,0:T(8,128)(2,1)S(1)}, u32[]{:S(2)}, u32[]{:S(2)}) %collective-permute-start.6) | collective-permute-done | bytes 294944 | tf_op jit(solution)/shard_map/ppermute | solution.py:170
  29.1 2.0 %collective-permute-start.9 = (bf16[48,3072]{1,0:T(8,128)(2,1)S(1)}, bf16[48,3072]{1,0:T(8,128)(2,1)S(1)}, u32[]{:S(2)}, u32[]{:S(2)}) collective-permute-start(bf16[48,3072]{1,0:T(8,128)(2,1)S(1)} %collective-permute-done.5.refs_3_), channel_id=1, source_target_pairs={{0,2},{2,4},{4,6},{6,7},{7,5},{5,3},{3,1},{1,0},{8,10},{10,12},{12... | collective-permute-start | bytes 884744 | tf_op jit(solution)/shard_map/ppermute | solution.py:170
  31.1 2.1 %collective-permute-done.7.refs_8_ = bf16[48,3072]{1,0:T(8,128)(2,1)S(1)} collective-permute-done((bf16[48,3072]{1,0:T(8,128)(2,1)S(1)}, bf16[48,3072]{1,0:T(8,128)(2,1)S(1)}, u32[]{:S(2)}, u32[]{:S(2)}) %collective-permute-start.7) | collective-permute-done | bytes 294944 | tf_op jit(solution)/shard_map/ppermute | solution.py:170
  33.2 2.2 %collective-permute-done.8.refs_4_ = bf16[48,3072]{1,0:T(8,128)(2,1)S(1)} collective-permute-done((bf16[48,3072]{1,0:T(8,128)(2,1)S(1)}, bf16[48,3072]{1,0:T(8,128)(2,1)S(1)}, u32[]{:S(2)}, u32[]{:S(2)}) %collective-permute-start.8) | collective-permute-done | bytes 294944 | tf_op jit(solution)/shard_map/ppermute | solution.py:170
  35.4 3.2 %near_gate.1.refs_11_ = f32[240,1024]{1,0:T(8,128)S(1)} custom-call(bf16[48,3072]{1,0:T(8,128)(2,1)S(1)} %get-tuple-element.148.refs_0_, bf16[48,3072]{1,0:T(8,128)(2,1)S(1)} %collective-permute-done.1.refs_1_, bf16[48,3072]{1,0:T(8,128)(2,1)S(1)} %collective-permute-done.4.refs_2_, bf16[48,3072]{1,0:T(8,128)(2,1)S(1)} %collective-permute-done.5.refs_3_, ...), custom_call_target="tpu_custom_call" | custom-call | flops 1024 | bytes 1024 | tf_op jit(solution)/shard_map/near_gate/pallas_call | solution.py:29
  38.6 1.6 %collective-permute-start.11 = (bf16[48,3072]{1,0:T(8,128)(2,1)S(1)}, bf16[48,3072]{1,0:T(8,128)(2,1)S(1)}, u32[]{:S(2)}, u32[]{:S(2)}) collective-permute-start(bf16[48,3072]{1,0:T(8,128)(2,1)S(1)} %collective-permute-done.7.refs_8_), channel_id=1, source_target_pairs={{0,2},{2,4},{4,6},{6,7},{7,5},{5,3},{3,1},{1,0},{8,10},{10,12},{12... | collective-permute-start | bytes 884744 | tf_op jit(solution)/shard_map/ppermute | solution.py:170
  40.2 0.4 collective-permute-start.12
  40.7 1.6 %collective-permute-start.13 = (bf16[48,3072]{1,0:T(8,128)(2,1)S(1)}, bf16[48,3072]{1,0:T(8,128)(2,1)S(1)}, u32[]{:S(2)}, u32[]{:S(2)}) collective-permute-start(bf16[48,3072]{1,0:T(8,128)(2,1)S(1)} %collective-permute-done.9.refs_0_), channel_id=1, source_target_pairs={{0,2},{2,4},{4,6},{6,7},{7,5},{5,3},{3,1},{1,0},{8,10},{10,12},{12... | collective-permute-start | bytes 884744 | tf_op jit(solution)/shard_map/ppermute | solution.py:170
  42.3 0.4 collective-permute-start.14
  42.7 3.2 %near_up.1.hidden = bf16[240,1024]{1,0:T(8,128)(2,1)S(1)} custom-call(bf16[48,3072]{1,0:T(8,128)(2,1)S(1)} %get-tuple-element.148.refs_0_, bf16[48,3072]{1,0:T(8,128)(2,1)S(1)} %collective-permute-done.1.refs_1_, bf16[48,3072]{1,0:T(8,128)(2,1)S(1)} %collective-permute-done.4.refs_2_, bf16[48,3072]{1,0:T(8,128)(2,1)S(1)} %collective-permute-done.5.refs_3_, ...), custom_call_target="tpu_custom_call" | custom-call | flops 1024 | bytes 1024 | tf_op jit(solution)/shard_map/near_up/pallas_call | solution.py:29
  46.0 2.9 %fetched.5.refs_8_.down = bf16[1,1024,3072]{2,1,0:T(8,128)(2,1)S(1)} custom-call(bf16[1,1024,6144]{2,1,0:T(8,128)(2,1)} %w_down), custom_call_target="tpu_custom_call" | custom-call | flops 1024 | bytes 1024 | tf_op jit(solution)/shard_map/fetched/pallas_call | solution.py:29
  48.9 1.2 %collective-permute-done.12.refs_1_ = bf16[48,3072]{1,0:T(8,128)(2,1)S(1)} collective-permute-done((bf16[48,3072]{1,0:T(8,128)(2,1)S(1)}, bf16[48,3072]{1,0:T(8,128)(2,1)S(1)}, u32[]{:S(2)}, u32[]{:S(2)}) %collective-permute-start.12) | collective-permute-done | bytes 294944 | tf_op jit(solution)/shard_map/ppermute | solution.py:170
  50.1 1.7 %collective-permute-done.13.refs_2_ = bf16[48,3072]{1,0:T(8,128)(2,1)S(1)} collective-permute-done((bf16[48,3072]{1,0:T(8,128)(2,1)S(1)}, bf16[48,3072]{1,0:T(8,128)(2,1)S(1)}, u32[]{:S(2)}, u32[]{:S(2)}) %collective-permute-start.13) | collective-permute-done | bytes 294944 | tf_op jit(solution)/shard_map/ppermute | solution.py:170
  51.7 1.5 %collective-permute-done.14.refs_5_ = bf16[48,3072]{1,0:T(8,128)(2,1)S(1)} collective-permute-done((bf16[48,3072]{1,0:T(8,128)(2,1)S(1)}, bf16[48,3072]{1,0:T(8,128)(2,1)S(1)}, u32[]{:S(2)}, u32[]{:S(2)}) %collective-permute-start.14) | collective-permute-done | bytes 294944 | tf_op jit(solution)/shard_map/ppermute | solution.py:170
  53.2 4.8 %rest_first.1 = (bf16[48,3072]{1,0:T(8,128)(2,1)S(1)}, bf16[48,3072]{1,0:T(8,128)(2,1)S(1)}, bf16[48,3072]{1,0:T(8,128)(2,1)S(1)}, bf16[144,1024]{1,0:T(8,128)(2,1)S(1)}) custom-call(bf16[48,3072]{1,0:T(8,128)(2,1)S(1)} %collective-permute-done.9.refs_0_, bf16[48,3072]{1,0:T(8,128)(2,1)S(1)} %collective-permute-done.12.refs_1_, ...), custom_call_target="tpu_custom_call" | custom-call | flops 1024 | bytes 1024 | tf_op jit(solution)/shard_map/rest_first/pallas_call | solution.py:29
  58.0 1.6 %collective-permute-start.22 = (bf16[48,3072]{1,0:T(8,128)(2,1)S(1)}, bf16[48,3072]{1,0:T(8,128)(2,1)S(1)}, u32[]{:S(2)}, u32[]{:S(2)}) collective-permute-start(bf16[48,3072]{1,0:T(8,128)(2,1)S(1)} %get-tuple-element.135), channel_id=1, source_target_pairs={{0,2},{2,4},{4,6},{6,7},{7,5},{5,3},{3,1},{1,0},{8,10},{10,12},{12... | collective-permute-start | bytes 884744 | tf_op jit(solution)/shard_map/ppermute | solution.py:170
  59.6 0.4 collective-permute-start.23
  60.2 4.0 %rest_second.1 = (bf16[48,3072]{1,0:T(8,128)(2,1)S(1)}, bf16[48,3072]{1,0:T(8,128)(2,1)S(1)}, bf16[48,3072]{1,0:T(8,128)(2,1)S(1)}, bf16[1,1024,3072]{2,1,0:T(8,128)(2,1)S(1)}) custom-call(bf16[144,1024]{1,0:T(8,128)(2,1)S(1)} %get-tuple-element.116.hidden, bf16[1,1024,6144]{2,1,0:T(8,128)(2,1)} %w_down), custom_call_target="tpu_custom_call" | custom-call | flops 1024 | bytes 1024 | tf_op jit(solution)/shard_map/rest_second/pallas_call | solution.py:29
  64.2 0.3 collective-permute-start.17
  64.5 1.7 %collective-permute-start.15 = (bf16[48,3072]{1,0:T(8,128)(2,1)S(1)}, bf16[48,3072]{1,0:T(8,128)(2,1)S(1)}, u32[]{:S(2)}, u32[]{:S(2)}) collective-permute-start(bf16[48,3072]{1,0:T(8,128)(2,1)S(1)} %get-tuple-element.117), channel_id=1, source_target_pairs={{0,2},{2,4},{4,6},{6,7},{7,5},{5,3},{3,1},{1,0},{8,10},{10,12},{12... | collective-permute-start | bytes 884744 | tf_op jit(solution)/shard_map/ppermute | solution.py:263
  66.3 1.7 %near_down.3 = (bf16[48,3072]{1,0:T(8,128)(2,1)S(1)}, bf16[48,3072]{1,0:T(8,128)(2,1)S(1)}, bf16[48,3072]{1,0:T(8,128)(2,1)S(1)}, bf16[48,3072]{1,0:T(8,128)(2,1)S(1)}, bf16[48,3072]{1,0:T(8,128)(2,1)S(1)}) custom-call(bf16[240,1024]{1,0:T(8,128)(2,1)S(1)} %near_up.1.hidden, bf16[1,1024,3072]{2,1,0:T(8,128)(2,1)S(1)} %fetched.5.refs_8_.down), custom_call_target="tpu_custom_call" | custom-call | flops 1024 | bytes 1024 | tf_op jit(solution)/shard_map/near_down/pallas_call | solution.py:29
  68.0 1.7 %near_down.2 = (bf16[48,3072]{1,0:T(8,128)(2,1)S(1)}, bf16[48,3072]{1,0:T(8,128)(2,1)S(1)}, bf16[48,3072]{1,0:T(8,128)(2,1)S(1)}, bf16[48,3072]{1,0:T(8,128)(2,1)S(1)}, bf16[48,3072]{1,0:T(8,128)(2,1)S(1)}) custom-call(bf16[240,1024]{1,0:T(8,128)(2,1)S(1)} %near_up.1.hidden, bf16[1,1024,3072]{2,1,0:T(8,128)(2,1)S(1)} %get-tuple-element.120.down), custom_call_target="tpu_custom_call" | custom-call | flops 1024 | bytes 1024 | tf_op jit(solution)/shard_map/near_down/pallas_call | solution.py:29
  69.8 0.3 collective-permute-start.25
  70.2 1.8 %collective-permute-start.24 = (bf16[48,3072]{1,0:T(8,128)(2,1)S(1)}, bf16[48,3072]{1,0:T(8,128)(2,1)S(1)}, u32[]{:S(2)}, u32[]{:S(2)}) collective-permute-start(bf16[48,3072]{1,0:T(8,128)(2,1)S(1)} %add_convert_fusion.6), channel_id=1, source_target_pairs={{0,2},{2,4},{4,6},{6,7},{7,5},{5,3},{3,1},{1,0},{8,10},{10,12},{12... | collective-permute-start | bytes 884744 | tf_op jit(solution)/shard_map/ppermute | solution.py:170
  72.0 3.4 %collective-permute-done.17 = bf16[48,3072]{1,0:T(8,128)(2,1)S(1)} collective-permute-done((bf16[48,3072]{1,0:T(8,128)(2,1)S(1)}, bf16[48,3072]{1,0:T(8,128)(2,1)S(1)}, u32[]{:S(2)}, u32[]{:S(2)}) %collective-permute-start.17) | collective-permute-done | bytes 294944 | tf_op jit(solution)/shard_map/ppermute | solution.py:262
  75.6 2.0 %collective-permute-start.16 = (bf16[48,3072]{1,0:T(8,128)(2,1)S(1)}, bf16[48,3072]{1,0:T(8,128)(2,1)S(1)}, u32[]{:S(2)}, u32[]{:S(2)}) collective-permute-start(bf16[48,3072]{1,0:T(8,128)(2,1)S(1)} %add_convert_fusion.11), channel_id=1, source_target_pairs={{0,2},{2,4},{4,6},{6,7},{7,5},{5,3},{3,1},{1,0},{8,10},{10,12},{12... | collective-permute-start | bytes 884744 | tf_op jit(solution)/shard_map/ppermute | solution.py:170
  77.7 4.0 %collective-permute-done.25 = bf16[48,3072]{1,0:T(8,128)(2,1)S(1)} collective-permute-done((bf16[48,3072]{1,0:T(8,128)(2,1)S(1)}, bf16[48,3072]{1,0:T(8,128)(2,1)S(1)}, u32[]{:S(2)}, u32[]{:S(2)}) %collective-permute-start.25) | collective-permute-done | bytes 294944 | tf_op jit(solution)/shard_map/ppermute | solution.py:170
  81.8 0.2 collective-permute-start.27
  82.1 1.9 %collective-permute-start.26 = (bf16[48,3072]{1,0:T(8,128)(2,1)S(1)}, bf16[48,3072]{1,0:T(8,128)(2,1)S(1)}, u32[]{:S(2)}, u32[]{:S(2)}) collective-permute-start(bf16[48,3072]{1,0:T(8,128)(2,1)S(1)} %add_convert_fusion.4), channel_id=1, source_target_pairs={{0,2},{2,4},{4,6},{6,7},{7,5},{5,3},{3,1},{1,0},{8,10},{10,12},{12... | collective-permute-start | bytes 884744 | tf_op jit(solution)/shard_map/ppermute | solution.py:170
  84.0 4.0 %collective-permute-done.18 = bf16[48,3072]{1,0:T(8,128)(2,1)S(1)} collective-permute-done((bf16[48,3072]{1,0:T(8,128)(2,1)S(1)}, bf16[48,3072]{1,0:T(8,128)(2,1)S(1)}, u32[]{:S(2)}, u32[]{:S(2)}) %collective-permute-start.18) | collective-permute-done | bytes 294944 | tf_op jit(solution)/shard_map/ppermute | solution.py:170
  88.1 0.2 collective-permute-start.20
  88.4 1.9 %collective-permute-start.19 = (bf16[48,3072]{1,0:T(8,128)(2,1)S(1)}, bf16[48,3072]{1,0:T(8,128)(2,1)S(1)}, u32[]{:S(2)}, u32[]{:S(2)}) collective-permute-start(bf16[48,3072]{1,0:T(8,128)(2,1)S(1)} %add_convert_fusion.9), channel_id=1, source_target_pairs={{0,2},{2,4},{4,6},{6,7},{7,5},{5,3},{3,1},{1,0},{8,10},{10,12},{12... | collective-permute-start | bytes 884744 | tf_op jit(solution)/shard_map/ppermute | solution.py:170
  90.3 4.0 %collective-permute-done.27 = bf16[48,3072]{1,0:T(8,128)(2,1)S(1)} collective-permute-done((bf16[48,3072]{1,0:T(8,128)(2,1)S(1)}, bf16[48,3072]{1,0:T(8,128)(2,1)S(1)}, u32[]{:S(2)}, u32[]{:S(2)}) %collective-permute-start.27) | collective-permute-done | bytes 294944 | tf_op jit(solution)/shard_map/ppermute | solution.py:170
  94.4 1.4 %collective-permute-start.28 = (bf16[48,3072]{1,0:T(8,128)(2,1)S(1)}, bf16[48,3072]{1,0:T(8,128)(2,1)S(1)}, u32[]{:S(2)}, u32[]{:S(2)}) collective-permute-start(bf16[48,3072]{1,0:T(8,128)(2,1)S(1)} %add_convert_fusion.2), channel_id=1, source_target_pairs={{0,2},{2,4},{4,6},{6,7},{7,5},{5,3},{3,1},{1,0},{8,10},{10,12},{12... | collective-permute-start | bytes 884744 | tf_op jit(solution)/shard_map/ppermute | solution.py:270
  95.9 2.1 %collective-permute-done.20 = bf16[48,3072]{1,0:T(8,128)(2,1)S(1)} collective-permute-done((bf16[48,3072]{1,0:T(8,128)(2,1)S(1)}, bf16[48,3072]{1,0:T(8,128)(2,1)S(1)}, u32[]{:S(2)}, u32[]{:S(2)}) %collective-permute-start.20) | collective-permute-done | bytes 294944 | tf_op jit(solution)/shard_map/ppermute | solution.py:170
  97.9 1.2 %collective-permute-done.19 = bf16[48,3072]{1,0:T(8,128)(2,1)S(1)} collective-permute-done((bf16[48,3072]{1,0:T(8,128)(2,1)S(1)}, bf16[48,3072]{1,0:T(8,128)(2,1)S(1)}, u32[]{:S(2)}, u32[]{:S(2)}) %collective-permute-start.19) | collective-permute-done | bytes 294944 | tf_op jit(solution)/shard_map/ppermute | solution.py:170
  99.2 1.7 %collective-permute-start.21 = (bf16[48,3072]{1,0:T(8,128)(2,1)S(1)}, bf16[48,3072]{1,0:T(8,128)(2,1)S(1)}, u32[]{:S(2)}, u32[]{:S(2)}) collective-permute-start(bf16[48,3072]{1,0:T(8,128)(2,1)S(1)} %add_convert_fusion.7), channel_id=1, source_target_pairs={{2,0},{4,2},{6,4},{7,6},{5,7},{3,5},{1,3},{0,1},{10,8},{12,10},{14... | collective-permute-start | bytes 884744 | tf_op jit(solution)/shard_map/ppermute | solution.py:271
  100.9 1.9 %collective-permute-done.28 = bf16[48,3072]{1,0:T(8,128)(2,1)S(1)} collective-permute-done((bf16[48,3072]{1,0:T(8,128)(2,1)S(1)}, bf16[48,3072]{1,0:T(8,128)(2,1)S(1)}, u32[]{:S(2)}, u32[]{:S(2)}) %collective-permute-start.28) | collective-permute-done | bytes 294944 | tf_op jit(solution)/shard_map/ppermute | solution.py:270
  102.9 0.1 add_convert_fusion.1
  103.1 0.1 select_convert_fusion.weights
  103.2 1.2 %collective-permute-done.29.swapped = bf16[24,3072]{1,0:T(8,128)(2,1)S(1)} collective-permute-done((bf16[24,3072]{1,0:T(8,128)(2,1)S(1)}, bf16[24,3072]{1,0:T(8,128)(2,1)S(1)}, u32[]{:S(2)}, u32[]{:S(2)}) %collective-permute-start.29) | collective-permute-done | bytes 147488 | tf_op jit(solution)/shard_map/ppermute | solution.py:281
  104.4 1.1 %combined.2.refs_0_ = bf16[64,6144]{1,0:T(8,128)(2,1)} custom-call(bf16[2,64,24]{2,1,0:T(8,128)(2,1)S(1)} %select_convert_fusion.weights, bf16[24,3072]{1,0:T(8,128)(2,1)S(1)} %get-tuple-element.154.kept, bf16[24,3072]{1,0:T(8,128)(2,1)S(1)} %collective-permute-done.29.swapped), custom_call_target="tpu_custom_call" | custom-call | flops 1024 | bytes 1024 | tf_op jit(solution)/shard_map/combined/pallas_call | solution.py:134
  105.5 0.5 collective-permute-done.21
  106.0 0.1 add_convert_fusion
  106.2 1.4 %collective-permute-done.30.swapped = bf16[24,3072]{1,0:T(8,128)(2,1)S(1)} collective-permute-done((bf16[24,3072]{1,0:T(8,128)(2,1)S(1)}, bf16[24,3072]{1,0:T(8,128)(2,1)S(1)}, u32[]{:S(2)}, u32[]{:S(2)}) %collective-permute-start.30) | collective-permute-done | bytes 147488 | tf_op jit(solution)/shard_map/ppermute | solution.py:281
  107.6 1.1 combined.3
  (47 shorter events, 1.5 us)
Async XLA Ops:
  0.0 1.4 %copy-start = (bf16[64,6144]{1,0:T(8,128)(2,1)S(1)}, bf16[64,6144]{1,0:T(8,128)(2,1)}, u32[]{:S(2)}) copy-start(bf16[64,6144]{1,0:T(8,128)(2,1)} %param.6) | copy-start | bytes 2359300
  1.7 1.7 %collective-permute-start = (bf16[24,6144]{1,0:T(8,128)(2,1)S(1)}, bf16[24,6144]{1,0:T(8,128)(2,1)S(1)}, u32[]{:S(2)}, u32[]{:S(2)}) collective-permute-start(bf16[24,6144]{1,0:T(8,128)(2,1)S(1)} %get-tuple-element.150), channel_id=1, source_target_pairs={{0,8},{8,0},{1,9},{9,1},{2,10},{10,2},{3,11},{11,3},{4,12},{12,4},... | collective-permute-start | bytes 884744 | tf_op jit(solution)/shard_map/ppermute | solution.py:184
  3.5 10.7 %collective-permute-start.1 = (bf16[48,3072]{1,0:T(8,128)(2,1)S(1)}, bf16[48,3072]{1,0:T(8,128)(2,1)S(1)}, u32[]{:S(2)}, u32[]{:S(2)}) collective-permute-start(bf16[48,3072]{1,0:T(8,128)(2,1)S(1)} %get-tuple-element.148.refs_0_), channel_id=1, source_target_pairs={{0,2},{2,4},{4,6},{6,7},{7,5},{5,3},{3,1},{1,0},{8,10},{10,12},{12... | collective-permute-start | bytes 884744 | tf_op jit(solution)/shard_map/ppermute | solution.py:170
  6.5 9.9 %collective-permute-start.2 = (bf16[48,3072]{1,0:T(8,128)(2,1)S(1)}, bf16[48,3072]{1,0:T(8,128)(2,1)S(1)}, u32[]{:S(2)}, u32[]{:S(2)}) collective-permute-start(bf16[48,3072]{1,0:T(8,128)(2,1)S(1)} %get-tuple-element.147.refs_5_), channel_id=1, source_target_pairs={{2,0},{4,2},{6,4},{7,6},{5,7},{3,5},{1,3},{0,1},{10,8},{12,10},{14... | collective-permute-start | bytes 884744 | tf_op jit(solution)/shard_map/ppermute | solution.py:170
  6.6 16.6 %collective-permute-start.3 = (bf16[48,3072]{1,0:T(8,128)(2,1)S(1)}, bf16[48,3072]{1,0:T(8,128)(2,1)S(1)}, u32[]{:S(2)}, u32[]{:S(2)}) collective-permute-start(bf16[48,3072]{1,0:T(8,128)(2,1)S(1)} %get-tuple-element.147.refs_5_), channel_id=1, source_target_pairs={{0,2},{2,4},{4,6},{6,7},{7,5},{5,3},{3,1},{1,0},{8,10},{10,12},{12... | collective-permute-start | bytes 884744 | tf_op jit(solution)/shard_map/ppermute | solution.py:170
  8.6 14.6 %collective-permute-start.4 = (bf16[48,3072]{1,0:T(8,128)(2,1)S(1)}, bf16[48,3072]{1,0:T(8,128)(2,1)S(1)}, u32[]{:S(2)}, u32[]{:S(2)}) collective-permute-start(bf16[48,3072]{1,0:T(8,128)(2,1)S(1)} %get-tuple-element.148.refs_0_), channel_id=1, source_target_pairs={{2,0},{4,2},{6,4},{7,6},{5,7},{3,5},{1,3},{0,1},{10,8},{12,10},{14... | collective-permute-start | bytes 884744 | tf_op jit(solution)/shard_map/ppermute | solution.py:170
  16.4 10.5 %collective-permute-start.5 = (bf16[48,3072]{1,0:T(8,128)(2,1)S(1)}, bf16[48,3072]{1,0:T(8,128)(2,1)S(1)}, u32[]{:S(2)}, u32[]{:S(2)}) collective-permute-start(bf16[48,3072]{1,0:T(8,128)(2,1)S(1)} %collective-permute-done.1.refs_1_), channel_id=1, source_target_pairs={{0,2},{2,4},{4,6},{6,7},{7,5},{5,3},{3,1},{1,0},{8,10},{10,12},{12... | collective-permute-start | bytes 884744 | tf_op jit(solution)/shard_map/ppermute | solution.py:170
  18.0 11.1 %collective-permute-start.6 = (bf16[48,3072]{1,0:T(8,128)(2,1)S(1)}, bf16[48,3072]{1,0:T(8,128)(2,1)S(1)}, u32[]{:S(2)}, u32[]{:S(2)}) collective-permute-start(bf16[48,3072]{1,0:T(8,128)(2,1)S(1)} %collective-permute-done.2.refs_7_), channel_id=1, source_target_pairs={{2,0},{4,2},{6,4},{7,6},{5,7},{3,5},{1,3},{0,1},{10,8},{12,10},{14... | collective-permute-start | bytes 884744 | tf_op jit(solution)/shard_map/ppermute | solution.py:170
  23.2 10.0 %collective-permute-start.7 = (bf16[48,3072]{1,0:T(8,128)(2,1)S(1)}, bf16[48,3072]{1,0:T(8,128)(2,1)S(1)}, u32[]{:S(2)}, u32[]{:S(2)}) collective-permute-start(bf16[48,3072]{1,0:T(8,128)(2,1)S(1)} %collective-permute-done.3.refs_6_), channel_id=1, source_target_pairs={{0,2},{2,4},{4,6},{6,7},{7,5},{5,3},{3,1},{1,0},{8,10},{10,12},{12... | collective-permute-start | bytes 884744 | tf_op jit(solution)/shard_map/ppermute | solution.py:170
  24.8 10.6 %collective-permute-start.8 = (bf16[48,3072]{1,0:T(8,128)(2,1)S(1)}, bf16[48,3072]{1,0:T(8,128)(2,1)S(1)}, u32[]{:S(2)}, u32[]{:S(2)}) collective-permute-start(bf16[48,3072]{1,0:T(8,128)(2,1)S(1)} %collective-permute-done.4.refs_2_), channel_id=1, source_target_pairs={{2,0},{4,2},{6,4},{7,6},{5,7},{3,5},{1,3},{0,1},{10,8},{12,10},{14... | collective-permute-start | bytes 884744 | tf_op jit(solution)/shard_map/ppermute | solution.py:170
  29.1 11.6 %collective-permute-start.10 = (bf16[48,3072]{1,0:T(8,128)(2,1)S(1)}, bf16[48,3072]{1,0:T(8,128)(2,1)S(1)}, u32[]{:S(2)}, u32[]{:S(2)}) collective-permute-start(bf16[48,3072]{1,0:T(8,128)(2,1)S(1)} %collective-permute-done.6.refs_9_), channel_id=1, source_target_pairs={{2,0},{4,2},{6,4},{7,6},{5,7},{3,5},{1,3},{0,1},{10,8},{12,10},{14... | collective-permute-start | bytes 884744 | tf_op jit(solution)/shard_map/ppermute | solution.py:170
  29.1 11.6 %collective-permute-start.9 = (bf16[48,3072]{1,0:T(8,128)(2,1)S(1)}, bf16[48,3072]{1,0:T(8,128)(2,1)S(1)}, u32[]{:S(2)}, u32[]{:S(2)}) collective-permute-start(bf16[48,3072]{1,0:T(8,128)(2,1)S(1)} %collective-permute-done.5.refs_3_), channel_id=1, source_target_pairs={{0,2},{2,4},{4,6},{6,7},{7,5},{5,3},{3,1},{1,0},{8,10},{10,12},{12... | collective-permute-start | bytes 884744 | tf_op jit(solution)/shard_map/ppermute | solution.py:170
  38.6 10.3 %collective-permute-start.11 = (bf16[48,3072]{1,0:T(8,128)(2,1)S(1)}, bf16[48,3072]{1,0:T(8,128)(2,1)S(1)}, u32[]{:S(2)}, u32[]{:S(2)}) collective-permute-start(bf16[48,3072]{1,0:T(8,128)(2,1)S(1)} %collective-permute-done.7.refs_8_), channel_id=1, source_target_pairs={{0,2},{2,4},{4,6},{6,7},{7,5},{5,3},{3,1},{1,0},{8,10},{10,12},{12... | collective-permute-start | bytes 884744 | tf_op jit(solution)/shard_map/ppermute | solution.py:170
  40.2 9.8 %collective-permute-start.12 = (bf16[48,3072]{1,0:T(8,128)(2,1)S(1)}, bf16[48,3072]{1,0:T(8,128)(2,1)S(1)}, u32[]{:S(2)}, u32[]{:S(2)}) collective-permute-start(bf16[48,3072]{1,0:T(8,128)(2,1)S(1)} %collective-permute-done.8.refs_4_), channel_id=1, source_target_pairs={{2,0},{4,2},{6,4},{7,6},{5,7},{3,5},{1,3},{0,1},{10,8},{12,10},{14... | collective-permute-start | bytes 884744 | tf_op jit(solution)/shard_map/ppermute | solution.py:170
  40.7 11.0 %collective-permute-start.13 = (bf16[48,3072]{1,0:T(8,128)(2,1)S(1)}, bf16[48,3072]{1,0:T(8,128)(2,1)S(1)}, u32[]{:S(2)}, u32[]{:S(2)}) collective-permute-start(bf16[48,3072]{1,0:T(8,128)(2,1)S(1)} %collective-permute-done.9.refs_0_), channel_id=1, source_target_pairs={{0,2},{2,4},{4,6},{6,7},{7,5},{5,3},{3,1},{1,0},{8,10},{10,12},{12... | collective-permute-start | bytes 884744 | tf_op jit(solution)/shard_map/ppermute | solution.py:170
  42.3 10.9 %collective-permute-start.14 = (bf16[48,3072]{1,0:T(8,128)(2,1)S(1)}, bf16[48,3072]{1,0:T(8,128)(2,1)S(1)}, u32[]{:S(2)}, u32[]{:S(2)}) collective-permute-start(bf16[48,3072]{1,0:T(8,128)(2,1)S(1)} %collective-permute-done.10.refs_4_), channel_id=1, source_target_pairs={{2,0},{4,2},{6,4},{7,6},{5,7},{3,5},{1,3},{0,1},{10,8},{12,10},{14... | collective-permute-start | bytes 884744 | tf_op jit(solution)/shard_map/ppermute | solution.py:170
  48.9 11.2 %copy-start.2 = (s32[64,2]{0,1:T(2,128)S(1)}, s32[64,2]{0,1:T(2,128)}, u32[]{:S(2)}) copy-start(s32[64,2]{0,1:T(2,128)} %param.7) | copy-start | bytes 1540
  48.9 11.2 %copy-start.3 = (f32[64,2]{0,1:T(2,128)S(1)}, f32[64,2]{0,1:T(2,128)}, u32[]{:S(2)}) copy-start(f32[64,2]{0,1:T(2,128)} %param.8) | copy-start | bytes 1540
  58.0 11.7 %collective-permute-start.22 = (bf16[48,3072]{1,0:T(8,128)(2,1)S(1)}, bf16[48,3072]{1,0:T(8,128)(2,1)S(1)}, u32[]{:S(2)}, u32[]{:S(2)}) collective-permute-start(bf16[48,3072]{1,0:T(8,128)(2,1)S(1)} %get-tuple-element.135), channel_id=1, source_target_pairs={{0,2},{2,4},{4,6},{6,7},{7,5},{5,3},{3,1},{1,0},{8,10},{10,12},{12... | collective-permute-start | bytes 884744 | tf_op jit(solution)/shard_map/ppermute | solution.py:170
  59.6 10.0 %collective-permute-start.23 = (bf16[48,3072]{1,0:T(8,128)(2,1)S(1)}, bf16[48,3072]{1,0:T(8,128)(2,1)S(1)}, u32[]{:S(2)}, u32[]{:S(2)}) collective-permute-start(bf16[48,3072]{1,0:T(8,128)(2,1)S(1)} %get-tuple-element.136), channel_id=1, source_target_pairs={{2,0},{4,2},{6,4},{7,6},{5,7},{3,5},{1,3},{0,1},{10,8},{12,10},{14... | collective-permute-start | bytes 884744 | tf_op jit(solution)/shard_map/ppermute | solution.py:170
  64.2 11.2 %collective-permute-start.17 = (bf16[48,3072]{1,0:T(8,128)(2,1)S(1)}, bf16[48,3072]{1,0:T(8,128)(2,1)S(1)}, u32[]{:S(2)}, u32[]{:S(2)}) collective-permute-start(bf16[48,3072]{1,0:T(8,128)(2,1)S(1)} %get-tuple-element.118), channel_id=1, source_target_pairs={{2,0},{4,2},{6,4},{7,6},{5,7},{3,5},{1,3},{0,1},{10,8},{12,10},{14... | collective-permute-start | bytes 884744 | tf_op jit(solution)/shard_map/ppermute | solution.py:262
  64.5 11.0 %collective-permute-start.15 = (bf16[48,3072]{1,0:T(8,128)(2,1)S(1)}, bf16[48,3072]{1,0:T(8,128)(2,1)S(1)}, u32[]{:S(2)}, u32[]{:S(2)}) collective-permute-start(bf16[48,3072]{1,0:T(8,128)(2,1)S(1)} %get-tuple-element.117), channel_id=1, source_target_pairs={{0,2},{2,4},{4,6},{6,7},{7,5},{5,3},{3,1},{1,0},{8,10},{10,12},{12... | collective-permute-start | bytes 884744 | tf_op jit(solution)/shard_map/ppermute | solution.py:263
  69.8 12.0 %collective-permute-start.25 = (bf16[48,3072]{1,0:T(8,128)(2,1)S(1)}, bf16[48,3072]{1,0:T(8,128)(2,1)S(1)}, u32[]{:S(2)}, u32[]{:S(2)}) collective-permute-start(bf16[48,3072]{1,0:T(8,128)(2,1)S(1)} %add_convert_fusion.5), channel_id=1, source_target_pairs={{2,0},{4,2},{6,4},{7,6},{5,7},{3,5},{1,3},{0,1},{10,8},{12,10},{14... | collective-permute-start | bytes 884744 | tf_op jit(solution)/shard_map/ppermute | solution.py:170
  70.2 11.6 %collective-permute-start.24 = (bf16[48,3072]{1,0:T(8,128)(2,1)S(1)}, bf16[48,3072]{1,0:T(8,128)(2,1)S(1)}, u32[]{:S(2)}, u32[]{:S(2)}) collective-permute-start(bf16[48,3072]{1,0:T(8,128)(2,1)S(1)} %add_convert_fusion.6), channel_id=1, source_target_pairs={{0,2},{2,4},{4,6},{6,7},{7,5},{5,3},{3,1},{1,0},{8,10},{10,12},{12... | collective-permute-start | bytes 884744 | tf_op jit(solution)/shard_map/ppermute | solution.py:170
  75.5 12.6 %collective-permute-start.18 = (bf16[48,3072]{1,0:T(8,128)(2,1)S(1)}, bf16[48,3072]{1,0:T(8,128)(2,1)S(1)}, u32[]{:S(2)}, u32[]{:S(2)}) collective-permute-start(bf16[48,3072]{1,0:T(8,128)(2,1)S(1)} %add_convert_fusion.10), channel_id=1, source_target_pairs={{2,0},{4,2},{6,4},{7,6},{5,7},{3,5},{1,3},{0,1},{10,8},{12,10},{14... | collective-permute-start | bytes 884744 | tf_op jit(solution)/shard_map/ppermute | solution.py:170
  75.6 33.1 %copy-start.1 = (bf16[64,6144]{1,0:T(8,128)(2,1)S(1)}, bf16[64,6144]{1,0:T(8,128)(2,1)}, u32[]{:S(2)}) copy-start(bf16[64,6144]{1,0:T(8,128)(2,1)} %param.6) | copy-start | bytes 2359300
  75.6 12.4 %collective-permute-start.16 = (bf16[48,3072]{1,0:T(8,128)(2,1)S(1)}, bf16[48,3072]{1,0:T(8,128)(2,1)S(1)}, u32[]{:S(2)}, u32[]{:S(2)}) collective-permute-start(bf16[48,3072]{1,0:T(8,128)(2,1)S(1)} %add_convert_fusion.11), channel_id=1, source_target_pairs={{0,2},{2,4},{4,6},{6,7},{7,5},{5,3},{3,1},{1,0},{8,10},{10,12},{12... | collective-permute-start | bytes 884744 | tf_op jit(solution)/shard_map/ppermute | solution.py:170
  81.8 12.6 %collective-permute-start.27 = (bf16[48,3072]{1,0:T(8,128)(2,1)S(1)}, bf16[48,3072]{1,0:T(8,128)(2,1)S(1)}, u32[]{:S(2)}, u32[]{:S(2)}) collective-permute-start(bf16[48,3072]{1,0:T(8,128)(2,1)S(1)} %add_convert_fusion.3), channel_id=1, source_target_pairs={{2,0},{4,2},{6,4},{7,6},{5,7},{3,5},{1,3},{0,1},{10,8},{12,10},{14... | collective-permute-start | bytes 884744 | tf_op jit(solution)/shard_map/ppermute | solution.py:170
  82.1 12.3 %collective-permute-start.26 = (bf16[48,3072]{1,0:T(8,128)(2,1)S(1)}, bf16[48,3072]{1,0:T(8,128)(2,1)S(1)}, u32[]{:S(2)}, u32[]{:S(2)}) collective-permute-start(bf16[48,3072]{1,0:T(8,128)(2,1)S(1)} %add_convert_fusion.4), channel_id=1, source_target_pairs={{0,2},{2,4},{4,6},{6,7},{7,5},{5,3},{3,1},{1,0},{8,10},{10,12},{12... | collective-permute-start | bytes 884744 | tf_op jit(solution)/shard_map/ppermute | solution.py:170
  88.1 9.8 %collective-permute-start.20 = (bf16[48,3072]{1,0:T(8,128)(2,1)S(1)}, bf16[48,3072]{1,0:T(8,128)(2,1)S(1)}, u32[]{:S(2)}, u32[]{:S(2)}) collective-permute-start(bf16[48,3072]{1,0:T(8,128)(2,1)S(1)} %add_convert_fusion.8), channel_id=1, source_target_pairs={{2,0},{4,2},{6,4},{7,6},{5,7},{3,5},{1,3},{0,1},{10,8},{12,10},{14... | collective-permute-start | bytes 884744 | tf_op jit(solution)/shard_map/ppermute | solution.py:170
  88.4 10.8 %collective-permute-start.19 = (bf16[48,3072]{1,0:T(8,128)(2,1)S(1)}, bf16[48,3072]{1,0:T(8,128)(2,1)S(1)}, u32[]{:S(2)}, u32[]{:S(2)}) collective-permute-start(bf16[48,3072]{1,0:T(8,128)(2,1)S(1)} %add_convert_fusion.9), channel_id=1, source_target_pairs={{0,2},{2,4},{4,6},{6,7},{7,5},{5,3},{3,1},{1,0},{8,10},{10,12},{12... | collective-permute-start | bytes 884744 | tf_op jit(solution)/shard_map/ppermute | solution.py:170
  94.4 8.4 %collective-permute-start.28 = (bf16[48,3072]{1,0:T(8,128)(2,1)S(1)}, bf16[48,3072]{1,0:T(8,128)(2,1)S(1)}, u32[]{:S(2)}, u32[]{:S(2)}) collective-permute-start(bf16[48,3072]{1,0:T(8,128)(2,1)S(1)} %add_convert_fusion.2), channel_id=1, source_target_pairs={{0,2},{2,4},{4,6},{6,7},{7,5},{5,3},{3,1},{1,0},{8,10},{10,12},{12... | collective-permute-start | bytes 884744 | tf_op jit(solution)/shard_map/ppermute | solution.py:270
  99.2 6.8 %collective-permute-start.21 = (bf16[48,3072]{1,0:T(8,128)(2,1)S(1)}, bf16[48,3072]{1,0:T(8,128)(2,1)S(1)}, u32[]{:S(2)}, u32[]{:S(2)}) collective-permute-start(bf16[48,3072]{1,0:T(8,128)(2,1)S(1)} %add_convert_fusion.7), channel_id=1, source_target_pairs={{2,0},{4,2},{6,4},{7,6},{5,7},{3,5},{1,3},{0,1},{10,8},{12,10},{14... | collective-permute-start | bytes 884744 | tf_op jit(solution)/shard_map/ppermute | solution.py:271
  103.0 1.4 %collective-permute-start.29 = (bf16[24,3072]{1,0:T(8,128)(2,1)S(1)}, bf16[24,3072]{1,0:T(8,128)(2,1)S(1)}, u32[]{:S(2)}, u32[]{:S(2)}) collective-permute-start(bf16[24,3072]{1,0:T(8,128)(2,1)S(1)} %get-tuple-element.153), channel_id=1, source_target_pairs={{0,8},{8,0},{1,9},{9,1},{2,10},{10,2},{3,11},{11,3},{4,12},{12,4},... | collective-permute-start | bytes 442376 | tf_op jit(solution)/shard_map/ppermute | solution.py:281
  106.1 1.4 %collective-permute-start.30 = (bf16[24,3072]{1,0:T(8,128)(2,1)S(1)}, bf16[24,3072]{1,0:T(8,128)(2,1)S(1)}, u32[]{:S(2)}, u32[]{:S(2)}) collective-permute-start(bf16[24,3072]{1,0:T(8,128)(2,1)S(1)} %get-tuple-element.151), channel_id=1, source_target_pairs={{0,8},{8,0},{1,9},{9,1},{2,10},{10,2},{3,11},{11,3},{4,12},{12,4},... | collective-permute-start | bytes 442376 | tf_op jit(solution)/shard_map/ppermute | solution.py:281

commit v21 on v20

--- a/solution.py
+++ b/solution.py
@@ -249,7 +249,7 @@
         )
 
     near_hidden, _, _ = tied(near_hidden, rest_1[1], rest_1[2])
-    near_parts = [near_down(0, near_hidden), near_down(1, near_hidden)]
+    near_parts = [near_down(0, near_hidden)]
 
     def part_of(chunk, distance, side):
         if distance == half - 1:
@@ -266,6 +266,9 @@
         for chunk in range(2):
             to_right = added(chunk, distance - chunk, 1, flows[chunk][0])
             to_left = added(chunk, distance - 1 + chunk, 0, flows[chunk][1])
+            if len(near_parts) == 1:
+                near_hidden, _, _ = tied(near_hidden, to_right, to_left)
+                near_parts.append(near_down(1, near_hidden))
             flows[chunk] = step(to_right, to_left)
     last_right = lax.ppermute(added(0, 1, 1, flows[0][0]), "tensor", right)
     last_left = lax.ppermute(added(1, 1, 0, flows[1][1]), "tensor", left)

time: 109 us -> 109 us (level)
  transfers between devices with their start and end apart: 31 -> 31, of which waited for: 20 -> 21; matrix products, arithmetic and copies ran while one was open for 1% -> 1% of each run, Pallas kernels for 25% -> 25%
where the time goes in v21:
time: 109 us
  waiting for transfers between devices  41.4 us (38%)
  Pallas kernels  33.1 us (30%)
  starting transfers between devices  31.5 us (29%)
  other arithmetic  2.25 us (2%)
    pallas_call x9, Pallas kernels, call(): pl.pallas_call(kernel, in_specs=[pl.BlockSpec(memory_space=memory) for _,...  30.9 us
    ppermute x12, waiting for transfers between devices, step(): lax.ppermute(to_left, 'tensor', left)  22.7 us
    ppermute x12, starting transfers between devices, step(): lax.ppermute(to_right, 'tensor', right)  22.5 us
    ppermute x12, waiting for transfers between devices, step(): lax.ppermute(to_right, 'tensor', right)  8.17 us
    ppermute x1, waiting for transfers between devices, per_device(): lax.ppermute(rest_1[2], 'tensor', left)  4.04 us
    ppermute x12, starting transfers between devices, step(): lax.ppermute(to_left, 'tensor', left)  3.34 us
    ppermute x2, waiting for transfers between devices, per_device(): swapped = lax.ppermute(total[CAP:], 'expert', swap)  2.59 us
  transfers between devices with their start and end apart: 31, of which 21 were waited for; matrix products, arithmetic and copies ran while one was open for 1% of the time, Pallas kernels for 25%

profile of v21, /device:TPU:0, one launch (start us, length us, event | category | flops | bytes accessed | tf_op | source)
XLA Modules:
  0.0 109.2 jit_solution(5673905658513775612)
XLA Ops:
  0.1 0.8 compare_reduce_fusion
  0.9 0.1 copy.22
  1.0 0.1 reduce_window_sum.11
  1.3 0.1 fusion.1
  1.4 0.3 convolution_convert_fusion
  1.7 0.5 collective-permute-start
  2.2 1.2 %collective-permute-done = bf16[24,6144]{1,0:T(8,128)(2,1)S(1)} collective-permute-done((bf16[24,6144]{1,0:T(8,128)(2,1)S(1)}, bf16[24,6144]{1,0:T(8,128)(2,1)S(1)}, u32[]{:S(2)}, u32[]{:S(2)}) %collective-permute-start) | collective-permute-done | bytes 294944 | tf_op jit(solution)/shard_map/ppermute | solution.py:184
  3.5 3.0 %collective-permute-start.1 = (bf16[48,3072]{1,0:T(8,128)(2,1)S(1)}, bf16[48,3072]{1,0:T(8,128)(2,1)S(1)}, u32[]{:S(2)}, u32[]{:S(2)}) collective-permute-start(bf16[48,3072]{1,0:T(8,128)(2,1)S(1)} %get-tuple-element.150.refs_0_), channel_id=1, source_target_pairs={{0,2},{2,4},{4,6},{6,7},{7,5},{5,3},{3,1},{1,0},{8,10},{10,12},{12... | collective-permute-start | bytes 884744 | tf_op jit(solution)/shard_map/ppermute | solution.py:170
  6.6 2.0 %collective-permute-start.3 = (bf16[48,3072]{1,0:T(8,128)(2,1)S(1)}, bf16[48,3072]{1,0:T(8,128)(2,1)S(1)}, u32[]{:S(2)}, u32[]{:S(2)}) collective-permute-start(bf16[48,3072]{1,0:T(8,128)(2,1)S(1)} %get-tuple-element.149.refs_5_), channel_id=1, source_target_pairs={{0,2},{2,4},{4,6},{6,7},{7,5},{5,3},{3,1},{1,0},{8,10},{10,12},{12... | collective-permute-start | bytes 884744 | tf_op jit(solution)/shard_map/ppermute | solution.py:170
  8.6 4.7 %fetched.3.refs_10_.refs_6_ = bf16[1,6144,1024]{2,1,0:T(8,128)(2,1)S(1)} custom-call(bf16[1,6144,1024]{2,1,0:T(8,128)(2,1)} %source), custom_call_target="tpu_custom_call" | custom-call | flops 1024 | bytes 1024 | tf_op jit(solution)/shard_map/fetched/pallas_call | solution.py:29
  13.3 1.0 collective-permute-done.1.refs_1_
  14.3 2.2 %collective-permute-done.2.refs_7_ = bf16[48,3072]{1,0:T(8,128)(2,1)S(1)} collective-permute-done((bf16[48,3072]{1,0:T(8,128)(2,1)S(1)}, bf16[48,3072]{1,0:T(8,128)(2,1)S(1)}, u32[]{:S(2)}, u32[]{:S(2)}) %collective-permute-start.2) | collective-permute-done | bytes 294944 | tf_op jit(solution)/shard_map/ppermute | solution.py:170
  16.4 1.6 %collective-permute-start.5 = (bf16[48,3072]{1,0:T(8,128)(2,1)S(1)}, bf16[48,3072]{1,0:T(8,128)(2,1)S(1)}, u32[]{:S(2)}, u32[]{:S(2)}) collective-permute-start(bf16[48,3072]{1,0:T(8,128)(2,1)S(1)} %collective-permute-done.1.refs_1_), channel_id=1, source_target_pairs={{0,2},{2,4},{4,6},{6,7},{7,5},{5,3},{3,1},{1,0},{8,10},{10,12},{12... | collective-permute-start | bytes 884744 | tf_op jit(solution)/shard_map/ppermute | solution.py:170
  18.0 0.4 collective-permute-start.6
  18.5 4.7 %fetched.4.refs_10_.refs_7_ = bf16[1,6144,1024]{2,1,0:T(8,128)(2,1)S(1)} custom-call(bf16[1,6144,1024]{2,1,0:T(8,128)(2,1)} %source.1), custom_call_target="tpu_custom_call" | custom-call | flops 1024 | bytes 1024 | tf_op jit(solution)/shard_map/fetched/pallas_call | solution.py:29
  23.2 1.6 %collective-permute-start.7 = (bf16[48,3072]{1,0:T(8,128)(2,1)S(1)}, bf16[48,3072]{1,0:T(8,128)(2,1)S(1)}, u32[]{:S(2)}, u32[]{:S(2)}) collective-permute-start(bf16[48,3072]{1,0:T(8,128)(2,1)S(1)} %collective-permute-done.3.refs_6_), channel_id=1, source_target_pairs={{0,2},{2,4},{4,6},{6,7},{7,5},{5,3},{3,1},{1,0},{8,10},{10,12},{12... | collective-permute-start | bytes 884744 | tf_op jit(solution)/shard_map/ppermute | solution.py:170
  24.8 0.4 collective-permute-start.8
  25.3 1.6 %collective-permute-done.5.refs_3_ = bf16[48,3072]{1,0:T(8,128)(2,1)S(1)} collective-permute-done((bf16[48,3072]{1,0:T(8,128)(2,1)S(1)}, bf16[48,3072]{1,0:T(8,128)(2,1)S(1)}, u32[]{:S(2)}, u32[]{:S(2)}) %collective-permute-start.5) | collective-permute-done | bytes 294944 | tf_op jit(solution)/shard_map/ppermute | solution.py:170
  26.9 2.2 %collective-permute-done.6.refs_9_ = bf16[48,3072]{1,0:T(8,128)(2,1)S(1)} collective-permute-done((bf16[48,3072]{1,0:T(8,128)(2,1)S(1)}, bf16[48,3072]{1,0:T(8,128)(2,1)S(1)}, u32[]{:S(2)}, u32[]{:S(2)}) %collective-permute-start.6) | collective-permute-done | bytes 294944 | tf_op jit(solution)/shard_map/ppermute | solution.py:170
  29.1 2.0 %collective-permute-start.9 = (bf16[48,3072]{1,0:T(8,128)(2,1)S(1)}, bf16[48,3072]{1,0:T(8,128)(2,1)S(1)}, u32[]{:S(2)}, u32[]{:S(2)}) collective-permute-start(bf16[48,3072]{1,0:T(8,128)(2,1)S(1)} %collective-permute-done.5.refs_3_), channel_id=1, source_target_pairs={{0,2},{2,4},{4,6},{6,7},{7,5},{5,3},{3,1},{1,0},{8,10},{10,12},{12... | collective-permute-start | bytes 884744 | tf_op jit(solution)/shard_map/ppermute | solution.py:170
  31.1 2.1 %collective-permute-done.7.refs_8_ = bf16[48,3072]{1,0:T(8,128)(2,1)S(1)} collective-permute-done((bf16[48,3072]{1,0:T(8,128)(2,1)S(1)}, bf16[48,3072]{1,0:T(8,128)(2,1)S(1)}, u32[]{:S(2)}, u32[]{:S(2)}) %collective-permute-start.7) | collective-permute-done | bytes 294944 | tf_op jit(solution)/shard_map/ppermute | solution.py:170
  33.2 2.2 %collective-permute-done.8.refs_4_ = bf16[48,3072]{1,0:T(8,128)(2,1)S(1)} collective-permute-done((bf16[48,3072]{1,0:T(8,128)(2,1)S(1)}, bf16[48,3072]{1,0:T(8,128)(2,1)S(1)}, u32[]{:S(2)}, u32[]{:S(2)}) %collective-permute-start.8) | collective-permute-done | bytes 294944 | tf_op jit(solution)/shard_map/ppermute | solution.py:170
  35.4 3.2 %near_gate.1.refs_11_ = f32[240,1024]{1,0:T(8,128)S(1)} custom-call(bf16[48,3072]{1,0:T(8,128)(2,1)S(1)} %get-tuple-element.150.refs_0_, bf16[48,3072]{1,0:T(8,128)(2,1)S(1)} %collective-permute-done.1.refs_1_, bf16[48,3072]{1,0:T(8,128)(2,1)S(1)} %collective-permute-done.4.refs_2_, bf16[48,3072]{1,0:T(8,128)(2,1)S(1)} %collective-permute-done.5.refs_3_, ...), custom_call_target="tpu_custom_call" | custom-call | flops 1024 | bytes 1024 | tf_op jit(solution)/shard_map/near_gate/pallas_call | solution.py:29
  38.6 1.6 %collective-permute-start.11 = (bf16[48,3072]{1,0:T(8,128)(2,1)S(1)}, bf16[48,3072]{1,0:T(8,128)(2,1)S(1)}, u32[]{:S(2)}, u32[]{:S(2)}) collective-permute-start(bf16[48,3072]{1,0:T(8,128)(2,1)S(1)} %collective-permute-done.7.refs_8_), channel_id=1, source_target_pairs={{0,2},{2,4},{4,6},{6,7},{7,5},{5,3},{3,1},{1,0},{8,10},{10,12},{12... | collective-permute-start | bytes 884744 | tf_op jit(solution)/shard_map/ppermute | solution.py:170
  40.2 0.4 collective-permute-start.12
  40.7 1.6 %collective-permute-start.13 = (bf16[48,3072]{1,0:T(8,128)(2,1)S(1)}, bf16[48,3072]{1,0:T(8,128)(2,1)S(1)}, u32[]{:S(2)}, u32[]{:S(2)}) collective-permute-start(bf16[48,3072]{1,0:T(8,128)(2,1)S(1)} %collective-permute-done.9.refs_0_), channel_id=1, source_target_pairs={{0,2},{2,4},{4,6},{6,7},{7,5},{5,3},{3,1},{1,0},{8,10},{10,12},{12... | collective-permute-start | bytes 884744 | tf_op jit(solution)/shard_map/ppermute | solution.py:170
  42.3 0.4 collective-permute-start.14
  42.7 3.2 %near_up.1.hidden = bf16[240,1024]{1,0:T(8,128)(2,1)S(1)} custom-call(bf16[48,3072]{1,0:T(8,128)(2,1)S(1)} %get-tuple-element.150.refs_0_, bf16[48,3072]{1,0:T(8,128)(2,1)S(1)} %collective-permute-done.1.refs_1_, bf16[48,3072]{1,0:T(8,128)(2,1)S(1)} %collective-permute-done.4.refs_2_, bf16[48,3072]{1,0:T(8,128)(2,1)S(1)} %collective-permute-done.5.refs_3_, ...), custom_call_target="tpu_custom_call" | custom-call | flops 1024 | bytes 1024 | tf_op jit(solution)/shard_map/near_up/pallas_call | solution.py:29
  46.0 2.9 %fetched.5.refs_8_.down = bf16[1,1024,3072]{2,1,0:T(8,128)(2,1)S(1)} custom-call(bf16[1,1024,6144]{2,1,0:T(8,128)(2,1)} %w_down), custom_call_target="tpu_custom_call" | custom-call | flops 1024 | bytes 1024 | tf_op jit(solution)/shard_map/fetched/pallas_call | solution.py:29
  48.9 1.2 %collective-permute-done.12.refs_1_ = bf16[48,3072]{1,0:T(8,128)(2,1)S(1)} collective-permute-done((bf16[48,3072]{1,0:T(8,128)(2,1)S(1)}, bf16[48,3072]{1,0:T(8,128)(2,1)S(1)}, u32[]{:S(2)}, u32[]{:S(2)}) %collective-permute-start.12) | collective-permute-done | bytes 294944 | tf_op jit(solution)/shard_map/ppermute | solution.py:170
  50.1 1.7 %collective-permute-done.13.refs_2_ = bf16[48,3072]{1,0:T(8,128)(2,1)S(1)} collective-permute-done((bf16[48,3072]{1,0:T(8,128)(2,1)S(1)}, bf16[48,3072]{1,0:T(8,128)(2,1)S(1)}, u32[]{:S(2)}, u32[]{:S(2)}) %collective-permute-start.13) | collective-permute-done | bytes 294944 | tf_op jit(solution)/shard_map/ppermute | solution.py:170
  51.7 1.5 %collective-permute-done.14.refs_5_ = bf16[48,3072]{1,0:T(8,128)(2,1)S(1)} collective-permute-done((bf16[48,3072]{1,0:T(8,128)(2,1)S(1)}, bf16[48,3072]{1,0:T(8,128)(2,1)S(1)}, u32[]{:S(2)}, u32[]{:S(2)}) %collective-permute-start.14) | collective-permute-done | bytes 294944 | tf_op jit(solution)/shard_map/ppermute | solution.py:170
  53.2 4.8 %rest_first.1 = (bf16[48,3072]{1,0:T(8,128)(2,1)S(1)}, bf16[48,3072]{1,0:T(8,128)(2,1)S(1)}, bf16[48,3072]{1,0:T(8,128)(2,1)S(1)}, bf16[144,1024]{1,0:T(8,128)(2,1)S(1)}) custom-call(bf16[48,3072]{1,0:T(8,128)(2,1)S(1)} %collective-permute-done.9.refs_0_, bf16[48,3072]{1,0:T(8,128)(2,1)S(1)} %collective-permute-done.12.refs_1_, ...), custom_call_target="tpu_custom_call" | custom-call | flops 1024 | bytes 1024 | tf_op jit(solution)/shard_map/rest_first/pallas_call | solution.py:29
  58.0 1.6 %collective-permute-start.15 = (bf16[48,3072]{1,0:T(8,128)(2,1)S(1)}, bf16[48,3072]{1,0:T(8,128)(2,1)S(1)}, u32[]{:S(2)}, u32[]{:S(2)}) collective-permute-start(bf16[48,3072]{1,0:T(8,128)(2,1)S(1)} %get-tuple-element.122), channel_id=1, source_target_pairs={{0,2},{2,4},{4,6},{6,7},{7,5},{5,3},{3,1},{1,0},{8,10},{10,12},{12... | collective-permute-start | bytes 884744 | tf_op jit(solution)/shard_map/ppermute | solution.py:170
  59.6 0.4 collective-permute-start.16
  60.2 4.0 %rest_second.1 = (bf16[48,3072]{1,0:T(8,128)(2,1)S(1)}, bf16[48,3072]{1,0:T(8,128)(2,1)S(1)}, bf16[48,3072]{1,0:T(8,128)(2,1)S(1)}, bf16[1,1024,3072]{2,1,0:T(8,128)(2,1)S(1)}) custom-call(bf16[144,1024]{1,0:T(8,128)(2,1)S(1)} %get-tuple-element.117.hidden, bf16[1,1024,6144]{2,1,0:T(8,128)(2,1)} %w_down), custom_call_target="tpu_custom_call" | custom-call | flops 1024 | bytes 1024 | tf_op jit(solution)/shard_map/rest_second/pallas_call | solution.py:29
  64.2 0.3 collective-permute-start.19
  64.5 1.7 %collective-permute-start.17 = (bf16[48,3072]{1,0:T(8,128)(2,1)S(1)}, bf16[48,3072]{1,0:T(8,128)(2,1)S(1)}, u32[]{:S(2)}, u32[]{:S(2)}) collective-permute-start(bf16[48,3072]{1,0:T(8,128)(2,1)S(1)} %get-tuple-element.118), channel_id=1, source_target_pairs={{0,2},{2,4},{4,6},{6,7},{7,5},{5,3},{3,1},{1,0},{8,10},{10,12},{12... | collective-permute-start | bytes 884744 | tf_op jit(solution)/shard_map/ppermute | solution.py:263
  66.3 1.7 %near_down.2 = (bf16[48,3072]{1,0:T(8,128)(2,1)S(1)}, bf16[48,3072]{1,0:T(8,128)(2,1)S(1)}, bf16[48,3072]{1,0:T(8,128)(2,1)S(1)}, bf16[48,3072]{1,0:T(8,128)(2,1)S(1)}, bf16[48,3072]{1,0:T(8,128)(2,1)S(1)}) custom-call(bf16[240,1024]{1,0:T(8,128)(2,1)S(1)} %near_up.1.hidden, bf16[1,1024,3072]{2,1,0:T(8,128)(2,1)S(1)} %fetched.5.refs_8_.down), custom_call_target="tpu_custom_call" | custom-call | flops 1024 | bytes 1024 | tf_op jit(solution)/shard_map/near_down/pallas_call | solution.py:29
  68.0 1.1 %collective-permute-done.16 = bf16[48,3072]{1,0:T(8,128)(2,1)S(1)} collective-permute-done((bf16[48,3072]{1,0:T(8,128)(2,1)S(1)}, bf16[48,3072]{1,0:T(8,128)(2,1)S(1)}, u32[]{:S(2)}, u32[]{:S(2)}) %collective-permute-start.16) | collective-permute-done | bytes 294944 | tf_op jit(solution)/shard_map/ppermute | solution.py:170
  69.3 2.1 %collective-permute-start.24 = (bf16[48,3072]{1,0:T(8,128)(2,1)S(1)}, bf16[48,3072]{1,0:T(8,128)(2,1)S(1)}, u32[]{:S(2)}, u32[]{:S(2)}) collective-permute-start(bf16[48,3072]{1,0:T(8,128)(2,1)S(1)} %add_convert_fusion.11), channel_id=1, source_target_pairs={{0,2},{2,4},{4,6},{6,7},{7,5},{5,3},{3,1},{1,0},{8,10},{10,12},{12... | collective-permute-start | bytes 884744 | tf_op jit(solution)/shard_map/ppermute | solution.py:170
  71.4 4.0 %collective-permute-done.19 = bf16[48,3072]{1,0:T(8,128)(2,1)S(1)} collective-permute-done((bf16[48,3072]{1,0:T(8,128)(2,1)S(1)}, bf16[48,3072]{1,0:T(8,128)(2,1)S(1)}, u32[]{:S(2)}, u32[]{:S(2)}) %collective-permute-start.19) | collective-permute-done | bytes 294944 | tf_op jit(solution)/shard_map/ppermute | solution.py:262
  75.5 1.7 %near_down.3 = (bf16[48,3072]{1,0:T(8,128)(2,1)S(1)}, bf16[48,3072]{1,0:T(8,128)(2,1)S(1)}, bf16[48,3072]{1,0:T(8,128)(2,1)S(1)}, bf16[48,3072]{1,0:T(8,128)(2,1)S(1)}, bf16[48,3072]{1,0:T(8,128)(2,1)S(1)}) custom-call(bf16[240,1024]{1,0:T(8,128)(2,1)S(1)} %near_up.1.hidden, bf16[1,1024,3072]{2,1,0:T(8,128)(2,1)S(1)} %get-tuple-element.128.down), custom_call_target="tpu_custom_call" | custom-call | flops 1024 | bytes 1024 | tf_op jit(solution)/shard_map/near_down/pallas_call | solution.py:29
  77.3 2.1 %collective-permute-start.18 = (bf16[48,3072]{1,0:T(8,128)(2,1)S(1)}, bf16[48,3072]{1,0:T(8,128)(2,1)S(1)}, u32[]{:S(2)}, u32[]{:S(2)}) collective-permute-start(bf16[48,3072]{1,0:T(8,128)(2,1)S(1)} %add_convert_fusion.9), channel_id=1, source_target_pairs={{0,2},{2,4},{4,6},{6,7},{7,5},{5,3},{3,1},{1,0},{8,10},{10,12},{12... | collective-permute-start | bytes 884744 | tf_op jit(solution)/shard_map/ppermute | solution.py:170
  79.4 2.3 %collective-permute-done.25 = bf16[48,3072]{1,0:T(8,128)(2,1)S(1)} collective-permute-done((bf16[48,3072]{1,0:T(8,128)(2,1)S(1)}, bf16[48,3072]{1,0:T(8,128)(2,1)S(1)}, u32[]{:S(2)}, u32[]{:S(2)}) %collective-permute-start.25) | collective-permute-done | bytes 294944 | tf_op jit(solution)/shard_map/ppermute | solution.py:170
  81.8 0.5 collective-permute-start.27
  82.4 1.6 %collective-permute-start.26 = (bf16[48,3072]{1,0:T(8,128)(2,1)S(1)}, bf16[48,3072]{1,0:T(8,128)(2,1)S(1)}, u32[]{:S(2)}, u32[]{:S(2)}) collective-permute-start(bf16[48,3072]{1,0:T(8,128)(2,1)S(1)} %add_convert_fusion.4), channel_id=1, source_target_pairs={{0,2},{2,4},{4,6},{6,7},{7,5},{5,3},{3,1},{1,0},{8,10},{10,12},{12... | collective-permute-start | bytes 884744 | tf_op jit(solution)/shard_map/ppermute | solution.py:170
  84.0 4.0 %collective-permute-done.20 = bf16[48,3072]{1,0:T(8,128)(2,1)S(1)} collective-permute-done((bf16[48,3072]{1,0:T(8,128)(2,1)S(1)}, bf16[48,3072]{1,0:T(8,128)(2,1)S(1)}, u32[]{:S(2)}, u32[]{:S(2)}) %collective-permute-start.20) | collective-permute-done | bytes 294944 | tf_op jit(solution)/shard_map/ppermute | solution.py:170
  88.1 0.5 collective-permute-start.22
  88.7 1.6 %collective-permute-start.21 = (bf16[48,3072]{1,0:T(8,128)(2,1)S(1)}, bf16[48,3072]{1,0:T(8,128)(2,1)S(1)}, u32[]{:S(2)}, u32[]{:S(2)}) collective-permute-start(bf16[48,3072]{1,0:T(8,128)(2,1)S(1)} %add_convert_fusion.7), channel_id=1, source_target_pairs={{0,2},{2,4},{4,6},{6,7},{7,5},{5,3},{3,1},{1,0},{8,10},{10,12},{12... | collective-permute-start | bytes 884744 | tf_op jit(solution)/shard_map/ppermute | solution.py:170
  90.3 4.0 %collective-permute-done.27 = bf16[48,3072]{1,0:T(8,128)(2,1)S(1)} collective-permute-done((bf16[48,3072]{1,0:T(8,128)(2,1)S(1)}, bf16[48,3072]{1,0:T(8,128)(2,1)S(1)}, u32[]{:S(2)}, u32[]{:S(2)}) %collective-permute-start.27) | collective-permute-done | bytes 294944 | tf_op jit(solution)/shard_map/ppermute | solution.py:170
  94.4 1.4 %collective-permute-start.28 = (bf16[48,3072]{1,0:T(8,128)(2,1)S(1)}, bf16[48,3072]{1,0:T(8,128)(2,1)S(1)}, u32[]{:S(2)}, u32[]{:S(2)}) collective-permute-start(bf16[48,3072]{1,0:T(8,128)(2,1)S(1)} %add_convert_fusion.2), channel_id=1, source_target_pairs={{0,2},{2,4},{4,6},{6,7},{7,5},{5,3},{3,1},{1,0},{8,10},{10,12},{12... | collective-permute-start | bytes 884744 | tf_op jit(solution)/shard_map/ppermute | solution.py:273
  95.9 2.1 %collective-permute-done.22 = bf16[48,3072]{1,0:T(8,128)(2,1)S(1)} collective-permute-done((bf16[48,3072]{1,0:T(8,128)(2,1)S(1)}, bf16[48,3072]{1,0:T(8,128)(2,1)S(1)}, u32[]{:S(2)}, u32[]{:S(2)}) %collective-permute-start.22) | collective-permute-done | bytes 294944 | tf_op jit(solution)/shard_map/ppermute | solution.py:170
  97.9 1.7 %collective-permute-done.21 = bf16[48,3072]{1,0:T(8,128)(2,1)S(1)} collective-permute-done((bf16[48,3072]{1,0:T(8,128)(2,1)S(1)}, bf16[48,3072]{1,0:T(8,128)(2,1)S(1)}, u32[]{:S(2)}, u32[]{:S(2)}) %collective-permute-start.21) | collective-permute-done | bytes 294944 | tf_op jit(solution)/shard_map/ppermute | solution.py:170
  99.8 1.5 %collective-permute-start.23 = (bf16[48,3072]{1,0:T(8,128)(2,1)S(1)}, bf16[48,3072]{1,0:T(8,128)(2,1)S(1)}, u32[]{:S(2)}, u32[]{:S(2)}) collective-permute-start(bf16[48,3072]{1,0:T(8,128)(2,1)S(1)} %add_convert_fusion.5), channel_id=1, source_target_pairs={{2,0},{4,2},{6,4},{7,6},{5,7},{3,5},{1,3},{0,1},{10,8},{12,10},{14... | collective-permute-start | bytes 884744 | tf_op jit(solution)/shard_map/ppermute | solution.py:274
  101.2 1.6 %collective-permute-done.28 = bf16[48,3072]{1,0:T(8,128)(2,1)S(1)} collective-permute-done((bf16[48,3072]{1,0:T(8,128)(2,1)S(1)}, bf16[48,3072]{1,0:T(8,128)(2,1)S(1)}, u32[]{:S(2)}, u32[]{:S(2)}) %collective-permute-start.28) | collective-permute-done | bytes 294944 | tf_op jit(solution)/shard_map/ppermute | solution.py:273
  102.9 0.1 add_convert_fusion.1
  103.1 0.1 select_convert_fusion.weights
  103.2 1.2 %collective-permute-done.29.swapped = bf16[24,3072]{1,0:T(8,128)(2,1)S(1)} collective-permute-done((bf16[24,3072]{1,0:T(8,128)(2,1)S(1)}, bf16[24,3072]{1,0:T(8,128)(2,1)S(1)}, u32[]{:S(2)}, u32[]{:S(2)}) %collective-permute-start.29) | collective-permute-done | bytes 147488 | tf_op jit(solution)/shard_map/ppermute | solution.py:284
  104.4 1.1 combined.2.refs_0_
  105.5 1.0 collective-permute-done.23
  106.5 0.1 add_convert_fusion
  106.8 1.4 %collective-permute-done.30.swapped = bf16[24,3072]{1,0:T(8,128)(2,1)S(1)} collective-permute-done((bf16[24,3072]{1,0:T(8,128)(2,1)S(1)}, bf16[24,3072]{1,0:T(8,128)(2,1)S(1)}, u32[]{:S(2)}, u32[]{:S(2)}) %collective-permute-start.30) | collective-permute-done | bytes 147488 | tf_op jit(solution)/shard_map/ppermute | solution.py:284
  108.1 1.1 combined.3
  (47 shorter events, 1.6 us)
Async XLA Ops:
  0.0 1.4 %copy-start = (bf16[64,6144]{1,0:T(8,128)(2,1)S(1)}, bf16[64,6144]{1,0:T(8,128)(2,1)}, u32[]{:S(2)}) copy-start(bf16[64,6144]{1,0:T(8,128)(2,1)} %param.6) | copy-start | bytes 2359300
  1.7 1.7 %collective-permute-start = (bf16[24,6144]{1,0:T(8,128)(2,1)S(1)}, bf16[24,6144]{1,0:T(8,128)(2,1)S(1)}, u32[]{:S(2)}, u32[]{:S(2)}) collective-permute-start(bf16[24,6144]{1,0:T(8,128)(2,1)S(1)} %get-tuple-element.152), channel_id=1, source_target_pairs={{0,8},{8,0},{1,9},{9,1},{2,10},{10,2},{3,11},{11,3},{4,12},{12,4},... | collective-permute-start | bytes 884744 | tf_op jit(solution)/shard_map/ppermute | solution.py:184
  3.5 10.7 %collective-permute-start.1 = (bf16[48,3072]{1,0:T(8,128)(2,1)S(1)}, bf16[48,3072]{1,0:T(8,128)(2,1)S(1)}, u32[]{:S(2)}, u32[]{:S(2)}) collective-permute-start(bf16[48,3072]{1,0:T(8,128)(2,1)S(1)} %get-tuple-element.150.refs_0_), channel_id=1, source_target_pairs={{0,2},{2,4},{4,6},{6,7},{7,5},{5,3},{3,1},{1,0},{8,10},{10,12},{12... | collective-permute-start | bytes 884744 | tf_op jit(solution)/shard_map/ppermute | solution.py:170
  6.5 9.9 %collective-permute-start.2 = (bf16[48,3072]{1,0:T(8,128)(2,1)S(1)}, bf16[48,3072]{1,0:T(8,128)(2,1)S(1)}, u32[]{:S(2)}, u32[]{:S(2)}) collective-permute-start(bf16[48,3072]{1,0:T(8,128)(2,1)S(1)} %get-tuple-element.149.refs_5_), channel_id=1, source_target_pairs={{2,0},{4,2},{6,4},{7,6},{5,7},{3,5},{1,3},{0,1},{10,8},{12,10},{14... | collective-permute-start | bytes 884744 | tf_op jit(solution)/shard_map/ppermute | solution.py:170
  6.6 16.6 %collective-permute-start.3 = (bf16[48,3072]{1,0:T(8,128)(2,1)S(1)}, bf16[48,3072]{1,0:T(8,128)(2,1)S(1)}, u32[]{:S(2)}, u32[]{:S(2)}) collective-permute-start(bf16[48,3072]{1,0:T(8,128)(2,1)S(1)} %get-tuple-element.149.refs_5_), channel_id=1, source_target_pairs={{0,2},{2,4},{4,6},{6,7},{7,5},{5,3},{3,1},{1,0},{8,10},{10,12},{12... | collective-permute-start | bytes 884744 | tf_op jit(solution)/shard_map/ppermute | solution.py:170
  8.6 14.6 %collective-permute-start.4 = (bf16[48,3072]{1,0:T(8,128)(2,1)S(1)}, bf16[48,3072]{1,0:T(8,128)(2,1)S(1)}, u32[]{:S(2)}, u32[]{:S(2)}) collective-permute-start(bf16[48,3072]{1,0:T(8,128)(2,1)S(1)} %get-tuple-element.150.refs_0_), channel_id=1, source_target_pairs={{2,0},{4,2},{6,4},{7,6},{5,7},{3,5},{1,3},{0,1},{10,8},{12,10},{14... | collective-permute-start | bytes 884744 | tf_op jit(solution)/shard_map/ppermute | solution.py:170
  16.4 10.5 %collective-permute-start.5 = (bf16[48,3072]{1,0:T(8,128)(2,1)S(1)}, bf16[48,3072]{1,0:T(8,128)(2,1)S(1)}, u32[]{:S(2)}, u32[]{:S(2)}) collective-permute-start(bf16[48,3072]{1,0:T(8,128)(2,1)S(1)} %collective-permute-done.1.refs_1_), channel_id=1, source_target_pairs={{0,2},{2,4},{4,6},{6,7},{7,5},{5,3},{3,1},{1,0},{8,10},{10,12},{12... | collective-permute-start | bytes 884744 | tf_op jit(solution)/shard_map/ppermute | solution.py:170
  18.0 11.1 %collective-permute-start.6 = (bf16[48,3072]{1,0:T(8,128)(2,1)S(1)}, bf16[48,3072]{1,0:T(8,128)(2,1)S(1)}, u32[]{:S(2)}, u32[]{:S(2)}) collective-permute-start(bf16[48,3072]{1,0:T(8,128)(2,1)S(1)} %collective-permute-done.2.refs_7_), channel_id=1, source_target_pairs={{2,0},{4,2},{6,4},{7,6},{5,7},{3,5},{1,3},{0,1},{10,8},{12,10},{14... | collective-permute-start | bytes 884744 | tf_op jit(solution)/shard_map/ppermute | solution.py:170
  23.2 10.0 %collective-permute-start.7 = (bf16[48,3072]{1,0:T(8,128)(2,1)S(1)}, bf16[48,3072]{1,0:T(8,128)(2,1)S(1)}, u32[]{:S(2)}, u32[]{:S(2)}) collective-permute-start(bf16[48,3072]{1,0:T(8,128)(2,1)S(1)} %collective-permute-done.3.refs_6_), channel_id=1, source_target_pairs={{0,2},{2,4},{4,6},{6,7},{7,5},{5,3},{3,1},{1,0},{8,10},{10,12},{12... | collective-permute-start | bytes 884744 | tf_op jit(solution)/shard_map/ppermute | solution.py:170
  24.8 10.6 %collective-permute-start.8 = (bf16[48,3072]{1,0:T(8,128)(2,1)S(1)}, bf16[48,3072]{1,0:T(8,128)(2,1)S(1)}, u32[]{:S(2)}, u32[]{:S(2)}) collective-permute-start(bf16[48,3072]{1,0:T(8,128)(2,1)S(1)} %collective-permute-done.4.refs_2_), channel_id=1, source_target_pairs={{2,0},{4,2},{6,4},{7,6},{5,7},{3,5},{1,3},{0,1},{10,8},{12,10},{14... | collective-permute-start | bytes 884744 | tf_op jit(solution)/shard_map/ppermute | solution.py:170
  29.1 11.6 %collective-permute-start.10 = (bf16[48,3072]{1,0:T(8,128)(2,1)S(1)}, bf16[48,3072]{1,0:T(8,128)(2,1)S(1)}, u32[]{:S(2)}, u32[]{:S(2)}) collective-permute-start(bf16[48,3072]{1,0:T(8,128)(2,1)S(1)} %collective-permute-done.6.refs_9_), channel_id=1, source_target_pairs={{2,0},{4,2},{6,4},{7,6},{5,7},{3,5},{1,3},{0,1},{10,8},{12,10},{14... | collective-permute-start | bytes 884744 | tf_op jit(solution)/shard_map/ppermute | solution.py:170
  29.1 11.6 %collective-permute-start.9 = (bf16[48,3072]{1,0:T(8,128)(2,1)S(1)}, bf16[48,3072]{1,0:T(8,128)(2,1)S(1)}, u32[]{:S(2)}, u32[]{:S(2)}) collective-permute-start(bf16[48,3072]{1,0:T(8,128)(2,1)S(1)} %collective-permute-done.5.refs_3_), channel_id=1, source_target_pairs={{0,2},{2,4},{4,6},{6,7},{7,5},{5,3},{3,1},{1,0},{8,10},{10,12},{12... | collective-permute-start | bytes 884744 | tf_op jit(solution)/shard_map/ppermute | solution.py:170
  38.6 10.3 %collective-permute-start.11 = (bf16[48,3072]{1,0:T(8,128)(2,1)S(1)}, bf16[48,3072]{1,0:T(8,128)(2,1)S(1)}, u32[]{:S(2)}, u32[]{:S(2)}) collective-permute-start(bf16[48,3072]{1,0:T(8,128)(2,1)S(1)} %collective-permute-done.7.refs_8_), channel_id=1, source_target_pairs={{0,2},{2,4},{4,6},{6,7},{7,5},{5,3},{3,1},{1,0},{8,10},{10,12},{12... | collective-permute-start | bytes 884744 | tf_op jit(solution)/shard_map/ppermute | solution.py:170
  40.2 9.8 %collective-permute-start.12 = (bf16[48,3072]{1,0:T(8,128)(2,1)S(1)}, bf16[48,3072]{1,0:T(8,128)(2,1)S(1)}, u32[]{:S(2)}, u32[]{:S(2)}) collective-permute-start(bf16[48,3072]{1,0:T(8,128)(2,1)S(1)} %collective-permute-done.8.refs_4_), channel_id=1, source_target_pairs={{2,0},{4,2},{6,4},{7,6},{5,7},{3,5},{1,3},{0,1},{10,8},{12,10},{14... | collective-permute-start | bytes 884744 | tf_op jit(solution)/shard_map/ppermute | solution.py:170
  40.7 11.0 %collective-permute-start.13 = (bf16[48,3072]{1,0:T(8,128)(2,1)S(1)}, bf16[48,3072]{1,0:T(8,128)(2,1)S(1)}, u32[]{:S(2)}, u32[]{:S(2)}) collective-permute-start(bf16[48,3072]{1,0:T(8,128)(2,1)S(1)} %collective-permute-done.9.refs_0_), channel_id=1, source_target_pairs={{0,2},{2,4},{4,6},{6,7},{7,5},{5,3},{3,1},{1,0},{8,10},{10,12},{12... | collective-permute-start | bytes 884744 | tf_op jit(solution)/shard_map/ppermute | solution.py:170
  42.3 10.9 %collective-permute-start.14 = (bf16[48,3072]{1,0:T(8,128)(2,1)S(1)}, bf16[48,3072]{1,0:T(8,128)(2,1)S(1)}, u32[]{:S(2)}, u32[]{:S(2)}) collective-permute-start(bf16[48,3072]{1,0:T(8,128)(2,1)S(1)} %collective-permute-done.10.refs_4_), channel_id=1, source_target_pairs={{2,0},{4,2},{6,4},{7,6},{5,7},{3,5},{1,3},{0,1},{10,8},{12,10},{14... | collective-permute-start | bytes 884744 | tf_op jit(solution)/shard_map/ppermute | solution.py:170
  48.9 11.2 %copy-start.2 = (s32[64,2]{0,1:T(2,128)S(1)}, s32[64,2]{0,1:T(2,128)}, u32[]{:S(2)}) copy-start(s32[64,2]{0,1:T(2,128)} %param.7) | copy-start | bytes 1540
  48.9 11.2 %copy-start.3 = (f32[64,2]{0,1:T(2,128)S(1)}, f32[64,2]{0,1:T(2,128)}, u32[]{:S(2)}) copy-start(f32[64,2]{0,1:T(2,128)} %param.8) | copy-start | bytes 1540
  58.0 10.0 %collective-permute-start.15 = (bf16[48,3072]{1,0:T(8,128)(2,1)S(1)}, bf16[48,3072]{1,0:T(8,128)(2,1)S(1)}, u32[]{:S(2)}, u32[]{:S(2)}) collective-permute-start(bf16[48,3072]{1,0:T(8,128)(2,1)S(1)} %get-tuple-element.122), channel_id=1, source_target_pairs={{0,2},{2,4},{4,6},{6,7},{7,5},{5,3},{3,1},{1,0},{8,10},{10,12},{12... | collective-permute-start | bytes 884744 | tf_op jit(solution)/shard_map/ppermute | solution.py:170
  59.6 9.5 %collective-permute-start.16 = (bf16[48,3072]{1,0:T(8,128)(2,1)S(1)}, bf16[48,3072]{1,0:T(8,128)(2,1)S(1)}, u32[]{:S(2)}, u32[]{:S(2)}) collective-permute-start(bf16[48,3072]{1,0:T(8,128)(2,1)S(1)} %get-tuple-element.123), channel_id=1, source_target_pairs={{2,0},{4,2},{6,4},{7,6},{5,7},{3,5},{1,3},{0,1},{10,8},{12,10},{14... | collective-permute-start | bytes 884744 | tf_op jit(solution)/shard_map/ppermute | solution.py:170
  64.2 11.2 %collective-permute-start.19 = (bf16[48,3072]{1,0:T(8,128)(2,1)S(1)}, bf16[48,3072]{1,0:T(8,128)(2,1)S(1)}, u32[]{:S(2)}, u32[]{:S(2)}) collective-permute-start(bf16[48,3072]{1,0:T(8,128)(2,1)S(1)} %get-tuple-element.119), channel_id=1, source_target_pairs={{2,0},{4,2},{6,4},{7,6},{5,7},{3,5},{1,3},{0,1},{10,8},{12,10},{14... | collective-permute-start | bytes 884744 | tf_op jit(solution)/shard_map/ppermute | solution.py:262
  64.5 12.7 %collective-permute-start.17 = (bf16[48,3072]{1,0:T(8,128)(2,1)S(1)}, bf16[48,3072]{1,0:T(8,128)(2,1)S(1)}, u32[]{:S(2)}, u32[]{:S(2)}) collective-permute-start(bf16[48,3072]{1,0:T(8,128)(2,1)S(1)} %get-tuple-element.118), channel_id=1, source_target_pairs={{0,2},{2,4},{4,6},{6,7},{7,5},{5,3},{3,1},{1,0},{8,10},{10,12},{12... | collective-permute-start | bytes 884744 | tf_op jit(solution)/shard_map/ppermute | solution.py:263
  69.2 12.6 %collective-permute-start.25 = (bf16[48,3072]{1,0:T(8,128)(2,1)S(1)}, bf16[48,3072]{1,0:T(8,128)(2,1)S(1)}, u32[]{:S(2)}, u32[]{:S(2)}) collective-permute-start(bf16[48,3072]{1,0:T(8,128)(2,1)S(1)} %add_convert_fusion.10), channel_id=1, source_target_pairs={{2,0},{4,2},{6,4},{7,6},{5,7},{3,5},{1,3},{0,1},{10,8},{12,10},{14... | collective-permute-start | bytes 884744 | tf_op jit(solution)/shard_map/ppermute | solution.py:170
  69.3 12.4 %collective-permute-start.24 = (bf16[48,3072]{1,0:T(8,128)(2,1)S(1)}, bf16[48,3072]{1,0:T(8,128)(2,1)S(1)}, u32[]{:S(2)}, u32[]{:S(2)}) collective-permute-start(bf16[48,3072]{1,0:T(8,128)(2,1)S(1)} %add_convert_fusion.11), channel_id=1, source_target_pairs={{0,2},{2,4},{4,6},{6,7},{7,5},{5,3},{3,1},{1,0},{8,10},{10,12},{12... | collective-permute-start | bytes 884744 | tf_op jit(solution)/shard_map/ppermute | solution.py:170
  75.5 12.6 %collective-permute-start.20 = (bf16[48,3072]{1,0:T(8,128)(2,1)S(1)}, bf16[48,3072]{1,0:T(8,128)(2,1)S(1)}, u32[]{:S(2)}, u32[]{:S(2)}) collective-permute-start(bf16[48,3072]{1,0:T(8,128)(2,1)S(1)} %add_convert_fusion.8), channel_id=1, source_target_pairs={{2,0},{4,2},{6,4},{7,6},{5,7},{3,5},{1,3},{0,1},{10,8},{12,10},{14... | collective-permute-start | bytes 884744 | tf_op jit(solution)/shard_map/ppermute | solution.py:170
  77.2 32.0 %copy-start.1 = (bf16[64,6144]{1,0:T(8,128)(2,1)S(1)}, bf16[64,6144]{1,0:T(8,128)(2,1)}, u32[]{:S(2)}) copy-start(bf16[64,6144]{1,0:T(8,128)(2,1)} %param.6) | copy-start | bytes 2359300
  77.3 10.7 %collective-permute-start.18 = (bf16[48,3072]{1,0:T(8,128)(2,1)S(1)}, bf16[48,3072]{1,0:T(8,128)(2,1)S(1)}, u32[]{:S(2)}, u32[]{:S(2)}) collective-permute-start(bf16[48,3072]{1,0:T(8,128)(2,1)S(1)} %add_convert_fusion.9), channel_id=1, source_target_pairs={{0,2},{2,4},{4,6},{6,7},{7,5},{5,3},{3,1},{1,0},{8,10},{10,12},{12... | collective-permute-start | bytes 884744 | tf_op jit(solution)/shard_map/ppermute | solution.py:170
  81.8 12.6 %collective-permute-start.27 = (bf16[48,3072]{1,0:T(8,128)(2,1)S(1)}, bf16[48,3072]{1,0:T(8,128)(2,1)S(1)}, u32[]{:S(2)}, u32[]{:S(2)}) collective-permute-start(bf16[48,3072]{1,0:T(8,128)(2,1)S(1)} %add_convert_fusion.3), channel_id=1, source_target_pairs={{2,0},{4,2},{6,4},{7,6},{5,7},{3,5},{1,3},{0,1},{10,8},{12,10},{14... | collective-permute-start | bytes 884744 | tf_op jit(solution)/shard_map/ppermute | solution.py:170
  82.4 12.0 %collective-permute-start.26 = (bf16[48,3072]{1,0:T(8,128)(2,1)S(1)}, bf16[48,3072]{1,0:T(8,128)(2,1)S(1)}, u32[]{:S(2)}, u32[]{:S(2)}) collective-permute-start(bf16[48,3072]{1,0:T(8,128)(2,1)S(1)} %add_convert_fusion.4), channel_id=1, source_target_pairs={{0,2},{2,4},{4,6},{6,7},{7,5},{5,3},{3,1},{1,0},{8,10},{10,12},{12... | collective-permute-start | bytes 884744 | tf_op jit(solution)/shard_map/ppermute | solution.py:170
  88.1 9.8 %collective-permute-start.22 = (bf16[48,3072]{1,0:T(8,128)(2,1)S(1)}, bf16[48,3072]{1,0:T(8,128)(2,1)S(1)}, u32[]{:S(2)}, u32[]{:S(2)}) collective-permute-start(bf16[48,3072]{1,0:T(8,128)(2,1)S(1)} %add_convert_fusion.6), channel_id=1, source_target_pairs={{2,0},{4,2},{6,4},{7,6},{5,7},{3,5},{1,3},{0,1},{10,8},{12,10},{14... | collective-permute-start | bytes 884744 | tf_op jit(solution)/shard_map/ppermute | solution.py:170
  88.7 11.0 %collective-permute-start.21 = (bf16[48,3072]{1,0:T(8,128)(2,1)S(1)}, bf16[48,3072]{1,0:T(8,128)(2,1)S(1)}, u32[]{:S(2)}, u32[]{:S(2)}) collective-permute-start(bf16[48,3072]{1,0:T(8,128)(2,1)S(1)} %add_convert_fusion.7), channel_id=1, source_target_pairs={{0,2},{2,4},{4,6},{6,7},{7,5},{5,3},{3,1},{1,0},{8,10},{10,12},{12... | collective-permute-start | bytes 884744 | tf_op jit(solution)/shard_map/ppermute | solution.py:170
  94.4 8.4 %collective-permute-start.28 = (bf16[48,3072]{1,0:T(8,128)(2,1)S(1)}, bf16[48,3072]{1,0:T(8,128)(2,1)S(1)}, u32[]{:S(2)}, u32[]{:S(2)}) collective-permute-start(bf16[48,3072]{1,0:T(8,128)(2,1)S(1)} %add_convert_fusion.2), channel_id=1, source_target_pairs={{0,2},{2,4},{4,6},{6,7},{7,5},{5,3},{3,1},{1,0},{8,10},{10,12},{12... | collective-permute-start | bytes 884744 | tf_op jit(solution)/shard_map/ppermute | solution.py:273
  99.8 6.8 %collective-permute-start.23 = (bf16[48,3072]{1,0:T(8,128)(2,1)S(1)}, bf16[48,3072]{1,0:T(8,128)(2,1)S(1)}, u32[]{:S(2)}, u32[]{:S(2)}) collective-permute-start(bf16[48,3072]{1,0:T(8,128)(2,1)S(1)} %add_convert_fusion.5), channel_id=1, source_target_pairs={{2,0},{4,2},{6,4},{7,6},{5,7},{3,5},{1,3},{0,1},{10,8},{12,10},{14... | collective-permute-start | bytes 884744 | tf_op jit(solution)/shard_map/ppermute | solution.py:274
  103.0 1.4 %collective-permute-start.29 = (bf16[24,3072]{1,0:T(8,128)(2,1)S(1)}, bf16[24,3072]{1,0:T(8,128)(2,1)S(1)}, u32[]{:S(2)}, u32[]{:S(2)}) collective-permute-start(bf16[24,3072]{1,0:T(8,128)(2,1)S(1)} %get-tuple-element.155), channel_id=1, source_target_pairs={{0,8},{8,0},{1,9},{9,1},{2,10},{10,2},{3,11},{11,3},{4,12},{12,4},... | collective-permute-start | bytes 442376 | tf_op jit(solution)/shard_map/ppermute | solution.py:284
  106.7 1.4 %collective-permute-start.30 = (bf16[24,3072]{1,0:T(8,128)(2,1)S(1)}, bf16[24,3072]{1,0:T(8,128)(2,1)S(1)}, u32[]{:S(2)}, u32[]{:S(2)}) collective-permute-start(bf16[24,3072]{1,0:T(8,128)(2,1)S(1)} %get-tuple-element.153), channel_id=1, source_target_pairs={{0,8},{8,0},{1,9},{9,1},{2,10},{10,2},{3,11},{11,3},{4,12},{12,4},... | collective-permute-start | bytes 442376 | tf_op jit(solution)/shard_map/ppermute | solution.py:284
